TPU v7x, 32 devices: a whole 2x2x4 slice. The times are simulated.
32 devices in a mesh: section: 16 (over z, y, x), rep: 2 (over core).
Axes of the slice: x: 2, y: 2, z: 4, core: 2. Of those that a mesh axis runs over, the one named last changes fastest.
Arguments:
- features: bfloat16 [16384, 512], P('section'), may hold values from -6 to 6
- weight: bfloat16 [512, 512], replicated, may hold values from -0.25 to 0.25
- tile_values: bfloat16 [16, 16, 24, 128, 128], P('section', 'rep'), may hold values from 0 to 0.033691406
- tile_rows: int32 [16, 16, 24], P('section', 'rep'), may hold values from 0 to 7
- tile_cols: int32 [16, 16, 24], P('section', 'rep'), may hold values from 0 to 7
- tile_count: int32 [16, 16], P('section', 'rep'), may hold values from 3 to 24, as said below
- cotangent: bfloat16 [16384, 512], P(('section', 'rep')), may hold values from -6 to 6
Outputs:
- activated: bfloat16 [16384, 512], P(('section', 'rep'))
- feat_grad: bfloat16 [2, 8192, 512], P('rep', 'section')
- weight_grad: float32 [512, 512], replicated
Inputs may be any that keep to these rules, and one draw needn't show every extreme that they name: Slots k >= tile_count[s, j] of a row block and panel are ignored; some row block and panel has all 24 slots live.
All inputs are finite; a program needn't handle non-finite values.
Results may differ from a plain program's by a relative error of at most 0.02.
Values may be sent and summed in bfloat16 or wider, within the bound.
No kernel may reach another device: no remote copies, remote signals or barrier semaphores. Data moves between devices by JAX's collectives and lax.ppermute only.
A program may use at most 128 MiB of HBM per device.

v0:
```python
import jax
import jax.numpy as jnp
from jax import lax
from jax.sharding import PartitionSpec as P


def from_root(value, axis, source):
    kept = jnp.where(lax.axis_index(axis) == source, value, 0).astype(value.dtype)
    return lax.psum(kept, axis)


def slope_grad(pre, cotangent):
    sigma = jax.nn.sigmoid(pre)
    return (cotangent.astype(jnp.float32) * sigma * (1.0 + pre * (1.0 - sigma))).astype(
        jnp.bfloat16
    )


def shards(features, weight, tile_values, tile_rows, tile_cols, tile_count, cotangent):
    panel_count = tile_values.shape[1]
    slot_count = tile_values.shape[2]
    tile_size = tile_values.shape[3]
    block_rows = features.shape[0]
    feat_width = features.shape[1]
    row_tiles = block_rows // tile_size
    rep_index = lax.axis_index("rep")
    is_live = lax.broadcasted_iota(jnp.int32, (panel_count, slot_count), 1) < tile_count[0][:, None]
    tile_index = lax.broadcasted_iota(jnp.int32, (panel_count, slot_count, row_tiles), 2)
    row_select = ((tile_rows[0][:, :, None] == tile_index) & is_live[:, :, None]).astype(
        jnp.float32
    )
    col_select = ((tile_cols[0][:, :, None] == tile_index) & is_live[:, :, None]).astype(
        jnp.float32
    )
    running = jnp.zeros((row_tiles, tile_size, feat_width), jnp.float32)
    for panel_pos in range(panel_count):
        owner_section = rep_index * panel_count + panel_pos
        source = from_root(features, "section", owner_section)
        picked = jnp.take(
            source.reshape(row_tiles, tile_size, feat_width), tile_cols[0, panel_pos], axis=0
        )
        product = jnp.einsum(
            "kab,kbf->kaf", tile_values[0, panel_pos], picked, preferred_element_type=jnp.float32
        )
        running = running + jnp.einsum(
            "ki,kaf->iaf", row_select[panel_pos], product, precision=lax.Precision.HIGHEST
        )
    agg_part = running.reshape(block_rows, feat_width)
    agg_rows = lax.psum_scatter(
        agg_part.astype(jnp.bfloat16), "rep", scatter_dimension=0, tiled=True
    )
    pre_rows = jnp.dot(agg_rows, weight, preferred_element_type=jnp.float32)
    activated = jax.nn.silu(pre_rows).astype(jnp.bfloat16)
    pre_grad = slope_grad(pre_rows, cotangent)
    weight_grad = lax.psum(
        jnp.dot(agg_rows.T, pre_grad, preferred_element_type=jnp.float32), ("section", "rep")
    )
    grad_own = jnp.dot(pre_grad, weight.T, preferred_element_type=jnp.float32).astype(jnp.bfloat16)
    grad_block = lax.all_gather(grad_own, "rep", axis=0, tiled=True)
    grad_tiles = grad_block.reshape(row_tiles, tile_size, feat_width)
    pieces = []
    for panel_pos in range(panel_count):
        picked = jnp.take(grad_tiles, tile_rows[0, panel_pos], axis=0)
        product = jnp.einsum(
            "kab,kaf->kbf", tile_values[0, panel_pos], picked, preferred_element_type=jnp.float32
        )
        spread = jnp.einsum(
            "ki,kbf->ibf", col_select[panel_pos], product, precision=lax.Precision.HIGHEST
        )
        pieces.append(spread.reshape(block_rows, feat_width))
    stacked = jnp.concatenate(pieces, axis=0)
    feat_grad = lax.psum_scatter(
        stacked.astype(jnp.bfloat16), "section", scatter_dimension=0, tiled=True
    )
    return (activated, feat_grad[None], weight_grad)


def solution(mesh):
    placed = (
        P("section", None),
        P(),
        P("section", "rep", None, None, None),
        P("section", "rep", None),
        P("section", "rep", None),
        P("section", "rep"),
        P(("section", "rep"), None),
    )
    return jax.shard_map(
        shards,
        mesh=mesh,
        in_specs=placed,
        out_specs=(P(("section", "rep"), None), P("rep", "section", None), P()),
        check_vma=False,
    )
```

profile of v0, /device:TPU:0, one launch (start us, length us, event | category | flops | bytes accessed | tf_op | source)
XLA Modules:
  0.0 845.8 jit_solution(7620001421513506131)
XLA Ops:
  7.2 4.7 broadcast_select_fusion.7
  12.8 267.5 %all-reduce.6.cloned.1.call-done = (bf16[8,128,512]{2,1,0:T(8,128)(2,1)}, bf16[8,128,512]{2,1,0:T(8,128)(2,1)}, bf16[8,128,512]{2,1,0:T(8,128)(2,1)}, bf16[8,128...) async-done(((bf16[8,128,512]{2,1,0:T(8,128)(2,1)}, ...) | async-done | bytes 8388624 | tf_op jit(solution)/shard_map/psum | solution.py:9
  280.3 3.7 gather_fusion.6
  284.0 5.8 fusion.50
  289.8 6.8 copy.25
  296.6 2.5 gather_fusion.5
  299.2 5.8 fusion.52
  305.0 6.7 copy.24
  311.6 6.5 fusion.18
  318.1 3.6 fusion.20
  321.7 2.5 gather_fusion.4
  324.2 5.8 fusion.54
  330.1 7.1 copy.23
  337.2 6.4 fusion.22
  343.6 2.5 gather_fusion.3
  346.2 5.8 fusion.56
  352.0 6.7 copy.22
  358.7 6.4 fusion.24
  365.1 2.5 gather_fusion.2
  367.7 5.8 fusion.58
  373.5 6.8 copy.21
  380.4 6.5 fusion.26
  386.8 2.5 gather_fusion.1
  389.4 5.8 fusion.60
  395.2 6.7 copy.20
  401.9 6.5 fusion.28
  408.4 2.5 gather_fusion.7
  411.0 5.8 fusion.48
  416.8 6.9 copy.26
  423.7 6.5 fusion.16
  432.6 5.8 fusion.62
  438.5 6.8 copy.19
  445.3 9.3 %add_convert_fusion = bf16[8,128,512]{2,0,1:T(8,128)(2,1)S(1)} fusion(f32[8,128,512]{2,0,1:T(8,128)} %fusion.16, f32[8,128,512]{2,0,1:T(8,128)S(1)} %copy-done.11, f32[8,128,512]{2,0,1:T(8,128)} %fusion.20, f32[8,128,512]{2,0,1:T(8,128)} %fusion.22, f32[8,128,512]{2,0,1:T(8,128)} %fusion.24, f32[8,128,512]{2,0,1:T(8,128)} %fusion.26, ...), kind=kOutput, calls=%fused_computation.96 | convolution fusion | flops 155189248 | bytes 22021120 | tf_op jit(solution)/shard_map/ki,kaf->iaf/dot_general | solution.py:45
  456.0 7.5 reduce-scatter.3.cloned.1.call-done
  463.5 2.7 multiply_convert_fusion
  469.2 8.7 %all-gather.2.cloned.1.call-done = bf16[1024,512]{1,0:T(8,128)(2,1)} async-done(((bf16[512,512]{1,0:T(8,128)(2,1)}), bf16[1024,512]{1,0:T(8,128)(2,1)}) %all-gather.2.cloned.1.call-update) | async-done | bytes 1048592 | tf_op jit(solution)/shard_map/all_gather | solution.py:59
  477.8 3.8 gather_fusion.8
  481.6 5.8 fusion.46
  487.4 7.1 copy.27
  494.5 5.1 fusion.98
  501.0 2.5 gather_fusion.9
  503.5 5.9 fusion.44
  509.4 6.7 copy.28
  516.1 5.1 fusion.101
  521.5 2.5 gather_fusion.10
  524.0 5.9 fusion.42
  529.9 6.8 copy.29
  536.8 5.1 fusion.104
  545.6 5.9 fusion.40
  551.5 6.7 copy.30
  558.2 5.0 fusion.107
  567.0 5.9 fusion.38
  572.9 6.8 copy.31
  579.8 5.1 fusion.110
  588.7 6.0 fusion.36
  594.7 6.7 copy.32
  601.4 5.1 fusion.113
  610.3 5.9 fusion.34
  616.2 6.9 copy.33
  623.1 5.0 fusion.116
  631.9 5.9 fusion.32
  637.8 6.7 copy.34
  644.5 5.0 fusion.119
  657.5 179.1 %reduce-scatter.5.cloned.1.call-done = bf16[512,512]{1,0:T(8,128)(2,1)} async-done(((bf16[8192,512]{1,0:T(8,128)(2,1)}), bf16[512,512]{1,0:T(8,128)(2,1)}) %reduce-scatter.5.cloned.1.call-update) | async-done | bytes 524304 | tf_op jit(solution)/shard_map/reduce_scatter | solution.py:72
  (93 shorter events, 38.4 us)
Async XLA Ops:
  7.2 456.3 %copy-start = (bf16[512,512]{1,0:T(8,128)(2,1)S(1)}, bf16[512,512]{1,0:T(8,128)(2,1)}, u32[]{:S(2)}) copy-start(bf16[512,512]{1,0:T(8,128)(2,1)} %param.10) | copy-start | bytes 1572868
  7.2 273.1 %all-reduce.6.cloned.1.call-start = ((), (), s32[]{:S(2)}) async-start(), calls=%async_computation.6 | async-start | bytes 16777216 | tf_op jit(solution)/shard_map/psum | solution.py:9
  11.9 0.7 copy-start.18
  11.9 0.8 copy-start.21
  11.9 0.8 copy-start.19
  12.0 451.5 %reduce-scatter.3.cloned.1.call-start = ((), (), s32[]{:S(2)}) async-start(), calls=%async_computation.2 | async-start | bytes 1572864 | tf_op jit(solution)/shard_map/reduce_scatter | solution.py:49
  289.8 6.8 copy-start.10
  311.6 6.5 copy-start.3
  318.1 3.6 copy-start.9
  337.2 6.5 copy-start.8
  358.7 6.4 copy-start.7
  380.4 6.5 copy-start.6
  401.9 6.5 copy-start.5
  423.7 6.5 copy-start.4
  438.5 6.8 copy-start.11
  454.6 8.9 %copy-start.20 = (bf16[512,512]{1,0:T(8,128)(2,1)S(1)}, bf16[512,512]{1,0:T(8,128)(2,1)}, u32[]{:S(2)}) copy-start(bf16[512,512]{1,0:T(8,128)(2,1)} %param.15) | copy-start | bytes 1572868
  455.9 21.9 %all-gather.2.cloned.1.call-start = ((), (), s32[]{:S(2)}) async-start(), calls=%async_computation.3 | async-start | bytes 1572864 | tf_op jit(solution)/shard_map/all_gather | solution.py:59
  463.5 4.1 copy-start.17
  467.5 190.0 %all-reduce.4.cloned.1.call-start = ((), (), s32[]{:S(2)}) async-start(), calls=%async_computation.5 | async-start | bytes 2097152 | tf_op jit(solution)/shard_map/psum | solution.py:55
  469.1 367.5 %reduce-scatter.5.cloned.1.call-start = ((), (), s32[]{:S(2)}) async-start(), calls=%async_computation.4 | async-start | bytes 8912896 | tf_op jit(solution)/shard_map/reduce_scatter | solution.py:72
  499.6 1.4 copy-start.2
  649.5 1.4 copy-start.12
  649.6 2.4 copy-start.13
  649.9 3.2 copy-start.14
  650.9 3.2 copy-start.15
  652.0 3.2 copy-start.16
  657.4 181.4 %copy-start.1 = (bf16[512,512]{1,0:T(8,128)(2,1)S(1)}, bf16[512,512]{1,0:T(8,128)(2,1)}, u32[]{:S(2)}) copy-start(bf16[512,512]{1,0:T(8,128)(2,1)} %param.10) | copy-start | bytes 1572868
Sparse Core Ops, SparseCore 0:
  15.0 265.2 all-reduce.5
  456.0 7.3 reduce-scatter.2
  467.6 10.1 all-gather.1
  482.9 130.9 all-reduce.3
  657.6 178.9 reduce-scatter.4
where the time goes:
time: 857 us; the launch traced here: 846 us
  waiting for transfers between devices  463 us (54%)
  matrix products  192 us (22%)
  local copies, waits for them, and re-layouts  172 us (20%)
  between operations  14.6 us (2%)
    psum x1, waiting for transfers between devices, from_root(): return lax.psum(kept, axis)  267 us
    reduce_scatter x1, waiting for transfers between devices, shards(): lax.psum_scatter(stacked.astype(jnp.bfloat16), 'section', scatter_dimensi...  179 us
    dot_general x8, local copies, waits for them, and re-layouts, shards(): jnp.einsum('kab,kbf->kaf', tile_values[0, panel_pos], picked, preferred_e...  54.4 us
    dot_general x8, local copies, waits for them, and re-layouts, shards(): jnp.einsum('kab,kaf->kbf', tile_values[0, panel_pos], picked, preferred_e...  54.4 us
    dot_general x8, matrix products, shards(): jnp.einsum('ki,kaf->iaf', row_select[panel_pos], product, precision=lax.P...  51.6 us
    dot_general x8, matrix products, shards(): jnp.einsum('kab,kaf->kbf', tile_values[0, panel_pos], picked, preferred_e...  47.4 us
    dot_general x8, matrix products, shards(): jnp.einsum('kab,kbf->kaf', tile_values[0, panel_pos], picked, preferred_e...  46.7 us
    dot_general x8, matrix products, shards(): jnp.einsum('ki,kbf->ibf', col_select[panel_pos], product, precision=lax.P...  40.5 us
  transfers between devices with their start and end apart: 5, of which 4 were waited for; matrix products, arithmetic and copies ran while one was open for 21% of the time, Pallas kernels for 0%

commit v1 on v0

v1 whole, which is shorter than its diff:
```python
import functools

import jax
import jax.numpy as jnp
import numpy as np
from jax import lax
from jax.experimental import pallas as pl
from jax.experimental.pallas import tpu as pltpu
from jax.sharding import PartitionSpec as P

BF16 = jnp.bfloat16
F32 = jnp.float32
BOTH = ("section", "rep")


def dense_kernel(count_ref, rows_ref, cols_ref, tiles_ref, out_ref):
    panel = pl.program_id(0)
    size = tiles_ref.shape[-1]
    out_ref[...] = jnp.zeros_like(out_ref)

    def add_tile(slot, carry):
        row = pl.multiple_of(rows_ref[panel, slot] * size, size)
        col = pl.multiple_of(cols_ref[panel, slot] * size, size)
        out_ref[0, pl.ds(row, size), pl.ds(col, size)] += tiles_ref[0, slot]
        return carry

    lax.fori_loop(0, count_ref[panel], add_tile, 0)


def make_dense(tiles, rows, cols, count, block_rows):
    panels, slots, size, _ = tiles.shape
    return pl.pallas_call(
        dense_kernel,
        out_shape=jax.ShapeDtypeStruct((panels, block_rows, block_rows), BF16),
        grid_spec=pltpu.PrefetchScalarGridSpec(
            num_scalar_prefetch=3,
            grid=(panels,),
            in_specs=[pl.BlockSpec((1, slots, size, size), lambda p, *_: (p, 0, 0, 0))],
            out_specs=pl.BlockSpec((1, block_rows, block_rows), lambda p, *_: (p, 0, 0)),
        ),
        compiler_params=pltpu.CompilerParams(vmem_limit_bytes=32 * 2**20),
        cost_estimate=pl.CostEstimate(
            flops=0,
            transcendentals=0,
            bytes_accessed=tiles.size * 2 + panels * block_rows * block_rows * 2,
        ),
    )(count, rows, cols, tiles)


def forward_kernel(has_total, place_ref, *refs):
    if has_total:
        total_ref, a_ref, own_ref, x_ref, y_ref, da_ref, db_ref, out_ref = refs
    else:
        a_ref, own_ref, x_ref, y_ref, da_ref, db_ref, out_ref = refs
    step = pl.program_id(0)

    @pl.when(step == 0)
    def _():
        out_ref[...] = total_ref[...] if has_total else jnp.zeros_like(out_ref)

    live = place_ref[0] > 0

    def add(feat, columns):
        out_ref[...] += jnp.dot(a_ref[0, :, columns], feat, preferred_element_type=F32)

    whole = slice(None)
    half = da_ref.shape[0]

    @pl.when(live & (step == 0))
    def _():
        add(own_ref[...], whole)

    @pl.when(live & (step == 1))
    def _():
        add(x_ref[...], whole)

    @pl.when(live & (step == 2))
    def _():
        add(y_ref[...], whole)

    @pl.when(live & (step == 3))
    def _():
        add(da_ref[...], slice(0, half))
        add(db_ref[...], slice(half, 2 * half))


def forward_part(place, total, dense, own, x_side, y_side, diag_a, diag_b):
    rows, width = own.shape
    fixed = lambda shape: pl.BlockSpec(shape, lambda i, place: (0, 0))
    in_specs = [
        pl.BlockSpec((1, rows, rows), lambda i, place: (place[1 + i], 0, 0)),
        fixed((rows, width)),
        fixed((rows, width)),
        fixed((rows, width)),
        fixed((rows // 2, width)),
        fixed((rows // 2, width)),
    ]
    args = [dense, own, x_side, y_side, diag_a, diag_b]
    has_total = total is not None
    if has_total:
        in_specs = [fixed((rows, width))] + in_specs
        args = [total] + args
    return pl.pallas_call(
        functools.partial(forward_kernel, has_total),
        out_shape=jax.ShapeDtypeStruct((rows, width), F32),
        grid_spec=pltpu.PrefetchScalarGridSpec(
            num_scalar_prefetch=1,
            grid=(4,),
            in_specs=in_specs,
            out_specs=fixed((rows, width)),
        ),
        input_output_aliases={1: 0} if has_total else {},
        compiler_params=pltpu.CompilerParams(vmem_limit_bytes=48 * 2**20),
        cost_estimate=pl.CostEstimate(
            flops=8 * rows * rows * width,
            transcendentals=0,
            bytes_accessed=4 * rows * rows * 2 + 8 * rows * width * 2,
        ),
    )(place, *args)


def middle_kernel(place_ref, agg_ref, weight_ref, cot_ref, grad_ref, act_ref, agg_out, pre_out):
    agg = agg_ref[...].astype(BF16)
    pre = jnp.dot(agg, weight_ref[...], preferred_element_type=F32)
    sigma = jax.nn.sigmoid(pre)
    act_ref[...] = (pre * sigma).astype(BF16)
    slope = cot_ref[...].astype(F32) * sigma * (1.0 + pre * (1.0 - sigma))
    pre_grad = slope.astype(BF16)
    grad_ref[...] = lax.dot_general(
        weight_ref[...], pre_grad, (((1,), (1,)), ((), ())), preferred_element_type=F32
    ).astype(BF16)
    agg_out[...] = agg
    pre_out[...] = pre_grad


def middle(place, agg, weight, cotangent, n_rep):
    rows, width = agg.shape
    part = rows // n_rep
    block = lambda i, place: ((place[0] + 1 + i) % n_rep, 0)
    last = pl.BlockSpec((part, width), lambda i, place: (0, 0))
    own = jax.ShapeDtypeStruct((part, width), BF16)
    return pl.pallas_call(
        middle_kernel,
        out_shape=[jax.ShapeDtypeStruct((width, rows), BF16), own, own, own],
        grid_spec=pltpu.PrefetchScalarGridSpec(
            num_scalar_prefetch=1,
            grid=(n_rep,),
            in_specs=[
                pl.BlockSpec((part, width), block),
                pl.BlockSpec((width, width), lambda i, place: (0, 0)),
                pl.BlockSpec((part, width), block),
            ],
            out_specs=[
                pl.BlockSpec((width, part), lambda i, place: (0, block(i, place)[0])),
                last,
                last,
                last,
            ],
        ),
        compiler_params=pltpu.CompilerParams(vmem_limit_bytes=40 * 2**20),
        cost_estimate=pl.CostEstimate(
            flops=4 * rows * width * width,
            transcendentals=rows * width,
            bytes_accessed=rows * width * 10,
        ),
    )(place, agg, weight, cotangent)


def backward_kernel(place_ref, grad_ref, a_ref, x_ref, y_ref, xb_ref, ya_ref, own_ref):
    step = pl.program_id(0)
    half = xb_ref.shape[0]
    chunk = jnp.dot(grad_ref[...], a_ref[0], preferred_element_type=F32).astype(BF16)

    @pl.when(step == 0)
    def _():
        x_ref[0] = chunk[:half]
        y_ref[0] = chunk[half:]

    @pl.when(step == 1)
    def _():
        x_ref[1] = chunk[:half]
        xb_ref[...] = chunk[half:]

    @pl.when(step == 2)
    def _():
        y_ref[1] = chunk[half:]
        ya_ref[...] = chunk[:half]

    @pl.when(step == 3)
    def _():
        own_ref[...] = chunk


def backward_part(place, grad, dense, cols):
    width, rows = grad.shape
    per_panel = dense.shape[2] // cols
    half = width // 2
    pair = pl.BlockSpec((2, half, cols), lambda i, place: (0, 0, 0))
    single = pl.BlockSpec((half, cols), lambda i, place: (0, 0))
    return pl.pallas_call(
        backward_kernel,
        out_shape=[
            jax.ShapeDtypeStruct((2, half, cols), BF16),
            jax.ShapeDtypeStruct((2, half, cols), BF16),
            jax.ShapeDtypeStruct((half, cols), BF16),
            jax.ShapeDtypeStruct((half, cols), BF16),
            jax.ShapeDtypeStruct((width, cols), BF16),
        ],
        grid_spec=pltpu.PrefetchScalarGridSpec(
            num_scalar_prefetch=1,
            grid=(4,),
            in_specs=[
                pl.BlockSpec((width, rows), lambda i, place: (0, 0)),
                pl.BlockSpec(
                    (1, rows, cols),
                    lambda i, place: (place[i] // per_panel, 0, place[i] % per_panel),
                ),
            ],
            out_specs=[
                pair,
                pair,
                single,
                single,
                pl.BlockSpec((width, cols), lambda i, place: (0, 0)),
            ],
        ),
        compiler_params=pltpu.CompilerParams(vmem_limit_bytes=40 * 2**20),
        cost_estimate=pl.CostEstimate(
            flops=8 * rows * width * cols,
            transcendentals=0,
            bytes_accessed=8 * rows * cols + 8 * width * cols + 2 * width * rows,
        ),
    )(place, grad, dense)


class Places:
    def __init__(self, n_section, n_rep):
        self.n_section, self.n_rep = n_section, n_rep
        self.depth = n_section // 4
        self.span = self.depth // n_rep
        self.panels = n_section // n_rep

    def devices(self):
        for section in range(self.n_section):
            for rep in range(self.n_rep):
                yield section // 4, section // 2 % 2, section % 2, rep

    def flat(self, z, y, x, rep):
        return ((z * 2 + y) * 2 + x) * self.n_rep + rep

    def wants(self, z, rep):
        return rep * self.span <= z < (rep + 1) * self.span

    def heading(self, rep):
        return 1 if rep < self.n_rep / 2 else -1

    def flow(self, step, way):
        pairs = []
        for z, y, x, rep in self.devices():
            head = way * self.heading(rep)
            source = z - head * (step - 1)
            if 0 <= z + head < self.depth and self.wants(source, rep):
                pairs.append((self.flat(z, y, x, rep), self.flat(z + head, y, x, rep)))
        return pairs

    def source(self, step, z, rep):
        for source in sorted({z - step, z + step}):
            if 0 <= source < self.depth and self.wants(source, rep):
                return source
        return None

    def across(self, step, axis):
        return [
            (self.flat(z, y, x, rep), self.flat(z, y ^ (axis == "y"), x ^ (axis == "x"), rep))
            for z, y, x, rep in self.devices()
            if step is None or self.source(step, z, rep) is not None
        ]

    def order(self, z):
        near_end = z < self.depth / 2
        return sorted(
            range(self.depth), key=lambda d: (-abs(d - z), (d < z) if near_end else (d > z))
        )

    def up_dest(self, step, z):
        dest = self.depth - step + z
        return dest if z < dest < self.depth else None

    def down_dest(self, step, z):
        dest = z - self.depth + step
        return dest if 0 <= dest < z else None

    def table(self):
        rows = []
        for z, y, x, rep in self.devices():
            row = []
            for step in range(self.depth):
                source = self.source(step, z, rep)
                if source is None:
                    row += [0, 0, 0, 0, 0]
                else:
                    base = (source - rep * self.span) * 4
                    row += [1] + [base + 2 * b + a for b, a in ((y, x), (y, 1 - x), (1 - y, x), (1 - y, 1 - x))]
            for dest in self.order(z):
                row += [dest * 4 + 2 * b + a for b, a in ((1 - y, 1 - x), (y, 1 - x), (1 - y, x), (y, x))]
            rows.append(row)
        return np.array(rows, np.int32)


def shards(sizes, features, weight, tile_values, tile_rows, tile_cols, tile_count, cotangent):
    places = Places(*sizes)
    depth, n_rep = places.depth, places.n_rep
    block_rows, width = features.shape
    cols = block_rows * places.panels // places.n_section
    section, rep = lax.axis_index("section"), lax.axis_index("rep")
    z = section // 4
    table = lax.dynamic_index_in_dim(
        jnp.asarray(places.table()), section * n_rep + rep, keepdims=False
    )
    send = lambda value, pairs: lax.ppermute(value, BOTH, pairs)
    rep_pairs = lambda shift: [
        (places.flat(a, b, c, r), places.flat(a, b, c, (r + shift) % n_rep))
        for a, b, c, r in places.devices()
    ]

    arrivals = []
    major = minor = features
    for step in range(depth):
        if step == 0:
            arrived = features
        else:
            with jax.named_scope("features_along_z"):
                parts = []
                pairs = places.flow(step, 1)
                if pairs:
                    major = send(major, pairs)
                    parts.append(major)
                pairs = places.flow(step, -1)
                if pairs:
                    minor = send(minor, pairs)
                    parts.append(minor)
                arrived = functools.reduce(jnp.add, parts)
        with jax.named_scope("features_across"):
            to_x, to_y = places.across(step, "x"), places.across(step, "y")
            x_side, y_side = send(arrived, to_x), send(arrived, to_y)
            half = block_rows // 2
            diag_a = send(x_side[:half], to_y)
            diag_b = send(y_side[half:], to_x)
        arrivals.append((arrived, x_side, y_side, diag_a, diag_b))

    with jax.named_scope("cotangent_rows"):
        held = [send(cotangent, rep_pairs(-shift)) if shift else cotangent for shift in range(n_rep)]
        cot_rows = jnp.roll(jnp.stack(held), rep, axis=0).reshape(block_rows, width)

    with jax.named_scope("dense_blocks"):
        dense = make_dense(tile_values[0], tile_rows[0], tile_cols[0], tile_count[0], block_rows)

    total = None
    for step, arrival in enumerate(arrivals):
        with jax.named_scope("forward"):
            total = forward_part(table[5 * step : 5 * step + 5], total, dense, *arrival)

    with jax.named_scope("partial_sums"):
        shift = 1
        while shift < n_rep:
            sent = total.astype(BF16)
            pairs = [
                (places.flat(a, b, c, r), places.flat(a, b, c, r ^ shift))
                for a, b, c, r in places.devices()
            ]
            total = sent.astype(F32) + send(sent, pairs).astype(F32)
            shift *= 2

    with jax.named_scope("middle"):
        grad, activated, agg_own, pre_own = middle(rep[None], total, weight, cot_rows, n_rep)

    with jax.named_scope("weight_grad"):
        weight_grad = lax.psum(
            lax.dot_general(
                agg_own, pre_own, (((0,), (0,)), ((), ())), preferred_element_type=F32
            ),
            BOTH,
        )

    to_x, to_y = places.across(None, "x"), places.across(None, "y")
    sums = []
    up = down = None
    for turn in range(depth):
        with jax.named_scope("backward"):
            start = 5 * depth + 4 * turn
            x_pair, y_pair, x_b, y_a, own = backward_part(
                table[start : start + 4], grad, dense, cols
            )
        with jax.named_scope("grads_across"):
            from_x, from_y = send(x_pair, to_x), send(y_pair, to_y)
            x_b = (x_b.astype(F32) + from_y[0].astype(F32)).astype(BF16)
            y_a = (y_a.astype(F32) + from_x[0].astype(F32)).astype(BF16)
            last_x, last_y = send(x_b, to_x), send(y_a, to_y)
            own = own.reshape(2, width // 2, cols).astype(F32)
            summed = jnp.stack(
                [
                    own[0] + from_x[1].astype(F32) + last_y.astype(F32),
                    own[1] + from_y[1].astype(F32) + last_x.astype(F32),
                ]
            )
            sums.append(summed)
        step = turn + 1
        if step == depth:
            break
        with jax.named_scope("grads_along_z"):
            passed = []
            for dest_of, way, carried in (
                (places.up_dest, 1, up),
                (places.down_dest, -1, down),
            ):
                pairs, picks = [], {}
                for a, b, c, r in places.devices():
                    dest = dest_of(step, a)
                    if dest is not None:
                        pairs.append((places.flat(a, b, c, r), places.flat(a + way, b, c, r)))
                        picks[a] = places.order(a).index(dest)
                chosen = None
                for pick in sorted(set(picks.values())):
                    if chosen is None:
                        chosen = sums[pick]
                    else:
                        here = functools.reduce(
                            jnp.logical_or, [z == a for a in picks if picks[a] == pick]
                        )
                        chosen = jnp.where(here, sums[pick], chosen)
                if carried is not None:
                    chosen = chosen + carried.astype(F32)
                passed.append(send(chosen.astype(BF16), pairs))
            up, down = passed
    with jax.named_scope("grads_out"):
        final = sums[-1] + up.astype(F32) + down.astype(F32)
        feat_grad = final.reshape(width, cols).astype(BF16).T
    return (activated, feat_grad[None], weight_grad)


def solution(mesh):
    placed = (
        P("section", None),
        P(),
        P("section", "rep", None, None, None),
        P("section", "rep", None),
        P("section", "rep", None),
        P("section", "rep"),
        P(("section", "rep"), None),
    )
    sizes = (mesh.shape["section"], mesh.shape["rep"])
    return jax.shard_map(
        functools.partial(shards, sizes),
        mesh=mesh,
        in_specs=placed,
        out_specs=(P(("section", "rep"), None), P("rep", "section", None), P()),
        check_vma=False,
    )
```

time: 857 us -> 396 us (0.46); the launches traced: 846 us -> 395 us
  waiting for transfers between devices: 463 us -> 210 us
  matrix products: 192 us -> 1.43 us
  local copies, waits for them, and re-layouts: 172 us -> 15.6 us
  starting transfers between devices: 0.21 us -> 79.1 us
  Pallas kernels: 0 us -> 62.5 us
    dot_general x35 -> x1, matrix products: 192 us -> 1.43 us  [shards(): lax.dot_general(agg_own, pre_own, (((0,), (0,)), ((), ())), preferred_ele...]
    reduce_scatter x2 -> x0, waiting for transfers between devices: 187 us -> none  [the longest x1 179 us: shards(): lax.psum_scatter(stacked.astype(jnp.bfloat16), 'section', scatter_dimensi...]
    psum x2 -> x1, waiting for transfers between devices: 268 us -> 121 us  [shards(): lax.psum(lax.dot_general(agg_own, pre_own, (((0,), (0,)), ((), ())), pref...]
    dot_general x16 -> x0, local copies, waits for them, and re-layouts: 109 us -> none  [the longest x8 54.4 us: shards(): jnp.einsum('kab,kbf->kaf', tile_values[0, panel_pos], picked, preferred_e...]
    ppermute x0 -> x44, waiting for transfers between devices: none -> 89.4 us  [shards(): send = lambda value, pairs: lax.ppermute(value, BOTH, pairs)]
    ppermute x0 -> x44, starting transfers between devices: none -> 79 us  [shards(): send = lambda value, pairs: lax.ppermute(value, BOTH, pairs)]
    pallas_call x0 -> x10, Pallas kernels: none -> 62.5 us  [the longest x4 29.3 us: forward_part(): pl.pallas_call(functools.partial(forward_kernel, has_total), out_shape=ja...]
    gather x16 -> x0, local copies, waits for them, and re-layouts: 42.6 us -> none  [the longest x8 21.5 us: shards(): jnp.take(source.reshape(row_tiles, tile_size, feat_width), tile_cols[0, p...]
  transfers between devices with their start and end apart: 5 -> 45, of which waited for: 4 -> 16; matrix products, arithmetic and copies ran while one was open for 21% -> 4% of each run, Pallas kernels for 0% -> 12%
where the time goes in v1:
time: 396 us; the launch traced here: 395 us
  waiting for transfers between devices  210 us (53%)
  starting transfers between devices  79.1 us (20%)
  Pallas kernels  62.5 us (16%)
  local copies, waits for them, and re-layouts  15.6 us (4%)
  between operations  14.7 us (4%)
  other arithmetic  11.4 us (3%)
    psum x1, waiting for transfers between devices, shards(): lax.psum(lax.dot_general(agg_own, pre_own, (((0,), (0,)), ((), ())), pref...  121 us
    ppermute x44, waiting for transfers between devices, shards(): send = lambda value, pairs: lax.ppermute(value, BOTH, pairs)  89.4 us
    ppermute x44, starting transfers between devices, shards(): send = lambda value, pairs: lax.ppermute(value, BOTH, pairs)  79 us
    pallas_call x4, Pallas kernels, forward_part(): pl.pallas_call(functools.partial(forward_kernel, has_total), out_shape=ja...  29.3 us
    pallas_call x4, Pallas kernels, backward_part(): pl.pallas_call(backward_kernel, out_shape=[jax.ShapeDtypeStruct((2, half,...  22.3 us
    unnamed x31, local copies, waits for them, and re-layouts  9.54 us
    pallas_call x1, Pallas kernels, make_dense(): pl.pallas_call(dense_kernel, out_shape=jax.ShapeDtypeStruct((panels, bloc...  7.96 us
  transfers between devices with their start and end apart: 45, of which 16 were waited for; matrix products, arithmetic and copies ran while one was open for 4% of the time, Pallas kernels for 12%

profile of v1, /device:TPU:0, one launch (start us, length us, event | category | flops | bytes accessed | tf_op | source)
XLA Modules:
  0.0 394.7 jit_solution(7961136492633631872)
XLA Ops:
  7.2 5.0 %collective-permute-start.4 = (bf16[1024,512]{1,0:T(8,128)(2,1)}, bf16[1024,512]{1,0:T(8,128)(2,1)S(1)}, u32[]{:S(2)}, u32[]{:S(2)}) collective-permute-start(bf16[1024,512]{1,0:T(8,128)(2,1)} %refs_1_.1), channel_id=1, source_target_pairs={{0,8},{2,10},{4,12},{6,14},{8,16},{10,18},{12,20},{14,22},{17,9},{... | collective-permute-start | bytes 3145736 | tf_op jit(solution)/shard_map/features_along_z/ppermute | solution.py:320
  12.2 12.5 %collective-permute-done.4 = bf16[1024,512]{1,0:T(8,128)(2,1)S(1)} collective-permute-done((bf16[1024,512]{1,0:T(8,128)(2,1)}, bf16[1024,512]{1,0:T(8,128)(2,1)S(1)}, u32[]{:S(2)}, u32[]{:S(2)}) %collective-permute-start.4) | collective-permute-done | bytes 1048608 | tf_op jit(solution)/shard_map/features_along_z/ppermute | solution.py:320
  24.8 1.7 collective-permute-start.10
  26.4 3.4 collective-permute-start
  29.8 1.3 collective-permute-start.5
  31.1 3.4 collective-permute-start.1
  34.6 1.7 collective-permute-start.15
  36.2 7.1 %collective-permute-done.refs_2_ = bf16[1024,512]{1,0:T(8,128)(2,1)S(1)} collective-permute-done((bf16[1024,512]{1,0:T(8,128)(2,1)}, bf16[1024,512]{1,0:T(8,128)(2,1)S(1)}, u32[]{:S(2)}, u32[]{:S(2)}) %collective-permute-start) | collective-permute-done | bytes 1048608 | tf_op jit(solution)/shard_map/features_across/ppermute | solution.py:320
  43.4 3.6 collective-permute-start.2
  47.0 8.8 %collective-permute-done.5 = bf16[1024,512]{1,0:T(8,128)(2,1)S(1)} collective-permute-done((bf16[1024,512]{1,0:T(8,128)(2,1)}, bf16[1024,512]{1,0:T(8,128)(2,1)S(1)}, u32[]{:S(2)}, u32[]{:S(2)}) %collective-permute-start.5) | collective-permute-done | bytes 1048608 | tf_op jit(solution)/shard_map/features_along_z/ppermute | solution.py:320
  56.0 2.4 collective-permute-start.6
  58.5 3.4 collective-permute-start.7
  61.9 1.7 collective-permute-start.11
  64.4 1.7 collective-permute-start.12
  66.8 14.0 %collective-permute-done.6.refs_3_ = bf16[1024,512]{1,0:T(8,128)(2,1)S(1)} collective-permute-done((bf16[1024,512]{1,0:T(8,128)(2,1)S(1)}, bf16[1024,512]{1,0:T(8,128)(2,1)S(1)}, u32[]{:S(2)}, u32[]{:S(2)}) %collective-permute-start.6) | collective-permute-done | bytes 1048608 | tf_op jit(solution)/shard_map/features_across/ppermute | solution.py:320
  80.8 1.0 copy-done.1
  81.8 1.6 collective-permute-start.17
  84.2 1.0 copy-done.3
  85.2 1.0 copy-done.5
  86.2 3.9 collective-permute-start.3
  90.1 2.8 copy-done
  92.9 8.0 %dense_blocks.1.refs_0_.refs_1_.a_ref = bf16[8,1024,1024]{2,1,0:T(8,128)(2,1)} custom-call(s32[8]{0:T(128)S(1)} %bitcast.130, s32[8,24]{1,0:T(8,128)S(1)} %bitcast.128, s32[8,24]{1,0:T(8,128)S(1)} %bitcast.129, bf16[8,24,128,128]{3,2,1,0:T(8,128)(2,1)S(1)} %bitcast.126), custom_call_target="tpu_custom_call" | custom-call | bytes 23068672 | tf_op jit(solution)/shard_map/dense_blocks/pallas_call | solution.py:32
  101.7 3.7 collective-permute-start.8
  105.4 2.0 collective-permute-start.9
  107.4 1.1 slice.204
  108.5 1.1 slice.205
  111.1 9.2 %forward.4.refs_0_ = f32[1024,512]{1,0:T(8,128)} custom-call(s32[5]{0:T(128)S(1)} %get-tuple-element.67.place_ref, bf16[8,1024,1024]{2,1,0:T(8,128)(2,1)} %dense_blocks.1.refs_0_.refs_1_.a_ref, bf16[1024,512]{1,0:T(8,128)(2,1)S(1)} %copy-done.7, bf16[1024,512]{1,0:T(8,128)(2,1)S(1)} %collective-permute-done.refs_2_, bf16[1024,512]{1,0:T(8,128)(2,1)S(1)} %copy-done.4, ...), custom_call_target="tpu_custom_call" | custom-call | flops 4294967296 | bytes 16777216 | tf_op jit(solution)/shard_map/forward/pallas_call | solution.py:103
  121.0 1.1 slice.207
  123.0 9.7 %forward.5.refs_0_ = f32[1024,512]{1,0:T(8,128)} custom-call(s32[5]{0:T(128)S(1)} %get-tuple-element.68.place_ref, f32[1024,512]{1,0:T(8,128)} %forward.4.refs_0_, bf16[8,1024,1024]{2,1,0:T(8,128)(2,1)} %dense_blocks.1.refs_0_.refs_1_.a_ref, bf16[1024,512]{1,0:T(8,128)(2,1)S(1)} %add.118.refs_2_, ...), custom_call_target="tpu_custom_call", output_to_operand_aliasing={{}: (1, {})} | custom-call | flops 4294967296 | bytes 16777216 | tf_op jit(solution)/shard_map/forward/pallas_call | solution.py:103
  132.7 5.3 %forward.6.refs_0_ = f32[1024,512]{1,0:T(8,128)} custom-call(s32[5]{0:T(128)S(1)} %get-tuple-element.69.place_ref, f32[1024,512]{1,0:T(8,128)} %forward.5.refs_0_, bf16[8,1024,1024]{2,1,0:T(8,128)(2,1)} %dense_blocks.1.refs_0_.refs_1_.a_ref, bf16[1024,512]{1,0:T(8,128)(2,1)} %collective-permute-done.10.refs_2_, ...), custom_call_target="tpu_custom_call", output_to_operand_aliasing={{}: (1, {})} | custom-call | flops 4294967296 | bytes 16777216 | tf_op jit(solution)/shard_map/forward/pallas_call | solution.py:103
  138.0 5.0 %forward.7 = f32[1024,512]{1,0:T(8,128)} custom-call(s32[5]{0:T(128)S(1)} %get-tuple-element.70.place_ref, f32[1024,512]{1,0:T(8,128)} %forward.6.refs_0_, bf16[8,1024,1024]{2,1,0:T(8,128)(2,1)} %dense_blocks.1.refs_0_.refs_1_.a_ref, bf16[1024,512]{1,0:T(8,128)(2,1)} %collective-permute-done.15.refs_2_, ...), custom_call_target="tpu_custom_call", output_to_operand_aliasing={{}: (1, {})} | custom-call | flops 4294967296 | bytes 16777216 | tf_op jit(solution)/shard_map/forward/pallas_call | solution.py:103
  143.1 2.8 convert_element_type.233
  146.5 2.8 collective-permute-done.21
  149.3 2.1 fusion.2
  152.4 3.0 middle.1
  155.5 5.5 %backward.4 = (bf16[2,256,512]{2,1,0:T(8,128)(2,1)S(1)}, bf16[2,256,512]{2,1,0:T(8,128)(2,1)S(1)}, bf16[256,512]{1,0:T(8,128)(2,1)S(1)}, bf16[256,512]{1,0:T(8,128)(2,1)S(1)}, bf16[512,512]{1,0:T(8,128)(2,1)S(1)}) custom-call(s32[4]{0:T(128)S(1)} %get-tuple-element.66.place_ref, bf16[512,1024]{1,0:T(8,128)(2,1)S(1)} %get-tuple-element.28.grad_ref, ...), custom_call_target="tpu_custom_call" | custom-call | flops 2147483648 | bytes 7340032 | tf_op jit(solution)/shard_map/backward/pallas_call | solution.py:200
  161.1 2.1 collective-permute-start.22
  163.6 5.7 %backward.7 = (bf16[2,256,512]{2,1,0:T(8,128)(2,1)S(1)}, bf16[2,256,512]{2,1,0:T(8,128)(2,1)S(1)}, bf16[256,512]{1,0:T(8,128)(2,1)S(1)}, bf16[256,512]{1,0:T(8,128)(2,1)S(1)}, bf16[512,512]{1,0:T(8,128)(2,1)S(1)}) custom-call(s32[4]{0:T(128)S(1)} %get-tuple-element.64.place_ref, bf16[512,1024]{1,0:T(8,128)(2,1)S(1)} %get-tuple-element.28.grad_ref, ...), custom_call_target="tpu_custom_call" | custom-call | flops 2147483648 | bytes 7340032 | tf_op jit(solution)/shard_map/backward/pallas_call | solution.py:200
  169.6 1.6 collective-permute-start.36
  171.2 5.5 %backward.6 = (bf16[2,256,512]{2,1,0:T(8,128)(2,1)S(1)}, bf16[2,256,512]{2,1,0:T(8,128)(2,1)S(1)}, bf16[256,512]{1,0:T(8,128)(2,1)S(1)}, bf16[256,512]{1,0:T(8,128)(2,1)S(1)}, bf16[512,512]{1,0:T(8,128)(2,1)S(1)}) custom-call(s32[4]{0:T(128)S(1)} %get-tuple-element.65.place_ref, bf16[512,1024]{1,0:T(8,128)(2,1)S(1)} %get-tuple-element.28.grad_ref, ...), custom_call_target="tpu_custom_call" | custom-call | flops 2147483648 | bytes 7340032 | tf_op jit(solution)/shard_map/backward/pallas_call | solution.py:200
  176.9 2.0 collective-permute-start.30
  178.9 5.5 %backward.5 = (bf16[2,256,512]{2,1,0:T(8,128)(2,1)S(1)}, bf16[2,256,512]{2,1,0:T(8,128)(2,1)S(1)}, bf16[256,512]{1,0:T(8,128)(2,1)S(1)}, bf16[256,512]{1,0:T(8,128)(2,1)S(1)}, bf16[512,512]{1,0:T(8,128)(2,1)S(1)}) custom-call(s32[4]{0:T(128)S(1)} %get-tuple-element.63.place_ref, bf16[512,1024]{1,0:T(8,128)(2,1)S(1)} %get-tuple-element.28.grad_ref, ...), custom_call_target="tpu_custom_call" | custom-call | flops 2147483648 | bytes 7340032 | tf_op jit(solution)/shard_map/backward/pallas_call | solution.py:200
  185.1 2.1 collective-permute-done.34
  187.1 2.0 collective-permute-start.26
  189.7 8.6 %collective-permute-done.30 = bf16[2,256,512]{2,1,0:T(8,128)(2,1)S(1)} collective-permute-done((bf16[2,256,512]{2,1,0:T(8,128)(2,1)S(1)}, bf16[2,256,512]{2,1,0:T(8,128)(2,1)S(1)}, u32[]{:S(2)}, u32[]{:S(2)}) %collective-permute-start.30) | collective-permute-done | bytes 524320 | tf_op jit(solution)/shard_map/grads_across/ppermute | solution.py:320
  198.9 1.5 collective-permute-done.32
  201.0 8.6 %collective-permute-done.26 = bf16[2,256,512]{2,1,0:T(8,128)(2,1)S(1)} collective-permute-done((bf16[2,256,512]{2,1,0:T(8,128)(2,1)S(1)}, bf16[2,256,512]{2,1,0:T(8,128)(2,1)S(1)}, u32[]{:S(2)}, u32[]{:S(2)}) %collective-permute-start.26) | collective-permute-done | bytes 524320 | tf_op jit(solution)/shard_map/grads_across/ppermute | solution.py:320
  210.1 7.2 %collective-permute-done.35 = bf16[256,512]{1,0:T(8,128)(2,1)S(1)} collective-permute-done((bf16[256,512]{1,0:T(8,128)(2,1)S(1)}, bf16[256,512]{1,0:T(8,128)(2,1)S(1)}, u32[]{:S(2)}, u32[]{:S(2)}) %collective-permute-start.35) | collective-permute-done | bytes 262176 | tf_op jit(solution)/shard_map/grads_across/ppermute | solution.py:320
  217.6 4.7 %collective-permute-start.38 = (bf16[2,256,512]{2,1,0:T(8,128)(2,1)S(1)}, bf16[2,256,512]{2,1,0:T(8,128)(2,1)S(1)}, u32[]{:S(2)}, u32[]{:S(2)}) collective-permute-start(bf16[2,256,512]{2,1,0:T(8,128)(2,1)S(1)} %fusion.5), channel_id=1, source_target_pairs={{0,8},{1,9},{2,10},{3,11},{4,12},{5,13},{6,14},{7,15}} | collective-permute-start | bytes 1572872 | tf_op jit(solution)/shard_map/grads_along_z/ppermute | solution.py:320
  223.8 1.4 collective-permute-start.27
  225.4 6.3 %collective-permute-done.38 = bf16[2,256,512]{2,1,0:T(8,128)(2,1)S(1)} collective-permute-done((bf16[2,256,512]{2,1,0:T(8,128)(2,1)S(1)}, bf16[2,256,512]{2,1,0:T(8,128)(2,1)S(1)}, u32[]{:S(2)}, u32[]{:S(2)}) %collective-permute-start.38) | collective-permute-done | bytes 524320 | tf_op jit(solution)/shard_map/grads_along_z/ppermute | solution.py:320
  232.5 4.4 %collective-permute-start.39 = (bf16[2,256,512]{2,1,0:T(8,128)(2,1)S(1)}, bf16[2,256,512]{2,1,0:T(8,128)(2,1)S(1)}, u32[]{:S(2)}, u32[]{:S(2)}) collective-permute-start(bf16[2,256,512]{2,1,0:T(8,128)(2,1)S(1)} %get-tuple-element.53), channel_id=1, source_target_pairs={{0,8},{1,9},{2,10},{3,11},{4,12},{5,13},{6,14},{7,15},{8,16},{9,17... | collective-permute-start | bytes 1572872 | tf_op jit(solution)/shard_map/grads_along_z/ppermute | solution.py:320
  238.4 1.7 collective-permute-start.25
  240.3 4.9 %collective-permute-done.39 = bf16[2,256,512]{2,1,0:T(8,128)(2,1)S(1)} collective-permute-done((bf16[2,256,512]{2,1,0:T(8,128)(2,1)S(1)}, bf16[2,256,512]{2,1,0:T(8,128)(2,1)S(1)}, u32[]{:S(2)}, u32[]{:S(2)}) %collective-permute-start.39) | collective-permute-done | bytes 524320 | tf_op jit(solution)/shard_map/grads_along_z/ppermute | solution.py:320
  245.6 1.3 collective-permute-start.43
  246.9 8.3 %collective-permute-start.40 = (bf16[2,256,512]{2,1,0:T(8,128)(2,1)S(1)}, bf16[2,256,512]{2,1,0:T(8,128)(2,1)}, u32[]{:S(2)}, u32[]{:S(2)}) collective-permute-start(bf16[2,256,512]{2,1,0:T(8,128)(2,1)S(1)} %get-tuple-element.51), channel_id=1, source_target_pairs={{0,8},{1,9},{2,10},{3,11},{4,12},{5,13},{6,14},{7,15},{8,16},{9,17... | collective-permute-start | bytes 1572872 | tf_op jit(solution)/shard_map/grads_along_z/ppermute | solution.py:320
  255.2 1.4 fusion.30
  256.7 1.2 fusion.21
  258.0 2.9 collective-permute-done.43
  260.9 1.8 collective-permute-done.40
  262.6 1.4 fusion.4
  264.1 1.0 copy.14
  265.1 120.6 %all-reduce.2.cloned.1.call-done = f32[512,512]{1,0:T(8,128)} async-done(((f32[512,512]{1,0:T(8,128)}), f32[512,512]{1,0:T(8,128)}) %all-reduce.2.cloned.1.call-update) | async-done | bytes 1048592 | tf_op jit(solution)/shard_map/weight_grad/psum | solution.py:378
  385.6 2.3 copy.19
  (105 shorter events, 16.8 us)
Async XLA Ops:
  7.2 378.4 %all-reduce.2.cloned.1.call-start = ((), (), s32[]{:S(2)}) async-start(), calls=%async_computation | async-start | bytes 2097152 | tf_op jit(solution)/shard_map/weight_grad/psum | solution.py:378
  7.2 17.6 %collective-permute-start.4 = (bf16[1024,512]{1,0:T(8,128)(2,1)}, bf16[1024,512]{1,0:T(8,128)(2,1)S(1)}, u32[]{:S(2)}, u32[]{:S(2)}) collective-permute-start(bf16[1024,512]{1,0:T(8,128)(2,1)} %refs_1_.1), channel_id=1, source_target_pairs={{0,8},{2,10},{4,12},{6,14},{8,16},{10,18},{12,20},{14,22},{17,9},{... | collective-permute-start | bytes 3145736 | tf_op jit(solution)/shard_map/features_along_z/ppermute | solution.py:320
  24.8 9.8 %collective-permute-start.10 = (bf16[1024,512]{1,0:T(8,128)(2,1)S(1)}, bf16[1024,512]{1,0:T(8,128)(2,1)}, u32[]{:S(2)}, u32[]{:S(2)}) collective-permute-start(bf16[1024,512]{1,0:T(8,128)(2,1)S(1)} %collective-permute-done.4), channel_id=1, source_target_pairs={{8,16},{9,1},{10,18},{11,3},{12,20},{13,5},{14,22},{15,7},{16,24},... | collective-permute-start | bytes 3145736 | tf_op jit(solution)/shard_map/features_along_z/ppermute | solution.py:320
  26.4 16.9 %collective-permute-start = (bf16[1024,512]{1,0:T(8,128)(2,1)}, bf16[1024,512]{1,0:T(8,128)(2,1)S(1)}, u32[]{:S(2)}, u32[]{:S(2)}) collective-permute-start(bf16[1024,512]{1,0:T(8,128)(2,1)} %refs_1_.1), channel_id=1, source_target_pairs={{0,2},{2,0},{4,6},{6,4},{8,10},{10,8},{12,14},{14,12},{17,19},{19,... | collective-permute-start | bytes 3145736 | tf_op jit(solution)/shard_map/features_across/ppermute | solution.py:320
  29.8 25.9 %collective-permute-start.5 = (bf16[1024,512]{1,0:T(8,128)(2,1)}, bf16[1024,512]{1,0:T(8,128)(2,1)S(1)}, u32[]{:S(2)}, u32[]{:S(2)}) collective-permute-start(bf16[1024,512]{1,0:T(8,128)(2,1)} %refs_1_.1), channel_id=1, source_target_pairs={{8,0},{10,2},{12,4},{14,6},{17,25},{19,27},{21,29},{23,31}} | collective-permute-start | bytes 3145736 | tf_op jit(solution)/shard_map/features_along_z/ppermute | solution.py:320
  31.1 30.8 %collective-permute-start.1 = (bf16[1024,512]{1,0:T(8,128)(2,1)}, bf16[1024,512]{1,0:T(8,128)(2,1)S(1)}, u32[]{:S(2)}, u32[]{:S(2)}) collective-permute-start(bf16[1024,512]{1,0:T(8,128)(2,1)} %refs_1_.1), channel_id=1, source_target_pairs={{0,4},{2,6},{4,0},{6,2},{8,12},{10,14},{12,8},{14,10},{17,21},{19,... | collective-permute-start | bytes 3145736 | tf_op jit(solution)/shard_map/features_across/ppermute | solution.py:320
  34.6 31.5 %collective-permute-start.15 = (bf16[1024,512]{1,0:T(8,128)(2,1)}, bf16[1024,512]{1,0:T(8,128)(2,1)}, u32[]{:S(2)}, u32[]{:S(2)}) collective-permute-start(bf16[1024,512]{1,0:T(8,128)(2,1)} %collective-permute-done.10.refs_2_), channel_id=1, source_target_pairs={{9,1},{11,3},{13,5},{15,7},{16,24},{18,26},{20,28},{22,30}} | collective-permute-start | bytes 3145736 | tf_op jit(solution)/shard_map/features_along_z/ppermute | solution.py:320
  43.4 46.7 %copy-start.10 = (s32[1,8,24]{2,1,0:T(8,128)S(1)}, s32[1,8,24]{2,1,0:T(8,128)}, u32[]{:S(2)}) copy-start(s32[1,8,24]{2,1,0:T(8,128)} %param.11) | copy-start | bytes 2308
  43.4 46.7 %copy-start.11 = (s32[1,8,24]{2,1,0:T(8,128)S(1)}, s32[1,8,24]{2,1,0:T(8,128)}, u32[]{:S(2)}) copy-start(s32[1,8,24]{2,1,0:T(8,128)} %param.12) | copy-start | bytes 2308
  43.4 46.7 %copy-start.12 = (s32[1,8]{1,0:T(1,128)S(1)}, s32[1,8]{1,0:T(1,128)}, u32[]{:S(2)}) copy-start(s32[1,8]{1,0:T(1,128)} %param.13) | copy-start | bytes 100
  43.4 20.2 %collective-permute-start.2 = (bf16[512,512]{1,0:T(8,128)(2,1)S(1)}, bf16[512,512]{1,0:T(8,128)(2,1)S(1)}, u32[]{:S(2)}, u32[]{:S(2)}) collective-permute-start(bf16[512,512]{1,0:T(8,128)(2,1)S(1)} %slice.200), channel_id=1, source_target_pairs={{0,4},{2,6},{4,0},{6,2},{8,12},{10,14},{12,8},{14,10},{17,21},{19,... | collective-permute-start | bytes 1572872 | tf_op jit(solution)/shard_map/features_across/ppermute | solution.py:320
  56.0 24.7 %collective-permute-start.6 = (bf16[1024,512]{1,0:T(8,128)(2,1)S(1)}, bf16[1024,512]{1,0:T(8,128)(2,1)S(1)}, u32[]{:S(2)}, u32[]{:S(2)}) collective-permute-start(bf16[1024,512]{1,0:T(8,128)(2,1)S(1)} %add.118.refs_2_), channel_id=1, source_target_pairs={{0,2},{2,0},{4,6},{6,4},{8,10},{9,11},{10,8},{11,9},{12,14},{13,15... | collective-permute-start | bytes 3145736 | tf_op jit(solution)/shard_map/features_across/ppermute | solution.py:320
  58.5 26.7 %collective-permute-start.7 = (bf16[1024,512]{1,0:T(8,128)(2,1)S(1)}, bf16[1024,512]{1,0:T(8,128)(2,1)S(1)}, u32[]{:S(2)}, u32[]{:S(2)}) collective-permute-start(bf16[1024,512]{1,0:T(8,128)(2,1)S(1)} %add.118.refs_2_), channel_id=1, source_target_pairs={{0,4},{2,6},{4,0},{6,2},{8,12},{9,13},{10,14},{11,15},{12,8},{13,9... | collective-permute-start | bytes 3145736 | tf_op jit(solution)/shard_map/features_across/ppermute | solution.py:320
  61.9 39.8 %collective-permute-start.11 = (bf16[1024,512]{1,0:T(8,128)(2,1)}, bf16[1024,512]{1,0:T(8,128)(2,1)}, u32[]{:S(2)}, u32[]{:S(2)}) collective-permute-start(bf16[1024,512]{1,0:T(8,128)(2,1)} %collective-permute-done.10.refs_2_), channel_id=1, source_target_pairs={{1,3},{3,1},{5,7},{7,5},{9,11},{11,9},{13,15},{15,13},{16,18},{18,... | collective-permute-start | bytes 3145736 | tf_op jit(solution)/shard_map/features_across/ppermute | solution.py:320
  63.6 0.8 copy-start.8
  64.4 41.0 %collective-permute-start.12 = (bf16[1024,512]{1,0:T(8,128)(2,1)}, bf16[1024,512]{1,0:T(8,128)(2,1)}, u32[]{:S(2)}, u32[]{:S(2)}) collective-permute-start(bf16[1024,512]{1,0:T(8,128)(2,1)} %collective-permute-done.10.refs_2_), channel_id=1, source_target_pairs={{1,5},{3,7},{5,1},{7,3},{9,13},{11,15},{13,9},{15,11},{16,20},{18,... | collective-permute-start | bytes 3145736 | tf_op jit(solution)/shard_map/features_across/ppermute | solution.py:320
  66.1 44.3 %collective-permute-start.16 = (bf16[1024,512]{1,0:T(8,128)(2,1)}, bf16[1024,512]{1,0:T(8,128)(2,1)S(1)}, u32[]{:S(2)}, u32[]{:S(2)}) collective-permute-start(bf16[1024,512]{1,0:T(8,128)(2,1)} %collective-permute-done.15.refs_2_), channel_id=1, source_target_pairs={{1,3},{3,1},{5,7},{7,5},{24,26},{26,24},{28,30},{30,28}} | collective-permute-start | bytes 3145736 | tf_op jit(solution)/shard_map/features_across/ppermute | solution.py:320
  80.8 1.0 copy-start.1
  81.8 38.5 %collective-permute-start.17 = (bf16[1024,512]{1,0:T(8,128)(2,1)}, bf16[1024,512]{1,0:T(8,128)(2,1)}, u32[]{:S(2)}, u32[]{:S(2)}) collective-permute-start(bf16[1024,512]{1,0:T(8,128)(2,1)} %collective-permute-done.15.refs_2_), channel_id=1, source_target_pairs={{1,5},{3,7},{5,1},{7,3},{24,28},{26,30},{28,24},{30,26}} | collective-permute-start | bytes 3145736 | tf_op jit(solution)/shard_map/features_across/ppermute | solution.py:320
  84.2 1.0 copy-start.3
  85.2 1.0 copy-start.5
  86.2 23.4 %collective-permute-start.3 = (bf16[512,512]{1,0:T(8,128)(2,1)}, bf16[512,512]{1,0:T(8,128)(2,1)}, u32[]{:S(2)}, u32[]{:S(2)}) collective-permute-start(bf16[512,512]{1,0:T(8,128)(2,1)} %slice.201), channel_id=1, source_target_pairs={{0,2},{2,0},{4,6},{6,4},{8,10},{10,8},{12,14},{14,12},{17,19},{19,... | collective-permute-start | bytes 1572872 | tf_op jit(solution)/shard_map/features_across/ppermute | solution.py:320
  90.1 2.8 copy-start
  92.9 8.7 %copy-start.2 = (bf16[1024,512]{1,0:T(8,128)(2,1)S(1)}, bf16[1024,512]{1,0:T(8,128)(2,1)}, u32[]{:S(2)}) copy-start(bf16[1024,512]{1,0:T(8,128)(2,1)} %copy-done.1) | copy-start | bytes 3145732
  92.9 8.7 %copy-start.6 = (bf16[1024,512]{1,0:T(8,128)(2,1)S(1)}, bf16[1024,512]{1,0:T(8,128)(2,1)}, u32[]{:S(2)}) copy-start(bf16[1024,512]{1,0:T(8,128)(2,1)} %copy-done.5) | copy-start | bytes 3145732
  101.6 9.5 %copy-start.4 = (bf16[1024,512]{1,0:T(8,128)(2,1)S(1)}, bf16[1024,512]{1,0:T(8,128)(2,1)}, u32[]{:S(2)}) copy-start(bf16[1024,512]{1,0:T(8,128)(2,1)} %copy-done.3) | copy-start | bytes 3145732
  101.6 9.5 %copy-start.7 = (bf16[1024,512]{1,0:T(8,128)(2,1)S(1)}, bf16[1024,512]{1,0:T(8,128)(2,1)}, u32[]{:S(2)}) copy-start(bf16[1024,512]{1,0:T(8,128)(2,1)} %refs_1_.1) | copy-start | bytes 3145732
  101.6 9.5 %copy-start.9 = (bf16[512,512]{1,0:T(8,128)(2,1)S(1)}, bf16[512,512]{1,0:T(8,128)(2,1)}, u32[]{:S(2)}) copy-start(bf16[512,512]{1,0:T(8,128)(2,1)} %copy-done.8) | copy-start | bytes 1572868
  101.7 20.4 %collective-permute-start.8 = (bf16[512,512]{1,0:T(8,128)(2,1)S(1)}, bf16[512,512]{1,0:T(8,128)(2,1)S(1)}, u32[]{:S(2)}, u32[]{:S(2)}) collective-permute-start(bf16[512,512]{1,0:T(8,128)(2,1)S(1)} %slice.202), channel_id=1, source_target_pairs={{0,4},{2,6},{4,0},{6,2},{8,12},{9,13},{10,14},{11,15},{12,8},{13,9... | collective-permute-start | bytes 1572872 | tf_op jit(solution)/shard_map/features_across/ppermute | solution.py:320
  105.4 17.6 %collective-permute-start.9 = (bf16[512,512]{1,0:T(8,128)(2,1)S(1)}, bf16[512,512]{1,0:T(8,128)(2,1)S(1)}, u32[]{:S(2)}, u32[]{:S(2)}) collective-permute-start(bf16[512,512]{1,0:T(8,128)(2,1)S(1)} %slice.203), channel_id=1, source_target_pairs={{0,2},{2,0},{4,6},{6,4},{8,10},{9,11},{10,8},{11,9},{12,14},{13,15... | collective-permute-start | bytes 1572872 | tf_op jit(solution)/shard_map/features_across/ppermute | solution.py:320
  109.6 23.1 %collective-permute-start.13 = (bf16[512,512]{1,0:T(8,128)(2,1)S(1)}, bf16[512,512]{1,0:T(8,128)(2,1)S(1)}, u32[]{:S(2)}, u32[]{:S(2)}) collective-permute-start(bf16[512,512]{1,0:T(8,128)(2,1)S(1)} %slice.204), channel_id=1, source_target_pairs={{1,5},{3,7},{5,1},{7,3},{9,13},{11,15},{13,9},{15,11},{16,20},{18,... | collective-permute-start | bytes 1572872 | tf_op jit(solution)/shard_map/features_across/ppermute | solution.py:320
  110.3 22.4 %collective-permute-start.14 = (bf16[512,512]{1,0:T(8,128)(2,1)S(1)}, bf16[512,512]{1,0:T(8,128)(2,1)S(1)}, u32[]{:S(2)}, u32[]{:S(2)}) collective-permute-start(bf16[512,512]{1,0:T(8,128)(2,1)S(1)} %slice.205), channel_id=1, source_target_pairs={{1,3},{3,1},{5,7},{7,5},{9,11},{11,9},{13,15},{15,13},{16,18},{18,... | collective-permute-start | bytes 1572872 | tf_op jit(solution)/shard_map/features_across/ppermute | solution.py:320
  120.3 17.7 %collective-permute-start.18 = (bf16[512,512]{1,0:T(8,128)(2,1)S(1)}, bf16[512,512]{1,0:T(8,128)(2,1)S(1)}, u32[]{:S(2)}, u32[]{:S(2)}) collective-permute-start(bf16[512,512]{1,0:T(8,128)(2,1)S(1)} %slice.206), channel_id=1, source_target_pairs={{1,5},{3,7},{5,1},{7,3},{24,28},{26,30},{28,24},{30,26}} | collective-permute-start | bytes 1572872 | tf_op jit(solution)/shard_map/features_across/ppermute | solution.py:320
  122.1 15.9 %collective-permute-start.19 = (bf16[512,512]{1,0:T(8,128)(2,1)S(1)}, bf16[512,512]{1,0:T(8,128)(2,1)S(1)}, u32[]{:S(2)}, u32[]{:S(2)}) collective-permute-start(bf16[512,512]{1,0:T(8,128)(2,1)S(1)} %slice.207), channel_id=1, source_target_pairs={{1,3},{3,1},{5,7},{7,5},{24,26},{26,24},{28,30},{30,28}} | collective-permute-start | bytes 1572872 | tf_op jit(solution)/shard_map/features_across/ppermute | solution.py:320
  143.1 8.3 %copy-start.14 = (f32[1024,512]{1,0:T(8,128)S(1)}, f32[1024,512]{1,0:T(8,128)}, u32[]{:S(2)}) copy-start(f32[1024,512]{1,0:T(8,128)} %forward.7) | copy-start | bytes 6291460
  145.9 5.5 %collective-permute-start.20 = (bf16[1024,512]{1,0:T(8,128)(2,1)}, bf16[1024,512]{1,0:T(8,128)(2,1)S(1)}, u32[]{:S(2)}, u32[]{:S(2)}) collective-permute-start(bf16[1024,512]{1,0:T(8,128)(2,1)} %convert_element_type.233), channel_id=1, source_target_pairs={{0,1},{1,0},{2,3},{3,2},{4,5},{5,4},{6,7},{7,6},{8,9},{9,8},{10,11... | collective-permute-start | bytes 3145736 | tf_op jit(solution)/shard_map/partial_sums/ppermute | solution.py:320
  145.9 3.4 collective-permute-start.21
  151.4 1.0 copy-start.13
  161.1 23.4 %collective-permute-start.22 = (bf16[2,256,512]{2,1,0:T(8,128)(2,1)S(1)}, bf16[2,256,512]{2,1,0:T(8,128)(2,1)S(1)}, u32[]{:S(2)}, u32[]{:S(2)}) collective-permute-start(bf16[2,256,512]{2,1,0:T(8,128)(2,1)S(1)} %get-tuple-element.30), channel_id=1, source_target_pairs={{0,2},{1,3},{2,0},{3,1},{4,6},{5,7},{6,4},{7,5},{8,10},{9,11},{10,... | collective-permute-start | bytes 1572872 | tf_op jit(solution)/shard_map/grads_across/ppermute | solution.py:320
  163.2 73.7 %collective-permute-start.24 = (bf16[2,256,512]{2,1,0:T(8,128)(2,1)S(1)}, bf16[2,256,512]{2,1,0:T(8,128)(2,1)S(1)}, u32[]{:S(2)}, u32[]{:S(2)}) collective-permute-start(bf16[2,256,512]{2,1,0:T(8,128)(2,1)S(1)} %get-tuple-element.32), channel_id=1, source_target_pairs={{0,4},{1,5},{2,6},{3,7},{4,0},{5,1},{6,2},{7,3},{8,12},{9,13},{10,... | collective-permute-start | bytes 1572872 | tf_op jit(solution)/shard_map/grads_across/ppermute | solution.py:320
  169.4 17.7 %collective-permute-start.34 = (bf16[2,256,512]{2,1,0:T(8,128)(2,1)S(1)}, bf16[2,256,512]{2,1,0:T(8,128)(2,1)S(1)}, u32[]{:S(2)}, u32[]{:S(2)}) collective-permute-start(bf16[2,256,512]{2,1,0:T(8,128)(2,1)S(1)} %get-tuple-element.45), channel_id=1, source_target_pairs={{0,2},{1,3},{2,0},{3,1},{4,6},{5,7},{6,4},{7,5},{8,10},{9,11},{10,... | collective-permute-start | bytes 1572872 | tf_op jit(solution)/shard_map/grads_across/ppermute | solution.py:320
  169.6 19.6 %collective-permute-start.36 = (bf16[2,256,512]{2,1,0:T(8,128)(2,1)S(1)}, bf16[2,256,512]{2,1,0:T(8,128)(2,1)S(1)}, u32[]{:S(2)}, u32[]{:S(2)}) collective-permute-start(bf16[2,256,512]{2,1,0:T(8,128)(2,1)S(1)} %get-tuple-element.47), channel_id=1, source_target_pairs={{0,4},{1,5},{2,6},{3,7},{4,0},{5,1},{6,2},{7,3},{8,12},{9,13},{10,... | collective-permute-start | bytes 1572872 | tf_op jit(solution)/shard_map/grads_across/ppermute | solution.py:320
  176.9 21.5 %collective-permute-start.30 = (bf16[2,256,512]{2,1,0:T(8,128)(2,1)S(1)}, bf16[2,256,512]{2,1,0:T(8,128)(2,1)S(1)}, u32[]{:S(2)}, u32[]{:S(2)}) collective-permute-start(bf16[2,256,512]{2,1,0:T(8,128)(2,1)S(1)} %get-tuple-element.40), channel_id=1, source_target_pairs={{0,2},{1,3},{2,0},{3,1},{4,6},{5,7},{6,4},{7,5},{8,10},{9,11},{10,... | collective-permute-start | bytes 1572872 | tf_op jit(solution)/shard_map/grads_across/ppermute | solution.py:320
  184.5 15.9 %collective-permute-start.32 = (bf16[2,256,512]{2,1,0:T(8,128)(2,1)S(1)}, bf16[2,256,512]{2,1,0:T(8,128)(2,1)S(1)}, u32[]{:S(2)}, u32[]{:S(2)}) collective-permute-start(bf16[2,256,512]{2,1,0:T(8,128)(2,1)S(1)} %get-tuple-element.42), channel_id=1, source_target_pairs={{0,4},{1,5},{2,6},{3,7},{4,0},{5,1},{6,2},{7,3},{8,12},{9,13},{10,... | collective-permute-start | bytes 1572872 | tf_op jit(solution)/shard_map/grads_across/ppermute | solution.py:320
  187.1 22.5 %collective-permute-start.26 = (bf16[2,256,512]{2,1,0:T(8,128)(2,1)S(1)}, bf16[2,256,512]{2,1,0:T(8,128)(2,1)S(1)}, u32[]{:S(2)}, u32[]{:S(2)}) collective-permute-start(bf16[2,256,512]{2,1,0:T(8,128)(2,1)S(1)} %get-tuple-element.35), channel_id=1, source_target_pairs={{0,2},{1,3},{2,0},{3,1},{4,6},{5,7},{6,4},{7,5},{8,10},{9,11},{10,... | collective-permute-start | bytes 1572872 | tf_op jit(solution)/shard_map/grads_across/ppermute | solution.py:320
  189.2 33.1 %collective-permute-start.28 = (bf16[2,256,512]{2,1,0:T(8,128)(2,1)S(1)}, bf16[2,256,512]{2,1,0:T(8,128)(2,1)S(1)}, u32[]{:S(2)}, u32[]{:S(2)}) collective-permute-start(bf16[2,256,512]{2,1,0:T(8,128)(2,1)S(1)} %get-tuple-element.37), channel_id=1, source_target_pairs={{0,4},{1,5},{2,6},{3,7},{4,0},{5,1},{6,2},{7,3},{8,12},{9,13},{10,... | collective-permute-start | bytes 1572872 | tf_op jit(solution)/shard_map/grads_across/ppermute | solution.py:320
  198.4 18.9 %collective-permute-start.35 = (bf16[256,512]{1,0:T(8,128)(2,1)S(1)}, bf16[256,512]{1,0:T(8,128)(2,1)S(1)}, u32[]{:S(2)}, u32[]{:S(2)}) collective-permute-start(bf16[256,512]{1,0:T(8,128)(2,1)S(1)} %fusion.23), channel_id=1, source_target_pairs={{0,4},{1,5},{2,6},{3,7},{4,0},{5,1},{6,2},{7,3},{8,12},{9,13},{10,... | collective-permute-start | bytes 786440 | tf_op jit(solution)/shard_map/grads_across/ppermute | solution.py:320
  200.4 16.9 %collective-permute-start.37 = (bf16[256,512]{1,0:T(8,128)(2,1)S(1)}, bf16[256,512]{1,0:T(8,128)(2,1)S(1)}, u32[]{:S(2)}, u32[]{:S(2)}) collective-permute-start(bf16[256,512]{1,0:T(8,128)(2,1)S(1)} %fusion.22), channel_id=1, source_target_pairs={{0,2},{1,3},{2,0},{3,1},{4,6},{5,7},{6,4},{7,5},{8,10},{9,11},{10,... | collective-permute-start | bytes 786440 | tf_op jit(solution)/shard_map/grads_across/ppermute | solution.py:320
  209.6 13.5 %collective-permute-start.31 = (bf16[256,512]{1,0:T(8,128)(2,1)S(1)}, bf16[256,512]{1,0:T(8,128)(2,1)S(1)}, u32[]{:S(2)}, u32[]{:S(2)}) collective-permute-start(bf16[256,512]{1,0:T(8,128)(2,1)S(1)} %fusion.25), channel_id=1, source_target_pairs={{0,4},{1,5},{2,6},{3,7},{4,0},{5,1},{6,2},{7,3},{8,12},{9,13},{10,... | collective-permute-start | bytes 786440 | tf_op jit(solution)/shard_map/grads_across/ppermute | solution.py:320
  217.3 6.6 %collective-permute-start.33 = (bf16[256,512]{1,0:T(8,128)(2,1)S(1)}, bf16[256,512]{1,0:T(8,128)(2,1)S(1)}, u32[]{:S(2)}, u32[]{:S(2)}) collective-permute-start(bf16[256,512]{1,0:T(8,128)(2,1)S(1)} %fusion.24), channel_id=1, source_target_pairs={{0,2},{1,3},{2,0},{3,1},{4,6},{5,7},{6,4},{7,5},{8,10},{9,11},{10,... | collective-permute-start | bytes 786440 | tf_op jit(solution)/shard_map/grads_across/ppermute | solution.py:320
  217.6 14.1 %collective-permute-start.38 = (bf16[2,256,512]{2,1,0:T(8,128)(2,1)S(1)}, bf16[2,256,512]{2,1,0:T(8,128)(2,1)S(1)}, u32[]{:S(2)}, u32[]{:S(2)}) collective-permute-start(bf16[2,256,512]{2,1,0:T(8,128)(2,1)S(1)} %fusion.5), channel_id=1, source_target_pairs={{0,8},{1,9},{2,10},{3,11},{4,12},{5,13},{6,14},{7,15}} | collective-permute-start | bytes 1572872 | tf_op jit(solution)/shard_map/grads_along_z/ppermute | solution.py:320
  222.3 9.8 %collective-permute-start.41 = (bf16[2,256,512]{2,1,0:T(8,128)(2,1)S(1)}, bf16[2,256,512]{2,1,0:T(8,128)(2,1)S(1)}, u32[]{:S(2)}, u32[]{:S(2)}) collective-permute-start(bf16[2,256,512]{2,1,0:T(8,128)(2,1)S(1)} %fusion.5), channel_id=1, source_target_pairs={{24,16},{25,17},{26,18},{27,19},{28,20},{29,21},{30,22},{31,23}} | collective-permute-start | bytes 1572872 | tf_op jit(solution)/shard_map/grads_along_z/ppermute | solution.py:320
  223.1 33.6 %collective-permute-start.23 = (bf16[256,512]{1,0:T(8,128)(2,1)S(1)}, bf16[256,512]{1,0:T(8,128)(2,1)}, u32[]{:S(2)}, u32[]{:S(2)}) collective-permute-start(bf16[256,512]{1,0:T(8,128)(2,1)S(1)} %fusion.29), channel_id=1, source_target_pairs={{0,4},{1,5},{2,6},{3,7},{4,0},{5,1},{6,2},{7,3},{8,12},{9,13},{10,... | collective-permute-start | bytes 786440 | tf_op jit(solution)/shard_map/grads_across/ppermute | solution.py:320
  223.8 14.5 %collective-permute-start.27 = (bf16[256,512]{1,0:T(8,128)(2,1)S(1)}, bf16[256,512]{1,0:T(8,128)(2,1)S(1)}, u32[]{:S(2)}, u32[]{:S(2)}) collective-permute-start(bf16[256,512]{1,0:T(8,128)(2,1)S(1)} %fusion.27), channel_id=1, source_target_pairs={{0,4},{1,5},{2,6},{3,7},{4,0},{5,1},{6,2},{7,3},{8,12},{9,13},{10,... | collective-permute-start | bytes 786440 | tf_op jit(solution)/shard_map/grads_across/ppermute | solution.py:320
  231.7 8.3 %collective-permute-start.29 = (bf16[256,512]{1,0:T(8,128)(2,1)S(1)}, bf16[256,512]{1,0:T(8,128)(2,1)S(1)}, u32[]{:S(2)}, u32[]{:S(2)}) collective-permute-start(bf16[256,512]{1,0:T(8,128)(2,1)S(1)} %fusion.26), channel_id=1, source_target_pairs={{0,2},{1,3},{2,0},{3,1},{4,6},{5,7},{6,4},{7,5},{8,10},{9,11},{10,... | collective-permute-start | bytes 786440 | tf_op jit(solution)/shard_map/grads_across/ppermute | solution.py:320
  232.5 12.7 %collective-permute-start.39 = (bf16[2,256,512]{2,1,0:T(8,128)(2,1)S(1)}, bf16[2,256,512]{2,1,0:T(8,128)(2,1)S(1)}, u32[]{:S(2)}, u32[]{:S(2)}) collective-permute-start(bf16[2,256,512]{2,1,0:T(8,128)(2,1)S(1)} %get-tuple-element.53), channel_id=1, source_target_pairs={{0,8},{1,9},{2,10},{3,11},{4,12},{5,13},{6,14},{7,15},{8,16},{9,17... | collective-permute-start | bytes 1572872 | tf_op jit(solution)/shard_map/grads_along_z/ppermute | solution.py:320
  236.9 8.3 %collective-permute-start.42 = (bf16[2,256,512]{2,1,0:T(8,128)(2,1)S(1)}, bf16[2,256,512]{2,1,0:T(8,128)(2,1)S(1)}, u32[]{:S(2)}, u32[]{:S(2)}) collective-permute-start(bf16[2,256,512]{2,1,0:T(8,128)(2,1)S(1)} %get-tuple-element.54), channel_id=1, source_target_pairs={{16,8},{17,9},{18,10},{19,11},{20,12},{21,13},{22,14},{23,15},{24,... | collective-permute-start | bytes 1572872 | tf_op jit(solution)/shard_map/grads_along_z/ppermute | solution.py:320
  238.4 18.3 %collective-permute-start.25 = (bf16[256,512]{1,0:T(8,128)(2,1)}, bf16[256,512]{1,0:T(8,128)(2,1)}, u32[]{:S(2)}, u32[]{:S(2)}) collective-permute-start(bf16[256,512]{1,0:T(8,128)(2,1)} %fusion.28), channel_id=1, source_target_pairs={{0,2},{1,3},{2,0},{3,1},{4,6},{5,7},{6,4},{7,5},{8,10},{9,11},{10,... | collective-permute-start | bytes 786440 | tf_op jit(solution)/shard_map/grads_across/ppermute | solution.py:320
  245.6 15.2 %collective-permute-start.43 = (bf16[2,256,512]{2,1,0:T(8,128)(2,1)S(1)}, bf16[2,256,512]{2,1,0:T(8,128)(2,1)}, u32[]{:S(2)}, u32[]{:S(2)}) collective-permute-start(bf16[2,256,512]{2,1,0:T(8,128)(2,1)S(1)} %get-tuple-element.52), channel_id=1, source_target_pairs={{8,0},{9,1},{10,2},{11,3},{12,4},{13,5},{14,6},{15,7},{16,8},{17,9... | collective-permute-start | bytes 1572872 | tf_op jit(solution)/shard_map/grads_along_z/ppermute | solution.py:320
  246.9 15.7 %collective-permute-start.40 = (bf16[2,256,512]{2,1,0:T(8,128)(2,1)S(1)}, bf16[2,256,512]{2,1,0:T(8,128)(2,1)}, u32[]{:S(2)}, u32[]{:S(2)}) collective-permute-start(bf16[2,256,512]{2,1,0:T(8,128)(2,1)S(1)} %get-tuple-element.51), channel_id=1, source_target_pairs={{0,8},{1,9},{2,10},{3,11},{4,12},{5,13},{6,14},{7,15},{8,16},{9,17... | collective-permute-start | bytes 1572872 | tf_op jit(solution)/shard_map/grads_along_z/ppermute | solution.py:320
Sparse Core Ops, SparseCore 0:
  256.8 128.7 all-reduce.1

commit v2 on v1

--- a/solution.py
+++ b/solution.py
@@ -119,7 +119,7 @@
     )(place, *args)
 
 
-def middle_kernel(place_ref, agg_ref, weight_ref, cot_ref, grad_ref, act_ref, agg_out, pre_out):
+def middle_kernel(place_ref, agg_ref, weight_ref, cot_ref, grad_ref, act_ref, term_ref, sum_ref):
     agg = agg_ref[...].astype(BF16)
     pre = jnp.dot(agg, weight_ref[...], preferred_element_type=F32)
     sigma = jax.nn.sigmoid(pre)
@@ -129,8 +129,24 @@
     grad_ref[...] = lax.dot_general(
         weight_ref[...], pre_grad, (((1,), (1,)), ((), ())), preferred_element_type=F32
     ).astype(BF16)
-    agg_out[...] = agg
-    pre_out[...] = pre_grad
+    term = lax.dot_general(
+        agg, pre_grad, (((0,), (0,)), ((), ())), preferred_element_type=F32
+    )
+    step = pl.program_id(0)
+
+    @pl.when(step == 0)
+    def _():
+        sum_ref[...] = term
+
+    @pl.when(step > 0)
+    def _():
+        sum_ref[...] += term
+
+    @pl.when(step == pl.num_programs(0) - 1)
+    def _():
+        size = term_ref.shape[0]
+        start = pl.multiple_of(place_ref[0] * size, size)
+        term_ref[...] = sum_ref[pl.ds(start, size), :].astype(BF16)
 
 
 def middle(place, agg, weight, cotangent, n_rep):
@@ -138,10 +154,13 @@
     part = rows // n_rep
     block = lambda i, place: ((place[0] + 1 + i) % n_rep, 0)
     last = pl.BlockSpec((part, width), lambda i, place: (0, 0))
-    own = jax.ShapeDtypeStruct((part, width), BF16)
     return pl.pallas_call(
         middle_kernel,
-        out_shape=[jax.ShapeDtypeStruct((width, rows), BF16), own, own, own],
+        out_shape=[
+            jax.ShapeDtypeStruct((width, rows), BF16),
+            jax.ShapeDtypeStruct((part, width), BF16),
+            jax.ShapeDtypeStruct((width // n_rep, width), BF16),
+        ],
         grid_spec=pltpu.PrefetchScalarGridSpec(
             num_scalar_prefetch=1,
             grid=(n_rep,),
@@ -153,13 +172,13 @@
             out_specs=[
                 pl.BlockSpec((width, part), lambda i, place: (0, block(i, place)[0])),
                 last,
-                last,
-                last,
+                pl.BlockSpec((width // n_rep, width), lambda i, place: (0, 0)),
             ],
+            scratch_shapes=[pltpu.VMEM((width, width), F32)],
         ),
         compiler_params=pltpu.CompilerParams(vmem_limit_bytes=40 * 2**20),
         cost_estimate=pl.CostEstimate(
-            flops=4 * rows * width * width,
+            flops=6 * rows * width * width,
             transcendentals=rows * width,
             bytes_accessed=rows * width * 10,
         ),
@@ -323,42 +342,55 @@
         for a, b, c, r in places.devices()
     ]
 
-    arrivals = []
-    major = minor = features
-    for step in range(depth):
-        if step == 0:
-            arrived = features
-        else:
+    half = block_rows // 2
+    fence = lax.optimization_barrier
+
+    def forward_step(step, total, dense, arrival):
+        with jax.named_scope("forward"):
+            return forward_part(table[5 * step : 5 * step + 5], total, dense, *arrival)
+
+    arrived = major = minor = features
+    crossed = complete = total = None
+    tiles = (tile_values[0], tile_rows[0], tile_cols[0], tile_count[0])
+    for phase in range(depth + 1):
+        next_arrived = next_crossed = next_complete = None
+        if phase + 1 < depth:
             with jax.named_scope("features_along_z"):
                 parts = []
-                pairs = places.flow(step, 1)
+                pairs = places.flow(phase + 1, 1)
                 if pairs:
                     major = send(major, pairs)
                     parts.append(major)
-                pairs = places.flow(step, -1)
+                pairs = places.flow(phase + 1, -1)
                 if pairs:
                     minor = send(minor, pairs)
                     parts.append(minor)
-                arrived = functools.reduce(jnp.add, parts)
+                next_arrived = functools.reduce(jnp.add, parts)
         with jax.named_scope("features_across"):
-            to_x, to_y = places.across(step, "x"), places.across(step, "y")
-            x_side, y_side = send(arrived, to_x), send(arrived, to_y)
-            half = block_rows // 2
-            diag_a = send(x_side[:half], to_y)
-            diag_b = send(y_side[half:], to_x)
-        arrivals.append((arrived, x_side, y_side, diag_a, diag_b))
-
-    with jax.named_scope("cotangent_rows"):
-        held = [send(cotangent, rep_pairs(-shift)) if shift else cotangent for shift in range(n_rep)]
-        cot_rows = jnp.roll(jnp.stack(held), rep, axis=0).reshape(block_rows, width)
-
-    with jax.named_scope("dense_blocks"):
-        dense = make_dense(tile_values[0], tile_rows[0], tile_cols[0], tile_count[0], block_rows)
-
-    total = None
-    for step, arrival in enumerate(arrivals):
-        with jax.named_scope("forward"):
-            total = forward_part(table[5 * step : 5 * step + 5], total, dense, *arrival)
+            if crossed is not None:
+                whole, x_side, y_side, x_top, y_bottom = crossed
+                to_x, to_y = places.across(phase - 1, "x"), places.across(phase - 1, "y")
+                next_complete = (whole, x_side, y_side, send(x_top, to_y), send(y_bottom, to_x))
+            if arrived is not None:
+                x_side = send(arrived, places.across(phase, "x"))
+                y_side = send(arrived, places.across(phase, "y"))
+                next_crossed = (arrived, x_side, y_side, x_side[:half], y_side[half:])
+        if phase == 0:
+            with jax.named_scope("dense_blocks"):
+                dense = make_dense(*tiles, block_rows)
+        if phase == depth:
+            with jax.named_scope("cotangent_rows"):
+                held = [
+                    send(cotangent, rep_pairs(-shift)) if shift else cotangent
+                    for shift in range(n_rep)
+                ]
+                cot_rows = jnp.roll(jnp.stack(held), rep, axis=0).reshape(block_rows, width)
+        if complete is not None:
+            total = forward_step(phase - 2, total, dense, complete)
+        arrived, crossed, complete, major, minor, total, dense = fence(
+            (next_arrived, next_crossed, next_complete, major, minor, total, dense)
+        )
+    total = forward_step(depth - 1, total, dense, complete)
 
     with jax.named_scope("partial_sums"):
         shift = 1
@@ -372,69 +404,80 @@
             shift *= 2
 
     with jax.named_scope("middle"):
-        grad, activated, agg_own, pre_own = middle(rep[None], total, weight, cot_rows, n_rep)
-
-    with jax.named_scope("weight_grad"):
-        weight_grad = lax.psum(
-            lax.dot_general(
-                agg_own, pre_own, (((0,), (0,)), ((), ())), preferred_element_type=F32
-            ),
-            BOTH,
-        )
+        grad, activated, term = middle(rep[None], total, weight, cot_rows, n_rep)
 
     to_x, to_y = places.across(None, "x"), places.across(None, "y")
-    sums = []
-    up = down = None
-    for turn in range(depth):
+    bits = places.n_section.bit_length() - 1
+
+    def backward_step(turn, grad, dense):
         with jax.named_scope("backward"):
             start = 5 * depth + 4 * turn
-            x_pair, y_pair, x_b, y_a, own = backward_part(
-                table[start : start + 4], grad, dense, cols
-            )
+            return backward_part(table[start : start + 4], grad, dense, cols)
+
+    def chosen_sum(step, way, dest_of, carried):
+        pairs, picks = [], {}
+        for a, b, c, r in places.devices():
+            dest = dest_of(step, a)
+            if dest is not None:
+                pairs.append((places.flat(a, b, c, r), places.flat(a + way, b, c, r)))
+                picks[a] = places.order(a).index(dest)
+        chosen = None
+        for pick in sorted(set(picks.values())):
+            if chosen is None:
+                chosen = sums[pick]
+            else:
+                here = functools.reduce(
+                    jnp.logical_or, [z == a for a in picks if picks[a] == pick]
+                )
+                chosen = jnp.where(here, sums[pick], chosen)
+        if carried is not None:
+            chosen = chosen + carried.astype(F32)
+        return chosen.astype(BF16), pairs
+
+    sums = []
+    up = down = waiting = None
+    parts = backward_step(0, grad, dense)
+    for phase in range(depth + 1):
+        next_waiting = next_parts = None
+        if phase >= 2:
+            to_up = chosen_sum(phase - 1, 1, places.up_dest, up)
+            to_down = chosen_sum(phase - 1, -1, places.down_dest, down)
+            with jax.named_scope("grads_along_z"):
+                up, down = send(*to_up), send(*to_down)
         with jax.named_scope("grads_across"):
-            from_x, from_y = send(x_pair, to_x), send(y_pair, to_y)
-            x_b = (x_b.astype(F32) + from_y[0].astype(F32)).astype(BF16)
-            y_a = (y_a.astype(F32) + from_x[0].astype(F32)).astype(BF16)
-            last_x, last_y = send(x_b, to_x), send(y_a, to_y)
-            own = own.reshape(2, width // 2, cols).astype(F32)
-            summed = jnp.stack(
-                [
-                    own[0] + from_x[1].astype(F32) + last_y.astype(F32),
-                    own[1] + from_y[1].astype(F32) + last_x.astype(F32),
+            if waiting is not None:
+                x_b, y_a, kept = waiting
+                last_x, last_y = send(x_b, to_x), send(y_a, to_y)
+                sums.append(kept + jnp.stack([last_y, last_x]).astype(F32))
+            if parts is not None:
+                x_pair, y_pair, x_b, y_a, own = parts
+                from_x, from_y = send(x_pair, to_x), send(y_pair, to_y)
+                x_b = (x_b.astype(F32) + from_y[0].astype(F32)).astype(BF16)
+                y_a = (y_a.astype(F32) + from_x[0].astype(F32)).astype(BF16)
+                kept = own.reshape(2, width // 2, cols).astype(F32) + jnp.stack(
+                    [from_x[1], from_y[1]]
+                ).astype(F32)
+                next_waiting = (x_b, y_a, kept)
+        if phase < bits:
+            with jax.named_scope("weight_grad"):
+                flip = 1 << phase
+                pairs = [
+                    (a * n_rep + r, (a ^ flip) * n_rep + r)
+                    for a in range(places.n_section)
+                    for r in range(n_rep)
                 ]
-            )
-            sums.append(summed)
-        step = turn + 1
-        if step == depth:
-            break
-        with jax.named_scope("grads_along_z"):
-            passed = []
-            for dest_of, way, carried in (
-                (places.up_dest, 1, up),
-                (places.down_dest, -1, down),
-            ):
-                pairs, picks = [], {}
-                for a, b, c, r in places.devices():
-                    dest = dest_of(step, a)
-                    if dest is not None:
-                        pairs.append((places.flat(a, b, c, r), places.flat(a + way, b, c, r)))
-                        picks[a] = places.order(a).index(dest)
-                chosen = None
-                for pick in sorted(set(picks.values())):
-                    if chosen is None:
-                        chosen = sums[pick]
-                    else:
-                        here = functools.reduce(
-                            jnp.logical_or, [z == a for a in picks if picks[a] == pick]
-                        )
-                        chosen = jnp.where(here, sums[pick], chosen)
-                if carried is not None:
-                    chosen = chosen + carried.astype(F32)
-                passed.append(send(chosen.astype(BF16), pairs))
-            up, down = passed
+                term = (term.astype(F32) + send(term, pairs).astype(F32)).astype(BF16)
+        if phase + 1 < depth:
+            next_parts = backward_step(phase + 1, grad, dense)
+        waiting, parts, sums, up, down, term, grad, dense = fence(
+            (next_waiting, next_parts, sums, up, down, term, grad, dense)
+        )
     with jax.named_scope("grads_out"):
         final = sums[-1] + up.astype(F32) + down.astype(F32)
         feat_grad = final.reshape(width, cols).astype(BF16).T
+    with jax.named_scope("weight_grad_out"):
+        parts = [send(term, rep_pairs(-shift)) if shift else term for shift in range(n_rep)]
+        weight_grad = jnp.roll(jnp.stack(parts), rep, axis=0).reshape(width, width).astype(F32)
     return (activated, feat_grad[None], weight_grad)
 
 

time: 396 us -> 267 us (0.67)
  waiting for transfers between devices: 210 us -> 72.1 us
  starting transfers between devices: 79.1 us -> 95.6 us
  between operations: 14.7 us -> 1.33 us
    psum x1 -> x0, waiting for transfers between devices: 121 us -> none  [shards(): lax.psum(lax.dot_general(agg_own, pre_own, (((0,), (0,)), ((), ())), pref...]
    ppermute x44 -> x49, waiting for transfers between devices: 89.4 us -> 72.1 us  [shards(): send = lambda value, pairs: lax.ppermute(value, BOTH, pairs)]
    ppermute x44 -> x49, starting transfers between devices: 79 us -> 95.6 us  [shards(): send = lambda value, pairs: lax.ppermute(value, BOTH, pairs)]
    unnamed x31 -> x34, local copies, waits for them, and re-layouts: 9.54 us -> 12.9 us
  transfers between devices with their start and end apart: 45 -> 49, of which waited for: 16 -> 20; matrix products, arithmetic and copies ran while one was open for 4% -> 5% of each run, Pallas kernels for 12% -> 19%
where the time goes in v2:
time: 267 us; the launch traced here: 266 us
  starting transfers between devices  95.6 us (36%)
  waiting for transfers between devices  72.1 us (27%)
  Pallas kernels  63.6 us (24%)
  local copies, waits for them, and re-layouts  18.9 us (7%)
  other arithmetic  14.4 us (5%)
    ppermute x49, starting transfers between devices, shards(): send = lambda value, pairs: lax.ppermute(value, BOTH, pairs)  95.6 us
    ppermute x49, waiting for transfers between devices, shards(): send = lambda value, pairs: lax.ppermute(value, BOTH, pairs)  72.1 us
    pallas_call x4, Pallas kernels, forward_part(): pl.pallas_call(functools.partial(forward_kernel, has_total), out_shape=ja...  28.8 us
    pallas_call x4, Pallas kernels, backward_part(): pl.pallas_call(backward_kernel, out_shape=[jax.ShapeDtypeStruct((2, half,...  22.3 us
    unnamed x34, local copies, waits for them, and re-layouts  12.9 us
    pallas_call x1, Pallas kernels, make_dense(): pl.pallas_call(dense_kernel, out_shape=jax.ShapeDtypeStruct((panels, bloc...  8.7 us
  transfers between devices with their start and end apart: 49, of which 20 were waited for; matrix products, arithmetic and copies ran while one was open for 5% of the time, Pallas kernels for 19%

profile of v2, /device:TPU:0, one launch (start us, length us, event | category | flops | bytes accessed | tf_op | source)
XLA Modules:
  0.0 265.9 jit_solution(137264775483540900)
XLA Ops:
  0.6 4.8 %collective-permute-start.2 = (bf16[1024,512]{1,0:T(8,128)(2,1)}, bf16[1024,512]{1,0:T(8,128)(2,1)S(1)}, u32[]{:S(2)}, u32[]{:S(2)}) collective-permute-start(bf16[1024,512]{1,0:T(8,128)(2,1)} %refs_1_), channel_id=1, source_target_pairs={{0,2},{2,0},{4,6},{6,4},{8,10},{10,8},{12,14},{14,12},{17,19},{19,... | collective-permute-start | bytes 3145736 | tf_op jit(solution)/shard_map/features_across/ppermute | solution.py:339
  5.5 3.4 %collective-permute-start.3 = (bf16[1024,512]{1,0:T(8,128)(2,1)}, bf16[1024,512]{1,0:T(8,128)(2,1)S(1)}, u32[]{:S(2)}, u32[]{:S(2)}) collective-permute-start(bf16[1024,512]{1,0:T(8,128)(2,1)} %refs_1_), channel_id=1, source_target_pairs={{0,4},{2,6},{4,0},{6,2},{8,12},{10,14},{12,8},{14,10},{17,21},{19,... | collective-permute-start | bytes 3145736 | tf_op jit(solution)/shard_map/features_across/ppermute | solution.py:339
  8.9 3.5 %collective-permute-start = (bf16[1024,512]{1,0:T(8,128)(2,1)}, bf16[1024,512]{1,0:T(8,128)(2,1)S(1)}, u32[]{:S(2)}, u32[]{:S(2)}) collective-permute-start(bf16[1024,512]{1,0:T(8,128)(2,1)} %refs_1_), channel_id=1, source_target_pairs={{0,8},{2,10},{4,12},{6,14},{8,16},{10,18},{12,20},{14,22},{17,9},{... | collective-permute-start | bytes 3145736 | tf_op jit(solution)/shard_map/features_along_z/ppermute | solution.py:339
  12.5 1.3 collective-permute-start.1
  13.8 2.8 %copy-done = bf16[1,8,24,128,128]{4,3,2,1,0:T(8,128)(2,1)S(1)} copy-done((bf16[1,8,24,128,128]{4,3,2,1,0:T(8,128)(2,1)S(1)}, bf16[1,8,24,128,128]{4,3,2,1,0:T(8,128)(2,1)}, u32[]{:S(2)}) %copy-start) | copy-done | bytes 6291480
  18.6 8.7 %dense_blocks.1.refs_0_.refs_1_.a_ref = bf16[8,1024,1024]{2,1,0:T(8,128)(2,1)} custom-call(s32[8]{0:T(128)S(1)} %bitcast.97, s32[8,24]{1,0:T(8,128)S(1)} %bitcast.95, s32[8,24]{1,0:T(8,128)S(1)} %bitcast.96, bf16[8,24,128,128]{3,2,1,0:T(8,128)(2,1)S(1)} %bitcast.89), custom_call_target="tpu_custom_call" | custom-call | bytes 23068672 | tf_op jit(solution)/shard_map/dense_blocks/pallas_call | solution.py:32
  27.4 2.0 collective-permute-done.1
  29.7 2.4 collective-permute-start.5
  32.1 2.4 collective-permute-start.6
  34.6 1.7 collective-permute-start.4
  36.2 3.4 %collective-permute-start.7 = (bf16[512,512]{1,0:T(8,128)(2,1)S(1)}, bf16[512,512]{1,0:T(8,128)(2,1)S(1)}, u32[]{:S(2)}, u32[]{:S(2)}) collective-permute-start(bf16[512,512]{1,0:T(8,128)(2,1)S(1)} %slice.160), channel_id=1, source_target_pairs={{0,4},{2,6},{4,0},{6,2},{8,12},{10,14},{12,8},{14,10},{17,21},{19,... | collective-permute-start | bytes 1572872 | tf_op jit(solution)/shard_map/features_across/ppermute | solution.py:339
  39.7 3.4 %collective-permute-start.8 = (bf16[512,512]{1,0:T(8,128)(2,1)S(1)}, bf16[512,512]{1,0:T(8,128)(2,1)S(1)}, u32[]{:S(2)}, u32[]{:S(2)}) collective-permute-start(bf16[512,512]{1,0:T(8,128)(2,1)S(1)} %slice.161), channel_id=1, source_target_pairs={{0,2},{2,0},{4,6},{6,4},{8,10},{10,8},{12,14},{14,12},{17,19},{19,... | collective-permute-start | bytes 1572872 | tf_op jit(solution)/shard_map/features_across/ppermute | solution.py:339
  43.1 3.3 %collective-permute-done.5.refs_3_ = bf16[1024,512]{1,0:T(8,128)(2,1)S(1)} collective-permute-done((bf16[1024,512]{1,0:T(8,128)(2,1)S(1)}, bf16[1024,512]{1,0:T(8,128)(2,1)S(1)}, u32[]{:S(2)}, u32[]{:S(2)}) %collective-permute-start.5) | collective-permute-done | bytes 1048608 | tf_op jit(solution)/shard_map/features_across/ppermute | solution.py:339
  47.2 1.6 collective-permute-done.6.refs_4_
  49.7 6.9 %collective-permute-done.7.refs_4_ = bf16[512,512]{1,0:T(8,128)(2,1)S(1)} collective-permute-done((bf16[512,512]{1,0:T(8,128)(2,1)S(1)}, bf16[512,512]{1,0:T(8,128)(2,1)S(1)}, u32[]{:S(2)}, u32[]{:S(2)}) %collective-permute-start.7) | collective-permute-done | bytes 524320 | tf_op jit(solution)/shard_map/features_across/ppermute | solution.py:339
  58.2 1.7 collective-permute-start.10
  59.9 1.7 collective-permute-start.11
  61.5 1.6 collective-permute-start.9
  63.8 1.9 collective-permute-start.12
  65.8 4.4 %collective-permute-start.13 = (bf16[512,512]{1,0:T(8,128)(2,1)}, bf16[512,512]{1,0:T(8,128)(2,1)S(1)}, u32[]{:S(2)}, u32[]{:S(2)}) collective-permute-start(bf16[512,512]{1,0:T(8,128)(2,1)} %slice.163), channel_id=1, source_target_pairs={{0,2},{2,0},{4,6},{6,4},{8,10},{9,11},{10,8},{11,9},{12,14},{13,15... | collective-permute-start | bytes 1572872 | tf_op jit(solution)/shard_map/features_across/ppermute | solution.py:339
  70.2 1.2 copy-done.2
  71.4 1.2 copy-done.4
  72.7 1.2 copy-done.5
  73.9 1.0 copy-done.7
  76.0 9.1 %forward.4.refs_0_ = f32[1024,512]{1,0:T(8,128)} custom-call(s32[5]{0:T(128)S(1)} %get-tuple-element.261.place_ref, bf16[8,1024,1024]{2,1,0:T(8,128)(2,1)} %dense_blocks.1.refs_0_.refs_1_.a_ref, bf16[1024,512]{1,0:T(8,128)(2,1)S(1)} %copy-done.5, bf16[1024,512]{1,0:T(8,128)(2,1)S(1)} %copy-done.2, bf16[1024,512]{1,0:T(8,128)(2,1)S(1)} %copy-done.4, ...), custom_call_target="tpu_custom_call" | custom-call | flops 4294967296 | bytes 16777216 | tf_op jit(solution)/shard_map/forward/pallas_call | solution.py:103
  85.0 1.1 slice.164
  86.1 1.1 slice.165
  90.1 9.7 %forward.5.refs_0_ = f32[1024,512]{1,0:T(8,128)} custom-call(s32[5]{0:T(128)S(1)} %get-tuple-element.260.place_ref, f32[1024,512]{1,0:T(8,128)} %forward.4.refs_0_, bf16[8,1024,1024]{2,1,0:T(8,128)(2,1)} %dense_blocks.1.refs_0_.refs_1_.a_ref, bf16[1024,512]{1,0:T(8,128)(2,1)S(1)} %add.108.refs_2_, ...), custom_call_target="tpu_custom_call", output_to_operand_aliasing={{}: (1, {})} | custom-call | flops 4294967296 | bytes 16777216 | tf_op jit(solution)/shard_map/forward/pallas_call | solution.py:103
  101.5 5.3 %forward.6.refs_0_ = f32[1024,512]{1,0:T(8,128)} custom-call(s32[5]{0:T(128)S(1)} %get-tuple-element.259.place_ref, f32[1024,512]{1,0:T(8,128)} %forward.5.refs_0_, bf16[8,1024,1024]{2,1,0:T(8,128)(2,1)} %dense_blocks.1.refs_0_.refs_1_.a_ref, bf16[1024,512]{1,0:T(8,128)(2,1)} %collective-permute-done.4.refs_2_, ...), custom_call_target="tpu_custom_call", output_to_operand_aliasing={{}: (1, {})} | custom-call | flops 4294967296 | bytes 16777216 | tf_op jit(solution)/shard_map/forward/pallas_call | solution.py:103
  106.9 4.7 %forward.7 = f32[1024,512]{1,0:T(8,128)} custom-call(s32[5]{0:T(128)S(1)} %get-tuple-element.262.place_ref, f32[1024,512]{1,0:T(8,128)} %forward.6.refs_0_, bf16[8,1024,1024]{2,1,0:T(8,128)(2,1)} %dense_blocks.1.refs_0_.refs_1_.a_ref, bf16[1024,512]{1,0:T(8,128)(2,1)} %collective-permute-done.9.refs_2_, ...), custom_call_target="tpu_custom_call", output_to_operand_aliasing={{}: (1, {})} | custom-call | flops 4294967296 | bytes 16777216 | tf_op jit(solution)/shard_map/forward/pallas_call | solution.py:103
  111.6 2.8 %convert_element_type.235 = bf16[1024,512]{1,0:T(8,128)(2,1)} convert(f32[1024,512]{1,0:T(8,128)} %forward.7) | non-fusion elementwise | flops 524288 | bytes 3145728 | tf_op jit(solution)/shard_map/partial_sums/convert_element_type | solution.py:398
  114.4 10.7 %collective-permute-start.20 = (bf16[1024,512]{1,0:T(8,128)(2,1)}, bf16[1024,512]{1,0:T(8,128)(2,1)S(1)}, u32[]{:S(2)}, u32[]{:S(2)}) collective-permute-start(bf16[1024,512]{1,0:T(8,128)(2,1)} %convert_element_type.235), channel_id=1, source_target_pairs={{0,1},{1,0},{2,3},{3,2},{4,5},{5,4},{6,7},{7,6},{8,9},{9,8},{10,11... | collective-permute-start | bytes 3145736 | tf_op jit(solution)/shard_map/partial_sums/ppermute | solution.py:339
  125.1 3.2 %collective-permute-done.21 = bf16[512,512]{1,0:T(8,128)(2,1)} collective-permute-done((bf16[512,512]{1,0:T(8,128)(2,1)}, bf16[512,512]{1,0:T(8,128)(2,1)}, u32[]{:S(2)}, u32[]{:S(2)}) %collective-permute-start.21) | collective-permute-done | bytes 524320 | tf_op jit(solution)/shard_map/cotangent_rows/ppermute | solution.py:339
  128.3 2.1 fusion.2
  131.4 3.8 %middle.1 = (bf16[512,1024]{1,0:T(8,128)(2,1)S(1)}, bf16[512,512]{1,0:T(8,128)(2,1)}, bf16[256,512]{1,0:T(8,128)(2,1)S(1)}) custom-call(s32[1]{0:T(128)} %bitcast.place_ref, f32[1024,512]{1,0:T(8,128)S(1)} %convert_add_fusion.agg_ref, bf16[512,512]{1,0:T(8,128)(2,1)S(1)} %copy-done.13, bf16[1024,512]{1,0:T(8,128)(2,1)S(1)} %bitcast.90), custom_call_target="tpu_custom_call" | custom-call | flops 1610612736 | bytes 5242880 | tf_op jit(solution)/shard_map/middle/pallas_call | solution.py:157
  135.3 5.5 %backward.4 = (bf16[2,256,512]{2,1,0:T(8,128)(2,1)S(1)}, bf16[2,256,512]{2,1,0:T(8,128)(2,1)S(1)}, bf16[256,512]{1,0:T(8,128)(2,1)S(1)}, bf16[256,512]{1,0:T(8,128)(2,1)S(1)}, bf16[512,512]{1,0:T(8,128)(2,1)S(1)}) custom-call(s32[4]{0:T(128)S(1)} %get-tuple-element.258.place_ref, bf16[512,1024]{1,0:T(8,128)(2,1)S(1)} %get-tuple-element.214.grad_ref, ...), custom_call_target="tpu_custom_call" | custom-call | flops 2147483648 | bytes 7340032 | tf_op jit(solution)/shard_map/backward/pallas_call | solution.py:219
  141.4 1.7 collective-permute-start.24
  143.1 5.5 %backward.5 = (bf16[2,256,512]{2,1,0:T(8,128)(2,1)S(1)}, bf16[2,256,512]{2,1,0:T(8,128)(2,1)S(1)}, bf16[256,512]{1,0:T(8,128)(2,1)S(1)}, bf16[256,512]{1,0:T(8,128)(2,1)S(1)}, bf16[512,512]{1,0:T(8,128)(2,1)S(1)}) custom-call(s32[4]{0:T(128)S(1)} %get-tuple-element.257.place_ref, bf16[512,1024]{1,0:T(8,128)(2,1)S(1)} %get-tuple-element.214.grad_ref, ...), custom_call_target="tpu_custom_call" | custom-call | flops 2147483648 | bytes 7340032 | tf_op jit(solution)/shard_map/backward/pallas_call | solution.py:219
  148.7 11.8 %collective-permute-done.24 = bf16[256,512]{1,0:T(8,128)(2,1)S(1)} collective-permute-done((bf16[256,512]{1,0:T(8,128)(2,1)S(1)}, bf16[256,512]{1,0:T(8,128)(2,1)S(1)}, u32[]{:S(2)}, u32[]{:S(2)}) %collective-permute-start.24) | collective-permute-done | bytes 262176 | tf_op jit(solution)/shard_map/weight_grad/ppermute | solution.py:339
  161.2 1.7 collective-permute-start.27
  163.2 1.7 collective-permute-start.26
  165.3 5.7 %backward.6 = (bf16[2,256,512]{2,1,0:T(8,128)(2,1)S(1)}, bf16[2,256,512]{2,1,0:T(8,128)(2,1)S(1)}, bf16[256,512]{1,0:T(8,128)(2,1)S(1)}, bf16[256,512]{1,0:T(8,128)(2,1)S(1)}, bf16[512,512]{1,0:T(8,128)(2,1)S(1)}) custom-call(s32[4]{0:T(128)S(1)} %get-tuple-element.256.place_ref, bf16[512,1024]{1,0:T(8,128)(2,1)S(1)} %get-tuple-element.214.grad_ref, ...), custom_call_target="tpu_custom_call" | custom-call | flops 2147483648 | bytes 7340032 | tf_op jit(solution)/shard_map/backward/pallas_call | solution.py:219
  171.1 4.7 %collective-permute-done.27 = bf16[256,512]{1,0:T(8,128)(2,1)S(1)} collective-permute-done((bf16[256,512]{1,0:T(8,128)(2,1)S(1)}, bf16[256,512]{1,0:T(8,128)(2,1)S(1)}, u32[]{:S(2)}, u32[]{:S(2)}) %collective-permute-start.27) | collective-permute-done | bytes 262176 | tf_op jit(solution)/shard_map/grads_across/ppermute | solution.py:339
  175.8 1.1 convert_add_fusion.8
  176.9 4.2 %collective-permute-done.26 = bf16[2,256,512]{2,1,0:T(8,128)(2,1)S(1)} collective-permute-done((bf16[2,256,512]{2,1,0:T(8,128)(2,1)S(1)}, bf16[2,256,512]{2,1,0:T(8,128)(2,1)S(1)}, u32[]{:S(2)}, u32[]{:S(2)}) %collective-permute-start.26) | collective-permute-done | bytes 524320 | tf_op jit(solution)/shard_map/grads_across/ppermute | solution.py:339
  181.2 4.1 %collective-permute-done.25 = bf16[2,256,512]{2,1,0:T(8,128)(2,1)S(1)} collective-permute-done((bf16[2,256,512]{2,1,0:T(8,128)(2,1)S(1)}, bf16[2,256,512]{2,1,0:T(8,128)(2,1)S(1)}, u32[]{:S(2)}, u32[]{:S(2)}) %collective-permute-start.25) | collective-permute-done | bytes 524320 | tf_op jit(solution)/shard_map/grads_across/ppermute | solution.py:339
  185.3 1.2 convert_add_fusion.3
  188.6 1.7 collective-permute-start.31
  190.3 1.7 collective-permute-start.30
  192.1 5.5 %backward.7 = (bf16[2,256,512]{2,1,0:T(8,128)(2,1)S(1)}, bf16[2,256,512]{2,1,0:T(8,128)(2,1)S(1)}, bf16[256,512]{1,0:T(8,128)(2,1)S(1)}, bf16[256,512]{1,0:T(8,128)(2,1)S(1)}, bf16[512,512]{1,0:T(8,128)(2,1)S(1)}) custom-call(s32[4]{0:T(128)S(1)} %get-tuple-element.255.place_ref, bf16[512,1024]{1,0:T(8,128)(2,1)S(1)} %get-tuple-element.214.grad_ref, ...), custom_call_target="tpu_custom_call" | custom-call | flops 2147483648 | bytes 7340032 | tf_op jit(solution)/shard_map/backward/pallas_call | solution.py:219
  197.7 4.1 %collective-permute-start.34 = (bf16[2,256,512]{2,1,0:T(8,128)(2,1)S(1)}, bf16[2,256,512]{2,1,0:T(8,128)(2,1)S(1)}, u32[]{:S(2)}, u32[]{:S(2)}) collective-permute-start(bf16[2,256,512]{2,1,0:T(8,128)(2,1)S(1)} %convert_element_type.279), channel_id=1, source_target_pairs={{0,8},{1,9},{2,10},{3,11},{4,12},{5,13},{6,14},{7,15}} | collective-permute-start | bytes 1572872 | tf_op jit(solution)/shard_map/grads_along_z/ppermute | solution.py:339
  203.7 2.3 collective-permute-done.31
  206.4 3.7 %collective-permute-done.34 = bf16[2,256,512]{2,1,0:T(8,128)(2,1)S(1)} collective-permute-done((bf16[2,256,512]{2,1,0:T(8,128)(2,1)S(1)}, bf16[2,256,512]{2,1,0:T(8,128)(2,1)S(1)}, u32[]{:S(2)}, u32[]{:S(2)}) %collective-permute-start.34) | collective-permute-done | bytes 524320 | tf_op jit(solution)/shard_map/grads_along_z/ppermute | solution.py:339
  210.1 16.5 %collective-permute-start.43 = (bf16[256,512]{1,0:T(8,128)(2,1)S(1)}, bf16[256,512]{1,0:T(8,128)(2,1)S(1)}, u32[]{:S(2)}, u32[]{:S(2)}) collective-permute-start(bf16[256,512]{1,0:T(8,128)(2,1)S(1)} %add_convert_fusion.6), channel_id=1, source_target_pairs={{0,16},{1,17},{2,18},{3,19},{4,20},{5,21},{6,22},{7,23},{8,24},{9,... | collective-permute-start | bytes 786440 | tf_op jit(solution)/shard_map/weight_grad/ppermute | solution.py:339
  228.0 1.3 collective-permute-start.38
  229.7 1.5 collective-permute-start.41
  231.2 3.7 %collective-permute-done.43 = bf16[256,512]{1,0:T(8,128)(2,1)S(1)} collective-permute-done((bf16[256,512]{1,0:T(8,128)(2,1)S(1)}, bf16[256,512]{1,0:T(8,128)(2,1)S(1)}, u32[]{:S(2)}, u32[]{:S(2)}) %collective-permute-start.43) | collective-permute-done | bytes 262176 | tf_op jit(solution)/shard_map/weight_grad/ppermute | solution.py:339
  236.6 3.0 %collective-permute-done.38 = bf16[2,256,512]{2,1,0:T(8,128)(2,1)S(1)} collective-permute-done((bf16[2,256,512]{2,1,0:T(8,128)(2,1)S(1)}, bf16[2,256,512]{2,1,0:T(8,128)(2,1)S(1)}, u32[]{:S(2)}, u32[]{:S(2)}) %collective-permute-start.38) | collective-permute-done | bytes 524320 | tf_op jit(solution)/shard_map/grads_across/ppermute | solution.py:339
  239.8 7.0 %collective-permute-done.37 = bf16[2,256,512]{2,1,0:T(8,128)(2,1)S(1)} collective-permute-done((bf16[2,256,512]{2,1,0:T(8,128)(2,1)S(1)}, bf16[2,256,512]{2,1,0:T(8,128)(2,1)S(1)}, u32[]{:S(2)}, u32[]{:S(2)}) %collective-permute-start.37) | collective-permute-done | bytes 524320 | tf_op jit(solution)/shard_map/grads_across/ppermute | solution.py:339
  248.7 3.1 %collective-permute-start.46 = (bf16[2,256,512]{2,1,0:T(8,128)(2,1)S(1)}, bf16[2,256,512]{2,1,0:T(8,128)(2,1)S(1)}, u32[]{:S(2)}, u32[]{:S(2)}) collective-permute-start(bf16[2,256,512]{2,1,0:T(8,128)(2,1)S(1)} %get-tuple-element.252), channel_id=1, source_target_pairs={{0,8},{1,9},{2,10},{3,11},{4,12},{5,13},{6,14},{7,15},{8,16},{9,17... | collective-permute-start | bytes 1572872 | tf_op jit(solution)/shard_map/grads_along_z/ppermute | solution.py:339
  251.8 1.3 collective-permute-start.47
  253.9 4.5 %collective-permute-done.46 = bf16[2,256,512]{2,1,0:T(8,128)(2,1)S(1)} collective-permute-done((bf16[2,256,512]{2,1,0:T(8,128)(2,1)S(1)}, bf16[2,256,512]{2,1,0:T(8,128)(2,1)S(1)}, u32[]{:S(2)}, u32[]{:S(2)}) %collective-permute-start.46) | collective-permute-done | bytes 524320 | tf_op jit(solution)/shard_map/grads_along_z/ppermute | solution.py:339
  258.4 4.4 %collective-permute-done.47 = bf16[2,256,512]{2,1,0:T(8,128)(2,1)S(1)} collective-permute-done((bf16[2,256,512]{2,1,0:T(8,128)(2,1)S(1)}, bf16[2,256,512]{2,1,0:T(8,128)(2,1)S(1)}, u32[]{:S(2)}, u32[]{:S(2)}) %collective-permute-start.47) | collective-permute-done | bytes 524320 | tf_op jit(solution)/shard_map/grads_along_z/ppermute | solution.py:339
  264.8 1.1 bitcast_convert_fusion
  (128 shorter events, 27.9 us)
Async XLA Ops:
  0.6 26.7 %collective-permute-start.2 = (bf16[1024,512]{1,0:T(8,128)(2,1)}, bf16[1024,512]{1,0:T(8,128)(2,1)S(1)}, u32[]{:S(2)}, u32[]{:S(2)}) collective-permute-start(bf16[1024,512]{1,0:T(8,128)(2,1)} %refs_1_), channel_id=1, source_target_pairs={{0,2},{2,0},{4,6},{6,4},{8,10},{10,8},{12,14},{14,12},{17,19},{19,... | collective-permute-start | bytes 3145736 | tf_op jit(solution)/shard_map/features_across/ppermute | solution.py:339
  5.5 21.9 %collective-permute-start.3 = (bf16[1024,512]{1,0:T(8,128)(2,1)}, bf16[1024,512]{1,0:T(8,128)(2,1)S(1)}, u32[]{:S(2)}, u32[]{:S(2)}) collective-permute-start(bf16[1024,512]{1,0:T(8,128)(2,1)} %refs_1_), channel_id=1, source_target_pairs={{0,4},{2,6},{4,0},{6,2},{8,12},{10,14},{12,8},{14,10},{17,21},{19,... | collective-permute-start | bytes 3145736 | tf_op jit(solution)/shard_map/features_across/ppermute | solution.py:339
  8.9 18.5 %collective-permute-start = (bf16[1024,512]{1,0:T(8,128)(2,1)}, bf16[1024,512]{1,0:T(8,128)(2,1)S(1)}, u32[]{:S(2)}, u32[]{:S(2)}) collective-permute-start(bf16[1024,512]{1,0:T(8,128)(2,1)} %refs_1_), channel_id=1, source_target_pairs={{0,8},{2,10},{4,12},{6,14},{8,16},{10,18},{12,20},{14,22},{17,9},{... | collective-permute-start | bytes 3145736 | tf_op jit(solution)/shard_map/features_along_z/ppermute | solution.py:339
  12.5 16.9 %collective-permute-start.1 = (bf16[1024,512]{1,0:T(8,128)(2,1)}, bf16[1024,512]{1,0:T(8,128)(2,1)S(1)}, u32[]{:S(2)}, u32[]{:S(2)}) collective-permute-start(bf16[1024,512]{1,0:T(8,128)(2,1)} %refs_1_), channel_id=1, source_target_pairs={{8,0},{10,2},{12,4},{14,6},{17,25},{19,27},{21,29},{23,31}} | collective-permute-start | bytes 3145736 | tf_op jit(solution)/shard_map/features_along_z/ppermute | solution.py:339
  13.8 2.8 %copy-start = (bf16[1,8,24,128,128]{4,3,2,1,0:T(8,128)(2,1)S(1)}, bf16[1,8,24,128,128]{4,3,2,1,0:T(8,128)(2,1)}, u32[]{:S(2)}) copy-start(bf16[1,8,24,128,128]{4,3,2,1,0:T(8,128)(2,1)} %param.10) | copy-start | bytes 18874372
  16.6 0.7 copy-start.10
  27.3 2.4 copy-start.1
  27.4 2.3 copy-start.3
  29.7 16.7 %collective-permute-start.5 = (bf16[1024,512]{1,0:T(8,128)(2,1)S(1)}, bf16[1024,512]{1,0:T(8,128)(2,1)S(1)}, u32[]{:S(2)}, u32[]{:S(2)}) collective-permute-start(bf16[1024,512]{1,0:T(8,128)(2,1)S(1)} %add.108.refs_2_), channel_id=1, source_target_pairs={{0,2},{2,0},{4,6},{6,4},{8,10},{9,11},{10,8},{11,9},{12,14},{13,15... | collective-permute-start | bytes 3145736 | tf_op jit(solution)/shard_map/features_across/ppermute | solution.py:339
  32.1 16.7 %collective-permute-start.6 = (bf16[1024,512]{1,0:T(8,128)(2,1)S(1)}, bf16[1024,512]{1,0:T(8,128)(2,1)S(1)}, u32[]{:S(2)}, u32[]{:S(2)}) collective-permute-start(bf16[1024,512]{1,0:T(8,128)(2,1)S(1)} %add.108.refs_2_), channel_id=1, source_target_pairs={{0,4},{2,6},{4,0},{6,2},{8,12},{9,13},{10,14},{11,15},{12,8},{13,9... | collective-permute-start | bytes 3145736 | tf_op jit(solution)/shard_map/features_across/ppermute | solution.py:339
  34.6 23.7 %collective-permute-start.4 = (bf16[1024,512]{1,0:T(8,128)(2,1)S(1)}, bf16[1024,512]{1,0:T(8,128)(2,1)}, u32[]{:S(2)}, u32[]{:S(2)}) collective-permute-start(bf16[1024,512]{1,0:T(8,128)(2,1)S(1)} %collective-permute-done), channel_id=1, source_target_pairs={{8,16},{9,1},{10,18},{11,3},{12,20},{13,5},{14,22},{15,7},{16,24},... | collective-permute-start | bytes 3145736 | tf_op jit(solution)/shard_map/features_along_z/ppermute | solution.py:339
  36.2 20.4 %collective-permute-start.7 = (bf16[512,512]{1,0:T(8,128)(2,1)S(1)}, bf16[512,512]{1,0:T(8,128)(2,1)S(1)}, u32[]{:S(2)}, u32[]{:S(2)}) collective-permute-start(bf16[512,512]{1,0:T(8,128)(2,1)S(1)} %slice.160), channel_id=1, source_target_pairs={{0,4},{2,6},{4,0},{6,2},{8,12},{10,14},{12,8},{14,10},{17,21},{19,... | collective-permute-start | bytes 1572872 | tf_op jit(solution)/shard_map/features_across/ppermute | solution.py:339
  39.7 17.8 %collective-permute-start.8 = (bf16[512,512]{1,0:T(8,128)(2,1)S(1)}, bf16[512,512]{1,0:T(8,128)(2,1)S(1)}, u32[]{:S(2)}, u32[]{:S(2)}) collective-permute-start(bf16[512,512]{1,0:T(8,128)(2,1)S(1)} %slice.161), channel_id=1, source_target_pairs={{0,2},{2,0},{4,6},{6,4},{8,10},{10,8},{12,14},{14,12},{17,19},{19,... | collective-permute-start | bytes 1572872 | tf_op jit(solution)/shard_map/features_across/ppermute | solution.py:339
  56.6 0.8 copy-start.6
  57.4 0.8 copy-start.8
  58.2 26.8 %collective-permute-start.10 = (bf16[1024,512]{1,0:T(8,128)(2,1)}, bf16[1024,512]{1,0:T(8,128)(2,1)}, u32[]{:S(2)}, u32[]{:S(2)}) collective-permute-start(bf16[1024,512]{1,0:T(8,128)(2,1)} %collective-permute-done.4.refs_2_), channel_id=1, source_target_pairs={{1,3},{3,1},{5,7},{7,5},{9,11},{11,9},{13,15},{15,13},{16,18},{18,... | collective-permute-start | bytes 3145736 | tf_op jit(solution)/shard_map/features_across/ppermute | solution.py:339
  59.9 26.2 %collective-permute-start.11 = (bf16[1024,512]{1,0:T(8,128)(2,1)}, bf16[1024,512]{1,0:T(8,128)(2,1)}, u32[]{:S(2)}, u32[]{:S(2)}) collective-permute-start(bf16[1024,512]{1,0:T(8,128)(2,1)} %collective-permute-done.4.refs_2_), channel_id=1, source_target_pairs={{1,5},{3,7},{5,1},{7,3},{9,13},{11,15},{13,9},{15,11},{16,20},{18,... | collective-permute-start | bytes 3145736 | tf_op jit(solution)/shard_map/features_across/ppermute | solution.py:339
  61.5 25.7 %collective-permute-start.9 = (bf16[1024,512]{1,0:T(8,128)(2,1)}, bf16[1024,512]{1,0:T(8,128)(2,1)}, u32[]{:S(2)}, u32[]{:S(2)}) collective-permute-start(bf16[1024,512]{1,0:T(8,128)(2,1)} %collective-permute-done.4.refs_2_), channel_id=1, source_target_pairs={{9,1},{11,3},{13,5},{15,7},{16,24},{18,26},{20,28},{22,30}} | collective-permute-start | bytes 3145736 | tf_op jit(solution)/shard_map/features_along_z/ppermute | solution.py:339
  63.8 23.4 %collective-permute-start.12 = (bf16[512,512]{1,0:T(8,128)(2,1)}, bf16[512,512]{1,0:T(8,128)(2,1)S(1)}, u32[]{:S(2)}, u32[]{:S(2)}) collective-permute-start(bf16[512,512]{1,0:T(8,128)(2,1)} %slice.162), channel_id=1, source_target_pairs={{0,4},{2,6},{4,0},{6,2},{8,12},{9,13},{10,14},{11,15},{12,8},{13,9... | collective-permute-start | bytes 1572872 | tf_op jit(solution)/shard_map/features_across/ppermute | solution.py:339
  65.8 21.5 %collective-permute-start.13 = (bf16[512,512]{1,0:T(8,128)(2,1)}, bf16[512,512]{1,0:T(8,128)(2,1)S(1)}, u32[]{:S(2)}, u32[]{:S(2)}) collective-permute-start(bf16[512,512]{1,0:T(8,128)(2,1)} %slice.163), channel_id=1, source_target_pairs={{0,2},{2,0},{4,6},{6,4},{8,10},{9,11},{10,8},{11,9},{12,14},{13,15... | collective-permute-start | bytes 1572872 | tf_op jit(solution)/shard_map/features_across/ppermute | solution.py:339
  70.2 1.2 copy-start.2
  71.4 1.2 copy-start.4
  72.7 1.2 copy-start.5
  73.9 1.0 copy-start.7
  74.9 1.0 copy-start.9
  87.2 12.6 %collective-permute-start.14 = (bf16[1024,512]{1,0:T(8,128)(2,1)}, bf16[1024,512]{1,0:T(8,128)(2,1)S(1)}, u32[]{:S(2)}, u32[]{:S(2)}) collective-permute-start(bf16[1024,512]{1,0:T(8,128)(2,1)} %collective-permute-done.9.refs_2_), channel_id=1, source_target_pairs={{1,3},{3,1},{5,7},{7,5},{24,26},{26,24},{28,30},{30,28}} | collective-permute-start | bytes 3145736 | tf_op jit(solution)/shard_map/features_across/ppermute | solution.py:339
  88.0 11.9 %collective-permute-start.15 = (bf16[1024,512]{1,0:T(8,128)(2,1)}, bf16[1024,512]{1,0:T(8,128)(2,1)S(1)}, u32[]{:S(2)}, u32[]{:S(2)}) collective-permute-start(bf16[1024,512]{1,0:T(8,128)(2,1)} %collective-permute-done.9.refs_2_), channel_id=1, source_target_pairs={{1,5},{3,7},{5,1},{7,3},{24,28},{26,30},{28,24},{30,26}} | collective-permute-start | bytes 3145736 | tf_op jit(solution)/shard_map/features_across/ppermute | solution.py:339
  88.7 11.2 %collective-permute-start.16 = (bf16[512,512]{1,0:T(8,128)(2,1)S(1)}, bf16[512,512]{1,0:T(8,128)(2,1)S(1)}, u32[]{:S(2)}, u32[]{:S(2)}) collective-permute-start(bf16[512,512]{1,0:T(8,128)(2,1)S(1)} %slice.164), channel_id=1, source_target_pairs={{1,5},{3,7},{5,1},{7,3},{9,13},{11,15},{13,9},{15,11},{16,20},{18,... | collective-permute-start | bytes 1572872 | tf_op jit(solution)/shard_map/features_across/ppermute | solution.py:339
  89.4 10.5 %collective-permute-start.17 = (bf16[512,512]{1,0:T(8,128)(2,1)S(1)}, bf16[512,512]{1,0:T(8,128)(2,1)S(1)}, u32[]{:S(2)}, u32[]{:S(2)}) collective-permute-start(bf16[512,512]{1,0:T(8,128)(2,1)S(1)} %slice.165), channel_id=1, source_target_pairs={{1,3},{3,1},{5,7},{7,5},{9,11},{11,9},{13,15},{15,13},{16,18},{18,... | collective-permute-start | bytes 1572872 | tf_op jit(solution)/shard_map/features_across/ppermute | solution.py:339
  100.0 6.9 %collective-permute-start.18 = (bf16[512,512]{1,0:T(8,128)(2,1)S(1)}, bf16[512,512]{1,0:T(8,128)(2,1)S(1)}, u32[]{:S(2)}, u32[]{:S(2)}) collective-permute-start(bf16[512,512]{1,0:T(8,128)(2,1)S(1)} %slice.166), channel_id=1, source_target_pairs={{1,5},{3,7},{5,1},{7,3},{24,28},{26,30},{28,24},{30,26}} | collective-permute-start | bytes 1572872 | tf_op jit(solution)/shard_map/features_across/ppermute | solution.py:339
  100.7 6.2 %collective-permute-start.19 = (bf16[512,512]{1,0:T(8,128)(2,1)S(1)}, bf16[512,512]{1,0:T(8,128)(2,1)S(1)}, u32[]{:S(2)}, u32[]{:S(2)}) collective-permute-start(bf16[512,512]{1,0:T(8,128)(2,1)S(1)} %slice.167), channel_id=1, source_target_pairs={{1,3},{3,1},{5,7},{7,5},{24,26},{26,24},{28,30},{30,28}} | collective-permute-start | bytes 1572872 | tf_op jit(solution)/shard_map/features_across/ppermute | solution.py:339
  111.6 18.9 %copy-start.14 = (f32[1024,512]{1,0:T(8,128)S(1)}, f32[1024,512]{1,0:T(8,128)}, u32[]{:S(2)}) copy-start(f32[1024,512]{1,0:T(8,128)} %forward.7) | copy-start | bytes 6291460
  114.4 16.0 %collective-permute-start.20 = (bf16[1024,512]{1,0:T(8,128)(2,1)}, bf16[1024,512]{1,0:T(8,128)(2,1)S(1)}, u32[]{:S(2)}, u32[]{:S(2)}) collective-permute-start(bf16[1024,512]{1,0:T(8,128)(2,1)} %convert_element_type.235), channel_id=1, source_target_pairs={{0,1},{1,0},{2,3},{3,2},{4,5},{5,4},{6,7},{7,6},{8,9},{9,8},{10,11... | collective-permute-start | bytes 3145736 | tf_op jit(solution)/shard_map/partial_sums/ppermute | solution.py:339
  125.1 3.2 %collective-permute-start.21 = (bf16[512,512]{1,0:T(8,128)(2,1)}, bf16[512,512]{1,0:T(8,128)(2,1)}, u32[]{:S(2)}, u32[]{:S(2)}) collective-permute-start(bf16[512,512]{1,0:T(8,128)(2,1)} %param.14), channel_id=1, source_target_pairs={{0,1},{1,0},{2,3},{3,2},{4,5},{5,4},{6,7},{7,6},{8,9},{9,8},{10,11... | collective-permute-start | bytes 1572872 | tf_op jit(solution)/shard_map/cotangent_rows/ppermute | solution.py:339
  130.4 1.0 copy-start.13
  140.8 19.7 %collective-permute-start.23 = (bf16[2,256,512]{2,1,0:T(8,128)(2,1)S(1)}, bf16[2,256,512]{2,1,0:T(8,128)(2,1)S(1)}, u32[]{:S(2)}, u32[]{:S(2)}) collective-permute-start(bf16[2,256,512]{2,1,0:T(8,128)(2,1)S(1)} %get-tuple-element.185), channel_id=1, source_target_pairs={{0,2},{1,3},{2,0},{3,1},{4,6},{5,7},{6,4},{7,5},{8,10},{9,11},{10,... | collective-permute-start | bytes 1572872 | tf_op jit(solution)/shard_map/grads_across/ppermute | solution.py:339
  141.1 19.4 %collective-permute-start.22 = (bf16[2,256,512]{2,1,0:T(8,128)(2,1)S(1)}, bf16[2,256,512]{2,1,0:T(8,128)(2,1)S(1)}, u32[]{:S(2)}, u32[]{:S(2)}) collective-permute-start(bf16[2,256,512]{2,1,0:T(8,128)(2,1)S(1)} %get-tuple-element.183), channel_id=1, source_target_pairs={{0,4},{1,5},{2,6},{3,7},{4,0},{5,1},{6,2},{7,3},{8,12},{9,13},{10,... | collective-permute-start | bytes 1572872 | tf_op jit(solution)/shard_map/grads_across/ppermute | solution.py:339
  141.4 19.0 %collective-permute-start.24 = (bf16[256,512]{1,0:T(8,128)(2,1)S(1)}, bf16[256,512]{1,0:T(8,128)(2,1)S(1)}, u32[]{:S(2)}, u32[]{:S(2)}) collective-permute-start(bf16[256,512]{1,0:T(8,128)(2,1)S(1)} %get-tuple-element.192), channel_id=1, source_target_pairs={{0,2},{1,3},{2,0},{3,1},{4,6},{5,7},{6,4},{7,5},{8,10},{9,11},{10,... | collective-permute-start | bytes 786440 | tf_op jit(solution)/shard_map/weight_grad/ppermute | solution.py:339
  160.9 10.1 %collective-permute-start.29 = (bf16[256,512]{1,0:T(8,128)(2,1)S(1)}, bf16[256,512]{1,0:T(8,128)(2,1)S(1)}, u32[]{:S(2)}, u32[]{:S(2)}) collective-permute-start(bf16[256,512]{1,0:T(8,128)(2,1)S(1)} %add_convert_fusion.8), channel_id=1, source_target_pairs={{0,4},{1,5},{2,6},{3,7},{4,0},{5,1},{6,2},{7,3},{8,12},{9,13},{10,... | collective-permute-start | bytes 786440 | tf_op jit(solution)/shard_map/weight_grad/ppermute | solution.py:339
  161.2 14.6 %collective-permute-start.27 = (bf16[256,512]{1,0:T(8,128)(2,1)S(1)}, bf16[256,512]{1,0:T(8,128)(2,1)S(1)}, u32[]{:S(2)}, u32[]{:S(2)}) collective-permute-start(bf16[256,512]{1,0:T(8,128)(2,1)S(1)} %fusion.12), channel_id=1, source_target_pairs={{0,4},{1,5},{2,6},{3,7},{4,0},{5,1},{6,2},{7,3},{8,12},{9,13},{10,... | collective-permute-start | bytes 786440 | tf_op jit(solution)/shard_map/grads_across/ppermute | solution.py:339
  163.0 12.8 %collective-permute-start.28 = (bf16[256,512]{1,0:T(8,128)(2,1)S(1)}, bf16[256,512]{1,0:T(8,128)(2,1)S(1)}, u32[]{:S(2)}, u32[]{:S(2)}) collective-permute-start(bf16[256,512]{1,0:T(8,128)(2,1)S(1)} %fusion.13), channel_id=1, source_target_pairs={{0,2},{1,3},{2,0},{3,1},{4,6},{5,7},{6,4},{7,5},{8,10},{9,11},{10,... | collective-permute-start | bytes 786440 | tf_op jit(solution)/shard_map/grads_across/ppermute | solution.py:339
  163.2 17.9 %collective-permute-start.26 = (bf16[2,256,512]{2,1,0:T(8,128)(2,1)S(1)}, bf16[2,256,512]{2,1,0:T(8,128)(2,1)S(1)}, u32[]{:S(2)}, u32[]{:S(2)}) collective-permute-start(bf16[2,256,512]{2,1,0:T(8,128)(2,1)S(1)} %get-tuple-element.196), channel_id=1, source_target_pairs={{0,2},{1,3},{2,0},{3,1},{4,6},{5,7},{6,4},{7,5},{8,10},{9,11},{10,... | collective-permute-start | bytes 1572872 | tf_op jit(solution)/shard_map/grads_across/ppermute | solution.py:339
  165.0 20.3 %collective-permute-start.25 = (bf16[2,256,512]{2,1,0:T(8,128)(2,1)S(1)}, bf16[2,256,512]{2,1,0:T(8,128)(2,1)S(1)}, u32[]{:S(2)}, u32[]{:S(2)}) collective-permute-start(bf16[2,256,512]{2,1,0:T(8,128)(2,1)S(1)} %get-tuple-element.194), channel_id=1, source_target_pairs={{0,4},{1,5},{2,6},{3,7},{4,0},{5,1},{6,2},{7,3},{8,12},{9,13},{10,... | collective-permute-start | bytes 1572872 | tf_op jit(solution)/shard_map/grads_across/ppermute | solution.py:339
  188.0 9.7 %collective-permute-start.36 = (bf16[256,512]{1,0:T(8,128)(2,1)S(1)}, bf16[256,512]{1,0:T(8,128)(2,1)}, u32[]{:S(2)}, u32[]{:S(2)}) collective-permute-start(bf16[256,512]{1,0:T(8,128)(2,1)S(1)} %add_convert_fusion.7), channel_id=1, source_target_pairs={{0,8},{1,9},{2,10},{3,11},{4,12},{5,13},{6,14},{7,15},{8,0},{9,1},... | collective-permute-start | bytes 786440 | tf_op jit(solution)/shard_map/weight_grad/ppermute | solution.py:339
  188.0 14.8 %collective-permute-start.32 = (bf16[256,512]{1,0:T(8,128)(2,1)}, bf16[256,512]{1,0:T(8,128)(2,1)S(1)}, u32[]{:S(2)}, u32[]{:S(2)}) collective-permute-start(bf16[256,512]{1,0:T(8,128)(2,1)} %fusion.10), channel_id=1, source_target_pairs={{0,4},{1,5},{2,6},{3,7},{4,0},{5,1},{6,2},{7,3},{8,12},{9,13},{10,... | collective-permute-start | bytes 786440 | tf_op jit(solution)/shard_map/grads_across/ppermute | solution.py:339
  188.3 15.2 %collective-permute-start.33 = (bf16[256,512]{1,0:T(8,128)(2,1)}, bf16[256,512]{1,0:T(8,128)(2,1)S(1)}, u32[]{:S(2)}, u32[]{:S(2)}) collective-permute-start(bf16[256,512]{1,0:T(8,128)(2,1)} %fusion.11), channel_id=1, source_target_pairs={{0,2},{1,3},{2,0},{3,1},{4,6},{5,7},{6,4},{7,5},{8,10},{9,11},{10,... | collective-permute-start | bytes 786440 | tf_op jit(solution)/shard_map/grads_across/ppermute | solution.py:339
  188.6 17.5 %collective-permute-start.31 = (bf16[2,256,512]{2,1,0:T(8,128)(2,1)S(1)}, bf16[2,256,512]{2,1,0:T(8,128)(2,1)S(1)}, u32[]{:S(2)}, u32[]{:S(2)}) collective-permute-start(bf16[2,256,512]{2,1,0:T(8,128)(2,1)S(1)} %get-tuple-element.212), channel_id=1, source_target_pairs={{0,2},{1,3},{2,0},{3,1},{4,6},{5,7},{6,4},{7,5},{8,10},{9,11},{10,... | collective-permute-start | bytes 1572872 | tf_op jit(solution)/shard_map/grads_across/ppermute | solution.py:339
  190.3 15.8 %collective-permute-start.30 = (bf16[2,256,512]{2,1,0:T(8,128)(2,1)S(1)}, bf16[2,256,512]{2,1,0:T(8,128)(2,1)S(1)}, u32[]{:S(2)}, u32[]{:S(2)}) collective-permute-start(bf16[2,256,512]{2,1,0:T(8,128)(2,1)S(1)} %get-tuple-element.210), channel_id=1, source_target_pairs={{0,4},{1,5},{2,6},{3,7},{4,0},{5,1},{6,2},{7,3},{8,12},{9,13},{10,... | collective-permute-start | bytes 1572872 | tf_op jit(solution)/shard_map/grads_across/ppermute | solution.py:339
  192.1 5.5 %copy-start.15 = (f32[2,256,512]{2,1,0:T(8,128)S(1)}, f32[2,256,512]{2,1,0:T(8,128)}, u32[]{:S(2)}) copy-start(f32[2,256,512]{2,1,0:T(8,128)} %convert_add_fusion.8) | copy-start | bytes 3145732
  197.6 5.9 %copy-start.16 = (f32[2,256,512]{2,1,0:T(8,128)S(1)}, f32[2,256,512]{2,1,0:T(8,128)}, u32[]{:S(2)}) copy-start(f32[2,256,512]{2,1,0:T(8,128)} %convert_add_fusion.3) | copy-start | bytes 3145732
  197.7 12.4 %collective-permute-start.34 = (bf16[2,256,512]{2,1,0:T(8,128)(2,1)S(1)}, bf16[2,256,512]{2,1,0:T(8,128)(2,1)S(1)}, u32[]{:S(2)}, u32[]{:S(2)}) collective-permute-start(bf16[2,256,512]{2,1,0:T(8,128)(2,1)S(1)} %convert_element_type.279), channel_id=1, source_target_pairs={{0,8},{1,9},{2,10},{3,11},{4,12},{5,13},{6,14},{7,15}} | collective-permute-start | bytes 1572872 | tf_op jit(solution)/shard_map/grads_along_z/ppermute | solution.py:339
  202.8 7.2 %collective-permute-start.35 = (bf16[2,256,512]{2,1,0:T(8,128)(2,1)S(1)}, bf16[2,256,512]{2,1,0:T(8,128)(2,1)S(1)}, u32[]{:S(2)}, u32[]{:S(2)}) collective-permute-start(bf16[2,256,512]{2,1,0:T(8,128)(2,1)S(1)} %convert_element_type.279), channel_id=1, source_target_pairs={{24,16},{25,17},{26,18},{27,19},{28,20},{29,21},{30,22},{31,23}} | collective-permute-start | bytes 1572872 | tf_op jit(solution)/shard_map/grads_along_z/ppermute | solution.py:339
  210.1 24.8 %collective-permute-start.43 = (bf16[256,512]{1,0:T(8,128)(2,1)S(1)}, bf16[256,512]{1,0:T(8,128)(2,1)S(1)}, u32[]{:S(2)}, u32[]{:S(2)}) collective-permute-start(bf16[256,512]{1,0:T(8,128)(2,1)S(1)} %add_convert_fusion.6), channel_id=1, source_target_pairs={{0,16},{1,17},{2,18},{3,19},{4,20},{5,21},{6,22},{7,23},{8,24},{9,... | collective-permute-start | bytes 786440 | tf_op jit(solution)/shard_map/weight_grad/ppermute | solution.py:339
  226.5 9.2 %collective-permute-start.39 = (bf16[256,512]{1,0:T(8,128)(2,1)S(1)}, bf16[256,512]{1,0:T(8,128)(2,1)S(1)}, u32[]{:S(2)}, u32[]{:S(2)}) collective-permute-start(bf16[256,512]{1,0:T(8,128)(2,1)S(1)} %fusion.8), channel_id=1, source_target_pairs={{0,4},{1,5},{2,6},{3,7},{4,0},{5,1},{6,2},{7,3},{8,12},{9,13},{10,... | collective-permute-start | bytes 786440 | tf_op jit(solution)/shard_map/grads_across/ppermute | solution.py:339
  227.3 9.2 %collective-permute-start.40 = (bf16[256,512]{1,0:T(8,128)(2,1)S(1)}, bf16[256,512]{1,0:T(8,128)(2,1)S(1)}, u32[]{:S(2)}, u32[]{:S(2)}) collective-permute-start(bf16[256,512]{1,0:T(8,128)(2,1)S(1)} %fusion.9), channel_id=1, source_target_pairs={{0,2},{1,3},{2,0},{3,1},{4,6},{5,7},{6,4},{7,5},{8,10},{9,11},{10,... | collective-permute-start | bytes 786440 | tf_op jit(solution)/shard_map/grads_across/ppermute | solution.py:339
  228.0 11.6 %collective-permute-start.38 = (bf16[2,256,512]{2,1,0:T(8,128)(2,1)S(1)}, bf16[2,256,512]{2,1,0:T(8,128)(2,1)S(1)}, u32[]{:S(2)}, u32[]{:S(2)}) collective-permute-start(bf16[2,256,512]{2,1,0:T(8,128)(2,1)S(1)} %get-tuple-element.229), channel_id=1, source_target_pairs={{0,2},{1,3},{2,0},{3,1},{4,6},{5,7},{6,4},{7,5},{8,10},{9,11},{10,... | collective-permute-start | bytes 1572872 | tf_op jit(solution)/shard_map/grads_across/ppermute | solution.py:339
  229.7 17.4 %collective-permute-start.41 = (bf16[2,256,512]{2,1,0:T(8,128)(2,1)S(1)}, bf16[2,256,512]{2,1,0:T(8,128)(2,1)S(1)}, u32[]{:S(2)}, u32[]{:S(2)}) collective-permute-start(bf16[2,256,512]{2,1,0:T(8,128)(2,1)S(1)} %get-tuple-element.254), channel_id=1, source_target_pairs={{0,8},{1,9},{2,10},{3,11},{4,12},{5,13},{6,14},{7,15},{8,16},{9,17... | collective-permute-start | bytes 1572872 | tf_op jit(solution)/shard_map/grads_along_z/ppermute | solution.py:339
  234.8 12.0 %collective-permute-start.37 = (bf16[2,256,512]{2,1,0:T(8,128)(2,1)S(1)}, bf16[2,256,512]{2,1,0:T(8,128)(2,1)S(1)}, u32[]{:S(2)}, u32[]{:S(2)}) collective-permute-start(bf16[2,256,512]{2,1,0:T(8,128)(2,1)S(1)} %get-tuple-element.227), channel_id=1, source_target_pairs={{0,4},{1,5},{2,6},{3,7},{4,0},{5,1},{6,2},{7,3},{8,12},{9,13},{10,... | collective-permute-start | bytes 1572872 | tf_op jit(solution)/shard_map/grads_across/ppermute | solution.py:339
  235.8 11.3 %collective-permute-start.42 = (bf16[2,256,512]{2,1,0:T(8,128)(2,1)S(1)}, bf16[2,256,512]{2,1,0:T(8,128)(2,1)S(1)}, u32[]{:S(2)}, u32[]{:S(2)}) collective-permute-start(bf16[2,256,512]{2,1,0:T(8,128)(2,1)S(1)} %get-tuple-element.253), channel_id=1, source_target_pairs={{16,8},{17,9},{18,10},{19,11},{20,12},{21,13},{22,14},{23,15},{24,... | collective-permute-start | bytes 1572872 | tf_op jit(solution)/shard_map/grads_along_z/ppermute | solution.py:339
  247.1 6.4 %collective-permute-start.44 = (bf16[256,512]{1,0:T(8,128)(2,1)S(1)}, bf16[256,512]{1,0:T(8,128)(2,1)S(1)}, u32[]{:S(2)}, u32[]{:S(2)}) collective-permute-start(bf16[256,512]{1,0:T(8,128)(2,1)S(1)} %fusion.6), channel_id=1, source_target_pairs={{0,4},{1,5},{2,6},{3,7},{4,0},{5,1},{6,2},{7,3},{8,12},{9,13},{10,... | collective-permute-start | bytes 786440 | tf_op jit(solution)/shard_map/grads_across/ppermute | solution.py:339
  247.4 6.4 %collective-permute-start.45 = (bf16[256,512]{1,0:T(8,128)(2,1)S(1)}, bf16[256,512]{1,0:T(8,128)(2,1)S(1)}, u32[]{:S(2)}, u32[]{:S(2)}) collective-permute-start(bf16[256,512]{1,0:T(8,128)(2,1)S(1)} %fusion.7), channel_id=1, source_target_pairs={{0,2},{1,3},{2,0},{3,1},{4,6},{5,7},{6,4},{7,5},{8,10},{9,11},{10,... | collective-permute-start | bytes 786440 | tf_op jit(solution)/shard_map/grads_across/ppermute | solution.py:339
  248.7 9.7 %collective-permute-start.46 = (bf16[2,256,512]{2,1,0:T(8,128)(2,1)S(1)}, bf16[2,256,512]{2,1,0:T(8,128)(2,1)S(1)}, u32[]{:S(2)}, u32[]{:S(2)}) collective-permute-start(bf16[2,256,512]{2,1,0:T(8,128)(2,1)S(1)} %get-tuple-element.252), channel_id=1, source_target_pairs={{0,8},{1,9},{2,10},{3,11},{4,12},{5,13},{6,14},{7,15},{8,16},{9,17... | collective-permute-start | bytes 1572872 | tf_op jit(solution)/shard_map/grads_along_z/ppermute | solution.py:339
  251.8 11.1 %collective-permute-start.47 = (bf16[2,256,512]{2,1,0:T(8,128)(2,1)S(1)}, bf16[2,256,512]{2,1,0:T(8,128)(2,1)S(1)}, u32[]{:S(2)}, u32[]{:S(2)}) collective-permute-start(bf16[2,256,512]{2,1,0:T(8,128)(2,1)S(1)} %get-tuple-element.251), channel_id=1, source_target_pairs={{8,0},{9,1},{10,2},{11,3},{12,4},{13,5},{14,6},{15,7},{16,8},{17,9... | collective-permute-start | bytes 1572872 | tf_op jit(solution)/shard_map/grads_along_z/ppermute | solution.py:339
  262.9 1.5 collective-permute-start.48
  (2 other events, 1.3 us)

commit v3 on v0

v3 whole, which is shorter than its diff:
```python
import functools

import jax
import jax.numpy as jnp
from jax import lax
from jax.experimental import pallas as pl
from jax.experimental.pallas import tpu as pltpu
from jax.sharding import PartitionSpec as P

BF16 = jnp.bfloat16
F32 = jnp.float32
BOTH = ("section", "rep")


def dense_kernel(where_ref, count_ref, rows_ref, cols_ref, tiles_ref, out_ref, *send_refs):
    panel = pl.program_id(0)
    size = tiles_ref.shape[-1]
    per_part = out_ref.shape[-1] // size
    out_ref[...] = jnp.zeros_like(out_ref)

    def add_tile(slot, carry):
        row = pl.multiple_of(rows_ref[panel, slot] * size, size)
        tile_col = cols_ref[panel, slot]
        part = tile_col // per_part
        col = pl.multiple_of((tile_col % per_part) * size, size)
        out_ref[part, 0, pl.ds(row, size), pl.ds(col, size)] += tiles_ref[0, slot]
        return carry

    lax.fori_loop(0, count_ref[panel], add_tile, 0)
    for shift, send_ref in enumerate(send_refs, 1):
        send_ref[0] = out_ref[where_ref[0] ^ shift, 0]


def make_dense(where, tiles, rows, cols, count, block_rows, n_rep):
    panels, slots, size, _ = tiles.shape
    part = block_rows // n_rep
    sent = jax.ShapeDtypeStruct((panels, block_rows, part), BF16)
    return pl.pallas_call(
        dense_kernel,
        out_shape=[jax.ShapeDtypeStruct((n_rep, panels, block_rows, part), BF16)]
        + [sent] * (n_rep - 1),
        grid_spec=pltpu.PrefetchScalarGridSpec(
            num_scalar_prefetch=4,
            grid=(panels,),
            in_specs=[pl.BlockSpec((1, slots, size, size), lambda p, *_: (p, 0, 0, 0))],
            out_specs=[pl.BlockSpec((n_rep, 1, block_rows, part), lambda p, *_: (0, p, 0, 0))]
            + [pl.BlockSpec((1, block_rows, part), lambda p, *_: (p, 0, 0))] * (n_rep - 1),
        ),
        compiler_params=pltpu.CompilerParams(vmem_limit_bytes=40 * 2**20),
        cost_estimate=pl.CostEstimate(
            flops=0,
            transcendentals=0,
            bytes_accessed=tiles.size * 2 + panels * block_rows * block_rows * 3,
        ),
    )(where, count, rows, cols, tiles)


def forward_kernel(offset, n_units, has_total, where_ref, *refs):
    dense_ref, others_ref = refs[:2]
    units = refs[2 : 2 + n_units]
    refs = refs[2 + n_units :]
    total_ref, refs = (refs[0], refs[1:]) if has_total else (None, refs)
    out_ref, sum_ref, a_buf, u_buf, sems = refs
    _, panels, _, part = dense_ref.shape
    rep = where_ref[0]

    def a_copy(source, slot, side):
        target = a_buf.at[slot, :, pl.ds(side * part, part)]
        return pltpu.make_async_copy(source, target, sems.at[0, slot, side])

    def u_copy(source, slot, side):
        target = u_buf.at[slot, pl.ds(side * part, part), :]
        return pltpu.make_async_copy(source, target, sems.at[1, slot, side])

    def fetch(pair, slot):
        for side in range(2):
            place = where_ref[offset + 2 * pair + side]
            owner, panel = place // panels, place % panels
            mine = owner == rep
            turn = jnp.maximum((owner ^ rep) - 1, 0)

            @pl.when(mine)
            def _():
                a_copy(dense_ref.at[rep, panel], slot, side).start()

            @pl.when(jnp.logical_not(mine))
            def _():
                a_copy(others_ref.at[turn, panel], slot, side).start()

            for number in range(side, n_units, 2):

                @pl.when(pair == number // 2)
                def _():
                    u_copy(units[number], slot, side).start()

    pairs = n_units // 2
    fetch(0, 0)
    sum_ref[...] = total_ref[...] if has_total else jnp.zeros_like(sum_ref)

    def step(pair, carry):
        slot = pair % 2

        @pl.when(pair + 1 < pairs)
        def _():
            fetch(pair + 1, 1 - slot)

        for side in range(2):
            a_copy(dense_ref.at[0, 0], slot, side).wait()
            u_copy(units[0], slot, side).wait()
        sum_ref[...] += jnp.dot(a_buf[slot], u_buf[slot], preferred_element_type=F32)
        return carry

    lax.fori_loop(0, pairs, step, 0)
    out_ref[...] = sum_ref[...].astype(out_ref.dtype)


def forward_part(where, offset, units, total, dense, others, kind):
    part, width = units[0].shape
    rows = dense.shape[2]
    hbm = pl.BlockSpec(memory_space=pl.ANY)
    whole = pl.BlockSpec((rows, width), lambda i, where: (0, 0))
    has_total = total is not None
    n_units = len(units)
    return pl.pallas_call(
        functools.partial(forward_kernel, offset, n_units, has_total),
        out_shape=jax.ShapeDtypeStruct((rows, width), kind),
        grid_spec=pltpu.PrefetchScalarGridSpec(
            num_scalar_prefetch=1,
            grid=(1,),
            in_specs=[hbm] * (2 + n_units) + [whole] * has_total,
            out_specs=whole,
            scratch_shapes=[
                pltpu.VMEM((rows, width), F32),
                pltpu.VMEM((2, rows, 2 * part), BF16),
                pltpu.VMEM((2, 2 * part, width), BF16),
                pltpu.SemaphoreType.DMA((2, 2, 2)),
            ],
        ),
        compiler_params=pltpu.CompilerParams(vmem_limit_bytes=50 * 2**20),
        cost_estimate=pl.CostEstimate(
            flops=2 * n_units * rows * part * width,
            transcendentals=0,
            bytes_accessed=n_units * rows * part * 2 + 8 * rows * width,
        ),
    )(where, dense, others, *units, *([total] if has_total else []))


def middle_kernel(
    where_ref, mine_ref, other_ref, weight_ref, cot_ref, grad_ref, act_ref, term_ref, sum_ref
):
    agg = (mine_ref[...].astype(F32) + other_ref[...].astype(F32)).astype(BF16)
    pre = jnp.dot(agg, weight_ref[...], preferred_element_type=F32)
    sigma = jax.nn.sigmoid(pre)
    act_ref[...] = (pre * sigma).astype(BF16)
    slope = cot_ref[...].astype(F32) * sigma * (1.0 + pre * (1.0 - sigma))
    pre_grad = slope.astype(BF16)
    grad_ref[...] = lax.dot_general(
        weight_ref[...], pre_grad, (((1,), (1,)), ((), ())), preferred_element_type=F32
    ).astype(BF16)
    term = lax.dot_general(
        agg, pre_grad, (((0,), (0,)), ((), ())), preferred_element_type=F32
    )
    step = pl.program_id(0)

    @pl.when(step == 0)
    def _():
        sum_ref[...] = term

    @pl.when(step > 0)
    def _():
        sum_ref[...] += term

    @pl.when(step == pl.num_programs(0) - 1)
    def _():
        size = term_ref.shape[0]
        start = pl.multiple_of(where_ref[0] * size, size)
        term_ref[...] = sum_ref[pl.ds(start, size), :].astype(BF16)


def middle(where, mine, other, weight, cotangent, n_rep):
    rows, width = mine.shape
    part = rows // n_rep
    block = lambda i, where: ((where[0] + 1 + i) % n_rep, 0)
    last = pl.BlockSpec((part, width), lambda i, where: (0, 0))
    return pl.pallas_call(
        middle_kernel,
        out_shape=[
            jax.ShapeDtypeStruct((width, rows), BF16),
            jax.ShapeDtypeStruct((part, width), BF16),
            jax.ShapeDtypeStruct((width // n_rep, width), BF16),
        ],
        grid_spec=pltpu.PrefetchScalarGridSpec(
            num_scalar_prefetch=1,
            grid=(n_rep,),
            in_specs=[
                pl.BlockSpec((part, width), block),
                pl.BlockSpec((part, width), block),
                pl.BlockSpec((width, width), lambda i, where: (0, 0)),
                pl.BlockSpec((part, width), block),
            ],
            out_specs=[
                pl.BlockSpec((width, part), lambda i, where: (0, block(i, where)[0])),
                last,
                pl.BlockSpec((width // n_rep, width), lambda i, where: (0, 0)),
            ],
            scratch_shapes=[pltpu.VMEM((width, width), F32)],
        ),
        compiler_params=pltpu.CompilerParams(vmem_limit_bytes=40 * 2**20),
        cost_estimate=pl.CostEstimate(
            flops=6 * rows * width * width,
            transcendentals=rows * width,
            bytes_accessed=rows * width * 10,
        ),
    )(where, mine, other, weight, cotangent)


def backward_kernel(where_ref, grad_ref, a_ref, *out_refs):
    chunk = jnp.dot(grad_ref[...], a_ref[0, 0], preferred_element_type=F32).astype(BF16)
    for number, out_ref in enumerate(out_refs):

        @pl.when(pl.program_id(0) == number)
        def _():
            out_ref[...] = chunk


def backward_part(where, offset, count, grad, dense):
    width, rows = grad.shape
    n_rep, _, _, cols = dense.shape

    def a_block(i, where):
        place = where[offset + i]
        return (place % n_rep, place // n_rep, 0, 0)

    return pl.pallas_call(
        backward_kernel,
        out_shape=[jax.ShapeDtypeStruct((width, cols), BF16)] * count,
        grid_spec=pltpu.PrefetchScalarGridSpec(
            num_scalar_prefetch=1,
            grid=(count,),
            in_specs=[
                pl.BlockSpec((width, rows), lambda i, where: (0, 0)),
                pl.BlockSpec((1, 1, rows, cols), a_block),
            ],
            out_specs=[pl.BlockSpec((width, cols), lambda i, where: (0, 0))] * count,
        ),
        compiler_params=pltpu.CompilerParams(vmem_limit_bytes=50 * 2**20),
        cost_estimate=pl.CostEstimate(
            flops=2 * count * rows * width * cols,
            transcendentals=0,
            bytes_accessed=2 * count * rows * cols + 2 * count * width * cols + 2 * width * rows,
        ),
    )(where, grad, dense)


def shards(sizes, features, weight, tile_values, tile_rows, tile_cols, tile_count, cotangent):
    n_section, n_rep = sizes
    block_rows, width = features.shape
    part = block_rows // n_rep
    section, rep = lax.axis_index("section"), lax.axis_index("rep")

    X, Y, Z = 1, 2, 4
    pair_count = n_section // 8
    low_bit = lambda mask: mask & -mask

    def flip(value, mask, rep_mask=0):
        pairs = [
            (s * n_rep + r, (s ^ mask) * n_rep + (r ^ rep_mask))
            for s in range(n_section)
            for r in range(n_rep)
        ]
        return lax.ppermute(value, BOTH, pairs)

    def gather_rep(value):
        held = [value] + [flip(value, 0, other) for other in range(1, n_rep)]
        order = rep ^ jnp.arange(n_rep)
        if n_rep == 2:
            held = [jnp.where(rep == 0, held[0], held[1]), jnp.where(rep == 0, held[1], held[0])]
            return jnp.concatenate(held)
        return jnp.stack(held)[order].reshape(-1, width)

    live = {}

    def close(*open_names):
        names = [name for name in live if name not in open_names]
        live.update(zip(names, lax.optimization_barrier([live[name] for name in names])))

    masks, offsets = [], {}

    def plan(name, wanted):
        offsets[name] = 1 + len(masks)
        masks.extend(wanted)

    for pair in range(pair_count):
        even, odd = 2 * pair * Z, (2 * pair + 1) * Z
        plan(("units", pair), [even, even + X, even + Y, odd, odd + X, odd + Y])
        plan(("crossed", pair), [even + X + Y, odd + X + Y])
        plan(("first", pair), [odd + X + Y, even + X + Y])
        plan(("odd", pair), [odd + X, odd + Y, odd])
        plan(("even", pair), [even + X, even + Y, even])
    where = jnp.concatenate([rep[None], section ^ jnp.array(masks, jnp.int32)]).astype(jnp.int32)

    def forward_step(names, units, total, kind=F32):
        with jax.named_scope("forward"):
            return forward_part(
                where, offsets[names], units, total, live["dense"], live["others"], kind
            )

    live[0] = lax.dynamic_slice_in_dim(features, rep * part, part, axis=0)
    total = None
    for pair in range(pair_count):
        even, odd = 2 * pair * Z, (2 * pair + 1) * Z
        later = even + 2 * Z
        last = pair + 1 == pair_count

        with jax.named_scope("features_across"):
            live["even_x"], live["even_y"] = flip(live[even], X), flip(live[even], Y)
        with jax.named_scope("features_along_z"):
            live[odd] = flip(live[even], Z)
        if pair == 0:
            with jax.named_scope("dense_blocks"):
                live["dense"], *live["sent"] = make_dense(
                    where,
                    tile_values[0],
                    tile_rows[0],
                    tile_cols[0],
                    tile_count[0],
                    block_rows,
                    n_rep,
                )
        else:
            live["total"] = forward_step(*waiting, live.pop("waiting"), live.get("total"))
        close()

        with jax.named_scope("features_across"):
            live["odd_x"], live["odd_y"] = flip(live[odd], X), flip(live[odd], Y)
        if pair == 0:
            with jax.named_scope("dense_exchange"):
                others = [flip(value, 0, n) for n, value in enumerate(live.pop("sent"), 1)]
                live["others"] = others[0][None] if n_rep == 2 else jnp.stack(others)
        if not last:
            with jax.named_scope("features_along_z"):
                live[later] = flip(live[later - low_bit(later)], low_bit(later))
        if last:
            with jax.named_scope("cotangent_rows"):
                live["cotangent"] = gather_rep(cotangent)
        close(*([] if last else [later]), *([] if pair else ["others"]))

        with jax.named_scope("features_across"):
            crossed = [flip(live["even_x"], Y), flip(live["odd_y"], X)]
        units = [live[even], live.pop("even_x"), live.pop("even_y")]
        units += [live[odd], live.pop("odd_x"), live.pop("odd_y")]
        if pair > 0:
            live["total"] = forward_step(("units", pair), units, live["total"])
            live["waiting"] = crossed
            waiting = [("crossed", pair)]
        else:
            live["waiting"] = units + crossed
            waiting = [("units", pair)]
        close()
    partial = forward_step(*waiting, live["waiting"], live.get("total"), BF16)

    with jax.named_scope("partial_sums"):
        other = flip(partial, 0, 1)
        for bit in range(1, n_rep.bit_length() - 1):
            partial = (partial.astype(F32) + other.astype(F32)).astype(BF16)
            other = flip(partial, 0, 1 << bit)

    with jax.named_scope("middle"):
        grad, activated, term = middle(where, partial, other, weight, live["cotangent"], n_rep)

    def backward_step(name, count):
        with jax.named_scope("backward"):
            return backward_part(where, offsets[name], count, live["grad"], live["dense"])

    add = lambda *values: functools.reduce(jnp.add, [value.astype(F32) for value in values])
    term_masks = [*(1 << bit for bit in range(2, n_section.bit_length() - 1)), X, Y]

    def end_phase(*open_names):
        if term_masks:
            with jax.named_scope("weight_grad"):
                mask = term_masks.pop(0)
                live["term"] = add(live["term"], flip(live["term"], mask)).astype(BF16)
        elif "weight_grad" not in live:
            with jax.named_scope("weight_grad"):
                live["weight_grad"] = gather_rep(live.pop("term"))
        close(*open_names)

    live = {"grad": grad, "dense": live["dense"], "term": term}
    live["first"] = backward_step(("first", pair_count - 1), 2)
    for pair in reversed(range(pair_count)):
        even = 2 * pair * Z
        passing = [name for name in live if isinstance(name, tuple)]

        with jax.named_scope("grads_across"):
            odd_diag, even_diag = live.pop("first")
            live["odd_diag"], live["even_diag"] = flip(odd_diag, Y), flip(even_diag, X)
        live["odd"] = backward_step(("odd", pair), 3)
        if "passed" in live:
            with jax.named_scope("grads_along_z"):
                mask = low_bit(even + 2 * Z)
                target = even + 2 * Z - mask
                live["to", target, mask] = flip(live.pop("passed"), mask)
                passing = [("to", target, mask)]
        end_phase(*passing)

        with jax.named_scope("grads_across"):
            to_x, to_y, own = live.pop("odd")
            to_x = add(to_x, live.pop("odd_diag")).astype(BF16)
            live["odd_sum"] = [own, flip(to_x, X), flip(to_y, Y)]
        live["even"] = backward_step(("even", pair), 3)
        end_phase()

        with jax.named_scope("grads_across"):
            to_x, to_y, own = live.pop("even")
            to_y = add(to_y, live.pop("even_diag")).astype(BF16)
            live["even_sum"] = [own, flip(to_x, X), flip(to_y, Y)]
        with jax.named_scope("grads_along_z"):
            odd_sum = add(*live.pop("odd_sum")).astype(BF16)
            live["even_sum"].append(flip(odd_sum, Z))
        if pair > 0:
            live["first"] = backward_step(("first", pair - 1), 2)
        end_phase()
        arrived = [name for name in live if isinstance(name, tuple) and name[1] == even]
        total = add(*live.pop("even_sum"), *(live.pop(name) for name in arrived)).astype(BF16)
        if pair > 0:
            live["passed"] = total
    with jax.named_scope("grads_out"):
        feat_grad = total.T
    return (activated, feat_grad[None], live["weight_grad"].astype(F32))


def solution(mesh):
    placed = (
        P("section", None),
        P(),
        P("section", "rep", None, None, None),
        P("section", "rep", None),
        P("section", "rep", None),
        P("section", "rep"),
        P(("section", "rep"), None),
    )
    sizes = (mesh.shape["section"], mesh.shape["rep"])
    return jax.shard_map(
        functools.partial(shards, sizes),
        mesh=mesh,
        in_specs=placed,
        out_specs=(P(("section", "rep"), None), P("rep", "section", None), P()),
        check_vma=False,
    )
```

time: 857 us -> 210 us (0.25); the launches traced: 846 us -> 209 us
  waiting for transfers between devices: 463 us -> 84.9 us
  matrix products: 192 us -> 0 us
  local copies, waits for them, and re-layouts: 172 us -> 8.65 us
  Pallas kernels: 0 us -> 63.1 us
  starting transfers between devices: 0.21 us -> 46.5 us
  between operations: 14.6 us -> 0.91 us
    psum x2 -> x0, waiting for transfers between devices: 268 us -> none  [the longest x1 267 us: from_root(): return lax.psum(kept, axis)]
    dot_general x35 -> x0, matrix products: 192 us -> none  [the longest x8 51.6 us: shards(): jnp.einsum('ki,kaf->iaf', row_select[panel_pos], product, precision=lax.P...]
    reduce_scatter x2 -> x0, waiting for transfers between devices: 187 us -> none  [the longest x1 179 us: shards(): lax.psum_scatter(stacked.astype(jnp.bfloat16), 'section', scatter_dimensi...]
    dot_general x16 -> x0, local copies, waits for them, and re-layouts: 109 us -> none  [the longest x8 54.4 us: shards(): jnp.einsum('kab,kbf->kaf', tile_values[0, panel_pos], picked, preferred_e...]
    ppermute x0 -> x38, waiting for transfers between devices: none -> 84.9 us  [flip(): return lax.ppermute(value, BOTH, pairs)]
    pallas_call x0 -> x11, Pallas kernels: none -> 63.1 us  [the longest x6 25.2 us: backward_part(): pl.pallas_call(backward_kernel, out_shape=[jax.ShapeDtypeStruct((width, c...]
    ppermute x0 -> x38, starting transfers between devices: none -> 46.5 us  [flip(): return lax.ppermute(value, BOTH, pairs)]
    gather x16 -> x0, local copies, waits for them, and re-layouts: 42.6 us -> none  [the longest x8 21.5 us: shards(): jnp.take(source.reshape(row_tiles, tile_size, feat_width), tile_cols[0, p...]
  transfers between devices with their start and end apart: 5 -> 38, of which waited for: 4 -> 24; matrix products, arithmetic and copies ran while one was open for 21% -> 2% of each run, Pallas kernels for 0% -> 24%
where the time goes in v3:
time: 210 us; the launch traced here: 209 us
  waiting for transfers between devices  84.9 us (40%)
  Pallas kernels  63.1 us (30%)
  starting transfers between devices  46.5 us (22%)
  local copies, waits for them, and re-layouts  8.65 us (4%)
  other arithmetic  5.18 us (2%)
    ppermute x38, waiting for transfers between devices, flip(): return lax.ppermute(value, BOTH, pairs)  84.9 us
    ppermute x38, starting transfers between devices, flip(): return lax.ppermute(value, BOTH, pairs)  46.5 us
    pallas_call x6, Pallas kernels, backward_part(): pl.pallas_call(backward_kernel, out_shape=[jax.ShapeDtypeStruct((width, c...  25.2 us
    pallas_call x3, Pallas kernels, forward_part(): pl.pallas_call(functools.partial(forward_kernel, offset, n_units, has_tot...  23.6 us
    pallas_call x1, Pallas kernels, make_dense(): pl.pallas_call(dense_kernel, out_shape=[jax.ShapeDtypeStruct((n_rep, pane...  9.92 us
    unnamed x23, local copies, waits for them, and re-layouts  8.62 us
    pallas_call x1, Pallas kernels, middle(): pl.pallas_call(middle_kernel, out_shape=[jax.ShapeDtypeStruct((width, row...  4.39 us
  transfers between devices with their start and end apart: 38, of which 24 were waited for; matrix products, arithmetic and copies ran while one was open for 2% of the time, Pallas kernels for 24%

profile of v3, /device:TPU:0, one launch (start us, length us, event | category | flops | bytes accessed | tf_op | source)
XLA Modules:
  0.0 209.2 jit_solution(16347829056596726870)
XLA Ops:
  0.7 1.2 copy-done
  1.9 3.0 %collective-permute-start = (bf16[512,512]{1,0:T(8,128)(2,1)S(1)}, bf16[512,512]{1,0:T(8,128)(2,1)S(1)}, u32[]{:S(2)}, u32[]{:S(2)}) collective-permute-start(bf16[512,512]{1,0:T(8,128)(2,1)S(1)} %constant_dynamic-slice_fusion.refs_2_), channel_id=1, source_target_pairs={{0,2},{1,3},{2,0},{3,1},{4,6},{5,7},{6,4},{7,5},{8,10},{9,11},{10,... | collective-permute-start | bytes 1572872 | tf_op jit(solution)/shard_map/features_across/ppermute | solution.py:271
  4.9 1.5 collective-permute-start.1
  6.4 1.6 collective-permute-start.2
  8.7 2.8 %copy-done.2 = bf16[1,8,24,128,128]{4,3,2,1,0:T(8,128)(2,1)S(1)} copy-done((bf16[1,8,24,128,128]{4,3,2,1,0:T(8,128)(2,1)S(1)}, bf16[1,8,24,128,128]{4,3,2,1,0:T(8,128)(2,1)}, u32[]{:S(2)}) %copy-start.2) | copy-done | bytes 6291480
  11.5 0.7 copy-done.5
  12.2 0.7 copy-done.6
  13.6 9.9 %dense_blocks.1 = (bf16[2,8,1024,512]{3,2,1,0:T(8,128)(2,1)}, bf16[8,1024,512]{2,1,0:T(8,128)(2,1)}) custom-call(s32[33]{0:T(128)S(1)} %pad_add_fusion.where_ref, s32[8]{0:T(128)S(1)} %bitcast.13, s32[8,24]{1,0:T(8,128)S(1)} %bitcast.11, s32[8,24]{1,0:T(8,128)S(1)} %bitcast.12, bf16[8,24,128,128]{3,2,1,0:T(8,128)(2,1)S(1)} %bitcast.10), custom_call_target="tpu_custom_call" | custom-call | bytes 31457280 | tf_op jit(solution)/shard_map/dense_blocks/pallas_call | solution.py:38
  23.6 1.6 collective-permute-start.3
  25.1 3.2 %collective-permute-start.6 = (bf16[512,512]{1,0:T(8,128)(2,1)S(1)}, bf16[512,512]{1,0:T(8,128)(2,1)S(1)}, u32[]{:S(2)}, u32[]{:S(2)}) collective-permute-start(bf16[512,512]{1,0:T(8,128)(2,1)S(1)} %constant_dynamic-slice_fusion.refs_2_), channel_id=1, source_target_pairs={{0,16},{1,17},{2,18},{3,19},{4,20},{5,21},{6,22},{7,23},{8,24},{9,... | collective-permute-start | bytes 1572872 | tf_op jit(solution)/shard_map/features_along_z/ppermute | solution.py:271
  28.4 9.6 %collective-permute-done.3.refs_6_ = bf16[512,512]{1,0:T(8,128)(2,1)S(1)} collective-permute-done((bf16[512,512]{1,0:T(8,128)(2,1)S(1)}, bf16[512,512]{1,0:T(8,128)(2,1)S(1)}, u32[]{:S(2)}, u32[]{:S(2)}) %collective-permute-start.3) | collective-permute-done | bytes 524320 | tf_op jit(solution)/shard_map/features_across/ppermute | solution.py:271
  37.9 1.2 collective-permute-done.4.refs_7_
  39.4 1.3 collective-permute-start.8
  40.7 9.8 %collective-permute-done.6.refs_2_ = bf16[512,512]{1,0:T(8,128)(2,1)S(1)} collective-permute-done((bf16[512,512]{1,0:T(8,128)(2,1)S(1)}, bf16[512,512]{1,0:T(8,128)(2,1)S(1)}, u32[]{:S(2)}, u32[]{:S(2)}) %collective-permute-start.6) | collective-permute-done | bytes 524320 | tf_op jit(solution)/shard_map/features_along_z/ppermute | solution.py:271
  50.5 1.8 collective-permute-done.7.refs_8_
  52.6 1.0 collective-permute-start.9
  53.7 1.1 collective-permute-start.10
  55.3 0.8 copy-done.9
  56.1 9.2 %forward.3.refs_8_ = f32[1024,512]{1,0:T(8,128)} custom-call(s32[33]{0:T(128)S(1)} %pad_add_fusion.where_ref, bf16[2,8,1024,512]{3,2,1,0:T(8,128)(2,1)} %get-tuple-element.210.refs_0_.a_ref, bf16[1,8,1024,512]{3,2,1,0:T(8,128)(2,1)} %bitcast.14, bf16[512,512]{1,0:T(8,128)(2,1)S(1)} %constant_dynamic-slice_fusion.refs_2_, ...), custom_call_target="tpu_custom_call" | custom-call | flops 4294967296 | bytes 12582912 | tf_op jit(solution)/shard_map/forward/pallas_call | solution.py:124
  65.7 0.8 copy-done.3
  66.5 0.7 collective-permute-done.11.refs_5_
  67.7 1.0 collective-permute-start.13
  68.7 1.3 broadcast_select_fusion.1
  70.1 9.8 %collective-permute-done.12.refs_6_ = bf16[512,512]{1,0:T(8,128)(2,1)S(1)} collective-permute-done((bf16[512,512]{1,0:T(8,128)(2,1)}, bf16[512,512]{1,0:T(8,128)(2,1)S(1)}, u32[]{:S(2)}, u32[]{:S(2)}) %collective-permute-start.12) | collective-permute-done | bytes 524320 | tf_op jit(solution)/shard_map/features_across/ppermute | solution.py:271
  81.1 1.0 collective-permute-start.16
  82.0 9.4 %forward.4.refs_4_ = f32[1024,512]{1,0:T(8,128)} custom-call(s32[33]{0:T(128)S(1)} %pad_add_fusion.where_ref, bf16[2,8,1024,512]{3,2,1,0:T(8,128)(2,1)} %get-tuple-element.210.refs_0_.a_ref, bf16[1,8,1024,512]{3,2,1,0:T(8,128)(2,1)} %bitcast.15, bf16[512,512]{1,0:T(8,128)(2,1)S(1)} %collective-permute-done.6.refs_2_, ...), custom_call_target="tpu_custom_call" | custom-call | flops 3221225472 | bytes 10485760 | tf_op jit(solution)/shard_map/forward/pallas_call | solution.py:124
  91.4 0.7 collective-permute-done.15.refs_2_
  92.1 5.0 %forward.5.mine_ref = bf16[1024,512]{1,0:T(8,128)(2,1)S(1)} custom-call(s32[33]{0:T(128)S(1)} %pad_add_fusion.where_ref, bf16[2,8,1024,512]{3,2,1,0:T(8,128)(2,1)} %get-tuple-element.210.refs_0_.a_ref, bf16[1,8,1024,512]{3,2,1,0:T(8,128)(2,1)} %bitcast.16, bf16[512,512]{1,0:T(8,128)(2,1)S(1)} %collective-permute-done.15.refs_2_, ...), custom_call_target="tpu_custom_call" | custom-call | flops 1073741824 | bytes 6291456 | tf_op jit(solution)/shard_map/forward/pallas_call | solution.py:124
  97.2 2.6 %collective-permute-done.17.other_ref = bf16[1024,512]{1,0:T(8,128)(2,1)S(1)} collective-permute-done((bf16[1024,512]{1,0:T(8,128)(2,1)S(1)}, bf16[1024,512]{1,0:T(8,128)(2,1)S(1)}, u32[]{:S(2)}, u32[]{:S(2)}) %collective-permute-start.17) | collective-permute-done | bytes 1048608 | tf_op jit(solution)/shard_map/partial_sums/ppermute | solution.py:271
  99.8 4.4 %middle.1 = (bf16[512,1024]{1,0:T(8,128)(2,1)S(1)}, bf16[512,512]{1,0:T(8,128)(2,1)}, bf16[256,512]{1,0:T(8,128)(2,1)S(1)}) custom-call(s32[33]{0:T(128)S(1)} %pad_add_fusion.where_ref, bf16[1024,512]{1,0:T(8,128)(2,1)S(1)} %forward.5.mine_ref, bf16[1024,512]{1,0:T(8,128)(2,1)S(1)} %collective-permute-done.17.other_ref, bf16[512,512]{1,0:T(8,128)(2,1)S(1)} %copy-done.8, ...), custom_call_target="tpu_custom_call" | custom-call | flops 1610612736 | bytes 5242880 | tf_op jit(solution)/shard_map/middle/pallas_call | solution.py:185
  104.2 3.4 %backward.6 = (bf16[512,512]{1,0:T(8,128)(2,1)S(1)}, bf16[512,512]{1,0:T(8,128)(2,1)S(1)}) custom-call(s32[33]{0:T(128)S(1)} %pad_add_fusion.where_ref, bf16[512,1024]{1,0:T(8,128)(2,1)S(1)} %get-tuple-element.209.grad_ref, bf16[2,8,1024,512]{3,2,1,0:T(8,128)(2,1)} %get-tuple-element.210.refs_0_.a_ref), custom_call_target="tpu_custom_call" | custom-call | flops 1073741824 | bytes 4194304 | tf_op jit(solution)/shard_map/backward/pallas_call | solution.py:234
  107.6 1.8 collective-permute-start.19
  109.4 0.9 collective-permute-start.20
  110.4 3.3 %collective-permute-start.18 = (bf16[256,512]{1,0:T(8,128)(2,1)S(1)}, bf16[256,512]{1,0:T(8,128)(2,1)S(1)}, u32[]{:S(2)}, u32[]{:S(2)}) collective-permute-start(bf16[256,512]{1,0:T(8,128)(2,1)S(1)} %get-tuple-element.172), channel_id=1, source_target_pairs={{0,8},{1,9},{2,10},{3,11},{4,12},{5,13},{6,14},{7,15},{8,0},{9,1},... | collective-permute-start | bytes 786440 | tf_op jit(solution)/shard_map/weight_grad/ppermute | solution.py:271
  113.7 4.6 %backward.7 = (bf16[512,512]{1,0:T(8,128)(2,1)S(1)}, bf16[512,512]{1,0:T(8,128)(2,1)S(1)}, bf16[512,512]{1,0:T(8,128)(2,1)S(1)}) custom-call(s32[33]{0:T(128)S(1)} %pad_add_fusion.where_ref, bf16[512,1024]{1,0:T(8,128)(2,1)S(1)} %get-tuple-element.209.grad_ref, bf16[2,8,1024,512]{3,2,1,0:T(8,128)(2,1)} %get-tuple-element.210.refs_0_.a_ref), custom_call_target="tpu_custom_call" | custom-call | flops 1610612736 | bytes 5767168 | tf_op jit(solution)/shard_map/backward/pallas_call | solution.py:234
  118.3 1.4 collective-permute-done.18
  119.8 1.9 collective-permute-done.19
  121.7 1.4 collective-permute-done.20
  123.3 1.0 collective-permute-start.22
  124.6 3.2 %collective-permute-start.21 = (bf16[256,512]{1,0:T(8,128)(2,1)S(1)}, bf16[256,512]{1,0:T(8,128)(2,1)S(1)}, u32[]{:S(2)}, u32[]{:S(2)}) collective-permute-start(bf16[256,512]{1,0:T(8,128)(2,1)S(1)} %add_convert_fusion.11), channel_id=1, source_target_pairs={{0,16},{1,17},{2,18},{3,19},{4,20},{5,21},{6,22},{7,23},{8,24},{9,... | collective-permute-start | bytes 786440 | tf_op jit(solution)/shard_map/weight_grad/ppermute | solution.py:271
  127.8 4.6 %backward.8 = (bf16[512,512]{1,0:T(8,128)(2,1)S(1)}, bf16[512,512]{1,0:T(8,128)(2,1)S(1)}, bf16[512,512]{1,0:T(8,128)(2,1)S(1)}) custom-call(s32[33]{0:T(128)S(1)} %pad_add_fusion.where_ref, bf16[512,1024]{1,0:T(8,128)(2,1)S(1)} %get-tuple-element.209.grad_ref, bf16[2,8,1024,512]{3,2,1,0:T(8,128)(2,1)} %get-tuple-element.210.refs_0_.a_ref), custom_call_target="tpu_custom_call" | custom-call | flops 1610612736 | bytes 5767168 | tf_op jit(solution)/shard_map/backward/pallas_call | solution.py:234
  132.5 6.1 %collective-permute-done.21 = bf16[256,512]{1,0:T(8,128)(2,1)S(1)} collective-permute-done((bf16[256,512]{1,0:T(8,128)(2,1)S(1)}, bf16[256,512]{1,0:T(8,128)(2,1)S(1)}, u32[]{:S(2)}, u32[]{:S(2)}) %collective-permute-start.21) | collective-permute-done | bytes 262176 | tf_op jit(solution)/shard_map/weight_grad/ppermute | solution.py:271
  139.5 1.5 collective-permute-start.26
  141.2 1.4 collective-permute-start.27
  142.6 0.9 collective-permute-start.24
  143.5 3.4 %backward.9 = (bf16[512,512]{1,0:T(8,128)(2,1)S(1)}, bf16[512,512]{1,0:T(8,128)(2,1)S(1)}) custom-call(s32[33]{0:T(128)S(1)} %pad_add_fusion.where_ref, bf16[512,1024]{1,0:T(8,128)(2,1)S(1)} %get-tuple-element.209.grad_ref, bf16[2,8,1024,512]{3,2,1,0:T(8,128)(2,1)} %get-tuple-element.210.refs_0_.a_ref), custom_call_target="tpu_custom_call" | custom-call | flops 1073741824 | bytes 4194304 | tf_op jit(solution)/shard_map/backward/pallas_call | solution.py:234
  146.9 9.3 %collective-permute-done.24 = bf16[256,512]{1,0:T(8,128)(2,1)S(1)} collective-permute-done((bf16[256,512]{1,0:T(8,128)(2,1)S(1)}, bf16[256,512]{1,0:T(8,128)(2,1)S(1)}, u32[]{:S(2)}, u32[]{:S(2)}) %collective-permute-start.24) | collective-permute-done | bytes 262176 | tf_op jit(solution)/shard_map/weight_grad/ppermute | solution.py:271
  156.3 1.2 collective-permute-start.28
  157.6 0.9 collective-permute-start.29
  159.1 1.6 collective-permute-start.31
  160.7 4.6 %backward.10 = (bf16[512,512]{1,0:T(8,128)(2,1)S(1)}, bf16[512,512]{1,0:T(8,128)(2,1)S(1)}, bf16[512,512]{1,0:T(8,128)(2,1)S(1)}) custom-call(s32[33]{0:T(128)S(1)} %pad_add_fusion.where_ref, bf16[512,1024]{1,0:T(8,128)(2,1)S(1)} %get-tuple-element.209.grad_ref, bf16[2,8,1024,512]{3,2,1,0:T(8,128)(2,1)} %get-tuple-element.210.refs_0_.a_ref), custom_call_target="tpu_custom_call" | custom-call | flops 1610612736 | bytes 5767168 | tf_op jit(solution)/shard_map/backward/pallas_call | solution.py:234
  165.7 7.2 %collective-permute-done.29 = bf16[512,512]{1,0:T(8,128)(2,1)S(1)} collective-permute-done((bf16[512,512]{1,0:T(8,128)(2,1)S(1)}, bf16[512,512]{1,0:T(8,128)(2,1)S(1)}, u32[]{:S(2)}, u32[]{:S(2)}) %collective-permute-start.29) | collective-permute-done | bytes 524320 | tf_op jit(solution)/shard_map/grads_across/ppermute | solution.py:271
  173.3 0.9 collective-permute-start.33
  174.2 4.6 %backward.11 = (bf16[512,512]{1,0:T(8,128)(2,1)S(1)}, bf16[512,512]{1,0:T(8,128)(2,1)S(1)}, bf16[512,512]{1,0:T(8,128)(2,1)S(1)}) custom-call(s32[33]{0:T(128)S(1)} %pad_add_fusion.where_ref, bf16[512,1024]{1,0:T(8,128)(2,1)S(1)} %get-tuple-element.209.grad_ref, bf16[2,8,1024,512]{3,2,1,0:T(8,128)(2,1)} %get-tuple-element.210.refs_0_.a_ref), custom_call_target="tpu_custom_call" | custom-call | flops 1610612736 | bytes 5767168 | tf_op jit(solution)/shard_map/backward/pallas_call | solution.py:234
  178.9 3.1 %collective-permute-done.31 = bf16[512,512]{1,0:T(8,128)(2,1)S(1)} collective-permute-done((bf16[512,512]{1,0:T(8,128)(2,1)S(1)}, bf16[512,512]{1,0:T(8,128)(2,1)S(1)}, u32[]{:S(2)}, u32[]{:S(2)}) %collective-permute-start.31) | collective-permute-done | bytes 524320 | tf_op jit(solution)/shard_map/grads_along_z/ppermute | solution.py:271
  182.0 5.5 %collective-permute-done.32 = bf16[512,512]{1,0:T(8,128)(2,1)S(1)} collective-permute-done((bf16[512,512]{1,0:T(8,128)(2,1)S(1)}, bf16[512,512]{1,0:T(8,128)(2,1)S(1)}, u32[]{:S(2)}, u32[]{:S(2)}) %collective-permute-start.32) | collective-permute-done | bytes 524320 | tf_op jit(solution)/shard_map/grads_across/ppermute | solution.py:271
  187.6 1.7 collective-permute-start.35
  189.4 1.0 collective-permute-start.36
  190.6 5.2 %collective-permute-start.37 = (bf16[512,512]{1,0:T(8,128)(2,1)S(1)}, bf16[512,512]{1,0:T(8,128)(2,1)S(1)}, u32[]{:S(2)}, u32[]{:S(2)}) collective-permute-start(bf16[512,512]{1,0:T(8,128)(2,1)S(1)} %add_convert_fusion.1), channel_id=1, source_target_pairs={{0,8},{1,9},{2,10},{3,11},{4,12},{5,13},{6,14},{7,15},{8,0},{9,1},... | collective-permute-start | bytes 1572872 | tf_op jit(solution)/shard_map/grads_along_z/ppermute | solution.py:271
  195.8 5.2 %collective-permute-done.35 = bf16[512,512]{1,0:T(8,128)(2,1)S(1)} collective-permute-done((bf16[512,512]{1,0:T(8,128)(2,1)S(1)}, bf16[512,512]{1,0:T(8,128)(2,1)S(1)}, u32[]{:S(2)}, u32[]{:S(2)}) %collective-permute-start.35) | collective-permute-done | bytes 524320 | tf_op jit(solution)/shard_map/grads_across/ppermute | solution.py:271
  201.1 1.3 collective-permute-done.36
  202.4 4.3 %collective-permute-done.37 = bf16[512,512]{1,0:T(8,128)(2,1)S(1)} collective-permute-done((bf16[512,512]{1,0:T(8,128)(2,1)S(1)}, bf16[512,512]{1,0:T(8,128)(2,1)S(1)}, u32[]{:S(2)}, u32[]{:S(2)}) %collective-permute-start.37) | collective-permute-done | bytes 524320 | tf_op jit(solution)/shard_map/grads_along_z/ppermute | solution.py:271
  207.1 1.0 copy.11
  208.1 1.1 convert_element_type.175
  (66 shorter events, 8.9 us)
Async XLA Ops:
  0.6 1.2 copy-start
  1.9 21.6 %collective-permute-start = (bf16[512,512]{1,0:T(8,128)(2,1)S(1)}, bf16[512,512]{1,0:T(8,128)(2,1)S(1)}, u32[]{:S(2)}, u32[]{:S(2)}) collective-permute-start(bf16[512,512]{1,0:T(8,128)(2,1)S(1)} %constant_dynamic-slice_fusion.refs_2_), channel_id=1, source_target_pairs={{0,2},{1,3},{2,0},{3,1},{4,6},{5,7},{6,4},{7,5},{8,10},{9,11},{10,... | collective-permute-start | bytes 1572872 | tf_op jit(solution)/shard_map/features_across/ppermute | solution.py:271
  4.9 18.6 %collective-permute-start.1 = (bf16[512,512]{1,0:T(8,128)(2,1)S(1)}, bf16[512,512]{1,0:T(8,128)(2,1)S(1)}, u32[]{:S(2)}, u32[]{:S(2)}) collective-permute-start(bf16[512,512]{1,0:T(8,128)(2,1)S(1)} %constant_dynamic-slice_fusion.refs_2_), channel_id=1, source_target_pairs={{0,4},{1,5},{2,6},{3,7},{4,0},{5,1},{6,2},{7,3},{8,12},{9,13},{10,... | collective-permute-start | bytes 1572872 | tf_op jit(solution)/shard_map/features_across/ppermute | solution.py:271
  6.4 17.1 %collective-permute-start.2 = (bf16[512,512]{1,0:T(8,128)(2,1)S(1)}, bf16[512,512]{1,0:T(8,128)(2,1)S(1)}, u32[]{:S(2)}, u32[]{:S(2)}) collective-permute-start(bf16[512,512]{1,0:T(8,128)(2,1)S(1)} %constant_dynamic-slice_fusion.refs_2_), channel_id=1, source_target_pairs={{0,8},{1,9},{2,10},{3,11},{4,12},{5,13},{6,14},{7,15},{8,0},{9,1},... | collective-permute-start | bytes 1572872 | tf_op jit(solution)/shard_map/features_along_z/ppermute | solution.py:271
  8.7 2.8 %copy-start.2 = (bf16[1,8,24,128,128]{4,3,2,1,0:T(8,128)(2,1)S(1)}, bf16[1,8,24,128,128]{4,3,2,1,0:T(8,128)(2,1)}, u32[]{:S(2)}) copy-start(bf16[1,8,24,128,128]{4,3,2,1,0:T(8,128)(2,1)} %param.10) | copy-start | bytes 18874372
  11.5 0.7 copy-start.5
  12.2 0.7 copy-start.6
  12.9 0.7 copy-start.7
  23.5 29.1 %collective-permute-start.5 = (bf16[8,1024,512]{2,1,0:T(8,128)(2,1)}, bf16[8,1024,512]{2,1,0:T(8,128)(2,1)S(1)}, u32[]{:S(2)}, u32[]{:S(2)}) collective-permute-start(bf16[8,1024,512]{2,1,0:T(8,128)(2,1)} %get-tuple-element.129), channel_id=1, source_target_pairs={{0,1},{1,0},{2,3},{3,2},{4,5},{5,4},{6,7},{7,6},{8,9},{9,8},{10,11... | collective-permute-start | bytes 25165832 | tf_op jit(solution)/shard_map/dense_exchange/ppermute | solution.py:271
  23.6 14.3 %collective-permute-start.3 = (bf16[512,512]{1,0:T(8,128)(2,1)S(1)}, bf16[512,512]{1,0:T(8,128)(2,1)S(1)}, u32[]{:S(2)}, u32[]{:S(2)}) collective-permute-start(bf16[512,512]{1,0:T(8,128)(2,1)S(1)} %collective-permute-done.2.refs_5_), channel_id=1, source_target_pairs={{0,2},{1,3},{2,0},{3,1},{4,6},{5,7},{6,4},{7,5},{8,10},{9,11},{10,... | collective-permute-start | bytes 1572872 | tf_op jit(solution)/shard_map/features_across/ppermute | solution.py:271
  25.1 14.0 %collective-permute-start.4 = (bf16[512,512]{1,0:T(8,128)(2,1)S(1)}, bf16[512,512]{1,0:T(8,128)(2,1)S(1)}, u32[]{:S(2)}, u32[]{:S(2)}) collective-permute-start(bf16[512,512]{1,0:T(8,128)(2,1)S(1)} %collective-permute-done.2.refs_5_), channel_id=1, source_target_pairs={{0,4},{1,5},{2,6},{3,7},{4,0},{5,1},{6,2},{7,3},{8,12},{9,13},{10,... | collective-permute-start | bytes 1572872 | tf_op jit(solution)/shard_map/features_across/ppermute | solution.py:271
  25.1 25.3 %collective-permute-start.6 = (bf16[512,512]{1,0:T(8,128)(2,1)S(1)}, bf16[512,512]{1,0:T(8,128)(2,1)S(1)}, u32[]{:S(2)}, u32[]{:S(2)}) collective-permute-start(bf16[512,512]{1,0:T(8,128)(2,1)S(1)} %constant_dynamic-slice_fusion.refs_2_), channel_id=1, source_target_pairs={{0,16},{1,17},{2,18},{3,19},{4,20},{5,21},{6,22},{7,23},{8,24},{9,... | collective-permute-start | bytes 1572872 | tf_op jit(solution)/shard_map/features_along_z/ppermute | solution.py:271
  39.1 13.2 %collective-permute-start.7 = (bf16[512,512]{1,0:T(8,128)(2,1)S(1)}, bf16[512,512]{1,0:T(8,128)(2,1)S(1)}, u32[]{:S(2)}, u32[]{:S(2)}) collective-permute-start(bf16[512,512]{1,0:T(8,128)(2,1)S(1)} %collective-permute-done.refs_3_), channel_id=1, source_target_pairs={{0,4},{1,5},{2,6},{3,7},{4,0},{5,1},{6,2},{7,3},{8,12},{9,13},{10,... | collective-permute-start | bytes 1572872 | tf_op jit(solution)/shard_map/features_across/ppermute | solution.py:271
  39.4 13.2 %collective-permute-start.8 = (bf16[512,512]{1,0:T(8,128)(2,1)S(1)}, bf16[512,512]{1,0:T(8,128)(2,1)S(1)}, u32[]{:S(2)}, u32[]{:S(2)}) collective-permute-start(bf16[512,512]{1,0:T(8,128)(2,1)S(1)} %collective-permute-done.4.refs_7_), channel_id=1, source_target_pairs={{0,2},{1,3},{2,0},{3,1},{4,6},{5,7},{6,4},{7,5},{8,10},{9,11},{10,... | collective-permute-start | bytes 1572872 | tf_op jit(solution)/shard_map/features_across/ppermute | solution.py:271
  52.6 2.7 %copy-start.10 = (bf16[512,512]{1,0:T(8,128)(2,1)}, bf16[512,512]{1,0:T(8,128)(2,1)S(1)}, u32[]{:S(2)}) copy-start(bf16[512,512]{1,0:T(8,128)(2,1)S(1)} %collective-permute-done.8.refs_9_) | copy-start | bytes 1572868
  52.6 3.5 %copy-start.9 = (bf16[8,1024,512]{2,1,0:T(8,128)(2,1)}, bf16[8,1024,512]{2,1,0:T(8,128)(2,1)S(1)}, u32[]{:S(2)}) copy-start(bf16[8,1024,512]{2,1,0:T(8,128)(2,1)S(1)} %collective-permute-done.5) | copy-start | bytes 25165828
  52.6 12.7 %collective-permute-start.9 = (bf16[512,512]{1,0:T(8,128)(2,1)S(1)}, bf16[512,512]{1,0:T(8,128)(2,1)S(1)}, u32[]{:S(2)}, u32[]{:S(2)}) collective-permute-start(bf16[512,512]{1,0:T(8,128)(2,1)S(1)} %collective-permute-done.6.refs_2_), channel_id=1, source_target_pairs={{0,2},{1,3},{2,0},{3,1},{4,6},{5,7},{6,4},{7,5},{8,10},{9,11},{10,... | collective-permute-start | bytes 1572872 | tf_op jit(solution)/shard_map/features_across/ppermute | solution.py:271
  53.7 12.0 %collective-permute-start.10 = (bf16[512,512]{1,0:T(8,128)(2,1)S(1)}, bf16[512,512]{1,0:T(8,128)(2,1)S(1)}, u32[]{:S(2)}, u32[]{:S(2)}) collective-permute-start(bf16[512,512]{1,0:T(8,128)(2,1)S(1)} %collective-permute-done.6.refs_2_), channel_id=1, source_target_pairs={{0,4},{1,5},{2,6},{3,7},{4,0},{5,1},{6,2},{7,3},{8,12},{9,13},{10,... | collective-permute-start | bytes 1572872 | tf_op jit(solution)/shard_map/features_across/ppermute | solution.py:271
  54.7 12.4 %collective-permute-start.11 = (bf16[512,512]{1,0:T(8,128)(2,1)S(1)}, bf16[512,512]{1,0:T(8,128)(2,1)}, u32[]{:S(2)}, u32[]{:S(2)}) collective-permute-start(bf16[512,512]{1,0:T(8,128)(2,1)S(1)} %collective-permute-done.6.refs_2_), channel_id=1, source_target_pairs={{0,8},{1,9},{2,10},{3,11},{4,12},{5,13},{6,14},{7,15},{8,0},{9,1},... | collective-permute-start | bytes 1572872 | tf_op jit(solution)/shard_map/features_along_z/ppermute | solution.py:271
  55.3 13.4 %collective-permute-start.14 = (bf16[512,512]{1,0:T(8,128)(2,1)}, bf16[512,512]{1,0:T(8,128)(2,1)}, u32[]{:S(2)}, u32[]{:S(2)}) collective-permute-start(bf16[512,512]{1,0:T(8,128)(2,1)} %param.14), channel_id=1, source_target_pairs={{0,1},{1,0},{2,3},{3,2},{4,5},{5,4},{6,7},{7,6},{8,9},{9,8},{10,11... | collective-permute-start | bytes 1572872 | tf_op jit(solution)/shard_map/cotangent_rows/ppermute | solution.py:271
  65.7 0.8 copy-start.3
  67.2 12.8 %collective-permute-start.12 = (bf16[512,512]{1,0:T(8,128)(2,1)}, bf16[512,512]{1,0:T(8,128)(2,1)S(1)}, u32[]{:S(2)}, u32[]{:S(2)}) collective-permute-start(bf16[512,512]{1,0:T(8,128)(2,1)} %collective-permute-done.11.refs_5_), channel_id=1, source_target_pairs={{0,2},{1,3},{2,0},{3,1},{4,6},{5,7},{6,4},{7,5},{8,10},{9,11},{10,... | collective-permute-start | bytes 1572872 | tf_op jit(solution)/shard_map/features_across/ppermute | solution.py:271
  67.7 12.8 %collective-permute-start.13 = (bf16[512,512]{1,0:T(8,128)(2,1)}, bf16[512,512]{1,0:T(8,128)(2,1)S(1)}, u32[]{:S(2)}, u32[]{:S(2)}) collective-permute-start(bf16[512,512]{1,0:T(8,128)(2,1)} %collective-permute-done.11.refs_5_), channel_id=1, source_target_pairs={{0,4},{1,5},{2,6},{3,7},{4,0},{5,1},{6,2},{7,3},{8,12},{9,13},{10,... | collective-permute-start | bytes 1572872 | tf_op jit(solution)/shard_map/features_across/ppermute | solution.py:271
  68.7 13.4 %copy-start.4 = (bf16[512,512]{1,0:T(8,128)(2,1)S(1)}, bf16[512,512]{1,0:T(8,128)(2,1)}, u32[]{:S(2)}) copy-start(bf16[512,512]{1,0:T(8,128)(2,1)} %copy-done.3) | copy-start | bytes 1572868
  80.5 11.6 %collective-permute-start.15 = (bf16[512,512]{1,0:T(8,128)(2,1)S(1)}, bf16[512,512]{1,0:T(8,128)(2,1)S(1)}, u32[]{:S(2)}, u32[]{:S(2)}) collective-permute-start(bf16[512,512]{1,0:T(8,128)(2,1)S(1)} %collective-permute-done.9.refs_3_), channel_id=1, source_target_pairs={{0,4},{1,5},{2,6},{3,7},{4,0},{5,1},{6,2},{7,3},{8,12},{9,13},{10,... | collective-permute-start | bytes 1572872 | tf_op jit(solution)/shard_map/features_across/ppermute | solution.py:271
  81.1 11.0 %collective-permute-start.16 = (bf16[512,512]{1,0:T(8,128)(2,1)S(1)}, bf16[512,512]{1,0:T(8,128)(2,1)S(1)}, u32[]{:S(2)}, u32[]{:S(2)}) collective-permute-start(bf16[512,512]{1,0:T(8,128)(2,1)S(1)} %collective-permute-done.13.refs_7_), channel_id=1, source_target_pairs={{0,2},{1,3},{2,0},{3,1},{4,6},{5,7},{6,4},{7,5},{8,10},{9,11},{10,... | collective-permute-start | bytes 1572872 | tf_op jit(solution)/shard_map/features_across/ppermute | solution.py:271
  91.4 8.4 %copy-start.8 = (bf16[512,512]{1,0:T(8,128)(2,1)S(1)}, bf16[512,512]{1,0:T(8,128)(2,1)}, u32[]{:S(2)}) copy-start(bf16[512,512]{1,0:T(8,128)(2,1)} %weight_ref.1) | copy-start | bytes 1572868
  97.1 2.7 %collective-permute-start.17 = (bf16[1024,512]{1,0:T(8,128)(2,1)S(1)}, bf16[1024,512]{1,0:T(8,128)(2,1)S(1)}, u32[]{:S(2)}, u32[]{:S(2)}) collective-permute-start(bf16[1024,512]{1,0:T(8,128)(2,1)S(1)} %forward.5.mine_ref), channel_id=1, source_target_pairs={{0,1},{1,0},{2,3},{3,2},{4,5},{5,4},{6,7},{7,6},{8,9},{9,8},{10,11... | collective-permute-start | bytes 3145736 | tf_op jit(solution)/shard_map/partial_sums/ppermute | solution.py:271
  107.6 14.0 %collective-permute-start.19 = (bf16[512,512]{1,0:T(8,128)(2,1)S(1)}, bf16[512,512]{1,0:T(8,128)(2,1)S(1)}, u32[]{:S(2)}, u32[]{:S(2)}) collective-permute-start(bf16[512,512]{1,0:T(8,128)(2,1)S(1)} %get-tuple-element.173), channel_id=1, source_target_pairs={{0,4},{1,5},{2,6},{3,7},{4,0},{5,1},{6,2},{7,3},{8,12},{9,13},{10,... | collective-permute-start | bytes 1572872 | tf_op jit(solution)/shard_map/grads_across/ppermute | solution.py:271
  109.4 13.7 %collective-permute-start.20 = (bf16[512,512]{1,0:T(8,128)(2,1)S(1)}, bf16[512,512]{1,0:T(8,128)(2,1)S(1)}, u32[]{:S(2)}, u32[]{:S(2)}) collective-permute-start(bf16[512,512]{1,0:T(8,128)(2,1)S(1)} %get-tuple-element.174), channel_id=1, source_target_pairs={{0,2},{1,3},{2,0},{3,1},{4,6},{5,7},{6,4},{7,5},{8,10},{9,11},{10,... | collective-permute-start | bytes 1572872 | tf_op jit(solution)/shard_map/grads_across/ppermute | solution.py:271
  110.4 9.3 %collective-permute-start.18 = (bf16[256,512]{1,0:T(8,128)(2,1)S(1)}, bf16[256,512]{1,0:T(8,128)(2,1)S(1)}, u32[]{:S(2)}, u32[]{:S(2)}) collective-permute-start(bf16[256,512]{1,0:T(8,128)(2,1)S(1)} %get-tuple-element.172), channel_id=1, source_target_pairs={{0,8},{1,9},{2,10},{3,11},{4,12},{5,13},{6,14},{7,15},{8,0},{9,1},... | collective-permute-start | bytes 786440 | tf_op jit(solution)/shard_map/weight_grad/ppermute | solution.py:271
  123.3 15.4 %collective-permute-start.22 = (bf16[512,512]{1,0:T(8,128)(2,1)S(1)}, bf16[512,512]{1,0:T(8,128)(2,1)S(1)}, u32[]{:S(2)}, u32[]{:S(2)}) collective-permute-start(bf16[512,512]{1,0:T(8,128)(2,1)S(1)} %add_convert_fusion.7), channel_id=1, source_target_pairs={{0,2},{1,3},{2,0},{3,1},{4,6},{5,7},{6,4},{7,5},{8,10},{9,11},{10,... | collective-permute-start | bytes 1572872 | tf_op jit(solution)/shard_map/grads_across/ppermute | solution.py:271
  124.2 14.4 %collective-permute-start.23 = (bf16[512,512]{1,0:T(8,128)(2,1)S(1)}, bf16[512,512]{1,0:T(8,128)(2,1)S(1)}, u32[]{:S(2)}, u32[]{:S(2)}) collective-permute-start(bf16[512,512]{1,0:T(8,128)(2,1)S(1)} %get-tuple-element.185), channel_id=1, source_target_pairs={{0,4},{1,5},{2,6},{3,7},{4,0},{5,1},{6,2},{7,3},{8,12},{9,13},{10,... | collective-permute-start | bytes 1572872 | tf_op jit(solution)/shard_map/grads_across/ppermute | solution.py:271
  124.6 14.0 %collective-permute-start.21 = (bf16[256,512]{1,0:T(8,128)(2,1)S(1)}, bf16[256,512]{1,0:T(8,128)(2,1)S(1)}, u32[]{:S(2)}, u32[]{:S(2)}) collective-permute-start(bf16[256,512]{1,0:T(8,128)(2,1)S(1)} %add_convert_fusion.11), channel_id=1, source_target_pairs={{0,16},{1,17},{2,18},{3,19},{4,20},{5,21},{6,22},{7,23},{8,24},{9,... | collective-permute-start | bytes 786440 | tf_op jit(solution)/shard_map/weight_grad/ppermute | solution.py:271
  138.7 17.6 %collective-permute-start.25 = (bf16[512,512]{1,0:T(8,128)(2,1)S(1)}, bf16[512,512]{1,0:T(8,128)(2,1)S(1)}, u32[]{:S(2)}, u32[]{:S(2)}) collective-permute-start(bf16[512,512]{1,0:T(8,128)(2,1)S(1)} %get-tuple-element.193), channel_id=1, source_target_pairs={{0,2},{1,3},{2,0},{3,1},{4,6},{5,7},{6,4},{7,5},{8,10},{9,11},{10,... | collective-permute-start | bytes 1572872 | tf_op jit(solution)/shard_map/grads_across/ppermute | solution.py:271
  139.5 16.8 %collective-permute-start.26 = (bf16[512,512]{1,0:T(8,128)(2,1)S(1)}, bf16[512,512]{1,0:T(8,128)(2,1)S(1)}, u32[]{:S(2)}, u32[]{:S(2)}) collective-permute-start(bf16[512,512]{1,0:T(8,128)(2,1)S(1)} %add_convert_fusion.6), channel_id=1, source_target_pairs={{0,4},{1,5},{2,6},{3,7},{4,0},{5,1},{6,2},{7,3},{8,12},{9,13},{10,... | collective-permute-start | bytes 1572872 | tf_op jit(solution)/shard_map/grads_across/ppermute | solution.py:271
  141.2 15.2 %collective-permute-start.27 = (bf16[512,512]{1,0:T(8,128)(2,1)S(1)}, bf16[512,512]{1,0:T(8,128)(2,1)S(1)}, u32[]{:S(2)}, u32[]{:S(2)}) collective-permute-start(bf16[512,512]{1,0:T(8,128)(2,1)S(1)} %add_convert_fusion.5), channel_id=1, source_target_pairs={{0,8},{1,9},{2,10},{3,11},{4,12},{5,13},{6,14},{7,15},{8,0},{9,1},... | collective-permute-start | bytes 1572872 | tf_op jit(solution)/shard_map/grads_along_z/ppermute | solution.py:271
  142.6 13.6 %collective-permute-start.24 = (bf16[256,512]{1,0:T(8,128)(2,1)S(1)}, bf16[256,512]{1,0:T(8,128)(2,1)S(1)}, u32[]{:S(2)}, u32[]{:S(2)}) collective-permute-start(bf16[256,512]{1,0:T(8,128)(2,1)S(1)} %add_convert_fusion.10), channel_id=1, source_target_pairs={{0,2},{1,3},{2,0},{3,1},{4,6},{5,7},{6,4},{7,5},{8,10},{9,11},{10,... | collective-permute-start | bytes 786440 | tf_op jit(solution)/shard_map/weight_grad/ppermute | solution.py:271
  156.3 9.3 %collective-permute-start.28 = (bf16[256,512]{1,0:T(8,128)(2,1)S(1)}, bf16[256,512]{1,0:T(8,128)(2,1)S(1)}, u32[]{:S(2)}, u32[]{:S(2)}) collective-permute-start(bf16[256,512]{1,0:T(8,128)(2,1)S(1)} %add_convert_fusion.9), channel_id=1, source_target_pairs={{0,4},{1,5},{2,6},{3,7},{4,0},{5,1},{6,2},{7,3},{8,12},{9,13},{10,... | collective-permute-start | bytes 786440 | tf_op jit(solution)/shard_map/weight_grad/ppermute | solution.py:271
  157.6 15.4 %collective-permute-start.29 = (bf16[512,512]{1,0:T(8,128)(2,1)S(1)}, bf16[512,512]{1,0:T(8,128)(2,1)S(1)}, u32[]{:S(2)}, u32[]{:S(2)}) collective-permute-start(bf16[512,512]{1,0:T(8,128)(2,1)S(1)} %get-tuple-element.204), channel_id=1, source_target_pairs={{0,4},{1,5},{2,6},{3,7},{4,0},{5,1},{6,2},{7,3},{8,12},{9,13},{10,... | collective-permute-start | bytes 1572872 | tf_op jit(solution)/shard_map/grads_across/ppermute | solution.py:271
  158.4 14.5 %collective-permute-start.30 = (bf16[512,512]{1,0:T(8,128)(2,1)S(1)}, bf16[512,512]{1,0:T(8,128)(2,1)S(1)}, u32[]{:S(2)}, u32[]{:S(2)}) collective-permute-start(bf16[512,512]{1,0:T(8,128)(2,1)S(1)} %get-tuple-element.205), channel_id=1, source_target_pairs={{0,2},{1,3},{2,0},{3,1},{4,6},{5,7},{6,4},{7,5},{8,10},{9,11},{10,... | collective-permute-start | bytes 1572872 | tf_op jit(solution)/shard_map/grads_across/ppermute | solution.py:271
  159.1 23.0 %collective-permute-start.31 = (bf16[512,512]{1,0:T(8,128)(2,1)S(1)}, bf16[512,512]{1,0:T(8,128)(2,1)S(1)}, u32[]{:S(2)}, u32[]{:S(2)}) collective-permute-start(bf16[512,512]{1,0:T(8,128)(2,1)S(1)} %add_convert_fusion.4), channel_id=1, source_target_pairs={{0,16},{1,17},{2,18},{3,19},{4,20},{5,21},{6,22},{7,23},{8,24},{9,... | collective-permute-start | bytes 1572872 | tf_op jit(solution)/shard_map/grads_along_z/ppermute | solution.py:271
  172.9 5.8 %collective-permute-start.34 = (bf16[256,512]{1,0:T(8,128)(2,1)S(1)}, bf16[256,512]{1,0:T(8,128)(2,1)S(1)}, u32[]{:S(2)}, u32[]{:S(2)}) collective-permute-start(bf16[256,512]{1,0:T(8,128)(2,1)S(1)} %add_convert_fusion.8), channel_id=1, source_target_pairs={{0,1},{1,0},{2,3},{3,2},{4,5},{5,4},{6,7},{7,6},{8,9},{9,8},{10,11... | collective-permute-start | bytes 786440 | tf_op jit(solution)/shard_map/weight_grad/ppermute | solution.py:271
  173.1 14.4 %collective-permute-start.32 = (bf16[512,512]{1,0:T(8,128)(2,1)S(1)}, bf16[512,512]{1,0:T(8,128)(2,1)S(1)}, u32[]{:S(2)}, u32[]{:S(2)}) collective-permute-start(bf16[512,512]{1,0:T(8,128)(2,1)S(1)} %add_convert_fusion.3), channel_id=1, source_target_pairs={{0,2},{1,3},{2,0},{3,1},{4,6},{5,7},{6,4},{7,5},{8,10},{9,11},{10,... | collective-permute-start | bytes 1572872 | tf_op jit(solution)/shard_map/grads_across/ppermute | solution.py:271
  173.3 14.3 %collective-permute-start.33 = (bf16[512,512]{1,0:T(8,128)(2,1)S(1)}, bf16[512,512]{1,0:T(8,128)(2,1)S(1)}, u32[]{:S(2)}, u32[]{:S(2)}) collective-permute-start(bf16[512,512]{1,0:T(8,128)(2,1)S(1)} %get-tuple-element.219), channel_id=1, source_target_pairs={{0,4},{1,5},{2,6},{3,7},{4,0},{5,1},{6,2},{7,3},{8,12},{9,13},{10,... | collective-permute-start | bytes 1572872 | tf_op jit(solution)/shard_map/grads_across/ppermute | solution.py:271
  187.6 13.5 %collective-permute-start.35 = (bf16[512,512]{1,0:T(8,128)(2,1)S(1)}, bf16[512,512]{1,0:T(8,128)(2,1)S(1)}, u32[]{:S(2)}, u32[]{:S(2)}) collective-permute-start(bf16[512,512]{1,0:T(8,128)(2,1)S(1)} %get-tuple-element.227), channel_id=1, source_target_pairs={{0,2},{1,3},{2,0},{3,1},{4,6},{5,7},{6,4},{7,5},{8,10},{9,11},{10,... | collective-permute-start | bytes 1572872 | tf_op jit(solution)/shard_map/grads_across/ppermute | solution.py:271
  189.4 13.0 %collective-permute-start.36 = (bf16[512,512]{1,0:T(8,128)(2,1)S(1)}, bf16[512,512]{1,0:T(8,128)(2,1)S(1)}, u32[]{:S(2)}, u32[]{:S(2)}) collective-permute-start(bf16[512,512]{1,0:T(8,128)(2,1)S(1)} %add_convert_fusion.2), channel_id=1, source_target_pairs={{0,4},{1,5},{2,6},{3,7},{4,0},{5,1},{6,2},{7,3},{8,12},{9,13},{10,... | collective-permute-start | bytes 1572872 | tf_op jit(solution)/shard_map/grads_across/ppermute | solution.py:271
  190.6 16.2 %collective-permute-start.37 = (bf16[512,512]{1,0:T(8,128)(2,1)S(1)}, bf16[512,512]{1,0:T(8,128)(2,1)S(1)}, u32[]{:S(2)}, u32[]{:S(2)}) collective-permute-start(bf16[512,512]{1,0:T(8,128)(2,1)S(1)} %add_convert_fusion.1), channel_id=1, source_target_pairs={{0,8},{1,9},{2,10},{3,11},{4,12},{5,13},{6,14},{7,15},{8,0},{9,1},... | collective-permute-start | bytes 1572872 | tf_op jit(solution)/shard_map/grads_along_z/ppermute | solution.py:271
  206.8 2.5 %copy-start.1 = (bf16[1024,512]{1,0:T(8,128)(2,1)S(1)}, bf16[1024,512]{1,0:T(8,128)(2,1)}, u32[]{:S(2)}) copy-start(bf16[1024,512]{1,0:T(8,128)(2,1)} %param.8) | copy-start | bytes 3145732

commit v4 on v3

--- a/solution.py
+++ b/solution.py
@@ -12,8 +12,9 @@
 BOTH = ("section", "rep")
 
 
-def dense_kernel(where_ref, count_ref, rows_ref, cols_ref, tiles_ref, out_ref, *send_refs):
-    panel = pl.program_id(0)
+def dense_kernel(first, where_ref, count_ref, rows_ref, cols_ref, tiles_ref, *refs):
+    out_ref, *send_refs = refs if first == 0 else refs[1:]
+    panel = first + pl.program_id(0)
     size = tiles_ref.shape[-1]
     per_part = out_ref.shape[-1] // size
     out_ref[...] = jnp.zeros_like(out_ref)
@@ -31,37 +32,41 @@
         send_ref[0] = out_ref[where_ref[0] ^ shift, 0]
 
 
-def make_dense(where, tiles, rows, cols, count, block_rows, n_rep):
+def make_dense(first, before, where, tiles, rows, cols, count, block_rows, n_rep):
     panels, slots, size, _ = tiles.shape
+    half = panels // 2
     part = block_rows // n_rep
-    sent = jax.ShapeDtypeStruct((panels, block_rows, part), BF16)
+    sent = jax.ShapeDtypeStruct((half, block_rows, part), BF16)
+    at = lambda p: first + p
     return pl.pallas_call(
-        dense_kernel,
+        functools.partial(dense_kernel, first),
         out_shape=[jax.ShapeDtypeStruct((n_rep, panels, block_rows, part), BF16)]
         + [sent] * (n_rep - 1),
         grid_spec=pltpu.PrefetchScalarGridSpec(
             num_scalar_prefetch=4,
-            grid=(panels,),
-            in_specs=[pl.BlockSpec((1, slots, size, size), lambda p, *_: (p, 0, 0, 0))],
-            out_specs=[pl.BlockSpec((n_rep, 1, block_rows, part), lambda p, *_: (0, p, 0, 0))]
+            grid=(half,),
+            in_specs=[pl.BlockSpec((1, slots, size, size), lambda p, *_: (at(p), 0, 0, 0))]
+            + [pl.BlockSpec(memory_space=pl.ANY)] * (first > 0),
+            out_specs=[pl.BlockSpec((n_rep, 1, block_rows, part), lambda p, *_: (0, at(p), 0, 0))]
             + [pl.BlockSpec((1, block_rows, part), lambda p, *_: (p, 0, 0))] * (n_rep - 1),
         ),
-        compiler_params=pltpu.CompilerParams(vmem_limit_bytes=40 * 2**20),
+        input_output_aliases={5: 0} if first else {},
+        compiler_params=pltpu.CompilerParams(vmem_limit_bytes=36 * 2**20),
         cost_estimate=pl.CostEstimate(
             flops=0,
             transcendentals=0,
-            bytes_accessed=tiles.size * 2 + panels * block_rows * block_rows * 3,
-        ),
-    )(where, count, rows, cols, tiles)
-
-
-def forward_kernel(offset, n_units, has_total, where_ref, *refs):
-    dense_ref, others_ref = refs[:2]
-    units = refs[2 : 2 + n_units]
-    refs = refs[2 + n_units :]
+            bytes_accessed=tiles.size + half * block_rows * block_rows * 3,
+        ),
+    )(where, count, rows, cols, tiles, *([before] if first else []))
+
+
+def forward_kernel(offset, n_units, n_others, has_total, where_ref, dense_ref, *refs):
+    others, refs = refs[:n_others], refs[n_others:]
+    units, refs = refs[:n_units], refs[n_units:]
     total_ref, refs = (refs[0], refs[1:]) if has_total else (None, refs)
-    out_ref, sum_ref, a_buf, u_buf, sems = refs
+    out_ref, sum_ref, a_buf, u_buf, sems, sum_sem = refs
     _, panels, _, part = dense_ref.shape
+    some = others[0].shape[0]
     rep = where_ref[0]
 
     def a_copy(source, slot, side):
@@ -76,16 +81,17 @@
         for side in range(2):
             place = where_ref[offset + 2 * pair + side]
             owner, panel = place // panels, place % panels
-            mine = owner == rep
-            turn = jnp.maximum((owner ^ rep) - 1, 0)
-
-            @pl.when(mine)
+            turn = ((owner ^ rep) - 1) * (panels // some) + panel // some
+
+            @pl.when(owner == rep)
             def _():
                 a_copy(dense_ref.at[rep, panel], slot, side).start()
 
-            @pl.when(jnp.logical_not(mine))
-            def _():
-                a_copy(others_ref.at[turn, panel], slot, side).start()
+            for number, other_ref in enumerate(others):
+
+                @pl.when((owner != rep) & (turn == number))
+                def _():
+                    a_copy(other_ref.at[panel % some], slot, side).start()
 
             for number in range(side, n_units, 2):
 
@@ -95,7 +101,12 @@
 
     pairs = n_units // 2
     fetch(0, 0)
-    sum_ref[...] = total_ref[...] if has_total else jnp.zeros_like(sum_ref)
+    if has_total:
+        load = pltpu.make_async_copy(total_ref, sum_ref, sum_sem)
+        load.start()
+        load.wait()
+    else:
+        sum_ref[...] = jnp.zeros_like(sum_ref)
 
     def step(pair, carry):
         slot = pair % 2
@@ -111,107 +122,133 @@
         return carry
 
     lax.fori_loop(0, pairs, step, 0)
-    out_ref[...] = sum_ref[...].astype(out_ref.dtype)
+    if out_ref.dtype == F32:
+        store = pltpu.make_async_copy(sum_ref, out_ref, sum_sem)
+        store.start()
+        store.wait()
+    else:
+        out_ref[...] = sum_ref[...].astype(out_ref.dtype)
 
 
 def forward_part(where, offset, units, total, dense, others, kind):
     part, width = units[0].shape
     rows = dense.shape[2]
     hbm = pl.BlockSpec(memory_space=pl.ANY)
-    whole = pl.BlockSpec((rows, width), lambda i, where: (0, 0))
     has_total = total is not None
-    n_units = len(units)
+    n_units, n_others = len(units), len(others)
     return pl.pallas_call(
-        functools.partial(forward_kernel, offset, n_units, has_total),
+        functools.partial(forward_kernel, offset, n_units, n_others, has_total),
         out_shape=jax.ShapeDtypeStruct((rows, width), kind),
         grid_spec=pltpu.PrefetchScalarGridSpec(
             num_scalar_prefetch=1,
             grid=(1,),
-            in_specs=[hbm] * (2 + n_units) + [whole] * has_total,
-            out_specs=whole,
+            in_specs=[hbm] * (1 + n_others + n_units + has_total),
+            out_specs=hbm if kind == F32 else pl.BlockSpec((rows, width), lambda i, where: (0, 0)),
             scratch_shapes=[
                 pltpu.VMEM((rows, width), F32),
                 pltpu.VMEM((2, rows, 2 * part), BF16),
                 pltpu.VMEM((2, 2 * part, width), BF16),
                 pltpu.SemaphoreType.DMA((2, 2, 2)),
+                pltpu.SemaphoreType.DMA,
             ],
         ),
-        compiler_params=pltpu.CompilerParams(vmem_limit_bytes=50 * 2**20),
+        compiler_params=pltpu.CompilerParams(vmem_limit_bytes=36 * 2**20),
         cost_estimate=pl.CostEstimate(
             flops=2 * n_units * rows * part * width,
             transcendentals=0,
             bytes_accessed=n_units * rows * part * 2 + 8 * rows * width,
         ),
-    )(where, dense, others, *units, *([total] if has_total else []))
+    )(where, dense, *others, *units, *([total] if has_total else []))
 
 
 def middle_kernel(
-    where_ref, mine_ref, other_ref, weight_ref, cot_ref, grad_ref, act_ref, term_ref, sum_ref
+    n_rep, where_ref, mine_ref, other_ref, weight_ref, cot_ref, a_ref, grad_ref, act_ref, *refs
 ):
-    agg = (mine_ref[...].astype(F32) + other_ref[...].astype(F32)).astype(BF16)
-    pre = jnp.dot(agg, weight_ref[...], preferred_element_type=F32)
-    sigma = jax.nn.sigmoid(pre)
-    act_ref[...] = (pre * sigma).astype(BF16)
-    slope = cot_ref[...].astype(F32) * sigma * (1.0 + pre * (1.0 - sigma))
-    pre_grad = slope.astype(BF16)
-    grad_ref[...] = lax.dot_general(
-        weight_ref[...], pre_grad, (((1,), (1,)), ((), ())), preferred_element_type=F32
-    ).astype(BF16)
-    term = lax.dot_general(
-        agg, pre_grad, (((0,), (0,)), ((), ())), preferred_element_type=F32
-    )
+    term_refs, (odd_ref, even_ref, sum_ref) = refs[:-3], refs[-3:]
     step = pl.program_id(0)
-
-    @pl.when(step == 0)
+    part = mine_ref.shape[0]
+
+    @pl.when(step < n_rep)
     def _():
-        sum_ref[...] = term
-
-    @pl.when(step > 0)
+        agg = (mine_ref[...].astype(F32) + other_ref[...].astype(F32)).astype(BF16)
+        pre = jnp.dot(agg, weight_ref[...], preferred_element_type=F32)
+        sigma = jax.nn.sigmoid(pre)
+        act_ref[...] = (pre * sigma).astype(BF16)
+        slope = cot_ref[...].astype(F32) * sigma * (1.0 + pre * (1.0 - sigma))
+        pre_grad = slope.astype(BF16)
+        block = (where_ref[0] + 1 + step) % n_rep
+        grad_ref[:, pl.ds(pl.multiple_of(block * part, part), part)] = lax.dot_general(
+            weight_ref[...], pre_grad, (((1,), (1,)), ((), ())), preferred_element_type=F32
+        ).astype(BF16)
+        term = lax.dot_general(
+            agg, pre_grad, (((0,), (0,)), ((), ())), preferred_element_type=F32
+        )
+
+        @pl.when(step == 0)
+        def _():
+            sum_ref[...] = term
+
+        @pl.when(step > 0)
+        def _():
+            sum_ref[...] += term
+
+    @pl.when(step >= n_rep)
     def _():
-        sum_ref[...] += term
-
-    @pl.when(step == pl.num_programs(0) - 1)
-    def _():
-        size = term_ref.shape[0]
-        start = pl.multiple_of(where_ref[0] * size, size)
-        term_ref[...] = sum_ref[pl.ds(start, size), :].astype(BF16)
-
-
-def middle(where, mine, other, weight, cotangent, n_rep):
+        chunk = jnp.dot(grad_ref[...], a_ref[0, 0], preferred_element_type=F32).astype(BF16)
+
+        @pl.when(step == n_rep)
+        def _():
+            odd_ref[...] = chunk
+            z = where_ref[1] // 4
+            size = term_refs[0].shape[0]
+            for number, term_ref in enumerate(term_refs):
+                start = (where_ref[0] * len(term_refs) + (z ^ number)) * size
+                term_ref[...] = sum_ref[pl.ds(pl.multiple_of(start, size), size), :].astype(BF16)
+
+        @pl.when(step > n_rep)
+        def _():
+            even_ref[...] = chunk
+
+
+def middle(where, offset, mine, other, weight, cotangent, dense, n_rep, depth):
     rows, width = mine.shape
     part = rows // n_rep
-    block = lambda i, where: ((where[0] + 1 + i) % n_rep, 0)
-    last = pl.BlockSpec((part, width), lambda i, where: (0, 0))
+    size = width // n_rep // depth
+    block = lambda i, where: ((where[0] + 1 + jnp.minimum(i, n_rep - 1)) % n_rep, 0)
+    fixed = lambda *shape: pl.BlockSpec(shape, lambda i, where: (0, 0))
+    kept = lambda *shape: jax.ShapeDtypeStruct(shape, BF16)
+
+    def a_block(i, where):
+        place = where[offset + jnp.maximum(i - n_rep, 0)]
+        return (place % n_rep, place // n_rep, 0, 0)
+
     return pl.pallas_call(
-        middle_kernel,
-        out_shape=[
-            jax.ShapeDtypeStruct((width, rows), BF16),
-            jax.ShapeDtypeStruct((part, width), BF16),
-            jax.ShapeDtypeStruct((width // n_rep, width), BF16),
-        ],
+        functools.partial(middle_kernel, n_rep),
+        out_shape=[kept(width, rows), kept(part, width)]
+        + [kept(size, width)] * depth
+        + [kept(width, part)] * 2,
         grid_spec=pltpu.PrefetchScalarGridSpec(
             num_scalar_prefetch=1,
-            grid=(n_rep,),
+            grid=(n_rep + 2,),
             in_specs=[
                 pl.BlockSpec((part, width), block),
                 pl.BlockSpec((part, width), block),
-                pl.BlockSpec((width, width), lambda i, where: (0, 0)),
+                fixed(width, width),
                 pl.BlockSpec((part, width), block),
+                pl.BlockSpec((1, 1, rows, part), a_block),
             ],
-            out_specs=[
-                pl.BlockSpec((width, part), lambda i, where: (0, block(i, where)[0])),
-                last,
-                pl.BlockSpec((width // n_rep, width), lambda i, where: (0, 0)),
-            ],
+            out_specs=[fixed(width, rows), fixed(part, width)]
+            + [fixed(size, width)] * depth
+            + [fixed(width, part)] * 2,
             scratch_shapes=[pltpu.VMEM((width, width), F32)],
         ),
-        compiler_params=pltpu.CompilerParams(vmem_limit_bytes=40 * 2**20),
+        compiler_params=pltpu.CompilerParams(vmem_limit_bytes=36 * 2**20),
         cost_estimate=pl.CostEstimate(
-            flops=6 * rows * width * width,
+            flops=6 * rows * width * width + 4 * rows * width * part,
             transcendentals=rows * width,
-            bytes_accessed=rows * width * 10,
-        ),
-    )(where, mine, other, weight, cotangent)
+            bytes_accessed=rows * width * 12,
+        ),
+    )(where, mine, other, weight, cotangent, dense)
 
 
 def backward_kernel(where_ref, grad_ref, a_ref, *out_refs):
@@ -243,13 +280,33 @@
             ],
             out_specs=[pl.BlockSpec((width, cols), lambda i, where: (0, 0))] * count,
         ),
-        compiler_params=pltpu.CompilerParams(vmem_limit_bytes=50 * 2**20),
+        compiler_params=pltpu.CompilerParams(vmem_limit_bytes=36 * 2**20),
         cost_estimate=pl.CostEstimate(
             flops=2 * count * rows * width * cols,
             transcendentals=0,
             bytes_accessed=2 * count * rows * cols + 2 * count * width * cols + 2 * width * rows,
         ),
     )(where, grad, dense)
+
+
+def final_kernel(*refs):
+    *parts, out_ref = refs
+    total = functools.reduce(jnp.add, [part[...].astype(F32) for part in parts])
+    out_ref[0] = total.T.astype(BF16)
+
+
+def final_sum(parts):
+    width, cols = parts[0].shape
+    return pl.pallas_call(
+        final_kernel,
+        out_shape=jax.ShapeDtypeStruct((1, cols, width), BF16),
+        compiler_params=pltpu.CompilerParams(vmem_limit_bytes=36 * 2**20),
+        cost_estimate=pl.CostEstimate(
+            flops=len(parts) * width * cols,
+            transcendentals=0,
+            bytes_accessed=2 * (len(parts) + 1) * width * cols,
+        ),
+    )(*parts)
 
 
 def shards(sizes, features, weight, tile_values, tile_rows, tile_cols, tile_count, cotangent):
@@ -287,7 +344,7 @@
     masks, offsets = [], {}
 
     def plan(name, wanted):
-        offsets[name] = 1 + len(masks)
+        offsets[name] = 2 + len(masks)
         masks.extend(wanted)
 
     for pair in range(pair_count):
@@ -297,7 +354,9 @@
         plan(("first", pair), [odd + X + Y, even + X + Y])
         plan(("odd", pair), [odd + X, odd + Y, odd])
         plan(("even", pair), [even + X, even + Y, even])
-    where = jnp.concatenate([rep[None], section ^ jnp.array(masks, jnp.int32)]).astype(jnp.int32)
+    where = jnp.concatenate(
+        [rep[None], section[None], section ^ jnp.array(masks, jnp.int32)]
+    ).astype(jnp.int32)
 
     def forward_step(names, units, total, kind=F32):
         with jax.named_scope("forward"):
@@ -305,6 +364,8 @@
                 where, offsets[names], units, total, live["dense"], live["others"], kind
             )
 
+    panels = tile_values.shape[1]
+    tiles = (where, tile_values[0], tile_rows[0], tile_cols[0], tile_count[0], block_rows, n_rep)
     live[0] = lax.dynamic_slice_in_dim(features, rep * part, part, axis=0)
     total = None
     for pair in range(pair_count):
@@ -318,15 +379,7 @@
             live[odd] = flip(live[even], Z)
         if pair == 0:
             with jax.named_scope("dense_blocks"):
-                live["dense"], *live["sent"] = make_dense(
-                    where,
-                    tile_values[0],
-                    tile_rows[0],
-                    tile_cols[0],
-                    tile_count[0],
-                    block_rows,
-                    n_rep,
-                )
+                live["dense"], *live["sent"] = make_dense(0, None, *tiles)
         else:
             live["total"] = forward_step(*waiting, live.pop("waiting"), live.get("total"))
         close()
@@ -335,18 +388,24 @@
             live["odd_x"], live["odd_y"] = flip(live[odd], X), flip(live[odd], Y)
         if pair == 0:
             with jax.named_scope("dense_exchange"):
-                others = [flip(value, 0, n) for n, value in enumerate(live.pop("sent"), 1)]
-                live["others"] = others[0][None] if n_rep == 2 else jnp.stack(others)
+                one = [flip(value, 0, n) for n, value in enumerate(live.pop("sent"), 1)]
+            with jax.named_scope("dense_blocks"):
+                first = panels // 2
+                live["dense"], *live["sent"] = make_dense(first, live["dense"], *tiles)
         if not last:
             with jax.named_scope("features_along_z"):
                 live[later] = flip(live[later - low_bit(later)], low_bit(later))
         if last:
             with jax.named_scope("cotangent_rows"):
                 live["cotangent"] = gather_rep(cotangent)
-        close(*([] if last else [later]), *([] if pair else ["others"]))
+        close(*([] if last else [later]))
 
         with jax.named_scope("features_across"):
             crossed = [flip(live["even_x"], Y), flip(live["odd_y"], X)]
+        if pair == 0:
+            with jax.named_scope("dense_exchange"):
+                two = [flip(value, 0, n) for n, value in enumerate(live.pop("sent"), 1)]
+                live["others"] = [half for halves in zip(one, two) for half in halves]
         units = [live[even], live.pop("even_x"), live.pop("even_y")]
         units += [live[odd], live.pop("odd_x"), live.pop("odd_y")]
         if pair > 0:
@@ -365,28 +424,50 @@
             partial = (partial.astype(F32) + other.astype(F32)).astype(BF16)
             other = flip(partial, 0, 1 << bit)
 
+    depth = n_section // 4
     with jax.named_scope("middle"):
-        grad, activated, term = middle(where, partial, other, weight, live["cotangent"], n_rep)
+        grad, activated, *terms, odd_diag, even_diag = middle(
+            where,
+            offsets["first", pair_count - 1],
+            partial,
+            other,
+            weight,
+            live["cotangent"],
+            live["dense"],
+            n_rep,
+            depth,
+        )
 
     def backward_step(name, count):
         with jax.named_scope("backward"):
             return backward_part(where, offsets[name], count, live["grad"], live["dense"])
 
     add = lambda *values: functools.reduce(jnp.add, [value.astype(F32) for value in values])
-    term_masks = [*(1 << bit for bit in range(2, n_section.bit_length() - 1)), X, Y]
+
+    def weight_step(phase):
+        terms = live["terms"]
+        if phase == 0:
+            sums = [terms[0]] + [flip(term, Z * n) for n, term in enumerate(terms[1:], 1)]
+            live["terms"] = [add(*sums).astype(BF16)]
+        elif phase == 1:
+            sums = [terms[0]] + [flip(terms[0], mask) for mask in (X, Y, X + Y)]
+            live["terms"] = [(add(*sums[:2]) + add(*sums[2:])).astype(BF16)]
+        elif 1 << phase - 2 < depth:
+            live["terms"] = terms + [flip(term, Z << phase - 2) for term in terms]
+        elif "weight_grad" not in live:
+            z = section // 4
+            rows = jnp.stack(terms)[z ^ jnp.arange(depth)].reshape(-1, width)
+            live["weight_grad"] = gather_rep(rows).astype(F32)
+
+    phases = iter(range(3 * pair_count))
 
     def end_phase(*open_names):
-        if term_masks:
-            with jax.named_scope("weight_grad"):
-                mask = term_masks.pop(0)
-                live["term"] = add(live["term"], flip(live["term"], mask)).astype(BF16)
-        elif "weight_grad" not in live:
-            with jax.named_scope("weight_grad"):
-                live["weight_grad"] = gather_rep(live.pop("term"))
+        with jax.named_scope("weight_grad"):
+            weight_step(next(phases))
         close(*open_names)
 
-    live = {"grad": grad, "dense": live["dense"], "term": term}
-    live["first"] = backward_step(("first", pair_count - 1), 2)
+    live = {"grad": grad, "dense": live["dense"], "terms": terms}
+    live["first"] = [odd_diag, even_diag]
     for pair in reversed(range(pair_count)):
         even = 2 * pair * Z
         passing = [name for name in live if isinstance(name, tuple)]
@@ -421,12 +502,12 @@
             live["first"] = backward_step(("first", pair - 1), 2)
         end_phase()
         arrived = [name for name in live if isinstance(name, tuple) and name[1] == even]
-        total = add(*live.pop("even_sum"), *(live.pop(name) for name in arrived)).astype(BF16)
+        sums = [*live.pop("even_sum"), *(live.pop(name) for name in arrived)]
         if pair > 0:
-            live["passed"] = total
+            live["passed"] = add(*sums).astype(BF16)
     with jax.named_scope("grads_out"):
-        feat_grad = total.T
-    return (activated, feat_grad[None], live["weight_grad"].astype(F32))
+        feat_grad = final_sum(sums)
+    return (activated, feat_grad, live["weight_grad"])
 
 
 def solution(mesh):

time: 210 us -> 218 us (1.038)
  local copies, waits for them, and re-layouts: 8.65 us -> 15.3 us
  Pallas kernels: 63.1 us -> 57.7 us
  other arithmetic: 5.18 us -> 9.19 us
  starting transfers between devices: 46.5 us -> 50.1 us
    unnamed x23 -> x44, local copies, waits for them, and re-layouts: 8.62 us -> 14 us
    ppermute x38 -> x44, starting transfers between devices: 46.5 us -> 50.1 us  [flip(): return lax.ppermute(value, BOTH, pairs)]
    pallas_call x6 -> x5, Pallas kernels: 25.2 us -> 21.7 us  [backward_part(): pl.pallas_call(backward_kernel, out_shape=[jax.ShapeDtypeStruct((width, c...]
    pallas_call x5 -> x7, Pallas kernels: 37.9 us -> 36 us  [the longest x3 16.7 us: forward_part(): pl.pallas_call(functools.partial(forward_kernel, offset, n_units, n_other...]
    ppermute x38 -> x44, waiting for transfers between devices: 84.9 us -> 83.9 us  [flip(): return lax.ppermute(value, BOTH, pairs)]
  transfers between devices with their start and end apart: 38 -> 44, of which waited for: 24 -> 24; matrix products, arithmetic and copies ran while one was open for 2% -> 4% of each run, Pallas kernels for 24% -> 21%
where the time goes in v4:
time: 218 us; the launch traced here: 217 us
  waiting for transfers between devices  83.9 us (38%)
  Pallas kernels  57.7 us (26%)
  starting transfers between devices  50.1 us (23%)
  local copies, waits for them, and re-layouts  15.3 us (7%)
  other arithmetic  9.19 us (4%)
    ppermute x44, waiting for transfers between devices, flip(): return lax.ppermute(value, BOTH, pairs)  83.9 us
    ppermute x44, starting transfers between devices, flip(): return lax.ppermute(value, BOTH, pairs)  50.1 us
    pallas_call x5, Pallas kernels, backward_part(): pl.pallas_call(backward_kernel, out_shape=[jax.ShapeDtypeStruct((width, c...  21.7 us
    pallas_call x3, Pallas kernels, forward_part(): pl.pallas_call(functools.partial(forward_kernel, offset, n_units, n_other...  16.7 us
    unnamed x44, local copies, waits for them, and re-layouts  14 us
    pallas_call x2, Pallas kernels, make_dense(): pl.pallas_call(functools.partial(dense_kernel, first), out_shape=[jax.Sha...  10.5 us
    pallas_call x1, Pallas kernels, middle(): pl.pallas_call(functools.partial(middle_kernel, n_rep), out_shape=[kept(w...  7.57 us
  transfers between devices with their start and end apart: 44, of which 24 were waited for; matrix products, arithmetic and copies ran while one was open for 4% of the time, Pallas kernels for 21%

profile of v4, /device:TPU:0, one launch (start us, length us, event | category | flops | bytes accessed | tf_op | source)
XLA Modules:
  0.0 217.3 jit_solution(1508155084916550999)
XLA Ops:
  0.7 1.2 copy-done
  1.9 3.0 %collective-permute-start = (bf16[512,512]{1,0:T(8,128)(2,1)S(1)}, bf16[512,512]{1,0:T(8,128)(2,1)S(1)}, u32[]{:S(2)}, u32[]{:S(2)}) collective-permute-start(bf16[512,512]{1,0:T(8,128)(2,1)S(1)} %constant_dynamic-slice_fusion.refs_2_), channel_id=1, source_target_pairs={{0,2},{1,3},{2,0},{3,1},{4,6},{5,7},{6,4},{7,5},{8,10},{9,11},{10,... | collective-permute-start | bytes 1572872 | tf_op jit(solution)/shard_map/features_across/ppermute | solution.py:328
  4.9 1.5 collective-permute-start.1
  6.4 1.6 collective-permute-start.2
  8.7 2.8 %copy-done.6 = bf16[1,8,24,128,128]{4,3,2,1,0:T(8,128)(2,1)S(1)} copy-done((bf16[1,8,24,128,128]{4,3,2,1,0:T(8,128)(2,1)S(1)}, bf16[1,8,24,128,128]{4,3,2,1,0:T(8,128)(2,1)}, u32[]{:S(2)}) %copy-start.6) | copy-done | bytes 6291480
  13.6 5.3 %dense_blocks.2 = (bf16[2,8,1024,512]{3,2,1,0:T(8,128)(2,1)}, bf16[4,1024,512]{2,1,0:T(8,128)(2,1)S(1)}) custom-call(s32[34]{0:T(128)S(1)} %pad_add_fusion.where_ref, s32[8]{0:T(128)S(1)} %bitcast.21, s32[8,24]{1,0:T(8,128)S(1)} %bitcast.17, s32[8,24]{1,0:T(8,128)S(1)} %bitcast.19, bf16[8,24,128,128]{3,2,1,0:T(8,128)(2,1)S(1)} %bitcast.15), custom_call_target="tpu_custom_call" | custom-call | bytes 15728640 | tf_op jit(solution)/shard_map/dense_blocks/pallas_call | solution.py:41
  20.4 5.2 %dense_blocks.3 = (bf16[2,8,1024,512]{3,2,1,0:T(8,128)(2,1)}, bf16[4,1024,512]{2,1,0:T(8,128)(2,1)S(1)}) custom-call(s32[34]{0:T(128)S(1)} %pad_add_fusion.where_ref, s32[8]{0:T(128)S(1)} %bitcast.22, s32[8,24]{1,0:T(8,128)S(1)} %bitcast.18, s32[8,24]{1,0:T(8,128)S(1)} %bitcast.20, ...), custom_call_target="tpu_custom_call", output_to_operand_aliasing={{0}: (5, {})} | custom-call | bytes 15728640 | tf_op jit(solution)/shard_map/dense_blocks/pallas_call | solution.py:41
  25.6 6.2 %collective-permute-done.3.refs_6_ = bf16[512,512]{1,0:T(8,128)(2,1)S(1)} collective-permute-done((bf16[512,512]{1,0:T(8,128)(2,1)S(1)}, bf16[512,512]{1,0:T(8,128)(2,1)S(1)}, u32[]{:S(2)}, u32[]{:S(2)}) %collective-permute-start.3) | collective-permute-done | bytes 524320 | tf_op jit(solution)/shard_map/features_across/ppermute | solution.py:328
  32.0 2.7 %collective-permute-start.5 = (bf16[512,512]{1,0:T(8,128)(2,1)S(1)}, bf16[512,512]{1,0:T(8,128)(2,1)S(1)}, u32[]{:S(2)}, u32[]{:S(2)}) collective-permute-start(bf16[512,512]{1,0:T(8,128)(2,1)S(1)} %constant_dynamic-slice_fusion.refs_2_), channel_id=1, source_target_pairs={{0,16},{1,17},{2,18},{3,19},{4,20},{5,21},{6,22},{7,23},{8,24},{9,... | collective-permute-start | bytes 1572872 | tf_op jit(solution)/shard_map/features_along_z/ppermute | solution.py:328
  35.3 1.4 collective-permute-start.9
  36.7 21.8 %collective-permute-done.5.refs_2_ = bf16[512,512]{1,0:T(8,128)(2,1)S(1)} collective-permute-done((bf16[512,512]{1,0:T(8,128)(2,1)S(1)}, bf16[512,512]{1,0:T(8,128)(2,1)S(1)}, u32[]{:S(2)}, u32[]{:S(2)}) %collective-permute-start.5) | collective-permute-done | bytes 524320 | tf_op jit(solution)/shard_map/features_along_z/ppermute | solution.py:328
  58.6 1.6 collective-permute-start.10
  61.4 1.0 copy-done.8
  62.4 1.0 copy-done.10
  63.5 7.8 %forward.3.refs_8_ = f32[1024,512]{1,0:T(8,128)S(1)} custom-call(s32[34]{0:T(128)S(1)} %pad_add_fusion.where_ref, bf16[2,8,1024,512]{3,2,1,0:T(8,128)(2,1)} %get-tuple-element.235.dense_ref.a_ref, bf16[4,1024,512]{2,1,0:T(8,128)(2,1)S(1)} %collective-permute-done.6.refs_0_, bf16[4,1024,512]{2,1,0:T(8,128)(2,1)S(1)} %collective-permute-done.7.refs_1_, ...), custom_call_target="tpu_custom_call" | custom-call | flops 4294967296 | bytes 12582912 | tf_op jit(solution)/shard_map/forward/pallas_call | solution.py:139
  71.3 1.0 collective-permute-done.10.refs_3_
  72.4 1.1 collective-permute-done.11.refs_4_
  74.8 1.1 collective-permute-start.14
  75.9 1.4 broadcast_select_fusion.1
  77.4 9.5 %collective-permute-done.13.refs_6_ = bf16[512,512]{1,0:T(8,128)(2,1)S(1)} collective-permute-done((bf16[512,512]{1,0:T(8,128)(2,1)}, bf16[512,512]{1,0:T(8,128)(2,1)S(1)}, u32[]{:S(2)}, u32[]{:S(2)}) %collective-permute-start.13) | collective-permute-done | bytes 524320 | tf_op jit(solution)/shard_map/features_across/ppermute | solution.py:328
  88.1 1.5 collective-permute-start.17
  89.6 2.2 %copy-done.5 = bf16[4,1024,512]{2,1,0:T(8,128)(2,1)S(1)} copy-done((bf16[4,1024,512]{2,1,0:T(8,128)(2,1)S(1)}, bf16[4,1024,512]{2,1,0:T(8,128)(2,1)}, u32[]{:S(2)}) %copy-start.5) | copy-done | bytes 4194328
  91.8 1.0 copy-done.12
  92.9 1.0 copy-done.14
  93.9 6.3 %forward.4.refs_4_ = f32[1024,512]{1,0:T(8,128)S(1)} custom-call(s32[34]{0:T(128)S(1)} %pad_add_fusion.where_ref, bf16[2,8,1024,512]{3,2,1,0:T(8,128)(2,1)} %get-tuple-element.235.dense_ref.a_ref, bf16[4,1024,512]{2,1,0:T(8,128)(2,1)S(1)} %copy-done.3, bf16[4,1024,512]{2,1,0:T(8,128)(2,1)S(1)} %copy-done.5, bf16[512,512]{1,0:T(8,128)(2,1)S(1)} %copy-done.12, ...), custom_call_target="tpu_custom_call" | custom-call | flops 3221225472 | bytes 10485760 | tf_op jit(solution)/shard_map/forward/pallas_call | solution.py:139
  100.2 2.6 %forward.5.mine_ref = bf16[1024,512]{1,0:T(8,128)(2,1)S(1)} custom-call(s32[34]{0:T(128)S(1)} %pad_add_fusion.where_ref, bf16[2,8,1024,512]{3,2,1,0:T(8,128)(2,1)} %get-tuple-element.235.dense_ref.a_ref, bf16[4,1024,512]{2,1,0:T(8,128)(2,1)S(1)} %copy-done.3, bf16[4,1024,512]{2,1,0:T(8,128)(2,1)S(1)} %copy-done.5, ...), custom_call_target="tpu_custom_call" | custom-call | flops 1073741824 | bytes 6291456 | tf_op jit(solution)/shard_map/forward/pallas_call | solution.py:139
  102.9 2.6 %collective-permute-done.18.other_ref = bf16[1024,512]{1,0:T(8,128)(2,1)S(1)} collective-permute-done((bf16[1024,512]{1,0:T(8,128)(2,1)S(1)}, bf16[1024,512]{1,0:T(8,128)(2,1)S(1)}, u32[]{:S(2)}, u32[]{:S(2)}) %collective-permute-start.18) | collective-permute-done | bytes 1048608 | tf_op jit(solution)/shard_map/partial_sums/ppermute | solution.py:328
  105.5 7.6 %middle.1 = (bf16[512,1024]{1,0:T(8,128)(2,1)S(1)}, bf16[512,512]{1,0:T(8,128)(2,1)}, bf16[64,512]{1,0:T(8,128)(2,1)S(1)}, bf16[64,512]{1,0:T(8,128)(2,1)S(1)}, ...) custom-call(s32[34]{0:T(128)S(1)} %pad_add_fusion.where_ref, ...), custom_call_target="tpu_custom_call" | custom-call | flops 2684354560 | bytes 6291456 | tf_op jit(solution)/shard_map/middle/pallas_call | solution.py:225
  113.1 1.1 collective-permute-start.22
  114.9 1.1 collective-permute-start.19
  116.0 4.5 %collective-permute-start.20 = (bf16[64,512]{1,0:T(8,128)(2,1)S(1)}, bf16[64,512]{1,0:T(8,128)(2,1)S(1)}, u32[]{:S(2)}, u32[]{:S(2)}) collective-permute-start(bf16[64,512]{1,0:T(8,128)(2,1)S(1)} %get-tuple-element.195), channel_id=1, source_target_pairs={{0,16},{1,17},{2,18},{3,19},{4,20},{5,21},{6,22},{7,23},{8,24},{9,... | collective-permute-start | bytes 196616 | tf_op jit(solution)/shard_map/weight_grad/ppermute | solution.py:328
  121.1 4.6 %backward.5 = (bf16[512,512]{1,0:T(8,128)(2,1)S(1)}, bf16[512,512]{1,0:T(8,128)(2,1)S(1)}, bf16[512,512]{1,0:T(8,128)(2,1)S(1)}) custom-call(s32[34]{0:T(128)S(1)} %pad_add_fusion.where_ref, bf16[512,1024]{1,0:T(8,128)(2,1)S(1)} %get-tuple-element.234.grad_ref, bf16[2,8,1024,512]{3,2,1,0:T(8,128)(2,1)} %get-tuple-element.235.dense_ref.a_ref), custom_call_target="tpu_custom_call" | custom-call | flops 1610612736 | bytes 5767168 | tf_op jit(solution)/shard_map/backward/pallas_call | solution.py:271
  129.6 1.5 collective-permute-start.24
  131.1 1.1 collective-permute-start.25
  133.1 4.6 %backward.6 = (bf16[512,512]{1,0:T(8,128)(2,1)S(1)}, bf16[512,512]{1,0:T(8,128)(2,1)S(1)}, bf16[512,512]{1,0:T(8,128)(2,1)S(1)}) custom-call(s32[34]{0:T(128)S(1)} %pad_add_fusion.where_ref, bf16[512,1024]{1,0:T(8,128)(2,1)S(1)} %get-tuple-element.234.grad_ref, bf16[2,8,1024,512]{3,2,1,0:T(8,128)(2,1)} %get-tuple-element.235.dense_ref.a_ref), custom_call_target="tpu_custom_call" | custom-call | flops 1610612736 | bytes 5767168 | tf_op jit(solution)/shard_map/backward/pallas_call | solution.py:271
  137.7 5.3 %collective-permute-done.24 = bf16[64,512]{1,0:T(8,128)(2,1)S(1)} collective-permute-done((bf16[64,512]{1,0:T(8,128)(2,1)S(1)}, bf16[64,512]{1,0:T(8,128)(2,1)S(1)}, u32[]{:S(2)}, u32[]{:S(2)}) %collective-permute-start.24) | collective-permute-done | bytes 65568 | tf_op jit(solution)/shard_map/weight_grad/ppermute | solution.py:328
  144.2 1.0 add_convert_fusion.4
  145.2 1.4 collective-permute-start.32
  147.4 1.0 collective-permute-start.31
  148.5 1.3 collective-permute-start.30
  150.4 3.4 %backward.7 = (bf16[512,512]{1,0:T(8,128)(2,1)S(1)}, bf16[512,512]{1,0:T(8,128)(2,1)S(1)}) custom-call(s32[34]{0:T(128)S(1)} %pad_add_fusion.where_ref, bf16[512,1024]{1,0:T(8,128)(2,1)S(1)} %get-tuple-element.234.grad_ref, bf16[2,8,1024,512]{3,2,1,0:T(8,128)(2,1)} %get-tuple-element.235.dense_ref.a_ref), custom_call_target="tpu_custom_call" | custom-call | flops 1073741824 | bytes 4194304 | tf_op jit(solution)/shard_map/backward/pallas_call | solution.py:271
  153.8 4.5 %collective-permute-done.29 = bf16[64,512]{1,0:T(8,128)(2,1)S(1)} collective-permute-done((bf16[64,512]{1,0:T(8,128)(2,1)S(1)}, bf16[64,512]{1,0:T(8,128)(2,1)S(1)}, u32[]{:S(2)}, u32[]{:S(2)}) %collective-permute-start.29) | collective-permute-done | bytes 65568 | tf_op jit(solution)/shard_map/weight_grad/ppermute | solution.py:328
  158.3 1.3 collective-permute-done.31
  159.6 1.4 collective-permute-start.35
  161.1 1.1 collective-permute-start.36
  162.2 3.3 %collective-permute-start.33 = (bf16[64,512]{1,0:T(8,128)(2,1)S(1)}, bf16[64,512]{1,0:T(8,128)(2,1)S(1)}, u32[]{:S(2)}, u32[]{:S(2)}) collective-permute-start(bf16[64,512]{1,0:T(8,128)(2,1)S(1)} %add_convert_fusion.7), channel_id=1, source_target_pairs={{0,16},{1,17},{2,18},{3,19},{4,20},{5,21},{6,22},{7,23},{8,24},{9,... | collective-permute-start | bytes 196616 | tf_op jit(solution)/shard_map/weight_grad/ppermute | solution.py:328
  165.6 2.1 add_convert_fusion.3
  167.7 2.9 %collective-permute-start.37 = (bf16[512,512]{1,0:T(8,128)(2,1)}, bf16[512,512]{1,0:T(8,128)(2,1)S(1)}, u32[]{:S(2)}, u32[]{:S(2)}) collective-permute-start(bf16[512,512]{1,0:T(8,128)(2,1)} %add_convert_fusion.3), channel_id=1, source_target_pairs={{0,16},{1,17},{2,18},{3,19},{4,20},{5,21},{6,22},{7,23},{8,24},{9,... | collective-permute-start | bytes 1572872 | tf_op jit(solution)/shard_map/grads_along_z/ppermute | solution.py:328
  170.6 4.6 %backward.8 = (bf16[512,512]{1,0:T(8,128)(2,1)S(1)}, bf16[512,512]{1,0:T(8,128)(2,1)S(1)}, bf16[512,512]{1,0:T(8,128)(2,1)S(1)}) custom-call(s32[34]{0:T(128)S(1)} %pad_add_fusion.where_ref, bf16[512,1024]{1,0:T(8,128)(2,1)S(1)} %get-tuple-element.234.grad_ref, bf16[2,8,1024,512]{3,2,1,0:T(8,128)(2,1)} %get-tuple-element.235.dense_ref.a_ref), custom_call_target="tpu_custom_call" | custom-call | flops 1610612736 | bytes 5767168 | tf_op jit(solution)/shard_map/backward/pallas_call | solution.py:271
  175.2 6.0 %collective-permute-done.33 = bf16[64,512]{1,0:T(8,128)(2,1)S(1)} collective-permute-done((bf16[64,512]{1,0:T(8,128)(2,1)S(1)}, bf16[64,512]{1,0:T(8,128)(2,1)S(1)}, u32[]{:S(2)}, u32[]{:S(2)}) %collective-permute-start.33) | collective-permute-done | bytes 65568 | tf_op jit(solution)/shard_map/weight_grad/ppermute | solution.py:328
  181.1 1.4 collective-permute-done.34
  183.4 1.3 gather_fusion
  184.6 1.2 add_convert_fusion.2
  185.8 1.5 collective-permute-start.38
  187.3 1.2 collective-permute-start.39
  188.5 4.6 %backward.9 = (bf16[512,512]{1,0:T(8,128)(2,1)S(1)}, bf16[512,512]{1,0:T(8,128)(2,1)S(1)}, bf16[512,512]{1,0:T(8,128)(2,1)S(1)}) custom-call(s32[34]{0:T(128)S(1)} %pad_add_fusion.where_ref, bf16[512,1024]{1,0:T(8,128)(2,1)S(1)} %get-tuple-element.234.grad_ref, bf16[2,8,1024,512]{3,2,1,0:T(8,128)(2,1)} %get-tuple-element.235.dense_ref.a_ref), custom_call_target="tpu_custom_call" | custom-call | flops 1610612736 | bytes 5767168 | tf_op jit(solution)/shard_map/backward/pallas_call | solution.py:271
  193.2 1.1 maximum_convert_fusion
  194.3 6.0 %collective-permute-done.38 = bf16[512,512]{1,0:T(8,128)(2,1)S(1)} collective-permute-done((bf16[512,512]{1,0:T(8,128)(2,1)S(1)}, bf16[512,512]{1,0:T(8,128)(2,1)S(1)}, u32[]{:S(2)}, u32[]{:S(2)}) %collective-permute-start.38) | collective-permute-done | bytes 524320 | tf_op jit(solution)/shard_map/grads_across/ppermute | solution.py:328
  200.2 1.1 collective-permute-done.39
  202.1 1.3 collective-permute-start.42
  203.4 1.1 collective-permute-start.41
  204.5 10.3 %collective-permute-done.43.refs_3_ = bf16[512,512]{1,0:T(8,128)(2,1)S(1)} collective-permute-done((bf16[512,512]{1,0:T(8,128)(2,1)S(1)}, bf16[512,512]{1,0:T(8,128)(2,1)S(1)}, u32[]{:S(2)}, u32[]{:S(2)}) %collective-permute-start.43) | collective-permute-done | bytes 524320 | tf_op jit(solution)/shard_map/grads_along_z/ppermute | solution.py:328
  215.1 1.0 collective-permute-done.41.refs_1_
  216.1 1.2 grads_out.1
  (100 shorter events, 19.8 us)
Async XLA Ops:
  0.6 1.2 copy-start
  1.9 17.0 %collective-permute-start = (bf16[512,512]{1,0:T(8,128)(2,1)S(1)}, bf16[512,512]{1,0:T(8,128)(2,1)S(1)}, u32[]{:S(2)}, u32[]{:S(2)}) collective-permute-start(bf16[512,512]{1,0:T(8,128)(2,1)S(1)} %constant_dynamic-slice_fusion.refs_2_), channel_id=1, source_target_pairs={{0,2},{1,3},{2,0},{3,1},{4,6},{5,7},{6,4},{7,5},{8,10},{9,11},{10,... | collective-permute-start | bytes 1572872 | tf_op jit(solution)/shard_map/features_across/ppermute | solution.py:328
  4.9 14.0 %collective-permute-start.1 = (bf16[512,512]{1,0:T(8,128)(2,1)S(1)}, bf16[512,512]{1,0:T(8,128)(2,1)S(1)}, u32[]{:S(2)}, u32[]{:S(2)}) collective-permute-start(bf16[512,512]{1,0:T(8,128)(2,1)S(1)} %constant_dynamic-slice_fusion.refs_2_), channel_id=1, source_target_pairs={{0,4},{1,5},{2,6},{3,7},{4,0},{5,1},{6,2},{7,3},{8,12},{9,13},{10,... | collective-permute-start | bytes 1572872 | tf_op jit(solution)/shard_map/features_across/ppermute | solution.py:328
  6.4 13.1 %collective-permute-start.2 = (bf16[512,512]{1,0:T(8,128)(2,1)S(1)}, bf16[512,512]{1,0:T(8,128)(2,1)S(1)}, u32[]{:S(2)}, u32[]{:S(2)}) collective-permute-start(bf16[512,512]{1,0:T(8,128)(2,1)S(1)} %constant_dynamic-slice_fusion.refs_2_), channel_id=1, source_target_pairs={{0,8},{1,9},{2,10},{3,11},{4,12},{5,13},{6,14},{7,15},{8,0},{9,1},... | collective-permute-start | bytes 1572872 | tf_op jit(solution)/shard_map/features_along_z/ppermute | solution.py:328
  8.7 2.8 %copy-start.6 = (bf16[1,8,24,128,128]{4,3,2,1,0:T(8,128)(2,1)S(1)}, bf16[1,8,24,128,128]{4,3,2,1,0:T(8,128)(2,1)}, u32[]{:S(2)}) copy-start(bf16[1,8,24,128,128]{4,3,2,1,0:T(8,128)(2,1)} %param.10) | copy-start | bytes 18874372
  12.2 0.7 copy-start.17
  18.9 6.7 %copy-start.7 = (bf16[512,512]{1,0:T(8,128)(2,1)}, bf16[512,512]{1,0:T(8,128)(2,1)S(1)}, u32[]{:S(2)}) copy-start(bf16[512,512]{1,0:T(8,128)(2,1)S(1)} %collective-permute-done.1.refs_4_) | copy-start | bytes 1572868
  19.5 6.1 %copy-start.9 = (bf16[512,512]{1,0:T(8,128)(2,1)}, bf16[512,512]{1,0:T(8,128)(2,1)S(1)}, u32[]{:S(2)}) copy-start(bf16[512,512]{1,0:T(8,128)(2,1)S(1)} %collective-permute-done.2.refs_5_) | copy-start | bytes 1572868
  19.5 12.3 %collective-permute-start.3 = (bf16[512,512]{1,0:T(8,128)(2,1)S(1)}, bf16[512,512]{1,0:T(8,128)(2,1)S(1)}, u32[]{:S(2)}, u32[]{:S(2)}) collective-permute-start(bf16[512,512]{1,0:T(8,128)(2,1)S(1)} %collective-permute-done.2.refs_5_), channel_id=1, source_target_pairs={{0,2},{1,3},{2,0},{3,1},{4,6},{5,7},{6,4},{7,5},{8,10},{9,11},{10,... | collective-permute-start | bytes 1572872 | tf_op jit(solution)/shard_map/features_across/ppermute | solution.py:328
  20.1 11.9 %collective-permute-start.4 = (bf16[512,512]{1,0:T(8,128)(2,1)S(1)}, bf16[512,512]{1,0:T(8,128)(2,1)S(1)}, u32[]{:S(2)}, u32[]{:S(2)}) collective-permute-start(bf16[512,512]{1,0:T(8,128)(2,1)S(1)} %collective-permute-done.2.refs_5_), channel_id=1, source_target_pairs={{0,4},{1,5},{2,6},{3,7},{4,0},{5,1},{6,2},{7,3},{8,12},{9,13},{10,... | collective-permute-start | bytes 1572872 | tf_op jit(solution)/shard_map/features_across/ppermute | solution.py:328
  25.6 32.9 %collective-permute-start.6 = (bf16[4,1024,512]{2,1,0:T(8,128)(2,1)S(1)}, bf16[4,1024,512]{2,1,0:T(8,128)(2,1)S(1)}, u32[]{:S(2)}, u32[]{:S(2)}) collective-permute-start(bf16[4,1024,512]{2,1,0:T(8,128)(2,1)S(1)} %get-tuple-element.145), channel_id=1, source_target_pairs={{0,1},{1,0},{2,3},{3,2},{4,5},{5,4},{6,7},{7,6},{8,9},{9,8},{10,11... | collective-permute-start | bytes 12582920 | tf_op jit(solution)/shard_map/dense_exchange/ppermute | solution.py:328
  32.0 26.6 %collective-permute-start.7 = (bf16[4,1024,512]{2,1,0:T(8,128)(2,1)S(1)}, bf16[4,1024,512]{2,1,0:T(8,128)(2,1)S(1)}, u32[]{:S(2)}, u32[]{:S(2)}) collective-permute-start(bf16[4,1024,512]{2,1,0:T(8,128)(2,1)S(1)} %get-tuple-element.146), channel_id=1, source_target_pairs={{0,1},{1,0},{2,3},{3,2},{4,5},{5,4},{6,7},{7,6},{8,9},{9,8},{10,11... | collective-permute-start | bytes 12582920 | tf_op jit(solution)/shard_map/dense_exchange/ppermute | solution.py:328
  32.0 26.5 %collective-permute-start.5 = (bf16[512,512]{1,0:T(8,128)(2,1)S(1)}, bf16[512,512]{1,0:T(8,128)(2,1)S(1)}, u32[]{:S(2)}, u32[]{:S(2)}) collective-permute-start(bf16[512,512]{1,0:T(8,128)(2,1)S(1)} %constant_dynamic-slice_fusion.refs_2_), channel_id=1, source_target_pairs={{0,16},{1,17},{2,18},{3,19},{4,20},{5,21},{6,22},{7,23},{8,24},{9,... | collective-permute-start | bytes 1572872 | tf_op jit(solution)/shard_map/features_along_z/ppermute | solution.py:328
  34.7 23.8 %collective-permute-start.8 = (bf16[512,512]{1,0:T(8,128)(2,1)S(1)}, bf16[512,512]{1,0:T(8,128)(2,1)S(1)}, u32[]{:S(2)}, u32[]{:S(2)}) collective-permute-start(bf16[512,512]{1,0:T(8,128)(2,1)S(1)} %collective-permute-done.refs_3_), channel_id=1, source_target_pairs={{0,4},{1,5},{2,6},{3,7},{4,0},{5,1},{6,2},{7,3},{8,12},{9,13},{10,... | collective-permute-start | bytes 1572872 | tf_op jit(solution)/shard_map/features_across/ppermute | solution.py:328
  35.3 23.2 %collective-permute-start.9 = (bf16[512,512]{1,0:T(8,128)(2,1)S(1)}, bf16[512,512]{1,0:T(8,128)(2,1)S(1)}, u32[]{:S(2)}, u32[]{:S(2)}) collective-permute-start(bf16[512,512]{1,0:T(8,128)(2,1)S(1)} %collective-permute-done.4.refs_7_), channel_id=1, source_target_pairs={{0,2},{1,3},{2,0},{3,1},{4,6},{5,7},{6,4},{7,5},{8,10},{9,11},{10,... | collective-permute-start | bytes 1572872 | tf_op jit(solution)/shard_map/features_across/ppermute | solution.py:328
  58.5 12.8 %copy-start.11 = (bf16[512,512]{1,0:T(8,128)(2,1)}, bf16[512,512]{1,0:T(8,128)(2,1)S(1)}, u32[]{:S(2)}) copy-start(bf16[512,512]{1,0:T(8,128)(2,1)S(1)} %collective-permute-done.5.refs_2_) | copy-start | bytes 1572868
  58.5 12.8 %copy-start.2 = (bf16[4,1024,512]{2,1,0:T(8,128)(2,1)}, bf16[4,1024,512]{2,1,0:T(8,128)(2,1)S(1)}, u32[]{:S(2)}) copy-start(bf16[4,1024,512]{2,1,0:T(8,128)(2,1)S(1)} %collective-permute-done.6.refs_0_) | copy-start | bytes 12582916
  58.6 12.8 %copy-start.4 = (bf16[4,1024,512]{2,1,0:T(8,128)(2,1)}, bf16[4,1024,512]{2,1,0:T(8,128)(2,1)S(1)}, u32[]{:S(2)}) copy-start(bf16[4,1024,512]{2,1,0:T(8,128)(2,1)S(1)} %collective-permute-done.7.refs_1_) | copy-start | bytes 12582916
  58.6 13.8 %collective-permute-start.10 = (bf16[512,512]{1,0:T(8,128)(2,1)S(1)}, bf16[512,512]{1,0:T(8,128)(2,1)}, u32[]{:S(2)}, u32[]{:S(2)}) collective-permute-start(bf16[512,512]{1,0:T(8,128)(2,1)S(1)} %collective-permute-done.5.refs_2_), channel_id=1, source_target_pairs={{0,2},{1,3},{2,0},{3,1},{4,6},{5,7},{6,4},{7,5},{8,10},{9,11},{10,... | collective-permute-start | bytes 1572872 | tf_op jit(solution)/shard_map/features_across/ppermute | solution.py:328
  60.2 13.3 %collective-permute-start.11 = (bf16[512,512]{1,0:T(8,128)(2,1)S(1)}, bf16[512,512]{1,0:T(8,128)(2,1)S(1)}, u32[]{:S(2)}, u32[]{:S(2)}) collective-permute-start(bf16[512,512]{1,0:T(8,128)(2,1)S(1)} %collective-permute-done.5.refs_2_), channel_id=1, source_target_pairs={{0,4},{1,5},{2,6},{3,7},{4,0},{5,1},{6,2},{7,3},{8,12},{9,13},{10,... | collective-permute-start | bytes 1572872 | tf_op jit(solution)/shard_map/features_across/ppermute | solution.py:328
  60.7 13.6 %collective-permute-start.12 = (bf16[512,512]{1,0:T(8,128)(2,1)S(1)}, bf16[512,512]{1,0:T(8,128)(2,1)}, u32[]{:S(2)}, u32[]{:S(2)}) collective-permute-start(bf16[512,512]{1,0:T(8,128)(2,1)S(1)} %collective-permute-done.5.refs_2_), channel_id=1, source_target_pairs={{0,8},{1,9},{2,10},{3,11},{4,12},{5,13},{6,14},{7,15},{8,0},{9,1},... | collective-permute-start | bytes 1572872 | tf_op jit(solution)/shard_map/features_along_z/ppermute | solution.py:328
  61.4 14.5 %collective-permute-start.15 = (bf16[512,512]{1,0:T(8,128)(2,1)}, bf16[512,512]{1,0:T(8,128)(2,1)}, u32[]{:S(2)}, u32[]{:S(2)}) collective-permute-start(bf16[512,512]{1,0:T(8,128)(2,1)} %param.14), channel_id=1, source_target_pairs={{0,1},{1,0},{2,3},{3,2},{4,5},{5,4},{6,7},{7,6},{8,9},{9,8},{10,11... | collective-permute-start | bytes 1572872 | tf_op jit(solution)/shard_map/cotangent_rows/ppermute | solution.py:328
  61.4 1.0 copy-start.8
  62.4 1.0 copy-start.10
  73.5 0.8 copy-start.13
  74.2 12.7 %collective-permute-start.13 = (bf16[512,512]{1,0:T(8,128)(2,1)}, bf16[512,512]{1,0:T(8,128)(2,1)S(1)}, u32[]{:S(2)}, u32[]{:S(2)}) collective-permute-start(bf16[512,512]{1,0:T(8,128)(2,1)} %collective-permute-done.12.refs_5_), channel_id=1, source_target_pairs={{0,2},{1,3},{2,0},{3,1},{4,6},{5,7},{6,4},{7,5},{8,10},{9,11},{10,... | collective-permute-start | bytes 1572872 | tf_op jit(solution)/shard_map/features_across/ppermute | solution.py:328
  74.8 12.5 %collective-permute-start.14 = (bf16[512,512]{1,0:T(8,128)(2,1)}, bf16[512,512]{1,0:T(8,128)(2,1)S(1)}, u32[]{:S(2)}, u32[]{:S(2)}) collective-permute-start(bf16[512,512]{1,0:T(8,128)(2,1)} %collective-permute-done.12.refs_5_), channel_id=1, source_target_pairs={{0,4},{1,5},{2,6},{3,7},{4,0},{5,1},{6,2},{7,3},{8,12},{9,13},{10,... | collective-permute-start | bytes 1572872 | tf_op jit(solution)/shard_map/features_across/ppermute | solution.py:328
  75.9 13.7 %copy-start.3 = (bf16[4,1024,512]{2,1,0:T(8,128)(2,1)S(1)}, bf16[4,1024,512]{2,1,0:T(8,128)(2,1)}, u32[]{:S(2)}) copy-start(bf16[4,1024,512]{2,1,0:T(8,128)(2,1)} %copy-done.2) | copy-start | bytes 12582916
  87.3 12.9 %collective-permute-start.16 = (bf16[512,512]{1,0:T(8,128)(2,1)}, bf16[512,512]{1,0:T(8,128)(2,1)S(1)}, u32[]{:S(2)}, u32[]{:S(2)}) collective-permute-start(bf16[512,512]{1,0:T(8,128)(2,1)} %collective-permute-done.10.refs_3_), channel_id=1, source_target_pairs={{0,4},{1,5},{2,6},{3,7},{4,0},{5,1},{6,2},{7,3},{8,12},{9,13},{10,... | collective-permute-start | bytes 1572872 | tf_op jit(solution)/shard_map/features_across/ppermute | solution.py:328
  88.1 12.1 %collective-permute-start.17 = (bf16[512,512]{1,0:T(8,128)(2,1)S(1)}, bf16[512,512]{1,0:T(8,128)(2,1)S(1)}, u32[]{:S(2)}, u32[]{:S(2)}) collective-permute-start(bf16[512,512]{1,0:T(8,128)(2,1)S(1)} %collective-permute-done.14.refs_7_), channel_id=1, source_target_pairs={{0,2},{1,3},{2,0},{3,1},{4,6},{5,7},{6,4},{7,5},{8,10},{9,11},{10,... | collective-permute-start | bytes 1572872 | tf_op jit(solution)/shard_map/features_across/ppermute | solution.py:328
  89.6 2.2 %copy-start.5 = (bf16[4,1024,512]{2,1,0:T(8,128)(2,1)S(1)}, bf16[4,1024,512]{2,1,0:T(8,128)(2,1)}, u32[]{:S(2)}) copy-start(bf16[4,1024,512]{2,1,0:T(8,128)(2,1)} %copy-done.4) | copy-start | bytes 12582916
  91.8 1.0 copy-start.12
  92.8 1.0 copy-start.14
  100.2 5.3 %copy-start.15 = (bf16[512,512]{1,0:T(8,128)(2,1)S(1)}, bf16[512,512]{1,0:T(8,128)(2,1)}, u32[]{:S(2)}) copy-start(bf16[512,512]{1,0:T(8,128)(2,1)} %weight_ref.1) | copy-start | bytes 1572868
  102.8 2.7 %collective-permute-start.18 = (bf16[1024,512]{1,0:T(8,128)(2,1)S(1)}, bf16[1024,512]{1,0:T(8,128)(2,1)S(1)}, u32[]{:S(2)}, u32[]{:S(2)}) collective-permute-start(bf16[1024,512]{1,0:T(8,128)(2,1)S(1)} %forward.5.mine_ref), channel_id=1, source_target_pairs={{0,1},{1,0},{2,3},{3,2},{4,5},{5,4},{6,7},{7,6},{8,9},{9,8},{10,11... | collective-permute-start | bytes 3145736 | tf_op jit(solution)/shard_map/partial_sums/ppermute | solution.py:328
  113.1 14.0 %collective-permute-start.22 = (bf16[512,512]{1,0:T(8,128)(2,1)S(1)}, bf16[512,512]{1,0:T(8,128)(2,1)S(1)}, u32[]{:S(2)}, u32[]{:S(2)}) collective-permute-start(bf16[512,512]{1,0:T(8,128)(2,1)S(1)} %get-tuple-element.197), channel_id=1, source_target_pairs={{0,4},{1,5},{2,6},{3,7},{4,0},{5,1},{6,2},{7,3},{8,12},{9,13},{10,... | collective-permute-start | bytes 1572872 | tf_op jit(solution)/shard_map/grads_across/ppermute | solution.py:328
  114.2 13.7 %collective-permute-start.23 = (bf16[512,512]{1,0:T(8,128)(2,1)S(1)}, bf16[512,512]{1,0:T(8,128)(2,1)S(1)}, u32[]{:S(2)}, u32[]{:S(2)}) collective-permute-start(bf16[512,512]{1,0:T(8,128)(2,1)S(1)} %get-tuple-element.198), channel_id=1, source_target_pairs={{0,2},{1,3},{2,0},{3,1},{4,6},{5,7},{6,4},{7,5},{8,10},{9,11},{10,... | collective-permute-start | bytes 1572872 | tf_op jit(solution)/shard_map/grads_across/ppermute | solution.py:328
  114.9 10.8 %collective-permute-start.19 = (bf16[64,512]{1,0:T(8,128)(2,1)S(1)}, bf16[64,512]{1,0:T(8,128)(2,1)S(1)}, u32[]{:S(2)}, u32[]{:S(2)}) collective-permute-start(bf16[64,512]{1,0:T(8,128)(2,1)S(1)} %get-tuple-element.194), channel_id=1, source_target_pairs={{0,8},{1,9},{2,10},{3,11},{4,12},{5,13},{6,14},{7,15},{8,0},{9,1},... | collective-permute-start | bytes 196616 | tf_op jit(solution)/shard_map/weight_grad/ppermute | solution.py:328
  116.0 9.7 %collective-permute-start.20 = (bf16[64,512]{1,0:T(8,128)(2,1)S(1)}, bf16[64,512]{1,0:T(8,128)(2,1)S(1)}, u32[]{:S(2)}, u32[]{:S(2)}) collective-permute-start(bf16[64,512]{1,0:T(8,128)(2,1)S(1)} %get-tuple-element.195), channel_id=1, source_target_pairs={{0,16},{1,17},{2,18},{3,19},{4,20},{5,21},{6,22},{7,23},{8,24},{9,... | collective-permute-start | bytes 196616 | tf_op jit(solution)/shard_map/weight_grad/ppermute | solution.py:328
  120.5 6.2 %collective-permute-start.21 = (bf16[64,512]{1,0:T(8,128)(2,1)S(1)}, bf16[64,512]{1,0:T(8,128)(2,1)S(1)}, u32[]{:S(2)}, u32[]{:S(2)}) collective-permute-start(bf16[64,512]{1,0:T(8,128)(2,1)S(1)} %get-tuple-element.196), channel_id=1, source_target_pairs={{0,24},{1,25},{2,26},{3,27},{4,28},{5,29},{6,30},{7,31},{8,16},{9,... | collective-permute-start | bytes 196616 | tf_op jit(solution)/shard_map/weight_grad/ppermute | solution.py:328
  128.0 16.1 %collective-permute-start.27 = (bf16[512,512]{1,0:T(8,128)(2,1)S(1)}, bf16[512,512]{1,0:T(8,128)(2,1)S(1)}, u32[]{:S(2)}, u32[]{:S(2)}) collective-permute-start(bf16[512,512]{1,0:T(8,128)(2,1)S(1)} %add_convert_fusion.6), channel_id=1, source_target_pairs={{0,2},{1,3},{2,0},{3,1},{4,6},{5,7},{6,4},{7,5},{8,10},{9,11},{10,... | collective-permute-start | bytes 1572872 | tf_op jit(solution)/shard_map/grads_across/ppermute | solution.py:328
  128.8 15.4 %collective-permute-start.28 = (bf16[512,512]{1,0:T(8,128)(2,1)S(1)}, bf16[512,512]{1,0:T(8,128)(2,1)S(1)}, u32[]{:S(2)}, u32[]{:S(2)}) collective-permute-start(bf16[512,512]{1,0:T(8,128)(2,1)S(1)} %get-tuple-element.209), channel_id=1, source_target_pairs={{0,4},{1,5},{2,6},{3,7},{4,0},{5,1},{6,2},{7,3},{8,12},{9,13},{10,... | collective-permute-start | bytes 1572872 | tf_op jit(solution)/shard_map/grads_across/ppermute | solution.py:328
  129.6 13.4 %collective-permute-start.24 = (bf16[64,512]{1,0:T(8,128)(2,1)S(1)}, bf16[64,512]{1,0:T(8,128)(2,1)S(1)}, u32[]{:S(2)}, u32[]{:S(2)}) collective-permute-start(bf16[64,512]{1,0:T(8,128)(2,1)S(1)} %add_convert_fusion.8), channel_id=1, source_target_pairs={{0,2},{1,3},{2,0},{3,1},{4,6},{5,7},{6,4},{7,5},{8,10},{9,11},{10,... | collective-permute-start | bytes 196616 | tf_op jit(solution)/shard_map/weight_grad/ppermute | solution.py:328
  131.1 12.4 %collective-permute-start.25 = (bf16[64,512]{1,0:T(8,128)(2,1)S(1)}, bf16[64,512]{1,0:T(8,128)(2,1)S(1)}, u32[]{:S(2)}, u32[]{:S(2)}) collective-permute-start(bf16[64,512]{1,0:T(8,128)(2,1)S(1)} %add_convert_fusion.8), channel_id=1, source_target_pairs={{0,4},{1,5},{2,6},{3,7},{4,0},{5,1},{6,2},{7,3},{8,12},{9,13},{10,... | collective-permute-start | bytes 196616 | tf_op jit(solution)/shard_map/weight_grad/ppermute | solution.py:328
  132.1 12.0 %collective-permute-start.26 = (bf16[64,512]{1,0:T(8,128)(2,1)S(1)}, bf16[64,512]{1,0:T(8,128)(2,1)S(1)}, u32[]{:S(2)}, u32[]{:S(2)}) collective-permute-start(bf16[64,512]{1,0:T(8,128)(2,1)S(1)} %add_convert_fusion.8), channel_id=1, source_target_pairs={{0,6},{1,7},{2,4},{3,5},{4,2},{5,3},{6,0},{7,1},{8,14},{9,15},{10,... | collective-permute-start | bytes 196616 | tf_op jit(solution)/shard_map/weight_grad/ppermute | solution.py:328
  145.2 13.2 %collective-permute-start.32 = (bf16[512,512]{1,0:T(8,128)(2,1)}, bf16[512,512]{1,0:T(8,128)(2,1)S(1)}, u32[]{:S(2)}, u32[]{:S(2)}) collective-permute-start(bf16[512,512]{1,0:T(8,128)(2,1)} %add_convert_fusion.4), channel_id=1, source_target_pairs={{0,8},{1,9},{2,10},{3,11},{4,12},{5,13},{6,14},{7,15},{8,0},{9,1},... | collective-permute-start | bytes 1572872 | tf_op jit(solution)/shard_map/grads_along_z/ppermute | solution.py:328
  147.4 12.2 %collective-permute-start.31 = (bf16[512,512]{1,0:T(8,128)(2,1)}, bf16[512,512]{1,0:T(8,128)(2,1)S(1)}, u32[]{:S(2)}, u32[]{:S(2)}) collective-permute-start(bf16[512,512]{1,0:T(8,128)(2,1)} %add_convert_fusion.5), channel_id=1, source_target_pairs={{0,4},{1,5},{2,6},{3,7},{4,0},{5,1},{6,2},{7,3},{8,12},{9,13},{10,... | collective-permute-start | bytes 1572872 | tf_op jit(solution)/shard_map/grads_across/ppermute | solution.py:328
  148.5 11.2 %collective-permute-start.30 = (bf16[512,512]{1,0:T(8,128)(2,1)S(1)}, bf16[512,512]{1,0:T(8,128)(2,1)}, u32[]{:S(2)}, u32[]{:S(2)}) collective-permute-start(bf16[512,512]{1,0:T(8,128)(2,1)S(1)} %get-tuple-element.217), channel_id=1, source_target_pairs={{0,2},{1,3},{2,0},{3,1},{4,6},{5,7},{6,4},{7,5},{8,10},{9,11},{10,... | collective-permute-start | bytes 1572872 | tf_op jit(solution)/shard_map/grads_across/ppermute | solution.py:328
  149.8 8.6 %collective-permute-start.29 = (bf16[64,512]{1,0:T(8,128)(2,1)S(1)}, bf16[64,512]{1,0:T(8,128)(2,1)S(1)}, u32[]{:S(2)}, u32[]{:S(2)}) collective-permute-start(bf16[64,512]{1,0:T(8,128)(2,1)S(1)} %add_convert_fusion.7), channel_id=1, source_target_pairs={{0,8},{1,9},{2,10},{3,11},{4,12},{5,13},{6,14},{7,15},{8,0},{9,1},... | collective-permute-start | bytes 196616 | tf_op jit(solution)/shard_map/weight_grad/ppermute | solution.py:328
  159.6 22.9 %collective-permute-start.35 = (bf16[512,512]{1,0:T(8,128)(2,1)S(1)}, bf16[512,512]{1,0:T(8,128)(2,1)}, u32[]{:S(2)}, u32[]{:S(2)}) collective-permute-start(bf16[512,512]{1,0:T(8,128)(2,1)S(1)} %get-tuple-element.229), channel_id=1, source_target_pairs={{0,4},{1,5},{2,6},{3,7},{4,0},{5,1},{6,2},{7,3},{8,12},{9,13},{10,... | collective-permute-start | bytes 1572872 | tf_op jit(solution)/shard_map/grads_across/ppermute | solution.py:328
  161.1 21.5 %collective-permute-start.36 = (bf16[512,512]{1,0:T(8,128)(2,1)S(1)}, bf16[512,512]{1,0:T(8,128)(2,1)S(1)}, u32[]{:S(2)}, u32[]{:S(2)}) collective-permute-start(bf16[512,512]{1,0:T(8,128)(2,1)S(1)} %get-tuple-element.230), channel_id=1, source_target_pairs={{0,2},{1,3},{2,0},{3,1},{4,6},{5,7},{6,4},{7,5},{8,10},{9,11},{10,... | collective-permute-start | bytes 1572872 | tf_op jit(solution)/shard_map/grads_across/ppermute | solution.py:328
  162.2 18.9 %collective-permute-start.33 = (bf16[64,512]{1,0:T(8,128)(2,1)S(1)}, bf16[64,512]{1,0:T(8,128)(2,1)S(1)}, u32[]{:S(2)}, u32[]{:S(2)}) collective-permute-start(bf16[64,512]{1,0:T(8,128)(2,1)S(1)} %add_convert_fusion.7), channel_id=1, source_target_pairs={{0,16},{1,17},{2,18},{3,19},{4,20},{5,21},{6,22},{7,23},{8,24},{9,... | collective-permute-start | bytes 196616 | tf_op jit(solution)/shard_map/weight_grad/ppermute | solution.py:328
  165.5 17.0 %collective-permute-start.34 = (bf16[64,512]{1,0:T(8,128)(2,1)S(1)}, bf16[64,512]{1,0:T(8,128)(2,1)S(1)}, u32[]{:S(2)}, u32[]{:S(2)}) collective-permute-start(bf16[64,512]{1,0:T(8,128)(2,1)S(1)} %collective-permute-done.29), channel_id=1, source_target_pairs={{0,16},{1,17},{2,18},{3,19},{4,20},{5,21},{6,22},{7,23},{8,24},{9,... | collective-permute-start | bytes 196616 | tf_op jit(solution)/shard_map/weight_grad/ppermute | solution.py:328
  167.7 26.6 %collective-permute-start.37 = (bf16[512,512]{1,0:T(8,128)(2,1)}, bf16[512,512]{1,0:T(8,128)(2,1)S(1)}, u32[]{:S(2)}, u32[]{:S(2)}) collective-permute-start(bf16[512,512]{1,0:T(8,128)(2,1)} %add_convert_fusion.3), channel_id=1, source_target_pairs={{0,16},{1,17},{2,18},{3,19},{4,20},{5,21},{6,22},{7,23},{8,24},{9,... | collective-permute-start | bytes 1572872 | tf_op jit(solution)/shard_map/grads_along_z/ppermute | solution.py:328
  182.5 0.8 copy-start.20
  184.6 8.4 %collective-permute-start.40 = (bf16[256,512]{1,0:T(8,128)(2,1)}, bf16[256,512]{1,0:T(8,128)(2,1)S(1)}, u32[]{:S(2)}, u32[]{:S(2)}) collective-permute-start(bf16[256,512]{1,0:T(8,128)(2,1)} %bitcast.23), channel_id=1, source_target_pairs={{0,1},{1,0},{2,3},{3,2},{4,5},{5,4},{6,7},{7,6},{8,9},{9,8},{10,11... | collective-permute-start | bytes 786440 | tf_op jit(solution)/shard_map/weight_grad/ppermute | solution.py:328
  185.8 7.3 %copy-start.19 = (bf16[4,64,512]{2,1,0:T(8,128)(2,1)S(1)}, bf16[4,64,512]{2,1,0:T(8,128)(2,1)}, u32[]{:S(2)}) copy-start(bf16[4,64,512]{2,1,0:T(8,128)(2,1)} %gather_fusion) | copy-start | bytes 786436
  185.8 14.4 %collective-permute-start.38 = (bf16[512,512]{1,0:T(8,128)(2,1)S(1)}, bf16[512,512]{1,0:T(8,128)(2,1)S(1)}, u32[]{:S(2)}, u32[]{:S(2)}) collective-permute-start(bf16[512,512]{1,0:T(8,128)(2,1)S(1)} %add_convert_fusion.2), channel_id=1, source_target_pairs={{0,2},{1,3},{2,0},{3,1},{4,6},{5,7},{6,4},{7,5},{8,10},{9,11},{10,... | collective-permute-start | bytes 1572872 | tf_op jit(solution)/shard_map/grads_across/ppermute | solution.py:328
  187.3 14.1 %collective-permute-start.39 = (bf16[512,512]{1,0:T(8,128)(2,1)S(1)}, bf16[512,512]{1,0:T(8,128)(2,1)S(1)}, u32[]{:S(2)}, u32[]{:S(2)}) collective-permute-start(bf16[512,512]{1,0:T(8,128)(2,1)S(1)} %get-tuple-element.248), channel_id=1, source_target_pairs={{0,4},{1,5},{2,6},{3,7},{4,0},{5,1},{6,2},{7,3},{8,12},{9,13},{10,... | collective-permute-start | bytes 1572872 | tf_op jit(solution)/shard_map/grads_across/ppermute | solution.py:328
  193.1 8.9 %copy-start.21 = (bf16[512,512]{1,0:T(8,128)(2,1)S(1)}, bf16[512,512]{1,0:T(8,128)(2,1)}, u32[]{:S(2)}) copy-start(bf16[512,512]{1,0:T(8,128)(2,1)} %copy-done.20) | copy-start | bytes 1572868
  193.2 24.1 %copy-start.1 = (bf16[1024,512]{1,0:T(8,128)(2,1)S(1)}, bf16[1024,512]{1,0:T(8,128)(2,1)}, u32[]{:S(2)}) copy-start(bf16[1024,512]{1,0:T(8,128)(2,1)} %param.8) | copy-start | bytes 3145732
  201.6 13.3 %collective-permute-start.43 = (bf16[512,512]{1,0:T(8,128)(2,1)S(1)}, bf16[512,512]{1,0:T(8,128)(2,1)S(1)}, u32[]{:S(2)}, u32[]{:S(2)}) collective-permute-start(bf16[512,512]{1,0:T(8,128)(2,1)S(1)} %add_convert_fusion), channel_id=1, source_target_pairs={{0,8},{1,9},{2,10},{3,11},{4,12},{5,13},{6,14},{7,15},{8,0},{9,1},... | collective-permute-start | bytes 1572872 | tf_op jit(solution)/shard_map/grads_along_z/ppermute | solution.py:328
  202.1 13.0 %collective-permute-start.42 = (bf16[512,512]{1,0:T(8,128)(2,1)S(1)}, bf16[512,512]{1,0:T(8,128)(2,1)S(1)}, u32[]{:S(2)}, u32[]{:S(2)}) collective-permute-start(bf16[512,512]{1,0:T(8,128)(2,1)S(1)} %add_convert_fusion.1), channel_id=1, source_target_pairs={{0,4},{1,5},{2,6},{3,7},{4,0},{5,1},{6,2},{7,3},{8,12},{9,13},{10,... | collective-permute-start | bytes 1572872 | tf_op jit(solution)/shard_map/grads_across/ppermute | solution.py:328
  203.4 12.7 %collective-permute-start.41 = (bf16[512,512]{1,0:T(8,128)(2,1)S(1)}, bf16[512,512]{1,0:T(8,128)(2,1)S(1)}, u32[]{:S(2)}, u32[]{:S(2)}) collective-permute-start(bf16[512,512]{1,0:T(8,128)(2,1)S(1)} %get-tuple-element.255), channel_id=1, source_target_pairs={{0,2},{1,3},{2,0},{3,1},{4,6},{5,7},{6,4},{7,5},{8,10},{9,11},{10,... | collective-permute-start | bytes 1572872 | tf_op jit(solution)/shard_map/grads_across/ppermute | solution.py:328
  (2 other events, 1.3 us)

commit v5 on v4

--- a/solution.py
+++ b/solution.py
@@ -12,52 +12,89 @@
 BOTH = ("section", "rep")
 
 
-def dense_kernel(first, where_ref, count_ref, rows_ref, cols_ref, tiles_ref, *refs):
-    out_ref, *send_refs = refs if first == 0 else refs[1:]
+def dense_kernel(first, where_ref, packed_ref, tiles_ref, *refs):
+    out_ref = refs[-1]
     panel = first + pl.program_id(0)
-    size = tiles_ref.shape[-1]
-    per_part = out_ref.shape[-1] // size
+    size, slots = tiles_ref.shape[-1], tiles_ref.shape[1]
+    row_tiles, per_part = out_ref.shape[2] // size, out_ref.shape[3] // size
     out_ref[...] = jnp.zeros_like(out_ref)
 
     def add_tile(slot, carry):
-        row = pl.multiple_of(rows_ref[panel, slot] * size, size)
-        tile_col = cols_ref[panel, slot]
-        part = tile_col // per_part
-        col = pl.multiple_of((tile_col % per_part) * size, size)
-        out_ref[part, 0, pl.ds(row, size), pl.ds(col, size)] += tiles_ref[0, slot]
+        place = packed_ref[panel, slot]
+        row = pl.multiple_of(place // row_tiles * size, size)
+        tile_col = place % row_tiles
+        col = pl.multiple_of(tile_col % per_part * size, size)
+        out_ref[tile_col // per_part, 0, pl.ds(row, size), pl.ds(col, size)] += tiles_ref[0, slot]
         return carry
 
-    lax.fori_loop(0, count_ref[panel], add_tile, 0)
-    for shift, send_ref in enumerate(send_refs, 1):
-        send_ref[0] = out_ref[where_ref[0] ^ shift, 0]
-
-
-def make_dense(first, before, where, tiles, rows, cols, count, block_rows, n_rep):
+    lax.fori_loop(0, packed_ref[panel, slots], add_tile, 0)
+
+
+def make_dense(first, before, where, tiles, packed, block_rows, n_rep):
     panels, slots, size, _ = tiles.shape
     half = panels // 2
     part = block_rows // n_rep
-    sent = jax.ShapeDtypeStruct((half, block_rows, part), BF16)
     at = lambda p: first + p
     return pl.pallas_call(
         functools.partial(dense_kernel, first),
-        out_shape=[jax.ShapeDtypeStruct((n_rep, panels, block_rows, part), BF16)]
-        + [sent] * (n_rep - 1),
+        out_shape=jax.ShapeDtypeStruct((n_rep, panels, block_rows, part), BF16),
         grid_spec=pltpu.PrefetchScalarGridSpec(
-            num_scalar_prefetch=4,
+            num_scalar_prefetch=2,
             grid=(half,),
             in_specs=[pl.BlockSpec((1, slots, size, size), lambda p, *_: (at(p), 0, 0, 0))]
             + [pl.BlockSpec(memory_space=pl.ANY)] * (first > 0),
-            out_specs=[pl.BlockSpec((n_rep, 1, block_rows, part), lambda p, *_: (0, at(p), 0, 0))]
-            + [pl.BlockSpec((1, block_rows, part), lambda p, *_: (p, 0, 0))] * (n_rep - 1),
-        ),
-        input_output_aliases={5: 0} if first else {},
+            out_specs=pl.BlockSpec((n_rep, 1, block_rows, part), lambda p, *_: (0, at(p), 0, 0)),
+        ),
+        input_output_aliases={3: 0} if first else {},
         compiler_params=pltpu.CompilerParams(vmem_limit_bytes=36 * 2**20),
         cost_estimate=pl.CostEstimate(
             flops=0,
             transcendentals=0,
-            bytes_accessed=tiles.size + half * block_rows * block_rows * 3,
-        ),
-    )(where, count, rows, cols, tiles, *([before] if first else []))
+            bytes_accessed=tiles.size // 8,
+        ),
+    )(where, packed, tiles, *([before] if first else []))
+
+
+def other_kernel(where_ref, packed_ref, tiles_ref, out_ref):
+    panel = pl.program_id(0)
+    size, slots = tiles_ref.shape[-1], tiles_ref.shape[1]
+    row_tiles, per_part = out_ref.shape[1] // size, out_ref.shape[2] // size
+    out_ref[...] = jnp.zeros_like(out_ref)
+
+    def add_tile(slot, carry):
+        place = packed_ref[panel, slot]
+        row = pl.multiple_of(place // row_tiles * size, size)
+        tile_col = place % row_tiles
+        col = pl.multiple_of(tile_col % per_part * size, size)
+
+        @pl.when(tile_col // per_part == where_ref[0])
+        def _():
+            out_ref[0, pl.ds(row, size), pl.ds(col, size)] += tiles_ref[0, slot]
+
+        return carry
+
+    lax.fori_loop(0, packed_ref[panel, slots], add_tile, 0)
+
+
+def make_other(where, tiles, packed, block_rows, n_rep):
+    panels, slots, size, _ = tiles.shape
+    part = block_rows // n_rep
+    return pl.pallas_call(
+        other_kernel,
+        out_shape=jax.ShapeDtypeStruct((panels, block_rows, part), BF16),
+        grid_spec=pltpu.PrefetchScalarGridSpec(
+            num_scalar_prefetch=2,
+            grid=(panels,),
+            in_specs=[pl.BlockSpec((1, slots, size, size), lambda p, *_: (p, 0, 0, 0))],
+            out_specs=pl.BlockSpec((1, block_rows, part), lambda p, *_: (p, 0, 0)),
+        ),
+        compiler_params=pltpu.CompilerParams(vmem_limit_bytes=36 * 2**20),
+        cost_estimate=pl.CostEstimate(
+            flops=0,
+            transcendentals=0,
+            bytes_accessed=tiles.size // 8,
+        ),
+    )(where, packed, tiles)
 
 
 def forward_kernel(offset, n_units, n_others, has_total, where_ref, dense_ref, *refs):
@@ -66,7 +103,6 @@
     total_ref, refs = (refs[0], refs[1:]) if has_total else (None, refs)
     out_ref, sum_ref, a_buf, u_buf, sems, sum_sem = refs
     _, panels, _, part = dense_ref.shape
-    some = others[0].shape[0]
     rep = where_ref[0]
 
     def a_copy(source, slot, side):
@@ -81,7 +117,7 @@
         for side in range(2):
             place = where_ref[offset + 2 * pair + side]
             owner, panel = place // panels, place % panels
-            turn = ((owner ^ rep) - 1) * (panels // some) + panel // some
+            turn = (owner ^ rep) - 1
 
             @pl.when(owner == rep)
             def _():
@@ -91,7 +127,7 @@
 
                 @pl.when((owner != rep) & (turn == number))
                 def _():
-                    a_copy(other_ref.at[panel % some], slot, side).start()
+                    a_copy(other_ref.at[panel], slot, side).start()
 
             for number in range(side, n_units, 2):
 
@@ -161,94 +197,125 @@
     )(where, dense, *others, *units, *([total] if has_total else []))
 
 
+def slopes(mine_ref, other_ref, weight_ref, cot_ref):
+    agg = (mine_ref[...].astype(F32) + other_ref[...].astype(F32)).astype(BF16)
+    pre = jnp.dot(agg, weight_ref[...], preferred_element_type=F32)
+    sigma = jax.nn.sigmoid(pre)
+    slope = cot_ref[...].astype(F32) * sigma * (1.0 + pre * (1.0 - sigma))
+    return agg, (pre * sigma).astype(BF16), slope.astype(BF16)
+
+
 def middle_kernel(
-    n_rep, where_ref, mine_ref, other_ref, weight_ref, cot_ref, a_ref, grad_ref, act_ref, *refs
+    blocks, where_ref, mine_ref, other_ref, weight_ref, cot_ref, a_ref, grad_ref, odd_ref, even_ref
 ):
-    term_refs, (odd_ref, even_ref, sum_ref) = refs[:-3], refs[-3:]
     step = pl.program_id(0)
     part = mine_ref.shape[0]
 
-    @pl.when(step < n_rep)
+    @pl.when(step < blocks)
     def _():
-        agg = (mine_ref[...].astype(F32) + other_ref[...].astype(F32)).astype(BF16)
-        pre = jnp.dot(agg, weight_ref[...], preferred_element_type=F32)
-        sigma = jax.nn.sigmoid(pre)
-        act_ref[...] = (pre * sigma).astype(BF16)
-        slope = cot_ref[...].astype(F32) * sigma * (1.0 + pre * (1.0 - sigma))
-        pre_grad = slope.astype(BF16)
-        block = (where_ref[0] + 1 + step) % n_rep
-        grad_ref[:, pl.ds(pl.multiple_of(block * part, part), part)] = lax.dot_general(
+        _, _, pre_grad = slopes(mine_ref, other_ref, weight_ref, cot_ref)
+        grad_ref[:, pl.ds(pl.multiple_of(step * part, part), part)] = lax.dot_general(
             weight_ref[...], pre_grad, (((1,), (1,)), ((), ())), preferred_element_type=F32
         ).astype(BF16)
-        term = lax.dot_general(
-            agg, pre_grad, (((0,), (0,)), ((), ())), preferred_element_type=F32
-        )
-
-        @pl.when(step == 0)
-        def _():
-            sum_ref[...] = term
-
-        @pl.when(step > 0)
-        def _():
-            sum_ref[...] += term
-
-    @pl.when(step >= n_rep)
+
+    @pl.when(step >= blocks)
     def _():
         chunk = jnp.dot(grad_ref[...], a_ref[0, 0], preferred_element_type=F32).astype(BF16)
 
-        @pl.when(step == n_rep)
+        @pl.when(step == blocks)
         def _():
             odd_ref[...] = chunk
-            z = where_ref[1] // 4
-            size = term_refs[0].shape[0]
-            for number, term_ref in enumerate(term_refs):
-                start = (where_ref[0] * len(term_refs) + (z ^ number)) * size
-                term_ref[...] = sum_ref[pl.ds(pl.multiple_of(start, size), size), :].astype(BF16)
-
-        @pl.when(step > n_rep)
+
+        @pl.when(step > blocks)
         def _():
             even_ref[...] = chunk
 
 
-def middle(where, offset, mine, other, weight, cotangent, dense, n_rep, depth):
+def middle(where, offset, mine, other, weight, cotangent, dense):
+    rows, width = mine.shape
+    n_rep, _, _, cols = dense.shape
+    blocks = 4
+    part = rows // blocks
+    block = pl.BlockSpec((part, width), lambda i, where: (jnp.minimum(i, blocks - 1), 0))
+    fixed = lambda *shape: pl.BlockSpec(shape, lambda i, where: (0, 0))
+    kept = lambda *shape: jax.ShapeDtypeStruct(shape, BF16)
+
+    def a_block(i, where):
+        place = where[offset + jnp.maximum(i - blocks, 0)]
+        return (place % n_rep, place // n_rep, 0, 0)
+
+    return pl.pallas_call(
+        functools.partial(middle_kernel, blocks),
+        out_shape=[kept(width, rows), kept(width, cols), kept(width, cols)],
+        grid_spec=pltpu.PrefetchScalarGridSpec(
+            num_scalar_prefetch=1,
+            grid=(blocks + 2,),
+            in_specs=[
+                block,
+                block,
+                fixed(width, width),
+                block,
+                pl.BlockSpec((1, 1, rows, cols), a_block),
+            ],
+            out_specs=[fixed(width, rows), fixed(width, cols), fixed(width, cols)],
+        ),
+        compiler_params=pltpu.CompilerParams(vmem_limit_bytes=36 * 2**20),
+        cost_estimate=pl.CostEstimate(
+            flops=4 * rows * width * width + 4 * rows * width * cols,
+            transcendentals=rows * width,
+            bytes_accessed=rows * width * 12,
+        ),
+    )(where, mine, other, weight, cotangent, dense)
+
+
+def term_kernel(n_rep, where_ref, mine_ref, other_ref, weight_ref, cot_ref, act_ref, *refs):
+    term_refs, sum_ref = refs[:-1], refs[-1]
+    step = pl.program_id(0)
+    agg, activated, pre_grad = slopes(mine_ref, other_ref, weight_ref, cot_ref)
+    act_ref[...] = activated
+    term = lax.dot_general(agg, pre_grad, (((0,), (0,)), ((), ())), preferred_element_type=F32)
+
+    @pl.when(step == 0)
+    def _():
+        sum_ref[...] = term
+
+    @pl.when(step > 0)
+    def _():
+        sum_ref[...] += term
+
+    @pl.when(step == n_rep - 1)
+    def _():
+        z = where_ref[1] // 4
+        size = term_refs[0].shape[0]
+        for number, term_ref in enumerate(term_refs):
+            start = (where_ref[0] * len(term_refs) + (z ^ number)) * size
+            term_ref[...] = sum_ref[pl.ds(pl.multiple_of(start, size), size), :].astype(BF16)
+
+
+def weight_terms(where, mine, other, weight, cotangent, n_rep, depth):
     rows, width = mine.shape
     part = rows // n_rep
     size = width // n_rep // depth
-    block = lambda i, where: ((where[0] + 1 + jnp.minimum(i, n_rep - 1)) % n_rep, 0)
+    block = pl.BlockSpec((part, width), lambda i, where: ((where[0] + 1 + i) % n_rep, 0))
     fixed = lambda *shape: pl.BlockSpec(shape, lambda i, where: (0, 0))
-    kept = lambda *shape: jax.ShapeDtypeStruct(shape, BF16)
-
-    def a_block(i, where):
-        place = where[offset + jnp.maximum(i - n_rep, 0)]
-        return (place % n_rep, place // n_rep, 0, 0)
-
     return pl.pallas_call(
-        functools.partial(middle_kernel, n_rep),
-        out_shape=[kept(width, rows), kept(part, width)]
-        + [kept(size, width)] * depth
-        + [kept(width, part)] * 2,
+        functools.partial(term_kernel, n_rep),
+        out_shape=[jax.ShapeDtypeStruct((part, width), BF16)]
+        + [jax.ShapeDtypeStruct((size, width), BF16)] * depth,
         grid_spec=pltpu.PrefetchScalarGridSpec(
             num_scalar_prefetch=1,
-            grid=(n_rep + 2,),
-            in_specs=[
-                pl.BlockSpec((part, width), block),
-                pl.BlockSpec((part, width), block),
-                fixed(width, width),
-                pl.BlockSpec((part, width), block),
-                pl.BlockSpec((1, 1, rows, part), a_block),
-            ],
-            out_specs=[fixed(width, rows), fixed(part, width)]
-            + [fixed(size, width)] * depth
-            + [fixed(width, part)] * 2,
+            grid=(n_rep,),
+            in_specs=[block, block, fixed(width, width), block],
+            out_specs=[fixed(part, width)] + [fixed(size, width)] * depth,
             scratch_shapes=[pltpu.VMEM((width, width), F32)],
         ),
         compiler_params=pltpu.CompilerParams(vmem_limit_bytes=36 * 2**20),
         cost_estimate=pl.CostEstimate(
-            flops=6 * rows * width * width + 4 * rows * width * part,
+            flops=4 * rows * width * width,
             transcendentals=rows * width,
-            bytes_accessed=rows * width * 12,
-        ),
-    )(where, mine, other, weight, cotangent, dense)
+            bytes_accessed=rows * width * 8,
+        ),
+    )(where, mine, other, weight, cotangent)
 
 
 def backward_kernel(where_ref, grad_ref, a_ref, *out_refs):
@@ -364,8 +431,11 @@
                 where, offsets[names], units, total, live["dense"], live["others"], kind
             )
 
+    row_tiles = block_rows // tile_values.shape[3]
+    packed = jnp.concatenate(
+        [tile_rows[0] * row_tiles + tile_cols[0], tile_count[0][:, None]], axis=1
+    )
     panels = tile_values.shape[1]
-    tiles = (where, tile_values[0], tile_rows[0], tile_cols[0], tile_count[0], block_rows, n_rep)
     live[0] = lax.dynamic_slice_in_dim(features, rep * part, part, axis=0)
     total = None
     for pair in range(pair_count):
@@ -379,19 +449,19 @@
             live[odd] = flip(live[even], Z)
         if pair == 0:
             with jax.named_scope("dense_blocks"):
-                live["dense"], *live["sent"] = make_dense(0, None, *tiles)
+                live["dense"] = make_dense(
+                    0, None, where, tile_values[0], packed, block_rows, n_rep
+                )
+            with jax.named_scope("tiles_exchange"):
+                live["tiles"] = [
+                    (flip(tile_values[0], 0, n), flip(packed, 0, n)) for n in range(1, n_rep)
+                ]
         else:
             live["total"] = forward_step(*waiting, live.pop("waiting"), live.get("total"))
         close()
 
         with jax.named_scope("features_across"):
             live["odd_x"], live["odd_y"] = flip(live[odd], X), flip(live[odd], Y)
-        if pair == 0:
-            with jax.named_scope("dense_exchange"):
-                one = [flip(value, 0, n) for n, value in enumerate(live.pop("sent"), 1)]
-            with jax.named_scope("dense_blocks"):
-                first = panels // 2
-                live["dense"], *live["sent"] = make_dense(first, live["dense"], *tiles)
         if not last:
             with jax.named_scope("features_along_z"):
                 live[later] = flip(live[later - low_bit(later)], low_bit(later))
@@ -403,9 +473,14 @@
         with jax.named_scope("features_across"):
             crossed = [flip(live["even_x"], Y), flip(live["odd_y"], X)]
         if pair == 0:
-            with jax.named_scope("dense_exchange"):
-                two = [flip(value, 0, n) for n, value in enumerate(live.pop("sent"), 1)]
-                live["others"] = [half for halves in zip(one, two) for half in halves]
+            with jax.named_scope("dense_blocks"):
+                live["dense"] = make_dense(
+                    panels // 2, live["dense"], where, tile_values[0], packed, block_rows, n_rep
+                )
+            with jax.named_scope("other_blocks"):
+                live["others"] = [
+                    make_other(where, *sent, block_rows, n_rep) for sent in live.pop("tiles")
+                ]
         units = [live[even], live.pop("even_x"), live.pop("even_y")]
         units += [live[odd], live.pop("odd_x"), live.pop("odd_y")]
         if pair > 0:
@@ -426,16 +501,9 @@
 
     depth = n_section // 4
     with jax.named_scope("middle"):
-        grad, activated, *terms, odd_diag, even_diag = middle(
-            where,
-            offsets["first", pair_count - 1],
-            partial,
-            other,
-            weight,
-            live["cotangent"],
-            live["dense"],
-            n_rep,
-            depth,
+        rows = (partial, other, weight, live["cotangent"])
+        grad, odd_diag, even_diag = middle(
+            where, offsets["first", pair_count - 1], *rows, live["dense"]
         )
 
     def backward_step(name, count):
@@ -445,19 +513,25 @@
     add = lambda *values: functools.reduce(jnp.add, [value.astype(F32) for value in values])
 
     def weight_step(phase):
+        if phase == 0:
+            live["activated"], *live["terms"] = weight_terms(where, *rows, n_rep, depth)
+            return
+        name = next((name for name in ("odd", "even", "first") if name in live), None)
+        if name:
+            live[name], live["terms"] = lax.optimization_barrier((live[name], live["terms"]))
         terms = live["terms"]
-        if phase == 0:
+        if phase == 1:
             sums = [terms[0]] + [flip(term, Z * n) for n, term in enumerate(terms[1:], 1)]
             live["terms"] = [add(*sums).astype(BF16)]
-        elif phase == 1:
+        elif phase == 2:
             sums = [terms[0]] + [flip(terms[0], mask) for mask in (X, Y, X + Y)]
             live["terms"] = [(add(*sums[:2]) + add(*sums[2:])).astype(BF16)]
-        elif 1 << phase - 2 < depth:
-            live["terms"] = terms + [flip(term, Z << phase - 2) for term in terms]
+        elif 1 << phase - 3 < depth:
+            live["terms"] = terms + [flip(term, Z << phase - 3) for term in terms]
         elif "weight_grad" not in live:
             z = section // 4
-            rows = jnp.stack(terms)[z ^ jnp.arange(depth)].reshape(-1, width)
-            live["weight_grad"] = gather_rep(rows).astype(F32)
+            rows_of = jnp.stack(terms)[z ^ jnp.arange(depth)].reshape(-1, width)
+            live["weight_grad"] = gather_rep(rows_of).astype(F32)
 
     phases = iter(range(3 * pair_count))
 
@@ -466,7 +540,7 @@
             weight_step(next(phases))
         close(*open_names)
 
-    live = {"grad": grad, "dense": live["dense"], "terms": terms}
+    live = {"grad": grad, "dense": live["dense"]}
     live["first"] = [odd_diag, even_diag]
     for pair in reversed(range(pair_count)):
         even = 2 * pair * Z
@@ -507,7 +581,7 @@
             live["passed"] = add(*sums).astype(BF16)
     with jax.named_scope("grads_out"):
         feat_grad = final_sum(sums)
-    return (activated, feat_grad, live["weight_grad"])
+    return (live["activated"], feat_grad, live["weight_grad"])
 
 
 def solution(mesh):

time: 218 us -> 213 us (0.977)
  waiting for transfers between devices: 83.9 us -> 69.3 us
  Pallas kernels: 57.7 us -> 67.6 us
    ppermute x44, waiting for transfers between devices: 83.9 us -> 69.3 us  [flip(): return lax.ppermute(value, BOTH, pairs)]
    pallas_call x3 -> x5, Pallas kernels: 18.1 us -> 26.5 us  [the longest x2 9.32 us: make_dense(): pl.pallas_call(functools.partial(dense_kernel, first), out_shape=jax.Shap...]
    unnamed x44 -> x36, local copies, waits for them, and re-layouts: 14 us -> 12.9 us
  transfers between devices with their start and end apart: 44 -> 44, of which waited for: 24 -> 23; matrix products, arithmetic and copies ran while one was open for 4% -> 6% of each run, Pallas kernels for 21% -> 27%
where the time goes in v5:
time: 213 us; the launch traced here: 212 us
  waiting for transfers between devices  69.3 us (33%)
  Pallas kernels  67.6 us (32%)
  starting transfers between devices  48.9 us (23%)
  local copies, waits for them, and re-layouts  14.9 us (7%)
  other arithmetic  9.96 us (5%)
    ppermute x44, waiting for transfers between devices, flip(): return lax.ppermute(value, BOTH, pairs)  69.3 us
    ppermute x44, starting transfers between devices, flip(): return lax.ppermute(value, BOTH, pairs)  48.9 us
    pallas_call x5, Pallas kernels, backward_part(): pl.pallas_call(backward_kernel, out_shape=[jax.ShapeDtypeStruct((width, c...  23.3 us
    pallas_call x3, Pallas kernels, forward_part(): pl.pallas_call(functools.partial(forward_kernel, offset, n_units, n_other...  16.6 us
    unnamed x36, local copies, waits for them, and re-layouts  12.9 us
    pallas_call x2, Pallas kernels, make_dense(): pl.pallas_call(functools.partial(dense_kernel, first), out_shape=jax.Shap...  9.32 us
    pallas_call x1, Pallas kernels, make_other(): pl.pallas_call(other_kernel, out_shape=jax.ShapeDtypeStruct((panels, bloc...  7 us
    pallas_call x1, Pallas kernels, middle(): pl.pallas_call(functools.partial(middle_kernel, blocks), out_shape=[kept(...  6.71 us
  transfers between devices with their start and end apart: 44, of which 23 were waited for; matrix products, arithmetic and copies ran while one was open for 6% of the time, Pallas kernels for 27%

profile of v5, /device:TPU:0, one launch (start us, length us, event | category | flops | bytes accessed | tf_op | source)
XLA Modules:
  0.0 211.7 jit_solution(16322897246904801756)
XLA Ops:
  1.9 3.0 %collective-permute-start = (bf16[512,512]{1,0:T(8,128)(2,1)S(1)}, bf16[512,512]{1,0:T(8,128)(2,1)S(1)}, u32[]{:S(2)}, u32[]{:S(2)}) collective-permute-start(bf16[512,512]{1,0:T(8,128)(2,1)S(1)} %constant_dynamic-slice_fusion.refs_1_), channel_id=1, source_target_pairs={{0,2},{1,3},{2,0},{3,1},{4,6},{5,7},{6,4},{7,5},{8,10},{9,11},{10,... | collective-permute-start | bytes 1572872 | tf_op jit(solution)/shard_map/features_across/ppermute | solution.py:395
  4.9 1.5 collective-permute-start.1
  6.4 1.6 collective-permute-start.2
  10.3 2.8 %copy-done.4 = bf16[1,8,24,128,128]{4,3,2,1,0:T(8,128)(2,1)S(1)} copy-done((bf16[1,8,24,128,128]{4,3,2,1,0:T(8,128)(2,1)S(1)}, bf16[1,8,24,128,128]{4,3,2,1,0:T(8,128)(2,1)}, u32[]{:S(2)}) %copy-start.4) | copy-done | bytes 6291480
  13.0 4.7 %dense_blocks.2.refs_0_ = bf16[2,8,1024,512]{3,2,1,0:T(8,128)(2,1)} custom-call(s32[34]{0:T(128)S(1)} %pad_add_fusion.1.where_ref, s32[8,25]{1,0:T(8,128)S(1)} %pad_add_fusion.packed_ref, bf16[8,24,128,128]{3,2,1,0:T(8,128)(2,1)S(1)} %bitcast.16), custom_call_target="tpu_custom_call" | custom-call | bytes 393216 | tf_op jit(solution)/shard_map/dense_blocks/pallas_call | solution.py:38
  18.3 1.2 collective-permute-done.2.refs_4_
  20.4 2.7 %collective-permute-start.7 = (bf16[512,512]{1,0:T(8,128)(2,1)S(1)}, bf16[512,512]{1,0:T(8,128)(2,1)S(1)}, u32[]{:S(2)}, u32[]{:S(2)}) collective-permute-start(bf16[512,512]{1,0:T(8,128)(2,1)S(1)} %constant_dynamic-slice_fusion.refs_1_), channel_id=1, source_target_pairs={{0,16},{1,17},{2,18},{3,19},{4,20},{5,21},{6,22},{7,23},{8,24},{9,... | collective-permute-start | bytes 1572872 | tf_op jit(solution)/shard_map/features_along_z/ppermute | solution.py:395
  23.2 9.1 %collective-permute-done.5.refs_5_ = bf16[512,512]{1,0:T(8,128)(2,1)S(1)} collective-permute-done((bf16[512,512]{1,0:T(8,128)(2,1)S(1)}, bf16[512,512]{1,0:T(8,128)(2,1)S(1)}, u32[]{:S(2)}, u32[]{:S(2)}) %collective-permute-start.5) | collective-permute-done | bytes 524320 | tf_op jit(solution)/shard_map/features_across/ppermute | solution.py:395
  34.4 4.6 %dense_blocks.3.dense_ref.a_ref = bf16[2,8,1024,512]{3,2,1,0:T(8,128)(2,1)} custom-call(s32[34]{0:T(128)S(1)} %pad_add_fusion.1.where_ref, s32[8,25]{1,0:T(8,128)S(1)} %pad_add_fusion.packed_ref, bf16[8,24,128,128]{3,2,1,0:T(8,128)(2,1)S(1)} %bitcast.17, bf16[2,8,1024,512]{3,2,1,0:T(8,128)(2,1)} %dense_blocks.2.refs_0_), custom_call_target="tpu_custom_call", output_to_operand_aliasing={{}: (3, {})} | custom-call | bytes 393216 | tf_op jit(solution)/shard_map/dense_blocks/pallas_call | solution.py:38
  39.1 7.0 %other_blocks.1.refs_0_ = bf16[8,1024,512]{2,1,0:T(8,128)(2,1)S(1)} custom-call(s32[34]{0:T(128)S(1)} %pad_add_fusion.1.where_ref, s32[8,25]{1,0:T(8,128)S(1)} %collective-permute-done.4.packed_ref, bf16[8,24,128,128]{3,2,1,0:T(8,128)(2,1)} %collective-permute-done.3.tiles_ref), custom_call_target="tpu_custom_call" | custom-call | bytes 393216 | tf_op jit(solution)/shard_map/other_blocks/pallas_call | solution.py:82
  46.1 3.6 %collective-permute-start.10 = (bf16[512,512]{1,0:T(8,128)(2,1)S(1)}, bf16[512,512]{1,0:T(8,128)(2,1)}, u32[]{:S(2)}, u32[]{:S(2)}) collective-permute-start(bf16[512,512]{1,0:T(8,128)(2,1)S(1)} %collective-permute-done.7.refs_1_), channel_id=1, source_target_pairs={{0,2},{1,3},{2,0},{3,1},{4,6},{5,7},{6,4},{7,5},{8,10},{9,11},{10,... | collective-permute-start | bytes 1572872 | tf_op jit(solution)/shard_map/features_across/ppermute | solution.py:395
  49.7 1.7 collective-permute-start.11
  51.4 1.0 copy-done.6
  52.4 1.0 copy-done.10
  53.5 7.8 %forward.3.refs_7_ = f32[1024,512]{1,0:T(8,128)S(1)} custom-call(s32[34]{0:T(128)S(1)} %pad_add_fusion.1.where_ref, bf16[2,8,1024,512]{3,2,1,0:T(8,128)(2,1)} %dense_blocks.3.dense_ref.a_ref, bf16[8,1024,512]{2,1,0:T(8,128)(2,1)S(1)} %other_blocks.1.refs_0_, bf16[512,512]{1,0:T(8,128)(2,1)S(1)} %constant_dynamic-slice_fusion.refs_1_, ...), custom_call_target="tpu_custom_call" | custom-call | flops 4294967296 | bytes 12582912 | tf_op jit(solution)/shard_map/forward/pallas_call | solution.py:175
  63.0 1.8 collective-permute-start.14
  64.9 1.3 broadcast_select_fusion.1
  66.2 10.1 %collective-permute-done.13.refs_5_ = bf16[512,512]{1,0:T(8,128)(2,1)S(1)} collective-permute-done((bf16[512,512]{1,0:T(8,128)(2,1)}, bf16[512,512]{1,0:T(8,128)(2,1)S(1)}, u32[]{:S(2)}, u32[]{:S(2)}) %collective-permute-start.13) | collective-permute-done | bytes 524320 | tf_op jit(solution)/shard_map/features_across/ppermute | solution.py:395
  76.7 1.7 collective-permute-start.16
  78.6 3.4 %copy-done.3 = bf16[8,1024,512]{2,1,0:T(8,128)(2,1)S(1)} copy-done((bf16[8,1024,512]{2,1,0:T(8,128)(2,1)S(1)}, bf16[8,1024,512]{2,1,0:T(8,128)(2,1)}, u32[]{:S(2)}) %copy-start.3) | copy-done | bytes 8388632
  82.0 1.0 copy-done.8
  83.1 1.0 copy-done.12
  84.1 6.3 %forward.4.refs_3_ = f32[1024,512]{1,0:T(8,128)S(1)} custom-call(s32[34]{0:T(128)S(1)} %pad_add_fusion.1.where_ref, bf16[2,8,1024,512]{3,2,1,0:T(8,128)(2,1)} %dense_blocks.3.dense_ref.a_ref, bf16[8,1024,512]{2,1,0:T(8,128)(2,1)S(1)} %copy-done.3, bf16[512,512]{1,0:T(8,128)(2,1)S(1)} %copy-done.8, bf16[512,512]{1,0:T(8,128)(2,1)} %collective-permute-done.10.refs_2_, ...), custom_call_target="tpu_custom_call" | custom-call | flops 3221225472 | bytes 10485760 | tf_op jit(solution)/shard_map/forward/pallas_call | solution.py:175
  90.5 2.5 %forward.5.mine_ref = bf16[1024,512]{1,0:T(8,128)(2,1)S(1)} custom-call(s32[34]{0:T(128)S(1)} %pad_add_fusion.1.where_ref, bf16[2,8,1024,512]{3,2,1,0:T(8,128)(2,1)} %dense_blocks.3.dense_ref.a_ref, bf16[8,1024,512]{2,1,0:T(8,128)(2,1)S(1)} %copy-done.3, bf16[512,512]{1,0:T(8,128)(2,1)S(1)} %collective-permute-done.16.refs_1_, ...), custom_call_target="tpu_custom_call" | custom-call | flops 1073741824 | bytes 6291456 | tf_op jit(solution)/shard_map/forward/pallas_call | solution.py:175
  93.1 2.6 %collective-permute-done.18.other_ref = bf16[1024,512]{1,0:T(8,128)(2,1)S(1)} collective-permute-done((bf16[1024,512]{1,0:T(8,128)(2,1)S(1)}, bf16[1024,512]{1,0:T(8,128)(2,1)S(1)}, u32[]{:S(2)}, u32[]{:S(2)}) %collective-permute-start.18) | collective-permute-done | bytes 1048608 | tf_op jit(solution)/shard_map/partial_sums/ppermute | solution.py:395
  95.7 6.7 %middle.1 = (bf16[512,1024]{1,0:T(8,128)(2,1)S(1)}, bf16[512,512]{1,0:T(8,128)(2,1)S(1)}, bf16[512,512]{1,0:T(8,128)(2,1)S(1)}) custom-call(s32[34]{0:T(128)S(1)} %pad_add_fusion.1.where_ref, bf16[1024,512]{1,0:T(8,128)(2,1)S(1)} %forward.5.mine_ref, bf16[1024,512]{1,0:T(8,128)(2,1)S(1)} %collective-permute-done.18.other_ref, ...), custom_call_target="tpu_custom_call" | custom-call | flops 2147483648 | bytes 6291456 | tf_op jit(solution)/shard_map/middle/pallas_call | solution.py:247
  102.5 1.4 collective-permute-start.19
  104.5 3.5 %weight_grad.1 = (bf16[512,512]{1,0:T(8,128)(2,1)}, bf16[64,512]{1,0:T(8,128)(2,1)S(1)}, bf16[64,512]{1,0:T(8,128)(2,1)S(1)}, bf16[64,512]{1,0:T(8,128)(2,1)S(1)}, bf16[64,512]{1,0:T(8,128)(2,1)S(1)}) custom-call(s32[34]{0:T(128)S(1)} %pad_add_fusion.1.where_ref, bf16[1024,512]{1,0:T(8,128)(2,1)S(1)} %forward.5.mine_ref, ...), custom_call_target="tpu_custom_call" | custom-call | flops 1073741824 | bytes 4194304 | tf_op jit(solution)/shard_map/weight_grad/pallas_call | solution.py:301
  108.0 4.6 %backward.5 = (bf16[512,512]{1,0:T(8,128)(2,1)S(1)}, bf16[512,512]{1,0:T(8,128)(2,1)S(1)}, bf16[512,512]{1,0:T(8,128)(2,1)S(1)}) custom-call(s32[34]{0:T(128)S(1)} %pad_add_fusion.1.where_ref, bf16[512,1024]{1,0:T(8,128)(2,1)S(1)} %get-tuple-element.269.grad_ref, bf16[2,8,1024,512]{3,2,1,0:T(8,128)(2,1)} %dense_blocks.3.dense_ref.a_ref), custom_call_target="tpu_custom_call" | custom-call | flops 1610612736 | bytes 5767168 | tf_op jit(solution)/shard_map/backward/pallas_call | solution.py:338
  112.6 3.9 %collective-permute-done.19 = bf16[512,512]{1,0:T(8,128)(2,1)S(1)} collective-permute-done((bf16[512,512]{1,0:T(8,128)(2,1)S(1)}, bf16[512,512]{1,0:T(8,128)(2,1)S(1)}, u32[]{:S(2)}, u32[]{:S(2)}) %collective-permute-start.19) | collective-permute-done | bytes 524320 | tf_op jit(solution)/shard_map/grads_across/ppermute | solution.py:395
  116.5 1.1 collective-permute-done.20
  118.5 1.7 collective-permute-start.25
  120.1 4.6 %backward.6 = (bf16[512,512]{1,0:T(8,128)(2,1)S(1)}, bf16[512,512]{1,0:T(8,128)(2,1)S(1)}, bf16[512,512]{1,0:T(8,128)(2,1)S(1)}) custom-call(s32[34]{0:T(128)S(1)} %pad_add_fusion.1.where_ref, bf16[512,1024]{1,0:T(8,128)(2,1)S(1)} %get-tuple-element.269.grad_ref, bf16[2,8,1024,512]{3,2,1,0:T(8,128)(2,1)} %dense_blocks.3.dense_ref.a_ref), custom_call_target="tpu_custom_call" | custom-call | flops 1610612736 | bytes 5767168 | tf_op jit(solution)/shard_map/backward/pallas_call | solution.py:338
  124.7 5.2 %collective-permute-start.23 = (bf16[64,512]{1,0:T(8,128)(2,1)S(1)}, bf16[64,512]{1,0:T(8,128)(2,1)S(1)}, u32[]{:S(2)}, u32[]{:S(2)}) collective-permute-start(bf16[64,512]{1,0:T(8,128)(2,1)S(1)} %get-tuple-element.232), channel_id=1, source_target_pairs={{0,24},{1,25},{2,26},{3,27},{4,28},{5,29},{6,30},{7,31},{8,16},{9,... | collective-permute-start | bytes 196616 | tf_op jit(solution)/shard_map/weight_grad/ppermute | solution.py:395
  130.6 1.8 collective-permute-done.23
  132.4 2.8 %collective-permute-done.22 = bf16[64,512]{1,0:T(8,128)(2,1)S(1)} collective-permute-done((bf16[64,512]{1,0:T(8,128)(2,1)S(1)}, bf16[64,512]{1,0:T(8,128)(2,1)S(1)}, u32[]{:S(2)}, u32[]{:S(2)}) %collective-permute-start.22) | collective-permute-done | bytes 65568 | tf_op jit(solution)/shard_map/weight_grad/ppermute | solution.py:395
  135.2 1.4 collective-permute-start.29
  138.2 3.4 %backward.7 = (bf16[512,512]{1,0:T(8,128)(2,1)S(1)}, bf16[512,512]{1,0:T(8,128)(2,1)S(1)}) custom-call(s32[34]{0:T(128)S(1)} %pad_add_fusion.1.where_ref, bf16[512,1024]{1,0:T(8,128)(2,1)S(1)} %get-tuple-element.269.grad_ref, bf16[2,8,1024,512]{3,2,1,0:T(8,128)(2,1)} %dense_blocks.3.dense_ref.a_ref), custom_call_target="tpu_custom_call" | custom-call | flops 1073741824 | bytes 4194304 | tf_op jit(solution)/shard_map/backward/pallas_call | solution.py:338
  141.6 1.7 collective-permute-start.28
  143.6 5.1 %collective-permute-done.28 = bf16[64,512]{1,0:T(8,128)(2,1)S(1)} collective-permute-done((bf16[64,512]{1,0:T(8,128)(2,1)S(1)}, bf16[64,512]{1,0:T(8,128)(2,1)S(1)}, u32[]{:S(2)}, u32[]{:S(2)}) %collective-permute-start.28) | collective-permute-done | bytes 65568 | tf_op jit(solution)/shard_map/weight_grad/ppermute | solution.py:395
  148.6 1.3 collective-permute-start.26
  149.9 1.3 collective-permute-done.27
  151.2 1.7 collective-permute-done.26
  153.0 2.9 %collective-permute-start.33 = (bf16[512,512]{1,0:T(8,128)(2,1)S(1)}, bf16[512,512]{1,0:T(8,128)(2,1)S(1)}, u32[]{:S(2)}, u32[]{:S(2)}) collective-permute-start(bf16[512,512]{1,0:T(8,128)(2,1)S(1)} %get-tuple-element.264), channel_id=1, source_target_pairs={{0,4},{1,5},{2,6},{3,7},{4,0},{5,1},{6,2},{7,3},{8,12},{9,13},{10,... | collective-permute-start | bytes 1572872 | tf_op jit(solution)/shard_map/grads_across/ppermute | solution.py:395
  155.8 1.2 collective-permute-start.34
  157.1 5.4 %backward.8 = (bf16[512,512]{1,0:T(8,128)(2,1)S(1)}, bf16[512,512]{1,0:T(8,128)(2,1)}, bf16[512,512]{1,0:T(8,128)(2,1)S(1)}) custom-call(s32[34]{0:T(128)S(1)} %pad_add_fusion.1.where_ref, bf16[512,1024]{1,0:T(8,128)(2,1)S(1)} %get-tuple-element.269.grad_ref, bf16[2,8,1024,512]{3,2,1,0:T(8,128)(2,1)} %dense_blocks.3.dense_ref.a_ref), custom_call_target="tpu_custom_call" | custom-call | flops 1610612736 | bytes 5767168 | tf_op jit(solution)/shard_map/backward/pallas_call | solution.py:338
  162.6 1.1 add_convert_fusion.3
  163.7 1.0 collective-permute-start.37
  164.7 2.0 collective-permute-done.32
  166.7 1.0 add_convert_fusion.2
  169.0 5.4 %backward.9 = (bf16[512,512]{1,0:T(8,128)(2,1)}, bf16[512,512]{1,0:T(8,128)(2,1)S(1)}, bf16[512,512]{1,0:T(8,128)(2,1)S(1)}) custom-call(s32[34]{0:T(128)S(1)} %pad_add_fusion.1.where_ref, bf16[512,1024]{1,0:T(8,128)(2,1)S(1)} %get-tuple-element.269.grad_ref, bf16[2,8,1024,512]{3,2,1,0:T(8,128)(2,1)} %dense_blocks.3.dense_ref.a_ref), custom_call_target="tpu_custom_call" | custom-call | flops 1610612736 | bytes 5767168 | tf_op jit(solution)/shard_map/backward/pallas_call | solution.py:338
  174.4 2.0 collective-permute-start.35
  177.3 10.7 %collective-permute-done.37.refs_4_ = bf16[512,512]{1,0:T(8,128)(2,1)S(1)} collective-permute-done((bf16[512,512]{1,0:T(8,128)(2,1)}, bf16[512,512]{1,0:T(8,128)(2,1)S(1)}, u32[]{:S(2)}, u32[]{:S(2)}) %collective-permute-start.37) | collective-permute-done | bytes 524320 | tf_op jit(solution)/shard_map/grads_along_z/ppermute | solution.py:395
  189.4 1.1 collective-permute-start.40
  191.4 0.9 collective-permute-start.41
  192.4 1.3 gather_fusion
  193.7 1.4 add_convert_fusion
  195.4 1.0 broadcast_select_fusion.3
  196.4 1.1 maximum_convert_fusion
  197.5 4.1 %collective-permute-done.40.refs_1_ = bf16[512,512]{1,0:T(8,128)(2,1)S(1)} collective-permute-done((bf16[512,512]{1,0:T(8,128)(2,1)}, bf16[512,512]{1,0:T(8,128)(2,1)S(1)}, u32[]{:S(2)}, u32[]{:S(2)}) %collective-permute-start.40) | collective-permute-done | bytes 524320 | tf_op jit(solution)/shard_map/grads_across/ppermute | solution.py:395
  201.6 1.7 collective-permute-done.41.refs_2_
  203.3 6.2 %collective-permute-done.42.refs_3_ = bf16[512,512]{1,0:T(8,128)(2,1)S(1)} collective-permute-done((bf16[512,512]{1,0:T(8,128)(2,1)S(1)}, bf16[512,512]{1,0:T(8,128)(2,1)S(1)}, u32[]{:S(2)}, u32[]{:S(2)}) %collective-permute-start.42) | collective-permute-done | bytes 524320 | tf_op jit(solution)/shard_map/grads_along_z/ppermute | solution.py:395
  209.5 1.0 copy-done.15
  210.5 1.2 grads_out.1
  (97 shorter events, 19.0 us)
Async XLA Ops:
  0.6 1.2 copy-start
  0.6 18.9 %collective-permute-start.3 = (bf16[8,24,128,128]{3,2,1,0:T(8,128)(2,1)}, bf16[8,24,128,128]{3,2,1,0:T(8,128)(2,1)}, u32[]{:S(2)}, u32[]{:S(2)}) collective-permute-start(bf16[8,24,128,128]{3,2,1,0:T(8,128)(2,1)} %bitcast.15), channel_id=1, source_target_pairs={{0,1},{1,0},{2,3},{3,2},{4,5},{5,4},{6,7},{7,6},{8,9},{9,8},{10,11... | collective-permute-start | bytes 18874376 | tf_op jit(solution)/shard_map/tiles_exchange/ppermute | solution.py:395
  1.9 15.9 %collective-permute-start = (bf16[512,512]{1,0:T(8,128)(2,1)S(1)}, bf16[512,512]{1,0:T(8,128)(2,1)S(1)}, u32[]{:S(2)}, u32[]{:S(2)}) collective-permute-start(bf16[512,512]{1,0:T(8,128)(2,1)S(1)} %constant_dynamic-slice_fusion.refs_1_), channel_id=1, source_target_pairs={{0,2},{1,3},{2,0},{3,1},{4,6},{5,7},{6,4},{7,5},{8,10},{9,11},{10,... | collective-permute-start | bytes 1572872 | tf_op jit(solution)/shard_map/features_across/ppermute | solution.py:395
  4.9 13.4 %collective-permute-start.1 = (bf16[512,512]{1,0:T(8,128)(2,1)S(1)}, bf16[512,512]{1,0:T(8,128)(2,1)S(1)}, u32[]{:S(2)}, u32[]{:S(2)}) collective-permute-start(bf16[512,512]{1,0:T(8,128)(2,1)S(1)} %constant_dynamic-slice_fusion.refs_1_), channel_id=1, source_target_pairs={{0,4},{1,5},{2,6},{3,7},{4,0},{5,1},{6,2},{7,3},{8,12},{9,13},{10,... | collective-permute-start | bytes 1572872 | tf_op jit(solution)/shard_map/features_across/ppermute | solution.py:395
  6.4 13.1 %collective-permute-start.2 = (bf16[512,512]{1,0:T(8,128)(2,1)S(1)}, bf16[512,512]{1,0:T(8,128)(2,1)S(1)}, u32[]{:S(2)}, u32[]{:S(2)}) collective-permute-start(bf16[512,512]{1,0:T(8,128)(2,1)S(1)} %constant_dynamic-slice_fusion.refs_1_), channel_id=1, source_target_pairs={{0,8},{1,9},{2,10},{3,11},{4,12},{5,13},{6,14},{7,15},{8,0},{9,1},... | collective-permute-start | bytes 1572872 | tf_op jit(solution)/shard_map/features_along_z/ppermute | solution.py:395
  9.5 8.2 %collective-permute-start.4 = (s32[8,25]{1,0:T(8,128)S(1)}, s32[8,25]{1,0:T(8,128)S(1)}, u32[]{:S(2)}, u32[]{:S(2)}) collective-permute-start(s32[8,25]{1,0:T(8,128)S(1)} %pad_add_fusion.packed_ref), channel_id=1, source_target_pairs={{0,1},{1,0},{2,3},{3,2},{4,5},{5,4},{6,7},{7,6},{8,9},{9,8},{10,11... | collective-permute-start | bytes 2408 | tf_op jit(solution)/shard_map/tiles_exchange/ppermute | solution.py:395
  10.3 2.8 %copy-start.4 = (bf16[1,8,24,128,128]{4,3,2,1,0:T(8,128)(2,1)S(1)}, bf16[1,8,24,128,128]{4,3,2,1,0:T(8,128)(2,1)}, u32[]{:S(2)}) copy-start(bf16[1,8,24,128,128]{4,3,2,1,0:T(8,128)(2,1)} %param.10) | copy-start | bytes 18874372
  18.3 20.8 %copy-start.5 = (bf16[512,512]{1,0:T(8,128)(2,1)}, bf16[512,512]{1,0:T(8,128)(2,1)S(1)}, u32[]{:S(2)}) copy-start(bf16[512,512]{1,0:T(8,128)(2,1)S(1)} %collective-permute-done.1.refs_3_) | copy-start | bytes 1572868
  19.5 19.5 %copy-start.9 = (bf16[512,512]{1,0:T(8,128)(2,1)}, bf16[512,512]{1,0:T(8,128)(2,1)S(1)}, u32[]{:S(2)}) copy-start(bf16[512,512]{1,0:T(8,128)(2,1)S(1)} %collective-permute-done.2.refs_4_) | copy-start | bytes 1572868
  19.5 12.7 %collective-permute-start.5 = (bf16[512,512]{1,0:T(8,128)(2,1)S(1)}, bf16[512,512]{1,0:T(8,128)(2,1)S(1)}, u32[]{:S(2)}, u32[]{:S(2)}) collective-permute-start(bf16[512,512]{1,0:T(8,128)(2,1)S(1)} %collective-permute-done.2.refs_4_), channel_id=1, source_target_pairs={{0,2},{1,3},{2,0},{3,1},{4,6},{5,7},{6,4},{7,5},{8,10},{9,11},{10,... | collective-permute-start | bytes 1572872 | tf_op jit(solution)/shard_map/features_across/ppermute | solution.py:395
  20.1 13.1 %collective-permute-start.6 = (bf16[512,512]{1,0:T(8,128)(2,1)S(1)}, bf16[512,512]{1,0:T(8,128)(2,1)S(1)}, u32[]{:S(2)}, u32[]{:S(2)}) collective-permute-start(bf16[512,512]{1,0:T(8,128)(2,1)S(1)} %collective-permute-done.2.refs_4_), channel_id=1, source_target_pairs={{0,4},{1,5},{2,6},{3,7},{4,0},{5,1},{6,2},{7,3},{8,12},{9,13},{10,... | collective-permute-start | bytes 1572872 | tf_op jit(solution)/shard_map/features_across/ppermute | solution.py:395
  20.4 25.7 %collective-permute-start.7 = (bf16[512,512]{1,0:T(8,128)(2,1)S(1)}, bf16[512,512]{1,0:T(8,128)(2,1)S(1)}, u32[]{:S(2)}, u32[]{:S(2)}) collective-permute-start(bf16[512,512]{1,0:T(8,128)(2,1)S(1)} %constant_dynamic-slice_fusion.refs_1_), channel_id=1, source_target_pairs={{0,16},{1,17},{2,18},{3,19},{4,20},{5,21},{6,22},{7,23},{8,24},{9,... | collective-permute-start | bytes 1572872 | tf_op jit(solution)/shard_map/features_along_z/ppermute | solution.py:395
  33.2 12.9 %collective-permute-start.8 = (bf16[512,512]{1,0:T(8,128)(2,1)S(1)}, bf16[512,512]{1,0:T(8,128)(2,1)S(1)}, u32[]{:S(2)}, u32[]{:S(2)}) collective-permute-start(bf16[512,512]{1,0:T(8,128)(2,1)S(1)} %collective-permute-done.refs_2_), channel_id=1, source_target_pairs={{0,4},{1,5},{2,6},{3,7},{4,0},{5,1},{6,2},{7,3},{8,12},{9,13},{10,... | collective-permute-start | bytes 1572872 | tf_op jit(solution)/shard_map/features_across/ppermute | solution.py:395
  33.5 12.6 %collective-permute-start.9 = (bf16[512,512]{1,0:T(8,128)(2,1)S(1)}, bf16[512,512]{1,0:T(8,128)(2,1)S(1)}, u32[]{:S(2)}, u32[]{:S(2)}) collective-permute-start(bf16[512,512]{1,0:T(8,128)(2,1)S(1)} %collective-permute-done.6.refs_6_), channel_id=1, source_target_pairs={{0,2},{1,3},{2,0},{3,1},{4,6},{5,7},{6,4},{7,5},{8,10},{9,11},{10,... | collective-permute-start | bytes 1572872 | tf_op jit(solution)/shard_map/features_across/ppermute | solution.py:395
  46.1 15.2 %copy-start.2 = (bf16[8,1024,512]{2,1,0:T(8,128)(2,1)}, bf16[8,1024,512]{2,1,0:T(8,128)(2,1)S(1)}, u32[]{:S(2)}) copy-start(bf16[8,1024,512]{2,1,0:T(8,128)(2,1)S(1)} %other_blocks.1.refs_0_) | copy-start | bytes 25165828
  46.1 15.2 %copy-start.7 = (bf16[512,512]{1,0:T(8,128)(2,1)}, bf16[512,512]{1,0:T(8,128)(2,1)S(1)}, u32[]{:S(2)}) copy-start(bf16[512,512]{1,0:T(8,128)(2,1)S(1)} %collective-permute-done.7.refs_1_) | copy-start | bytes 1572868
  46.1 15.2 %collective-permute-start.10 = (bf16[512,512]{1,0:T(8,128)(2,1)S(1)}, bf16[512,512]{1,0:T(8,128)(2,1)}, u32[]{:S(2)}, u32[]{:S(2)}) collective-permute-start(bf16[512,512]{1,0:T(8,128)(2,1)S(1)} %collective-permute-done.7.refs_1_), channel_id=1, source_target_pairs={{0,2},{1,3},{2,0},{3,1},{4,6},{5,7},{6,4},{7,5},{8,10},{9,11},{10,... | collective-permute-start | bytes 1572872 | tf_op jit(solution)/shard_map/features_across/ppermute | solution.py:395
  49.7 11.6 %collective-permute-start.11 = (bf16[512,512]{1,0:T(8,128)(2,1)S(1)}, bf16[512,512]{1,0:T(8,128)(2,1)S(1)}, u32[]{:S(2)}, u32[]{:S(2)}) collective-permute-start(bf16[512,512]{1,0:T(8,128)(2,1)S(1)} %collective-permute-done.7.refs_1_), channel_id=1, source_target_pairs={{0,4},{1,5},{2,6},{3,7},{4,0},{5,1},{6,2},{7,3},{8,12},{9,13},{10,... | collective-permute-start | bytes 1572872 | tf_op jit(solution)/shard_map/features_across/ppermute | solution.py:395
  51.4 11.3 %collective-permute-start.12 = (bf16[512,512]{1,0:T(8,128)(2,1)S(1)}, bf16[512,512]{1,0:T(8,128)(2,1)}, u32[]{:S(2)}, u32[]{:S(2)}) collective-permute-start(bf16[512,512]{1,0:T(8,128)(2,1)S(1)} %collective-permute-done.7.refs_1_), channel_id=1, source_target_pairs={{0,8},{1,9},{2,10},{3,11},{4,12},{5,13},{6,14},{7,15},{8,0},{9,1},... | collective-permute-start | bytes 1572872 | tf_op jit(solution)/shard_map/features_along_z/ppermute | solution.py:395
  51.4 13.5 %collective-permute-start.15 = (bf16[512,512]{1,0:T(8,128)(2,1)}, bf16[512,512]{1,0:T(8,128)(2,1)}, u32[]{:S(2)}, u32[]{:S(2)}) collective-permute-start(bf16[512,512]{1,0:T(8,128)(2,1)} %param.14), channel_id=1, source_target_pairs={{0,1},{1,0},{2,3},{3,2},{4,5},{5,4},{6,7},{7,6},{8,9},{9,8},{10,11... | collective-permute-start | bytes 1572872 | tf_op jit(solution)/shard_map/cotangent_rows/ppermute | solution.py:395
  51.4 1.0 copy-start.6
  52.4 1.0 copy-start.10
  61.3 0.8 copy-start.11
  62.6 13.7 %collective-permute-start.13 = (bf16[512,512]{1,0:T(8,128)(2,1)}, bf16[512,512]{1,0:T(8,128)(2,1)S(1)}, u32[]{:S(2)}, u32[]{:S(2)}) collective-permute-start(bf16[512,512]{1,0:T(8,128)(2,1)} %collective-permute-done.12.refs_4_), channel_id=1, source_target_pairs={{0,2},{1,3},{2,0},{3,1},{4,6},{5,7},{6,4},{7,5},{8,10},{9,11},{10,... | collective-permute-start | bytes 1572872 | tf_op jit(solution)/shard_map/features_across/ppermute | solution.py:395
  63.0 13.6 %collective-permute-start.14 = (bf16[512,512]{1,0:T(8,128)(2,1)}, bf16[512,512]{1,0:T(8,128)(2,1)S(1)}, u32[]{:S(2)}, u32[]{:S(2)}) collective-permute-start(bf16[512,512]{1,0:T(8,128)(2,1)} %collective-permute-done.12.refs_4_), channel_id=1, source_target_pairs={{0,4},{1,5},{2,6},{3,7},{4,0},{5,1},{6,2},{7,3},{8,12},{9,13},{10,... | collective-permute-start | bytes 1572872 | tf_op jit(solution)/shard_map/features_across/ppermute | solution.py:395
  76.7 13.8 %collective-permute-start.16 = (bf16[512,512]{1,0:T(8,128)(2,1)}, bf16[512,512]{1,0:T(8,128)(2,1)S(1)}, u32[]{:S(2)}, u32[]{:S(2)}) collective-permute-start(bf16[512,512]{1,0:T(8,128)(2,1)} %collective-permute-done.10.refs_2_), channel_id=1, source_target_pairs={{0,4},{1,5},{2,6},{3,7},{4,0},{5,1},{6,2},{7,3},{8,12},{9,13},{10,... | collective-permute-start | bytes 1572872 | tf_op jit(solution)/shard_map/features_across/ppermute | solution.py:395
  78.4 12.1 %collective-permute-start.17 = (bf16[512,512]{1,0:T(8,128)(2,1)S(1)}, bf16[512,512]{1,0:T(8,128)(2,1)S(1)}, u32[]{:S(2)}, u32[]{:S(2)}) collective-permute-start(bf16[512,512]{1,0:T(8,128)(2,1)S(1)} %collective-permute-done.14.refs_6_), channel_id=1, source_target_pairs={{0,2},{1,3},{2,0},{3,1},{4,6},{5,7},{6,4},{7,5},{8,10},{9,11},{10,... | collective-permute-start | bytes 1572872 | tf_op jit(solution)/shard_map/features_across/ppermute | solution.py:395
  78.6 3.4 %copy-start.3 = (bf16[8,1024,512]{2,1,0:T(8,128)(2,1)S(1)}, bf16[8,1024,512]{2,1,0:T(8,128)(2,1)}, u32[]{:S(2)}) copy-start(bf16[8,1024,512]{2,1,0:T(8,128)(2,1)} %copy-done.2) | copy-start | bytes 25165828
  82.0 1.0 copy-start.8
  83.1 1.0 copy-start.12
  90.4 5.4 %copy-start.13 = (bf16[512,512]{1,0:T(8,128)(2,1)S(1)}, bf16[512,512]{1,0:T(8,128)(2,1)}, u32[]{:S(2)}) copy-start(bf16[512,512]{1,0:T(8,128)(2,1)} %weight_ref.3) | copy-start | bytes 1572868
  93.0 2.7 %collective-permute-start.18 = (bf16[1024,512]{1,0:T(8,128)(2,1)S(1)}, bf16[1024,512]{1,0:T(8,128)(2,1)S(1)}, u32[]{:S(2)}, u32[]{:S(2)}) collective-permute-start(bf16[1024,512]{1,0:T(8,128)(2,1)S(1)} %forward.5.mine_ref), channel_id=1, source_target_pairs={{0,1},{1,0},{2,3},{3,2},{4,5},{5,4},{6,7},{7,6},{8,9},{9,8},{10,11... | collective-permute-start | bytes 3145736 | tf_op jit(solution)/shard_map/partial_sums/ppermute | solution.py:395
  102.5 14.0 %collective-permute-start.19 = (bf16[512,512]{1,0:T(8,128)(2,1)S(1)}, bf16[512,512]{1,0:T(8,128)(2,1)S(1)}, u32[]{:S(2)}, u32[]{:S(2)}) collective-permute-start(bf16[512,512]{1,0:T(8,128)(2,1)S(1)} %get-tuple-element.208), channel_id=1, source_target_pairs={{0,4},{1,5},{2,6},{3,7},{4,0},{5,1},{6,2},{7,3},{8,12},{9,13},{10,... | collective-permute-start | bytes 1572872 | tf_op jit(solution)/shard_map/grads_across/ppermute | solution.py:395
  103.9 13.7 %collective-permute-start.20 = (bf16[512,512]{1,0:T(8,128)(2,1)S(1)}, bf16[512,512]{1,0:T(8,128)(2,1)S(1)}, u32[]{:S(2)}, u32[]{:S(2)}) collective-permute-start(bf16[512,512]{1,0:T(8,128)(2,1)S(1)} %get-tuple-element.209), channel_id=1, source_target_pairs={{0,2},{1,3},{2,0},{3,1},{4,6},{5,7},{6,4},{7,5},{8,10},{9,11},{10,... | collective-permute-start | bytes 1572872 | tf_op jit(solution)/shard_map/grads_across/ppermute | solution.py:395
  117.7 17.4 %collective-permute-start.24 = (bf16[512,512]{1,0:T(8,128)(2,1)S(1)}, bf16[512,512]{1,0:T(8,128)(2,1)S(1)}, u32[]{:S(2)}, u32[]{:S(2)}) collective-permute-start(bf16[512,512]{1,0:T(8,128)(2,1)S(1)} %add_convert_fusion.6), channel_id=1, source_target_pairs={{0,2},{1,3},{2,0},{3,1},{4,6},{5,7},{6,4},{7,5},{8,10},{9,11},{10,... | collective-permute-start | bytes 1572872 | tf_op jit(solution)/shard_map/grads_across/ppermute | solution.py:395
  118.5 16.7 %collective-permute-start.25 = (bf16[512,512]{1,0:T(8,128)(2,1)S(1)}, bf16[512,512]{1,0:T(8,128)(2,1)S(1)}, u32[]{:S(2)}, u32[]{:S(2)}) collective-permute-start(bf16[512,512]{1,0:T(8,128)(2,1)S(1)} %get-tuple-element.236), channel_id=1, source_target_pairs={{0,4},{1,5},{2,6},{3,7},{4,0},{5,1},{6,2},{7,3},{8,12},{9,13},{10,... | collective-permute-start | bytes 1572872 | tf_op jit(solution)/shard_map/grads_across/ppermute | solution.py:395
  124.7 7.6 %collective-permute-start.23 = (bf16[64,512]{1,0:T(8,128)(2,1)S(1)}, bf16[64,512]{1,0:T(8,128)(2,1)S(1)}, u32[]{:S(2)}, u32[]{:S(2)}) collective-permute-start(bf16[64,512]{1,0:T(8,128)(2,1)S(1)} %get-tuple-element.232), channel_id=1, source_target_pairs={{0,24},{1,25},{2,26},{3,27},{4,28},{5,29},{6,30},{7,31},{8,16},{9,... | collective-permute-start | bytes 196616 | tf_op jit(solution)/shard_map/weight_grad/ppermute | solution.py:395
  130.0 5.2 %collective-permute-start.22 = (bf16[64,512]{1,0:T(8,128)(2,1)S(1)}, bf16[64,512]{1,0:T(8,128)(2,1)S(1)}, u32[]{:S(2)}, u32[]{:S(2)}) collective-permute-start(bf16[64,512]{1,0:T(8,128)(2,1)S(1)} %get-tuple-element.231), channel_id=1, source_target_pairs={{0,16},{1,17},{2,18},{3,19},{4,20},{5,21},{6,22},{7,23},{8,24},{9,... | collective-permute-start | bytes 196616 | tf_op jit(solution)/shard_map/weight_grad/ppermute | solution.py:395
  130.0 5.2 %collective-permute-start.21 = (bf16[64,512]{1,0:T(8,128)(2,1)S(1)}, bf16[64,512]{1,0:T(8,128)(2,1)S(1)}, u32[]{:S(2)}, u32[]{:S(2)}) collective-permute-start(bf16[64,512]{1,0:T(8,128)(2,1)S(1)} %get-tuple-element.230), channel_id=1, source_target_pairs={{0,8},{1,9},{2,10},{3,11},{4,12},{5,13},{6,14},{7,15},{8,0},{9,1},... | collective-permute-start | bytes 196616 | tf_op jit(solution)/shard_map/weight_grad/ppermute | solution.py:395
  135.2 17.7 %collective-permute-start.29 = (bf16[512,512]{1,0:T(8,128)(2,1)S(1)}, bf16[512,512]{1,0:T(8,128)(2,1)S(1)}, u32[]{:S(2)}, u32[]{:S(2)}) collective-permute-start(bf16[512,512]{1,0:T(8,128)(2,1)S(1)} %get-tuple-element.248), channel_id=1, source_target_pairs={{0,2},{1,3},{2,0},{3,1},{4,6},{5,7},{6,4},{7,5},{8,10},{9,11},{10,... | collective-permute-start | bytes 1572872 | tf_op jit(solution)/shard_map/grads_across/ppermute | solution.py:395
  136.8 16.2 %collective-permute-start.30 = (bf16[512,512]{1,0:T(8,128)(2,1)S(1)}, bf16[512,512]{1,0:T(8,128)(2,1)S(1)}, u32[]{:S(2)}, u32[]{:S(2)}) collective-permute-start(bf16[512,512]{1,0:T(8,128)(2,1)S(1)} %add_convert_fusion.5), channel_id=1, source_target_pairs={{0,4},{1,5},{2,6},{3,7},{4,0},{5,1},{6,2},{7,3},{8,12},{9,13},{10,... | collective-permute-start | bytes 1572872 | tf_op jit(solution)/shard_map/grads_across/ppermute | solution.py:395
  137.6 15.4 %collective-permute-start.31 = (bf16[512,512]{1,0:T(8,128)(2,1)S(1)}, bf16[512,512]{1,0:T(8,128)(2,1)S(1)}, u32[]{:S(2)}, u32[]{:S(2)}) collective-permute-start(bf16[512,512]{1,0:T(8,128)(2,1)S(1)} %add_convert_fusion.4), channel_id=1, source_target_pairs={{0,8},{1,9},{2,10},{3,11},{4,12},{5,13},{6,14},{7,15},{8,0},{9,1},... | collective-permute-start | bytes 1572872 | tf_op jit(solution)/shard_map/grads_along_z/ppermute | solution.py:395
  141.6 7.1 %collective-permute-start.28 = (bf16[64,512]{1,0:T(8,128)(2,1)S(1)}, bf16[64,512]{1,0:T(8,128)(2,1)S(1)}, u32[]{:S(2)}, u32[]{:S(2)}) collective-permute-start(bf16[64,512]{1,0:T(8,128)(2,1)S(1)} %add_convert_fusion.8), channel_id=1, source_target_pairs={{0,6},{1,7},{2,4},{3,5},{4,2},{5,3},{6,0},{7,1},{8,14},{9,15},{10,... | collective-permute-start | bytes 196616 | tf_op jit(solution)/shard_map/weight_grad/ppermute | solution.py:395
  143.2 8.0 %collective-permute-start.27 = (bf16[64,512]{1,0:T(8,128)(2,1)S(1)}, bf16[64,512]{1,0:T(8,128)(2,1)S(1)}, u32[]{:S(2)}, u32[]{:S(2)}) collective-permute-start(bf16[64,512]{1,0:T(8,128)(2,1)S(1)} %add_convert_fusion.8), channel_id=1, source_target_pairs={{0,4},{1,5},{2,6},{3,7},{4,0},{5,1},{6,2},{7,3},{8,12},{9,13},{10,... | collective-permute-start | bytes 196616 | tf_op jit(solution)/shard_map/weight_grad/ppermute | solution.py:395
  148.6 4.3 %collective-permute-start.26 = (bf16[64,512]{1,0:T(8,128)(2,1)S(1)}, bf16[64,512]{1,0:T(8,128)(2,1)S(1)}, u32[]{:S(2)}, u32[]{:S(2)}) collective-permute-start(bf16[64,512]{1,0:T(8,128)(2,1)S(1)} %add_convert_fusion.8), channel_id=1, source_target_pairs={{0,2},{1,3},{2,0},{3,1},{4,6},{5,7},{6,4},{7,5},{8,10},{9,11},{10,... | collective-permute-start | bytes 196616 | tf_op jit(solution)/shard_map/weight_grad/ppermute | solution.py:395
  153.0 13.7 %collective-permute-start.33 = (bf16[512,512]{1,0:T(8,128)(2,1)S(1)}, bf16[512,512]{1,0:T(8,128)(2,1)S(1)}, u32[]{:S(2)}, u32[]{:S(2)}) collective-permute-start(bf16[512,512]{1,0:T(8,128)(2,1)S(1)} %get-tuple-element.264), channel_id=1, source_target_pairs={{0,4},{1,5},{2,6},{3,7},{4,0},{5,1},{6,2},{7,3},{8,12},{9,13},{10,... | collective-permute-start | bytes 1572872 | tf_op jit(solution)/shard_map/grads_across/ppermute | solution.py:395
  155.8 10.9 %collective-permute-start.34 = (bf16[512,512]{1,0:T(8,128)(2,1)S(1)}, bf16[512,512]{1,0:T(8,128)(2,1)S(1)}, u32[]{:S(2)}, u32[]{:S(2)}) collective-permute-start(bf16[512,512]{1,0:T(8,128)(2,1)S(1)} %get-tuple-element.265), channel_id=1, source_target_pairs={{0,2},{1,3},{2,0},{3,1},{4,6},{5,7},{6,4},{7,5},{8,10},{9,11},{10,... | collective-permute-start | bytes 1572872 | tf_op jit(solution)/shard_map/grads_across/ppermute | solution.py:395
  162.4 4.3 %collective-permute-start.32 = (bf16[64,512]{1,0:T(8,128)(2,1)S(1)}, bf16[64,512]{1,0:T(8,128)(2,1)S(1)}, u32[]{:S(2)}, u32[]{:S(2)}) collective-permute-start(bf16[64,512]{1,0:T(8,128)(2,1)S(1)} %add_convert_fusion.7), channel_id=1, source_target_pairs={{0,8},{1,9},{2,10},{3,11},{4,12},{5,13},{6,14},{7,15},{8,0},{9,1},... | collective-permute-start | bytes 196616 | tf_op jit(solution)/shard_map/weight_grad/ppermute | solution.py:395
  163.7 24.3 %collective-permute-start.37 = (bf16[512,512]{1,0:T(8,128)(2,1)}, bf16[512,512]{1,0:T(8,128)(2,1)S(1)}, u32[]{:S(2)}, u32[]{:S(2)}) collective-permute-start(bf16[512,512]{1,0:T(8,128)(2,1)} %add_convert_fusion.3), channel_id=1, source_target_pairs={{0,16},{1,17},{2,18},{3,19},{4,20},{5,21},{6,22},{7,23},{8,24},{9,... | collective-permute-start | bytes 1572872 | tf_op jit(solution)/shard_map/grads_along_z/ppermute | solution.py:395
  166.7 1.0 copy-start.16
  167.7 21.7 %collective-permute-start.38 = (bf16[512,512]{1,0:T(8,128)(2,1)}, bf16[512,512]{1,0:T(8,128)(2,1)}, u32[]{:S(2)}, u32[]{:S(2)}) collective-permute-start(bf16[512,512]{1,0:T(8,128)(2,1)} %add_convert_fusion.2), channel_id=1, source_target_pairs={{0,2},{1,3},{2,0},{3,1},{4,6},{5,7},{6,4},{7,5},{8,10},{9,11},{10,... | collective-permute-start | bytes 1572872 | tf_op jit(solution)/shard_map/grads_across/ppermute | solution.py:395
  168.6 20.8 %collective-permute-start.39 = (bf16[512,512]{1,0:T(8,128)(2,1)}, bf16[512,512]{1,0:T(8,128)(2,1)}, u32[]{:S(2)}, u32[]{:S(2)}) collective-permute-start(bf16[512,512]{1,0:T(8,128)(2,1)} %get-tuple-element.287), channel_id=1, source_target_pairs={{0,4},{1,5},{2,6},{3,7},{4,0},{5,1},{6,2},{7,3},{8,12},{9,13},{10,... | collective-permute-start | bytes 1572872 | tf_op jit(solution)/shard_map/grads_across/ppermute | solution.py:395
  169.0 21.5 %copy-start.17 = (bf16[512,512]{1,0:T(8,128)(2,1)S(1)}, bf16[512,512]{1,0:T(8,128)(2,1)}, u32[]{:S(2)}) copy-start(bf16[512,512]{1,0:T(8,128)(2,1)} %copy-done.16) | copy-start | bytes 1572868
  169.0 42.7 %copy-start.1 = (bf16[1024,512]{1,0:T(8,128)(2,1)S(1)}, bf16[1024,512]{1,0:T(8,128)(2,1)}, u32[]{:S(2)}) copy-start(bf16[1024,512]{1,0:T(8,128)(2,1)} %param.8) | copy-start | bytes 3145732
  174.4 17.0 %copy-start.14 = (bf16[512,512]{1,0:T(8,128)(2,1)}, bf16[512,512]{1,0:T(8,128)(2,1)S(1)}, u32[]{:S(2)}) copy-start(bf16[512,512]{1,0:T(8,128)(2,1)S(1)} %get-tuple-element.305.refs_0_) | copy-start | bytes 1572868
  174.4 14.3 %collective-permute-start.35 = (bf16[64,512]{1,0:T(8,128)(2,1)S(1)}, bf16[64,512]{1,0:T(8,128)(2,1)S(1)}, u32[]{:S(2)}, u32[]{:S(2)}) collective-permute-start(bf16[64,512]{1,0:T(8,128)(2,1)S(1)} %add_convert_fusion.7), channel_id=1, source_target_pairs={{0,16},{1,17},{2,18},{3,19},{4,20},{5,21},{6,22},{7,23},{8,24},{9,... | collective-permute-start | bytes 196616 | tf_op jit(solution)/shard_map/weight_grad/ppermute | solution.py:395
  176.4 13.0 %collective-permute-start.36 = (bf16[64,512]{1,0:T(8,128)(2,1)S(1)}, bf16[64,512]{1,0:T(8,128)(2,1)S(1)}, u32[]{:S(2)}, u32[]{:S(2)}) collective-permute-start(bf16[64,512]{1,0:T(8,128)(2,1)S(1)} %collective-permute-done.32), channel_id=1, source_target_pairs={{0,16},{1,17},{2,18},{3,19},{4,20},{5,21},{6,22},{7,23},{8,24},{9,... | collective-permute-start | bytes 196616 | tf_op jit(solution)/shard_map/weight_grad/ppermute | solution.py:395
  189.4 12.2 %collective-permute-start.40 = (bf16[512,512]{1,0:T(8,128)(2,1)}, bf16[512,512]{1,0:T(8,128)(2,1)S(1)}, u32[]{:S(2)}, u32[]{:S(2)}) collective-permute-start(bf16[512,512]{1,0:T(8,128)(2,1)} %get-tuple-element.298), channel_id=1, source_target_pairs={{0,2},{1,3},{2,0},{3,1},{4,6},{5,7},{6,4},{7,5},{8,10},{9,11},{10,... | collective-permute-start | bytes 1572872 | tf_op jit(solution)/shard_map/grads_across/ppermute | solution.py:395
  191.4 11.9 %collective-permute-start.41 = (bf16[512,512]{1,0:T(8,128)(2,1)}, bf16[512,512]{1,0:T(8,128)(2,1)S(1)}, u32[]{:S(2)}, u32[]{:S(2)}) collective-permute-start(bf16[512,512]{1,0:T(8,128)(2,1)} %add_convert_fusion.1), channel_id=1, source_target_pairs={{0,4},{1,5},{2,6},{3,7},{4,0},{5,1},{6,2},{7,3},{8,12},{9,13},{10,... | collective-permute-start | bytes 1572872 | tf_op jit(solution)/shard_map/grads_across/ppermute | solution.py:395
  193.7 1.7 collective-permute-start.43
  195.1 14.4 %collective-permute-start.42 = (bf16[512,512]{1,0:T(8,128)(2,1)S(1)}, bf16[512,512]{1,0:T(8,128)(2,1)S(1)}, u32[]{:S(2)}, u32[]{:S(2)}) collective-permute-start(bf16[512,512]{1,0:T(8,128)(2,1)S(1)} %add_convert_fusion), channel_id=1, source_target_pairs={{0,8},{1,9},{2,10},{3,11},{4,12},{5,13},{6,14},{7,15},{8,0},{9,1},... | collective-permute-start | bytes 1572872 | tf_op jit(solution)/shard_map/grads_along_z/ppermute | solution.py:395
  209.5 1.0 copy-start.15

commit v6 on v5

--- a/solution.py
+++ b/solution.py
@@ -55,8 +55,8 @@
     )(where, packed, tiles, *([before] if first else []))
 
 
-def other_kernel(where_ref, packed_ref, tiles_ref, out_ref):
-    panel = pl.program_id(0)
+def other_kernel(first, where_ref, packed_ref, tiles_ref, out_ref):
+    panel = first + pl.program_id(0)
     size, slots = tiles_ref.shape[-1], tiles_ref.shape[1]
     row_tiles, per_part = out_ref.shape[1] // size, out_ref.shape[2] // size
     out_ref[...] = jnp.zeros_like(out_ref)
@@ -76,23 +76,22 @@
     lax.fori_loop(0, packed_ref[panel, slots], add_tile, 0)
 
 
-def make_other(where, tiles, packed, block_rows, n_rep):
+def make_other(first, where, tiles, packed, block_rows, n_rep):
     panels, slots, size, _ = tiles.shape
+    half = panels // 2
     part = block_rows // n_rep
     return pl.pallas_call(
-        other_kernel,
-        out_shape=jax.ShapeDtypeStruct((panels, block_rows, part), BF16),
+        functools.partial(other_kernel, first),
+        out_shape=jax.ShapeDtypeStruct((half, block_rows, part), BF16),
         grid_spec=pltpu.PrefetchScalarGridSpec(
             num_scalar_prefetch=2,
-            grid=(panels,),
-            in_specs=[pl.BlockSpec((1, slots, size, size), lambda p, *_: (p, 0, 0, 0))],
+            grid=(half,),
+            in_specs=[pl.BlockSpec((1, slots, size, size), lambda p, *_: (first + p, 0, 0, 0))],
             out_specs=pl.BlockSpec((1, block_rows, part), lambda p, *_: (p, 0, 0)),
         ),
         compiler_params=pltpu.CompilerParams(vmem_limit_bytes=36 * 2**20),
         cost_estimate=pl.CostEstimate(
-            flops=0,
-            transcendentals=0,
-            bytes_accessed=tiles.size // 8,
+            flops=0, transcendentals=0, bytes_accessed=tiles.size // 8
         ),
     )(where, packed, tiles)
 
@@ -103,6 +102,7 @@
     total_ref, refs = (refs[0], refs[1:]) if has_total else (None, refs)
     out_ref, sum_ref, a_buf, u_buf, sems, sum_sem = refs
     _, panels, _, part = dense_ref.shape
+    some = others[0].shape[0]
     rep = where_ref[0]
 
     def a_copy(source, slot, side):
@@ -117,7 +117,7 @@
         for side in range(2):
             place = where_ref[offset + 2 * pair + side]
             owner, panel = place // panels, place % panels
-            turn = (owner ^ rep) - 1
+            turn = ((owner ^ rep) - 1) * (panels // some) + panel // some
 
             @pl.when(owner == rep)
             def _():
@@ -127,7 +127,7 @@
 
                 @pl.when((owner != rep) & (turn == number))
                 def _():
-                    a_copy(other_ref.at[panel], slot, side).start()
+                    a_copy(other_ref.at[panel % some], slot, side).start()
 
             for number in range(side, n_units, 2):
 
@@ -169,7 +169,8 @@
 def forward_part(where, offset, units, total, dense, others, kind):
     part, width = units[0].shape
     rows = dense.shape[2]
-    hbm = pl.BlockSpec(memory_space=pl.ANY)
+    near = pl.BlockSpec(memory_space=pl.ANY)
+    hbm = pl.BlockSpec(memory_space=pltpu.HBM)
     has_total = total is not None
     n_units, n_others = len(units), len(others)
     return pl.pallas_call(
@@ -178,8 +179,8 @@
         grid_spec=pltpu.PrefetchScalarGridSpec(
             num_scalar_prefetch=1,
             grid=(1,),
-            in_specs=[hbm] * (1 + n_others + n_units + has_total),
-            out_specs=hbm if kind == F32 else pl.BlockSpec((rows, width), lambda i, where: (0, 0)),
+            in_specs=[hbm] * (1 + n_others) + [near] * (n_units + has_total),
+            out_specs=near if kind == F32 else pl.BlockSpec((rows, width), lambda i, where: (0, 0)),
             scratch_shapes=[
                 pltpu.VMEM((rows, width), F32),
                 pltpu.VMEM((2, rows, 2 * part), BF16),
@@ -205,18 +206,27 @@
     return agg, (pre * sigma).astype(BF16), slope.astype(BF16)
 
 
-def middle_kernel(
-    blocks, where_ref, mine_ref, other_ref, weight_ref, cot_ref, a_ref, grad_ref, odd_ref, even_ref
-):
+def middle_kernel(blocks, where_ref, mine_ref, other_ref, weight_ref, cot_ref, a_ref, *refs):
+    grad_ref, odd_ref, even_ref, term_ref, sum_ref = refs
     step = pl.program_id(0)
     part = mine_ref.shape[0]
+    width = sum_ref.shape[0]
 
     @pl.when(step < blocks)
     def _():
-        _, _, pre_grad = slopes(mine_ref, other_ref, weight_ref, cot_ref)
+        agg, _, pre_grad = slopes(mine_ref, other_ref, weight_ref, cot_ref)
         grad_ref[:, pl.ds(pl.multiple_of(step * part, part), part)] = lax.dot_general(
             weight_ref[...], pre_grad, (((1,), (1,)), ((), ())), preferred_element_type=F32
         ).astype(BF16)
+        term = lax.dot_general(agg, pre_grad, (((0,), (0,)), ((), ())), preferred_element_type=F32)
+
+        @pl.when(step == 0)
+        def _():
+            sum_ref[...] = term
+
+        @pl.when(step > 0)
+        def _():
+            sum_ref[...] += term
 
     @pl.when(step >= blocks)
     def _():
@@ -224,7 +234,17 @@
 
         @pl.when(step == blocks)
         def _():
-            odd_ref[...] = chunk
+            _, extra, cols = term_ref.shape
+            quarter = extra * cols // width
+            for number in range(4):
+                start = pl.multiple_of((where_ref[0] * 4 + number) * quarter, quarter)
+                rows = sum_ref[pl.ds(start, quarter), :].astype(BF16)
+                for turn in range(width // cols):
+                    term_ref[number, turn * quarter : (turn + 1) * quarter] = rows[
+                        :, turn * cols : (turn + 1) * cols
+                    ]
+            odd_ref[:width] = chunk
+            odd_ref[width:] = term_ref[(where_ref[1] % 4) ^ 3]
 
         @pl.when(step > blocks)
         def _():
@@ -236,9 +256,10 @@
     n_rep, _, _, cols = dense.shape
     blocks = 4
     part = rows // blocks
+    extra = width // n_rep // 4 * (width // cols)
     block = pl.BlockSpec((part, width), lambda i, where: (jnp.minimum(i, blocks - 1), 0))
-    fixed = lambda *shape: pl.BlockSpec(shape, lambda i, where: (0, 0))
-    kept = lambda *shape: jax.ShapeDtypeStruct(shape, BF16)
+    fixed = lambda *shape: pl.BlockSpec(shape, lambda i, where: (0,) * len(shape))
+    shapes = [(width, rows), (width + extra, cols), (width, cols), (4, extra, cols)]
 
     def a_block(i, where):
         place = where[offset + jnp.maximum(i - blocks, 0)]
@@ -246,7 +267,7 @@
 
     return pl.pallas_call(
         functools.partial(middle_kernel, blocks),
-        out_shape=[kept(width, rows), kept(width, cols), kept(width, cols)],
+        out_shape=[jax.ShapeDtypeStruct(shape, BF16) for shape in shapes],
         grid_spec=pltpu.PrefetchScalarGridSpec(
             num_scalar_prefetch=1,
             grid=(blocks + 2,),
@@ -257,95 +278,78 @@
                 block,
                 pl.BlockSpec((1, 1, rows, cols), a_block),
             ],
-            out_specs=[fixed(width, rows), fixed(width, cols), fixed(width, cols)],
+            out_specs=[fixed(*shape) for shape in shapes],
+            scratch_shapes=[pltpu.VMEM((width, width), F32)],
         ),
         compiler_params=pltpu.CompilerParams(vmem_limit_bytes=36 * 2**20),
         cost_estimate=pl.CostEstimate(
-            flops=4 * rows * width * width + 4 * rows * width * cols,
+            flops=6 * rows * width * width + 4 * rows * width * cols,
             transcendentals=rows * width,
             bytes_accessed=rows * width * 12,
         ),
     )(where, mine, other, weight, cotangent, dense)
 
 
-def term_kernel(n_rep, where_ref, mine_ref, other_ref, weight_ref, cot_ref, act_ref, *refs):
-    term_refs, sum_ref = refs[:-1], refs[-1]
-    step = pl.program_id(0)
-    agg, activated, pre_grad = slopes(mine_ref, other_ref, weight_ref, cot_ref)
-    act_ref[...] = activated
-    term = lax.dot_general(agg, pre_grad, (((0,), (0,)), ((), ())), preferred_element_type=F32)
-
-    @pl.when(step == 0)
-    def _():
-        sum_ref[...] = term
-
-    @pl.when(step > 0)
-    def _():
-        sum_ref[...] += term
-
-    @pl.when(step == n_rep - 1)
-    def _():
-        z = where_ref[1] // 4
-        size = term_refs[0].shape[0]
-        for number, term_ref in enumerate(term_refs):
-            start = (where_ref[0] * len(term_refs) + (z ^ number)) * size
-            term_ref[...] = sum_ref[pl.ds(pl.multiple_of(start, size), size), :].astype(BF16)
-
-
-def weight_terms(where, mine, other, weight, cotangent, n_rep, depth):
+def activated_kernel(where_ref, mine_ref, other_ref, weight_ref, cot_ref, act_ref):
+    act_ref[...] = slopes(mine_ref, other_ref, weight_ref, cot_ref)[1]
+
+
+def activated_rows(where, mine, other, weight, cotangent, n_rep):
     rows, width = mine.shape
     part = rows // n_rep
-    size = width // n_rep // depth
-    block = pl.BlockSpec((part, width), lambda i, where: ((where[0] + 1 + i) % n_rep, 0))
+    block = pl.BlockSpec((part, width), lambda i, where: (where[0], 0))
     fixed = lambda *shape: pl.BlockSpec(shape, lambda i, where: (0, 0))
     return pl.pallas_call(
-        functools.partial(term_kernel, n_rep),
-        out_shape=[jax.ShapeDtypeStruct((part, width), BF16)]
-        + [jax.ShapeDtypeStruct((size, width), BF16)] * depth,
+        activated_kernel,
+        out_shape=jax.ShapeDtypeStruct((part, width), BF16),
         grid_spec=pltpu.PrefetchScalarGridSpec(
             num_scalar_prefetch=1,
-            grid=(n_rep,),
+            grid=(1,),
             in_specs=[block, block, fixed(width, width), block],
-            out_specs=[fixed(part, width)] + [fixed(size, width)] * depth,
-            scratch_shapes=[pltpu.VMEM((width, width), F32)],
+            out_specs=fixed(part, width),
         ),
         compiler_params=pltpu.CompilerParams(vmem_limit_bytes=36 * 2**20),
         cost_estimate=pl.CostEstimate(
-            flops=4 * rows * width * width,
-            transcendentals=rows * width,
-            bytes_accessed=rows * width * 8,
+            flops=2 * part * width * width,
+            transcendentals=part * width,
+            bytes_accessed=part * width * 8,
         ),
     )(where, mine, other, weight, cotangent)
 
 
-def backward_kernel(where_ref, grad_ref, a_ref, *out_refs):
+def backward_kernel(masks, where_ref, grad_ref, a_ref, *refs):
+    term_ref, out_refs = (refs[0], refs[1:]) if masks else (None, refs)
+    width = grad_ref.shape[0]
     chunk = jnp.dot(grad_ref[...], a_ref[0, 0], preferred_element_type=F32).astype(BF16)
     for number, out_ref in enumerate(out_refs):
 
         @pl.when(pl.program_id(0) == number)
         def _():
-            out_ref[...] = chunk
-
-
-def backward_part(where, offset, count, grad, dense):
+            out_ref[:width] = chunk
+            if number < len(masks):
+                out_ref[width:] = term_ref[(where_ref[1] % 4) ^ masks[number]]
+
+
+def backward_part(where, offset, count, grad, dense, masks=(), term=None):
     width, rows = grad.shape
     n_rep, _, _, cols = dense.shape
+    fixed = lambda *shape: pl.BlockSpec(shape, lambda i, where: (0,) * len(shape))
+    extra = term.shape[1] if masks else 0
+    shapes = [(width + extra * (number < len(masks)), cols) for number in range(count)]
 
     def a_block(i, where):
         place = where[offset + i]
         return (place % n_rep, place // n_rep, 0, 0)
 
     return pl.pallas_call(
-        backward_kernel,
-        out_shape=[jax.ShapeDtypeStruct((width, cols), BF16)] * count,
+        functools.partial(backward_kernel, masks),
+        out_shape=[jax.ShapeDtypeStruct(shape, BF16) for shape in shapes],
         grid_spec=pltpu.PrefetchScalarGridSpec(
             num_scalar_prefetch=1,
             grid=(count,),
-            in_specs=[
-                pl.BlockSpec((width, rows), lambda i, where: (0, 0)),
-                pl.BlockSpec((1, 1, rows, cols), a_block),
-            ],
-            out_specs=[pl.BlockSpec((width, cols), lambda i, where: (0, 0))] * count,
+            in_specs=[fixed(width, rows), pl.BlockSpec((1, 1, rows, cols), a_block)]
+            + ([fixed(*term.shape)] if masks else []),
+            out_specs=[fixed(*shape) for shape in shapes],
         ),
         compiler_params=pltpu.CompilerParams(vmem_limit_bytes=36 * 2**20),
         cost_estimate=pl.CostEstimate(
@@ -353,27 +357,50 @@
             transcendentals=0,
             bytes_accessed=2 * count * rows * cols + 2 * count * width * cols + 2 * width * rows,
         ),
-    )(where, grad, dense)
-
-
-def final_kernel(*refs):
-    *parts, out_ref = refs
-    total = functools.reduce(jnp.add, [part[...].astype(F32) for part in parts])
+    )(where, grad, dense, *([term] if masks else []))
+
+
+def final_kernel(n_parts, where_ref, *refs):
+    parts, terms = refs[:n_parts], refs[n_parts:-2]
+    out_ref, weight_out = refs[-2:]
+    width = out_ref.shape[2]
+    total = functools.reduce(jnp.add, [part[:width].astype(F32) for part in parts])
     out_ref[0] = total.T.astype(BF16)
-
-
-def final_sum(parts):
+    _, extra, cols = terms[0].shape
+    quarter = extra * cols // width
+    for other, term_ref in enumerate(terms):
+        for number in range(4):
+            place = (where_ref[0] ^ other) * 4 + ((where_ref[1] % 4) ^ number)
+            rows = pl.ds(pl.multiple_of(place * quarter, quarter), quarter)
+            for turn in range(width // cols):
+                weight_out[rows, turn * cols : (turn + 1) * cols] = term_ref[
+                    number, turn * quarter : (turn + 1) * quarter
+                ].astype(F32)
+
+
+def final_sum(where, parts, terms):
     width, cols = parts[0].shape
+    whole = lambda value: pl.BlockSpec(value.shape, lambda i, where: (0,) * value.ndim)
+    outs = [
+        jax.ShapeDtypeStruct((1, cols, width), BF16),
+        jax.ShapeDtypeStruct((width, width), F32),
+    ]
     return pl.pallas_call(
-        final_kernel,
-        out_shape=jax.ShapeDtypeStruct((1, cols, width), BF16),
+        functools.partial(final_kernel, len(parts)),
+        out_shape=outs,
+        grid_spec=pltpu.PrefetchScalarGridSpec(
+            num_scalar_prefetch=1,
+            grid=(1,),
+            in_specs=[whole(value) for value in [*parts, *terms]],
+            out_specs=[whole(value) for value in outs],
+        ),
         compiler_params=pltpu.CompilerParams(vmem_limit_bytes=36 * 2**20),
         cost_estimate=pl.CostEstimate(
             flops=len(parts) * width * cols,
             transcendentals=0,
             bytes_accessed=2 * (len(parts) + 1) * width * cols,
         ),
-    )(*parts)
+    )(where, *parts, *terms)
 
 
 def shards(sizes, features, weight, tile_values, tile_rows, tile_cols, tile_count, cotangent):
@@ -436,8 +463,20 @@
         [tile_rows[0] * row_tiles + tile_cols[0], tile_count[0][:, None]], axis=1
     )
     panels = tile_values.shape[1]
+    def build(first):
+        with jax.named_scope("dense_blocks"):
+            live["dense"] = make_dense(
+                first, live.get("dense"), where, tile_values[0], packed, block_rows, n_rep
+            )
+        with jax.named_scope("other_blocks"):
+            return [make_other(first, where, *sent, block_rows, n_rep) for sent in live["tiles"]]
+
     live[0] = lax.dynamic_slice_in_dim(features, rep * part, part, axis=0)
-    total = None
+    with jax.named_scope("tiles_exchange"):
+        live["tiles"] = [
+            (flip(tile_values[0], 0, n), flip(packed, 0, n)) for n in range(1, n_rep)
+        ]
+    waiting = []
     for pair in range(pair_count):
         even, odd = 2 * pair * Z, (2 * pair + 1) * Z
         later = even + 2 * Z
@@ -447,17 +486,10 @@
             live["even_x"], live["even_y"] = flip(live[even], X), flip(live[even], Y)
         with jax.named_scope("features_along_z"):
             live[odd] = flip(live[even], Z)
-        if pair == 0:
-            with jax.named_scope("dense_blocks"):
-                live["dense"] = make_dense(
-                    0, None, where, tile_values[0], packed, block_rows, n_rep
-                )
-            with jax.named_scope("tiles_exchange"):
-                live["tiles"] = [
-                    (flip(tile_values[0], 0, n), flip(packed, 0, n)) for n in range(1, n_rep)
-                ]
-        else:
-            live["total"] = forward_step(*waiting, live.pop("waiting"), live.get("total"))
+        if pair == 1:
+            two = build(panels // 2)
+            live["others"] = [half for halves in zip(live.pop("one"), two) for half in halves]
+            del live["tiles"]
         close()
 
         with jax.named_scope("features_across"):
@@ -465,31 +497,24 @@
         if not last:
             with jax.named_scope("features_along_z"):
                 live[later] = flip(live[later - low_bit(later)], low_bit(later))
-        if last:
+        if pair > 0:
+            live["total"] = forward_step(*waiting, live.pop("waiting"), live.get("total"))
+        close(*([] if last else [later]))
+
+        with jax.named_scope("features_across"):
+            crossed = [flip(live["even_x"], Y), flip(live["odd_y"], X)]
+        units = [live[even], live.pop("even_x"), live.pop("even_y")]
+        units += [live[odd], live.pop("odd_x"), live.pop("odd_y")]
+        if pair == 0:
+            live["one"] = build(0)
             with jax.named_scope("cotangent_rows"):
                 live["cotangent"] = gather_rep(cotangent)
-        close(*([] if last else [later]))
-
-        with jax.named_scope("features_across"):
-            crossed = [flip(live["even_x"], Y), flip(live["odd_y"], X)]
-        if pair == 0:
-            with jax.named_scope("dense_blocks"):
-                live["dense"] = make_dense(
-                    panels // 2, live["dense"], where, tile_values[0], packed, block_rows, n_rep
-                )
-            with jax.named_scope("other_blocks"):
-                live["others"] = [
-                    make_other(where, *sent, block_rows, n_rep) for sent in live.pop("tiles")
-                ]
-        units = [live[even], live.pop("even_x"), live.pop("even_y")]
-        units += [live[odd], live.pop("odd_x"), live.pop("odd_y")]
-        if pair > 0:
+            live["waiting"] = units + crossed
+            waiting = [("units", pair)]
+        else:
             live["total"] = forward_step(("units", pair), units, live["total"])
             live["waiting"] = crossed
             waiting = [("crossed", pair)]
-        else:
-            live["waiting"] = units + crossed
-            waiting = [("units", pair)]
         close()
     partial = forward_step(*waiting, live["waiting"], live.get("total"), BF16)
 
@@ -499,89 +524,102 @@
             partial = (partial.astype(F32) + other.astype(F32)).astype(BF16)
             other = flip(partial, 0, 1 << bit)
 
-    depth = n_section // 4
     with jax.named_scope("middle"):
         rows = (partial, other, weight, live["cotangent"])
-        grad, odd_diag, even_diag = middle(
+        grad, odd_diag, even_diag, term = middle(
             where, offsets["first", pair_count - 1], *rows, live["dense"]
         )
 
-    def backward_step(name, count):
+    live = {"grad": grad, "dense": live["dense"], "term": term}
+    add = lambda *values: functools.reduce(jnp.add, [value.astype(F32) for value in values])
+
+    def backward_step(names, *carried):
         with jax.named_scope("backward"):
-            return backward_part(where, offsets[name], count, live["grad"], live["dense"])
-
-    add = lambda *values: functools.reduce(jnp.add, [value.astype(F32) for value in values])
-
-    def weight_step(phase):
-        if phase == 0:
-            live["activated"], *live["terms"] = weight_terms(where, *rows, n_rep, depth)
-            return
-        name = next((name for name in ("odd", "even", "first") if name in live), None)
-        if name:
-            live[name], live["terms"] = lax.optimization_barrier((live[name], live["terms"]))
-        terms = live["terms"]
-        if phase == 1:
-            sums = [terms[0]] + [flip(term, Z * n) for n, term in enumerate(terms[1:], 1)]
-            live["terms"] = [add(*sums).astype(BF16)]
-        elif phase == 2:
-            sums = [terms[0]] + [flip(terms[0], mask) for mask in (X, Y, X + Y)]
-            live["terms"] = [(add(*sums[:2]) + add(*sums[2:])).astype(BF16)]
-        elif 1 << phase - 3 < depth:
-            live["terms"] = terms + [flip(term, Z << phase - 3) for term in terms]
-        elif "weight_grad" not in live:
-            z = section // 4
-            rows_of = jnp.stack(terms)[z ^ jnp.arange(depth)].reshape(-1, width)
-            live["weight_grad"] = gather_rep(rows_of).astype(F32)
-
-    phases = iter(range(3 * pair_count))
-
-    def end_phase(*open_names):
+            count = sum(2 if name[0] == "first" else 3 for name in names)
+            chunks = backward_part(
+                where, offsets[names[0]], count, live["grad"], live["dense"], *carried
+            )
+            for name in names:
+                size = 2 if name[0] == "first" else 3
+                live[name[0]], chunks = chunks[:size], chunks[size:]
+
+    z_masks = [1 << bit for bit in range(3, n_section.bit_length() - 1)]
+
+    def weight_step():
         with jax.named_scope("weight_grad"):
-            weight_step(next(phases))
-        close(*open_names)
-
-    live = {"grad": grad, "dense": live["dense"]}
+            if z_masks:
+                flipped = flip(live["weight"], z_masks.pop(0))
+                live["weight"] = add(live["weight"], flipped).astype(BF16)
+            elif "weight" in live:
+                own = live.pop("weight")
+                live["quarters"] = [own, *(flip(own, mask) for mask in (X, Y, X + Y))]
+            elif "quarters" in live:
+                own = jnp.stack(live.pop("quarters"))
+                live["terms"] = [own, *(flip(own, 0, n) for n in range(1, n_rep))]
+
     live["first"] = [odd_diag, even_diag]
     for pair in reversed(range(pair_count)):
         even = 2 * pair * Z
+        top = pair + 1 == pair_count
         passing = [name for name in live if isinstance(name, tuple)]
 
         with jax.named_scope("grads_across"):
             odd_diag, even_diag = live.pop("first")
             live["odd_diag"], live["even_diag"] = flip(odd_diag, Y), flip(even_diag, X)
-        live["odd"] = backward_step(("odd", pair), 3)
-        if "passed" in live:
+        if top:
+            backward_step([("odd", pair), ("even", pair)], (X, Y, 0), live.pop("term"))
+        else:
             with jax.named_scope("grads_along_z"):
                 mask = low_bit(even + 2 * Z)
                 target = even + 2 * Z - mask
                 live["to", target, mask] = flip(live.pop("passed"), mask)
                 passing = [("to", target, mask)]
-        end_phase(*passing)
+            if "activated" not in live:
+                with jax.named_scope("activated"):
+                    live["activated"] = activated_rows(where, *rows, n_rep)
+                live["activated"], live["weight"] = lax.optimization_barrier(
+                    (live["activated"], live["weight"])
+                )
+            weight_step()
+        close(*passing)
 
         with jax.named_scope("grads_across"):
             to_x, to_y, own = live.pop("odd")
             to_x = add(to_x, live.pop("odd_diag")).astype(BF16)
             live["odd_sum"] = [own, flip(to_x, X), flip(to_y, Y)]
-        live["even"] = backward_step(("even", pair), 3)
-        end_phase()
+            to_x, to_y, own = live.pop("even")
+            live["even"] = [to_x, add(to_y, live.pop("even_diag")).astype(BF16), own]
+        if pair > 0:
+            following = live.pop("even")
+            backward_step([("first", pair - 1), ("odd", pair - 1)])
+            live["following"], live["even"] = live.pop("odd"), following
+        if not top:
+            weight_step()
+        close()
 
         with jax.named_scope("grads_across"):
             to_x, to_y, own = live.pop("even")
-            to_y = add(to_y, live.pop("even_diag")).astype(BF16)
             live["even_sum"] = [own, flip(to_x, X), flip(to_y, Y)]
         with jax.named_scope("grads_along_z"):
             odd_sum = add(*live.pop("odd_sum")).astype(BF16)
-            live["even_sum"].append(flip(odd_sum, Z))
+            from_odd = flip(odd_sum, Z)
+            live["even_sum"].append(from_odd[:width] if top and pair else from_odd)
         if pair > 0:
-            live["first"] = backward_step(("first", pair - 1), 2)
-        end_phase()
+            backward_step([("even", pair - 1)])
+            live["odd"] = live.pop("following")
+        if top:
+            with jax.named_scope("weight_grad"):
+                live["weight"] = add(odd_sum[width:], from_odd[width:]).astype(BF16)
+        else:
+            weight_step()
+        close()
         arrived = [name for name in live if isinstance(name, tuple) and name[1] == even]
         sums = [*live.pop("even_sum"), *(live.pop(name) for name in arrived)]
         if pair > 0:
             live["passed"] = add(*sums).astype(BF16)
     with jax.named_scope("grads_out"):
-        feat_grad = final_sum(sums)
-    return (live["activated"], feat_grad, live["weight_grad"])
+        feat_grad, weight_grad = final_sum(where, sums, live["terms"])
+    return (live["activated"], feat_grad, weight_grad)
 
 
 def solution(mesh):

time: 213 us -> 200 us (0.939)
  waiting for transfers between devices: 69.3 us -> 78.1 us
  local copies, waits for them, and re-layouts: 14.9 us -> 6.41 us
  other arithmetic: 9.96 us -> 4.1 us
  starting transfers between devices: 48.9 us -> 44.2 us
  Pallas kernels: 67.6 us -> 65.3 us
    ppermute x44 -> x39, waiting for transfers between devices: 69.3 us -> 78.1 us  [flip(): return lax.ppermute(value, BOTH, pairs)]
    unnamed x36 -> x22, local copies, waits for them, and re-layouts: 12.9 us -> 5.61 us
    ppermute x44 -> x39, starting transfers between devices: 48.9 us -> 44.2 us  [flip(): return lax.ppermute(value, BOTH, pairs)]
    pallas_call x9 -> x8, Pallas kernels: 41.7 us -> 38.9 us  [the longest x3 19 us: backward_part(): pl.pallas_call(functools.partial(backward_kernel, masks), out_shape=[jax....]
  transfers between devices with their start and end apart: 44 -> 39, of which waited for: 23 -> 28; matrix products, arithmetic and copies ran while one was open for 6% -> 2% of each run, Pallas kernels for 27% -> 27%
where the time goes in v6:
time: 200 us; the launch traced here: 199 us
  waiting for transfers between devices  78.1 us (39%)
  Pallas kernels  65.3 us (33%)
  starting transfers between devices  44.2 us (22%)
  local copies, waits for them, and re-layouts  6.41 us (3%)
  other arithmetic  4.1 us (2%)
    ppermute x39, waiting for transfers between devices, flip(): return lax.ppermute(value, BOTH, pairs)  78.1 us
    ppermute x39, starting transfers between devices, flip(): return lax.ppermute(value, BOTH, pairs)  44.2 us
    pallas_call x3, Pallas kernels, backward_part(): pl.pallas_call(functools.partial(backward_kernel, masks), out_shape=[jax....  19 us
    pallas_call x3, Pallas kernels, forward_part(): pl.pallas_call(functools.partial(forward_kernel, offset, n_units, n_other...  16.7 us
    pallas_call x2, Pallas kernels, make_dense(): pl.pallas_call(functools.partial(dense_kernel, first), out_shape=jax.Shap...  9.72 us
    pallas_call x2, Pallas kernels, make_other(): pl.pallas_call(functools.partial(other_kernel, first), out_shape=jax.Shap...  8.35 us
    pallas_call x1, Pallas kernels, middle(): pl.pallas_call(functools.partial(middle_kernel, blocks), out_shape=[jax.S...  7.65 us
    unnamed x22, local copies, waits for them, and re-layouts  5.61 us
  transfers between devices with their start and end apart: 39, of which 28 were waited for; matrix products, arithmetic and copies ran while one was open for 2% of the time, Pallas kernels for 27%

profile of v6, /device:TPU:0, one launch (start us, length us, event | category | flops | bytes accessed | tf_op | source)
XLA Modules:
  0.0 199.0 jit_solution(11905609964287733995)
XLA Ops:
  1.9 3.0 %collective-permute-start.2 = (bf16[512,512]{1,0:T(8,128)(2,1)S(1)}, bf16[512,512]{1,0:T(8,128)(2,1)S(1)}, u32[]{:S(2)}, u32[]{:S(2)}) collective-permute-start(bf16[512,512]{1,0:T(8,128)(2,1)S(1)} %constant_dynamic-slice_fusion.refs_2_), channel_id=1, source_target_pairs={{0,2},{1,3},{2,0},{3,1},{4,6},{5,7},{6,4},{7,5},{8,10},{9,11},{10,... | collective-permute-start | bytes 1572872 | tf_op jit(solution)/shard_map/features_across/ppermute | solution.py:422
  4.9 1.5 collective-permute-start.3
  6.4 1.6 collective-permute-start.4
  8.0 0.7 copy.12
  9.5 1.4 collective-permute-done.1.packed_ref
  11.0 5.9 %collective-permute-done.2.refs_3_ = bf16[512,512]{1,0:T(8,128)(2,1)S(1)} collective-permute-done((bf16[512,512]{1,0:T(8,128)(2,1)S(1)}, bf16[512,512]{1,0:T(8,128)(2,1)S(1)}, u32[]{:S(2)}, u32[]{:S(2)}) %collective-permute-start.2) | collective-permute-done | bytes 524320 | tf_op jit(solution)/shard_map/features_across/ppermute | solution.py:422
  16.8 1.5 collective-permute-done.3.refs_4_
  18.3 1.2 collective-permute-done.4.refs_5_
  21.1 2.8 %collective-permute-start.7 = (bf16[512,512]{1,0:T(8,128)(2,1)S(1)}, bf16[512,512]{1,0:T(8,128)(2,1)S(1)}, u32[]{:S(2)}, u32[]{:S(2)}) collective-permute-start(bf16[512,512]{1,0:T(8,128)(2,1)S(1)} %constant_dynamic-slice_fusion.refs_2_), channel_id=1, source_target_pairs={{0,16},{1,17},{2,18},{3,19},{4,20},{5,21},{6,22},{7,23},{8,24},{9,... | collective-permute-start | bytes 1572872 | tf_op jit(solution)/shard_map/features_along_z/ppermute | solution.py:422
  23.8 7.9 %collective-permute-done.5.refs_6_ = bf16[512,512]{1,0:T(8,128)(2,1)S(1)} collective-permute-done((bf16[512,512]{1,0:T(8,128)(2,1)S(1)}, bf16[512,512]{1,0:T(8,128)(2,1)S(1)}, u32[]{:S(2)}, u32[]{:S(2)}) %collective-permute-start.5) | collective-permute-done | bytes 524320 | tf_op jit(solution)/shard_map/features_across/ppermute | solution.py:422
  32.0 1.5 collective-permute-start.10
  34.1 2.8 %copy-done.2 = bf16[1,8,24,128,128]{4,3,2,1,0:T(8,128)(2,1)S(1)} copy-done((bf16[1,8,24,128,128]{4,3,2,1,0:T(8,128)(2,1)S(1)}, bf16[1,8,24,128,128]{4,3,2,1,0:T(8,128)(2,1)}, u32[]{:S(2)}) %copy-start.2) | copy-done | bytes 6291480
  36.9 4.9 %dense_blocks.2.refs_0_ = bf16[2,8,1024,512]{3,2,1,0:T(8,128)(2,1)} custom-call(s32[34]{0:T(128)S(1)} %pad_add_fusion.1.where_ref, s32[8,25]{1,0:T(8,128)S(1)} %pad_add_fusion.packed_ref, bf16[8,24,128,128]{3,2,1,0:T(8,128)(2,1)S(1)} %bitcast.11), custom_call_target="tpu_custom_call" | custom-call | bytes 393216 | tf_op jit(solution)/shard_map/dense_blocks/pallas_call | solution.py:38
  41.8 1.1 broadcast_select_fusion.1
  43.0 4.2 %other_blocks.2.refs_0_ = bf16[4,1024,512]{2,1,0:T(8,128)(2,1)S(1)} custom-call(s32[34]{0:T(128)S(1)} %pad_add_fusion.1.where_ref, s32[8,25]{1,0:T(8,128)S(1)} %collective-permute-done.1.packed_ref, bf16[8,24,128,128]{3,2,1,0:T(8,128)(2,1)} %collective-permute-done.tiles_ref), custom_call_target="tpu_custom_call" | custom-call | bytes 393216 | tf_op jit(solution)/shard_map/other_blocks/pallas_call | solution.py:83
  47.7 1.5 collective-permute-start.11
  49.2 1.5 collective-permute-start.12
  50.7 1.6 collective-permute-start.13
  52.3 4.8 %dense_blocks.3.dense_ref.a_ref = bf16[2,8,1024,512]{3,2,1,0:T(8,128)(2,1)} custom-call(s32[34]{0:T(128)S(1)} %pad_add_fusion.1.where_ref, s32[8,25]{1,0:T(8,128)S(1)} %pad_add_fusion.packed_ref, bf16[8,24,128,128]{3,2,1,0:T(8,128)(2,1)S(1)} %bitcast.14, bf16[2,8,1024,512]{3,2,1,0:T(8,128)(2,1)} %dense_blocks.2.refs_0_), custom_call_target="tpu_custom_call", output_to_operand_aliasing={{}: (3, {})} | custom-call | bytes 393216 | tf_op jit(solution)/shard_map/dense_blocks/pallas_call | solution.py:38
  57.1 4.2 %other_blocks.3.refs_1_ = bf16[4,1024,512]{2,1,0:T(8,128)(2,1)S(1)} custom-call(s32[34]{0:T(128)S(1)} %pad_add_fusion.1.where_ref, s32[8,25]{1,0:T(8,128)S(1)} %collective-permute-done.1.packed_ref, bf16[8,24,128,128]{3,2,1,0:T(8,128)(2,1)} %collective-permute-done.tiles_ref), custom_call_target="tpu_custom_call" | custom-call | bytes 393216 | tf_op jit(solution)/shard_map/other_blocks/pallas_call | solution.py:83
  61.5 1.0 collective-permute-done.12.refs_4_
  62.5 1.2 collective-permute-done.13.refs_5_
  64.8 7.8 %forward.3.refs_8_ = f32[1024,512]{1,0:T(8,128)S(1)} custom-call(s32[34]{0:T(128)S(1)} %pad_add_fusion.1.where_ref, bf16[2,8,1024,512]{3,2,1,0:T(8,128)(2,1)} %dense_blocks.3.dense_ref.a_ref, bf16[4,1024,512]{2,1,0:T(8,128)(2,1)S(1)} %other_blocks.2.refs_0_, bf16[4,1024,512]{2,1,0:T(8,128)(2,1)S(1)} %other_blocks.3.refs_1_, ...), custom_call_target="tpu_custom_call" | custom-call | flops 4294967296 | bytes 12582912 | tf_op jit(solution)/shard_map/forward/pallas_call | solution.py:176
  72.7 3.1 %collective-permute-done.14.refs_6_ = bf16[512,512]{1,0:T(8,128)(2,1)S(1)} collective-permute-done((bf16[512,512]{1,0:T(8,128)(2,1)S(1)}, bf16[512,512]{1,0:T(8,128)(2,1)S(1)}, u32[]{:S(2)}, u32[]{:S(2)}) %collective-permute-start.14) | collective-permute-done | bytes 524320 | tf_op jit(solution)/shard_map/features_across/ppermute | solution.py:422
  76.2 0.7 collective-permute-start.16
  76.9 1.4 collective-permute-start.17
  78.3 1.0 copy-done.5
  79.3 1.0 copy-done.7
  80.4 6.3 %forward.4.refs_4_ = f32[1024,512]{1,0:T(8,128)S(1)} custom-call(s32[34]{0:T(128)S(1)} %pad_add_fusion.1.where_ref, bf16[2,8,1024,512]{3,2,1,0:T(8,128)(2,1)} %dense_blocks.3.dense_ref.a_ref, bf16[4,1024,512]{2,1,0:T(8,128)(2,1)S(1)} %other_blocks.2.refs_0_, bf16[4,1024,512]{2,1,0:T(8,128)(2,1)S(1)} %other_blocks.3.refs_1_, ...), custom_call_target="tpu_custom_call" | custom-call | flops 3221225472 | bytes 10485760 | tf_op jit(solution)/shard_map/forward/pallas_call | solution.py:176
  87.7 2.6 %forward.5.mine_ref = bf16[1024,512]{1,0:T(8,128)(2,1)S(1)} custom-call(s32[34]{0:T(128)S(1)} %pad_add_fusion.1.where_ref, bf16[2,8,1024,512]{3,2,1,0:T(8,128)(2,1)} %dense_blocks.3.dense_ref.a_ref, bf16[4,1024,512]{2,1,0:T(8,128)(2,1)S(1)} %other_blocks.2.refs_0_, bf16[4,1024,512]{2,1,0:T(8,128)(2,1)S(1)} %other_blocks.3.refs_1_, ...), custom_call_target="tpu_custom_call" | custom-call | flops 1073741824 | bytes 6291456 | tf_op jit(solution)/shard_map/forward/pallas_call | solution.py:176
  90.4 2.6 %collective-permute-done.18.other_ref = bf16[1024,512]{1,0:T(8,128)(2,1)S(1)} collective-permute-done((bf16[1024,512]{1,0:T(8,128)(2,1)S(1)}, bf16[1024,512]{1,0:T(8,128)(2,1)S(1)}, u32[]{:S(2)}, u32[]{:S(2)}) %collective-permute-start.18) | collective-permute-done | bytes 1048608 | tf_op jit(solution)/shard_map/partial_sums/ppermute | solution.py:422
  93.0 7.7 %middle.1 = (bf16[512,1024]{1,0:T(8,128)(2,1)S(1)}, bf16[576,512]{1,0:T(8,128)(2,1)S(1)}, bf16[512,512]{1,0:T(8,128)(2,1)S(1)}, bf16[4,64,512]{2,1,0:T(8,128)(2,1)S(1)}) custom-call(s32[34]{0:T(128)S(1)} %pad_add_fusion.1.where_ref, bf16[1024,512]{1,0:T(8,128)(2,1)S(1)} %forward.5.mine_ref, bf16[1024,512]{1,0:T(8,128)(2,1)S(1)} %collective-permute-done.18.other_ref, ...), custom_call_target="tpu_custom_call" | custom-call | flops 2684354560 | bytes 6291456 | tf_op jit(solution)/shard_map/middle/pallas_call | solution.py:268
  100.7 1.2 collective-permute-start.19
  101.9 1.3 collective-permute-start.20
  103.2 7.7 %backward.3 = (bf16[576,512]{1,0:T(8,128)(2,1)S(1)}, bf16[576,512]{1,0:T(8,128)(2,1)S(1)}, bf16[576,512]{1,0:T(8,128)(2,1)S(1)}, bf16[512,512]{1,0:T(8,128)(2,1)...) custom-call(s32[34]{0:T(128)S(1)} %pad_add_fusion.1.where_ref, ...), custom_call_target="tpu_custom_call" | custom-call | flops 3221225472 | bytes 10485760 | tf_op jit(solution)/shard_map/backward/pallas_call | solution.py:344
  110.9 4.7 %collective-permute-done.20 = bf16[512,512]{1,0:T(8,128)(2,1)S(1)} collective-permute-done((bf16[512,512]{1,0:T(8,128)(2,1)S(1)}, bf16[512,512]{1,0:T(8,128)(2,1)S(1)}, u32[]{:S(2)}, u32[]{:S(2)}) %collective-permute-start.20) | collective-permute-done | bytes 524320 | tf_op jit(solution)/shard_map/grads_across/ppermute | solution.py:422
  116.2 1.5 collective-permute-start.21
  117.7 1.1 collective-permute-start.22
  118.8 6.7 %backward.4 = (bf16[512,512]{1,0:T(8,128)(2,1)S(1)}, bf16[512,512]{1,0:T(8,128)(2,1)S(1)}, bf16[512,512]{1,0:T(8,128)(2,1)S(1)}, bf16[512,512]{1,0:T(8,128)(2,1)S(1)}, bf16[512,512]{1,0:T(8,128)(2,1)S(1)}) custom-call(s32[34]{0:T(128)S(1)} %pad_add_fusion.1.where_ref, bf16[512,1024]{1,0:T(8,128)(2,1)S(1)} %get-tuple-element.240.grad_ref, ...), custom_call_target="tpu_custom_call" | custom-call | flops 2684354560 | bytes 8912896 | tf_op jit(solution)/shard_map/backward/pallas_call | solution.py:344
  125.6 5.2 %collective-permute-done.21 = bf16[576,512]{1,0:T(8,128)(2,1)S(1)} collective-permute-done((bf16[576,512]{1,0:T(8,128)(2,1)S(1)}, bf16[576,512]{1,0:T(8,128)(2,1)S(1)}, u32[]{:S(2)}, u32[]{:S(2)}) %collective-permute-start.21) | collective-permute-done | bytes 589856 | tf_op jit(solution)/shard_map/grads_across/ppermute | solution.py:422
  130.8 1.1 collective-permute-done.22
  132.2 0.8 collective-permute-start.25
  133.6 1.3 collective-permute-start.24
  134.9 4.6 %backward.5 = (bf16[512,512]{1,0:T(8,128)(2,1)S(1)}, bf16[512,512]{1,0:T(8,128)(2,1)S(1)}, bf16[512,512]{1,0:T(8,128)(2,1)S(1)}) custom-call(s32[34]{0:T(128)S(1)} %pad_add_fusion.1.where_ref, bf16[512,1024]{1,0:T(8,128)(2,1)S(1)} %get-tuple-element.240.grad_ref, bf16[2,8,1024,512]{3,2,1,0:T(8,128)(2,1)} %dense_blocks.3.dense_ref.a_ref), custom_call_target="tpu_custom_call" | custom-call | flops 1610612736 | bytes 5767168 | tf_op jit(solution)/shard_map/backward/pallas_call | solution.py:344
  139.5 6.1 %collective-permute-done.25 = bf16[576,512]{1,0:T(8,128)(2,1)S(1)} collective-permute-done((bf16[576,512]{1,0:T(8,128)(2,1)S(1)}, bf16[576,512]{1,0:T(8,128)(2,1)S(1)}, u32[]{:S(2)}, u32[]{:S(2)}) %collective-permute-start.25) | collective-permute-done | bytes 589856 | tf_op jit(solution)/shard_map/grads_along_z/ppermute | solution.py:422
  145.7 1.1 collective-permute-start.28
  146.8 0.7 collective-permute-start.29
  147.5 1.8 activated.1
  149.3 5.8 %collective-permute-start.27 = (bf16[64,512]{1,0:T(8,128)(2,1)S(1)}, bf16[64,512]{1,0:T(8,128)(2,1)S(1)}, u32[]{:S(2)}, u32[]{:S(2)}) collective-permute-start(bf16[64,512]{1,0:T(8,128)(2,1)S(1)} %add_convert_fusion.8), channel_id=1, source_target_pairs={{0,16},{1,17},{2,18},{3,19},{4,20},{5,21},{6,22},{7,23},{8,24},{9,... | collective-permute-start | bytes 196616 | tf_op jit(solution)/shard_map/weight_grad/ppermute | solution.py:422
  155.5 12.9 %collective-permute-done.27 = bf16[64,512]{1,0:T(8,128)(2,1)S(1)} collective-permute-done((bf16[64,512]{1,0:T(8,128)(2,1)S(1)}, bf16[64,512]{1,0:T(8,128)(2,1)S(1)}, u32[]{:S(2)}, u32[]{:S(2)}) %collective-permute-start.27) | collective-permute-done | bytes 65568 | tf_op jit(solution)/shard_map/weight_grad/ppermute | solution.py:422
  168.6 1.2 collective-permute-start.30
  169.8 1.0 collective-permute-start.31
  171.6 1.1 collective-permute-start.33
  172.7 5.1 %collective-permute-done.26.refs_4_ = bf16[512,512]{1,0:T(8,128)(2,1)S(1)} collective-permute-done((bf16[512,512]{1,0:T(8,128)(2,1)S(1)}, bf16[512,512]{1,0:T(8,128)(2,1)S(1)}, u32[]{:S(2)}, u32[]{:S(2)}) %collective-permute-start.26) | collective-permute-done | bytes 524320 | tf_op jit(solution)/shard_map/grads_along_z/ppermute | solution.py:422
  177.9 1.7 collective-permute-start.34
  179.7 3.3 %collective-permute-done.34 = bf16[64,512]{1,0:T(8,128)(2,1)S(1)} collective-permute-done((bf16[64,512]{1,0:T(8,128)(2,1)S(1)}, bf16[64,512]{1,0:T(8,128)(2,1)S(1)}, u32[]{:S(2)}, u32[]{:S(2)}) %collective-permute-start.34) | collective-permute-done | bytes 65568 | tf_op jit(solution)/shard_map/weight_grad/ppermute | solution.py:422
  183.2 0.8 collective-permute-start.37
  184.1 0.9 collective-permute-start.35
  185.0 0.8 collective-permute-start.36
  185.9 1.5 collective-permute-done.38.refs_6_
  187.5 7.0 %collective-permute-done.37.refs_3_ = bf16[512,512]{1,0:T(8,128)(2,1)S(1)} collective-permute-done((bf16[512,512]{1,0:T(8,128)(2,1)S(1)}, bf16[512,512]{1,0:T(8,128)(2,1)S(1)}, u32[]{:S(2)}, u32[]{:S(2)}) %collective-permute-start.37) | collective-permute-done | bytes 524320 | tf_op jit(solution)/shard_map/grads_along_z/ppermute | solution.py:422
  194.5 1.5 collective-permute-done.35.refs_1_
  195.9 1.0 collective-permute-done.36.refs_2_
  196.9 2.1 %grads_out.1 = (bf16[1,512,512]{2,1,0:T(8,128)(2,1)}, f32[512,512]{1,0:T(8,128)}) custom-call(s32[34]{0:T(128)S(1)} %pad_add_fusion.1.where_ref, bf16[512,512]{1,0:T(8,128)(2,1)S(1)} %get-tuple-element.294.refs_0_, bf16[512,512]{1,0:T(8,128)(2,1)S(1)} %collective-permute-done.35.refs_1_, bf16[512,512]{1,0:T(8,128)(2,1)S(1)} %collective-permute-done.36.refs_2_, ...), custom_call_target="tpu_custom_call" | custom-call | flops 1310720 | bytes 3145728 | tf_op jit(solution)/shard_map/grads_out/pallas_call | solution.py:388
  (69 shorter events, 11.3 us)
Async XLA Ops:
  0.6 1.2 copy-start
  0.6 18.9 %collective-permute-start = (bf16[8,24,128,128]{3,2,1,0:T(8,128)(2,1)}, bf16[8,24,128,128]{3,2,1,0:T(8,128)(2,1)}, u32[]{:S(2)}, u32[]{:S(2)}) collective-permute-start(bf16[8,24,128,128]{3,2,1,0:T(8,128)(2,1)} %bitcast.10), channel_id=1, source_target_pairs={{0,1},{1,0},{2,3},{3,2},{4,5},{5,4},{6,7},{7,6},{8,9},{9,8},{10,11... | collective-permute-start | bytes 18874376 | tf_op jit(solution)/shard_map/tiles_exchange/ppermute | solution.py:422
  1.9 14.9 %collective-permute-start.2 = (bf16[512,512]{1,0:T(8,128)(2,1)S(1)}, bf16[512,512]{1,0:T(8,128)(2,1)S(1)}, u32[]{:S(2)}, u32[]{:S(2)}) collective-permute-start(bf16[512,512]{1,0:T(8,128)(2,1)S(1)} %constant_dynamic-slice_fusion.refs_2_), channel_id=1, source_target_pairs={{0,2},{1,3},{2,0},{3,1},{4,6},{5,7},{6,4},{7,5},{8,10},{9,11},{10,... | collective-permute-start | bytes 1572872 | tf_op jit(solution)/shard_map/features_across/ppermute | solution.py:422
  4.9 13.4 %collective-permute-start.3 = (bf16[512,512]{1,0:T(8,128)(2,1)S(1)}, bf16[512,512]{1,0:T(8,128)(2,1)S(1)}, u32[]{:S(2)}, u32[]{:S(2)}) collective-permute-start(bf16[512,512]{1,0:T(8,128)(2,1)S(1)} %constant_dynamic-slice_fusion.refs_2_), channel_id=1, source_target_pairs={{0,4},{1,5},{2,6},{3,7},{4,0},{5,1},{6,2},{7,3},{8,12},{9,13},{10,... | collective-permute-start | bytes 1572872 | tf_op jit(solution)/shard_map/features_across/ppermute | solution.py:422
  6.4 13.1 %collective-permute-start.4 = (bf16[512,512]{1,0:T(8,128)(2,1)S(1)}, bf16[512,512]{1,0:T(8,128)(2,1)S(1)}, u32[]{:S(2)}, u32[]{:S(2)}) collective-permute-start(bf16[512,512]{1,0:T(8,128)(2,1)S(1)} %constant_dynamic-slice_fusion.refs_2_), channel_id=1, source_target_pairs={{0,8},{1,9},{2,10},{3,11},{4,12},{5,13},{6,14},{7,15},{8,0},{9,1},... | collective-permute-start | bytes 1572872 | tf_op jit(solution)/shard_map/features_along_z/ppermute | solution.py:422
  9.5 1.4 collective-permute-start.1
  19.5 12.2 %collective-permute-start.5 = (bf16[512,512]{1,0:T(8,128)(2,1)S(1)}, bf16[512,512]{1,0:T(8,128)(2,1)S(1)}, u32[]{:S(2)}, u32[]{:S(2)}) collective-permute-start(bf16[512,512]{1,0:T(8,128)(2,1)S(1)} %collective-permute-done.4.refs_5_), channel_id=1, source_target_pairs={{0,2},{1,3},{2,0},{3,1},{4,6},{5,7},{6,4},{7,5},{8,10},{9,11},{10,... | collective-permute-start | bytes 1572872 | tf_op jit(solution)/shard_map/features_across/ppermute | solution.py:422
  20.1 11.9 %collective-permute-start.6 = (bf16[512,512]{1,0:T(8,128)(2,1)S(1)}, bf16[512,512]{1,0:T(8,128)(2,1)S(1)}, u32[]{:S(2)}, u32[]{:S(2)}) collective-permute-start(bf16[512,512]{1,0:T(8,128)(2,1)S(1)} %collective-permute-done.4.refs_5_), channel_id=1, source_target_pairs={{0,4},{1,5},{2,6},{3,7},{4,0},{5,1},{6,2},{7,3},{8,12},{9,13},{10,... | collective-permute-start | bytes 1572872 | tf_op jit(solution)/shard_map/features_across/ppermute | solution.py:422
  20.4 21.4 %collective-permute-start.8 = (bf16[512,512]{1,0:T(8,128)(2,1)}, bf16[512,512]{1,0:T(8,128)(2,1)}, u32[]{:S(2)}, u32[]{:S(2)}) collective-permute-start(bf16[512,512]{1,0:T(8,128)(2,1)} %param.14), channel_id=1, source_target_pairs={{0,1},{1,0},{2,3},{3,2},{4,5},{5,4},{6,7},{7,6},{8,9},{9,8},{10,11... | collective-permute-start | bytes 1572872 | tf_op jit(solution)/shard_map/cotangent_rows/ppermute | solution.py:422
  21.1 26.6 %collective-permute-start.7 = (bf16[512,512]{1,0:T(8,128)(2,1)S(1)}, bf16[512,512]{1,0:T(8,128)(2,1)S(1)}, u32[]{:S(2)}, u32[]{:S(2)}) collective-permute-start(bf16[512,512]{1,0:T(8,128)(2,1)S(1)} %constant_dynamic-slice_fusion.refs_2_), channel_id=1, source_target_pairs={{0,16},{1,17},{2,18},{3,19},{4,20},{5,21},{6,22},{7,23},{8,24},{9,... | collective-permute-start | bytes 1572872 | tf_op jit(solution)/shard_map/features_along_z/ppermute | solution.py:422
  32.0 15.7 %collective-permute-start.10 = (bf16[512,512]{1,0:T(8,128)(2,1)S(1)}, bf16[512,512]{1,0:T(8,128)(2,1)S(1)}, u32[]{:S(2)}, u32[]{:S(2)}) collective-permute-start(bf16[512,512]{1,0:T(8,128)(2,1)S(1)} %collective-permute-done.6.refs_7_), channel_id=1, source_target_pairs={{0,2},{1,3},{2,0},{3,1},{4,6},{5,7},{6,4},{7,5},{8,10},{9,11},{10,... | collective-permute-start | bytes 1572872 | tf_op jit(solution)/shard_map/features_across/ppermute | solution.py:422
  33.5 14.2 %collective-permute-start.9 = (bf16[512,512]{1,0:T(8,128)(2,1)S(1)}, bf16[512,512]{1,0:T(8,128)(2,1)S(1)}, u32[]{:S(2)}, u32[]{:S(2)}) collective-permute-start(bf16[512,512]{1,0:T(8,128)(2,1)S(1)} %collective-permute-done.2.refs_3_), channel_id=1, source_target_pairs={{0,4},{1,5},{2,6},{3,7},{4,0},{5,1},{6,2},{7,3},{8,12},{9,13},{10,... | collective-permute-start | bytes 1572872 | tf_op jit(solution)/shard_map/features_across/ppermute | solution.py:422
  34.1 2.8 %copy-start.2 = (bf16[1,8,24,128,128]{4,3,2,1,0:T(8,128)(2,1)S(1)}, bf16[1,8,24,128,128]{4,3,2,1,0:T(8,128)(2,1)}, u32[]{:S(2)}) copy-start(bf16[1,8,24,128,128]{4,3,2,1,0:T(8,128)(2,1)} %param.10) | copy-start | bytes 18874372
  36.9 4.9 %copy-start.8 = (bf16[512,512]{1,0:T(8,128)(2,1)S(1)}, bf16[512,512]{1,0:T(8,128)(2,1)}, u32[]{:S(2)}) copy-start(bf16[512,512]{1,0:T(8,128)(2,1)} %param.14) | copy-start | bytes 1572868
  42.9 9.4 %slice-start = ((s8[6291456]{0:T(1024)(128)(4,1)}), s8[4194304]{0:T(1024)(128)(4,1)S(1)}, s32[]{:S(2)}) async-start(s8[6291456]{0:T(1024)(128)(4,1)} %bitcast.12), calls=%async_computation | async-start | bytes 8388608
  43.0 9.3 %slice-start.1 = ((s8[6291456]{0:T(1024)(128)(4,1)}), s8[2097152]{0:T(1024)(128)(4,1)S(1)}, s32[]{:S(2)}) async-start(s8[6291456]{0:T(1024)(128)(4,1)} %bitcast.12), calls=%async_computation.1 | async-start | bytes 4194304
  47.7 13.8 %collective-permute-start.11 = (bf16[512,512]{1,0:T(8,128)(2,1)S(1)}, bf16[512,512]{1,0:T(8,128)(2,1)}, u32[]{:S(2)}, u32[]{:S(2)}) collective-permute-start(bf16[512,512]{1,0:T(8,128)(2,1)S(1)} %collective-permute-done.7.refs_2_), channel_id=1, source_target_pairs={{0,2},{1,3},{2,0},{3,1},{4,6},{5,7},{6,4},{7,5},{8,10},{9,11},{10,... | collective-permute-start | bytes 1572872 | tf_op jit(solution)/shard_map/features_across/ppermute | solution.py:422
  49.2 13.3 %collective-permute-start.12 = (bf16[512,512]{1,0:T(8,128)(2,1)S(1)}, bf16[512,512]{1,0:T(8,128)(2,1)S(1)}, u32[]{:S(2)}, u32[]{:S(2)}) collective-permute-start(bf16[512,512]{1,0:T(8,128)(2,1)S(1)} %collective-permute-done.7.refs_2_), channel_id=1, source_target_pairs={{0,4},{1,5},{2,6},{3,7},{4,0},{5,1},{6,2},{7,3},{8,12},{9,13},{10,... | collective-permute-start | bytes 1572872 | tf_op jit(solution)/shard_map/features_across/ppermute | solution.py:422
  50.7 13.0 %collective-permute-start.13 = (bf16[512,512]{1,0:T(8,128)(2,1)S(1)}, bf16[512,512]{1,0:T(8,128)(2,1)S(1)}, u32[]{:S(2)}, u32[]{:S(2)}) collective-permute-start(bf16[512,512]{1,0:T(8,128)(2,1)S(1)} %collective-permute-done.7.refs_2_), channel_id=1, source_target_pairs={{0,8},{1,9},{2,10},{3,11},{4,12},{5,13},{6,14},{7,15},{8,0},{9,1},... | collective-permute-start | bytes 1572872 | tf_op jit(solution)/shard_map/features_along_z/ppermute | solution.py:422
  62.5 10.2 %copy-start.4 = (bf16[512,512]{1,0:T(8,128)(2,1)}, bf16[512,512]{1,0:T(8,128)(2,1)S(1)}, u32[]{:S(2)}) copy-start(bf16[512,512]{1,0:T(8,128)(2,1)S(1)} %collective-permute-done.12.refs_4_) | copy-start | bytes 1572868
  63.7 9.0 %copy-start.6 = (bf16[512,512]{1,0:T(8,128)(2,1)}, bf16[512,512]{1,0:T(8,128)(2,1)S(1)}, u32[]{:S(2)}) copy-start(bf16[512,512]{1,0:T(8,128)(2,1)S(1)} %collective-permute-done.13.refs_5_) | copy-start | bytes 1572868
  63.7 12.1 %collective-permute-start.14 = (bf16[512,512]{1,0:T(8,128)(2,1)S(1)}, bf16[512,512]{1,0:T(8,128)(2,1)S(1)}, u32[]{:S(2)}, u32[]{:S(2)}) collective-permute-start(bf16[512,512]{1,0:T(8,128)(2,1)S(1)} %collective-permute-done.13.refs_5_), channel_id=1, source_target_pairs={{0,2},{1,3},{2,0},{3,1},{4,6},{5,7},{6,4},{7,5},{8,10},{9,11},{10,... | collective-permute-start | bytes 1572872 | tf_op jit(solution)/shard_map/features_across/ppermute | solution.py:422
  64.3 11.9 %collective-permute-start.15 = (bf16[512,512]{1,0:T(8,128)(2,1)S(1)}, bf16[512,512]{1,0:T(8,128)(2,1)S(1)}, u32[]{:S(2)}, u32[]{:S(2)}) collective-permute-start(bf16[512,512]{1,0:T(8,128)(2,1)S(1)} %collective-permute-done.13.refs_5_), channel_id=1, source_target_pairs={{0,4},{1,5},{2,6},{3,7},{4,0},{5,1},{6,2},{7,3},{8,12},{9,13},{10,... | collective-permute-start | bytes 1572872 | tf_op jit(solution)/shard_map/features_across/ppermute | solution.py:422
  76.2 11.2 %collective-permute-start.16 = (bf16[512,512]{1,0:T(8,128)(2,1)}, bf16[512,512]{1,0:T(8,128)(2,1)S(1)}, u32[]{:S(2)}, u32[]{:S(2)}) collective-permute-start(bf16[512,512]{1,0:T(8,128)(2,1)} %collective-permute-done.11.refs_3_), channel_id=1, source_target_pairs={{0,4},{1,5},{2,6},{3,7},{4,0},{5,1},{6,2},{7,3},{8,12},{9,13},{10,... | collective-permute-start | bytes 1572872 | tf_op jit(solution)/shard_map/features_across/ppermute | solution.py:422
  76.9 10.8 %collective-permute-start.17 = (bf16[512,512]{1,0:T(8,128)(2,1)S(1)}, bf16[512,512]{1,0:T(8,128)(2,1)S(1)}, u32[]{:S(2)}, u32[]{:S(2)}) collective-permute-start(bf16[512,512]{1,0:T(8,128)(2,1)S(1)} %collective-permute-done.15.refs_7_), channel_id=1, source_target_pairs={{0,2},{1,3},{2,0},{3,1},{4,6},{5,7},{6,4},{7,5},{8,10},{9,11},{10,... | collective-permute-start | bytes 1572872 | tf_op jit(solution)/shard_map/features_across/ppermute | solution.py:422
  78.3 1.0 copy-start.5
  79.3 1.0 copy-start.7
  86.7 6.3 %copy-start.3 = (bf16[512,512]{1,0:T(8,128)(2,1)S(1)}, bf16[512,512]{1,0:T(8,128)(2,1)}, u32[]{:S(2)}) copy-start(bf16[512,512]{1,0:T(8,128)(2,1)} %weight_ref.3) | copy-start | bytes 1572868
  90.3 2.7 %collective-permute-start.18 = (bf16[1024,512]{1,0:T(8,128)(2,1)S(1)}, bf16[1024,512]{1,0:T(8,128)(2,1)S(1)}, u32[]{:S(2)}, u32[]{:S(2)}) collective-permute-start(bf16[1024,512]{1,0:T(8,128)(2,1)S(1)} %forward.5.mine_ref), channel_id=1, source_target_pairs={{0,1},{1,0},{2,3},{3,2},{4,5},{5,4},{6,7},{7,6},{8,9},{9,8},{10,11... | collective-permute-start | bytes 3145736 | tf_op jit(solution)/shard_map/partial_sums/ppermute | solution.py:422
  100.7 15.4 %collective-permute-start.19 = (bf16[576,512]{1,0:T(8,128)(2,1)S(1)}, bf16[576,512]{1,0:T(8,128)(2,1)S(1)}, u32[]{:S(2)}, u32[]{:S(2)}) collective-permute-start(bf16[576,512]{1,0:T(8,128)(2,1)S(1)} %get-tuple-element.216), channel_id=1, source_target_pairs={{0,4},{1,5},{2,6},{3,7},{4,0},{5,1},{6,2},{7,3},{8,12},{9,13},{10,... | collective-permute-start | bytes 1769480 | tf_op jit(solution)/shard_map/grads_across/ppermute | solution.py:422
  101.9 13.7 %collective-permute-start.20 = (bf16[512,512]{1,0:T(8,128)(2,1)S(1)}, bf16[512,512]{1,0:T(8,128)(2,1)S(1)}, u32[]{:S(2)}, u32[]{:S(2)}) collective-permute-start(bf16[512,512]{1,0:T(8,128)(2,1)S(1)} %get-tuple-element.217), channel_id=1, source_target_pairs={{0,2},{1,3},{2,0},{3,1},{4,6},{5,7},{6,4},{7,5},{8,10},{9,11},{10,... | collective-permute-start | bytes 1572872 | tf_op jit(solution)/shard_map/grads_across/ppermute | solution.py:422
  116.2 14.6 %collective-permute-start.21 = (bf16[576,512]{1,0:T(8,128)(2,1)S(1)}, bf16[576,512]{1,0:T(8,128)(2,1)S(1)}, u32[]{:S(2)}, u32[]{:S(2)}) collective-permute-start(bf16[576,512]{1,0:T(8,128)(2,1)S(1)} %add_convert_fusion.1), channel_id=1, source_target_pairs={{0,2},{1,3},{2,0},{3,1},{4,6},{5,7},{6,4},{7,5},{8,10},{9,11},{10,... | collective-permute-start | bytes 1769480 | tf_op jit(solution)/shard_map/grads_across/ppermute | solution.py:422
  117.7 14.2 %collective-permute-start.22 = (bf16[576,512]{1,0:T(8,128)(2,1)S(1)}, bf16[576,512]{1,0:T(8,128)(2,1)S(1)}, u32[]{:S(2)}, u32[]{:S(2)}) collective-permute-start(bf16[576,512]{1,0:T(8,128)(2,1)S(1)} %get-tuple-element.230), channel_id=1, source_target_pairs={{0,4},{1,5},{2,6},{3,7},{4,0},{5,1},{6,2},{7,3},{8,12},{9,13},{10,... | collective-permute-start | bytes 1769480 | tf_op jit(solution)/shard_map/grads_across/ppermute | solution.py:422
  132.2 13.4 %collective-permute-start.25 = (bf16[576,512]{1,0:T(8,128)(2,1)S(1)}, bf16[576,512]{1,0:T(8,128)(2,1)S(1)}, u32[]{:S(2)}, u32[]{:S(2)}) collective-permute-start(bf16[576,512]{1,0:T(8,128)(2,1)S(1)} %add_convert_fusion), channel_id=1, source_target_pairs={{0,8},{1,9},{2,10},{3,11},{4,12},{5,13},{6,14},{7,15},{8,0},{9,1},... | collective-permute-start | bytes 1769480 | tf_op jit(solution)/shard_map/grads_along_z/ppermute | solution.py:422
  133.0 12.7 %collective-permute-start.23 = (bf16[512,512]{1,0:T(8,128)(2,1)S(1)}, bf16[512,512]{1,0:T(8,128)(2,1)S(1)}, u32[]{:S(2)}, u32[]{:S(2)}) collective-permute-start(bf16[512,512]{1,0:T(8,128)(2,1)S(1)} %get-tuple-element.245), channel_id=1, source_target_pairs={{0,2},{1,3},{2,0},{3,1},{4,6},{5,7},{6,4},{7,5},{8,10},{9,11},{10,... | collective-permute-start | bytes 1572872 | tf_op jit(solution)/shard_map/grads_across/ppermute | solution.py:422
  133.6 12.1 %collective-permute-start.24 = (bf16[512,512]{1,0:T(8,128)(2,1)S(1)}, bf16[512,512]{1,0:T(8,128)(2,1)S(1)}, u32[]{:S(2)}, u32[]{:S(2)}) collective-permute-start(bf16[512,512]{1,0:T(8,128)(2,1)S(1)} %add_convert_fusion.6), channel_id=1, source_target_pairs={{0,4},{1,5},{2,6},{3,7},{4,0},{5,1},{6,2},{7,3},{8,12},{9,13},{10,... | collective-permute-start | bytes 1572872 | tf_op jit(solution)/shard_map/grads_across/ppermute | solution.py:422
  145.7 22.8 %collective-permute-start.28 = (bf16[512,512]{1,0:T(8,128)(2,1)S(1)}, bf16[512,512]{1,0:T(8,128)(2,1)S(1)}, u32[]{:S(2)}, u32[]{:S(2)}) collective-permute-start(bf16[512,512]{1,0:T(8,128)(2,1)S(1)} %get-tuple-element.268), channel_id=1, source_target_pairs={{0,4},{1,5},{2,6},{3,7},{4,0},{5,1},{6,2},{7,3},{8,12},{9,13},{10,... | collective-permute-start | bytes 1572872 | tf_op jit(solution)/shard_map/grads_across/ppermute | solution.py:422
  146.8 21.7 %collective-permute-start.29 = (bf16[512,512]{1,0:T(8,128)(2,1)S(1)}, bf16[512,512]{1,0:T(8,128)(2,1)S(1)}, u32[]{:S(2)}, u32[]{:S(2)}) collective-permute-start(bf16[512,512]{1,0:T(8,128)(2,1)S(1)} %get-tuple-element.269), channel_id=1, source_target_pairs={{0,2},{1,3},{2,0},{3,1},{4,6},{5,7},{6,4},{7,5},{8,10},{9,11},{10,... | collective-permute-start | bytes 1572872 | tf_op jit(solution)/shard_map/grads_across/ppermute | solution.py:422
  149.3 19.1 %collective-permute-start.27 = (bf16[64,512]{1,0:T(8,128)(2,1)S(1)}, bf16[64,512]{1,0:T(8,128)(2,1)S(1)}, u32[]{:S(2)}, u32[]{:S(2)}) collective-permute-start(bf16[64,512]{1,0:T(8,128)(2,1)S(1)} %add_convert_fusion.8), channel_id=1, source_target_pairs={{0,16},{1,17},{2,18},{3,19},{4,20},{5,21},{6,22},{7,23},{8,24},{9,... | collective-permute-start | bytes 196616 | tf_op jit(solution)/shard_map/weight_grad/ppermute | solution.py:422
  155.4 22.4 %collective-permute-start.26 = (bf16[512,512]{1,0:T(8,128)(2,1)S(1)}, bf16[512,512]{1,0:T(8,128)(2,1)S(1)}, u32[]{:S(2)}, u32[]{:S(2)}) collective-permute-start(bf16[512,512]{1,0:T(8,128)(2,1)S(1)} %add_convert_fusion.5), channel_id=1, source_target_pairs={{0,16},{1,17},{2,18},{3,19},{4,20},{5,21},{6,22},{7,23},{8,24},{9,... | collective-permute-start | bytes 1572872 | tf_op jit(solution)/shard_map/grads_along_z/ppermute | solution.py:422
  168.6 14.4 %collective-permute-start.30 = (bf16[512,512]{1,0:T(8,128)(2,1)S(1)}, bf16[512,512]{1,0:T(8,128)(2,1)S(1)}, u32[]{:S(2)}, u32[]{:S(2)}) collective-permute-start(bf16[512,512]{1,0:T(8,128)(2,1)S(1)} %add_convert_fusion.4), channel_id=1, source_target_pairs={{0,2},{1,3},{2,0},{3,1},{4,6},{5,7},{6,4},{7,5},{8,10},{9,11},{10,... | collective-permute-start | bytes 1572872 | tf_op jit(solution)/shard_map/grads_across/ppermute | solution.py:422
  169.8 13.2 %collective-permute-start.31 = (bf16[512,512]{1,0:T(8,128)(2,1)S(1)}, bf16[512,512]{1,0:T(8,128)(2,1)S(1)}, u32[]{:S(2)}, u32[]{:S(2)}) collective-permute-start(bf16[512,512]{1,0:T(8,128)(2,1)S(1)} %get-tuple-element.275), channel_id=1, source_target_pairs={{0,4},{1,5},{2,6},{3,7},{4,0},{5,1},{6,2},{7,3},{8,12},{9,13},{10,... | collective-permute-start | bytes 1572872 | tf_op jit(solution)/shard_map/grads_across/ppermute | solution.py:422
  170.9 8.8 %collective-permute-start.32 = (bf16[64,512]{1,0:T(8,128)(2,1)S(1)}, bf16[64,512]{1,0:T(8,128)(2,1)S(1)}, u32[]{:S(2)}, u32[]{:S(2)}) collective-permute-start(bf16[64,512]{1,0:T(8,128)(2,1)S(1)} %add_convert_fusion.7), channel_id=1, source_target_pairs={{0,2},{1,3},{2,0},{3,1},{4,6},{5,7},{6,4},{7,5},{8,10},{9,11},{10,... | collective-permute-start | bytes 196616 | tf_op jit(solution)/shard_map/weight_grad/ppermute | solution.py:422
  171.6 8.2 %collective-permute-start.33 = (bf16[64,512]{1,0:T(8,128)(2,1)S(1)}, bf16[64,512]{1,0:T(8,128)(2,1)S(1)}, u32[]{:S(2)}, u32[]{:S(2)}) collective-permute-start(bf16[64,512]{1,0:T(8,128)(2,1)S(1)} %add_convert_fusion.7), channel_id=1, source_target_pairs={{0,4},{1,5},{2,6},{3,7},{4,0},{5,1},{6,2},{7,3},{8,12},{9,13},{10,... | collective-permute-start | bytes 196616 | tf_op jit(solution)/shard_map/weight_grad/ppermute | solution.py:422
  177.9 5.2 %collective-permute-start.34 = (bf16[64,512]{1,0:T(8,128)(2,1)S(1)}, bf16[64,512]{1,0:T(8,128)(2,1)S(1)}, u32[]{:S(2)}, u32[]{:S(2)}) collective-permute-start(bf16[64,512]{1,0:T(8,128)(2,1)S(1)} %add_convert_fusion.7), channel_id=1, source_target_pairs={{0,6},{1,7},{2,4},{3,5},{4,2},{5,3},{6,0},{7,1},{8,14},{9,15},{10,... | collective-permute-start | bytes 196616 | tf_op jit(solution)/shard_map/weight_grad/ppermute | solution.py:422
  183.0 16.0 %copy-start.1 = (bf16[1024,512]{1,0:T(8,128)(2,1)S(1)}, bf16[1024,512]{1,0:T(8,128)(2,1)}, u32[]{:S(2)}) copy-start(bf16[1024,512]{1,0:T(8,128)(2,1)} %param.8) | copy-start | bytes 3145732
  183.2 11.2 %collective-permute-start.37 = (bf16[512,512]{1,0:T(8,128)(2,1)S(1)}, bf16[512,512]{1,0:T(8,128)(2,1)S(1)}, u32[]{:S(2)}, u32[]{:S(2)}) collective-permute-start(bf16[512,512]{1,0:T(8,128)(2,1)S(1)} %add_convert_fusion.2), channel_id=1, source_target_pairs={{0,8},{1,9},{2,10},{3,11},{4,12},{5,13},{6,14},{7,15},{8,0},{9,1},... | collective-permute-start | bytes 1572872 | tf_op jit(solution)/shard_map/grads_along_z/ppermute | solution.py:422
  184.1 11.9 %collective-permute-start.35 = (bf16[512,512]{1,0:T(8,128)(2,1)S(1)}, bf16[512,512]{1,0:T(8,128)(2,1)S(1)}, u32[]{:S(2)}, u32[]{:S(2)}) collective-permute-start(bf16[512,512]{1,0:T(8,128)(2,1)S(1)} %get-tuple-element.284), channel_id=1, source_target_pairs={{0,2},{1,3},{2,0},{3,1},{4,6},{5,7},{6,4},{7,5},{8,10},{9,11},{10,... | collective-permute-start | bytes 1572872 | tf_op jit(solution)/shard_map/grads_across/ppermute | solution.py:422
  185.0 11.9 %collective-permute-start.36 = (bf16[512,512]{1,0:T(8,128)(2,1)S(1)}, bf16[512,512]{1,0:T(8,128)(2,1)S(1)}, u32[]{:S(2)}, u32[]{:S(2)}) collective-permute-start(bf16[512,512]{1,0:T(8,128)(2,1)S(1)} %add_convert_fusion.3), channel_id=1, source_target_pairs={{0,4},{1,5},{2,6},{3,7},{4,0},{5,1},{6,2},{7,3},{8,12},{9,13},{10,... | collective-permute-start | bytes 1572872 | tf_op jit(solution)/shard_map/grads_across/ppermute | solution.py:422
  185.8 1.6 collective-permute-start.38

commit v7 on v6

--- a/solution.py
+++ b/solution.py
@@ -10,6 +10,10 @@
 BF16 = jnp.bfloat16
 F32 = jnp.float32
 BOTH = ("section", "rep")
+
+
+def in_hbm(value):
+    return pltpu.with_memory_space_constraint(value, pltpu.HBM)
 
 
 def dense_kernel(first, where_ref, packed_ref, tiles_ref, *refs):
@@ -37,7 +41,7 @@
     at = lambda p: first + p
     return pl.pallas_call(
         functools.partial(dense_kernel, first),
-        out_shape=jax.ShapeDtypeStruct((n_rep, panels, block_rows, part), BF16),
+        out_shape=pltpu.HBM((n_rep, panels, block_rows, part), BF16),
         grid_spec=pltpu.PrefetchScalarGridSpec(
             num_scalar_prefetch=2,
             grid=(half,),
@@ -52,7 +56,7 @@
             transcendentals=0,
             bytes_accessed=tiles.size // 8,
         ),
-    )(where, packed, tiles, *([before] if first else []))
+    )(where, packed, in_hbm(tiles), *([in_hbm(before)] if first else []))
 
 
 def other_kernel(first, where_ref, packed_ref, tiles_ref, out_ref):
@@ -82,7 +86,7 @@
     part = block_rows // n_rep
     return pl.pallas_call(
         functools.partial(other_kernel, first),
-        out_shape=jax.ShapeDtypeStruct((half, block_rows, part), BF16),
+        out_shape=pltpu.HBM((half, block_rows, part), BF16),
         grid_spec=pltpu.PrefetchScalarGridSpec(
             num_scalar_prefetch=2,
             grid=(half,),
@@ -195,19 +199,19 @@
             transcendentals=0,
             bytes_accessed=n_units * rows * part * 2 + 8 * rows * width,
         ),
-    )(where, dense, *others, *units, *([total] if has_total else []))
+    )(where, in_hbm(dense), *map(in_hbm, others), *units, *([total] if has_total else []))
 
 
 def slopes(mine_ref, other_ref, weight_ref, cot_ref):
     agg = (mine_ref[...].astype(F32) + other_ref[...].astype(F32)).astype(BF16)
     pre = jnp.dot(agg, weight_ref[...], preferred_element_type=F32)
-    sigma = jax.nn.sigmoid(pre)
+    sigma = 0.5 * jnp.tanh(0.5 * pre) + 0.5
     slope = cot_ref[...].astype(F32) * sigma * (1.0 + pre * (1.0 - sigma))
     return agg, (pre * sigma).astype(BF16), slope.astype(BF16)
 
 
 def middle_kernel(blocks, where_ref, mine_ref, other_ref, weight_ref, cot_ref, a_ref, *refs):
-    grad_ref, odd_ref, even_ref, term_ref, sum_ref = refs
+    grad_ref, odd_ref, even_ref, term_ref, sum_ref, full_ref = refs
     step = pl.program_id(0)
     part = mine_ref.shape[0]
     width = sum_ref.shape[0]
@@ -215,9 +219,11 @@
     @pl.when(step < blocks)
     def _():
         agg, _, pre_grad = slopes(mine_ref, other_ref, weight_ref, cot_ref)
-        grad_ref[:, pl.ds(pl.multiple_of(step * part, part), part)] = lax.dot_general(
+        grad = lax.dot_general(
             weight_ref[...], pre_grad, (((1,), (1,)), ((), ())), preferred_element_type=F32
         ).astype(BF16)
+        grad_ref[...] = grad
+        full_ref[:, pl.ds(pl.multiple_of(step * part, part), part)] = grad
         term = lax.dot_general(agg, pre_grad, (((0,), (0,)), ((), ())), preferred_element_type=F32)
 
         @pl.when(step == 0)
@@ -230,7 +236,7 @@
 
     @pl.when(step >= blocks)
     def _():
-        chunk = jnp.dot(grad_ref[...], a_ref[0, 0], preferred_element_type=F32).astype(BF16)
+        chunk = jnp.dot(full_ref[...], a_ref[0, 0], preferred_element_type=F32).astype(BF16)
 
         @pl.when(step == blocks)
         def _():
@@ -278,8 +284,11 @@
                 block,
                 pl.BlockSpec((1, 1, rows, cols), a_block),
             ],
-            out_specs=[fixed(*shape) for shape in shapes],
-            scratch_shapes=[pltpu.VMEM((width, width), F32)],
+            out_specs=[
+                pl.BlockSpec((width, part), lambda i, where: (0, jnp.minimum(i, blocks - 1))),
+                *(fixed(*shape) for shape in shapes[1:]),
+            ],
+            scratch_shapes=[pltpu.VMEM((width, width), F32), pltpu.VMEM((width, rows), BF16)],
         ),
         compiler_params=pltpu.CompilerParams(vmem_limit_bytes=36 * 2**20),
         cost_estimate=pl.CostEstimate(
@@ -287,7 +296,7 @@
             transcendentals=rows * width,
             bytes_accessed=rows * width * 12,
         ),
-    )(where, mine, other, weight, cotangent, dense)
+    )(where, mine, other, weight, cotangent, in_hbm(dense))
 
 
 def activated_kernel(where_ref, mine_ref, other_ref, weight_ref, cot_ref, act_ref):
@@ -357,7 +366,7 @@
             transcendentals=0,
             bytes_accessed=2 * count * rows * cols + 2 * count * width * cols + 2 * width * rows,
         ),
-    )(where, grad, dense, *([term] if masks else []))
+    )(where, grad, in_hbm(dense), *([term] if masks else []))
 
 
 def final_kernel(n_parts, where_ref, *refs):
@@ -368,13 +377,13 @@
     out_ref[0] = total.T.astype(BF16)
     _, extra, cols = terms[0].shape
     quarter = extra * cols // width
-    for other, term_ref in enumerate(terms):
-        for number in range(4):
+    for number, term_ref in enumerate(terms):
+        for other in range(term_ref.shape[0]):
             place = (where_ref[0] ^ other) * 4 + ((where_ref[1] % 4) ^ number)
             rows = pl.ds(pl.multiple_of(place * quarter, quarter), quarter)
             for turn in range(width // cols):
                 weight_out[rows, turn * cols : (turn + 1) * cols] = term_ref[
-                    number, turn * quarter : (turn + 1) * quarter
+                    other, turn * quarter : (turn + 1) * quarter
                 ].astype(F32)
 
 
@@ -463,11 +472,13 @@
         [tile_rows[0] * row_tiles + tile_cols[0], tile_count[0][:, None]], axis=1
     )
     panels = tile_values.shape[1]
-    def build(first):
+    def build_own(first):
         with jax.named_scope("dense_blocks"):
             live["dense"] = make_dense(
                 first, live.get("dense"), where, tile_values[0], packed, block_rows, n_rep
             )
+
+    def build_others(first):
         with jax.named_scope("other_blocks"):
             return [make_other(first, where, *sent, block_rows, n_rep) for sent in live["tiles"]]
 
@@ -486,8 +497,10 @@
             live["even_x"], live["even_y"] = flip(live[even], X), flip(live[even], Y)
         with jax.named_scope("features_along_z"):
             live[odd] = flip(live[even], Z)
+        if pair == 0:
+            build_own(0)
         if pair == 1:
-            two = build(panels // 2)
+            two = build_others(panels // 2)
             live["others"] = [half for halves in zip(live.pop("one"), two) for half in halves]
             del live["tiles"]
         close()
@@ -499,6 +512,9 @@
                 live[later] = flip(live[later - low_bit(later)], low_bit(later))
         if pair > 0:
             live["total"] = forward_step(*waiting, live.pop("waiting"), live.get("total"))
+        if pair == 1:
+            with jax.named_scope("cotangent_rows"):
+                live["cotangent"] = gather_rep(cotangent)
         close(*([] if last else [later]))
 
         with jax.named_scope("features_across"):
@@ -506,9 +522,8 @@
         units = [live[even], live.pop("even_x"), live.pop("even_y")]
         units += [live[odd], live.pop("odd_x"), live.pop("odd_y")]
         if pair == 0:
-            live["one"] = build(0)
-            with jax.named_scope("cotangent_rows"):
-                live["cotangent"] = gather_rep(cotangent)
+            build_own(panels // 2)
+            live["one"] = build_others(0)
             live["waiting"] = units + crossed
             waiting = [("units", pair)]
         else:
@@ -544,18 +559,6 @@
                 live[name[0]], chunks = chunks[:size], chunks[size:]
 
     z_masks = [1 << bit for bit in range(3, n_section.bit_length() - 1)]
-
-    def weight_step():
-        with jax.named_scope("weight_grad"):
-            if z_masks:
-                flipped = flip(live["weight"], z_masks.pop(0))
-                live["weight"] = add(live["weight"], flipped).astype(BF16)
-            elif "weight" in live:
-                own = live.pop("weight")
-                live["quarters"] = [own, *(flip(own, mask) for mask in (X, Y, X + Y))]
-            elif "quarters" in live:
-                own = jnp.stack(live.pop("quarters"))
-                live["terms"] = [own, *(flip(own, 0, n) for n in range(1, n_rep))]
 
     live["first"] = [odd_diag, even_diag]
     for pair in reversed(range(pair_count)):
@@ -577,10 +580,6 @@
             if "activated" not in live:
                 with jax.named_scope("activated"):
                     live["activated"] = activated_rows(where, *rows, n_rep)
-                live["activated"], live["weight"] = lax.optimization_barrier(
-                    (live["activated"], live["weight"])
-                )
-            weight_step()
         close(*passing)
 
         with jax.named_scope("grads_across"):
@@ -593,30 +592,37 @@
             following = live.pop("even")
             backward_step([("first", pair - 1), ("odd", pair - 1)])
             live["following"], live["even"] = live.pop("odd"), following
-        if not top:
-            weight_step()
         close()
 
+        with jax.named_scope("weight_grad"):
+            if not top and z_masks and mask == z_masks[0]:
+                z_masks.pop(0)
+                arrived = live["to", target, mask][width:]
+                live["weight"] = add(live["weight"], arrived).astype(BF16)
+            if pair == 0:
+                own = live.pop("weight")
+                own = jnp.stack([own, *(flip(own, 0, n) for n in range(1, n_rep))])
+                live["terms"] = [own, *(flip(own, m) for m in (X, Y, X + Y))]
         with jax.named_scope("grads_across"):
             to_x, to_y, own = live.pop("even")
             live["even_sum"] = [own, flip(to_x, X), flip(to_y, Y)]
         with jax.named_scope("grads_along_z"):
             odd_sum = add(*live.pop("odd_sum")).astype(BF16)
             from_odd = flip(odd_sum, Z)
-            live["even_sum"].append(from_odd[:width] if top and pair else from_odd)
+            live["even_sum"].append(from_odd)
         if pair > 0:
             backward_step([("even", pair - 1)])
             live["odd"] = live.pop("following")
         if top:
             with jax.named_scope("weight_grad"):
                 live["weight"] = add(odd_sum[width:], from_odd[width:]).astype(BF16)
-        else:
-            weight_step()
         close()
         arrived = [name for name in live if isinstance(name, tuple) and name[1] == even]
         sums = [*live.pop("even_sum"), *(live.pop(name) for name in arrived)]
         if pair > 0:
-            live["passed"] = add(*sums).astype(BF16)
+            live["passed"] = add(*(value[:width] for value in sums)).astype(BF16)
+            if z_masks and low_bit(even) == z_masks[0]:
+                live["passed"] = jnp.concatenate([live["passed"], live["weight"]])
     with jax.named_scope("grads_out"):
         feat_grad, weight_grad = final_sum(where, sums, live["terms"])
     return (live["activated"], feat_grad, weight_grad)

time: 200 us -> 206 us (1.030)
  Pallas kernels: 65.3 us -> 73.2 us
  waiting for transfers between devices: 78.1 us -> 84.5 us
  starting transfers between devices: 44.2 us -> 39.2 us
  local copies, waits for them, and re-layouts: 6.41 us -> 3.08 us
    ppermute x39 -> x38, waiting for transfers between devices: 78.1 us -> 84.5 us  [flip(): return lax.ppermute(value, BOTH, pairs)]
    pallas_call x4, Pallas kernels: 18.1 us -> 24.5 us  [the longest x2 13.5 us: make_dense(): pl.pallas_call(functools.partial(dense_kernel, first), out_shape=pltpu.HB...]
    ppermute x39 -> x38, starting transfers between devices: 44.2 us -> 39.2 us  [flip(): return lax.ppermute(value, BOTH, pairs)]
    unnamed x22 -> x18, local copies, waits for them, and re-layouts: 5.61 us -> 2.31 us
  transfers between devices with their start and end apart: 39 -> 38, of which waited for: 28 -> 24; matrix products, arithmetic and copies ran while one was open for 2% -> 2% of each run, Pallas kernels for 27% -> 29%
where the time goes in v7:
time: 206 us; the launch traced here: 205 us
  waiting for transfers between devices  84.5 us (41%)
  Pallas kernels  73.2 us (36%)
  starting transfers between devices  39.2 us (19%)
  other arithmetic  4.27 us (2%)
  local copies, waits for them, and re-layouts  3.08 us (1%)
    ppermute x38, waiting for transfers between devices, flip(): return lax.ppermute(value, BOTH, pairs)  84.5 us
    ppermute x38, starting transfers between devices, flip(): return lax.ppermute(value, BOTH, pairs)  39.2 us
    pallas_call x3, Pallas kernels, backward_part(): pl.pallas_call(functools.partial(backward_kernel, masks), out_shape=[jax....  19.2 us
    pallas_call x3, Pallas kernels, forward_part(): pl.pallas_call(functools.partial(forward_kernel, offset, n_units, n_other...  17.8 us
    pallas_call x2, Pallas kernels, make_dense(): pl.pallas_call(functools.partial(dense_kernel, first), out_shape=pltpu.HB...  13.5 us
    pallas_call x2, Pallas kernels, make_other(): pl.pallas_call(functools.partial(other_kernel, first), out_shape=pltpu.HB...  11 us
    pallas_call x1, Pallas kernels, middle(): pl.pallas_call(functools.partial(middle_kernel, blocks), out_shape=[jax.S...  7.88 us
  transfers between devices with their start and end apart: 38, of which 24 were waited for; matrix products, arithmetic and copies ran while one was open for 2% of the time, Pallas kernels for 29%

profile of v7, /device:TPU:0, one launch (start us, length us, event | category | flops | bytes accessed | tf_op | source)
XLA Modules:
  0.0 205.2 jit_solution(16125003273858872894)
XLA Ops:
  1.2 0.7 copy-done
  1.9 3.0 %collective-permute-start.2 = (bf16[512,512]{1,0:T(8,128)(2,1)S(1)}, bf16[512,512]{1,0:T(8,128)(2,1)S(1)}, u32[]{:S(2)}, u32[]{:S(2)}) collective-permute-start(bf16[512,512]{1,0:T(8,128)(2,1)S(1)} %constant_dynamic-slice_fusion.refs_2_), channel_id=1, source_target_pairs={{0,2},{1,3},{2,0},{3,1},{4,6},{5,7},{6,4},{7,5},{8,10},{9,11},{10,... | collective-permute-start | bytes 1572872 | tf_op jit(solution)/shard_map/features_across/ppermute | solution.py:431
  4.9 1.5 collective-permute-start.3
  6.4 1.6 collective-permute-start.4
  8.0 0.7 add_bitcast_fusion
  8.7 0.7 copy.12
  9.5 0.7 broadcast_xor_fusion
  10.3 6.7 %dense_blocks.2.refs_0_ = bf16[2,8,1024,512]{3,2,1,0:T(8,128)(2,1)} custom-call(s32[34]{0:T(128)S(1)} %pad_add_fusion.1.where_ref, s32[8,25]{1,0:T(8,128)S(1)} %pad_add_fusion.packed_ref, bf16[8,24,128,128]{3,2,1,0:T(8,128)(2,1)} %bitcast.9), custom_call_target="tpu_custom_call" | custom-call | bytes 393216 | tf_op jit(solution)/shard_map/dense_blocks/pallas_call | solution.py:42
  17.0 1.3 collective-permute-done.3.refs_4_
  18.3 1.2 collective-permute-done.4.refs_5_
  20.4 2.8 %collective-permute-start.7 = (bf16[512,512]{1,0:T(8,128)(2,1)S(1)}, bf16[512,512]{1,0:T(8,128)(2,1)S(1)}, u32[]{:S(2)}, u32[]{:S(2)}) collective-permute-start(bf16[512,512]{1,0:T(8,128)(2,1)S(1)} %constant_dynamic-slice_fusion.refs_2_), channel_id=1, source_target_pairs={{0,16},{1,17},{2,18},{3,19},{4,20},{5,21},{6,22},{7,23},{8,24},{9,... | collective-permute-start | bytes 1572872 | tf_op jit(solution)/shard_map/features_along_z/ppermute | solution.py:431
  23.2 8.5 %collective-permute-done.5.refs_6_ = bf16[512,512]{1,0:T(8,128)(2,1)S(1)} collective-permute-done((bf16[512,512]{1,0:T(8,128)(2,1)S(1)}, bf16[512,512]{1,0:T(8,128)(2,1)S(1)}, u32[]{:S(2)}, u32[]{:S(2)}) %collective-permute-start.5) | collective-permute-done | bytes 524320 | tf_op jit(solution)/shard_map/features_across/ppermute | solution.py:431
  32.1 0.6 collective-permute-start.8
  32.7 1.4 collective-permute-start.9
  34.2 6.7 %dense_blocks.3.dense_ref.a_ref = bf16[2,8,1024,512]{3,2,1,0:T(8,128)(2,1)} custom-call(s32[34]{0:T(128)S(1)} %pad_add_fusion.1.where_ref, s32[8,25]{1,0:T(8,128)S(1)} %pad_add_fusion.packed_ref, bf16[8,24,128,128]{3,2,1,0:T(8,128)(2,1)} %bitcast.10, bf16[2,8,1024,512]{3,2,1,0:T(8,128)(2,1)} %dense_blocks.2.refs_0_), custom_call_target="tpu_custom_call", output_to_operand_aliasing={{}: (3, {})} | custom-call | bytes 393216 | tf_op jit(solution)/shard_map/dense_blocks/pallas_call | solution.py:42
  40.9 5.5 %other_blocks.2.refs_0_ = bf16[4,1024,512]{2,1,0:T(8,128)(2,1)} custom-call(s32[34]{0:T(128)S(1)} %pad_add_fusion.1.where_ref, s32[8,25]{1,0:T(8,128)S(1)} %collective-permute-done.1.packed_ref, bf16[8,24,128,128]{3,2,1,0:T(8,128)(2,1)} %collective-permute-done.tiles_ref), custom_call_target="tpu_custom_call" | custom-call | bytes 393216 | tf_op jit(solution)/shard_map/other_blocks/pallas_call | solution.py:87
  46.4 0.8 copy-done.5
  47.2 0.8 copy-done.7
  48.4 3.2 %collective-permute-start.11 = (bf16[512,512]{1,0:T(8,128)(2,1)S(1)}, bf16[512,512]{1,0:T(8,128)(2,1)}, u32[]{:S(2)}, u32[]{:S(2)}) collective-permute-start(bf16[512,512]{1,0:T(8,128)(2,1)S(1)} %collective-permute-done.7.refs_2_), channel_id=1, source_target_pairs={{0,4},{1,5},{2,6},{3,7},{4,0},{5,1},{6,2},{7,3},{8,12},{9,13},{10,... | collective-permute-start | bytes 1572872 | tf_op jit(solution)/shard_map/features_across/ppermute | solution.py:431
  51.8 1.3 broadcast_select_fusion.1
  53.1 5.5 %other_blocks.3.refs_1_ = bf16[4,1024,512]{2,1,0:T(8,128)(2,1)} custom-call(s32[34]{0:T(128)S(1)} %pad_add_fusion.1.where_ref, s32[8,25]{1,0:T(8,128)S(1)} %collective-permute-done.1.packed_ref, bf16[8,24,128,128]{3,2,1,0:T(8,128)(2,1)} %collective-permute-done.tiles_ref), custom_call_target="tpu_custom_call" | custom-call | bytes 393216 | tf_op jit(solution)/shard_map/other_blocks/pallas_call | solution.py:87
  58.6 3.9 %collective-permute-done.10.refs_3_ = bf16[512,512]{1,0:T(8,128)(2,1)} collective-permute-done((bf16[512,512]{1,0:T(8,128)(2,1)S(1)}, bf16[512,512]{1,0:T(8,128)(2,1)}, u32[]{:S(2)}, u32[]{:S(2)}) %collective-permute-start.10) | collective-permute-done | bytes 524320 | tf_op jit(solution)/shard_map/features_across/ppermute | solution.py:431
  62.4 1.5 collective-permute-done.11.refs_4_
  63.9 1.5 collective-permute-done.12.refs_5_
  66.1 7.8 %forward.3.refs_8_ = f32[1024,512]{1,0:T(8,128)S(1)} custom-call(s32[34]{0:T(128)S(1)} %pad_add_fusion.1.where_ref, bf16[2,8,1024,512]{3,2,1,0:T(8,128)(2,1)} %dense_blocks.3.dense_ref.a_ref, bf16[4,1024,512]{2,1,0:T(8,128)(2,1)} %other_blocks.2.refs_0_, bf16[4,1024,512]{2,1,0:T(8,128)(2,1)} %other_blocks.3.refs_1_, ...), custom_call_target="tpu_custom_call" | custom-call | flops 4294967296 | bytes 12582912 | tf_op jit(solution)/shard_map/forward/pallas_call | solution.py:180
  73.9 4.4 %collective-permute-done.13.refs_6_ = bf16[512,512]{1,0:T(8,128)(2,1)S(1)} collective-permute-done((bf16[512,512]{1,0:T(8,128)(2,1)}, bf16[512,512]{1,0:T(8,128)(2,1)S(1)}, u32[]{:S(2)}, u32[]{:S(2)}) %collective-permute-start.13) | collective-permute-done | bytes 524320 | tf_op jit(solution)/shard_map/features_across/ppermute | solution.py:431
  78.7 0.6 collective-permute-start.16
  79.3 1.5 collective-permute-start.17
  80.8 6.5 %forward.4.refs_4_ = f32[1024,512]{1,0:T(8,128)S(1)} custom-call(s32[34]{0:T(128)S(1)} %pad_add_fusion.1.where_ref, bf16[2,8,1024,512]{3,2,1,0:T(8,128)(2,1)} %dense_blocks.3.dense_ref.a_ref, bf16[4,1024,512]{2,1,0:T(8,128)(2,1)} %other_blocks.2.refs_0_, bf16[4,1024,512]{2,1,0:T(8,128)(2,1)} %other_blocks.3.refs_1_, ...), custom_call_target="tpu_custom_call" | custom-call | flops 3221225472 | bytes 10485760 | tf_op jit(solution)/shard_map/forward/pallas_call | solution.py:180
  87.3 3.4 %collective-permute-done.16.refs_2_ = bf16[512,512]{1,0:T(8,128)(2,1)S(1)} collective-permute-done((bf16[512,512]{1,0:T(8,128)(2,1)}, bf16[512,512]{1,0:T(8,128)(2,1)S(1)}, u32[]{:S(2)}, u32[]{:S(2)}) %collective-permute-start.16) | collective-permute-done | bytes 524320 | tf_op jit(solution)/shard_map/features_across/ppermute | solution.py:431
  91.1 3.4 %forward.5.mine_ref = bf16[1024,512]{1,0:T(8,128)(2,1)S(1)} custom-call(s32[34]{0:T(128)S(1)} %pad_add_fusion.1.where_ref, bf16[2,8,1024,512]{3,2,1,0:T(8,128)(2,1)} %dense_blocks.3.dense_ref.a_ref, bf16[4,1024,512]{2,1,0:T(8,128)(2,1)} %other_blocks.2.refs_0_, bf16[4,1024,512]{2,1,0:T(8,128)(2,1)} %other_blocks.3.refs_1_, ...), custom_call_target="tpu_custom_call" | custom-call | flops 1073741824 | bytes 6291456 | tf_op jit(solution)/shard_map/forward/pallas_call | solution.py:180
  94.7 2.6 %collective-permute-done.18.other_ref = bf16[1024,512]{1,0:T(8,128)(2,1)S(1)} collective-permute-done((bf16[1024,512]{1,0:T(8,128)(2,1)S(1)}, bf16[1024,512]{1,0:T(8,128)(2,1)S(1)}, u32[]{:S(2)}, u32[]{:S(2)}) %collective-permute-start.18) | collective-permute-done | bytes 1048608 | tf_op jit(solution)/shard_map/partial_sums/ppermute | solution.py:431
  97.3 7.9 %middle.1 = (bf16[512,1024]{1,0:T(8,128)(2,1)S(1)}, bf16[576,512]{1,0:T(8,128)(2,1)S(1)}, bf16[512,512]{1,0:T(8,128)(2,1)S(1)}, bf16[4,64,512]{2,1,0:T(8,128)(2,1)S(1)}) custom-call(s32[34]{0:T(128)S(1)} %pad_add_fusion.1.where_ref, bf16[1024,512]{1,0:T(8,128)(2,1)S(1)} %forward.5.mine_ref, bf16[1024,512]{1,0:T(8,128)(2,1)S(1)} %collective-permute-done.18.other_ref, ...), custom_call_target="tpu_custom_call" | custom-call | flops 2684354560 | bytes 6291456 | tf_op jit(solution)/shard_map/middle/pallas_call | solution.py:274
  105.2 1.2 collective-permute-start.19
  106.4 1.1 collective-permute-start.20
  107.5 7.7 %backward.3 = (bf16[576,512]{1,0:T(8,128)(2,1)S(1)}, bf16[576,512]{1,0:T(8,128)(2,1)S(1)}, bf16[576,512]{1,0:T(8,128)(2,1)S(1)}, bf16[512,512]{1,0:T(8,128)(2,1)...) custom-call(s32[34]{0:T(128)S(1)} %pad_add_fusion.1.where_ref, ...), custom_call_target="tpu_custom_call" | custom-call | flops 3221225472 | bytes 10485760 | tf_op jit(solution)/shard_map/backward/pallas_call | solution.py:353
  115.2 4.9 %collective-permute-done.20 = bf16[512,512]{1,0:T(8,128)(2,1)S(1)} collective-permute-done((bf16[512,512]{1,0:T(8,128)(2,1)S(1)}, bf16[512,512]{1,0:T(8,128)(2,1)S(1)}, u32[]{:S(2)}, u32[]{:S(2)}) %collective-permute-start.20) | collective-permute-done | bytes 524320 | tf_op jit(solution)/shard_map/grads_across/ppermute | solution.py:431
  120.8 1.4 collective-permute-start.21
  122.2 0.9 collective-permute-start.22
  123.1 6.7 %backward.4 = (bf16[512,512]{1,0:T(8,128)(2,1)S(1)}, bf16[512,512]{1,0:T(8,128)(2,1)S(1)}, bf16[512,512]{1,0:T(8,128)(2,1)S(1)}, bf16[512,512]{1,0:T(8,128)(2,1)S(1)}, bf16[512,512]{1,0:T(8,128)(2,1)S(1)}) custom-call(s32[34]{0:T(128)S(1)} %pad_add_fusion.1.where_ref, bf16[512,1024]{1,0:T(8,128)(2,1)S(1)} %get-tuple-element.237.grad_ref, ...), custom_call_target="tpu_custom_call" | custom-call | flops 2684354560 | bytes 8912896 | tf_op jit(solution)/shard_map/backward/pallas_call | solution.py:353
  129.9 5.4 %collective-permute-done.21 = bf16[576,512]{1,0:T(8,128)(2,1)S(1)} collective-permute-done((bf16[576,512]{1,0:T(8,128)(2,1)S(1)}, bf16[576,512]{1,0:T(8,128)(2,1)S(1)}, u32[]{:S(2)}, u32[]{:S(2)}) %collective-permute-start.21) | collective-permute-done | bytes 589856 | tf_op jit(solution)/shard_map/grads_across/ppermute | solution.py:431
  135.4 1.0 collective-permute-done.22
  136.7 1.3 collective-permute-start.25
  138.0 0.9 collective-permute-start.23
  139.5 4.8 %backward.5 = (bf16[512,512]{1,0:T(8,128)(2,1)S(1)}, bf16[512,512]{1,0:T(8,128)(2,1)S(1)}, bf16[512,512]{1,0:T(8,128)(2,1)S(1)}) custom-call(s32[34]{0:T(128)S(1)} %pad_add_fusion.1.where_ref, bf16[512,1024]{1,0:T(8,128)(2,1)S(1)} %get-tuple-element.237.grad_ref, bf16[2,8,1024,512]{3,2,1,0:T(8,128)(2,1)} %dense_blocks.3.dense_ref.a_ref), custom_call_target="tpu_custom_call" | custom-call | flops 1610612736 | bytes 5767168 | tf_op jit(solution)/shard_map/backward/pallas_call | solution.py:353
  144.3 5.8 %collective-permute-done.25 = bf16[576,512]{1,0:T(8,128)(2,1)S(1)} collective-permute-done((bf16[576,512]{1,0:T(8,128)(2,1)S(1)}, bf16[576,512]{1,0:T(8,128)(2,1)S(1)}, u32[]{:S(2)}, u32[]{:S(2)}) %collective-permute-start.25) | collective-permute-done | bytes 589856 | tf_op jit(solution)/shard_map/grads_along_z/ppermute | solution.py:431
  150.6 0.6 collective-permute-start.26
  151.1 1.6 collective-permute-start.27
  152.7 1.8 activated.1
  154.9 3.0 %collective-permute-start.28 = (bf16[576,512]{1,0:T(8,128)(2,1)S(1)}, bf16[576,512]{1,0:T(8,128)(2,1)S(1)}, u32[]{:S(2)}, u32[]{:S(2)}) collective-permute-start(bf16[576,512]{1,0:T(8,128)(2,1)S(1)} %pad_maximum_fusion.1), channel_id=1, source_target_pairs={{0,16},{1,17},{2,18},{3,19},{4,20},{5,21},{6,22},{7,23},{8,24},{9,... | collective-permute-start | bytes 1769480 | tf_op jit(solution)/shard_map/grads_along_z/ppermute | solution.py:431
  157.9 4.0 %collective-permute-done.26 = bf16[512,512]{1,0:T(8,128)(2,1)S(1)} collective-permute-done((bf16[512,512]{1,0:T(8,128)(2,1)S(1)}, bf16[512,512]{1,0:T(8,128)(2,1)S(1)}, u32[]{:S(2)}, u32[]{:S(2)}) %collective-permute-start.26) | collective-permute-done | bytes 524320 | tf_op jit(solution)/shard_map/grads_across/ppermute | solution.py:431
  162.0 1.0 collective-permute-done.27
  163.2 1.3 collective-permute-start.29
  164.4 0.6 collective-permute-start.30
  165.2 15.4 %collective-permute-done.28.refs_4_ = bf16[576,512]{1,0:T(8,128)(2,1)S(1)} collective-permute-done((bf16[576,512]{1,0:T(8,128)(2,1)S(1)}, bf16[576,512]{1,0:T(8,128)(2,1)S(1)}, u32[]{:S(2)}, u32[]{:S(2)}) %collective-permute-start.28) | collective-permute-done | bytes 589856 | tf_op jit(solution)/shard_map/grads_along_z/ppermute | solution.py:431
  180.6 0.9 collective-permute-start.35
  181.5 1.2 collective-permute-start.36
  183.1 1.2 collective-permute-done.31
  184.3 1.2 collective-permute-start.32
  185.6 0.8 collective-permute-start.33
  186.4 10.9 %collective-permute-done.32.refs_6_ = bf16[2,64,512]{2,1,0:T(8,128)(2,1)S(1)} collective-permute-done((bf16[2,64,512]{2,1,0:T(8,128)(2,1)S(1)}, bf16[2,64,512]{2,1,0:T(8,128)(2,1)S(1)}, u32[]{:S(2)}, u32[]{:S(2)}) %collective-permute-start.32) | collective-permute-done | bytes 131104 | tf_op jit(solution)/shard_map/weight_grad/ppermute | solution.py:431
  197.2 1.5 collective-permute-start.34
  198.8 4.3 %collective-permute-done.34.refs_8_ = bf16[2,64,512]{2,1,0:T(8,128)(2,1)S(1)} collective-permute-done((bf16[2,64,512]{2,1,0:T(8,128)(2,1)S(1)}, bf16[2,64,512]{2,1,0:T(8,128)(2,1)S(1)}, u32[]{:S(2)}, u32[]{:S(2)}) %collective-permute-start.34) | collective-permute-done | bytes 131104 | tf_op jit(solution)/shard_map/weight_grad/ppermute | solution.py:431
  203.1 2.1 %grads_out.1 = (bf16[1,512,512]{2,1,0:T(8,128)(2,1)}, f32[512,512]{1,0:T(8,128)}) custom-call(s32[34]{0:T(128)S(1)} %pad_add_fusion.1.where_ref, bf16[512,512]{1,0:T(8,128)(2,1)S(1)} %get-tuple-element.286.refs_0_, bf16[512,512]{1,0:T(8,128)(2,1)S(1)} %collective-permute-done.35.refs_1_, bf16[512,512]{1,0:T(8,128)(2,1)S(1)} %collective-permute-done.36.refs_2_, ...), custom_call_target="tpu_custom_call" | custom-call | flops 1310720 | bytes 3145728 | tf_op jit(solution)/shard_map/grads_out/pallas_call | solution.py:397
  (62 shorter events, 7.2 us)
Async XLA Ops:
  0.6 1.2 copy-start
  0.6 18.9 %collective-permute-start = (bf16[8,24,128,128]{3,2,1,0:T(8,128)(2,1)}, bf16[8,24,128,128]{3,2,1,0:T(8,128)(2,1)}, u32[]{:S(2)}, u32[]{:S(2)}) collective-permute-start(bf16[8,24,128,128]{3,2,1,0:T(8,128)(2,1)} %bitcast.8), channel_id=1, source_target_pairs={{0,1},{1,0},{2,3},{3,2},{4,5},{5,4},{6,7},{7,6},{8,9},{9,8},{10,11... | collective-permute-start | bytes 18874376 | tf_op jit(solution)/shard_map/tiles_exchange/ppermute | solution.py:431
  1.9 15.1 %collective-permute-start.2 = (bf16[512,512]{1,0:T(8,128)(2,1)S(1)}, bf16[512,512]{1,0:T(8,128)(2,1)S(1)}, u32[]{:S(2)}, u32[]{:S(2)}) collective-permute-start(bf16[512,512]{1,0:T(8,128)(2,1)S(1)} %constant_dynamic-slice_fusion.refs_2_), channel_id=1, source_target_pairs={{0,2},{1,3},{2,0},{3,1},{4,6},{5,7},{6,4},{7,5},{8,10},{9,11},{10,... | collective-permute-start | bytes 1572872 | tf_op jit(solution)/shard_map/features_across/ppermute | solution.py:431
  4.9 13.4 %collective-permute-start.3 = (bf16[512,512]{1,0:T(8,128)(2,1)S(1)}, bf16[512,512]{1,0:T(8,128)(2,1)S(1)}, u32[]{:S(2)}, u32[]{:S(2)}) collective-permute-start(bf16[512,512]{1,0:T(8,128)(2,1)S(1)} %constant_dynamic-slice_fusion.refs_2_), channel_id=1, source_target_pairs={{0,4},{1,5},{2,6},{3,7},{4,0},{5,1},{6,2},{7,3},{8,12},{9,13},{10,... | collective-permute-start | bytes 1572872 | tf_op jit(solution)/shard_map/features_across/ppermute | solution.py:431
  6.4 13.1 %collective-permute-start.4 = (bf16[512,512]{1,0:T(8,128)(2,1)S(1)}, bf16[512,512]{1,0:T(8,128)(2,1)S(1)}, u32[]{:S(2)}, u32[]{:S(2)}) collective-permute-start(bf16[512,512]{1,0:T(8,128)(2,1)S(1)} %constant_dynamic-slice_fusion.refs_2_), channel_id=1, source_target_pairs={{0,8},{1,9},{2,10},{3,11},{4,12},{5,13},{6,14},{7,15},{8,0},{9,1},... | collective-permute-start | bytes 1572872 | tf_op jit(solution)/shard_map/features_along_z/ppermute | solution.py:431
  9.5 7.5 %collective-permute-start.1 = (s32[8,25]{1,0:T(8,128)S(1)}, s32[8,25]{1,0:T(8,128)S(1)}, u32[]{:S(2)}, u32[]{:S(2)}) collective-permute-start(s32[8,25]{1,0:T(8,128)S(1)} %pad_add_fusion.packed_ref), channel_id=1, source_target_pairs={{0,1},{1,0},{2,3},{3,2},{4,5},{5,4},{6,7},{7,6},{8,9},{9,8},{10,11... | collective-permute-start | bytes 2408 | tf_op jit(solution)/shard_map/tiles_exchange/ppermute | solution.py:431
  19.5 12.2 %collective-permute-start.5 = (bf16[512,512]{1,0:T(8,128)(2,1)S(1)}, bf16[512,512]{1,0:T(8,128)(2,1)S(1)}, u32[]{:S(2)}, u32[]{:S(2)}) collective-permute-start(bf16[512,512]{1,0:T(8,128)(2,1)S(1)} %collective-permute-done.4.refs_5_), channel_id=1, source_target_pairs={{0,2},{1,3},{2,0},{3,1},{4,6},{5,7},{6,4},{7,5},{8,10},{9,11},{10,... | collective-permute-start | bytes 1572872 | tf_op jit(solution)/shard_map/features_across/ppermute | solution.py:431
  20.1 12.1 %collective-permute-start.6 = (bf16[512,512]{1,0:T(8,128)(2,1)S(1)}, bf16[512,512]{1,0:T(8,128)(2,1)S(1)}, u32[]{:S(2)}, u32[]{:S(2)}) collective-permute-start(bf16[512,512]{1,0:T(8,128)(2,1)S(1)} %collective-permute-done.4.refs_5_), channel_id=1, source_target_pairs={{0,4},{1,5},{2,6},{3,7},{4,0},{5,1},{6,2},{7,3},{8,12},{9,13},{10,... | collective-permute-start | bytes 1572872 | tf_op jit(solution)/shard_map/features_across/ppermute | solution.py:431
  20.4 26.0 %collective-permute-start.7 = (bf16[512,512]{1,0:T(8,128)(2,1)S(1)}, bf16[512,512]{1,0:T(8,128)(2,1)S(1)}, u32[]{:S(2)}, u32[]{:S(2)}) collective-permute-start(bf16[512,512]{1,0:T(8,128)(2,1)S(1)} %constant_dynamic-slice_fusion.refs_2_), channel_id=1, source_target_pairs={{0,16},{1,17},{2,18},{3,19},{4,20},{5,21},{6,22},{7,23},{8,24},{9,... | collective-permute-start | bytes 1572872 | tf_op jit(solution)/shard_map/features_along_z/ppermute | solution.py:431
  32.1 8.8 %copy-start.3 = (bf16[512,512]{1,0:T(8,128)(2,1)}, bf16[512,512]{1,0:T(8,128)(2,1)S(1)}, u32[]{:S(2)}) copy-start(bf16[512,512]{1,0:T(8,128)(2,1)S(1)} %collective-permute-done.6.refs_7_) | copy-start | bytes 1572868
  32.1 14.3 %collective-permute-start.8 = (bf16[512,512]{1,0:T(8,128)(2,1)S(1)}, bf16[512,512]{1,0:T(8,128)(2,1)S(1)}, u32[]{:S(2)}, u32[]{:S(2)}) collective-permute-start(bf16[512,512]{1,0:T(8,128)(2,1)S(1)} %collective-permute-done.2.refs_3_), channel_id=1, source_target_pairs={{0,4},{1,5},{2,6},{3,7},{4,0},{5,1},{6,2},{7,3},{8,12},{9,13},{10,... | collective-permute-start | bytes 1572872 | tf_op jit(solution)/shard_map/features_across/ppermute | solution.py:431
  32.7 14.5 %collective-permute-start.9 = (bf16[512,512]{1,0:T(8,128)(2,1)S(1)}, bf16[512,512]{1,0:T(8,128)(2,1)S(1)}, u32[]{:S(2)}, u32[]{:S(2)}) collective-permute-start(bf16[512,512]{1,0:T(8,128)(2,1)S(1)} %collective-permute-done.6.refs_7_), channel_id=1, source_target_pairs={{0,2},{1,3},{2,0},{3,1},{4,6},{5,7},{6,4},{7,5},{8,10},{9,11},{10,... | collective-permute-start | bytes 1572872 | tf_op jit(solution)/shard_map/features_across/ppermute | solution.py:431
  34.2 17.6 %collective-permute-start.15 = (bf16[512,512]{1,0:T(8,128)(2,1)}, bf16[512,512]{1,0:T(8,128)(2,1)}, u32[]{:S(2)}, u32[]{:S(2)}) collective-permute-start(bf16[512,512]{1,0:T(8,128)(2,1)} %param.14), channel_id=1, source_target_pairs={{0,1},{1,0},{2,3},{3,2},{4,5},{5,4},{6,7},{7,6},{8,9},{9,8},{10,11... | collective-permute-start | bytes 1572872 | tf_op jit(solution)/shard_map/cotangent_rows/ppermute | solution.py:431
  46.4 0.8 copy-start.5
  47.2 0.8 copy-start.7
  48.0 14.5 %collective-permute-start.10 = (bf16[512,512]{1,0:T(8,128)(2,1)S(1)}, bf16[512,512]{1,0:T(8,128)(2,1)}, u32[]{:S(2)}, u32[]{:S(2)}) collective-permute-start(bf16[512,512]{1,0:T(8,128)(2,1)S(1)} %collective-permute-done.7.refs_2_), channel_id=1, source_target_pairs={{0,2},{1,3},{2,0},{3,1},{4,6},{5,7},{6,4},{7,5},{8,10},{9,11},{10,... | collective-permute-start | bytes 1572872 | tf_op jit(solution)/shard_map/features_across/ppermute | solution.py:431
  48.4 15.5 %collective-permute-start.11 = (bf16[512,512]{1,0:T(8,128)(2,1)S(1)}, bf16[512,512]{1,0:T(8,128)(2,1)}, u32[]{:S(2)}, u32[]{:S(2)}) collective-permute-start(bf16[512,512]{1,0:T(8,128)(2,1)S(1)} %collective-permute-done.7.refs_2_), channel_id=1, source_target_pairs={{0,4},{1,5},{2,6},{3,7},{4,0},{5,1},{6,2},{7,3},{8,12},{9,13},{10,... | collective-permute-start | bytes 1572872 | tf_op jit(solution)/shard_map/features_across/ppermute | solution.py:431
  51.6 13.7 %collective-permute-start.12 = (bf16[512,512]{1,0:T(8,128)(2,1)S(1)}, bf16[512,512]{1,0:T(8,128)(2,1)}, u32[]{:S(2)}, u32[]{:S(2)}) collective-permute-start(bf16[512,512]{1,0:T(8,128)(2,1)S(1)} %collective-permute-done.7.refs_2_), channel_id=1, source_target_pairs={{0,8},{1,9},{2,10},{3,11},{4,12},{5,13},{6,14},{7,15},{8,0},{9,1},... | collective-permute-start | bytes 1572872 | tf_op jit(solution)/shard_map/features_along_z/ppermute | solution.py:431
  58.6 7.5 %copy-start.4 = (bf16[512,512]{1,0:T(8,128)(2,1)S(1)}, bf16[512,512]{1,0:T(8,128)(2,1)}, u32[]{:S(2)}) copy-start(bf16[512,512]{1,0:T(8,128)(2,1)} %copy-done.3) | copy-start | bytes 1572868
  58.6 7.5 %copy-start.6 = (bf16[512,512]{1,0:T(8,128)(2,1)S(1)}, bf16[512,512]{1,0:T(8,128)(2,1)}, u32[]{:S(2)}) copy-start(bf16[512,512]{1,0:T(8,128)(2,1)} %copy-done.5) | copy-start | bytes 1572868
  58.6 7.5 %copy-start.8 = (bf16[512,512]{1,0:T(8,128)(2,1)S(1)}, bf16[512,512]{1,0:T(8,128)(2,1)}, u32[]{:S(2)}) copy-start(bf16[512,512]{1,0:T(8,128)(2,1)} %copy-done.7) | copy-start | bytes 1572868
  65.4 13.0 %collective-permute-start.13 = (bf16[512,512]{1,0:T(8,128)(2,1)}, bf16[512,512]{1,0:T(8,128)(2,1)S(1)}, u32[]{:S(2)}, u32[]{:S(2)}) collective-permute-start(bf16[512,512]{1,0:T(8,128)(2,1)} %collective-permute-done.12.refs_5_), channel_id=1, source_target_pairs={{0,2},{1,3},{2,0},{3,1},{4,6},{5,7},{6,4},{7,5},{8,10},{9,11},{10,... | collective-permute-start | bytes 1572872 | tf_op jit(solution)/shard_map/features_across/ppermute | solution.py:431
  65.7 13.0 %collective-permute-start.14 = (bf16[512,512]{1,0:T(8,128)(2,1)}, bf16[512,512]{1,0:T(8,128)(2,1)S(1)}, u32[]{:S(2)}, u32[]{:S(2)}) collective-permute-start(bf16[512,512]{1,0:T(8,128)(2,1)} %collective-permute-done.12.refs_5_), channel_id=1, source_target_pairs={{0,4},{1,5},{2,6},{3,7},{4,0},{5,1},{6,2},{7,3},{8,12},{9,13},{10,... | collective-permute-start | bytes 1572872 | tf_op jit(solution)/shard_map/features_across/ppermute | solution.py:431
  78.7 12.1 %collective-permute-start.16 = (bf16[512,512]{1,0:T(8,128)(2,1)}, bf16[512,512]{1,0:T(8,128)(2,1)S(1)}, u32[]{:S(2)}, u32[]{:S(2)}) collective-permute-start(bf16[512,512]{1,0:T(8,128)(2,1)} %collective-permute-done.10.refs_3_), channel_id=1, source_target_pairs={{0,4},{1,5},{2,6},{3,7},{4,0},{5,1},{6,2},{7,3},{8,12},{9,13},{10,... | collective-permute-start | bytes 1572872 | tf_op jit(solution)/shard_map/features_across/ppermute | solution.py:431
  79.3 11.9 %collective-permute-start.17 = (bf16[512,512]{1,0:T(8,128)(2,1)S(1)}, bf16[512,512]{1,0:T(8,128)(2,1)S(1)}, u32[]{:S(2)}, u32[]{:S(2)}) collective-permute-start(bf16[512,512]{1,0:T(8,128)(2,1)S(1)} %collective-permute-done.14.refs_7_), channel_id=1, source_target_pairs={{0,2},{1,3},{2,0},{3,1},{4,6},{5,7},{6,4},{7,5},{8,10},{9,11},{10,... | collective-permute-start | bytes 1572872 | tf_op jit(solution)/shard_map/features_across/ppermute | solution.py:431
  87.3 10.0 %copy-start.2 = (bf16[512,512]{1,0:T(8,128)(2,1)S(1)}, bf16[512,512]{1,0:T(8,128)(2,1)}, u32[]{:S(2)}) copy-start(bf16[512,512]{1,0:T(8,128)(2,1)} %weight_ref.3) | copy-start | bytes 1572868
  94.6 2.7 %collective-permute-start.18 = (bf16[1024,512]{1,0:T(8,128)(2,1)S(1)}, bf16[1024,512]{1,0:T(8,128)(2,1)S(1)}, u32[]{:S(2)}, u32[]{:S(2)}) collective-permute-start(bf16[1024,512]{1,0:T(8,128)(2,1)S(1)} %forward.5.mine_ref), channel_id=1, source_target_pairs={{0,1},{1,0},{2,3},{3,2},{4,5},{5,4},{6,7},{7,6},{8,9},{9,8},{10,11... | collective-permute-start | bytes 3145736 | tf_op jit(solution)/shard_map/partial_sums/ppermute | solution.py:431
  105.2 15.4 %collective-permute-start.19 = (bf16[576,512]{1,0:T(8,128)(2,1)S(1)}, bf16[576,512]{1,0:T(8,128)(2,1)S(1)}, u32[]{:S(2)}, u32[]{:S(2)}) collective-permute-start(bf16[576,512]{1,0:T(8,128)(2,1)S(1)} %get-tuple-element.213), channel_id=1, source_target_pairs={{0,4},{1,5},{2,6},{3,7},{4,0},{5,1},{6,2},{7,3},{8,12},{9,13},{10,... | collective-permute-start | bytes 1769480 | tf_op jit(solution)/shard_map/grads_across/ppermute | solution.py:431
  106.4 13.7 %collective-permute-start.20 = (bf16[512,512]{1,0:T(8,128)(2,1)S(1)}, bf16[512,512]{1,0:T(8,128)(2,1)S(1)}, u32[]{:S(2)}, u32[]{:S(2)}) collective-permute-start(bf16[512,512]{1,0:T(8,128)(2,1)S(1)} %get-tuple-element.214), channel_id=1, source_target_pairs={{0,2},{1,3},{2,0},{3,1},{4,6},{5,7},{6,4},{7,5},{8,10},{9,11},{10,... | collective-permute-start | bytes 1572872 | tf_op jit(solution)/shard_map/grads_across/ppermute | solution.py:431
  120.8 14.6 %collective-permute-start.21 = (bf16[576,512]{1,0:T(8,128)(2,1)S(1)}, bf16[576,512]{1,0:T(8,128)(2,1)S(1)}, u32[]{:S(2)}, u32[]{:S(2)}) collective-permute-start(bf16[576,512]{1,0:T(8,128)(2,1)S(1)} %add_convert_fusion.1), channel_id=1, source_target_pairs={{0,2},{1,3},{2,0},{3,1},{4,6},{5,7},{6,4},{7,5},{8,10},{9,11},{10,... | collective-permute-start | bytes 1769480 | tf_op jit(solution)/shard_map/grads_across/ppermute | solution.py:431
  122.2 14.3 %collective-permute-start.22 = (bf16[576,512]{1,0:T(8,128)(2,1)S(1)}, bf16[576,512]{1,0:T(8,128)(2,1)S(1)}, u32[]{:S(2)}, u32[]{:S(2)}) collective-permute-start(bf16[576,512]{1,0:T(8,128)(2,1)S(1)} %get-tuple-element.227), channel_id=1, source_target_pairs={{0,4},{1,5},{2,6},{3,7},{4,0},{5,1},{6,2},{7,3},{8,12},{9,13},{10,... | collective-permute-start | bytes 1769480 | tf_op jit(solution)/shard_map/grads_across/ppermute | solution.py:431
  136.7 13.4 %collective-permute-start.25 = (bf16[576,512]{1,0:T(8,128)(2,1)S(1)}, bf16[576,512]{1,0:T(8,128)(2,1)S(1)}, u32[]{:S(2)}, u32[]{:S(2)}) collective-permute-start(bf16[576,512]{1,0:T(8,128)(2,1)S(1)} %add_convert_fusion), channel_id=1, source_target_pairs={{0,8},{1,9},{2,10},{3,11},{4,12},{5,13},{6,14},{7,15},{8,0},{9,1},... | collective-permute-start | bytes 1769480 | tf_op jit(solution)/shard_map/grads_along_z/ppermute | solution.py:431
  138.0 12.1 %collective-permute-start.23 = (bf16[512,512]{1,0:T(8,128)(2,1)S(1)}, bf16[512,512]{1,0:T(8,128)(2,1)S(1)}, u32[]{:S(2)}, u32[]{:S(2)}) collective-permute-start(bf16[512,512]{1,0:T(8,128)(2,1)S(1)} %get-tuple-element.242), channel_id=1, source_target_pairs={{0,2},{1,3},{2,0},{3,1},{4,6},{5,7},{6,4},{7,5},{8,10},{9,11},{10,... | collective-permute-start | bytes 1572872 | tf_op jit(solution)/shard_map/grads_across/ppermute | solution.py:431
  138.9 11.6 %collective-permute-start.24 = (bf16[512,512]{1,0:T(8,128)(2,1)S(1)}, bf16[512,512]{1,0:T(8,128)(2,1)S(1)}, u32[]{:S(2)}, u32[]{:S(2)}) collective-permute-start(bf16[512,512]{1,0:T(8,128)(2,1)S(1)} %add_convert_fusion.6), channel_id=1, source_target_pairs={{0,4},{1,5},{2,6},{3,7},{4,0},{5,1},{6,2},{7,3},{8,12},{9,13},{10,... | collective-permute-start | bytes 1572872 | tf_op jit(solution)/shard_map/grads_across/ppermute | solution.py:431
  150.6 11.4 %collective-permute-start.26 = (bf16[512,512]{1,0:T(8,128)(2,1)S(1)}, bf16[512,512]{1,0:T(8,128)(2,1)S(1)}, u32[]{:S(2)}, u32[]{:S(2)}) collective-permute-start(bf16[512,512]{1,0:T(8,128)(2,1)S(1)} %get-tuple-element.260), channel_id=1, source_target_pairs={{0,4},{1,5},{2,6},{3,7},{4,0},{5,1},{6,2},{7,3},{8,12},{9,13},{10,... | collective-permute-start | bytes 1572872 | tf_op jit(solution)/shard_map/grads_across/ppermute | solution.py:431
  151.1 11.9 %collective-permute-start.27 = (bf16[512,512]{1,0:T(8,128)(2,1)S(1)}, bf16[512,512]{1,0:T(8,128)(2,1)S(1)}, u32[]{:S(2)}, u32[]{:S(2)}) collective-permute-start(bf16[512,512]{1,0:T(8,128)(2,1)S(1)} %get-tuple-element.261), channel_id=1, source_target_pairs={{0,2},{1,3},{2,0},{3,1},{4,6},{5,7},{6,4},{7,5},{8,10},{9,11},{10,... | collective-permute-start | bytes 1572872 | tf_op jit(solution)/shard_map/grads_across/ppermute | solution.py:431
  154.9 25.7 %collective-permute-start.28 = (bf16[576,512]{1,0:T(8,128)(2,1)S(1)}, bf16[576,512]{1,0:T(8,128)(2,1)S(1)}, u32[]{:S(2)}, u32[]{:S(2)}) collective-permute-start(bf16[576,512]{1,0:T(8,128)(2,1)S(1)} %pad_maximum_fusion.1), channel_id=1, source_target_pairs={{0,16},{1,17},{2,18},{3,19},{4,20},{5,21},{6,22},{7,23},{8,24},{9,... | collective-permute-start | bytes 1769480 | tf_op jit(solution)/shard_map/grads_along_z/ppermute | solution.py:431
  163.2 17.4 %collective-permute-start.29 = (bf16[512,512]{1,0:T(8,128)(2,1)S(1)}, bf16[512,512]{1,0:T(8,128)(2,1)S(1)}, u32[]{:S(2)}, u32[]{:S(2)}) collective-permute-start(bf16[512,512]{1,0:T(8,128)(2,1)S(1)} %add_convert_fusion.4), channel_id=1, source_target_pairs={{0,2},{1,3},{2,0},{3,1},{4,6},{5,7},{6,4},{7,5},{8,10},{9,11},{10,... | collective-permute-start | bytes 1572872 | tf_op jit(solution)/shard_map/grads_across/ppermute | solution.py:431
  164.4 16.1 %collective-permute-start.30 = (bf16[512,512]{1,0:T(8,128)(2,1)S(1)}, bf16[512,512]{1,0:T(8,128)(2,1)S(1)}, u32[]{:S(2)}, u32[]{:S(2)}) collective-permute-start(bf16[512,512]{1,0:T(8,128)(2,1)S(1)} %get-tuple-element.271), channel_id=1, source_target_pairs={{0,4},{1,5},{2,6},{3,7},{4,0},{5,1},{6,2},{7,3},{8,12},{9,13},{10,... | collective-permute-start | bytes 1572872 | tf_op jit(solution)/shard_map/grads_across/ppermute | solution.py:431
  180.6 22.5 %collective-permute-start.35 = (bf16[512,512]{1,0:T(8,128)(2,1)S(1)}, bf16[512,512]{1,0:T(8,128)(2,1)S(1)}, u32[]{:S(2)}, u32[]{:S(2)}) collective-permute-start(bf16[512,512]{1,0:T(8,128)(2,1)S(1)} %get-tuple-element.280), channel_id=1, source_target_pairs={{0,2},{1,3},{2,0},{3,1},{4,6},{5,7},{6,4},{7,5},{8,10},{9,11},{10,... | collective-permute-start | bytes 1572872 | tf_op jit(solution)/shard_map/grads_across/ppermute | solution.py:431
  181.5 21.6 %collective-permute-start.36 = (bf16[512,512]{1,0:T(8,128)(2,1)S(1)}, bf16[512,512]{1,0:T(8,128)(2,1)S(1)}, u32[]{:S(2)}, u32[]{:S(2)}) collective-permute-start(bf16[512,512]{1,0:T(8,128)(2,1)S(1)} %add_convert_fusion.3), channel_id=1, source_target_pairs={{0,4},{1,5},{2,6},{3,7},{4,0},{5,1},{6,2},{7,3},{8,12},{9,13},{10,... | collective-permute-start | bytes 1572872 | tf_op jit(solution)/shard_map/grads_across/ppermute | solution.py:431
  182.7 22.6 %copy-start.1 = (bf16[1024,512]{1,0:T(8,128)(2,1)S(1)}, bf16[1024,512]{1,0:T(8,128)(2,1)}, u32[]{:S(2)}) copy-start(bf16[1024,512]{1,0:T(8,128)(2,1)} %param.8) | copy-start | bytes 3145732
  182.9 20.2 %collective-permute-start.37 = (bf16[512,512]{1,0:T(8,128)(2,1)S(1)}, bf16[512,512]{1,0:T(8,128)(2,1)S(1)}, u32[]{:S(2)}, u32[]{:S(2)}) collective-permute-start(bf16[512,512]{1,0:T(8,128)(2,1)S(1)} %add_convert_fusion.2), channel_id=1, source_target_pairs={{0,8},{1,9},{2,10},{3,11},{4,12},{5,13},{6,14},{7,15},{8,0},{9,1},... | collective-permute-start | bytes 1572872 | tf_op jit(solution)/shard_map/grads_along_z/ppermute | solution.py:431
  183.0 1.3 collective-permute-start.31
  184.3 12.9 %collective-permute-start.32 = (bf16[2,64,512]{2,1,0:T(8,128)(2,1)S(1)}, bf16[2,64,512]{2,1,0:T(8,128)(2,1)S(1)}, u32[]{:S(2)}, u32[]{:S(2)}) collective-permute-start(bf16[2,64,512]{2,1,0:T(8,128)(2,1)S(1)} %pad_maximum_fusion.2.refs_5_), channel_id=1, source_target_pairs={{0,2},{1,3},{2,0},{3,1},{4,6},{5,7},{6,4},{7,5},{8,10},{9,11},{10,... | collective-permute-start | bytes 393224 | tf_op jit(solution)/shard_map/weight_grad/ppermute | solution.py:431
  185.6 13.2 %collective-permute-start.33 = (bf16[2,64,512]{2,1,0:T(8,128)(2,1)S(1)}, bf16[2,64,512]{2,1,0:T(8,128)(2,1)S(1)}, u32[]{:S(2)}, u32[]{:S(2)}) collective-permute-start(bf16[2,64,512]{2,1,0:T(8,128)(2,1)S(1)} %pad_maximum_fusion.2.refs_5_), channel_id=1, source_target_pairs={{0,4},{1,5},{2,6},{3,7},{4,0},{5,1},{6,2},{7,3},{8,12},{9,13},{10,... | collective-permute-start | bytes 393224 | tf_op jit(solution)/shard_map/weight_grad/ppermute | solution.py:431
  197.2 5.9 %collective-permute-start.34 = (bf16[2,64,512]{2,1,0:T(8,128)(2,1)S(1)}, bf16[2,64,512]{2,1,0:T(8,128)(2,1)S(1)}, u32[]{:S(2)}, u32[]{:S(2)}) collective-permute-start(bf16[2,64,512]{2,1,0:T(8,128)(2,1)S(1)} %pad_maximum_fusion.2.refs_5_), channel_id=1, source_target_pairs={{0,6},{1,7},{2,4},{3,5},{4,2},{5,3},{6,0},{7,1},{8,14},{9,15},{10,... | collective-permute-start | bytes 393224 | tf_op jit(solution)/shard_map/weight_grad/ppermute | solution.py:431

commit v8 on v7

--- a/solution.py
+++ b/solution.py
@@ -59,8 +59,8 @@
     )(where, packed, in_hbm(tiles), *([in_hbm(before)] if first else []))
 
 
-def other_kernel(first, where_ref, packed_ref, tiles_ref, out_ref):
-    panel = first + pl.program_id(0)
+def other_kernel(where_ref, packed_ref, tiles_ref, out_ref):
+    panel = pl.program_id(0)
     size, slots = tiles_ref.shape[-1], tiles_ref.shape[1]
     row_tiles, per_part = out_ref.shape[1] // size, out_ref.shape[2] // size
     out_ref[...] = jnp.zeros_like(out_ref)
@@ -80,17 +80,16 @@
     lax.fori_loop(0, packed_ref[panel, slots], add_tile, 0)
 
 
-def make_other(first, where, tiles, packed, block_rows, n_rep):
+def make_other(where, tiles, packed, block_rows, n_rep):
     panels, slots, size, _ = tiles.shape
-    half = panels // 2
     part = block_rows // n_rep
     return pl.pallas_call(
-        functools.partial(other_kernel, first),
-        out_shape=pltpu.HBM((half, block_rows, part), BF16),
+        other_kernel,
+        out_shape=pltpu.HBM((panels, block_rows, part), BF16),
         grid_spec=pltpu.PrefetchScalarGridSpec(
             num_scalar_prefetch=2,
-            grid=(half,),
-            in_specs=[pl.BlockSpec((1, slots, size, size), lambda p, *_: (first + p, 0, 0, 0))],
+            grid=(panels,),
+            in_specs=[pl.BlockSpec((1, slots, size, size), lambda p, *_: (p, 0, 0, 0))],
             out_specs=pl.BlockSpec((1, block_rows, part), lambda p, *_: (p, 0, 0)),
         ),
         compiler_params=pltpu.CompilerParams(vmem_limit_bytes=36 * 2**20),
@@ -106,7 +105,6 @@
     total_ref, refs = (refs[0], refs[1:]) if has_total else (None, refs)
     out_ref, sum_ref, a_buf, u_buf, sems, sum_sem = refs
     _, panels, _, part = dense_ref.shape
-    some = others[0].shape[0]
     rep = where_ref[0]
 
     def a_copy(source, slot, side):
@@ -121,7 +119,7 @@
         for side in range(2):
             place = where_ref[offset + 2 * pair + side]
             owner, panel = place // panels, place % panels
-            turn = ((owner ^ rep) - 1) * (panels // some) + panel // some
+            turn = (owner ^ rep) - 1
 
             @pl.when(owner == rep)
             def _():
@@ -131,7 +129,7 @@
 
                 @pl.when((owner != rep) & (turn == number))
                 def _():
-                    a_copy(other_ref.at[panel % some], slot, side).start()
+                    a_copy(other_ref.at[panel], slot, side).start()
 
             for number in range(side, n_units, 2):
 
@@ -214,7 +212,6 @@
     grad_ref, odd_ref, even_ref, term_ref, sum_ref, full_ref = refs
     step = pl.program_id(0)
     part = mine_ref.shape[0]
-    width = sum_ref.shape[0]
 
     @pl.when(step < blocks)
     def _():
@@ -240,32 +237,28 @@
 
         @pl.when(step == blocks)
         def _():
-            _, extra, cols = term_ref.shape
-            quarter = extra * cols // width
-            for number in range(4):
-                start = pl.multiple_of((where_ref[0] * 4 + number) * quarter, quarter)
-                rows = sum_ref[pl.ds(start, quarter), :].astype(BF16)
-                for turn in range(width // cols):
-                    term_ref[number, turn * quarter : (turn + 1) * quarter] = rows[
-                        :, turn * cols : (turn + 1) * cols
-                    ]
-            odd_ref[:width] = chunk
-            odd_ref[width:] = term_ref[(where_ref[1] % 4) ^ 3]
+            odd_ref[...] = chunk
+            depth, size, _ = term_ref.shape
+            z = where_ref[1] // 4
+            for number in range(depth):
+                start = (where_ref[0] * depth + (z ^ number)) * size
+                rows = sum_ref[pl.ds(pl.multiple_of(start, size), size), :]
+                term_ref[number] = rows.astype(BF16)
 
         @pl.when(step > blocks)
         def _():
             even_ref[...] = chunk
 
 
-def middle(where, offset, mine, other, weight, cotangent, dense):
+def middle(where, offset, mine, other, weight, cotangent, dense, depth):
     rows, width = mine.shape
     n_rep, _, _, cols = dense.shape
     blocks = 4
     part = rows // blocks
-    extra = width // n_rep // 4 * (width // cols)
+    size = width // n_rep // depth
     block = pl.BlockSpec((part, width), lambda i, where: (jnp.minimum(i, blocks - 1), 0))
     fixed = lambda *shape: pl.BlockSpec(shape, lambda i, where: (0,) * len(shape))
-    shapes = [(width, rows), (width + extra, cols), (width, cols), (4, extra, cols)]
+    shapes = [(width, rows), (width, cols), (width, cols), (depth, size, width)]
 
     def a_block(i, where):
         place = where[offset + jnp.maximum(i - blocks, 0)]
@@ -326,39 +319,32 @@
     )(where, mine, other, weight, cotangent)
 
 
-def backward_kernel(masks, where_ref, grad_ref, a_ref, *refs):
-    term_ref, out_refs = (refs[0], refs[1:]) if masks else (None, refs)
-    width = grad_ref.shape[0]
+def backward_kernel(where_ref, grad_ref, a_ref, *out_refs):
     chunk = jnp.dot(grad_ref[...], a_ref[0, 0], preferred_element_type=F32).astype(BF16)
     for number, out_ref in enumerate(out_refs):
 
         @pl.when(pl.program_id(0) == number)
         def _():
-            out_ref[:width] = chunk
-            if number < len(masks):
-                out_ref[width:] = term_ref[(where_ref[1] % 4) ^ masks[number]]
-
-
-def backward_part(where, offset, count, grad, dense, masks=(), term=None):
+            out_ref[...] = chunk
+
+
+def backward_part(where, offset, count, grad, dense):
     width, rows = grad.shape
     n_rep, _, _, cols = dense.shape
-    fixed = lambda *shape: pl.BlockSpec(shape, lambda i, where: (0,) * len(shape))
-    extra = term.shape[1] if masks else 0
-    shapes = [(width + extra * (number < len(masks)), cols) for number in range(count)]
+    fixed = lambda *shape: pl.BlockSpec(shape, lambda i, where: (0, 0))
 
     def a_block(i, where):
         place = where[offset + i]
         return (place % n_rep, place // n_rep, 0, 0)
 
     return pl.pallas_call(
-        functools.partial(backward_kernel, masks),
-        out_shape=[jax.ShapeDtypeStruct(shape, BF16) for shape in shapes],
+        backward_kernel,
+        out_shape=[jax.ShapeDtypeStruct((width, cols), BF16)] * count,
         grid_spec=pltpu.PrefetchScalarGridSpec(
             num_scalar_prefetch=1,
             grid=(count,),
-            in_specs=[fixed(width, rows), pl.BlockSpec((1, 1, rows, cols), a_block)]
-            + ([fixed(*term.shape)] if masks else []),
-            out_specs=[fixed(*shape) for shape in shapes],
+            in_specs=[fixed(width, rows), pl.BlockSpec((1, 1, rows, cols), a_block)],
+            out_specs=[fixed(width, cols)] * count,
         ),
         compiler_params=pltpu.CompilerParams(vmem_limit_bytes=36 * 2**20),
         cost_estimate=pl.CostEstimate(
@@ -366,25 +352,20 @@
             transcendentals=0,
             bytes_accessed=2 * count * rows * cols + 2 * count * width * cols + 2 * width * rows,
         ),
-    )(where, grad, in_hbm(dense), *([term] if masks else []))
+    )(where, grad, in_hbm(dense))
 
 
 def final_kernel(n_parts, where_ref, *refs):
     parts, terms = refs[:n_parts], refs[n_parts:-2]
     out_ref, weight_out = refs[-2:]
-    width = out_ref.shape[2]
-    total = functools.reduce(jnp.add, [part[:width].astype(F32) for part in parts])
+    total = functools.reduce(jnp.add, [part[...].astype(F32) for part in parts])
     out_ref[0] = total.T.astype(BF16)
-    _, extra, cols = terms[0].shape
-    quarter = extra * cols // width
-    for number, term_ref in enumerate(terms):
-        for other in range(term_ref.shape[0]):
-            place = (where_ref[0] ^ other) * 4 + ((where_ref[1] % 4) ^ number)
-            rows = pl.ds(pl.multiple_of(place * quarter, quarter), quarter)
-            for turn in range(width // cols):
-                weight_out[rows, turn * cols : (turn + 1) * cols] = term_ref[
-                    other, turn * quarter : (turn + 1) * quarter
-                ].astype(F32)
+    depth, size, _ = terms[0].shape
+    for other, term_ref in enumerate(terms):
+        for number in range(depth):
+            place = (where_ref[0] ^ other) * depth + ((where_ref[1] // 4) ^ number)
+            rows = pl.ds(pl.multiple_of(place * size, size), size)
+            weight_out[rows, :] = term_ref[number].astype(F32)
 
 
 def final_sum(where, parts, terms):
@@ -478,10 +459,6 @@
                 first, live.get("dense"), where, tile_values[0], packed, block_rows, n_rep
             )
 
-    def build_others(first):
-        with jax.named_scope("other_blocks"):
-            return [make_other(first, where, *sent, block_rows, n_rep) for sent in live["tiles"]]
-
     live[0] = lax.dynamic_slice_in_dim(features, rep * part, part, axis=0)
     with jax.named_scope("tiles_exchange"):
         live["tiles"] = [
@@ -500,9 +477,10 @@
         if pair == 0:
             build_own(0)
         if pair == 1:
-            two = build_others(panels // 2)
-            live["others"] = [half for halves in zip(live.pop("one"), two) for half in halves]
-            del live["tiles"]
+            with jax.named_scope("other_blocks"):
+                live["others"] = [
+                    make_other(where, *sent, block_rows, n_rep) for sent in live.pop("tiles")
+                ]
         close()
 
         with jax.named_scope("features_across"):
@@ -523,7 +501,6 @@
         units += [live[odd], live.pop("odd_x"), live.pop("odd_y")]
         if pair == 0:
             build_own(panels // 2)
-            live["one"] = build_others(0)
             live["waiting"] = units + crossed
             waiting = [("units", pair)]
         else:
@@ -540,25 +517,40 @@
             other = flip(partial, 0, 1 << bit)
 
     with jax.named_scope("middle"):
+        depth = n_section // 4
         rows = (partial, other, weight, live["cotangent"])
         grad, odd_diag, even_diag, term = middle(
-            where, offsets["first", pair_count - 1], *rows, live["dense"]
+            where, offsets["first", pair_count - 1], *rows, live["dense"], depth
         )
 
     live = {"grad": grad, "dense": live["dense"], "term": term}
     add = lambda *values: functools.reduce(jnp.add, [value.astype(F32) for value in values])
 
-    def backward_step(names, *carried):
+    def backward_step(names):
         with jax.named_scope("backward"):
             count = sum(2 if name[0] == "first" else 3 for name in names)
-            chunks = backward_part(
-                where, offsets[names[0]], count, live["grad"], live["dense"], *carried
-            )
+            chunks = backward_part(where, offsets[names[0]], count, live["grad"], live["dense"])
             for name in names:
                 size = 2 if name[0] == "first" else 3
                 live[name[0]], chunks = chunks[:size], chunks[size:]
 
-    z_masks = [1 << bit for bit in range(3, n_section.bit_length() - 1)]
+    def weight_step(phase, after=None):
+        if after:
+            live[after], live["term"] = lax.optimization_barrier((live[after], live["term"]))
+        term = live["term"]
+        with jax.named_scope("weight_grad"):
+            if phase == 0:
+                parts = [term[0], *(flip(term[n], Z * n) for n in range(1, depth))]
+                live["term"] = add(*parts).astype(BF16)
+            elif phase == 1:
+                parts = [term, *(flip(term, mask) for mask in (X, Y, X + Y))]
+                live["term"] = (add(*parts[:2]) + add(*parts[2:])).astype(BF16)
+            elif phase == 2:
+                live["term"] = [term, *(flip(term, Z * n) for n in range(1, depth))]
+            else:
+                term = jnp.stack(term)
+                live["terms"] = [term, *(flip(term, 0, n) for n in range(1, n_rep))]
+                del live["term"]
 
     live["first"] = [odd_diag, even_diag]
     for pair in reversed(range(pair_count)):
@@ -570,16 +562,16 @@
             odd_diag, even_diag = live.pop("first")
             live["odd_diag"], live["even_diag"] = flip(odd_diag, Y), flip(even_diag, X)
         if top:
-            backward_step([("odd", pair), ("even", pair)], (X, Y, 0), live.pop("term"))
+            backward_step([("odd", pair), ("even", pair)])
+            weight_step(0)
         else:
             with jax.named_scope("grads_along_z"):
                 mask = low_bit(even + 2 * Z)
                 target = even + 2 * Z - mask
                 live["to", target, mask] = flip(live.pop("passed"), mask)
                 passing = [("to", target, mask)]
-            if "activated" not in live:
-                with jax.named_scope("activated"):
-                    live["activated"] = activated_rows(where, *rows, n_rep)
+            if "term" in live:
+                weight_step(3)
         close(*passing)
 
         with jax.named_scope("grads_across"):
@@ -592,37 +584,29 @@
             following = live.pop("even")
             backward_step([("first", pair - 1), ("odd", pair - 1)])
             live["following"], live["even"] = live.pop("odd"), following
+            if top:
+                weight_step(1, "following")
         close()
 
-        with jax.named_scope("weight_grad"):
-            if not top and z_masks and mask == z_masks[0]:
-                z_masks.pop(0)
-                arrived = live["to", target, mask][width:]
-                live["weight"] = add(live["weight"], arrived).astype(BF16)
-            if pair == 0:
-                own = live.pop("weight")
-                own = jnp.stack([own, *(flip(own, 0, n) for n in range(1, n_rep))])
-                live["terms"] = [own, *(flip(own, m) for m in (X, Y, X + Y))]
         with jax.named_scope("grads_across"):
             to_x, to_y, own = live.pop("even")
             live["even_sum"] = [own, flip(to_x, X), flip(to_y, Y)]
         with jax.named_scope("grads_along_z"):
             odd_sum = add(*live.pop("odd_sum")).astype(BF16)
-            from_odd = flip(odd_sum, Z)
-            live["even_sum"].append(from_odd)
+            live["even_sum"].append(flip(odd_sum, Z))
+        if top:
+            weight_step(2)
         if pair > 0:
             backward_step([("even", pair - 1)])
             live["odd"] = live.pop("following")
-        if top:
-            with jax.named_scope("weight_grad"):
-                live["weight"] = add(odd_sum[width:], from_odd[width:]).astype(BF16)
+        else:
+            with jax.named_scope("activated"):
+                live["activated"] = activated_rows(where, *rows, n_rep)
         close()
         arrived = [name for name in live if isinstance(name, tuple) and name[1] == even]
         sums = [*live.pop("even_sum"), *(live.pop(name) for name in arrived)]
         if pair > 0:
-            live["passed"] = add(*(value[:width] for value in sums)).astype(BF16)
-            if z_masks and low_bit(even) == z_masks[0]:
-                live["passed"] = jnp.concatenate([live["passed"], live["weight"]])
+            live["passed"] = add(*sums).astype(BF16)
     with jax.named_scope("grads_out"):
         feat_grad, weight_grad = final_sum(where, sums, live["terms"])
     return (live["activated"], feat_grad, weight_grad)

time: 206 us -> 202 us (0.981)
  waiting for transfers between devices: 84.5 us -> 70.6 us
  starting transfers between devices: 39.2 us -> 49.5 us
    ppermute x38 -> x44, waiting for transfers between devices: 84.5 us -> 70.6 us  [flip(): return lax.ppermute(value, BOTH, pairs)]
    ppermute x38 -> x44, starting transfers between devices: 39.2 us -> 49.5 us  [flip(): return lax.ppermute(value, BOTH, pairs)]
    pallas_call x5 -> x4, Pallas kernels: 30.1 us -> 28.8 us  [the longest x3 19.1 us: backward_part(): pl.pallas_call(backward_kernel, out_shape=[jax.ShapeDtypeStruct((width, c...]
  transfers between devices with their start and end apart: 38 -> 44, of which waited for: 24 -> 22; matrix products, arithmetic and copies ran while one was open for 2% -> 2% of each run, Pallas kernels for 29% -> 29%
where the time goes in v8:
time: 202 us; the launch traced here: 200 us
  Pallas kernels  72 us (36%)
  waiting for transfers between devices  70.6 us (35%)
  starting transfers between devices  49.5 us (25%)
  other arithmetic  4.22 us (2%)
  local copies, waits for them, and re-layouts  3.11 us (2%)
    ppermute x44, waiting for transfers between devices, flip(): return lax.ppermute(value, BOTH, pairs)  70.6 us
    ppermute x44, starting transfers between devices, flip(): return lax.ppermute(value, BOTH, pairs)  49.5 us
    pallas_call x3, Pallas kernels, backward_part(): pl.pallas_call(backward_kernel, out_shape=[jax.ShapeDtypeStruct((width, c...  19.1 us
    pallas_call x3, Pallas kernels, forward_part(): pl.pallas_call(functools.partial(forward_kernel, offset, n_units, n_other...  17.8 us
    pallas_call x2, Pallas kernels, make_dense(): pl.pallas_call(functools.partial(dense_kernel, first), out_shape=pltpu.HB...  13.6 us
    pallas_call x1, Pallas kernels, make_other(): pl.pallas_call(other_kernel, out_shape=pltpu.HBM((panels, block_rows, par...  9.64 us
    pallas_call x1, Pallas kernels, middle(): pl.pallas_call(functools.partial(middle_kernel, blocks), out_shape=[jax.S...  7.88 us
  transfers between devices with their start and end apart: 44, of which 22 were waited for; matrix products, arithmetic and copies ran while one was open for 2% of the time, Pallas kernels for 29%

profile of v8, /device:TPU:0, one launch (start us, length us, event | category | flops | bytes accessed | tf_op | source)
XLA Modules:
  0.0 200.4 jit_solution(4352581381956746882)
XLA Ops:
  1.2 0.7 copy-done
  1.9 3.0 %collective-permute-start.2 = (bf16[512,512]{1,0:T(8,128)(2,1)S(1)}, bf16[512,512]{1,0:T(8,128)(2,1)S(1)}, u32[]{:S(2)}, u32[]{:S(2)}) collective-permute-start(bf16[512,512]{1,0:T(8,128)(2,1)S(1)} %constant_dynamic-slice_fusion.refs_1_), channel_id=1, source_target_pairs={{0,2},{1,3},{2,0},{3,1},{4,6},{5,7},{6,4},{7,5},{8,10},{9,11},{10,... | collective-permute-start | bytes 1572872 | tf_op jit(solution)/shard_map/features_across/ppermute | solution.py:412
  4.9 1.5 collective-permute-start.3
  6.4 1.6 collective-permute-start.4
  8.0 0.7 add_bitcast_fusion
  8.7 0.7 copy.12
  9.5 0.7 broadcast_xor_fusion
  10.3 6.9 %dense_blocks.2.refs_0_ = bf16[2,8,1024,512]{3,2,1,0:T(8,128)(2,1)} custom-call(s32[34]{0:T(128)S(1)} %pad_add_fusion.1.where_ref, s32[8,25]{1,0:T(8,128)S(1)} %pad_add_fusion.packed_ref, bf16[8,24,128,128]{3,2,1,0:T(8,128)(2,1)} %bitcast.20), custom_call_target="tpu_custom_call" | custom-call | bytes 393216 | tf_op jit(solution)/shard_map/dense_blocks/pallas_call | solution.py:42
  17.1 1.2 collective-permute-done.3.refs_3_
  18.3 1.2 collective-permute-done.4.refs_4_
  20.4 2.8 %collective-permute-start.7 = (bf16[512,512]{1,0:T(8,128)(2,1)S(1)}, bf16[512,512]{1,0:T(8,128)(2,1)S(1)}, u32[]{:S(2)}, u32[]{:S(2)}) collective-permute-start(bf16[512,512]{1,0:T(8,128)(2,1)S(1)} %constant_dynamic-slice_fusion.refs_1_), channel_id=1, source_target_pairs={{0,16},{1,17},{2,18},{3,19},{4,20},{5,21},{6,22},{7,23},{8,24},{9,... | collective-permute-start | bytes 1572872 | tf_op jit(solution)/shard_map/features_along_z/ppermute | solution.py:412
  23.2 8.5 %collective-permute-done.5.refs_5_ = bf16[512,512]{1,0:T(8,128)(2,1)S(1)} collective-permute-done((bf16[512,512]{1,0:T(8,128)(2,1)S(1)}, bf16[512,512]{1,0:T(8,128)(2,1)S(1)}, u32[]{:S(2)}, u32[]{:S(2)}) %collective-permute-start.5) | collective-permute-done | bytes 524320 | tf_op jit(solution)/shard_map/features_across/ppermute | solution.py:412
  32.1 0.6 collective-permute-start.8
  32.7 1.7 collective-permute-start.9
  34.4 6.7 %dense_blocks.3.dense_ref.a_ref = bf16[2,8,1024,512]{3,2,1,0:T(8,128)(2,1)} custom-call(s32[34]{0:T(128)S(1)} %pad_add_fusion.1.where_ref, s32[8,25]{1,0:T(8,128)S(1)} %pad_add_fusion.packed_ref, bf16[8,24,128,128]{3,2,1,0:T(8,128)(2,1)} %bitcast.21, bf16[2,8,1024,512]{3,2,1,0:T(8,128)(2,1)} %dense_blocks.2.refs_0_), custom_call_target="tpu_custom_call", output_to_operand_aliasing={{}: (3, {})} | custom-call | bytes 393216 | tf_op jit(solution)/shard_map/dense_blocks/pallas_call | solution.py:42
  41.2 3.4 %collective-permute-done.7.refs_1_ = bf16[512,512]{1,0:T(8,128)(2,1)S(1)} collective-permute-done((bf16[512,512]{1,0:T(8,128)(2,1)S(1)}, bf16[512,512]{1,0:T(8,128)(2,1)S(1)}, u32[]{:S(2)}, u32[]{:S(2)}) %collective-permute-start.7) | collective-permute-done | bytes 524320 | tf_op jit(solution)/shard_map/features_along_z/ppermute | solution.py:412
  44.6 0.8 copy-done.5
  45.4 0.8 copy-done.7
  46.2 1.7 collective-permute-start.10
  47.9 1.1 collective-permute-start.11
  48.9 0.7 collective-permute-start.12
  49.6 1.3 broadcast_select_fusion.1
  50.9 9.6 %other_blocks.1.refs_0_ = bf16[8,1024,512]{2,1,0:T(8,128)(2,1)} custom-call(s32[34]{0:T(128)S(1)} %pad_add_fusion.1.where_ref, s32[8,25]{1,0:T(8,128)S(1)} %collective-permute-done.1.packed_ref, bf16[8,24,128,128]{3,2,1,0:T(8,128)(2,1)} %collective-permute-done.tiles_ref), custom_call_target="tpu_custom_call" | custom-call | bytes 393216 | tf_op jit(solution)/shard_map/other_blocks/pallas_call | solution.py:86
  61.8 1.1 collective-permute-start.14
  62.9 7.8 %forward.3.refs_7_ = f32[1024,512]{1,0:T(8,128)S(1)} custom-call(s32[34]{0:T(128)S(1)} %pad_add_fusion.1.where_ref, bf16[2,8,1024,512]{3,2,1,0:T(8,128)(2,1)} %dense_blocks.3.dense_ref.a_ref, bf16[8,1024,512]{2,1,0:T(8,128)(2,1)} %other_blocks.1.refs_0_, bf16[512,512]{1,0:T(8,128)(2,1)S(1)} %constant_dynamic-slice_fusion.refs_1_, ...), custom_call_target="tpu_custom_call" | custom-call | flops 4294967296 | bytes 12582912 | tf_op jit(solution)/shard_map/forward/pallas_call | solution.py:178
  70.8 3.2 %collective-permute-done.13.refs_5_ = bf16[512,512]{1,0:T(8,128)(2,1)S(1)} collective-permute-done((bf16[512,512]{1,0:T(8,128)(2,1)}, bf16[512,512]{1,0:T(8,128)(2,1)S(1)}, u32[]{:S(2)}, u32[]{:S(2)}) %collective-permute-start.13) | collective-permute-done | bytes 524320 | tf_op jit(solution)/shard_map/features_across/ppermute | solution.py:412
  74.4 1.6 collective-permute-start.16
  75.9 1.7 collective-permute-start.17
  77.6 6.5 %forward.4.refs_3_ = f32[1024,512]{1,0:T(8,128)S(1)} custom-call(s32[34]{0:T(128)S(1)} %pad_add_fusion.1.where_ref, bf16[2,8,1024,512]{3,2,1,0:T(8,128)(2,1)} %dense_blocks.3.dense_ref.a_ref, bf16[8,1024,512]{2,1,0:T(8,128)(2,1)} %other_blocks.1.refs_0_, bf16[512,512]{1,0:T(8,128)(2,1)S(1)} %collective-permute-done.7.refs_1_, ...), custom_call_target="tpu_custom_call" | custom-call | flops 3221225472 | bytes 10485760 | tf_op jit(solution)/shard_map/forward/pallas_call | solution.py:178
  84.2 2.4 %collective-permute-done.16.refs_1_ = bf16[512,512]{1,0:T(8,128)(2,1)S(1)} collective-permute-done((bf16[512,512]{1,0:T(8,128)(2,1)}, bf16[512,512]{1,0:T(8,128)(2,1)S(1)}, u32[]{:S(2)}, u32[]{:S(2)}) %collective-permute-start.16) | collective-permute-done | bytes 524320 | tf_op jit(solution)/shard_map/features_across/ppermute | solution.py:412
  86.5 1.3 collective-permute-done.17.refs_2_
  87.8 3.4 %forward.5.mine_ref = bf16[1024,512]{1,0:T(8,128)(2,1)S(1)} custom-call(s32[34]{0:T(128)S(1)} %pad_add_fusion.1.where_ref, bf16[2,8,1024,512]{3,2,1,0:T(8,128)(2,1)} %dense_blocks.3.dense_ref.a_ref, bf16[8,1024,512]{2,1,0:T(8,128)(2,1)} %other_blocks.1.refs_0_, bf16[512,512]{1,0:T(8,128)(2,1)S(1)} %collective-permute-done.16.refs_1_, ...), custom_call_target="tpu_custom_call" | custom-call | flops 1073741824 | bytes 6291456 | tf_op jit(solution)/shard_map/forward/pallas_call | solution.py:178
  91.3 2.6 %collective-permute-done.18.other_ref = bf16[1024,512]{1,0:T(8,128)(2,1)S(1)} collective-permute-done((bf16[1024,512]{1,0:T(8,128)(2,1)S(1)}, bf16[1024,512]{1,0:T(8,128)(2,1)S(1)}, u32[]{:S(2)}, u32[]{:S(2)}) %collective-permute-start.18) | collective-permute-done | bytes 1048608 | tf_op jit(solution)/shard_map/partial_sums/ppermute | solution.py:412
  93.9 7.9 %middle.1 = (bf16[512,1024]{1,0:T(8,128)(2,1)S(1)}, bf16[512,512]{1,0:T(8,128)(2,1)S(1)}, bf16[512,512]{1,0:T(8,128)(2,1)S(1)}, bf16[4,64,512]{2,1,0:T(8,128)(2,1)S(1)}) custom-call(s32[34]{0:T(128)S(1)} %pad_add_fusion.1.where_ref, bf16[1024,512]{1,0:T(8,128)(2,1)S(1)} %forward.5.mine_ref, bf16[1024,512]{1,0:T(8,128)(2,1)S(1)} %collective-permute-done.18.other_ref, ...), custom_call_target="tpu_custom_call" | custom-call | flops 2684354560 | bytes 6291456 | tf_op jit(solution)/shard_map/middle/pallas_call | solution.py:267
  102.4 1.5 collective-permute-start.23
  103.9 0.6 collective-permute-start.19
  104.4 3.4 %collective-permute-start.20 = (bf16[64,512]{1,0:T(8,128)(2,1)S(1)}, bf16[64,512]{1,0:T(8,128)(2,1)S(1)}, u32[]{:S(2)}, u32[]{:S(2)}) collective-permute-start(bf16[64,512]{1,0:T(8,128)(2,1)S(1)} %get-tuple-element.307), channel_id=1, source_target_pairs={{0,16},{1,17},{2,18},{3,19},{4,20},{5,21},{6,22},{7,23},{8,24},{9,... | collective-permute-start | bytes 196616 | tf_op jit(solution)/shard_map/weight_grad/ppermute | solution.py:412
  108.3 7.7 %backward.3 = (bf16[512,512]{1,0:T(8,128)(2,1)S(1)}, bf16[512,512]{1,0:T(8,128)(2,1)S(1)}, bf16[512,512]{1,0:T(8,128)(2,1)S(1)}, bf16[512,512]{1,0:T(8,128)(2,1)...) custom-call(s32[34]{0:T(128)S(1)} %pad_add_fusion.1.where_ref, ...), custom_call_target="tpu_custom_call" | custom-call | flops 3221225472 | bytes 10485760 | tf_op jit(solution)/shard_map/backward/pallas_call | solution.py:340
  116.2 1.5 collective-permute-start.27
  117.7 1.5 collective-permute-start.28
  119.3 6.7 %backward.4 = (bf16[512,512]{1,0:T(8,128)(2,1)S(1)}, bf16[512,512]{1,0:T(8,128)(2,1)S(1)}, bf16[512,512]{1,0:T(8,128)(2,1)S(1)}, bf16[512,512]{1,0:T(8,128)(2,1)S(1)}, bf16[512,512]{1,0:T(8,128)(2,1)S(1)}) custom-call(s32[34]{0:T(128)S(1)} %pad_add_fusion.1.where_ref, bf16[512,1024]{1,0:T(8,128)(2,1)S(1)} %get-tuple-element.241.grad_ref, ...), custom_call_target="tpu_custom_call" | custom-call | flops 2684354560 | bytes 8912896 | tf_op jit(solution)/shard_map/backward/pallas_call | solution.py:340
  126.0 0.7 collective-permute-start.24
  127.1 2.4 %collective-permute-start.26 = (bf16[64,512]{1,0:T(8,128)(2,1)S(1)}, bf16[64,512]{1,0:T(8,128)(2,1)S(1)}, u32[]{:S(2)}, u32[]{:S(2)}) collective-permute-start(bf16[64,512]{1,0:T(8,128)(2,1)S(1)} %fusion.2), channel_id=1, source_target_pairs={{0,6},{1,7},{2,4},{3,5},{4,2},{5,3},{6,0},{7,1},{8,14},{9,15},{10,... | collective-permute-start | bytes 196616 | tf_op jit(solution)/shard_map/weight_grad/ppermute | solution.py:412
  129.7 1.6 collective-permute-done.24
  131.3 1.9 collective-permute-done.25
  133.9 0.8 collective-permute-start.32
  134.8 0.9 collective-permute-start.33
  135.7 1.9 collective-permute-start.29
  137.6 2.3 %collective-permute-start.30 = (bf16[64,512]{1,0:T(8,128)(2,1)S(1)}, bf16[64,512]{1,0:T(8,128)(2,1)S(1)}, u32[]{:S(2)}, u32[]{:S(2)}) collective-permute-start(bf16[64,512]{1,0:T(8,128)(2,1)S(1)} %add_convert_fusion.7), channel_id=1, source_target_pairs={{0,16},{1,17},{2,18},{3,19},{4,20},{5,21},{6,22},{7,23},{8,24},{9,... | collective-permute-start | bytes 196616 | tf_op jit(solution)/shard_map/weight_grad/ppermute | solution.py:412
  140.0 7.6 %collective-permute-done.29 = bf16[64,512]{1,0:T(8,128)(2,1)S(1)} collective-permute-done((bf16[64,512]{1,0:T(8,128)(2,1)S(1)}, bf16[64,512]{1,0:T(8,128)(2,1)S(1)}, u32[]{:S(2)}, u32[]{:S(2)}) %collective-permute-start.29) | collective-permute-done | bytes 65568 | tf_op jit(solution)/shard_map/weight_grad/ppermute | solution.py:412
  147.6 2.9 %collective-permute-start.31 = (bf16[64,512]{1,0:T(8,128)(2,1)S(1)}, bf16[64,512]{1,0:T(8,128)(2,1)S(1)}, u32[]{:S(2)}, u32[]{:S(2)}) collective-permute-start(bf16[64,512]{1,0:T(8,128)(2,1)S(1)} %add_convert_fusion.7), channel_id=1, source_target_pairs={{0,24},{1,25},{2,26},{3,27},{4,28},{5,29},{6,30},{7,31},{8,16},{9,... | collective-permute-start | bytes 196616 | tf_op jit(solution)/shard_map/weight_grad/ppermute | solution.py:412
  150.5 4.8 %backward.5 = (bf16[512,512]{1,0:T(8,128)(2,1)S(1)}, bf16[512,512]{1,0:T(8,128)(2,1)S(1)}, bf16[512,512]{1,0:T(8,128)(2,1)S(1)}) custom-call(s32[34]{0:T(128)S(1)} %pad_add_fusion.1.where_ref, bf16[512,1024]{1,0:T(8,128)(2,1)S(1)} %get-tuple-element.241.grad_ref, bf16[2,8,1024,512]{3,2,1,0:T(8,128)(2,1)} %dense_blocks.3.dense_ref.a_ref), custom_call_target="tpu_custom_call" | custom-call | flops 1610612736 | bytes 5767168 | tf_op jit(solution)/shard_map/backward/pallas_call | solution.py:340
  155.3 1.0 collective-permute-start.36
  156.3 1.5 collective-permute-start.37
  158.3 1.1 collective-permute-done.38.refs_6_
  159.5 5.7 %collective-permute-done.36 = bf16[512,512]{1,0:T(8,128)(2,1)S(1)} collective-permute-done((bf16[512,512]{1,0:T(8,128)(2,1)S(1)}, bf16[512,512]{1,0:T(8,128)(2,1)S(1)}, u32[]{:S(2)}, u32[]{:S(2)}) %collective-permute-start.36) | collective-permute-done | bytes 524320 | tf_op jit(solution)/shard_map/grads_across/ppermute | solution.py:412
  165.1 2.8 %collective-permute-done.37 = bf16[512,512]{1,0:T(8,128)(2,1)S(1)} collective-permute-done((bf16[512,512]{1,0:T(8,128)(2,1)S(1)}, bf16[512,512]{1,0:T(8,128)(2,1)S(1)}, u32[]{:S(2)}, u32[]{:S(2)}) %collective-permute-start.37) | collective-permute-done | bytes 524320 | tf_op jit(solution)/shard_map/grads_across/ppermute | solution.py:412
  168.1 1.8 collective-permute-start.39
  170.2 13.5 %collective-permute-done.35.refs_4_ = bf16[512,512]{1,0:T(8,128)(2,1)S(1)} collective-permute-done((bf16[512,512]{1,0:T(8,128)(2,1)S(1)}, bf16[512,512]{1,0:T(8,128)(2,1)S(1)}, u32[]{:S(2)}, u32[]{:S(2)}) %collective-permute-start.35) | collective-permute-done | bytes 524320 | tf_op jit(solution)/shard_map/grads_along_z/ppermute | solution.py:412
  184.0 0.8 collective-permute-start.41
  184.7 0.8 collective-permute-start.42
  185.6 1.8 activated.1
  187.4 10.4 %collective-permute-done.43.refs_3_ = bf16[512,512]{1,0:T(8,128)(2,1)S(1)} collective-permute-done((bf16[512,512]{1,0:T(8,128)(2,1)S(1)}, bf16[512,512]{1,0:T(8,128)(2,1)S(1)}, u32[]{:S(2)}, u32[]{:S(2)}) %collective-permute-start.43) | collective-permute-done | bytes 524320 | tf_op jit(solution)/shard_map/grads_along_z/ppermute | solution.py:412
  198.3 2.1 %grads_out.1 = (bf16[1,512,512]{2,1,0:T(8,128)(2,1)}, f32[512,512]{1,0:T(8,128)}) custom-call(s32[34]{0:T(128)S(1)} %pad_add_fusion.1.where_ref, bf16[512,512]{1,0:T(8,128)(2,1)S(1)} %get-tuple-element.294.refs_0_, bf16[512,512]{1,0:T(8,128)(2,1)S(1)} %collective-permute-done.41.refs_1_, bf16[512,512]{1,0:T(8,128)(2,1)S(1)} %collective-permute-done.42.refs_2_, ...), custom_call_target="tpu_custom_call" | custom-call | flops 1310720 | bytes 3145728 | tf_op jit(solution)/shard_map/grads_out/pallas_call | solution.py:378
  (73 shorter events, 8.1 us)
Async XLA Ops:
  0.6 1.2 copy-start
  0.6 18.9 %collective-permute-start = (bf16[8,24,128,128]{3,2,1,0:T(8,128)(2,1)}, bf16[8,24,128,128]{3,2,1,0:T(8,128)(2,1)}, u32[]{:S(2)}, u32[]{:S(2)}) collective-permute-start(bf16[8,24,128,128]{3,2,1,0:T(8,128)(2,1)} %bitcast.19), channel_id=1, source_target_pairs={{0,1},{1,0},{2,3},{3,2},{4,5},{5,4},{6,7},{7,6},{8,9},{9,8},{10,11... | collective-permute-start | bytes 18874376 | tf_op jit(solution)/shard_map/tiles_exchange/ppermute | solution.py:412
  1.9 15.2 %collective-permute-start.2 = (bf16[512,512]{1,0:T(8,128)(2,1)S(1)}, bf16[512,512]{1,0:T(8,128)(2,1)S(1)}, u32[]{:S(2)}, u32[]{:S(2)}) collective-permute-start(bf16[512,512]{1,0:T(8,128)(2,1)S(1)} %constant_dynamic-slice_fusion.refs_1_), channel_id=1, source_target_pairs={{0,2},{1,3},{2,0},{3,1},{4,6},{5,7},{6,4},{7,5},{8,10},{9,11},{10,... | collective-permute-start | bytes 1572872 | tf_op jit(solution)/shard_map/features_across/ppermute | solution.py:412
  4.9 13.4 %collective-permute-start.3 = (bf16[512,512]{1,0:T(8,128)(2,1)S(1)}, bf16[512,512]{1,0:T(8,128)(2,1)S(1)}, u32[]{:S(2)}, u32[]{:S(2)}) collective-permute-start(bf16[512,512]{1,0:T(8,128)(2,1)S(1)} %constant_dynamic-slice_fusion.refs_1_), channel_id=1, source_target_pairs={{0,4},{1,5},{2,6},{3,7},{4,0},{5,1},{6,2},{7,3},{8,12},{9,13},{10,... | collective-permute-start | bytes 1572872 | tf_op jit(solution)/shard_map/features_across/ppermute | solution.py:412
  6.4 13.1 %collective-permute-start.4 = (bf16[512,512]{1,0:T(8,128)(2,1)S(1)}, bf16[512,512]{1,0:T(8,128)(2,1)S(1)}, u32[]{:S(2)}, u32[]{:S(2)}) collective-permute-start(bf16[512,512]{1,0:T(8,128)(2,1)S(1)} %constant_dynamic-slice_fusion.refs_1_), channel_id=1, source_target_pairs={{0,8},{1,9},{2,10},{3,11},{4,12},{5,13},{6,14},{7,15},{8,0},{9,1},... | collective-permute-start | bytes 1572872 | tf_op jit(solution)/shard_map/features_along_z/ppermute | solution.py:412
  9.5 7.6 %collective-permute-start.1 = (s32[8,25]{1,0:T(8,128)S(1)}, s32[8,25]{1,0:T(8,128)S(1)}, u32[]{:S(2)}, u32[]{:S(2)}) collective-permute-start(s32[8,25]{1,0:T(8,128)S(1)} %pad_add_fusion.packed_ref), channel_id=1, source_target_pairs={{0,1},{1,0},{2,3},{3,2},{4,5},{5,4},{6,7},{7,6},{8,9},{9,8},{10,11... | collective-permute-start | bytes 2408 | tf_op jit(solution)/shard_map/tiles_exchange/ppermute | solution.py:412
  19.5 12.2 %collective-permute-start.5 = (bf16[512,512]{1,0:T(8,128)(2,1)S(1)}, bf16[512,512]{1,0:T(8,128)(2,1)S(1)}, u32[]{:S(2)}, u32[]{:S(2)}) collective-permute-start(bf16[512,512]{1,0:T(8,128)(2,1)S(1)} %collective-permute-done.4.refs_4_), channel_id=1, source_target_pairs={{0,2},{1,3},{2,0},{3,1},{4,6},{5,7},{6,4},{7,5},{8,10},{9,11},{10,... | collective-permute-start | bytes 1572872 | tf_op jit(solution)/shard_map/features_across/ppermute | solution.py:412
  20.1 12.1 %collective-permute-start.6 = (bf16[512,512]{1,0:T(8,128)(2,1)S(1)}, bf16[512,512]{1,0:T(8,128)(2,1)S(1)}, u32[]{:S(2)}, u32[]{:S(2)}) collective-permute-start(bf16[512,512]{1,0:T(8,128)(2,1)S(1)} %collective-permute-done.4.refs_4_), channel_id=1, source_target_pairs={{0,4},{1,5},{2,6},{3,7},{4,0},{5,1},{6,2},{7,3},{8,12},{9,13},{10,... | collective-permute-start | bytes 1572872 | tf_op jit(solution)/shard_map/features_across/ppermute | solution.py:412
  20.4 24.2 %collective-permute-start.7 = (bf16[512,512]{1,0:T(8,128)(2,1)S(1)}, bf16[512,512]{1,0:T(8,128)(2,1)S(1)}, u32[]{:S(2)}, u32[]{:S(2)}) collective-permute-start(bf16[512,512]{1,0:T(8,128)(2,1)S(1)} %constant_dynamic-slice_fusion.refs_1_), channel_id=1, source_target_pairs={{0,16},{1,17},{2,18},{3,19},{4,20},{5,21},{6,22},{7,23},{8,24},{9,... | collective-permute-start | bytes 1572872 | tf_op jit(solution)/shard_map/features_along_z/ppermute | solution.py:412
  32.1 9.0 %copy-start.3 = (bf16[512,512]{1,0:T(8,128)(2,1)}, bf16[512,512]{1,0:T(8,128)(2,1)S(1)}, u32[]{:S(2)}) copy-start(bf16[512,512]{1,0:T(8,128)(2,1)S(1)} %collective-permute-done.6.refs_6_) | copy-start | bytes 1572868
  32.1 12.5 %collective-permute-start.8 = (bf16[512,512]{1,0:T(8,128)(2,1)S(1)}, bf16[512,512]{1,0:T(8,128)(2,1)S(1)}, u32[]{:S(2)}, u32[]{:S(2)}) collective-permute-start(bf16[512,512]{1,0:T(8,128)(2,1)S(1)} %collective-permute-done.2.refs_2_), channel_id=1, source_target_pairs={{0,4},{1,5},{2,6},{3,7},{4,0},{5,1},{6,2},{7,3},{8,12},{9,13},{10,... | collective-permute-start | bytes 1572872 | tf_op jit(solution)/shard_map/features_across/ppermute | solution.py:412
  32.7 12.7 %collective-permute-start.9 = (bf16[512,512]{1,0:T(8,128)(2,1)S(1)}, bf16[512,512]{1,0:T(8,128)(2,1)S(1)}, u32[]{:S(2)}, u32[]{:S(2)}) collective-permute-start(bf16[512,512]{1,0:T(8,128)(2,1)S(1)} %collective-permute-done.6.refs_6_), channel_id=1, source_target_pairs={{0,2},{1,3},{2,0},{3,1},{4,6},{5,7},{6,4},{7,5},{8,10},{9,11},{10,... | collective-permute-start | bytes 1572872 | tf_op jit(solution)/shard_map/features_across/ppermute | solution.py:412
  34.4 15.2 %collective-permute-start.15 = (bf16[512,512]{1,0:T(8,128)(2,1)}, bf16[512,512]{1,0:T(8,128)(2,1)}, u32[]{:S(2)}, u32[]{:S(2)}) collective-permute-start(bf16[512,512]{1,0:T(8,128)(2,1)} %param.14), channel_id=1, source_target_pairs={{0,1},{1,0},{2,3},{3,2},{4,5},{5,4},{6,7},{7,6},{8,9},{9,8},{10,11... | collective-permute-start | bytes 1572872 | tf_op jit(solution)/shard_map/cotangent_rows/ppermute | solution.py:412
  44.6 0.8 copy-start.5
  45.4 0.8 copy-start.7
  46.2 14.4 %collective-permute-start.10 = (bf16[512,512]{1,0:T(8,128)(2,1)S(1)}, bf16[512,512]{1,0:T(8,128)(2,1)}, u32[]{:S(2)}, u32[]{:S(2)}) collective-permute-start(bf16[512,512]{1,0:T(8,128)(2,1)S(1)} %collective-permute-done.7.refs_1_), channel_id=1, source_target_pairs={{0,2},{1,3},{2,0},{3,1},{4,6},{5,7},{6,4},{7,5},{8,10},{9,11},{10,... | collective-permute-start | bytes 1572872 | tf_op jit(solution)/shard_map/features_across/ppermute | solution.py:412
  47.9 13.0 %collective-permute-start.11 = (bf16[512,512]{1,0:T(8,128)(2,1)S(1)}, bf16[512,512]{1,0:T(8,128)(2,1)}, u32[]{:S(2)}, u32[]{:S(2)}) collective-permute-start(bf16[512,512]{1,0:T(8,128)(2,1)S(1)} %collective-permute-done.7.refs_1_), channel_id=1, source_target_pairs={{0,4},{1,5},{2,6},{3,7},{4,0},{5,1},{6,2},{7,3},{8,12},{9,13},{10,... | collective-permute-start | bytes 1572872 | tf_op jit(solution)/shard_map/features_across/ppermute | solution.py:412
  48.9 12.3 %collective-permute-start.12 = (bf16[512,512]{1,0:T(8,128)(2,1)S(1)}, bf16[512,512]{1,0:T(8,128)(2,1)}, u32[]{:S(2)}, u32[]{:S(2)}) collective-permute-start(bf16[512,512]{1,0:T(8,128)(2,1)S(1)} %collective-permute-done.7.refs_1_), channel_id=1, source_target_pairs={{0,8},{1,9},{2,10},{3,11},{4,12},{5,13},{6,14},{7,15},{8,0},{9,1},... | collective-permute-start | bytes 1572872 | tf_op jit(solution)/shard_map/features_along_z/ppermute | solution.py:412
  50.9 12.0 %copy-start.4 = (bf16[512,512]{1,0:T(8,128)(2,1)S(1)}, bf16[512,512]{1,0:T(8,128)(2,1)}, u32[]{:S(2)}) copy-start(bf16[512,512]{1,0:T(8,128)(2,1)} %copy-done.3) | copy-start | bytes 1572868
  50.9 12.0 %copy-start.6 = (bf16[512,512]{1,0:T(8,128)(2,1)S(1)}, bf16[512,512]{1,0:T(8,128)(2,1)}, u32[]{:S(2)}) copy-start(bf16[512,512]{1,0:T(8,128)(2,1)} %copy-done.5) | copy-start | bytes 1572868
  50.9 12.0 %copy-start.8 = (bf16[512,512]{1,0:T(8,128)(2,1)S(1)}, bf16[512,512]{1,0:T(8,128)(2,1)}, u32[]{:S(2)}) copy-start(bf16[512,512]{1,0:T(8,128)(2,1)} %copy-done.7) | copy-start | bytes 1572868
  61.3 12.7 %collective-permute-start.13 = (bf16[512,512]{1,0:T(8,128)(2,1)}, bf16[512,512]{1,0:T(8,128)(2,1)S(1)}, u32[]{:S(2)}, u32[]{:S(2)}) collective-permute-start(bf16[512,512]{1,0:T(8,128)(2,1)} %collective-permute-done.12.refs_4_), channel_id=1, source_target_pairs={{0,2},{1,3},{2,0},{3,1},{4,6},{5,7},{6,4},{7,5},{8,10},{9,11},{10,... | collective-permute-start | bytes 1572872 | tf_op jit(solution)/shard_map/features_across/ppermute | solution.py:412
  61.8 12.6 %collective-permute-start.14 = (bf16[512,512]{1,0:T(8,128)(2,1)}, bf16[512,512]{1,0:T(8,128)(2,1)S(1)}, u32[]{:S(2)}, u32[]{:S(2)}) collective-permute-start(bf16[512,512]{1,0:T(8,128)(2,1)} %collective-permute-done.12.refs_4_), channel_id=1, source_target_pairs={{0,4},{1,5},{2,6},{3,7},{4,0},{5,1},{6,2},{7,3},{8,12},{9,13},{10,... | collective-permute-start | bytes 1572872 | tf_op jit(solution)/shard_map/features_across/ppermute | solution.py:412
  74.4 12.1 %collective-permute-start.16 = (bf16[512,512]{1,0:T(8,128)(2,1)}, bf16[512,512]{1,0:T(8,128)(2,1)S(1)}, u32[]{:S(2)}, u32[]{:S(2)}) collective-permute-start(bf16[512,512]{1,0:T(8,128)(2,1)} %collective-permute-done.10.refs_2_), channel_id=1, source_target_pairs={{0,4},{1,5},{2,6},{3,7},{4,0},{5,1},{6,2},{7,3},{8,12},{9,13},{10,... | collective-permute-start | bytes 1572872 | tf_op jit(solution)/shard_map/features_across/ppermute | solution.py:412
  75.9 11.8 %collective-permute-start.17 = (bf16[512,512]{1,0:T(8,128)(2,1)S(1)}, bf16[512,512]{1,0:T(8,128)(2,1)S(1)}, u32[]{:S(2)}, u32[]{:S(2)}) collective-permute-start(bf16[512,512]{1,0:T(8,128)(2,1)S(1)} %collective-permute-done.14.refs_6_), channel_id=1, source_target_pairs={{0,2},{1,3},{2,0},{3,1},{4,6},{5,7},{6,4},{7,5},{8,10},{9,11},{10,... | collective-permute-start | bytes 1572872 | tf_op jit(solution)/shard_map/features_across/ppermute | solution.py:412
  84.2 9.8 %copy-start.2 = (bf16[512,512]{1,0:T(8,128)(2,1)S(1)}, bf16[512,512]{1,0:T(8,128)(2,1)}, u32[]{:S(2)}) copy-start(bf16[512,512]{1,0:T(8,128)(2,1)} %weight_ref.3) | copy-start | bytes 1572868
  91.2 2.7 %collective-permute-start.18 = (bf16[1024,512]{1,0:T(8,128)(2,1)S(1)}, bf16[1024,512]{1,0:T(8,128)(2,1)S(1)}, u32[]{:S(2)}, u32[]{:S(2)}) collective-permute-start(bf16[1024,512]{1,0:T(8,128)(2,1)S(1)} %forward.5.mine_ref), channel_id=1, source_target_pairs={{0,1},{1,0},{2,3},{3,2},{4,5},{5,4},{6,7},{7,6},{8,9},{9,8},{10,11... | collective-permute-start | bytes 3145736 | tf_op jit(solution)/shard_map/partial_sums/ppermute | solution.py:412
  101.8 14.2 %collective-permute-start.22 = (bf16[512,512]{1,0:T(8,128)(2,1)S(1)}, bf16[512,512]{1,0:T(8,128)(2,1)S(1)}, u32[]{:S(2)}, u32[]{:S(2)}) collective-permute-start(bf16[512,512]{1,0:T(8,128)(2,1)S(1)} %get-tuple-element.213), channel_id=1, source_target_pairs={{0,4},{1,5},{2,6},{3,7},{4,0},{5,1},{6,2},{7,3},{8,12},{9,13},{10,... | collective-permute-start | bytes 1572872 | tf_op jit(solution)/shard_map/grads_across/ppermute | solution.py:412
  102.4 13.7 %collective-permute-start.23 = (bf16[512,512]{1,0:T(8,128)(2,1)S(1)}, bf16[512,512]{1,0:T(8,128)(2,1)S(1)}, u32[]{:S(2)}, u32[]{:S(2)}) collective-permute-start(bf16[512,512]{1,0:T(8,128)(2,1)S(1)} %get-tuple-element.214), channel_id=1, source_target_pairs={{0,2},{1,3},{2,0},{3,1},{4,6},{5,7},{6,4},{7,5},{8,10},{9,11},{10,... | collective-permute-start | bytes 1572872 | tf_op jit(solution)/shard_map/grads_across/ppermute | solution.py:412
  103.9 12.1 %collective-permute-start.19 = (bf16[64,512]{1,0:T(8,128)(2,1)S(1)}, bf16[64,512]{1,0:T(8,128)(2,1)S(1)}, u32[]{:S(2)}, u32[]{:S(2)}) collective-permute-start(bf16[64,512]{1,0:T(8,128)(2,1)S(1)} %get-tuple-element.305), channel_id=1, source_target_pairs={{0,8},{1,9},{2,10},{3,11},{4,12},{5,13},{6,14},{7,15},{8,0},{9,1},... | collective-permute-start | bytes 196616 | tf_op jit(solution)/shard_map/weight_grad/ppermute | solution.py:412
  104.4 11.6 %collective-permute-start.20 = (bf16[64,512]{1,0:T(8,128)(2,1)S(1)}, bf16[64,512]{1,0:T(8,128)(2,1)S(1)}, u32[]{:S(2)}, u32[]{:S(2)}) collective-permute-start(bf16[64,512]{1,0:T(8,128)(2,1)S(1)} %get-tuple-element.307), channel_id=1, source_target_pairs={{0,16},{1,17},{2,18},{3,19},{4,20},{5,21},{6,22},{7,23},{8,24},{9,... | collective-permute-start | bytes 196616 | tf_op jit(solution)/shard_map/weight_grad/ppermute | solution.py:412
  107.8 8.2 %collective-permute-start.21 = (bf16[64,512]{1,0:T(8,128)(2,1)S(1)}, bf16[64,512]{1,0:T(8,128)(2,1)S(1)}, u32[]{:S(2)}, u32[]{:S(2)}) collective-permute-start(bf16[64,512]{1,0:T(8,128)(2,1)S(1)} %get-tuple-element.306), channel_id=1, source_target_pairs={{0,24},{1,25},{2,26},{3,27},{4,28},{5,29},{6,30},{7,31},{8,16},{9,... | collective-permute-start | bytes 196616 | tf_op jit(solution)/shard_map/weight_grad/ppermute | solution.py:412
  116.2 17.0 %collective-permute-start.27 = (bf16[512,512]{1,0:T(8,128)(2,1)S(1)}, bf16[512,512]{1,0:T(8,128)(2,1)S(1)}, u32[]{:S(2)}, u32[]{:S(2)}) collective-permute-start(bf16[512,512]{1,0:T(8,128)(2,1)S(1)} %add_convert_fusion.6), channel_id=1, source_target_pairs={{0,2},{1,3},{2,0},{3,1},{4,6},{5,7},{6,4},{7,5},{8,10},{9,11},{10,... | collective-permute-start | bytes 1572872 | tf_op jit(solution)/shard_map/grads_across/ppermute | solution.py:412
  117.7 15.5 %collective-permute-start.28 = (bf16[512,512]{1,0:T(8,128)(2,1)S(1)}, bf16[512,512]{1,0:T(8,128)(2,1)S(1)}, u32[]{:S(2)}, u32[]{:S(2)}) collective-permute-start(bf16[512,512]{1,0:T(8,128)(2,1)S(1)} %get-tuple-element.231), channel_id=1, source_target_pairs={{0,4},{1,5},{2,6},{3,7},{4,0},{5,1},{6,2},{7,3},{8,12},{9,13},{10,... | collective-permute-start | bytes 1572872 | tf_op jit(solution)/shard_map/grads_across/ppermute | solution.py:412
  126.0 5.3 %collective-permute-start.24 = (bf16[64,512]{1,0:T(8,128)(2,1)S(1)}, bf16[64,512]{1,0:T(8,128)(2,1)S(1)}, u32[]{:S(2)}, u32[]{:S(2)}) collective-permute-start(bf16[64,512]{1,0:T(8,128)(2,1)S(1)} %fusion.2), channel_id=1, source_target_pairs={{0,2},{1,3},{2,0},{3,1},{4,6},{5,7},{6,4},{7,5},{8,10},{9,11},{10,... | collective-permute-start | bytes 196616 | tf_op jit(solution)/shard_map/weight_grad/ppermute | solution.py:412
  126.6 6.6 %collective-permute-start.25 = (bf16[64,512]{1,0:T(8,128)(2,1)S(1)}, bf16[64,512]{1,0:T(8,128)(2,1)S(1)}, u32[]{:S(2)}, u32[]{:S(2)}) collective-permute-start(bf16[64,512]{1,0:T(8,128)(2,1)S(1)} %fusion.2), channel_id=1, source_target_pairs={{0,4},{1,5},{2,6},{3,7},{4,0},{5,1},{6,2},{7,3},{8,12},{9,13},{10,... | collective-permute-start | bytes 196616 | tf_op jit(solution)/shard_map/weight_grad/ppermute | solution.py:412
  127.1 6.1 %collective-permute-start.26 = (bf16[64,512]{1,0:T(8,128)(2,1)S(1)}, bf16[64,512]{1,0:T(8,128)(2,1)S(1)}, u32[]{:S(2)}, u32[]{:S(2)}) collective-permute-start(bf16[64,512]{1,0:T(8,128)(2,1)S(1)} %fusion.2), channel_id=1, source_target_pairs={{0,6},{1,7},{2,4},{3,5},{4,2},{5,3},{6,0},{7,1},{8,14},{9,15},{10,... | collective-permute-start | bytes 196616 | tf_op jit(solution)/shard_map/weight_grad/ppermute | solution.py:412
  133.5 21.8 %collective-permute-start.34 = (bf16[512,512]{1,0:T(8,128)(2,1)S(1)}, bf16[512,512]{1,0:T(8,128)(2,1)S(1)}, u32[]{:S(2)}, u32[]{:S(2)}) collective-permute-start(bf16[512,512]{1,0:T(8,128)(2,1)S(1)} %add_convert_fusion.4), channel_id=1, source_target_pairs={{0,8},{1,9},{2,10},{3,11},{4,12},{5,13},{6,14},{7,15},{8,0},{9,1},... | collective-permute-start | bytes 1572872 | tf_op jit(solution)/shard_map/grads_along_z/ppermute | solution.py:412
  133.9 21.4 %collective-permute-start.32 = (bf16[512,512]{1,0:T(8,128)(2,1)S(1)}, bf16[512,512]{1,0:T(8,128)(2,1)S(1)}, u32[]{:S(2)}, u32[]{:S(2)}) collective-permute-start(bf16[512,512]{1,0:T(8,128)(2,1)S(1)} %get-tuple-element.247), channel_id=1, source_target_pairs={{0,2},{1,3},{2,0},{3,1},{4,6},{5,7},{6,4},{7,5},{8,10},{9,11},{10,... | collective-permute-start | bytes 1572872 | tf_op jit(solution)/shard_map/grads_across/ppermute | solution.py:412
  134.8 20.6 %collective-permute-start.33 = (bf16[512,512]{1,0:T(8,128)(2,1)S(1)}, bf16[512,512]{1,0:T(8,128)(2,1)S(1)}, u32[]{:S(2)}, u32[]{:S(2)}) collective-permute-start(bf16[512,512]{1,0:T(8,128)(2,1)S(1)} %add_convert_fusion.5), channel_id=1, source_target_pairs={{0,4},{1,5},{2,6},{3,7},{4,0},{5,1},{6,2},{7,3},{8,12},{9,13},{10,... | collective-permute-start | bytes 1572872 | tf_op jit(solution)/shard_map/grads_across/ppermute | solution.py:412
  135.7 11.9 %collective-permute-start.29 = (bf16[64,512]{1,0:T(8,128)(2,1)S(1)}, bf16[64,512]{1,0:T(8,128)(2,1)S(1)}, u32[]{:S(2)}, u32[]{:S(2)}) collective-permute-start(bf16[64,512]{1,0:T(8,128)(2,1)S(1)} %add_convert_fusion.7), channel_id=1, source_target_pairs={{0,8},{1,9},{2,10},{3,11},{4,12},{5,13},{6,14},{7,15},{8,0},{9,1},... | collective-permute-start | bytes 196616 | tf_op jit(solution)/shard_map/weight_grad/ppermute | solution.py:412
  137.6 17.7 %collective-permute-start.30 = (bf16[64,512]{1,0:T(8,128)(2,1)S(1)}, bf16[64,512]{1,0:T(8,128)(2,1)S(1)}, u32[]{:S(2)}, u32[]{:S(2)}) collective-permute-start(bf16[64,512]{1,0:T(8,128)(2,1)S(1)} %add_convert_fusion.7), channel_id=1, source_target_pairs={{0,16},{1,17},{2,18},{3,19},{4,20},{5,21},{6,22},{7,23},{8,24},{9,... | collective-permute-start | bytes 196616 | tf_op jit(solution)/shard_map/weight_grad/ppermute | solution.py:412
  147.6 7.7 %collective-permute-start.31 = (bf16[64,512]{1,0:T(8,128)(2,1)S(1)}, bf16[64,512]{1,0:T(8,128)(2,1)S(1)}, u32[]{:S(2)}, u32[]{:S(2)}) collective-permute-start(bf16[64,512]{1,0:T(8,128)(2,1)S(1)} %add_convert_fusion.7), channel_id=1, source_target_pairs={{0,24},{1,25},{2,26},{3,27},{4,28},{5,29},{6,30},{7,31},{8,16},{9,... | collective-permute-start | bytes 196616 | tf_op jit(solution)/shard_map/weight_grad/ppermute | solution.py:412
  155.3 9.8 %collective-permute-start.36 = (bf16[512,512]{1,0:T(8,128)(2,1)S(1)}, bf16[512,512]{1,0:T(8,128)(2,1)S(1)}, u32[]{:S(2)}, u32[]{:S(2)}) collective-permute-start(bf16[512,512]{1,0:T(8,128)(2,1)S(1)} %get-tuple-element.268), channel_id=1, source_target_pairs={{0,4},{1,5},{2,6},{3,7},{4,0},{5,1},{6,2},{7,3},{8,12},{9,13},{10,... | collective-permute-start | bytes 1572872 | tf_op jit(solution)/shard_map/grads_across/ppermute | solution.py:412
  156.3 11.7 %collective-permute-start.37 = (bf16[512,512]{1,0:T(8,128)(2,1)S(1)}, bf16[512,512]{1,0:T(8,128)(2,1)S(1)}, u32[]{:S(2)}, u32[]{:S(2)}) collective-permute-start(bf16[512,512]{1,0:T(8,128)(2,1)S(1)} %get-tuple-element.269), channel_id=1, source_target_pairs={{0,2},{1,3},{2,0},{3,1},{4,6},{5,7},{6,4},{7,5},{8,10},{9,11},{10,... | collective-permute-start | bytes 1572872 | tf_op jit(solution)/shard_map/grads_across/ppermute | solution.py:412
  157.9 1.6 collective-permute-start.38
  157.9 42.5 %copy-start.1 = (bf16[1024,512]{1,0:T(8,128)(2,1)S(1)}, bf16[1024,512]{1,0:T(8,128)(2,1)}, u32[]{:S(2)}) copy-start(bf16[1024,512]{1,0:T(8,128)(2,1)} %param.8) | copy-start | bytes 3145732
  158.2 25.4 %collective-permute-start.35 = (bf16[512,512]{1,0:T(8,128)(2,1)S(1)}, bf16[512,512]{1,0:T(8,128)(2,1)S(1)}, u32[]{:S(2)}, u32[]{:S(2)}) collective-permute-start(bf16[512,512]{1,0:T(8,128)(2,1)S(1)} %add_convert_fusion.3), channel_id=1, source_target_pairs={{0,16},{1,17},{2,18},{3,19},{4,20},{5,21},{6,22},{7,23},{8,24},{9,... | collective-permute-start | bytes 1572872 | tf_op jit(solution)/shard_map/grads_along_z/ppermute | solution.py:412
  168.1 15.6 %collective-permute-start.39 = (bf16[512,512]{1,0:T(8,128)(2,1)S(1)}, bf16[512,512]{1,0:T(8,128)(2,1)S(1)}, u32[]{:S(2)}, u32[]{:S(2)}) collective-permute-start(bf16[512,512]{1,0:T(8,128)(2,1)S(1)} %add_convert_fusion.2), channel_id=1, source_target_pairs={{0,2},{1,3},{2,0},{3,1},{4,6},{5,7},{6,4},{7,5},{8,10},{9,11},{10,... | collective-permute-start | bytes 1572872 | tf_op jit(solution)/shard_map/grads_across/ppermute | solution.py:412
  169.9 13.7 %collective-permute-start.40 = (bf16[512,512]{1,0:T(8,128)(2,1)S(1)}, bf16[512,512]{1,0:T(8,128)(2,1)S(1)}, u32[]{:S(2)}, u32[]{:S(2)}) collective-permute-start(bf16[512,512]{1,0:T(8,128)(2,1)S(1)} %get-tuple-element.279), channel_id=1, source_target_pairs={{0,4},{1,5},{2,6},{3,7},{4,0},{5,1},{6,2},{7,3},{8,12},{9,13},{10,... | collective-permute-start | bytes 1572872 | tf_op jit(solution)/shard_map/grads_across/ppermute | solution.py:412
  183.9 14.0 %collective-permute-start.43 = (bf16[512,512]{1,0:T(8,128)(2,1)S(1)}, bf16[512,512]{1,0:T(8,128)(2,1)S(1)}, u32[]{:S(2)}, u32[]{:S(2)}) collective-permute-start(bf16[512,512]{1,0:T(8,128)(2,1)S(1)} %add_convert_fusion), channel_id=1, source_target_pairs={{0,8},{1,9},{2,10},{3,11},{4,12},{5,13},{6,14},{7,15},{8,0},{9,1},... | collective-permute-start | bytes 1572872 | tf_op jit(solution)/shard_map/grads_along_z/ppermute | solution.py:412
  184.0 14.0 %collective-permute-start.41 = (bf16[512,512]{1,0:T(8,128)(2,1)S(1)}, bf16[512,512]{1,0:T(8,128)(2,1)S(1)}, u32[]{:S(2)}, u32[]{:S(2)}) collective-permute-start(bf16[512,512]{1,0:T(8,128)(2,1)S(1)} %get-tuple-element.288), channel_id=1, source_target_pairs={{0,2},{1,3},{2,0},{3,1},{4,6},{5,7},{6,4},{7,5},{8,10},{9,11},{10,... | collective-permute-start | bytes 1572872 | tf_op jit(solution)/shard_map/grads_across/ppermute | solution.py:412
  184.7 13.6 %collective-permute-start.42 = (bf16[512,512]{1,0:T(8,128)(2,1)S(1)}, bf16[512,512]{1,0:T(8,128)(2,1)S(1)}, u32[]{:S(2)}, u32[]{:S(2)}) collective-permute-start(bf16[512,512]{1,0:T(8,128)(2,1)S(1)} %add_convert_fusion.1), channel_id=1, source_target_pairs={{0,4},{1,5},{2,6},{3,7},{4,0},{5,1},{6,2},{7,3},{8,12},{9,13},{10,... | collective-permute-start | bytes 1572872 | tf_op jit(solution)/shard_map/grads_across/ppermute | solution.py:412

commit v9 on v8

--- a/solution.py
+++ b/solution.py
@@ -355,33 +355,38 @@
     )(where, grad, in_hbm(dense))
 
 
-def final_kernel(n_parts, where_ref, *refs):
-    parts, terms = refs[:n_parts], refs[n_parts:-2]
+def final_kernel(n_parts, n_halves, z_order, where_ref, *refs):
+    parts, terms = refs[:n_parts], refs[n_parts + n_halves : -2]
+    halves = refs[n_parts : n_parts + n_halves]
     out_ref, weight_out = refs[-2:]
-    total = functools.reduce(jnp.add, [part[...].astype(F32) for part in parts])
+    values = [part[...].astype(F32) for part in parts]
+    for top, end in zip(halves[::2], halves[1::2]):
+        values.append(jnp.concatenate([top[...].astype(F32), end[...].astype(F32)]))
+    total = functools.reduce(jnp.add, values)
     out_ref[0] = total.T.astype(BF16)
     depth, size, _ = terms[0].shape
     for other, term_ref in enumerate(terms):
-        for number in range(depth):
-            place = (where_ref[0] ^ other) * depth + ((where_ref[1] // 4) ^ number)
+        for number, offset in enumerate(z_order):
+            place = (where_ref[0] ^ other) * depth + ((where_ref[1] // 4) ^ offset)
             rows = pl.ds(pl.multiple_of(place * size, size), size)
             weight_out[rows, :] = term_ref[number].astype(F32)
 
 
-def final_sum(where, parts, terms):
+def final_sum(where, parts, halves, terms, z_order):
     width, cols = parts[0].shape
+    halves = [half for pair in halves for half in pair]
     whole = lambda value: pl.BlockSpec(value.shape, lambda i, where: (0,) * value.ndim)
     outs = [
         jax.ShapeDtypeStruct((1, cols, width), BF16),
         jax.ShapeDtypeStruct((width, width), F32),
     ]
     return pl.pallas_call(
-        functools.partial(final_kernel, len(parts)),
+        functools.partial(final_kernel, len(parts), len(halves), z_order),
         out_shape=outs,
         grid_spec=pltpu.PrefetchScalarGridSpec(
             num_scalar_prefetch=1,
             grid=(1,),
-            in_specs=[whole(value) for value in [*parts, *terms]],
+            in_specs=[whole(value) for value in [*parts, *halves, *terms]],
             out_specs=[whole(value) for value in outs],
         ),
         compiler_params=pltpu.CompilerParams(vmem_limit_bytes=36 * 2**20),
@@ -390,7 +395,7 @@
             transcendentals=0,
             bytes_accessed=2 * (len(parts) + 1) * width * cols,
         ),
-    )(where, *parts, *terms)
+    )(where, *parts, *halves, *terms)
 
 
 def shards(sizes, features, weight, tile_values, tile_rows, tile_cols, tile_count, cotangent):
@@ -490,9 +495,6 @@
                 live[later] = flip(live[later - low_bit(later)], low_bit(later))
         if pair > 0:
             live["total"] = forward_step(*waiting, live.pop("waiting"), live.get("total"))
-        if pair == 1:
-            with jax.named_scope("cotangent_rows"):
-                live["cotangent"] = gather_rep(cotangent)
         close(*([] if last else [later]))
 
         with jax.named_scope("features_across"):
@@ -507,6 +509,9 @@
             live["total"] = forward_step(("units", pair), units, live["total"])
             live["waiting"] = crossed
             waiting = [("crossed", pair)]
+        if last:
+            with jax.named_scope("cotangent_rows"):
+                live["cotangent"] = gather_rep(cotangent)
         close()
     partial = forward_step(*waiting, live["waiting"], live.get("total"), BF16)
 
@@ -533,6 +538,9 @@
             for name in names:
                 size = 2 if name[0] == "first" else 3
                 live[name[0]], chunks = chunks[:size], chunks[size:]
+
+    gather_masks = [Z << bit for bit in reversed(range(depth.bit_length() - 1))]
+    z_order = [0]
 
     def weight_step(phase, after=None):
         if after:
@@ -545,10 +553,13 @@
             elif phase == 1:
                 parts = [term, *(flip(term, mask) for mask in (X, Y, X + Y))]
                 live["term"] = (add(*parts[:2]) + add(*parts[2:])).astype(BF16)
-            elif phase == 2:
-                live["term"] = [term, *(flip(term, Z * n) for n in range(1, depth))]
+            elif gather_masks:
+                if term.ndim == 2:
+                    term = term[None]
+                mask = gather_masks.pop(0)
+                live["term"] = jnp.concatenate([term, flip(term, mask)])
+                z_order.extend([mask // Z ^ other for other in z_order])
             else:
-                term = jnp.stack(term)
                 live["terms"] = [term, *(flip(term, 0, n) for n in range(1, n_rep))]
                 del live["term"]
 
@@ -556,8 +567,6 @@
     for pair in reversed(range(pair_count)):
         even = 2 * pair * Z
         top = pair + 1 == pair_count
-        passing = [name for name in live if isinstance(name, tuple)]
-
         with jax.named_scope("grads_across"):
             odd_diag, even_diag = live.pop("first")
             live["odd_diag"], live["even_diag"] = flip(odd_diag, Y), flip(even_diag, X)
@@ -568,11 +577,10 @@
             with jax.named_scope("grads_along_z"):
                 mask = low_bit(even + 2 * Z)
                 target = even + 2 * Z - mask
-                live["to", target, mask] = flip(live.pop("passed"), mask)
-                passing = [("to", target, mask)]
+                live["to", target, mask] = [flip(live["passed"][0], mask)]
             if "term" in live:
                 weight_step(3)
-        close(*passing)
+        close()
 
         with jax.named_scope("grads_across"):
             to_x, to_y, own = live.pop("odd")
@@ -586,6 +594,11 @@
             live["following"], live["even"] = live.pop("odd"), following
             if top:
                 weight_step(1, "following")
+        if not top:
+            with jax.named_scope("grads_along_z"):
+                live["to", target, mask].append(flip(live.pop("passed")[1], mask))
+            if "term" in live:
+                weight_step(4)
         close()
 
         with jax.named_scope("grads_across"):
@@ -604,11 +617,15 @@
                 live["activated"] = activated_rows(where, *rows, n_rep)
         close()
         arrived = [name for name in live if isinstance(name, tuple) and name[1] == even]
-        sums = [*live.pop("even_sum"), *(live.pop(name) for name in arrived)]
+        sums = live.pop("even_sum")
+        halves = [live.pop(name) for name in arrived]
         if pair > 0:
-            live["passed"] = add(*sums).astype(BF16)
+            half = width // 2
+            tops = [value[:half] for value in sums] + [value[0] for value in halves]
+            ends = [value[half:] for value in sums] + [value[1] for value in halves]
+            live["passed"] = [add(*tops).astype(BF16), add(*ends).astype(BF16)]
     with jax.named_scope("grads_out"):
-        feat_grad, weight_grad = final_sum(where, sums, live["terms"])
+        feat_grad, weight_grad = final_sum(where, sums, halves, live["terms"], tuple(z_order))
     return (live["activated"], feat_grad, weight_grad)
 
 

time: 202 us -> 191 us (0.946)
  waiting for transfers between devices: 70.6 us -> 52.9 us
  local copies, waits for them, and re-layouts: 3.11 us -> 7.02 us
  starting transfers between devices: 49.5 us -> 52.4 us
    ppermute x44, waiting for transfers between devices: 70.6 us -> 52.9 us  [flip(): return lax.ppermute(value, BOTH, pairs)]
    unnamed x18 -> x26, local copies, waits for them, and re-layouts: 2.33 us -> 6.24 us
    ppermute x44, starting transfers between devices: 49.5 us -> 52.4 us  [flip(): return lax.ppermute(value, BOTH, pairs)]
  transfers between devices with their start and end apart: 44 -> 44, of which waited for: 22 -> 20; matrix products, arithmetic and copies ran while one was open for 2% -> 2% of each run, Pallas kernels for 29% -> 31%
where the time goes in v9:
time: 191 us; the launch traced here: 190 us
  Pallas kernels  72.1 us (38%)
  waiting for transfers between devices  52.9 us (28%)
  starting transfers between devices  52.4 us (27%)
  local copies, waits for them, and re-layouts  7.02 us (4%)
  other arithmetic  4.24 us (2%)
    ppermute x44, waiting for transfers between devices, flip(): return lax.ppermute(value, BOTH, pairs)  52.9 us
    ppermute x44, starting transfers between devices, flip(): return lax.ppermute(value, BOTH, pairs)  52.4 us
    pallas_call x3, Pallas kernels, backward_part(): pl.pallas_call(backward_kernel, out_shape=[jax.ShapeDtypeStruct((width, c...  19.1 us
    pallas_call x3, Pallas kernels, forward_part(): pl.pallas_call(functools.partial(forward_kernel, offset, n_units, n_other...  17.9 us
    pallas_call x2, Pallas kernels, make_dense(): pl.pallas_call(functools.partial(dense_kernel, first), out_shape=pltpu.HB...  13.4 us
    pallas_call x1, Pallas kernels, make_other(): pl.pallas_call(other_kernel, out_shape=pltpu.HBM((panels, block_rows, par...  9.75 us
    pallas_call x1, Pallas kernels, middle(): pl.pallas_call(functools.partial(middle_kernel, blocks), out_shape=[jax.S...  7.88 us
    unnamed x26, local copies, waits for them, and re-layouts  6.24 us
  transfers between devices with their start and end apart: 44, of which 20 were waited for; matrix products, arithmetic and copies ran while one was open for 2% of the time, Pallas kernels for 31%

profile of v9, /device:TPU:0, one launch (start us, length us, event | category | flops | bytes accessed | tf_op | source)
XLA Modules:
  0.0 189.6 jit_solution(956837301456730664)
XLA Ops:
  1.9 3.0 %collective-permute-start.2 = (bf16[512,512]{1,0:T(8,128)(2,1)S(1)}, bf16[512,512]{1,0:T(8,128)(2,1)S(1)}, u32[]{:S(2)}, u32[]{:S(2)}) collective-permute-start(bf16[512,512]{1,0:T(8,128)(2,1)S(1)} %constant_dynamic-slice_fusion.refs_1_), channel_id=1, source_target_pairs={{0,2},{1,3},{2,0},{3,1},{4,6},{5,7},{6,4},{7,5},{8,10},{9,11},{10,... | collective-permute-start | bytes 1572872 | tf_op jit(solution)/shard_map/features_across/ppermute | solution.py:417
  4.9 1.5 collective-permute-start.3
  6.4 1.6 collective-permute-start.4
  10.3 6.8 %dense_blocks.2.refs_0_ = bf16[2,8,1024,512]{3,2,1,0:T(8,128)(2,1)} custom-call(s32[34]{0:T(128)S(1)} %pad_add_fusion.1.where_ref, s32[8,25]{1,0:T(8,128)S(1)} %pad_add_fusion.packed_ref, bf16[8,24,128,128]{3,2,1,0:T(8,128)(2,1)} %bitcast.17), custom_call_target="tpu_custom_call" | custom-call | bytes 393216 | tf_op jit(solution)/shard_map/dense_blocks/pallas_call | solution.py:42
  17.1 1.2 collective-permute-done.3.refs_3_
  18.3 1.2 collective-permute-done.4.refs_4_
  20.4 2.8 %collective-permute-start.7 = (bf16[512,512]{1,0:T(8,128)(2,1)S(1)}, bf16[512,512]{1,0:T(8,128)(2,1)S(1)}, u32[]{:S(2)}, u32[]{:S(2)}) collective-permute-start(bf16[512,512]{1,0:T(8,128)(2,1)S(1)} %constant_dynamic-slice_fusion.refs_1_), channel_id=1, source_target_pairs={{0,16},{1,17},{2,18},{3,19},{4,20},{5,21},{6,22},{7,23},{8,24},{9,... | collective-permute-start | bytes 1572872 | tf_op jit(solution)/shard_map/features_along_z/ppermute | solution.py:417
  23.2 8.5 %collective-permute-done.5.refs_5_ = bf16[512,512]{1,0:T(8,128)(2,1)S(1)} collective-permute-done((bf16[512,512]{1,0:T(8,128)(2,1)S(1)}, bf16[512,512]{1,0:T(8,128)(2,1)S(1)}, u32[]{:S(2)}, u32[]{:S(2)}) %collective-permute-start.5) | collective-permute-done | bytes 524320 | tf_op jit(solution)/shard_map/features_across/ppermute | solution.py:417
  32.7 1.6 collective-permute-start.9
  34.3 6.6 %dense_blocks.3.dense_ref.a_ref = bf16[2,8,1024,512]{3,2,1,0:T(8,128)(2,1)} custom-call(s32[34]{0:T(128)S(1)} %pad_add_fusion.1.where_ref, s32[8,25]{1,0:T(8,128)S(1)} %pad_add_fusion.packed_ref, bf16[8,24,128,128]{3,2,1,0:T(8,128)(2,1)} %bitcast.18, bf16[2,8,1024,512]{3,2,1,0:T(8,128)(2,1)} %dense_blocks.2.refs_0_), custom_call_target="tpu_custom_call", output_to_operand_aliasing={{}: (3, {})} | custom-call | bytes 393216 | tf_op jit(solution)/shard_map/dense_blocks/pallas_call | solution.py:42
  40.9 3.8 %collective-permute-done.7.refs_1_ = bf16[512,512]{1,0:T(8,128)(2,1)S(1)} collective-permute-done((bf16[512,512]{1,0:T(8,128)(2,1)S(1)}, bf16[512,512]{1,0:T(8,128)(2,1)S(1)}, u32[]{:S(2)}, u32[]{:S(2)}) %collective-permute-start.7) | collective-permute-done | bytes 524320 | tf_op jit(solution)/shard_map/features_along_z/ppermute | solution.py:417
  44.7 0.8 copy-done.9
  45.5 0.8 copy-done.11
  46.3 1.4 collective-permute-start.10
  47.7 1.2 collective-permute-start.11
  49.6 9.8 %other_blocks.1.refs_0_ = bf16[8,1024,512]{2,1,0:T(8,128)(2,1)} custom-call(s32[34]{0:T(128)S(1)} %pad_add_fusion.1.where_ref, s32[8,25]{1,0:T(8,128)S(1)} %collective-permute-done.1.packed_ref, bf16[8,24,128,128]{3,2,1,0:T(8,128)(2,1)} %collective-permute-done.tiles_ref), custom_call_target="tpu_custom_call" | custom-call | bytes 393216 | tf_op jit(solution)/shard_map/other_blocks/pallas_call | solution.py:86
  59.4 1.1 collective-permute-done.11.refs_3_
  60.4 0.8 copy-done.7
  61.8 1.0 collective-permute-start.14
  62.8 1.0 copy-done.6
  63.9 1.0 copy-done.10
  64.9 1.0 copy-done.12
  66.0 7.8 %forward.3.refs_7_ = f32[1024,512]{1,0:T(8,128)S(1)} custom-call(s32[34]{0:T(128)S(1)} %pad_add_fusion.1.where_ref, bf16[2,8,1024,512]{3,2,1,0:T(8,128)(2,1)} %dense_blocks.3.dense_ref.a_ref, bf16[8,1024,512]{2,1,0:T(8,128)(2,1)} %other_blocks.1.refs_0_, bf16[512,512]{1,0:T(8,128)(2,1)S(1)} %constant_dynamic-slice_fusion.refs_1_, ...), custom_call_target="tpu_custom_call" | custom-call | flops 4294967296 | bytes 12582912 | tf_op jit(solution)/shard_map/forward/pallas_call | solution.py:178
  74.0 1.7 collective-permute-start.15
  75.7 1.7 collective-permute-start.16
  77.4 1.3 broadcast_select_fusion.1
  78.8 6.7 %forward.4.refs_3_ = f32[1024,512]{1,0:T(8,128)S(1)} custom-call(s32[34]{0:T(128)S(1)} %pad_add_fusion.1.where_ref, bf16[2,8,1024,512]{3,2,1,0:T(8,128)(2,1)} %dense_blocks.3.dense_ref.a_ref, bf16[8,1024,512]{2,1,0:T(8,128)(2,1)} %other_blocks.1.refs_0_, bf16[512,512]{1,0:T(8,128)(2,1)S(1)} %collective-permute-done.7.refs_1_, ...), custom_call_target="tpu_custom_call" | custom-call | flops 3221225472 | bytes 10485760 | tf_op jit(solution)/shard_map/forward/pallas_call | solution.py:178
  85.5 2.7 %collective-permute-done.15.refs_1_ = bf16[512,512]{1,0:T(8,128)(2,1)S(1)} collective-permute-done((bf16[512,512]{1,0:T(8,128)(2,1)S(1)}, bf16[512,512]{1,0:T(8,128)(2,1)S(1)}, u32[]{:S(2)}, u32[]{:S(2)}) %collective-permute-start.15) | collective-permute-done | bytes 524320 | tf_op jit(solution)/shard_map/features_across/ppermute | solution.py:417
  88.2 0.9 collective-permute-done.16.refs_2_
  89.1 3.4 %forward.5.mine_ref = bf16[1024,512]{1,0:T(8,128)(2,1)S(1)} custom-call(s32[34]{0:T(128)S(1)} %pad_add_fusion.1.where_ref, bf16[2,8,1024,512]{3,2,1,0:T(8,128)(2,1)} %dense_blocks.3.dense_ref.a_ref, bf16[8,1024,512]{2,1,0:T(8,128)(2,1)} %other_blocks.1.refs_0_, bf16[512,512]{1,0:T(8,128)(2,1)S(1)} %collective-permute-done.15.refs_1_, ...), custom_call_target="tpu_custom_call" | custom-call | flops 1073741824 | bytes 6291456 | tf_op jit(solution)/shard_map/forward/pallas_call | solution.py:178
  92.7 2.6 %collective-permute-done.18.other_ref = bf16[1024,512]{1,0:T(8,128)(2,1)S(1)} collective-permute-done((bf16[1024,512]{1,0:T(8,128)(2,1)S(1)}, bf16[1024,512]{1,0:T(8,128)(2,1)S(1)}, u32[]{:S(2)}, u32[]{:S(2)}) %collective-permute-start.18) | collective-permute-done | bytes 1048608 | tf_op jit(solution)/shard_map/partial_sums/ppermute | solution.py:417
  95.3 7.9 %middle.1 = (bf16[512,1024]{1,0:T(8,128)(2,1)S(1)}, bf16[512,512]{1,0:T(8,128)(2,1)S(1)}, bf16[512,512]{1,0:T(8,128)(2,1)S(1)}, bf16[4,64,512]{2,1,0:T(8,128)(2,1)S(1)}) custom-call(s32[34]{0:T(128)S(1)} %pad_add_fusion.1.where_ref, bf16[1024,512]{1,0:T(8,128)(2,1)S(1)} %forward.5.mine_ref, bf16[1024,512]{1,0:T(8,128)(2,1)S(1)} %collective-permute-done.18.other_ref, ...), custom_call_target="tpu_custom_call" | custom-call | flops 2684354560 | bytes 6291456 | tf_op jit(solution)/shard_map/middle/pallas_call | solution.py:267
  103.2 1.1 collective-permute-start.22
  104.3 1.5 collective-permute-start.23
  105.8 1.7 collective-permute-start.19
  107.5 3.4 %collective-permute-start.20 = (bf16[64,512]{1,0:T(8,128)(2,1)S(1)}, bf16[64,512]{1,0:T(8,128)(2,1)S(1)}, u32[]{:S(2)}, u32[]{:S(2)}) collective-permute-start(bf16[64,512]{1,0:T(8,128)(2,1)S(1)} %get-tuple-element.307), channel_id=1, source_target_pairs={{0,16},{1,17},{2,18},{3,19},{4,20},{5,21},{6,22},{7,23},{8,24},{9,... | collective-permute-start | bytes 196616 | tf_op jit(solution)/shard_map/weight_grad/ppermute | solution.py:417
  110.9 7.7 %backward.3 = (bf16[512,512]{1,0:T(8,128)(2,1)S(1)}, bf16[512,512]{1,0:T(8,128)(2,1)S(1)}, bf16[512,512]{1,0:T(8,128)(2,1)S(1)}, bf16[512,512]{1,0:T(8,128)(2,1)...) custom-call(s32[34]{0:T(128)S(1)} %pad_add_fusion.1.where_ref, ...), custom_call_target="tpu_custom_call" | custom-call | flops 3221225472 | bytes 10485760 | tf_op jit(solution)/shard_map/backward/pallas_call | solution.py:340
  118.8 1.0 collective-permute-start.27
  119.8 0.9 collective-permute-start.28
  120.7 6.7 %backward.4 = (bf16[512,512]{1,0:T(8,128)(2,1)S(1)}, bf16[512,512]{1,0:T(8,128)(2,1)S(1)}, bf16[512,512]{1,0:T(8,128)(2,1)S(1)}, bf16[512,512]{1,0:T(8,128)(2,1)S(1)}, bf16[512,512]{1,0:T(8,128)(2,1)S(1)}) custom-call(s32[34]{0:T(128)S(1)} %pad_add_fusion.1.where_ref, bf16[512,1024]{1,0:T(8,128)(2,1)S(1)} %get-tuple-element.239.grad_ref, ...), custom_call_target="tpu_custom_call" | custom-call | flops 2684354560 | bytes 8912896 | tf_op jit(solution)/shard_map/backward/pallas_call | solution.py:340
  127.4 1.4 collective-permute-start.24
  128.8 1.0 collective-permute-start.25
  129.7 1.2 collective-permute-start.26
  131.1 2.8 %collective-permute-done.24 = bf16[64,512]{1,0:T(8,128)(2,1)S(1)} collective-permute-done((bf16[64,512]{1,0:T(8,128)(2,1)S(1)}, bf16[64,512]{1,0:T(8,128)(2,1)S(1)}, u32[]{:S(2)}, u32[]{:S(2)}) %collective-permute-start.24) | collective-permute-done | bytes 65568 | tf_op jit(solution)/shard_map/weight_grad/ppermute | solution.py:417
  133.9 1.3 collective-permute-done.25
  135.5 1.6 collective-permute-start.32
  137.0 0.8 collective-permute-start.30
  137.8 1.0 collective-permute-start.31
  138.8 3.4 %collective-permute-start.29 = (bf16[1,64,512]{2,1,0:T(8,128)(2,1)S(1)}, bf16[1,64,512]{2,1,0:T(8,128)(2,1)S(1)}, u32[]{:S(2)}, u32[]{:S(2)}) collective-permute-start(bf16[1,64,512]{2,1,0:T(8,128)(2,1)S(1)} %bitcast.19), channel_id=1, source_target_pairs={{0,16},{1,17},{2,18},{3,19},{4,20},{5,21},{6,22},{7,23},{8,24},{9,... | collective-permute-start | bytes 196616 | tf_op jit(solution)/shard_map/weight_grad/ppermute | solution.py:417
  142.2 4.8 %backward.5 = (bf16[512,512]{1,0:T(8,128)(2,1)S(1)}, bf16[512,512]{1,0:T(8,128)(2,1)S(1)}, bf16[512,512]{1,0:T(8,128)(2,1)S(1)}) custom-call(s32[34]{0:T(128)S(1)} %pad_add_fusion.1.where_ref, bf16[512,1024]{1,0:T(8,128)(2,1)S(1)} %get-tuple-element.239.grad_ref, bf16[2,8,1024,512]{3,2,1,0:T(8,128)(2,1)} %dense_blocks.3.dense_ref.a_ref), custom_call_target="tpu_custom_call" | custom-call | flops 1610612736 | bytes 5767168 | tf_op jit(solution)/shard_map/backward/pallas_call | solution.py:340
  147.0 1.4 collective-permute-done.32
  148.4 1.4 collective-permute-done.31
  149.9 0.8 collective-permute-start.34
  151.7 3.3 %collective-permute-start.36 = (bf16[256,512]{1,0:T(8,128)(2,1)S(1)}, bf16[256,512]{1,0:T(8,128)(2,1)S(1)}, u32[]{:S(2)}, u32[]{:S(2)}) collective-permute-start(bf16[256,512]{1,0:T(8,128)(2,1)S(1)} %get-tuple-element.302), channel_id=1, source_target_pairs={{0,16},{1,17},{2,18},{3,19},{4,20},{5,21},{6,22},{7,23},{8,24},{9,... | collective-permute-start | bytes 786440 | tf_op jit(solution)/shard_map/grads_along_z/ppermute | solution.py:417
  155.5 4.7 %collective-permute-done.33 = bf16[2,64,512]{2,1,0:T(8,128)(2,1)S(1)} collective-permute-done((bf16[2,64,512]{2,1,0:T(8,128)(2,1)S(1)}, bf16[2,64,512]{2,1,0:T(8,128)(2,1)S(1)}, u32[]{:S(2)}, u32[]{:S(2)}) %collective-permute-start.33) | collective-permute-done | bytes 131104 | tf_op jit(solution)/shard_map/weight_grad/ppermute | solution.py:417
  160.3 2.1 %collective-permute-done.36.refs_4_ = bf16[256,512]{1,0:T(8,128)(2,1)S(1)} collective-permute-done((bf16[256,512]{1,0:T(8,128)(2,1)S(1)}, bf16[256,512]{1,0:T(8,128)(2,1)S(1)}, u32[]{:S(2)}, u32[]{:S(2)}) %collective-permute-start.36) | collective-permute-done | bytes 262176 | tf_op jit(solution)/shard_map/grads_along_z/ppermute | solution.py:417
  162.5 2.2 %collective-permute-start.38 = (bf16[512,512]{1,0:T(8,128)(2,1)S(1)}, bf16[512,512]{1,0:T(8,128)(2,1)S(1)}, u32[]{:S(2)}, u32[]{:S(2)}) collective-permute-start(bf16[512,512]{1,0:T(8,128)(2,1)S(1)} %add_convert_fusion.2), channel_id=1, source_target_pairs={{0,2},{1,3},{2,0},{3,1},{4,6},{5,7},{6,4},{7,5},{8,10},{9,11},{10,... | collective-permute-start | bytes 1572872 | tf_op jit(solution)/shard_map/grads_across/ppermute | solution.py:417
  164.7 1.6 collective-permute-start.39
  166.7 9.8 %collective-permute-done.37.refs_5_ = bf16[256,512]{1,0:T(8,128)(2,1)S(1)} collective-permute-done((bf16[256,512]{1,0:T(8,128)(2,1)S(1)}, bf16[256,512]{1,0:T(8,128)(2,1)S(1)}, u32[]{:S(2)}, u32[]{:S(2)}) %collective-permute-start.37) | collective-permute-done | bytes 262176 | tf_op jit(solution)/shard_map/grads_along_z/ppermute | solution.py:417
  176.9 1.1 collective-permute-start.41
  178.0 1.2 collective-permute-start.42
  179.2 1.8 activated.1
  181.1 5.5 %collective-permute-done.43.refs_3_ = bf16[512,512]{1,0:T(8,128)(2,1)S(1)} collective-permute-done((bf16[512,512]{1,0:T(8,128)(2,1)S(1)}, bf16[512,512]{1,0:T(8,128)(2,1)S(1)}, u32[]{:S(2)}, u32[]{:S(2)}) %collective-permute-start.43) | collective-permute-done | bytes 524320 | tf_op jit(solution)/shard_map/grads_along_z/ppermute | solution.py:417
  187.5 2.1 %grads_out.1 = (bf16[1,512,512]{2,1,0:T(8,128)(2,1)}, f32[512,512]{1,0:T(8,128)}) custom-call(s32[34]{0:T(128)S(1)} %pad_add_fusion.1.where_ref, bf16[512,512]{1,0:T(8,128)(2,1)S(1)} %get-tuple-element.291.refs_0_, bf16[512,512]{1,0:T(8,128)(2,1)S(1)} %collective-permute-done.41.refs_1_, bf16[512,512]{1,0:T(8,128)(2,1)S(1)} %collective-permute-done.42.refs_2_, ...), custom_call_target="tpu_custom_call" | custom-call | flops 1048576 | bytes 2621440 | tf_op jit(solution)/shard_map/grads_out/pallas_call | solution.py:383
  (82 shorter events, 11.0 us)
Async XLA Ops:
  0.6 1.2 copy-start
  0.6 18.9 %collective-permute-start = (bf16[8,24,128,128]{3,2,1,0:T(8,128)(2,1)}, bf16[8,24,128,128]{3,2,1,0:T(8,128)(2,1)}, u32[]{:S(2)}, u32[]{:S(2)}) collective-permute-start(bf16[8,24,128,128]{3,2,1,0:T(8,128)(2,1)} %bitcast.16), channel_id=1, source_target_pairs={{0,1},{1,0},{2,3},{3,2},{4,5},{5,4},{6,7},{7,6},{8,9},{9,8},{10,11... | collective-permute-start | bytes 18874376 | tf_op jit(solution)/shard_map/tiles_exchange/ppermute | solution.py:417
  1.9 15.2 %collective-permute-start.2 = (bf16[512,512]{1,0:T(8,128)(2,1)S(1)}, bf16[512,512]{1,0:T(8,128)(2,1)S(1)}, u32[]{:S(2)}, u32[]{:S(2)}) collective-permute-start(bf16[512,512]{1,0:T(8,128)(2,1)S(1)} %constant_dynamic-slice_fusion.refs_1_), channel_id=1, source_target_pairs={{0,2},{1,3},{2,0},{3,1},{4,6},{5,7},{6,4},{7,5},{8,10},{9,11},{10,... | collective-permute-start | bytes 1572872 | tf_op jit(solution)/shard_map/features_across/ppermute | solution.py:417
  4.9 13.4 %collective-permute-start.3 = (bf16[512,512]{1,0:T(8,128)(2,1)S(1)}, bf16[512,512]{1,0:T(8,128)(2,1)S(1)}, u32[]{:S(2)}, u32[]{:S(2)}) collective-permute-start(bf16[512,512]{1,0:T(8,128)(2,1)S(1)} %constant_dynamic-slice_fusion.refs_1_), channel_id=1, source_target_pairs={{0,4},{1,5},{2,6},{3,7},{4,0},{5,1},{6,2},{7,3},{8,12},{9,13},{10,... | collective-permute-start | bytes 1572872 | tf_op jit(solution)/shard_map/features_across/ppermute | solution.py:417
  6.4 13.1 %collective-permute-start.4 = (bf16[512,512]{1,0:T(8,128)(2,1)S(1)}, bf16[512,512]{1,0:T(8,128)(2,1)S(1)}, u32[]{:S(2)}, u32[]{:S(2)}) collective-permute-start(bf16[512,512]{1,0:T(8,128)(2,1)S(1)} %constant_dynamic-slice_fusion.refs_1_), channel_id=1, source_target_pairs={{0,8},{1,9},{2,10},{3,11},{4,12},{5,13},{6,14},{7,15},{8,0},{9,1},... | collective-permute-start | bytes 1572872 | tf_op jit(solution)/shard_map/features_along_z/ppermute | solution.py:417
  9.5 7.6 %collective-permute-start.1 = (s32[8,25]{1,0:T(8,128)S(1)}, s32[8,25]{1,0:T(8,128)S(1)}, u32[]{:S(2)}, u32[]{:S(2)}) collective-permute-start(s32[8,25]{1,0:T(8,128)S(1)} %pad_add_fusion.packed_ref), channel_id=1, source_target_pairs={{0,1},{1,0},{2,3},{3,2},{4,5},{5,4},{6,7},{7,6},{8,9},{9,8},{10,11... | collective-permute-start | bytes 2408 | tf_op jit(solution)/shard_map/tiles_exchange/ppermute | solution.py:417
  19.5 12.2 %collective-permute-start.5 = (bf16[512,512]{1,0:T(8,128)(2,1)S(1)}, bf16[512,512]{1,0:T(8,128)(2,1)S(1)}, u32[]{:S(2)}, u32[]{:S(2)}) collective-permute-start(bf16[512,512]{1,0:T(8,128)(2,1)S(1)} %collective-permute-done.4.refs_4_), channel_id=1, source_target_pairs={{0,2},{1,3},{2,0},{3,1},{4,6},{5,7},{6,4},{7,5},{8,10},{9,11},{10,... | collective-permute-start | bytes 1572872 | tf_op jit(solution)/shard_map/features_across/ppermute | solution.py:417
  20.1 12.1 %collective-permute-start.6 = (bf16[512,512]{1,0:T(8,128)(2,1)S(1)}, bf16[512,512]{1,0:T(8,128)(2,1)S(1)}, u32[]{:S(2)}, u32[]{:S(2)}) collective-permute-start(bf16[512,512]{1,0:T(8,128)(2,1)S(1)} %collective-permute-done.4.refs_4_), channel_id=1, source_target_pairs={{0,4},{1,5},{2,6},{3,7},{4,0},{5,1},{6,2},{7,3},{8,12},{9,13},{10,... | collective-permute-start | bytes 1572872 | tf_op jit(solution)/shard_map/features_across/ppermute | solution.py:417
  20.4 24.3 %collective-permute-start.7 = (bf16[512,512]{1,0:T(8,128)(2,1)S(1)}, bf16[512,512]{1,0:T(8,128)(2,1)S(1)}, u32[]{:S(2)}, u32[]{:S(2)}) collective-permute-start(bf16[512,512]{1,0:T(8,128)(2,1)S(1)} %constant_dynamic-slice_fusion.refs_1_), channel_id=1, source_target_pairs={{0,16},{1,17},{2,18},{3,19},{4,20},{5,21},{6,22},{7,23},{8,24},{9,... | collective-permute-start | bytes 1572872 | tf_op jit(solution)/shard_map/features_along_z/ppermute | solution.py:417
  32.1 8.7 %copy-start.5 = (bf16[512,512]{1,0:T(8,128)(2,1)}, bf16[512,512]{1,0:T(8,128)(2,1)S(1)}, u32[]{:S(2)}) copy-start(bf16[512,512]{1,0:T(8,128)(2,1)S(1)} %collective-permute-done.6.refs_6_) | copy-start | bytes 1572868
  32.1 12.6 %collective-permute-start.8 = (bf16[512,512]{1,0:T(8,128)(2,1)S(1)}, bf16[512,512]{1,0:T(8,128)(2,1)S(1)}, u32[]{:S(2)}, u32[]{:S(2)}) collective-permute-start(bf16[512,512]{1,0:T(8,128)(2,1)S(1)} %collective-permute-done.2.refs_2_), channel_id=1, source_target_pairs={{0,4},{1,5},{2,6},{3,7},{4,0},{5,1},{6,2},{7,3},{8,12},{9,13},{10,... | collective-permute-start | bytes 1572872 | tf_op jit(solution)/shard_map/features_across/ppermute | solution.py:417
  32.7 12.8 %collective-permute-start.9 = (bf16[512,512]{1,0:T(8,128)(2,1)S(1)}, bf16[512,512]{1,0:T(8,128)(2,1)S(1)}, u32[]{:S(2)}, u32[]{:S(2)}) collective-permute-start(bf16[512,512]{1,0:T(8,128)(2,1)S(1)} %collective-permute-done.6.refs_6_), channel_id=1, source_target_pairs={{0,2},{1,3},{2,0},{3,1},{4,6},{5,7},{6,4},{7,5},{8,10},{9,11},{10,... | collective-permute-start | bytes 1572872 | tf_op jit(solution)/shard_map/features_across/ppermute | solution.py:417
  44.7 0.8 copy-start.9
  45.5 0.8 copy-start.11
  46.3 13.1 %collective-permute-start.10 = (bf16[512,512]{1,0:T(8,128)(2,1)S(1)}, bf16[512,512]{1,0:T(8,128)(2,1)S(1)}, u32[]{:S(2)}, u32[]{:S(2)}) collective-permute-start(bf16[512,512]{1,0:T(8,128)(2,1)S(1)} %collective-permute-done.7.refs_1_), channel_id=1, source_target_pairs={{0,2},{1,3},{2,0},{3,1},{4,6},{5,7},{6,4},{7,5},{8,10},{9,11},{10,... | collective-permute-start | bytes 1572872 | tf_op jit(solution)/shard_map/features_across/ppermute | solution.py:417
  47.7 12.7 %collective-permute-start.11 = (bf16[512,512]{1,0:T(8,128)(2,1)S(1)}, bf16[512,512]{1,0:T(8,128)(2,1)S(1)}, u32[]{:S(2)}, u32[]{:S(2)}) collective-permute-start(bf16[512,512]{1,0:T(8,128)(2,1)S(1)} %collective-permute-done.7.refs_1_), channel_id=1, source_target_pairs={{0,4},{1,5},{2,6},{3,7},{4,0},{5,1},{6,2},{7,3},{8,12},{9,13},{10,... | collective-permute-start | bytes 1572872 | tf_op jit(solution)/shard_map/features_across/ppermute | solution.py:417
  48.9 12.3 %collective-permute-start.12 = (bf16[512,512]{1,0:T(8,128)(2,1)S(1)}, bf16[512,512]{1,0:T(8,128)(2,1)}, u32[]{:S(2)}, u32[]{:S(2)}) collective-permute-start(bf16[512,512]{1,0:T(8,128)(2,1)S(1)} %collective-permute-done.7.refs_1_), channel_id=1, source_target_pairs={{0,8},{1,9},{2,10},{3,11},{4,12},{5,13},{6,14},{7,15},{8,0},{9,1},... | collective-permute-start | bytes 1572872 | tf_op jit(solution)/shard_map/features_along_z/ppermute | solution.py:417
  59.4 1.9 copy-start.3
  60.4 0.8 copy-start.7
  61.3 12.5 %collective-permute-start.13 = (bf16[512,512]{1,0:T(8,128)(2,1)}, bf16[512,512]{1,0:T(8,128)(2,1)}, u32[]{:S(2)}, u32[]{:S(2)}) collective-permute-start(bf16[512,512]{1,0:T(8,128)(2,1)} %collective-permute-done.12.refs_4_), channel_id=1, source_target_pairs={{0,2},{1,3},{2,0},{3,1},{4,6},{5,7},{6,4},{7,5},{8,10},{9,11},{10,... | collective-permute-start | bytes 1572872 | tf_op jit(solution)/shard_map/features_across/ppermute | solution.py:417
  61.8 12.2 %collective-permute-start.14 = (bf16[512,512]{1,0:T(8,128)(2,1)}, bf16[512,512]{1,0:T(8,128)(2,1)}, u32[]{:S(2)}, u32[]{:S(2)}) collective-permute-start(bf16[512,512]{1,0:T(8,128)(2,1)} %collective-permute-done.12.refs_4_), channel_id=1, source_target_pairs={{0,4},{1,5},{2,6},{3,7},{4,0},{5,1},{6,2},{7,3},{8,12},{9,13},{10,... | collective-permute-start | bytes 1572872 | tf_op jit(solution)/shard_map/features_across/ppermute | solution.py:417
  62.8 14.6 %collective-permute-start.17 = (bf16[512,512]{1,0:T(8,128)(2,1)}, bf16[512,512]{1,0:T(8,128)(2,1)}, u32[]{:S(2)}, u32[]{:S(2)}) collective-permute-start(bf16[512,512]{1,0:T(8,128)(2,1)} %param.14), channel_id=1, source_target_pairs={{0,1},{1,0},{2,3},{3,2},{4,5},{5,4},{6,7},{7,6},{8,9},{9,8},{10,11... | collective-permute-start | bytes 1572872 | tf_op jit(solution)/shard_map/cotangent_rows/ppermute | solution.py:417
  62.8 1.0 copy-start.6
  63.9 1.0 copy-start.10
  64.9 1.0 copy-start.12
  66.0 8.0 %copy-start.4 = (bf16[512,512]{1,0:T(8,128)(2,1)S(1)}, bf16[512,512]{1,0:T(8,128)(2,1)}, u32[]{:S(2)}) copy-start(bf16[512,512]{1,0:T(8,128)(2,1)} %copy-done.3) | copy-start | bytes 1572868
  66.0 12.8 %copy-start.8 = (bf16[512,512]{1,0:T(8,128)(2,1)S(1)}, bf16[512,512]{1,0:T(8,128)(2,1)}, u32[]{:S(2)}) copy-start(bf16[512,512]{1,0:T(8,128)(2,1)} %copy-done.7) | copy-start | bytes 1572868
  74.0 14.3 %collective-permute-start.15 = (bf16[512,512]{1,0:T(8,128)(2,1)S(1)}, bf16[512,512]{1,0:T(8,128)(2,1)S(1)}, u32[]{:S(2)}, u32[]{:S(2)}) collective-permute-start(bf16[512,512]{1,0:T(8,128)(2,1)S(1)} %copy-done.4), channel_id=1, source_target_pairs={{0,4},{1,5},{2,6},{3,7},{4,0},{5,1},{6,2},{7,3},{8,12},{9,13},{10,... | collective-permute-start | bytes 1572872 | tf_op jit(solution)/shard_map/features_across/ppermute | solution.py:417
  75.7 13.4 %collective-permute-start.16 = (bf16[512,512]{1,0:T(8,128)(2,1)}, bf16[512,512]{1,0:T(8,128)(2,1)S(1)}, u32[]{:S(2)}, u32[]{:S(2)}) collective-permute-start(bf16[512,512]{1,0:T(8,128)(2,1)} %collective-permute-done.14.refs_6_), channel_id=1, source_target_pairs={{0,2},{1,3},{2,0},{3,1},{4,6},{5,7},{6,4},{7,5},{8,10},{9,11},{10,... | collective-permute-start | bytes 1572872 | tf_op jit(solution)/shard_map/features_across/ppermute | solution.py:417
  85.5 9.8 %copy-start.2 = (bf16[512,512]{1,0:T(8,128)(2,1)S(1)}, bf16[512,512]{1,0:T(8,128)(2,1)}, u32[]{:S(2)}) copy-start(bf16[512,512]{1,0:T(8,128)(2,1)} %weight_ref.3) | copy-start | bytes 1572868
  92.6 2.7 %collective-permute-start.18 = (bf16[1024,512]{1,0:T(8,128)(2,1)S(1)}, bf16[1024,512]{1,0:T(8,128)(2,1)S(1)}, u32[]{:S(2)}, u32[]{:S(2)}) collective-permute-start(bf16[1024,512]{1,0:T(8,128)(2,1)S(1)} %forward.5.mine_ref), channel_id=1, source_target_pairs={{0,1},{1,0},{2,3},{3,2},{4,5},{5,4},{6,7},{7,6},{8,9},{9,8},{10,11... | collective-permute-start | bytes 3145736 | tf_op jit(solution)/shard_map/partial_sums/ppermute | solution.py:417
  103.2 15.5 %collective-permute-start.22 = (bf16[512,512]{1,0:T(8,128)(2,1)S(1)}, bf16[512,512]{1,0:T(8,128)(2,1)S(1)}, u32[]{:S(2)}, u32[]{:S(2)}) collective-permute-start(bf16[512,512]{1,0:T(8,128)(2,1)S(1)} %get-tuple-element.211), channel_id=1, source_target_pairs={{0,4},{1,5},{2,6},{3,7},{4,0},{5,1},{6,2},{7,3},{8,12},{9,13},{10,... | collective-permute-start | bytes 1572872 | tf_op jit(solution)/shard_map/grads_across/ppermute | solution.py:417
  104.3 14.4 %collective-permute-start.23 = (bf16[512,512]{1,0:T(8,128)(2,1)S(1)}, bf16[512,512]{1,0:T(8,128)(2,1)S(1)}, u32[]{:S(2)}, u32[]{:S(2)}) collective-permute-start(bf16[512,512]{1,0:T(8,128)(2,1)S(1)} %get-tuple-element.212), channel_id=1, source_target_pairs={{0,2},{1,3},{2,0},{3,1},{4,6},{5,7},{6,4},{7,5},{8,10},{9,11},{10,... | collective-permute-start | bytes 1572872 | tf_op jit(solution)/shard_map/grads_across/ppermute | solution.py:417
  105.8 12.8 %collective-permute-start.19 = (bf16[64,512]{1,0:T(8,128)(2,1)S(1)}, bf16[64,512]{1,0:T(8,128)(2,1)S(1)}, u32[]{:S(2)}, u32[]{:S(2)}) collective-permute-start(bf16[64,512]{1,0:T(8,128)(2,1)S(1)} %get-tuple-element.305), channel_id=1, source_target_pairs={{0,8},{1,9},{2,10},{3,11},{4,12},{5,13},{6,14},{7,15},{8,0},{9,1},... | collective-permute-start | bytes 196616 | tf_op jit(solution)/shard_map/weight_grad/ppermute | solution.py:417
  107.5 11.1 %collective-permute-start.20 = (bf16[64,512]{1,0:T(8,128)(2,1)S(1)}, bf16[64,512]{1,0:T(8,128)(2,1)S(1)}, u32[]{:S(2)}, u32[]{:S(2)}) collective-permute-start(bf16[64,512]{1,0:T(8,128)(2,1)S(1)} %get-tuple-element.307), channel_id=1, source_target_pairs={{0,16},{1,17},{2,18},{3,19},{4,20},{5,21},{6,22},{7,23},{8,24},{9,... | collective-permute-start | bytes 196616 | tf_op jit(solution)/shard_map/weight_grad/ppermute | solution.py:417
  110.9 7.7 %collective-permute-start.21 = (bf16[64,512]{1,0:T(8,128)(2,1)S(1)}, bf16[64,512]{1,0:T(8,128)(2,1)S(1)}, u32[]{:S(2)}, u32[]{:S(2)}) collective-permute-start(bf16[64,512]{1,0:T(8,128)(2,1)S(1)} %get-tuple-element.306), channel_id=1, source_target_pairs={{0,24},{1,25},{2,26},{3,27},{4,28},{5,29},{6,30},{7,31},{8,16},{9,... | collective-permute-start | bytes 196616 | tf_op jit(solution)/shard_map/weight_grad/ppermute | solution.py:417
  118.8 16.4 %collective-permute-start.27 = (bf16[512,512]{1,0:T(8,128)(2,1)S(1)}, bf16[512,512]{1,0:T(8,128)(2,1)S(1)}, u32[]{:S(2)}, u32[]{:S(2)}) collective-permute-start(bf16[512,512]{1,0:T(8,128)(2,1)S(1)} %add_convert_fusion.5), channel_id=1, source_target_pairs={{0,2},{1,3},{2,0},{3,1},{4,6},{5,7},{6,4},{7,5},{8,10},{9,11},{10,... | collective-permute-start | bytes 1572872 | tf_op jit(solution)/shard_map/grads_across/ppermute | solution.py:417
  119.8 15.4 %collective-permute-start.28 = (bf16[512,512]{1,0:T(8,128)(2,1)S(1)}, bf16[512,512]{1,0:T(8,128)(2,1)S(1)}, u32[]{:S(2)}, u32[]{:S(2)}) collective-permute-start(bf16[512,512]{1,0:T(8,128)(2,1)S(1)} %get-tuple-element.229), channel_id=1, source_target_pairs={{0,4},{1,5},{2,6},{3,7},{4,0},{5,1},{6,2},{7,3},{8,12},{9,13},{10,... | collective-permute-start | bytes 1572872 | tf_op jit(solution)/shard_map/grads_across/ppermute | solution.py:417
  127.4 6.5 %collective-permute-start.24 = (bf16[64,512]{1,0:T(8,128)(2,1)S(1)}, bf16[64,512]{1,0:T(8,128)(2,1)S(1)}, u32[]{:S(2)}, u32[]{:S(2)}) collective-permute-start(bf16[64,512]{1,0:T(8,128)(2,1)S(1)} %fusion.2), channel_id=1, source_target_pairs={{0,2},{1,3},{2,0},{3,1},{4,6},{5,7},{6,4},{7,5},{8,10},{9,11},{10,... | collective-permute-start | bytes 196616 | tf_op jit(solution)/shard_map/weight_grad/ppermute | solution.py:417
  128.8 6.4 %collective-permute-start.25 = (bf16[64,512]{1,0:T(8,128)(2,1)S(1)}, bf16[64,512]{1,0:T(8,128)(2,1)S(1)}, u32[]{:S(2)}, u32[]{:S(2)}) collective-permute-start(bf16[64,512]{1,0:T(8,128)(2,1)S(1)} %fusion.2), channel_id=1, source_target_pairs={{0,4},{1,5},{2,6},{3,7},{4,0},{5,1},{6,2},{7,3},{8,12},{9,13},{10,... | collective-permute-start | bytes 196616 | tf_op jit(solution)/shard_map/weight_grad/ppermute | solution.py:417
  129.7 5.5 %collective-permute-start.26 = (bf16[64,512]{1,0:T(8,128)(2,1)S(1)}, bf16[64,512]{1,0:T(8,128)(2,1)S(1)}, u32[]{:S(2)}, u32[]{:S(2)}) collective-permute-start(bf16[64,512]{1,0:T(8,128)(2,1)S(1)} %fusion.2), channel_id=1, source_target_pairs={{0,6},{1,7},{2,4},{3,5},{4,2},{5,3},{6,0},{7,1},{8,14},{9,15},{10,... | collective-permute-start | bytes 196616 | tf_op jit(solution)/shard_map/weight_grad/ppermute | solution.py:417
  135.5 13.0 %collective-permute-start.32 = (bf16[512,512]{1,0:T(8,128)(2,1)S(1)}, bf16[512,512]{1,0:T(8,128)(2,1)S(1)}, u32[]{:S(2)}, u32[]{:S(2)}) collective-permute-start(bf16[512,512]{1,0:T(8,128)(2,1)S(1)} %add_convert_fusion.3), channel_id=1, source_target_pairs={{0,8},{1,9},{2,10},{3,11},{4,12},{5,13},{6,14},{7,15},{8,0},{9,1},... | collective-permute-start | bytes 1572872 | tf_op jit(solution)/shard_map/grads_along_z/ppermute | solution.py:417
  137.0 11.4 %collective-permute-start.30 = (bf16[512,512]{1,0:T(8,128)(2,1)S(1)}, bf16[512,512]{1,0:T(8,128)(2,1)S(1)}, u32[]{:S(2)}, u32[]{:S(2)}) collective-permute-start(bf16[512,512]{1,0:T(8,128)(2,1)S(1)} %get-tuple-element.245), channel_id=1, source_target_pairs={{0,2},{1,3},{2,0},{3,1},{4,6},{5,7},{6,4},{7,5},{8,10},{9,11},{10,... | collective-permute-start | bytes 1572872 | tf_op jit(solution)/shard_map/grads_across/ppermute | solution.py:417
  137.8 12.0 %collective-permute-start.31 = (bf16[512,512]{1,0:T(8,128)(2,1)S(1)}, bf16[512,512]{1,0:T(8,128)(2,1)S(1)}, u32[]{:S(2)}, u32[]{:S(2)}) collective-permute-start(bf16[512,512]{1,0:T(8,128)(2,1)S(1)} %add_convert_fusion.4), channel_id=1, source_target_pairs={{0,4},{1,5},{2,6},{3,7},{4,0},{5,1},{6,2},{7,3},{8,12},{9,13},{10,... | collective-permute-start | bytes 1572872 | tf_op jit(solution)/shard_map/grads_across/ppermute | solution.py:417
  138.8 8.2 %collective-permute-start.29 = (bf16[1,64,512]{2,1,0:T(8,128)(2,1)S(1)}, bf16[1,64,512]{2,1,0:T(8,128)(2,1)S(1)}, u32[]{:S(2)}, u32[]{:S(2)}) collective-permute-start(bf16[1,64,512]{2,1,0:T(8,128)(2,1)S(1)} %bitcast.19), channel_id=1, source_target_pairs={{0,16},{1,17},{2,18},{3,19},{4,20},{5,21},{6,22},{7,23},{8,24},{9,... | collective-permute-start | bytes 196616 | tf_op jit(solution)/shard_map/weight_grad/ppermute | solution.py:417
  149.9 12.5 %collective-permute-start.34 = (bf16[512,512]{1,0:T(8,128)(2,1)S(1)}, bf16[512,512]{1,0:T(8,128)(2,1)S(1)}, u32[]{:S(2)}, u32[]{:S(2)}) collective-permute-start(bf16[512,512]{1,0:T(8,128)(2,1)S(1)} %get-tuple-element.267), channel_id=1, source_target_pairs={{0,4},{1,5},{2,6},{3,7},{4,0},{5,1},{6,2},{7,3},{8,12},{9,13},{10,... | collective-permute-start | bytes 1572872 | tf_op jit(solution)/shard_map/grads_across/ppermute | solution.py:417
  150.7 11.7 %collective-permute-start.35 = (bf16[512,512]{1,0:T(8,128)(2,1)S(1)}, bf16[512,512]{1,0:T(8,128)(2,1)S(1)}, u32[]{:S(2)}, u32[]{:S(2)}) collective-permute-start(bf16[512,512]{1,0:T(8,128)(2,1)S(1)} %get-tuple-element.268), channel_id=1, source_target_pairs={{0,2},{1,3},{2,0},{3,1},{4,6},{5,7},{6,4},{7,5},{8,10},{9,11},{10,... | collective-permute-start | bytes 1572872 | tf_op jit(solution)/shard_map/grads_across/ppermute | solution.py:417
  151.7 10.7 %collective-permute-start.36 = (bf16[256,512]{1,0:T(8,128)(2,1)S(1)}, bf16[256,512]{1,0:T(8,128)(2,1)S(1)}, u32[]{:S(2)}, u32[]{:S(2)}) collective-permute-start(bf16[256,512]{1,0:T(8,128)(2,1)S(1)} %get-tuple-element.302), channel_id=1, source_target_pairs={{0,16},{1,17},{2,18},{3,19},{4,20},{5,21},{6,22},{7,23},{8,24},{9,... | collective-permute-start | bytes 786440 | tf_op jit(solution)/shard_map/grads_along_z/ppermute | solution.py:417
  154.9 5.3 %collective-permute-start.33 = (bf16[2,64,512]{2,1,0:T(8,128)(2,1)S(1)}, bf16[2,64,512]{2,1,0:T(8,128)(2,1)S(1)}, u32[]{:S(2)}, u32[]{:S(2)}) collective-permute-start(bf16[2,64,512]{2,1,0:T(8,128)(2,1)S(1)} %pad_maximum_fusion.2), channel_id=1, source_target_pairs={{0,8},{1,9},{2,10},{3,11},{4,12},{5,13},{6,14},{7,15},{8,0},{9,1},... | collective-permute-start | bytes 393224 | tf_op jit(solution)/shard_map/weight_grad/ppermute | solution.py:417
  162.4 27.2 %copy-start.1 = (bf16[1024,512]{1,0:T(8,128)(2,1)S(1)}, bf16[1024,512]{1,0:T(8,128)(2,1)}, u32[]{:S(2)}) copy-start(bf16[1024,512]{1,0:T(8,128)(2,1)} %param.8) | copy-start | bytes 3145732
  162.5 14.0 %collective-permute-start.38 = (bf16[512,512]{1,0:T(8,128)(2,1)S(1)}, bf16[512,512]{1,0:T(8,128)(2,1)S(1)}, u32[]{:S(2)}, u32[]{:S(2)}) collective-permute-start(bf16[512,512]{1,0:T(8,128)(2,1)S(1)} %add_convert_fusion.2), channel_id=1, source_target_pairs={{0,2},{1,3},{2,0},{3,1},{4,6},{5,7},{6,4},{7,5},{8,10},{9,11},{10,... | collective-permute-start | bytes 1572872 | tf_op jit(solution)/shard_map/grads_across/ppermute | solution.py:417
  164.7 11.8 %collective-permute-start.39 = (bf16[512,512]{1,0:T(8,128)(2,1)S(1)}, bf16[512,512]{1,0:T(8,128)(2,1)S(1)}, u32[]{:S(2)}, u32[]{:S(2)}) collective-permute-start(bf16[512,512]{1,0:T(8,128)(2,1)S(1)} %get-tuple-element.274), channel_id=1, source_target_pairs={{0,4},{1,5},{2,6},{3,7},{4,0},{5,1},{6,2},{7,3},{8,12},{9,13},{10,... | collective-permute-start | bytes 1572872 | tf_op jit(solution)/shard_map/grads_across/ppermute | solution.py:417
  166.3 10.2 %collective-permute-start.37 = (bf16[256,512]{1,0:T(8,128)(2,1)S(1)}, bf16[256,512]{1,0:T(8,128)(2,1)S(1)}, u32[]{:S(2)}, u32[]{:S(2)}) collective-permute-start(bf16[256,512]{1,0:T(8,128)(2,1)S(1)} %get-tuple-element.270), channel_id=1, source_target_pairs={{0,16},{1,17},{2,18},{3,19},{4,20},{5,21},{6,22},{7,23},{8,24},{9,... | collective-permute-start | bytes 786440 | tf_op jit(solution)/shard_map/grads_along_z/ppermute | solution.py:417
  166.5 10.0 %collective-permute-start.40 = (bf16[4,64,512]{2,1,0:T(8,128)(2,1)S(1)}, bf16[4,64,512]{2,1,0:T(8,128)(2,1)S(1)}, u32[]{:S(2)}, u32[]{:S(2)}) collective-permute-start(bf16[4,64,512]{2,1,0:T(8,128)(2,1)S(1)} %pad_maximum_fusion.1.refs_6_), channel_id=1, source_target_pairs={{0,1},{1,0},{2,3},{3,2},{4,5},{5,4},{6,7},{7,6},{8,9},{9,8},{10,11... | collective-permute-start | bytes 786440 | tf_op jit(solution)/shard_map/weight_grad/ppermute | solution.py:417
  176.7 9.8 %collective-permute-start.43 = (bf16[512,512]{1,0:T(8,128)(2,1)S(1)}, bf16[512,512]{1,0:T(8,128)(2,1)S(1)}, u32[]{:S(2)}, u32[]{:S(2)}) collective-permute-start(bf16[512,512]{1,0:T(8,128)(2,1)S(1)} %add_convert_fusion), channel_id=1, source_target_pairs={{0,8},{1,9},{2,10},{3,11},{4,12},{5,13},{6,14},{7,15},{8,0},{9,1},... | collective-permute-start | bytes 1572872 | tf_op jit(solution)/shard_map/grads_along_z/ppermute | solution.py:417
  176.9 10.2 %collective-permute-start.41 = (bf16[512,512]{1,0:T(8,128)(2,1)S(1)}, bf16[512,512]{1,0:T(8,128)(2,1)S(1)}, u32[]{:S(2)}, u32[]{:S(2)}) collective-permute-start(bf16[512,512]{1,0:T(8,128)(2,1)S(1)} %get-tuple-element.285), channel_id=1, source_target_pairs={{0,2},{1,3},{2,0},{3,1},{4,6},{5,7},{6,4},{7,5},{8,10},{9,11},{10,... | collective-permute-start | bytes 1572872 | tf_op jit(solution)/shard_map/grads_across/ppermute | solution.py:417
  178.0 9.5 %collective-permute-start.42 = (bf16[512,512]{1,0:T(8,128)(2,1)S(1)}, bf16[512,512]{1,0:T(8,128)(2,1)S(1)}, u32[]{:S(2)}, u32[]{:S(2)}) collective-permute-start(bf16[512,512]{1,0:T(8,128)(2,1)S(1)} %add_convert_fusion.1), channel_id=1, source_target_pairs={{0,4},{1,5},{2,6},{3,7},{4,0},{5,1},{6,2},{7,3},{8,12},{9,13},{10,... | collective-permute-start | bytes 1572872 | tf_op jit(solution)/shard_map/grads_across/ppermute | solution.py:417

commit v10 on v9

--- a/solution.py
+++ b/solution.py
@@ -59,8 +59,8 @@
     )(where, packed, in_hbm(tiles), *([in_hbm(before)] if first else []))
 
 
-def other_kernel(where_ref, packed_ref, tiles_ref, out_ref):
-    panel = pl.program_id(0)
+def other_kernel(first, where_ref, packed_ref, tiles_ref, out_ref):
+    panel = first + pl.program_id(0)
     size, slots = tiles_ref.shape[-1], tiles_ref.shape[1]
     row_tiles, per_part = out_ref.shape[1] // size, out_ref.shape[2] // size
     out_ref[...] = jnp.zeros_like(out_ref)
@@ -80,16 +80,17 @@
     lax.fori_loop(0, packed_ref[panel, slots], add_tile, 0)
 
 
-def make_other(where, tiles, packed, block_rows, n_rep):
+def make_other(first, where, tiles, packed, block_rows, n_rep):
     panels, slots, size, _ = tiles.shape
+    half = panels // 2
     part = block_rows // n_rep
     return pl.pallas_call(
-        other_kernel,
-        out_shape=pltpu.HBM((panels, block_rows, part), BF16),
+        functools.partial(other_kernel, first),
+        out_shape=pltpu.HBM((half, block_rows, part), BF16),
         grid_spec=pltpu.PrefetchScalarGridSpec(
             num_scalar_prefetch=2,
-            grid=(panels,),
-            in_specs=[pl.BlockSpec((1, slots, size, size), lambda p, *_: (p, 0, 0, 0))],
+            grid=(half,),
+            in_specs=[pl.BlockSpec((1, slots, size, size), lambda p, *_: (first + p, 0, 0, 0))],
             out_specs=pl.BlockSpec((1, block_rows, part), lambda p, *_: (p, 0, 0)),
         ),
         compiler_params=pltpu.CompilerParams(vmem_limit_bytes=36 * 2**20),
@@ -99,27 +100,34 @@
     )(where, packed, tiles)
 
 
-def forward_kernel(offset, n_units, n_others, has_total, where_ref, dense_ref, *refs):
+def forward_kernel(offset, n_pieces, n_others, has_total, where_ref, dense_ref, *refs):
     others, refs = refs[:n_others], refs[n_others:]
-    units, refs = refs[:n_units], refs[n_units:]
+    units = []
+    for pieces in n_pieces:
+        tops, refs = refs[:pieces], refs[pieces:]
+        half = tops[0].shape[0] // (2 if pieces == 1 else 1)
+        units.append([tops[0].at[pl.ds(0, half)], tops[-1].at[pl.ds(half * (2 - pieces), half)]])
+    n_units = len(units)
     total_ref, refs = (refs[0], refs[1:]) if has_total else (None, refs)
     out_ref, sum_ref, a_buf, u_buf, sems, sum_sem = refs
     _, panels, _, part = dense_ref.shape
+    some = others[0].shape[0]
     rep = where_ref[0]
 
     def a_copy(source, slot, side):
         target = a_buf.at[slot, :, pl.ds(side * part, part)]
         return pltpu.make_async_copy(source, target, sems.at[0, slot, side])
 
-    def u_copy(source, slot, side):
-        target = u_buf.at[slot, pl.ds(side * part, part), :]
-        return pltpu.make_async_copy(source, target, sems.at[1, slot, side])
+    def u_copy(source, slot, side, piece):
+        half = part // 2
+        target = u_buf.at[slot, pl.ds(side * part + piece * half, half), :]
+        return pltpu.make_async_copy(source, target, sems.at[1 + piece, slot, side])
 
     def fetch(pair, slot):
         for side in range(2):
             place = where_ref[offset + 2 * pair + side]
             owner, panel = place // panels, place % panels
-            turn = (owner ^ rep) - 1
+            turn = ((owner ^ rep) - 1) * (panels // some) + panel // some
 
             @pl.when(owner == rep)
             def _():
@@ -129,13 +137,14 @@
 
                 @pl.when((owner != rep) & (turn == number))
                 def _():
-                    a_copy(other_ref.at[panel], slot, side).start()
+                    a_copy(other_ref.at[panel % some], slot, side).start()
 
             for number in range(side, n_units, 2):
 
                 @pl.when(pair == number // 2)
                 def _():
-                    u_copy(units[number], slot, side).start()
+                    for piece in range(2):
+                        u_copy(units[number][piece], slot, side, piece).start()
 
     pairs = n_units // 2
     fetch(0, 0)
@@ -155,7 +164,8 @@
 
         for side in range(2):
             a_copy(dense_ref.at[0, 0], slot, side).wait()
-            u_copy(units[0], slot, side).wait()
+            for piece in range(2):
+                u_copy(units[0][piece], slot, side, piece).wait()
         sum_ref[...] += jnp.dot(a_buf[slot], u_buf[slot], preferred_element_type=F32)
         return carry
 
@@ -169,25 +179,27 @@
 
 
 def forward_part(where, offset, units, total, dense, others, kind):
-    part, width = units[0].shape
-    rows = dense.shape[2]
+    _, _, rows, part = dense.shape
+    width = units[0].shape[1]
+    n_pieces = [len(unit) if isinstance(unit, list) else 1 for unit in units]
+    pieces = [piece for unit in units for piece in (unit if isinstance(unit, list) else [unit])]
     near = pl.BlockSpec(memory_space=pl.ANY)
     hbm = pl.BlockSpec(memory_space=pltpu.HBM)
     has_total = total is not None
     n_units, n_others = len(units), len(others)
     return pl.pallas_call(
-        functools.partial(forward_kernel, offset, n_units, n_others, has_total),
+        functools.partial(forward_kernel, offset, n_pieces, n_others, has_total),
         out_shape=jax.ShapeDtypeStruct((rows, width), kind),
         grid_spec=pltpu.PrefetchScalarGridSpec(
             num_scalar_prefetch=1,
             grid=(1,),
-            in_specs=[hbm] * (1 + n_others) + [near] * (n_units + has_total),
+            in_specs=[hbm] * (1 + n_others) + [near] * (len(pieces) + has_total),
             out_specs=near if kind == F32 else pl.BlockSpec((rows, width), lambda i, where: (0, 0)),
             scratch_shapes=[
                 pltpu.VMEM((rows, width), F32),
                 pltpu.VMEM((2, rows, 2 * part), BF16),
                 pltpu.VMEM((2, 2 * part, width), BF16),
-                pltpu.SemaphoreType.DMA((2, 2, 2)),
+                pltpu.SemaphoreType.DMA((3, 2, 2)),
                 pltpu.SemaphoreType.DMA,
             ],
         ),
@@ -197,7 +209,7 @@
             transcendentals=0,
             bytes_accessed=n_units * rows * part * 2 + 8 * rows * width,
         ),
-    )(where, in_hbm(dense), *map(in_hbm, others), *units, *([total] if has_total else []))
+    )(where, in_hbm(dense), *map(in_hbm, others), *pieces, *([total] if has_total else []))
 
 
 def slopes(mine_ref, other_ref, weight_ref, cot_ref):
@@ -209,7 +221,7 @@
 
 
 def middle_kernel(blocks, where_ref, mine_ref, other_ref, weight_ref, cot_ref, a_ref, *refs):
-    grad_ref, odd_ref, even_ref, term_ref, sum_ref, full_ref = refs
+    grad_ref, top_ref, end_ref, term_ref, sum_ref, full_ref = refs
     step = pl.program_id(0)
     part = mine_ref.shape[0]
 
@@ -231,23 +243,18 @@
         def _():
             sum_ref[...] += term
 
-    @pl.when(step >= blocks)
+    @pl.when(step == blocks)
     def _():
         chunk = jnp.dot(full_ref[...], a_ref[0, 0], preferred_element_type=F32).astype(BF16)
-
-        @pl.when(step == blocks)
-        def _():
-            odd_ref[...] = chunk
-            depth, size, _ = term_ref.shape
-            z = where_ref[1] // 4
-            for number in range(depth):
-                start = (where_ref[0] * depth + (z ^ number)) * size
-                rows = sum_ref[pl.ds(pl.multiple_of(start, size), size), :]
-                term_ref[number] = rows.astype(BF16)
-
-        @pl.when(step > blocks)
-        def _():
-            even_ref[...] = chunk
+        half = top_ref.shape[0]
+        top_ref[...] = chunk[:half]
+        end_ref[...] = chunk[half:]
+        depth, size, _ = term_ref.shape
+        z = where_ref[1] // 4
+        for number in range(depth):
+            start = (where_ref[0] * depth + (z ^ number)) * size
+            rows = sum_ref[pl.ds(pl.multiple_of(start, size), size), :]
+            term_ref[number] = rows.astype(BF16)
 
 
 def middle(where, offset, mine, other, weight, cotangent, dense, depth):
@@ -258,10 +265,11 @@
     size = width // n_rep // depth
     block = pl.BlockSpec((part, width), lambda i, where: (jnp.minimum(i, blocks - 1), 0))
     fixed = lambda *shape: pl.BlockSpec(shape, lambda i, where: (0,) * len(shape))
-    shapes = [(width, rows), (width, cols), (width, cols), (depth, size, width)]
+    half = width // 2
+    shapes = [(width, rows), (half, cols), (half, cols), (depth, size, width)]
 
     def a_block(i, where):
-        place = where[offset + jnp.maximum(i - blocks, 0)]
+        place = where[offset]
         return (place % n_rep, place // n_rep, 0, 0)
 
     return pl.pallas_call(
@@ -269,7 +277,7 @@
         out_shape=[jax.ShapeDtypeStruct(shape, BF16) for shape in shapes],
         grid_spec=pltpu.PrefetchScalarGridSpec(
             num_scalar_prefetch=1,
-            grid=(blocks + 2,),
+            grid=(blocks + 1,),
             in_specs=[
                 block,
                 block,
@@ -353,6 +361,25 @@
             bytes_accessed=2 * count * rows * cols + 2 * count * width * cols + 2 * width * rows,
         ),
     )(where, grad, in_hbm(dense))
+
+
+def diagonals_kernel(y_ref, x_ref, top_ref, end_ref, y_out, x_out):
+    half = top_ref.shape[0]
+    y_out[:half] = (y_ref[:half].astype(F32) + top_ref[...].astype(F32)).astype(BF16)
+    y_out[half:] = y_ref[half:]
+    x_out[:half] = x_ref[:half]
+    x_out[half:] = (x_ref[half:].astype(F32) + end_ref[...].astype(F32)).astype(BF16)
+
+
+def add_diagonals(odd_y, odd_x, top, end):
+    return pl.pallas_call(
+        diagonals_kernel,
+        out_shape=[jax.ShapeDtypeStruct(odd_y.shape, BF16)] * 2,
+        compiler_params=pltpu.CompilerParams(vmem_limit_bytes=36 * 2**20),
+        cost_estimate=pl.CostEstimate(
+            flops=odd_y.size, transcendentals=0, bytes_accessed=10 * odd_y.size
+        ),
+    )(odd_y, odd_x, top, end)
 
 
 def final_kernel(n_parts, n_halves, z_order, where_ref, *refs):
@@ -438,11 +465,19 @@
 
     for pair in range(pair_count):
         even, odd = 2 * pair * Z, (2 * pair + 1) * Z
-        plan(("units", pair), [even, even + X, even + Y, odd, odd + X, odd + Y])
-        plan(("crossed", pair), [even + X + Y, odd + X + Y])
-        plan(("first", pair), [odd + X + Y, even + X + Y])
-        plan(("odd", pair), [odd + X, odd + Y, odd])
-        plan(("even", pair), [even + X, even + Y, even])
+        plan(("early", pair), [even, even + X, even + Y, odd])
+        plan(("more", pair), [even + X + Y, odd + Y])
+        plan(("late", pair), [odd + X, odd + X + Y])
+        if pair == 0:
+            plan(("first", pair), [odd + X + Y, even + X + Y])
+            plan(("odd", pair), [odd + X, odd + Y, odd])
+            plan(("even", pair), [even + X, even + Y, even])
+        else:
+            plan(("first", pair), [odd + X + Y])
+            plan(("mid", pair), [even + X + Y, odd + Y, odd + X])
+            plan(("last", pair), [even + X, even + Y, odd, even])
+    offsets["joined"] = 2 + len(masks)
+    masks += [0, X, Y, Z, Z + X, Z + Y, X + Y, Z + X + Y, 2 * Z, 2 * Z + X, 2 * Z + Y, 3 * Z]
     where = jnp.concatenate(
         [rep[None], section[None], section ^ jnp.array(masks, jnp.int32)]
     ).astype(jnp.int32)
@@ -464,12 +499,16 @@
                 first, live.get("dense"), where, tile_values[0], packed, block_rows, n_rep
             )
 
+    def build_others(first):
+        with jax.named_scope("other_blocks"):
+            return [make_other(first, where, *sent, block_rows, n_rep) for sent in live["tiles"]]
+
     live[0] = lax.dynamic_slice_in_dim(features, rep * part, part, axis=0)
     with jax.named_scope("tiles_exchange"):
         live["tiles"] = [
             (flip(tile_values[0], 0, n), flip(packed, 0, n)) for n in range(1, n_rep)
         ]
-    waiting = []
+    half = part // 2
     for pair in range(pair_count):
         even, odd = 2 * pair * Z, (2 * pair + 1) * Z
         later = even + 2 * Z
@@ -482,38 +521,60 @@
         if pair == 0:
             build_own(0)
         if pair == 1:
-            with jax.named_scope("other_blocks"):
-                live["others"] = [
-                    make_other(where, *sent, block_rows, n_rep) for sent in live.pop("tiles")
-                ]
+            two = build_others(panels // 2)
+            live["others"] = [side for sides in zip(live.pop("one"), two) for side in sides]
+            del live["tiles"]
+        if pair > 1:
+            live["total"] = forward_step(("late", pair - 1), live.pop("waiting"), live["total"])
         close()
 
-        with jax.named_scope("features_across"):
-            live["odd_x"], live["odd_y"] = flip(live[odd], X), flip(live[odd], Y)
+        if pair == 0:
+            with jax.named_scope("features_across"):
+                live["odd_x"], live["odd_y"] = flip(live[odd], X), flip(live[odd], Y)
+            build_own(panels // 2)
+        else:
+            with jax.named_scope("features_across"):
+                live["even_xy"], live["odd_y"] = flip(live["even_y"], X), flip(live[odd], Y)
+            with jax.named_scope("features_along_z"):
+                live["odd_x"] = flip(live["even_x"], Z)
+            units = [live[even], live["even_x"], live["even_y"], live[odd]]
+            if pair == 1:
+                live["total"] = forward_step("joined", live.pop("waiting") + units, None)
+            else:
+                live["total"] = forward_step(("early", pair), units, live["total"])
         if not last:
             with jax.named_scope("features_along_z"):
-                live[later] = flip(live[later - low_bit(later)], low_bit(later))
-        if pair > 0:
-            live["total"] = forward_step(*waiting, live.pop("waiting"), live.get("total"))
-        close(*([] if last else [later]))
-
-        with jax.named_scope("features_across"):
-            crossed = [flip(live["even_x"], Y), flip(live["odd_y"], X)]
-        units = [live[even], live.pop("even_x"), live.pop("even_y")]
-        units += [live[odd], live.pop("odd_x"), live.pop("odd_y")]
+                source, mask = live[later - low_bit(later)], low_bit(later)
+                live["coming"] = [flip(source[:half], mask)]
+        close()
+
         if pair == 0:
-            build_own(panels // 2)
-            live["waiting"] = units + crossed
-            waiting = [("units", pair)]
+            units = [live[even], live["even_x"], live["even_y"]]
+            units += [live[odd], live["odd_x"], live["odd_y"]]
+            with jax.named_scope("features_across"):
+                units += [flip(live["even_x"], Y), flip(live["odd_y"], X)]
+            live["waiting"] = units
+            live["one"] = build_others(0)
         else:
-            live["total"] = forward_step(("units", pair), units, live["total"])
-            live["waiting"] = crossed
-            waiting = [("crossed", pair)]
-        if last:
+            with jax.named_scope("features_across"):
+                odd_xy = [flip(live["odd_y"][:half], X), flip(live["odd_x"][half:], Y)]
+            live["waiting"] = [live["odd_x"], odd_xy]
+            units = [live.pop("even_xy"), live["odd_y"]]
+            live["total"] = forward_step(("more", pair), units, live["total"])
+        if not last:
+            with jax.named_scope("features_along_z"):
+                live["coming"].append(flip(source[half:], mask))
+        else:
             with jax.named_scope("cotangent_rows"):
                 live["cotangent"] = gather_rep(cotangent)
+        for name in ("even_x", "even_y", "odd_x", "odd_y"):
+            del live[name]
         close()
-    partial = forward_step(*waiting, live["waiting"], live.get("total"), BF16)
+        if not last:
+            live[later] = jnp.concatenate(live.pop("coming"))
+    partial = forward_step(
+        ("late", pair_count - 1), live.pop("waiting"), live.get("total"), BF16
+    )
 
     with jax.named_scope("partial_sums"):
         other = flip(partial, 0, 1)
@@ -524,106 +585,128 @@
     with jax.named_scope("middle"):
         depth = n_section // 4
         rows = (partial, other, weight, live["cotangent"])
-        grad, odd_diag, even_diag, term = middle(
+        grad, top_diag, end_diag, term = middle(
             where, offsets["first", pair_count - 1], *rows, live["dense"], depth
         )
 
     live = {"grad": grad, "dense": live["dense"], "term": term}
     add = lambda *values: functools.reduce(jnp.add, [value.astype(F32) for value in values])
 
-    def backward_step(names):
+    sizes_of = {"mid": 3, "last": 4, "odd": 3, "even": 3}
+
+    def backward_step(pair, *names):
         with jax.named_scope("backward"):
-            count = sum(2 if name[0] == "first" else 3 for name in names)
-            chunks = backward_part(where, offsets[names[0]], count, live["grad"], live["dense"])
-            for name in names:
-                size = 2 if name[0] == "first" else 3
-                live[name[0]], chunks = chunks[:size], chunks[size:]
-
-    gather_masks = [Z << bit for bit in reversed(range(depth.bit_length() - 1))]
+            counts = [sizes_of.get(name, 1 if pair else 2) for name in names]
+            chunks = backward_part(
+                where, offsets[names[0], pair], sum(counts), live["grad"], live["dense"]
+            )
+            for name, count in zip(names, counts):
+                live[name], chunks = chunks[:count], chunks[count:]
+
+    steps = ["along_z", X, Y, *(-(Z << bit) for bit in reversed(range(depth.bit_length() - 1)))]
+    steps.append("between_cores")
     z_order = [0]
 
-    def weight_step(phase, after=None):
+    def weight_step(after=None):
+        if not steps:
+            return
+        step = steps.pop(0)
         if after:
             live[after], live["term"] = lax.optimization_barrier((live[after], live["term"]))
         term = live["term"]
         with jax.named_scope("weight_grad"):
-            if phase == 0:
+            if step == "along_z":
                 parts = [term[0], *(flip(term[n], Z * n) for n in range(1, depth))]
                 live["term"] = add(*parts).astype(BF16)
-            elif phase == 1:
-                parts = [term, *(flip(term, mask) for mask in (X, Y, X + Y))]
-                live["term"] = (add(*parts[:2]) + add(*parts[2:])).astype(BF16)
-            elif gather_masks:
-                if term.ndim == 2:
-                    term = term[None]
-                mask = gather_masks.pop(0)
-                live["term"] = jnp.concatenate([term, flip(term, mask)])
-                z_order.extend([mask // Z ^ other for other in z_order])
-            else:
+            elif step == "between_cores":
                 live["terms"] = [term, *(flip(term, 0, n) for n in range(1, n_rep))]
                 del live["term"]
-
-    live["first"] = [odd_diag, even_diag]
+            elif step > 0:
+                live["term"] = add(term, flip(term, step)).astype(BF16)
+            else:
+                term = term[None] if term.ndim == 2 else term
+                live["term"] = jnp.concatenate([term, flip(term, -step)])
+                z_order.extend([-step // Z ^ other for other in z_order])
+
+    half = width // 2
+    tops = lambda values: [value[:half] for value in values]
+    ends = lambda values: [value[half:] for value in values]
+    live["first"] = [top_diag, end_diag]
     for pair in reversed(range(pair_count)):
         even = 2 * pair * Z
         top = pair + 1 == pair_count
+        if not top:
+            mask = low_bit(even + 2 * Z)
+            name = ("to", even + 2 * Z - mask, mask)
+
         with jax.named_scope("grads_across"):
-            odd_diag, even_diag = live.pop("first")
-            live["odd_diag"], live["even_diag"] = flip(odd_diag, Y), flip(even_diag, X)
-        if top:
-            backward_step([("odd", pair), ("even", pair)])
-            weight_step(0)
-        else:
-            with jax.named_scope("grads_along_z"):
-                mask = low_bit(even + 2 * Z)
-                target = even + 2 * Z - mask
-                live["to", target, mask] = [flip(live["passed"][0], mask)]
-            if "term" in live:
-                weight_step(3)
-        close()
-
-        with jax.named_scope("grads_across"):
-            to_x, to_y, own = live.pop("odd")
-            to_x = add(to_x, live.pop("odd_diag")).astype(BF16)
-            live["odd_sum"] = [own, flip(to_x, X), flip(to_y, Y)]
-            to_x, to_y, own = live.pop("even")
-            live["even"] = [to_x, add(to_y, live.pop("even_diag")).astype(BF16), own]
-        if pair > 0:
-            following = live.pop("even")
-            backward_step([("first", pair - 1), ("odd", pair - 1)])
-            live["following"], live["even"] = live.pop("odd"), following
-            if top:
-                weight_step(1, "following")
+            if pair == 0:
+                odd_diag, even_diag = live.pop("first")
+                live["odd_diag"], live["even_diag"] = flip(odd_diag, Y), flip(even_diag, X)
+            else:
+                top_diag, end_diag = live.pop("first")
+                live["top_diag"], live["end_diag"] = flip(top_diag, X), flip(end_diag, Y)
         if not top:
             with jax.named_scope("grads_along_z"):
-                live["to", target, mask].append(flip(live.pop("passed")[1], mask))
-            if "term" in live:
-                weight_step(4)
+                live[name] = [flip(live["passed"][0], mask)]
+        backward_step(pair, "even" if pair == 0 else "mid")
+        weight_step(None if top else "even" if pair == 0 else "mid")
         close()
 
-        with jax.named_scope("grads_across"):
-            to_x, to_y, own = live.pop("even")
-            live["even_sum"] = [own, flip(to_x, X), flip(to_y, Y)]
-        with jax.named_scope("grads_along_z"):
-            odd_sum = add(*live.pop("odd_sum")).astype(BF16)
-            live["even_sum"].append(flip(odd_sum, Z))
-        if top:
-            weight_step(2)
-        if pair > 0:
-            backward_step([("even", pair - 1)])
-            live["odd"] = live.pop("following")
+        if pair == 0:
+            with jax.named_scope("grads_across"):
+                to_x, to_y, own = live.pop("odd")
+                to_x = add(to_x, live.pop("odd_diag")).astype(BF16)
+                live["odd_sum"] = [own, flip(to_x, X), flip(to_y, Y)]
+                to_x, to_y, own = live.pop("even")
+                live["even"] = [to_x, add(to_y, live.pop("even_diag")).astype(BF16), own]
         else:
+            with jax.named_scope("grads_across"):
+                even_xy, odd_y, odd_x = live.pop("mid")
+                live["to_even_y"] = flip(even_xy, X)
+                odd_y, odd_x = add_diagonals(
+                    odd_y, odd_x, live.pop("top_diag"), live.pop("end_diag")
+                )
+                live["to_odd"] = flip(odd_y, Y)
+            with jax.named_scope("grads_along_z"):
+                live["to_even_x"] = flip(odd_x, Z)
+            backward_step(pair, "last")
+        if not top:
+            with jax.named_scope("grads_along_z"):
+                live[name].append(flip(live.pop("passed")[1], mask))
+        weight_step("last" if pair else None)
+        close()
+
+        if pair == 0:
+            with jax.named_scope("grads_across"):
+                to_x, to_y, own = live.pop("even")
+                sums = [own, flip(to_x, X), flip(to_y, Y)]
+            with jax.named_scope("grads_along_z"):
+                sums.append(flip(add(*live.pop("odd_sum")).astype(BF16), Z))
             with jax.named_scope("activated"):
                 live["activated"] = activated_rows(where, *rows, n_rep)
+        else:
+            to_x, to_y, odd, own = live.pop("last")
+            with jax.named_scope("grads_across"):
+                to_x = add(to_x, live.pop("to_even_x")).astype(BF16)
+                to_y = add(to_y, live.pop("to_even_y")).astype(BF16)
+                sums = [own, flip(to_x, X), flip(to_y, Y)]
+            with jax.named_scope("grads_along_z"):
+                sums.append(flip(add(odd, live.pop("to_odd")).astype(BF16), Z))
+            backward_step(pair - 1, "first", *([] if pair > 1 else ["odd"]))
+        live["sums"] = sums
+        weight_step("first" if pair else None)
         close()
-        arrived = [name for name in live if isinstance(name, tuple) and name[1] == even]
-        sums = live.pop("even_sum")
-        halves = [live.pop(name) for name in arrived]
+        sums = live.pop("sums")
+        halves = [live.pop(key) for key in list(live) if isinstance(key, tuple) and key[1] == even]
         if pair > 0:
-            half = width // 2
-            tops = [value[:half] for value in sums] + [value[0] for value in halves]
-            ends = [value[half:] for value in sums] + [value[1] for value in halves]
-            live["passed"] = [add(*tops).astype(BF16), add(*ends).astype(BF16)]
+            live["passed"] = [
+                add(*tops(sums), *(value[0] for value in halves)).astype(BF16),
+                add(*ends(sums), *(value[1] for value in halves)).astype(BF16),
+            ]
+        if pair > 1:
+            (chunk,) = live["first"]
+            live["first"] = [chunk[:half], chunk[half:]]
     with jax.named_scope("grads_out"):
         feat_grad, weight_grad = final_sum(where, sums, halves, live["terms"], tuple(z_order))
     return (live["activated"], feat_grad, weight_grad)

time: 191 us -> 186 us (0.974)
  starting transfers between devices: 52.4 us -> 45 us
  Pallas kernels: 72.1 us -> 77.8 us
  local copies, waits for them, and re-layouts: 7.02 us -> 1.82 us
    ppermute x44 -> x46, starting transfers between devices: 52.4 us -> 45 us  [flip(): return lax.ppermute(value, BOTH, pairs)]
    unnamed x26 -> x19, local copies, waits for them, and re-layouts: 6.24 us -> 0.95 us
    pallas_call x4 -> x6, Pallas kernels: 27.7 us -> 31.2 us  [the longest x3 18.1 us: forward_part(): pl.pallas_call(functools.partial(forward_kernel, offset, n_pieces, n_othe...]
    pallas_call x3 -> x4, Pallas kernels: 19.1 us -> 21.4 us  [backward_part(): pl.pallas_call(backward_kernel, out_shape=[jax.ShapeDtypeStruct((width, c...]
    ppermute x44 -> x46, waiting for transfers between devices: 52.9 us -> 54.4 us  [flip(): return lax.ppermute(value, BOTH, pairs)]
  transfers between devices with their start and end apart: 44 -> 46, of which waited for: 20 -> 19; matrix products, arithmetic and copies ran while one was open for 2% -> 3% of each run, Pallas kernels for 31% -> 36%
where the time goes in v10:
time: 186 us; the launch traced here: 184 us
  Pallas kernels  77.8 us (42%)
  waiting for transfers between devices  54.4 us (29%)
  starting transfers between devices  45 us (24%)
  other arithmetic  4.16 us (2%)
    ppermute x46, waiting for transfers between devices, flip(): return lax.ppermute(value, BOTH, pairs)  54.4 us
    ppermute x46, starting transfers between devices, flip(): return lax.ppermute(value, BOTH, pairs)  45 us
    pallas_call x4, Pallas kernels, backward_part(): pl.pallas_call(backward_kernel, out_shape=[jax.ShapeDtypeStruct((width, c...  21.4 us
    pallas_call x3, Pallas kernels, forward_part(): pl.pallas_call(functools.partial(forward_kernel, offset, n_pieces, n_othe...  18.1 us
    pallas_call x2, Pallas kernels, make_dense(): pl.pallas_call(functools.partial(dense_kernel, first), out_shape=pltpu.HB...  14.8 us
    pallas_call x2, Pallas kernels, make_other(): pl.pallas_call(functools.partial(other_kernel, first), out_shape=pltpu.HB...  12.9 us
    pallas_call x1, Pallas kernels, middle(): pl.pallas_call(functools.partial(middle_kernel, blocks), out_shape=[jax.S...  6.49 us
  transfers between devices with their start and end apart: 46, of which 19 were waited for; matrix products, arithmetic and copies ran while one was open for 3% of the time, Pallas kernels for 36%

profile of v10, /device:TPU:0, one launch (start us, length us, event | category | flops | bytes accessed | tf_op | source)
XLA Modules:
  0.0 184.2 jit_solution(12018094052921585152)
XLA Ops:
  1.2 0.7 copy-done
  1.9 3.0 %collective-permute-start.2 = (bf16[512,512]{1,0:T(8,128)(2,1)S(1)}, bf16[512,512]{1,0:T(8,128)(2,1)S(1)}, u32[]{:S(2)}, u32[]{:S(2)}) collective-permute-start(bf16[512,512]{1,0:T(8,128)(2,1)S(1)} %constant_dynamic-slice_fusion.refs_2_), channel_id=1, source_target_pairs={{0,2},{1,3},{2,0},{3,1},{4,6},{5,7},{6,4},{7,5},{8,10},{9,11},{10,... | collective-permute-start | bytes 1572872 | tf_op jit(solution)/shard_map/features_across/ppermute | solution.py:444
  4.9 1.5 collective-permute-start.3
  6.4 1.6 collective-permute-start.4
  8.0 0.7 add_bitcast_fusion
  8.7 0.7 copy.12
  10.3 7.4 %dense_blocks.2.refs_0_ = bf16[2,8,1024,512]{3,2,1,0:T(8,128)(2,1)} custom-call(s32[46]{0:T(128)S(1)} %pad_add_fusion.1.where_ref, s32[8,25]{1,0:T(8,128)S(1)} %pad_add_fusion.packed_ref, bf16[8,24,128,128]{3,2,1,0:T(8,128)(2,1)} %bitcast.17), custom_call_target="tpu_custom_call" | custom-call | bytes 393216 | tf_op jit(solution)/shard_map/dense_blocks/pallas_call | solution.py:42
  18.3 1.2 collective-permute-done.4.refs_5_
  20.4 2.8 %collective-permute-start.7 = (bf16[256,512]{1,0:T(8,128)(2,1)S(1)}, bf16[256,512]{1,0:T(8,128)(2,1)S(1)}, u32[]{:S(2)}, u32[]{:S(2)}) collective-permute-start(bf16[256,512]{1,0:T(8,128)(2,1)S(1)} %get-tuple-element.318), channel_id=1, source_target_pairs={{0,16},{1,17},{2,18},{3,19},{4,20},{5,21},{6,22},{7,23},{8,24},{9,... | collective-permute-start | bytes 786440 | tf_op jit(solution)/shard_map/features_along_z/ppermute | solution.py:444
  23.3 7.4 %dense_blocks.3.dense_ref.a_ref = bf16[2,8,1024,512]{3,2,1,0:T(8,128)(2,1)} custom-call(s32[46]{0:T(128)S(1)} %pad_add_fusion.1.where_ref, s32[8,25]{1,0:T(8,128)S(1)} %pad_add_fusion.packed_ref, bf16[8,24,128,128]{3,2,1,0:T(8,128)(2,1)} %bitcast.18, bf16[2,8,1024,512]{3,2,1,0:T(8,128)(2,1)} %dense_blocks.2.refs_0_), custom_call_target="tpu_custom_call", output_to_operand_aliasing={{}: (3, {})} | custom-call | bytes 393216 | tf_op jit(solution)/shard_map/dense_blocks/pallas_call | solution.py:42
  30.6 2.8 %collective-permute-done.7 = bf16[256,512]{1,0:T(8,128)(2,1)S(1)} collective-permute-done((bf16[256,512]{1,0:T(8,128)(2,1)S(1)}, bf16[256,512]{1,0:T(8,128)(2,1)S(1)}, u32[]{:S(2)}, u32[]{:S(2)}) %collective-permute-start.7) | collective-permute-done | bytes 262176 | tf_op jit(solution)/shard_map/features_along_z/ppermute | solution.py:444
  33.5 1.5 collective-permute-start.9
  35.0 1.5 collective-permute-start.10
  36.6 6.5 %other_blocks.2.refs_0_ = bf16[4,1024,512]{2,1,0:T(8,128)(2,1)} custom-call(s32[46]{0:T(128)S(1)} %pad_add_fusion.1.where_ref, s32[8,25]{1,0:T(8,128)S(1)} %collective-permute-done.1.packed_ref, bf16[8,24,128,128]{3,2,1,0:T(8,128)(2,1)} %collective-permute-done.tiles_ref), custom_call_target="tpu_custom_call" | custom-call | bytes 393216 | tf_op jit(solution)/shard_map/other_blocks/pallas_call | solution.py:87
  43.1 6.8 %collective-permute-done.8 = bf16[256,512]{1,0:T(8,128)(2,1)S(1)} collective-permute-done((bf16[256,512]{1,0:T(8,128)(2,1)S(1)}, bf16[256,512]{1,0:T(8,128)(2,1)S(1)}, u32[]{:S(2)}, u32[]{:S(2)}) %collective-permute-start.8) | collective-permute-done | bytes 262176 | tf_op jit(solution)/shard_map/features_along_z/ppermute | solution.py:444
  51.1 6.4 %other_blocks.3.refs_1_ = bf16[4,1024,512]{2,1,0:T(8,128)(2,1)} custom-call(s32[46]{0:T(128)S(1)} %pad_add_fusion.1.where_ref, s32[8,25]{1,0:T(8,128)S(1)} %collective-permute-done.1.packed_ref, bf16[8,24,128,128]{3,2,1,0:T(8,128)(2,1)} %collective-permute-done.tiles_ref), custom_call_target="tpu_custom_call" | custom-call | bytes 393216 | tf_op jit(solution)/shard_map/other_blocks/pallas_call | solution.py:87
  57.5 5.4 %collective-permute-done.11.refs_11_ = bf16[512,512]{1,0:T(8,128)(2,1)} collective-permute-done((bf16[512,512]{1,0:T(8,128)(2,1)S(1)}, bf16[512,512]{1,0:T(8,128)(2,1)}, u32[]{:S(2)}, u32[]{:S(2)}) %collective-permute-start.11) | collective-permute-done | bytes 524320 | tf_op jit(solution)/shard_map/features_across/ppermute | solution.py:444
  63.7 1.0 collective-permute-start.14
  64.7 1.7 collective-permute-start.15
  66.7 11.0 %forward.3.refs_4_ = f32[1024,512]{1,0:T(8,128)S(1)} custom-call(s32[46]{0:T(128)S(1)} %pad_add_fusion.1.where_ref, bf16[2,8,1024,512]{3,2,1,0:T(8,128)(2,1)} %dense_blocks.3.dense_ref.a_ref, bf16[4,1024,512]{2,1,0:T(8,128)(2,1)} %other_blocks.2.refs_0_, bf16[4,1024,512]{2,1,0:T(8,128)(2,1)} %other_blocks.3.refs_1_, ...), custom_call_target="tpu_custom_call" | custom-call | flops 6442450944 | bytes 16777216 | tf_op jit(solution)/shard_map/forward/pallas_call | solution.py:190
  77.8 1.0 collective-permute-start.17
  79.3 1.3 broadcast_select_fusion.1
  80.7 3.6 %forward.4.refs_5_ = f32[1024,512]{1,0:T(8,128)S(1)} custom-call(s32[46]{0:T(128)S(1)} %pad_add_fusion.1.where_ref, bf16[2,8,1024,512]{3,2,1,0:T(8,128)(2,1)} %dense_blocks.3.dense_ref.a_ref, bf16[4,1024,512]{2,1,0:T(8,128)(2,1)} %other_blocks.2.refs_0_, bf16[4,1024,512]{2,1,0:T(8,128)(2,1)} %other_blocks.3.refs_1_, ...), custom_call_target="tpu_custom_call" | custom-call | flops 1073741824 | bytes 6291456 | tf_op jit(solution)/shard_map/forward/pallas_call | solution.py:190
  84.3 0.9 collective-permute-done.18.refs_4_
  85.2 3.5 %forward.5.mine_ref = bf16[1024,512]{1,0:T(8,128)(2,1)S(1)} custom-call(s32[46]{0:T(128)S(1)} %pad_add_fusion.1.where_ref, bf16[2,8,1024,512]{3,2,1,0:T(8,128)(2,1)} %dense_blocks.3.dense_ref.a_ref, bf16[4,1024,512]{2,1,0:T(8,128)(2,1)} %other_blocks.2.refs_0_, bf16[4,1024,512]{2,1,0:T(8,128)(2,1)} %other_blocks.3.refs_1_, ...), custom_call_target="tpu_custom_call" | custom-call | flops 1073741824 | bytes 6291456 | tf_op jit(solution)/shard_map/forward/pallas_call | solution.py:190
  88.8 2.6 %collective-permute-done.20.other_ref = bf16[1024,512]{1,0:T(8,128)(2,1)S(1)} collective-permute-done((bf16[1024,512]{1,0:T(8,128)(2,1)S(1)}, bf16[1024,512]{1,0:T(8,128)(2,1)S(1)}, u32[]{:S(2)}, u32[]{:S(2)}) %collective-permute-start.20) | collective-permute-done | bytes 1048608 | tf_op jit(solution)/shard_map/partial_sums/ppermute | solution.py:444
  91.4 6.5 %middle.1 = (bf16[512,1024]{1,0:T(8,128)(2,1)S(1)}, bf16[256,512]{1,0:T(8,128)(2,1)S(1)}, bf16[256,512]{1,0:T(8,128)(2,1)S(1)}, bf16[4,64,512]{2,1,0:T(8,128)(2,1)S(1)}) custom-call(s32[46]{0:T(128)S(1)} %pad_add_fusion.1.where_ref, bf16[1024,512]{1,0:T(8,128)(2,1)S(1)} %forward.5.mine_ref, bf16[1024,512]{1,0:T(8,128)(2,1)S(1)} %collective-permute-done.20.other_ref, ...), custom_call_target="tpu_custom_call" | custom-call | flops 2684354560 | bytes 6291456 | tf_op jit(solution)/shard_map/middle/pallas_call | solution.py:275
  98.0 2.4 %collective-permute-start.23 = (bf16[64,512]{1,0:T(8,128)(2,1)S(1)}, bf16[64,512]{1,0:T(8,128)(2,1)S(1)}, u32[]{:S(2)}, u32[]{:S(2)}) collective-permute-start(bf16[64,512]{1,0:T(8,128)(2,1)S(1)} %get-tuple-element.320), channel_id=1, source_target_pairs={{0,24},{1,25},{2,26},{3,27},{4,28},{5,29},{6,30},{7,31},{8,16},{9,... | collective-permute-start | bytes 196616 | tf_op jit(solution)/shard_map/weight_grad/ppermute | solution.py:444
  100.3 0.9 collective-permute-start.22
  101.2 1.2 collective-permute-start.21
  102.4 1.1 collective-permute-start.24
  104.2 4.6 %backward.4 = (bf16[512,512]{1,0:T(8,128)(2,1)S(1)}, bf16[512,512]{1,0:T(8,128)(2,1)S(1)}, bf16[512,512]{1,0:T(8,128)(2,1)S(1)}) custom-call(s32[46]{0:T(128)S(1)} %pad_add_fusion.1.where_ref, bf16[512,1024]{1,0:T(8,128)(2,1)S(1)} %get-tuple-element.263.grad_ref, bf16[2,8,1024,512]{3,2,1,0:T(8,128)(2,1)} %dense_blocks.3.dense_ref.a_ref), custom_call_target="tpu_custom_call" | custom-call | flops 1610612736 | bytes 5767168 | tf_op jit(solution)/shard_map/backward/pallas_call | solution.py:348
  108.9 1.0 collective-permute-done.24.top_ref
  109.9 0.8 collective-permute-done.25.end_ref
  110.7 0.9 collective-permute-start.27
  111.8 0.8 collective-permute-start.28
  112.6 0.9 collective-permute-start.29
  113.4 5.5 %backward.5 = (bf16[512,512]{1,0:T(8,128)(2,1)S(1)}, bf16[512,512]{1,0:T(8,128)(2,1)S(1)}, bf16[512,512]{1,0:T(8,128)(2,1)S(1)}, bf16[512,512]{1,0:T(8,128)(2,1)S(1)}) custom-call(s32[46]{0:T(128)S(1)} %pad_add_fusion.1.where_ref, bf16[512,1024]{1,0:T(8,128)(2,1)S(1)} %get-tuple-element.263.grad_ref, bf16[2,8,1024,512]{3,2,1,0:T(8,128)(2,1)} %dense_blocks.3.dense_ref.a_ref), custom_call_target="tpu_custom_call" | custom-call | flops 2147483648 | bytes 7340032 | tf_op jit(solution)/shard_map/backward/pallas_call | solution.py:348
  118.9 1.2 collective-permute-start.26
  120.1 4.0 %collective-permute-done.26 = bf16[64,512]{1,0:T(8,128)(2,1)S(1)} collective-permute-done((bf16[64,512]{1,0:T(8,128)(2,1)S(1)}, bf16[64,512]{1,0:T(8,128)(2,1)S(1)}, u32[]{:S(2)}, u32[]{:S(2)}) %collective-permute-start.26) | collective-permute-done | bytes 65568 | tf_op jit(solution)/shard_map/weight_grad/ppermute | solution.py:444
  124.3 1.0 collective-permute-start.31
  125.4 1.4 collective-permute-start.32
  126.9 0.9 collective-permute-start.33
  127.8 6.7 %backward.6 = (bf16[512,512]{1,0:T(8,128)(2,1)S(1)}, bf16[512,512]{1,0:T(8,128)(2,1)S(1)}, bf16[512,512]{1,0:T(8,128)(2,1)S(1)}, bf16[512,512]{1,0:T(8,128)(2,1)S(1)}, bf16[512,512]{1,0:T(8,128)(2,1)S(1)}) custom-call(s32[46]{0:T(128)S(1)} %pad_add_fusion.1.where_ref, bf16[512,1024]{1,0:T(8,128)(2,1)S(1)} %get-tuple-element.263.grad_ref, ...), custom_call_target="tpu_custom_call" | custom-call | flops 2684354560 | bytes 8912896 | tf_op jit(solution)/shard_map/backward/pallas_call | solution.py:348
  134.5 0.8 collective-permute-start.30
  135.3 4.2 %collective-permute-done.30 = bf16[64,512]{1,0:T(8,128)(2,1)S(1)} collective-permute-done((bf16[64,512]{1,0:T(8,128)(2,1)S(1)}, bf16[64,512]{1,0:T(8,128)(2,1)S(1)}, u32[]{:S(2)}, u32[]{:S(2)}) %collective-permute-start.30) | collective-permute-done | bytes 65568 | tf_op jit(solution)/shard_map/weight_grad/ppermute | solution.py:444
  139.6 0.8 collective-permute-start.35
  140.4 1.1 collective-permute-start.36
  141.8 2.0 %collective-permute-start.37 = (bf16[256,512]{1,0:T(8,128)(2,1)S(1)}, bf16[256,512]{1,0:T(8,128)(2,1)S(1)}, u32[]{:S(2)}, u32[]{:S(2)}) collective-permute-start(bf16[256,512]{1,0:T(8,128)(2,1)S(1)} %get-tuple-element.314), channel_id=1, source_target_pairs={{0,16},{1,17},{2,18},{3,19},{4,20},{5,21},{6,22},{7,23},{8,24},{9,... | collective-permute-start | bytes 786440 | tf_op jit(solution)/shard_map/grads_along_z/ppermute | solution.py:444
  143.8 4.6 %backward.7 = (bf16[512,512]{1,0:T(8,128)(2,1)S(1)}, bf16[512,512]{1,0:T(8,128)(2,1)S(1)}, bf16[512,512]{1,0:T(8,128)(2,1)S(1)}) custom-call(s32[46]{0:T(128)S(1)} %pad_add_fusion.1.where_ref, bf16[512,1024]{1,0:T(8,128)(2,1)S(1)} %get-tuple-element.263.grad_ref, bf16[2,8,1024,512]{3,2,1,0:T(8,128)(2,1)} %dense_blocks.3.dense_ref.a_ref), custom_call_target="tpu_custom_call" | custom-call | flops 1610612736 | bytes 5767168 | tf_op jit(solution)/shard_map/backward/pallas_call | solution.py:348
  148.4 1.0 collective-permute-start.34
  149.5 5.3 %collective-permute-done.34 = bf16[1,64,512]{2,1,0:T(8,128)(2,1)S(1)} collective-permute-done((bf16[1,64,512]{2,1,0:T(8,128)(2,1)S(1)}, bf16[1,64,512]{2,1,0:T(8,128)(2,1)S(1)}, u32[]{:S(2)}, u32[]{:S(2)}) %collective-permute-start.34) | collective-permute-done | bytes 65568 | tf_op jit(solution)/shard_map/weight_grad/ppermute | solution.py:444
  154.9 1.0 collective-permute-start.40
  155.9 1.2 collective-permute-start.41
  157.1 2.3 %collective-permute-start.39 = (bf16[256,512]{1,0:T(8,128)(2,1)S(1)}, bf16[256,512]{1,0:T(8,128)(2,1)S(1)}, u32[]{:S(2)}, u32[]{:S(2)}) collective-permute-start(bf16[256,512]{1,0:T(8,128)(2,1)S(1)} %get-tuple-element.284), channel_id=1, source_target_pairs={{0,16},{1,17},{2,18},{3,19},{4,20},{5,21},{6,22},{7,23},{8,24},{9,... | collective-permute-start | bytes 786440 | tf_op jit(solution)/shard_map/grads_along_z/ppermute | solution.py:444
  159.6 4.9 %collective-permute-done.38 = bf16[2,64,512]{2,1,0:T(8,128)(2,1)S(1)} collective-permute-done((bf16[2,64,512]{2,1,0:T(8,128)(2,1)S(1)}, bf16[2,64,512]{2,1,0:T(8,128)(2,1)S(1)}, u32[]{:S(2)}, u32[]{:S(2)}) %collective-permute-start.38) | collective-permute-done | bytes 131104 | tf_op jit(solution)/shard_map/weight_grad/ppermute | solution.py:444
  164.5 3.4 %collective-permute-done.39.refs_5_ = bf16[256,512]{1,0:T(8,128)(2,1)S(1)} collective-permute-done((bf16[256,512]{1,0:T(8,128)(2,1)S(1)}, bf16[256,512]{1,0:T(8,128)(2,1)S(1)}, u32[]{:S(2)}, u32[]{:S(2)}) %collective-permute-start.39) | collective-permute-done | bytes 262176 | tf_op jit(solution)/shard_map/grads_along_z/ppermute | solution.py:444
  167.9 1.1 collective-permute-start.42
  169.0 1.3 collective-permute-start.43
  170.6 1.8 %activated.1 = bf16[512,512]{1,0:T(8,128)(2,1)} custom-call(s32[46]{0:T(128)S(1)} %pad_add_fusion.1.where_ref, bf16[1024,512]{1,0:T(8,128)(2,1)S(1)} %forward.5.mine_ref, bf16[1024,512]{1,0:T(8,128)(2,1)S(1)} %collective-permute-done.20.other_ref, bf16[512,512]{1,0:T(8,128)(2,1)S(1)} %copy-done.2, bf16[1024,512]{1,0:T(8,128)(2,1)S(1)} %pad_maximum_fusion.cot_ref), custom_call_target="tpu_custom_call" | custom-call | flops 268435456 | bytes 2097152 | tf_op jit(solution)/shard_map/activated/pallas_call | solution.py:312
  172.5 4.6 %collective-permute-done.42.refs_1_ = bf16[512,512]{1,0:T(8,128)(2,1)S(1)} collective-permute-done((bf16[512,512]{1,0:T(8,128)(2,1)S(1)}, bf16[512,512]{1,0:T(8,128)(2,1)S(1)}, u32[]{:S(2)}, u32[]{:S(2)}) %collective-permute-start.42) | collective-permute-done | bytes 524320 | tf_op jit(solution)/shard_map/grads_across/ppermute | solution.py:444
  177.1 3.3 %collective-permute-done.43.refs_2_ = bf16[512,512]{1,0:T(8,128)(2,1)S(1)} collective-permute-done((bf16[512,512]{1,0:T(8,128)(2,1)S(1)}, bf16[512,512]{1,0:T(8,128)(2,1)S(1)}, u32[]{:S(2)}, u32[]{:S(2)}) %collective-permute-start.43) | collective-permute-done | bytes 524320 | tf_op jit(solution)/shard_map/grads_across/ppermute | solution.py:444
  180.4 1.7 collective-permute-done.44.refs_3_
  182.1 2.1 %grads_out.1 = (bf16[1,512,512]{2,1,0:T(8,128)(2,1)}, f32[512,512]{1,0:T(8,128)}) custom-call(s32[46]{0:T(128)S(1)} %pad_add_fusion.1.where_ref, bf16[512,512]{1,0:T(8,128)(2,1)S(1)} %get-tuple-element.303.refs_0_, bf16[512,512]{1,0:T(8,128)(2,1)S(1)} %collective-permute-done.42.refs_1_, bf16[512,512]{1,0:T(8,128)(2,1)S(1)} %collective-permute-done.43.refs_2_, ...), custom_call_target="tpu_custom_call" | custom-call | flops 1048576 | bytes 2621440 | tf_op jit(solution)/shard_map/grads_out/pallas_call | solution.py:410
  (87 shorter events, 8.3 us)
Async XLA Ops:
  0.6 1.2 copy-start
  0.6 18.9 %collective-permute-start = (bf16[8,24,128,128]{3,2,1,0:T(8,128)(2,1)}, bf16[8,24,128,128]{3,2,1,0:T(8,128)(2,1)}, u32[]{:S(2)}, u32[]{:S(2)}) collective-permute-start(bf16[8,24,128,128]{3,2,1,0:T(8,128)(2,1)} %bitcast.16), channel_id=1, source_target_pairs={{0,1},{1,0},{2,3},{3,2},{4,5},{5,4},{6,7},{7,6},{8,9},{9,8},{10,11... | collective-permute-start | bytes 18874376 | tf_op jit(solution)/shard_map/tiles_exchange/ppermute | solution.py:444
  1.9 15.8 %collective-permute-start.2 = (bf16[512,512]{1,0:T(8,128)(2,1)S(1)}, bf16[512,512]{1,0:T(8,128)(2,1)S(1)}, u32[]{:S(2)}, u32[]{:S(2)}) collective-permute-start(bf16[512,512]{1,0:T(8,128)(2,1)S(1)} %constant_dynamic-slice_fusion.refs_2_), channel_id=1, source_target_pairs={{0,2},{1,3},{2,0},{3,1},{4,6},{5,7},{6,4},{7,5},{8,10},{9,11},{10,... | collective-permute-start | bytes 1572872 | tf_op jit(solution)/shard_map/features_across/ppermute | solution.py:444
  4.9 13.4 %collective-permute-start.3 = (bf16[512,512]{1,0:T(8,128)(2,1)S(1)}, bf16[512,512]{1,0:T(8,128)(2,1)S(1)}, u32[]{:S(2)}, u32[]{:S(2)}) collective-permute-start(bf16[512,512]{1,0:T(8,128)(2,1)S(1)} %constant_dynamic-slice_fusion.refs_2_), channel_id=1, source_target_pairs={{0,4},{1,5},{2,6},{3,7},{4,0},{5,1},{6,2},{7,3},{8,12},{9,13},{10,... | collective-permute-start | bytes 1572872 | tf_op jit(solution)/shard_map/features_across/ppermute | solution.py:444
  6.4 13.1 %collective-permute-start.4 = (bf16[512,512]{1,0:T(8,128)(2,1)S(1)}, bf16[512,512]{1,0:T(8,128)(2,1)S(1)}, u32[]{:S(2)}, u32[]{:S(2)}) collective-permute-start(bf16[512,512]{1,0:T(8,128)(2,1)S(1)} %constant_dynamic-slice_fusion.refs_2_), channel_id=1, source_target_pairs={{0,8},{1,9},{2,10},{3,11},{4,12},{5,13},{6,14},{7,15},{8,0},{9,1},... | collective-permute-start | bytes 1572872 | tf_op jit(solution)/shard_map/features_along_z/ppermute | solution.py:444
  9.5 8.2 %collective-permute-start.1 = (s32[8,25]{1,0:T(8,128)S(1)}, s32[8,25]{1,0:T(8,128)S(1)}, u32[]{:S(2)}, u32[]{:S(2)}) collective-permute-start(s32[8,25]{1,0:T(8,128)S(1)} %pad_add_fusion.packed_ref), channel_id=1, source_target_pairs={{0,1},{1,0},{2,3},{3,2},{4,5},{5,4},{6,7},{7,6},{8,9},{9,8},{10,11... | collective-permute-start | bytes 2408 | tf_op jit(solution)/shard_map/tiles_exchange/ppermute | solution.py:444
  19.5 13.9 %collective-permute-start.5 = (bf16[512,512]{1,0:T(8,128)(2,1)S(1)}, bf16[512,512]{1,0:T(8,128)(2,1)S(1)}, u32[]{:S(2)}, u32[]{:S(2)}) collective-permute-start(bf16[512,512]{1,0:T(8,128)(2,1)S(1)} %collective-permute-done.4.refs_5_), channel_id=1, source_target_pairs={{0,2},{1,3},{2,0},{3,1},{4,6},{5,7},{6,4},{7,5},{8,10},{9,11},{10,... | collective-permute-start | bytes 1572872 | tf_op jit(solution)/shard_map/features_across/ppermute | solution.py:444
  20.1 13.4 %collective-permute-start.6 = (bf16[512,512]{1,0:T(8,128)(2,1)S(1)}, bf16[512,512]{1,0:T(8,128)(2,1)S(1)}, u32[]{:S(2)}, u32[]{:S(2)}) collective-permute-start(bf16[512,512]{1,0:T(8,128)(2,1)S(1)} %collective-permute-done.4.refs_5_), channel_id=1, source_target_pairs={{0,4},{1,5},{2,6},{3,7},{4,0},{5,1},{6,2},{7,3},{8,12},{9,13},{10,... | collective-permute-start | bytes 1572872 | tf_op jit(solution)/shard_map/features_across/ppermute | solution.py:444
  20.4 13.0 %collective-permute-start.7 = (bf16[256,512]{1,0:T(8,128)(2,1)S(1)}, bf16[256,512]{1,0:T(8,128)(2,1)S(1)}, u32[]{:S(2)}, u32[]{:S(2)}) collective-permute-start(bf16[256,512]{1,0:T(8,128)(2,1)S(1)} %get-tuple-element.318), channel_id=1, source_target_pairs={{0,16},{1,17},{2,18},{3,19},{4,20},{5,21},{6,22},{7,23},{8,24},{9,... | collective-permute-start | bytes 786440 | tf_op jit(solution)/shard_map/features_along_z/ppermute | solution.py:444
  33.5 9.6 %copy-start.3 = (bf16[512,512]{1,0:T(8,128)(2,1)}, bf16[512,512]{1,0:T(8,128)(2,1)S(1)}, u32[]{:S(2)}) copy-start(bf16[512,512]{1,0:T(8,128)(2,1)S(1)} %collective-permute-done.6.refs_7_) | copy-start | bytes 1572868
  33.5 16.4 %collective-permute-start.9 = (bf16[512,512]{1,0:T(8,128)(2,1)S(1)}, bf16[512,512]{1,0:T(8,128)(2,1)S(1)}, u32[]{:S(2)}, u32[]{:S(2)}) collective-permute-start(bf16[512,512]{1,0:T(8,128)(2,1)S(1)} %collective-permute-done.2.refs_3_), channel_id=1, source_target_pairs={{0,4},{1,5},{2,6},{3,7},{4,0},{5,1},{6,2},{7,3},{8,12},{9,13},{10,... | collective-permute-start | bytes 1572872 | tf_op jit(solution)/shard_map/features_across/ppermute | solution.py:444
  35.0 14.9 %collective-permute-start.10 = (bf16[512,512]{1,0:T(8,128)(2,1)S(1)}, bf16[512,512]{1,0:T(8,128)(2,1)S(1)}, u32[]{:S(2)}, u32[]{:S(2)}) collective-permute-start(bf16[512,512]{1,0:T(8,128)(2,1)S(1)} %collective-permute-done.6.refs_7_), channel_id=1, source_target_pairs={{0,2},{1,3},{2,0},{3,1},{4,6},{5,7},{6,4},{7,5},{8,10},{9,11},{10,... | collective-permute-start | bytes 1572872 | tf_op jit(solution)/shard_map/features_across/ppermute | solution.py:444
  36.6 13.4 %collective-permute-start.8 = (bf16[256,512]{1,0:T(8,128)(2,1)S(1)}, bf16[256,512]{1,0:T(8,128)(2,1)S(1)}, u32[]{:S(2)}, u32[]{:S(2)}) collective-permute-start(bf16[256,512]{1,0:T(8,128)(2,1)S(1)} %get-tuple-element.317), channel_id=1, source_target_pairs={{0,16},{1,17},{2,18},{3,19},{4,20},{5,21},{6,22},{7,23},{8,24},{9,... | collective-permute-start | bytes 786440 | tf_op jit(solution)/shard_map/features_along_z/ppermute | solution.py:444
  49.9 0.8 copy-start.5
  49.9 1.1 copy-start.7
  50.0 12.9 %collective-permute-start.11 = (bf16[512,512]{1,0:T(8,128)(2,1)S(1)}, bf16[512,512]{1,0:T(8,128)(2,1)}, u32[]{:S(2)}, u32[]{:S(2)}) collective-permute-start(bf16[512,512]{1,0:T(8,128)(2,1)S(1)} %constant_dynamic-update-slice_fusion.refs_10_), channel_id=1, source_target_pairs={{0,2},{1,3},{2,0},{3,1},{4,6},{5,7},{6,4},{7,5},{8,10},{9,11},{10,... | collective-permute-start | bytes 1572872 | tf_op jit(solution)/shard_map/features_across/ppermute | solution.py:444
  50.7 12.8 %collective-permute-start.12 = (bf16[512,512]{1,0:T(8,128)(2,1)S(1)}, bf16[512,512]{1,0:T(8,128)(2,1)}, u32[]{:S(2)}, u32[]{:S(2)}) collective-permute-start(bf16[512,512]{1,0:T(8,128)(2,1)S(1)} %constant_dynamic-update-slice_fusion.refs_10_), channel_id=1, source_target_pairs={{0,4},{1,5},{2,6},{3,7},{4,0},{5,1},{6,2},{7,3},{8,12},{9,13},{10,... | collective-permute-start | bytes 1572872 | tf_op jit(solution)/shard_map/features_across/ppermute | solution.py:444
  51.1 12.6 %collective-permute-start.13 = (bf16[512,512]{1,0:T(8,128)(2,1)S(1)}, bf16[512,512]{1,0:T(8,128)(2,1)}, u32[]{:S(2)}, u32[]{:S(2)}) collective-permute-start(bf16[512,512]{1,0:T(8,128)(2,1)S(1)} %constant_dynamic-update-slice_fusion.refs_10_), channel_id=1, source_target_pairs={{0,8},{1,9},{2,10},{3,11},{4,12},{5,13},{6,14},{7,15},{8,0},{9,1},... | collective-permute-start | bytes 1572872 | tf_op jit(solution)/shard_map/features_along_z/ppermute | solution.py:444
  51.1 28.2 %collective-permute-start.19 = (bf16[512,512]{1,0:T(8,128)(2,1)}, bf16[512,512]{1,0:T(8,128)(2,1)}, u32[]{:S(2)}, u32[]{:S(2)}) collective-permute-start(bf16[512,512]{1,0:T(8,128)(2,1)} %param.14), channel_id=1, source_target_pairs={{0,1},{1,0},{2,3},{3,2},{4,5},{5,4},{6,7},{7,6},{8,9},{9,8},{10,11... | collective-permute-start | bytes 1572872 | tf_op jit(solution)/shard_map/cotangent_rows/ppermute | solution.py:444
  51.1 15.6 %copy-start.4 = (bf16[512,512]{1,0:T(8,128)(2,1)S(1)}, bf16[512,512]{1,0:T(8,128)(2,1)}, u32[]{:S(2)}) copy-start(bf16[512,512]{1,0:T(8,128)(2,1)} %copy-done.3) | copy-start | bytes 1572868
  51.1 15.6 %copy-start.6 = (bf16[512,512]{1,0:T(8,128)(2,1)S(1)}, bf16[512,512]{1,0:T(8,128)(2,1)}, u32[]{:S(2)}) copy-start(bf16[512,512]{1,0:T(8,128)(2,1)} %copy-done.5) | copy-start | bytes 1572868
  51.1 15.6 %copy-start.8 = (bf16[512,512]{1,0:T(8,128)(2,1)S(1)}, bf16[512,512]{1,0:T(8,128)(2,1)}, u32[]{:S(2)}) copy-start(bf16[512,512]{1,0:T(8,128)(2,1)} %copy-done.7) | copy-start | bytes 1572868
  63.7 14.0 %collective-permute-start.14 = (bf16[512,512]{1,0:T(8,128)(2,1)}, bf16[512,512]{1,0:T(8,128)(2,1)S(1)}, u32[]{:S(2)}, u32[]{:S(2)}) collective-permute-start(bf16[512,512]{1,0:T(8,128)(2,1)} %collective-permute-done.12.refs_12_), channel_id=1, source_target_pairs={{0,2},{1,3},{2,0},{3,1},{4,6},{5,7},{6,4},{7,5},{8,10},{9,11},{10,... | collective-permute-start | bytes 1572872 | tf_op jit(solution)/shard_map/features_across/ppermute | solution.py:444
  64.7 13.0 %collective-permute-start.15 = (bf16[512,512]{1,0:T(8,128)(2,1)}, bf16[512,512]{1,0:T(8,128)(2,1)S(1)}, u32[]{:S(2)}, u32[]{:S(2)}) collective-permute-start(bf16[512,512]{1,0:T(8,128)(2,1)} %collective-permute-done.13.refs_13_), channel_id=1, source_target_pairs={{0,4},{1,5},{2,6},{3,7},{4,0},{5,1},{6,2},{7,3},{8,12},{9,13},{10,... | collective-permute-start | bytes 1572872 | tf_op jit(solution)/shard_map/features_across/ppermute | solution.py:444
  66.4 11.3 %collective-permute-start.16 = (bf16[512,512]{1,0:T(8,128)(2,1)}, bf16[512,512]{1,0:T(8,128)(2,1)S(1)}, u32[]{:S(2)}, u32[]{:S(2)}) collective-permute-start(bf16[512,512]{1,0:T(8,128)(2,1)} %collective-permute-done.11.refs_11_), channel_id=1, source_target_pairs={{0,8},{1,9},{2,10},{3,11},{4,12},{5,13},{6,14},{7,15},{8,0},{9,1},... | collective-permute-start | bytes 1572872 | tf_op jit(solution)/shard_map/features_along_z/ppermute | solution.py:444
  77.8 6.6 %collective-permute-start.17 = (bf16[256,512]{1,0:T(8,128)(2,1)S(1)}, bf16[256,512]{1,0:T(8,128)(2,1)S(1)}, u32[]{:S(2)}, u32[]{:S(2)}) collective-permute-start(bf16[256,512]{1,0:T(8,128)(2,1)S(1)} %slice.50), channel_id=1, source_target_pairs={{0,2},{1,3},{2,0},{3,1},{4,6},{5,7},{6,4},{7,5},{8,10},{9,11},{10,... | collective-permute-start | bytes 786440 | tf_op jit(solution)/shard_map/features_across/ppermute | solution.py:444
  78.8 6.4 %collective-permute-start.18 = (bf16[256,512]{1,0:T(8,128)(2,1)S(1)}, bf16[256,512]{1,0:T(8,128)(2,1)S(1)}, u32[]{:S(2)}, u32[]{:S(2)}) collective-permute-start(bf16[256,512]{1,0:T(8,128)(2,1)S(1)} %slice.51), channel_id=1, source_target_pairs={{0,4},{1,5},{2,6},{3,7},{4,0},{5,1},{6,2},{7,3},{8,12},{9,13},{10,... | collective-permute-start | bytes 786440 | tf_op jit(solution)/shard_map/features_across/ppermute | solution.py:444
  84.3 7.1 %copy-start.2 = (bf16[512,512]{1,0:T(8,128)(2,1)S(1)}, bf16[512,512]{1,0:T(8,128)(2,1)}, u32[]{:S(2)}) copy-start(bf16[512,512]{1,0:T(8,128)(2,1)} %weight_ref.3) | copy-start | bytes 1572868
  88.7 2.7 %collective-permute-start.20 = (bf16[1024,512]{1,0:T(8,128)(2,1)S(1)}, bf16[1024,512]{1,0:T(8,128)(2,1)S(1)}, u32[]{:S(2)}, u32[]{:S(2)}) collective-permute-start(bf16[1024,512]{1,0:T(8,128)(2,1)S(1)} %forward.5.mine_ref), channel_id=1, source_target_pairs={{0,1},{1,0},{2,3},{3,2},{4,5},{5,4},{6,7},{7,6},{8,9},{9,8},{10,11... | collective-permute-start | bytes 3145736 | tf_op jit(solution)/shard_map/partial_sums/ppermute | solution.py:444
  98.0 10.9 %collective-permute-start.23 = (bf16[64,512]{1,0:T(8,128)(2,1)S(1)}, bf16[64,512]{1,0:T(8,128)(2,1)S(1)}, u32[]{:S(2)}, u32[]{:S(2)}) collective-permute-start(bf16[64,512]{1,0:T(8,128)(2,1)S(1)} %get-tuple-element.320), channel_id=1, source_target_pairs={{0,24},{1,25},{2,26},{3,27},{4,28},{5,29},{6,30},{7,31},{8,16},{9,... | collective-permute-start | bytes 196616 | tf_op jit(solution)/shard_map/weight_grad/ppermute | solution.py:444
  100.3 8.5 %collective-permute-start.22 = (bf16[64,512]{1,0:T(8,128)(2,1)S(1)}, bf16[64,512]{1,0:T(8,128)(2,1)S(1)}, u32[]{:S(2)}, u32[]{:S(2)}) collective-permute-start(bf16[64,512]{1,0:T(8,128)(2,1)S(1)} %get-tuple-element.321), channel_id=1, source_target_pairs={{0,16},{1,17},{2,18},{3,19},{4,20},{5,21},{6,22},{7,23},{8,24},{9,... | collective-permute-start | bytes 196616 | tf_op jit(solution)/shard_map/weight_grad/ppermute | solution.py:444
  101.2 7.6 %collective-permute-start.21 = (bf16[64,512]{1,0:T(8,128)(2,1)S(1)}, bf16[64,512]{1,0:T(8,128)(2,1)S(1)}, u32[]{:S(2)}, u32[]{:S(2)}) collective-permute-start(bf16[64,512]{1,0:T(8,128)(2,1)S(1)} %get-tuple-element.319), channel_id=1, source_target_pairs={{0,8},{1,9},{2,10},{3,11},{4,12},{5,13},{6,14},{7,15},{8,0},{9,1},... | collective-permute-start | bytes 196616 | tf_op jit(solution)/shard_map/weight_grad/ppermute | solution.py:444
  102.4 7.5 %collective-permute-start.24 = (bf16[256,512]{1,0:T(8,128)(2,1)S(1)}, bf16[256,512]{1,0:T(8,128)(2,1)S(1)}, u32[]{:S(2)}, u32[]{:S(2)}) collective-permute-start(bf16[256,512]{1,0:T(8,128)(2,1)S(1)} %get-tuple-element.221), channel_id=1, source_target_pairs={{0,2},{1,3},{2,0},{3,1},{4,6},{5,7},{6,4},{7,5},{8,10},{9,11},{10,... | collective-permute-start | bytes 786440 | tf_op jit(solution)/shard_map/grads_across/ppermute | solution.py:444
  103.5 7.2 %collective-permute-start.25 = (bf16[256,512]{1,0:T(8,128)(2,1)S(1)}, bf16[256,512]{1,0:T(8,128)(2,1)S(1)}, u32[]{:S(2)}, u32[]{:S(2)}) collective-permute-start(bf16[256,512]{1,0:T(8,128)(2,1)S(1)} %get-tuple-element.222), channel_id=1, source_target_pairs={{0,4},{1,5},{2,6},{3,7},{4,0},{5,1},{6,2},{7,3},{8,12},{9,13},{10,... | collective-permute-start | bytes 786440 | tf_op jit(solution)/shard_map/grads_across/ppermute | solution.py:444
  110.7 13.3 %collective-permute-start.27 = (bf16[512,512]{1,0:T(8,128)(2,1)S(1)}, bf16[512,512]{1,0:T(8,128)(2,1)S(1)}, u32[]{:S(2)}, u32[]{:S(2)}) collective-permute-start(bf16[512,512]{1,0:T(8,128)(2,1)S(1)} %get-tuple-element.234), channel_id=1, source_target_pairs={{0,2},{1,3},{2,0},{3,1},{4,6},{5,7},{6,4},{7,5},{8,10},{9,11},{10,... | collective-permute-start | bytes 1572872 | tf_op jit(solution)/shard_map/grads_across/ppermute | solution.py:444
  111.8 12.3 %collective-permute-start.28 = (bf16[512,512]{1,0:T(8,128)(2,1)S(1)}, bf16[512,512]{1,0:T(8,128)(2,1)S(1)}, u32[]{:S(2)}, u32[]{:S(2)}) collective-permute-start(bf16[512,512]{1,0:T(8,128)(2,1)S(1)} %get-tuple-element.239), channel_id=1, source_target_pairs={{0,4},{1,5},{2,6},{3,7},{4,0},{5,1},{6,2},{7,3},{8,12},{9,13},{10,... | collective-permute-start | bytes 1572872 | tf_op jit(solution)/shard_map/grads_across/ppermute | solution.py:444
  112.6 11.5 %collective-permute-start.29 = (bf16[512,512]{1,0:T(8,128)(2,1)S(1)}, bf16[512,512]{1,0:T(8,128)(2,1)S(1)}, u32[]{:S(2)}, u32[]{:S(2)}) collective-permute-start(bf16[512,512]{1,0:T(8,128)(2,1)S(1)} %get-tuple-element.240), channel_id=1, source_target_pairs={{0,8},{1,9},{2,10},{3,11},{4,12},{5,13},{6,14},{7,15},{8,0},{9,1},... | collective-permute-start | bytes 1572872 | tf_op jit(solution)/shard_map/grads_along_z/ppermute | solution.py:444
  118.9 5.1 %collective-permute-start.26 = (bf16[64,512]{1,0:T(8,128)(2,1)S(1)}, bf16[64,512]{1,0:T(8,128)(2,1)S(1)}, u32[]{:S(2)}, u32[]{:S(2)}) collective-permute-start(bf16[64,512]{1,0:T(8,128)(2,1)S(1)} %fusion.2), channel_id=1, source_target_pairs={{0,2},{1,3},{2,0},{3,1},{4,6},{5,7},{6,4},{7,5},{8,10},{9,11},{10,... | collective-permute-start | bytes 196616 | tf_op jit(solution)/shard_map/weight_grad/ppermute | solution.py:444
  124.3 15.3 %collective-permute-start.31 = (bf16[512,512]{1,0:T(8,128)(2,1)S(1)}, bf16[512,512]{1,0:T(8,128)(2,1)S(1)}, u32[]{:S(2)}, u32[]{:S(2)}) collective-permute-start(bf16[512,512]{1,0:T(8,128)(2,1)S(1)} %add_convert_fusion.5), channel_id=1, source_target_pairs={{0,2},{1,3},{2,0},{3,1},{4,6},{5,7},{6,4},{7,5},{8,10},{9,11},{10,... | collective-permute-start | bytes 1572872 | tf_op jit(solution)/shard_map/grads_across/ppermute | solution.py:444
  125.4 14.1 %collective-permute-start.32 = (bf16[512,512]{1,0:T(8,128)(2,1)S(1)}, bf16[512,512]{1,0:T(8,128)(2,1)S(1)}, u32[]{:S(2)}, u32[]{:S(2)}) collective-permute-start(bf16[512,512]{1,0:T(8,128)(2,1)S(1)} %add_convert_fusion.4), channel_id=1, source_target_pairs={{0,4},{1,5},{2,6},{3,7},{4,0},{5,1},{6,2},{7,3},{8,12},{9,13},{10,... | collective-permute-start | bytes 1572872 | tf_op jit(solution)/shard_map/grads_across/ppermute | solution.py:444
  126.9 12.7 %collective-permute-start.33 = (bf16[512,512]{1,0:T(8,128)(2,1)S(1)}, bf16[512,512]{1,0:T(8,128)(2,1)S(1)}, u32[]{:S(2)}, u32[]{:S(2)}) collective-permute-start(bf16[512,512]{1,0:T(8,128)(2,1)S(1)} %add_convert_fusion.3), channel_id=1, source_target_pairs={{0,8},{1,9},{2,10},{3,11},{4,12},{5,13},{6,14},{7,15},{8,0},{9,1},... | collective-permute-start | bytes 1572872 | tf_op jit(solution)/shard_map/grads_along_z/ppermute | solution.py:444
  134.5 5.0 %collective-permute-start.30 = (bf16[64,512]{1,0:T(8,128)(2,1)S(1)}, bf16[64,512]{1,0:T(8,128)(2,1)S(1)}, u32[]{:S(2)}, u32[]{:S(2)}) collective-permute-start(bf16[64,512]{1,0:T(8,128)(2,1)S(1)} %add_convert_fusion.9), channel_id=1, source_target_pairs={{0,4},{1,5},{2,6},{3,7},{4,0},{5,1},{6,2},{7,3},{8,12},{9,13},{10,... | collective-permute-start | bytes 196616 | tf_op jit(solution)/shard_map/weight_grad/ppermute | solution.py:444
  139.6 15.2 %collective-permute-start.35 = (bf16[512,512]{1,0:T(8,128)(2,1)S(1)}, bf16[512,512]{1,0:T(8,128)(2,1)S(1)}, u32[]{:S(2)}, u32[]{:S(2)}) collective-permute-start(bf16[512,512]{1,0:T(8,128)(2,1)S(1)} %get-tuple-element.277), channel_id=1, source_target_pairs={{0,4},{1,5},{2,6},{3,7},{4,0},{5,1},{6,2},{7,3},{8,12},{9,13},{10,... | collective-permute-start | bytes 1572872 | tf_op jit(solution)/shard_map/grads_across/ppermute | solution.py:444
  140.4 14.4 %collective-permute-start.36 = (bf16[512,512]{1,0:T(8,128)(2,1)S(1)}, bf16[512,512]{1,0:T(8,128)(2,1)S(1)}, u32[]{:S(2)}, u32[]{:S(2)}) collective-permute-start(bf16[512,512]{1,0:T(8,128)(2,1)S(1)} %get-tuple-element.278), channel_id=1, source_target_pairs={{0,2},{1,3},{2,0},{3,1},{4,6},{5,7},{6,4},{7,5},{8,10},{9,11},{10,... | collective-permute-start | bytes 1572872 | tf_op jit(solution)/shard_map/grads_across/ppermute | solution.py:444
  141.8 13.0 %collective-permute-start.37 = (bf16[256,512]{1,0:T(8,128)(2,1)S(1)}, bf16[256,512]{1,0:T(8,128)(2,1)S(1)}, u32[]{:S(2)}, u32[]{:S(2)}) collective-permute-start(bf16[256,512]{1,0:T(8,128)(2,1)S(1)} %get-tuple-element.314), channel_id=1, source_target_pairs={{0,16},{1,17},{2,18},{3,19},{4,20},{5,21},{6,22},{7,23},{8,24},{9,... | collective-permute-start | bytes 786440 | tf_op jit(solution)/shard_map/grads_along_z/ppermute | solution.py:444
  148.4 6.3 %collective-permute-start.34 = (bf16[1,64,512]{2,1,0:T(8,128)(2,1)S(1)}, bf16[1,64,512]{2,1,0:T(8,128)(2,1)S(1)}, u32[]{:S(2)}, u32[]{:S(2)}) collective-permute-start(bf16[1,64,512]{2,1,0:T(8,128)(2,1)S(1)} %bitcast.19), channel_id=1, source_target_pairs={{0,16},{1,17},{2,18},{3,19},{4,20},{5,21},{6,22},{7,23},{8,24},{9,... | collective-permute-start | bytes 196616 | tf_op jit(solution)/shard_map/weight_grad/ppermute | solution.py:444
  154.9 12.9 %collective-permute-start.40 = (bf16[512,512]{1,0:T(8,128)(2,1)S(1)}, bf16[512,512]{1,0:T(8,128)(2,1)S(1)}, u32[]{:S(2)}, u32[]{:S(2)}) collective-permute-start(bf16[512,512]{1,0:T(8,128)(2,1)S(1)} %add_convert_fusion.2), channel_id=1, source_target_pairs={{0,2},{1,3},{2,0},{3,1},{4,6},{5,7},{6,4},{7,5},{8,10},{9,11},{10,... | collective-permute-start | bytes 1572872 | tf_op jit(solution)/shard_map/grads_across/ppermute | solution.py:444
  155.9 11.9 %collective-permute-start.41 = (bf16[512,512]{1,0:T(8,128)(2,1)S(1)}, bf16[512,512]{1,0:T(8,128)(2,1)S(1)}, u32[]{:S(2)}, u32[]{:S(2)}) collective-permute-start(bf16[512,512]{1,0:T(8,128)(2,1)S(1)} %get-tuple-element.288), channel_id=1, source_target_pairs={{0,4},{1,5},{2,6},{3,7},{4,0},{5,1},{6,2},{7,3},{8,12},{9,13},{10,... | collective-permute-start | bytes 1572872 | tf_op jit(solution)/shard_map/grads_across/ppermute | solution.py:444
  157.1 7.4 %collective-permute-start.38 = (bf16[2,64,512]{2,1,0:T(8,128)(2,1)S(1)}, bf16[2,64,512]{2,1,0:T(8,128)(2,1)S(1)}, u32[]{:S(2)}, u32[]{:S(2)}) collective-permute-start(bf16[2,64,512]{2,1,0:T(8,128)(2,1)S(1)} %pad_maximum_fusion.2), channel_id=1, source_target_pairs={{0,8},{1,9},{2,10},{3,11},{4,12},{5,13},{6,14},{7,15},{8,0},{9,1},... | collective-permute-start | bytes 393224 | tf_op jit(solution)/shard_map/weight_grad/ppermute | solution.py:444
  157.1 10.8 %collective-permute-start.39 = (bf16[256,512]{1,0:T(8,128)(2,1)S(1)}, bf16[256,512]{1,0:T(8,128)(2,1)S(1)}, u32[]{:S(2)}, u32[]{:S(2)}) collective-permute-start(bf16[256,512]{1,0:T(8,128)(2,1)S(1)} %get-tuple-element.284), channel_id=1, source_target_pairs={{0,16},{1,17},{2,18},{3,19},{4,20},{5,21},{6,22},{7,23},{8,24},{9,... | collective-permute-start | bytes 786440 | tf_op jit(solution)/shard_map/grads_along_z/ppermute | solution.py:444
  167.9 9.2 %collective-permute-start.42 = (bf16[512,512]{1,0:T(8,128)(2,1)S(1)}, bf16[512,512]{1,0:T(8,128)(2,1)S(1)}, u32[]{:S(2)}, u32[]{:S(2)}) collective-permute-start(bf16[512,512]{1,0:T(8,128)(2,1)S(1)} %get-tuple-element.296), channel_id=1, source_target_pairs={{0,2},{1,3},{2,0},{3,1},{4,6},{5,7},{6,4},{7,5},{8,10},{9,11},{10,... | collective-permute-start | bytes 1572872 | tf_op jit(solution)/shard_map/grads_across/ppermute | solution.py:444
  169.0 11.4 %collective-permute-start.43 = (bf16[512,512]{1,0:T(8,128)(2,1)S(1)}, bf16[512,512]{1,0:T(8,128)(2,1)S(1)}, u32[]{:S(2)}, u32[]{:S(2)}) collective-permute-start(bf16[512,512]{1,0:T(8,128)(2,1)S(1)} %add_convert_fusion.1), channel_id=1, source_target_pairs={{0,4},{1,5},{2,6},{3,7},{4,0},{5,1},{6,2},{7,3},{8,12},{9,13},{10,... | collective-permute-start | bytes 1572872 | tf_op jit(solution)/shard_map/grads_across/ppermute | solution.py:444
  170.3 14.0 %copy-start.1 = (bf16[1024,512]{1,0:T(8,128)(2,1)S(1)}, bf16[1024,512]{1,0:T(8,128)(2,1)}, u32[]{:S(2)}) copy-start(bf16[1024,512]{1,0:T(8,128)(2,1)} %param.8) | copy-start | bytes 3145732
  170.5 11.7 %collective-permute-start.44 = (bf16[512,512]{1,0:T(8,128)(2,1)S(1)}, bf16[512,512]{1,0:T(8,128)(2,1)S(1)}, u32[]{:S(2)}, u32[]{:S(2)}) collective-permute-start(bf16[512,512]{1,0:T(8,128)(2,1)S(1)} %add_convert_fusion), channel_id=1, source_target_pairs={{0,8},{1,9},{2,10},{3,11},{4,12},{5,13},{6,14},{7,15},{8,0},{9,1},... | collective-permute-start | bytes 1572872 | tf_op jit(solution)/shard_map/grads_along_z/ppermute | solution.py:444
  170.6 1.9 %collective-permute-start.45 = (bf16[4,64,512]{2,1,0:T(8,128)(2,1)S(1)}, bf16[4,64,512]{2,1,0:T(8,128)(2,1)S(1)}, u32[]{:S(2)}, u32[]{:S(2)}) collective-permute-start(bf16[4,64,512]{2,1,0:T(8,128)(2,1)S(1)} %pad_maximum_fusion.1.refs_6_), channel_id=1, source_target_pairs={{0,1},{1,0},{2,3},{3,2},{4,5},{5,4},{6,7},{7,6},{8,9},{9,8},{10,11... | collective-permute-start | bytes 786440 | tf_op jit(solution)/shard_map/weight_grad/ppermute | solution.py:444

commit v11 on v10

--- a/solution.py
+++ b/solution.py
@@ -10,6 +10,8 @@
 BF16 = jnp.bfloat16
 F32 = jnp.float32
 BOTH = ("section", "rep")
+FEATURES_ACROSS, FEATURES_ALONG = "features_xy", "features_z"
+GRADS_ACROSS, GRADS_ALONG = "grads_xy", "grads_z"
 
 
 def in_hbm(value):
@@ -465,8 +467,8 @@
 
     for pair in range(pair_count):
         even, odd = 2 * pair * Z, (2 * pair + 1) * Z
-        plan(("early", pair), [even, even + X, even + Y, odd])
-        plan(("more", pair), [even + X + Y, odd + Y])
+        plan(("early", pair), [even, even + X])
+        plan(("more", pair), [even + Y, odd, even + X + Y, odd + Y])
         plan(("late", pair), [odd + X, odd + X + Y])
         if pair == 0:
             plan(("first", pair), [odd + X + Y, even + X + Y])
@@ -477,7 +479,7 @@
             plan(("mid", pair), [even + X + Y, odd + Y, odd + X])
             plan(("last", pair), [even + X, even + Y, odd, even])
     offsets["joined"] = 2 + len(masks)
-    masks += [0, X, Y, Z, Z + X, Z + Y, X + Y, Z + X + Y, 2 * Z, 2 * Z + X, 2 * Z + Y, 3 * Z]
+    masks += [0, X, Y, Z, Z + X, Z + Y, X + Y, Z + X + Y, 2 * Z, 2 * Z + X]
     where = jnp.concatenate(
         [rep[None], section[None], section ^ jnp.array(masks, jnp.int32)]
     ).astype(jnp.int32)
@@ -514,9 +516,9 @@
         later = even + 2 * Z
         last = pair + 1 == pair_count
 
-        with jax.named_scope("features_across"):
+        with jax.named_scope(FEATURES_ACROSS):
             live["even_x"], live["even_y"] = flip(live[even], X), flip(live[even], Y)
-        with jax.named_scope("features_along_z"):
+        with jax.named_scope(FEATURES_ALONG):
             live[odd] = flip(live[even], Z)
         if pair == 0:
             build_own(0)
@@ -524,26 +526,28 @@
             two = build_others(panels // 2)
             live["others"] = [side for sides in zip(live.pop("one"), two) for side in sides]
             del live["tiles"]
+            with jax.named_scope("cotangents"):
+                live["cot"] = gather_rep(cotangent)
         if pair > 1:
-            live["total"] = forward_step(("late", pair - 1), live.pop("waiting"), live["total"])
-        close()
+            live["total"] = forward_step(("late", pair - 1), live.pop("units"), live["total"])
+        close(*(["even_x", "even_y"] if pair == 0 else []))
 
         if pair == 0:
-            with jax.named_scope("features_across"):
+            with jax.named_scope(FEATURES_ACROSS):
                 live["odd_x"], live["odd_y"] = flip(live[odd], X), flip(live[odd], Y)
             build_own(panels // 2)
         else:
-            with jax.named_scope("features_across"):
+            with jax.named_scope(FEATURES_ACROSS):
                 live["even_xy"], live["odd_y"] = flip(live["even_y"], X), flip(live[odd], Y)
-            with jax.named_scope("features_along_z"):
+            with jax.named_scope(FEATURES_ALONG):
                 live["odd_x"] = flip(live["even_x"], Z)
-            units = [live[even], live["even_x"], live["even_y"], live[odd]]
+            units = [live[even], live["even_x"]]
             if pair == 1:
-                live["total"] = forward_step("joined", live.pop("waiting") + units, None)
+                live["total"] = forward_step("joined", live.pop("units") + units, None)
             else:
                 live["total"] = forward_step(("early", pair), units, live["total"])
         if not last:
-            with jax.named_scope("features_along_z"):
+            with jax.named_scope(FEATURES_ALONG):
                 source, mask = live[later - low_bit(later)], low_bit(later)
                 live["coming"] = [flip(source[:half], mask)]
         close()
@@ -551,29 +555,26 @@
         if pair == 0:
             units = [live[even], live["even_x"], live["even_y"]]
             units += [live[odd], live["odd_x"], live["odd_y"]]
-            with jax.named_scope("features_across"):
+            with jax.named_scope(FEATURES_ACROSS):
                 units += [flip(live["even_x"], Y), flip(live["odd_y"], X)]
-            live["waiting"] = units
+            live["units"] = units
             live["one"] = build_others(0)
         else:
-            with jax.named_scope("features_across"):
+            with jax.named_scope(FEATURES_ACROSS):
                 odd_xy = [flip(live["odd_y"][:half], X), flip(live["odd_x"][half:], Y)]
-            live["waiting"] = [live["odd_x"], odd_xy]
-            units = [live.pop("even_xy"), live["odd_y"]]
+            live["units"] = [live["odd_x"], odd_xy]
+            units = [live["even_y"], live[odd], live.pop("even_xy"), live["odd_y"]]
             live["total"] = forward_step(("more", pair), units, live["total"])
         if not last:
-            with jax.named_scope("features_along_z"):
+            with jax.named_scope(FEATURES_ALONG):
                 live["coming"].append(flip(source[half:], mask))
-        else:
-            with jax.named_scope("cotangent_rows"):
-                live["cotangent"] = gather_rep(cotangent)
         for name in ("even_x", "even_y", "odd_x", "odd_y"):
             del live[name]
         close()
         if not last:
             live[later] = jnp.concatenate(live.pop("coming"))
     partial = forward_step(
-        ("late", pair_count - 1), live.pop("waiting"), live.get("total"), BF16
+        ("late", pair_count - 1), live.pop("units"), live.get("total"), BF16
     )
 
     with jax.named_scope("partial_sums"):
@@ -584,7 +585,7 @@
 
     with jax.named_scope("middle"):
         depth = n_section // 4
-        rows = (partial, other, weight, live["cotangent"])
+        rows = (partial, other, weight, live["cot"])
         grad, top_diag, end_diag, term = middle(
             where, offsets["first", pair_count - 1], *rows, live["dense"], depth
         )
@@ -603,8 +604,8 @@
             for name, count in zip(names, counts):
                 live[name], chunks = chunks[:count], chunks[count:]
 
-    steps = ["along_z", X, Y, *(-(Z << bit) for bit in reversed(range(depth.bit_length() - 1)))]
-    steps.append("between_cores")
+    steps = ["z", X, Y, *(-(Z << bit) for bit in reversed(range(depth.bit_length() - 1)))]
+    steps.append("cores")
     z_order = [0]
 
     def weight_step(after=None):
@@ -615,10 +616,10 @@
             live[after], live["term"] = lax.optimization_barrier((live[after], live["term"]))
         term = live["term"]
         with jax.named_scope("weight_grad"):
-            if step == "along_z":
+            if step == "z":
                 parts = [term[0], *(flip(term[n], Z * n) for n in range(1, depth))]
                 live["term"] = add(*parts).astype(BF16)
-            elif step == "between_cores":
+            elif step == "cores":
                 live["terms"] = [term, *(flip(term, 0, n) for n in range(1, n_rep))]
                 del live["term"]
             elif step > 0:
@@ -639,64 +640,71 @@
             mask = low_bit(even + 2 * Z)
             name = ("to", even + 2 * Z - mask, mask)
 
-        with jax.named_scope("grads_across"):
-            if pair == 0:
-                odd_diag, even_diag = live.pop("first")
-                live["odd_diag"], live["even_diag"] = flip(odd_diag, Y), flip(even_diag, X)
-            else:
+        with jax.named_scope(GRADS_ACROSS):
+            if pair > 0:
                 top_diag, end_diag = live.pop("first")
-                live["top_diag"], live["end_diag"] = flip(top_diag, X), flip(end_diag, Y)
+                live["top"], live["end"] = flip(top_diag, X), flip(end_diag, Y)
         if not top:
-            with jax.named_scope("grads_along_z"):
+            with jax.named_scope(GRADS_ALONG):
                 live[name] = [flip(live["passed"][0], mask)]
         backward_step(pair, "even" if pair == 0 else "mid")
         weight_step(None if top else "even" if pair == 0 else "mid")
-        close()
+        with jax.named_scope(GRADS_ACROSS):
+            if pair == 0:
+                to_x, to_y, own = live.pop("odd")
+                live["odd"], live["ahead"] = [to_x, own], flip(to_y, Y)
+            else:
+                even_xy, *live["mid"] = live["mid"]
+                live["ahead"] = flip(even_xy, X)
+        close("ahead")
 
         if pair == 0:
-            with jax.named_scope("grads_across"):
-                to_x, to_y, own = live.pop("odd")
-                to_x = add(to_x, live.pop("odd_diag")).astype(BF16)
-                live["odd_sum"] = [own, flip(to_x, X), flip(to_y, Y)]
+            with jax.named_scope(GRADS_ACROSS):
+                to_x, own = live.pop("odd")
+                to_x = add(to_x, live.pop("o_diag")).astype(BF16)
+                live["odd_sum"] = [own, flip(to_x, X), live.pop("ahead")]
                 to_x, to_y, own = live.pop("even")
-                live["even"] = [to_x, add(to_y, live.pop("even_diag")).astype(BF16), own]
+                to_y = add(to_y, live.pop("e_diag")).astype(BF16)
+                live["sums"] = [own, flip(to_x, X), flip(to_y, Y)]
         else:
-            with jax.named_scope("grads_across"):
-                even_xy, odd_y, odd_x = live.pop("mid")
-                live["to_even_y"] = flip(even_xy, X)
+            with jax.named_scope(GRADS_ACROSS):
+                odd_y, odd_x = live.pop("mid")
+                live["to_y"] = live.pop("ahead")
                 odd_y, odd_x = add_diagonals(
-                    odd_y, odd_x, live.pop("top_diag"), live.pop("end_diag")
+                    odd_y, odd_x, live.pop("top"), live.pop("end")
                 )
                 live["to_odd"] = flip(odd_y, Y)
-            with jax.named_scope("grads_along_z"):
-                live["to_even_x"] = flip(odd_x, Z)
+            with jax.named_scope(GRADS_ALONG):
+                live["to_x"] = flip(odd_x, Z)
             backward_step(pair, "last")
         if not top:
-            with jax.named_scope("grads_along_z"):
+            with jax.named_scope(GRADS_ALONG):
                 live[name].append(flip(live.pop("passed")[1], mask))
         weight_step("last" if pair else None)
-        close()
+        close(*([] if pair else ["sums"]))
 
         if pair == 0:
-            with jax.named_scope("grads_across"):
-                to_x, to_y, own = live.pop("even")
-                sums = [own, flip(to_x, X), flip(to_y, Y)]
-            with jax.named_scope("grads_along_z"):
+            sums = live["sums"]
+            with jax.named_scope(GRADS_ALONG):
                 sums.append(flip(add(*live.pop("odd_sum")).astype(BF16), Z))
             with jax.named_scope("activated"):
                 live["activated"] = activated_rows(where, *rows, n_rep)
         else:
             to_x, to_y, odd, own = live.pop("last")
-            with jax.named_scope("grads_across"):
-                to_x = add(to_x, live.pop("to_even_x")).astype(BF16)
-                to_y = add(to_y, live.pop("to_even_y")).astype(BF16)
+            with jax.named_scope(GRADS_ACROSS):
+                to_x = add(to_x, live.pop("to_x")).astype(BF16)
+                to_y = add(to_y, live.pop("to_y")).astype(BF16)
                 sums = [own, flip(to_x, X), flip(to_y, Y)]
-            with jax.named_scope("grads_along_z"):
+            with jax.named_scope(GRADS_ALONG):
                 sums.append(flip(add(odd, live.pop("to_odd")).astype(BF16), Z))
             backward_step(pair - 1, "first", *([] if pair > 1 else ["odd"]))
         live["sums"] = sums
         weight_step("first" if pair else None)
-        close()
+        if pair == 1:
+            with jax.named_scope(GRADS_ACROSS):
+                odd_diag, even_diag = live.pop("first")
+                live["o_diag"], live["e_diag"] = flip(odd_diag, Y), flip(even_diag, X)
+        close("o_diag", "e_diag")
         sums = live.pop("sums")
         halves = [live.pop(key) for key in list(live) if isinstance(key, tuple) and key[1] == even]
         if pair > 0:

time: 186 us -> 184 us (0.989)
  waiting for transfers between devices: 54.4 us -> 50.1 us
  starting transfers between devices: 45 us -> 48 us
    ppermute x46, waiting for transfers between devices: 54.4 us -> 50.1 us  [flip(): return lax.ppermute(value, BOTH, pairs)]
    ppermute x46, starting transfers between devices: 45 us -> 48 us  [flip(): return lax.ppermute(value, BOTH, pairs)]
  transfers between devices with their start and end apart: 46 -> 46, of which waited for: 19 -> 20; matrix products, arithmetic and copies ran while one was open for 3% -> 3% of each run, Pallas kernels for 36% -> 36%
where the time goes in v11:
time: 184 us; the launch traced here: 182 us
  Pallas kernels  77.4 us (42%)
  waiting for transfers between devices  50.1 us (27%)
  starting transfers between devices  48 us (26%)
  other arithmetic  4.16 us (2%)
    ppermute x46, waiting for transfers between devices, flip(): return lax.ppermute(value, BOTH, pairs)  50.1 us
    ppermute x46, starting transfers between devices, flip(): return lax.ppermute(value, BOTH, pairs)  48 us
    pallas_call x4, Pallas kernels, backward_part(): pl.pallas_call(backward_kernel, out_shape=[jax.ShapeDtypeStruct((width, c...  21.4 us
    pallas_call x3, Pallas kernels, forward_part(): pl.pallas_call(functools.partial(forward_kernel, offset, n_pieces, n_othe...  18 us
    pallas_call x2, Pallas kernels, make_dense(): pl.pallas_call(functools.partial(dense_kernel, first), out_shape=pltpu.HB...  14.6 us
    pallas_call x2, Pallas kernels, make_other(): pl.pallas_call(functools.partial(other_kernel, first), out_shape=pltpu.HB...  12.7 us
    pallas_call x1, Pallas kernels, middle(): pl.pallas_call(functools.partial(middle_kernel, blocks), out_shape=[jax.S...  6.49 us
  transfers between devices with their start and end apart: 46, of which 20 were waited for; matrix products, arithmetic and copies ran while one was open for 3% of the time, Pallas kernels for 36%

profile of v11, /device:TPU:0, one launch (start us, length us, event | category | flops | bytes accessed | tf_op | source)
XLA Modules:
  0.0 182.2 jit_solution(7742261007281083289)
XLA Ops:
  1.9 3.1 %collective-permute-start.2 = (bf16[512,512]{1,0:T(8,128)(2,1)S(1)}, bf16[512,512]{1,0:T(8,128)(2,1)S(1)}, u32[]{:S(2)}, u32[]{:S(2)}) collective-permute-start(bf16[512,512]{1,0:T(8,128)(2,1)S(1)} %constant_dynamic-slice_fusion.refs_2_), channel_id=1, source_target_pairs={{0,8},{1,9},{2,10},{3,11},{4,12},{5,13},{6,14},{7,15},{8,0},{9,1},... | collective-permute-start | bytes 1572872 | tf_op jit(solution)/shard_map/features_z/ppermute | solution.py:446
  5.0 1.5 collective-permute-start.3
  6.5 1.5 collective-permute-start.4
  8.0 0.7 add_bitcast_fusion
  8.7 0.7 copy.12
  10.3 7.2 %dense_blocks.2.refs_0_ = bf16[2,8,1024,512]{3,2,1,0:T(8,128)(2,1)} custom-call(s32[44]{0:T(128)S(1)} %pad_add_fusion.1.where_ref, s32[8,25]{1,0:T(8,128)S(1)} %pad_add_fusion.packed_ref, bf16[8,24,128,128]{3,2,1,0:T(8,128)(2,1)} %bitcast.17), custom_call_target="tpu_custom_call" | custom-call | bytes 393216 | tf_op jit(solution)/shard_map/dense_blocks/pallas_call | solution.py:44
  17.5 1.1 collective-permute-start.5
  18.6 1.5 collective-permute-start.6
  20.1 2.7 %collective-permute-start.7 = (bf16[256,512]{1,0:T(8,128)(2,1)S(1)}, bf16[256,512]{1,0:T(8,128)(2,1)S(1)}, u32[]{:S(2)}, u32[]{:S(2)}) collective-permute-start(bf16[256,512]{1,0:T(8,128)(2,1)S(1)} %get-tuple-element.308), channel_id=1, source_target_pairs={{0,16},{1,17},{2,18},{3,19},{4,20},{5,21},{6,22},{7,23},{8,24},{9,... | collective-permute-start | bytes 786440 | tf_op jit(solution)/shard_map/features_z/ppermute | solution.py:446
  22.8 7.4 %dense_blocks.3.dense_ref.a_ref = bf16[2,8,1024,512]{3,2,1,0:T(8,128)(2,1)} custom-call(s32[44]{0:T(128)S(1)} %pad_add_fusion.1.where_ref, s32[8,25]{1,0:T(8,128)S(1)} %pad_add_fusion.packed_ref, bf16[8,24,128,128]{3,2,1,0:T(8,128)(2,1)} %bitcast.18, bf16[2,8,1024,512]{3,2,1,0:T(8,128)(2,1)} %dense_blocks.2.refs_0_), custom_call_target="tpu_custom_call", output_to_operand_aliasing={{}: (3, {})} | custom-call | bytes 393216 | tf_op jit(solution)/shard_map/dense_blocks/pallas_call | solution.py:44
  30.2 3.2 %collective-permute-done.7 = bf16[256,512]{1,0:T(8,128)(2,1)S(1)} collective-permute-done((bf16[256,512]{1,0:T(8,128)(2,1)S(1)}, bf16[256,512]{1,0:T(8,128)(2,1)S(1)}, u32[]{:S(2)}, u32[]{:S(2)}) %collective-permute-start.7) | collective-permute-done | bytes 262176 | tf_op jit(solution)/shard_map/features_z/ppermute | solution.py:446
  33.4 1.7 collective-permute-start.10
  35.1 1.3 collective-permute-start.9
  36.5 6.6 %other_blocks.2.refs_0_ = bf16[4,1024,512]{2,1,0:T(8,128)(2,1)} custom-call(s32[44]{0:T(128)S(1)} %pad_add_fusion.1.where_ref, s32[8,25]{1,0:T(8,128)S(1)} %collective-permute-done.1.packed_ref, bf16[8,24,128,128]{3,2,1,0:T(8,128)(2,1)} %collective-permute-done.tiles_ref), custom_call_target="tpu_custom_call" | custom-call | bytes 393216 | tf_op jit(solution)/shard_map/other_blocks/pallas_call | solution.py:89
  43.2 6.7 %collective-permute-done.8 = bf16[256,512]{1,0:T(8,128)(2,1)S(1)} collective-permute-done((bf16[256,512]{1,0:T(8,128)(2,1)S(1)}, bf16[256,512]{1,0:T(8,128)(2,1)S(1)}, u32[]{:S(2)}, u32[]{:S(2)}) %collective-permute-start.8) | collective-permute-done | bytes 262176 | tf_op jit(solution)/shard_map/features_z/ppermute | solution.py:446
  49.9 0.9 collective-permute-start.11
  50.9 0.9 collective-permute-start.12
  51.8 1.3 broadcast_select_fusion.1
  53.2 6.1 %other_blocks.3.refs_1_ = bf16[4,1024,512]{2,1,0:T(8,128)(2,1)} custom-call(s32[44]{0:T(128)S(1)} %pad_add_fusion.1.where_ref, s32[8,25]{1,0:T(8,128)S(1)} %collective-permute-done.1.packed_ref, bf16[8,24,128,128]{3,2,1,0:T(8,128)(2,1)} %collective-permute-done.tiles_ref), custom_call_target="tpu_custom_call" | custom-call | bytes 393216 | tf_op jit(solution)/shard_map/other_blocks/pallas_call | solution.py:89
  59.3 4.6 %collective-permute-done.11.refs_11_ = bf16[512,512]{1,0:T(8,128)(2,1)} collective-permute-done((bf16[512,512]{1,0:T(8,128)(2,1)S(1)}, bf16[512,512]{1,0:T(8,128)(2,1)}, u32[]{:S(2)}, u32[]{:S(2)}) %collective-permute-start.11) | collective-permute-done | bytes 524320 | tf_op jit(solution)/shard_map/features_xy/ppermute | solution.py:446
  64.6 0.9 collective-permute-done.13.refs_3_
  65.5 1.1 collective-permute-start.15
  66.6 0.9 collective-permute-start.16
  67.7 9.4 %forward.3.refs_6_ = f32[1024,512]{1,0:T(8,128)S(1)} custom-call(s32[44]{0:T(128)S(1)} %pad_add_fusion.1.where_ref, bf16[2,8,1024,512]{3,2,1,0:T(8,128)(2,1)} %dense_blocks.3.dense_ref.a_ref, bf16[4,1024,512]{2,1,0:T(8,128)(2,1)} %other_blocks.2.refs_0_, bf16[4,1024,512]{2,1,0:T(8,128)(2,1)} %other_blocks.3.refs_1_, ...), custom_call_target="tpu_custom_call" | custom-call | flops 5368709120 | bytes 14680064 | tf_op jit(solution)/shard_map/forward/pallas_call | solution.py:192
  77.2 1.2 collective-permute-done.15.refs_4_
  79.5 1.1 collective-permute-start.18
  80.6 1.5 collective-permute-start.19
  82.0 5.2 %forward.4.refs_5_ = f32[1024,512]{1,0:T(8,128)S(1)} custom-call(s32[44]{0:T(128)S(1)} %pad_add_fusion.1.where_ref, bf16[2,8,1024,512]{3,2,1,0:T(8,128)(2,1)} %dense_blocks.3.dense_ref.a_ref, bf16[4,1024,512]{2,1,0:T(8,128)(2,1)} %other_blocks.2.refs_0_, bf16[4,1024,512]{2,1,0:T(8,128)(2,1)} %other_blocks.3.refs_1_, ...), custom_call_target="tpu_custom_call" | custom-call | flops 2147483648 | bytes 8388608 | tf_op jit(solution)/shard_map/forward/pallas_call | solution.py:192
  87.2 3.5 %forward.5.mine_ref = bf16[1024,512]{1,0:T(8,128)(2,1)S(1)} custom-call(s32[44]{0:T(128)S(1)} %pad_add_fusion.1.where_ref, bf16[2,8,1024,512]{3,2,1,0:T(8,128)(2,1)} %dense_blocks.3.dense_ref.a_ref, bf16[4,1024,512]{2,1,0:T(8,128)(2,1)} %other_blocks.2.refs_0_, bf16[4,1024,512]{2,1,0:T(8,128)(2,1)} %other_blocks.3.refs_1_, ...), custom_call_target="tpu_custom_call" | custom-call | flops 1073741824 | bytes 6291456 | tf_op jit(solution)/shard_map/forward/pallas_call | solution.py:192
  90.8 2.6 %collective-permute-done.20.other_ref = bf16[1024,512]{1,0:T(8,128)(2,1)S(1)} collective-permute-done((bf16[1024,512]{1,0:T(8,128)(2,1)S(1)}, bf16[1024,512]{1,0:T(8,128)(2,1)S(1)}, u32[]{:S(2)}, u32[]{:S(2)}) %collective-permute-start.20) | collective-permute-done | bytes 1048608 | tf_op jit(solution)/shard_map/partial_sums/ppermute | solution.py:446
  93.4 6.5 %middle.1 = (bf16[512,1024]{1,0:T(8,128)(2,1)S(1)}, bf16[256,512]{1,0:T(8,128)(2,1)S(1)}, bf16[256,512]{1,0:T(8,128)(2,1)S(1)}, bf16[4,64,512]{2,1,0:T(8,128)(2,1)S(1)}) custom-call(s32[44]{0:T(128)S(1)} %pad_add_fusion.1.where_ref, bf16[1024,512]{1,0:T(8,128)(2,1)S(1)} %forward.5.mine_ref, bf16[1024,512]{1,0:T(8,128)(2,1)S(1)} %collective-permute-done.20.other_ref, ...), custom_call_target="tpu_custom_call" | custom-call | flops 2684354560 | bytes 6291456 | tf_op jit(solution)/shard_map/middle/pallas_call | solution.py:277
  100.6 1.9 %collective-permute-start.22 = (bf16[64,512]{1,0:T(8,128)(2,1)S(1)}, bf16[64,512]{1,0:T(8,128)(2,1)S(1)}, u32[]{:S(2)}, u32[]{:S(2)}) collective-permute-start(bf16[64,512]{1,0:T(8,128)(2,1)S(1)} %get-tuple-element.311), channel_id=1, source_target_pairs={{0,16},{1,17},{2,18},{3,19},{4,20},{5,21},{6,22},{7,23},{8,24},{9,... | collective-permute-start | bytes 196616 | tf_op jit(solution)/shard_map/weight_grad/ppermute | solution.py:446
  102.5 1.9 %collective-permute-start.23 = (bf16[64,512]{1,0:T(8,128)(2,1)S(1)}, bf16[64,512]{1,0:T(8,128)(2,1)S(1)}, u32[]{:S(2)}, u32[]{:S(2)}) collective-permute-start(bf16[64,512]{1,0:T(8,128)(2,1)S(1)} %get-tuple-element.310), channel_id=1, source_target_pairs={{0,24},{1,25},{2,26},{3,27},{4,28},{5,29},{6,30},{7,31},{8,16},{9,... | collective-permute-start | bytes 196616 | tf_op jit(solution)/shard_map/weight_grad/ppermute | solution.py:446
  104.4 0.8 collective-permute-start.24
  105.2 1.1 collective-permute-start.25
  106.4 4.6 %backward.4 = (bf16[512,512]{1,0:T(8,128)(2,1)S(1)}, bf16[512,512]{1,0:T(8,128)(2,1)S(1)}, bf16[512,512]{1,0:T(8,128)(2,1)S(1)}) custom-call(s32[44]{0:T(128)S(1)} %pad_add_fusion.1.where_ref, bf16[512,1024]{1,0:T(8,128)(2,1)S(1)} %get-tuple-element.257.grad_ref, bf16[2,8,1024,512]{3,2,1,0:T(8,128)(2,1)} %dense_blocks.3.dense_ref.a_ref), custom_call_target="tpu_custom_call" | custom-call | flops 1610612736 | bytes 5767168 | tf_op jit(solution)/shard_map/backward/pallas_call | solution.py:350
  111.0 1.3 collective-permute-start.27
  112.6 1.2 collective-permute-start.28
  113.8 5.5 %backward.5 = (bf16[512,512]{1,0:T(8,128)(2,1)S(1)}, bf16[512,512]{1,0:T(8,128)(2,1)S(1)}, bf16[512,512]{1,0:T(8,128)(2,1)S(1)}, bf16[512,512]{1,0:T(8,128)(2,1)S(1)}) custom-call(s32[44]{0:T(128)S(1)} %pad_add_fusion.1.where_ref, bf16[512,1024]{1,0:T(8,128)(2,1)S(1)} %get-tuple-element.257.grad_ref, bf16[2,8,1024,512]{3,2,1,0:T(8,128)(2,1)} %dense_blocks.3.dense_ref.a_ref), custom_call_target="tpu_custom_call" | custom-call | flops 2147483648 | bytes 7340032 | tf_op jit(solution)/shard_map/backward/pallas_call | solution.py:350
  119.3 1.3 collective-permute-start.26
  120.6 4.4 %collective-permute-done.26 = bf16[64,512]{1,0:T(8,128)(2,1)S(1)} collective-permute-done((bf16[64,512]{1,0:T(8,128)(2,1)S(1)}, bf16[64,512]{1,0:T(8,128)(2,1)S(1)}, u32[]{:S(2)}, u32[]{:S(2)}) %collective-permute-start.26) | collective-permute-done | bytes 65568 | tf_op jit(solution)/shard_map/weight_grad/ppermute | solution.py:446
  126.1 1.2 collective-permute-start.32
  127.5 1.0 collective-permute-start.31
  128.5 6.7 %backward.6 = (bf16[512,512]{1,0:T(8,128)(2,1)S(1)}, bf16[512,512]{1,0:T(8,128)(2,1)S(1)}, bf16[512,512]{1,0:T(8,128)(2,1)S(1)}, bf16[512,512]{1,0:T(8,128)(2,1)S(1)}, bf16[512,512]{1,0:T(8,128)(2,1)S(1)}) custom-call(s32[44]{0:T(128)S(1)} %pad_add_fusion.1.where_ref, bf16[512,1024]{1,0:T(8,128)(2,1)S(1)} %get-tuple-element.257.grad_ref, ...), custom_call_target="tpu_custom_call" | custom-call | flops 2684354560 | bytes 8912896 | tf_op jit(solution)/shard_map/backward/pallas_call | solution.py:350
  135.1 1.2 collective-permute-start.30
  136.4 0.9 collective-permute-start.35
  137.2 4.0 %collective-permute-done.30 = bf16[64,512]{1,0:T(8,128)(2,1)S(1)} collective-permute-done((bf16[64,512]{1,0:T(8,128)(2,1)S(1)}, bf16[64,512]{1,0:T(8,128)(2,1)S(1)}, u32[]{:S(2)}, u32[]{:S(2)}) %collective-permute-start.30) | collective-permute-done | bytes 65568 | tf_op jit(solution)/shard_map/weight_grad/ppermute | solution.py:446
  141.3 1.3 collective-permute-start.36
  142.9 2.1 %collective-permute-start.37 = (bf16[256,512]{1,0:T(8,128)(2,1)S(1)}, bf16[256,512]{1,0:T(8,128)(2,1)S(1)}, u32[]{:S(2)}, u32[]{:S(2)}) collective-permute-start(bf16[256,512]{1,0:T(8,128)(2,1)S(1)} %get-tuple-element.304), channel_id=1, source_target_pairs={{0,16},{1,17},{2,18},{3,19},{4,20},{5,21},{6,22},{7,23},{8,24},{9,... | collective-permute-start | bytes 786440 | tf_op jit(solution)/shard_map/grads_z/ppermute | solution.py:446
  145.1 4.6 %backward.7 = (bf16[512,512]{1,0:T(8,128)(2,1)S(1)}, bf16[512,512]{1,0:T(8,128)(2,1)S(1)}, bf16[512,512]{1,0:T(8,128)(2,1)S(1)}) custom-call(s32[44]{0:T(128)S(1)} %pad_add_fusion.1.where_ref, bf16[512,1024]{1,0:T(8,128)(2,1)S(1)} %get-tuple-element.257.grad_ref, bf16[2,8,1024,512]{3,2,1,0:T(8,128)(2,1)} %dense_blocks.3.dense_ref.a_ref), custom_call_target="tpu_custom_call" | custom-call | flops 1610612736 | bytes 5767168 | tf_op jit(solution)/shard_map/backward/pallas_call | solution.py:350
  149.7 0.9 collective-permute-start.34
  150.6 0.8 collective-permute-start.41
  151.4 3.8 %collective-permute-done.34 = bf16[1,64,512]{2,1,0:T(8,128)(2,1)S(1)} collective-permute-done((bf16[1,64,512]{2,1,0:T(8,128)(2,1)S(1)}, bf16[1,64,512]{2,1,0:T(8,128)(2,1)S(1)}, u32[]{:S(2)}, u32[]{:S(2)}) %collective-permute-start.34) | collective-permute-done | bytes 65568 | tf_op jit(solution)/shard_map/weight_grad/ppermute | solution.py:446
  155.5 1.2 collective-permute-start.40
  156.7 2.4 %collective-permute-start.39 = (bf16[256,512]{1,0:T(8,128)(2,1)S(1)}, bf16[256,512]{1,0:T(8,128)(2,1)S(1)}, u32[]{:S(2)}, u32[]{:S(2)}) collective-permute-start(bf16[256,512]{1,0:T(8,128)(2,1)S(1)} %get-tuple-element.277), channel_id=1, source_target_pairs={{0,16},{1,17},{2,18},{3,19},{4,20},{5,21},{6,22},{7,23},{8,24},{9,... | collective-permute-start | bytes 786440 | tf_op jit(solution)/shard_map/grads_z/ppermute | solution.py:446
  159.3 1.1 collective-permute-start.43
  160.4 3.4 %collective-permute-done.38 = bf16[2,64,512]{2,1,0:T(8,128)(2,1)S(1)} collective-permute-done((bf16[2,64,512]{2,1,0:T(8,128)(2,1)S(1)}, bf16[2,64,512]{2,1,0:T(8,128)(2,1)S(1)}, u32[]{:S(2)}, u32[]{:S(2)}) %collective-permute-start.38) | collective-permute-done | bytes 131104 | tf_op jit(solution)/shard_map/weight_grad/ppermute | solution.py:446
  163.8 1.2 collective-permute-start.42
  165.0 2.8 %collective-permute-done.39.refs_5_ = bf16[256,512]{1,0:T(8,128)(2,1)S(1)} collective-permute-done((bf16[256,512]{1,0:T(8,128)(2,1)S(1)}, bf16[256,512]{1,0:T(8,128)(2,1)S(1)}, u32[]{:S(2)}, u32[]{:S(2)}) %collective-permute-start.39) | collective-permute-done | bytes 262176 | tf_op jit(solution)/shard_map/grads_z/ppermute | solution.py:446
  167.8 1.9 %collective-permute-done.40 = bf16[512,512]{1,0:T(8,128)(2,1)S(1)} collective-permute-done((bf16[512,512]{1,0:T(8,128)(2,1)S(1)}, bf16[512,512]{1,0:T(8,128)(2,1)S(1)}, u32[]{:S(2)}, u32[]{:S(2)}) %collective-permute-start.40) | collective-permute-done | bytes 524320 | tf_op jit(solution)/shard_map/grads_xy/ppermute | solution.py:446
  170.0 1.9 %activated.1 = bf16[512,512]{1,0:T(8,128)(2,1)} custom-call(s32[44]{0:T(128)S(1)} %pad_add_fusion.1.where_ref, bf16[1024,512]{1,0:T(8,128)(2,1)S(1)} %forward.5.mine_ref, bf16[1024,512]{1,0:T(8,128)(2,1)S(1)} %collective-permute-done.20.other_ref, bf16[512,512]{1,0:T(8,128)(2,1)S(1)} %copy-done.2, bf16[1024,512]{1,0:T(8,128)(2,1)S(1)} %pad_maximum_fusion.cot_ref), custom_call_target="tpu_custom_call" | custom-call | flops 268435456 | bytes 2097152 | tf_op jit(solution)/shard_map/activated/pallas_call | solution.py:314
  172.3 4.3 %collective-permute-done.42.refs_1_ = bf16[512,512]{1,0:T(8,128)(2,1)S(1)} collective-permute-done((bf16[512,512]{1,0:T(8,128)(2,1)S(1)}, bf16[512,512]{1,0:T(8,128)(2,1)S(1)}, u32[]{:S(2)}, u32[]{:S(2)}) %collective-permute-start.42) | collective-permute-done | bytes 524320 | tf_op jit(solution)/shard_map/grads_xy/ppermute | solution.py:446
  176.6 3.5 %collective-permute-done.44.refs_3_ = bf16[512,512]{1,0:T(8,128)(2,1)S(1)} collective-permute-done((bf16[512,512]{1,0:T(8,128)(2,1)S(1)}, bf16[512,512]{1,0:T(8,128)(2,1)S(1)}, u32[]{:S(2)}, u32[]{:S(2)}) %collective-permute-start.44) | collective-permute-done | bytes 524320 | tf_op jit(solution)/shard_map/grads_z/ppermute | solution.py:446
  180.1 2.1 %grads_out.1 = (bf16[1,512,512]{2,1,0:T(8,128)(2,1)}, f32[512,512]{1,0:T(8,128)}) custom-call(s32[44]{0:T(128)S(1)} %pad_add_fusion.1.where_ref, bf16[512,512]{1,0:T(8,128)(2,1)S(1)} %get-tuple-element.293.refs_0_, bf16[512,512]{1,0:T(8,128)(2,1)S(1)} %collective-permute-done.42.refs_1_, bf16[512,512]{1,0:T(8,128)(2,1)S(1)} %collective-permute-done.43.refs_2_, ...), custom_call_target="tpu_custom_call" | custom-call | flops 1048576 | bytes 2621440 | tf_op jit(solution)/shard_map/grads_out/pallas_call | solution.py:412
  (87 shorter events, 8.1 us)
Async XLA Ops:
  0.6 1.2 copy-start
  0.6 16.8 %collective-permute-start = (bf16[8,24,128,128]{3,2,1,0:T(8,128)(2,1)}, bf16[8,24,128,128]{3,2,1,0:T(8,128)(2,1)}, u32[]{:S(2)}, u32[]{:S(2)}) collective-permute-start(bf16[8,24,128,128]{3,2,1,0:T(8,128)(2,1)} %bitcast.16), channel_id=1, source_target_pairs={{0,1},{1,0},{2,3},{3,2},{4,5},{5,4},{6,7},{7,6},{8,9},{9,8},{10,11... | collective-permute-start | bytes 18874376 | tf_op jit(solution)/shard_map/tiles_exchange/ppermute | solution.py:446
  1.9 15.6 %collective-permute-start.2 = (bf16[512,512]{1,0:T(8,128)(2,1)S(1)}, bf16[512,512]{1,0:T(8,128)(2,1)S(1)}, u32[]{:S(2)}, u32[]{:S(2)}) collective-permute-start(bf16[512,512]{1,0:T(8,128)(2,1)S(1)} %constant_dynamic-slice_fusion.refs_2_), channel_id=1, source_target_pairs={{0,8},{1,9},{2,10},{3,11},{4,12},{5,13},{6,14},{7,15},{8,0},{9,1},... | collective-permute-start | bytes 1572872 | tf_op jit(solution)/shard_map/features_z/ppermute | solution.py:446
  5.0 25.2 %collective-permute-start.3 = (bf16[512,512]{1,0:T(8,128)(2,1)S(1)}, bf16[512,512]{1,0:T(8,128)(2,1)S(1)}, u32[]{:S(2)}, u32[]{:S(2)}) collective-permute-start(bf16[512,512]{1,0:T(8,128)(2,1)S(1)} %constant_dynamic-slice_fusion.refs_2_), channel_id=1, source_target_pairs={{0,2},{1,3},{2,0},{3,1},{4,6},{5,7},{6,4},{7,5},{8,10},{9,11},{10,... | collective-permute-start | bytes 1572872 | tf_op jit(solution)/shard_map/features_xy/ppermute | solution.py:446
  6.5 23.7 %collective-permute-start.4 = (bf16[512,512]{1,0:T(8,128)(2,1)S(1)}, bf16[512,512]{1,0:T(8,128)(2,1)S(1)}, u32[]{:S(2)}, u32[]{:S(2)}) collective-permute-start(bf16[512,512]{1,0:T(8,128)(2,1)S(1)} %constant_dynamic-slice_fusion.refs_2_), channel_id=1, source_target_pairs={{0,4},{1,5},{2,6},{3,7},{4,0},{5,1},{6,2},{7,3},{8,12},{9,13},{10,... | collective-permute-start | bytes 1572872 | tf_op jit(solution)/shard_map/features_xy/ppermute | solution.py:446
  9.5 8.0 %collective-permute-start.1 = (s32[8,25]{1,0:T(8,128)S(1)}, s32[8,25]{1,0:T(8,128)S(1)}, u32[]{:S(2)}, u32[]{:S(2)}) collective-permute-start(s32[8,25]{1,0:T(8,128)S(1)} %pad_add_fusion.packed_ref), channel_id=1, source_target_pairs={{0,1},{1,0},{2,3},{3,2},{4,5},{5,4},{6,7},{7,6},{8,9},{9,8},{10,11... | collective-permute-start | bytes 2408 | tf_op jit(solution)/shard_map/tiles_exchange/ppermute | solution.py:446
  17.5 15.9 %collective-permute-start.5 = (bf16[512,512]{1,0:T(8,128)(2,1)S(1)}, bf16[512,512]{1,0:T(8,128)(2,1)S(1)}, u32[]{:S(2)}, u32[]{:S(2)}) collective-permute-start(bf16[512,512]{1,0:T(8,128)(2,1)S(1)} %collective-permute-done.2.refs_5_), channel_id=1, source_target_pairs={{0,2},{1,3},{2,0},{3,1},{4,6},{5,7},{6,4},{7,5},{8,10},{9,11},{10,... | collective-permute-start | bytes 1572872 | tf_op jit(solution)/shard_map/features_xy/ppermute | solution.py:446
  18.6 14.8 %collective-permute-start.6 = (bf16[512,512]{1,0:T(8,128)(2,1)S(1)}, bf16[512,512]{1,0:T(8,128)(2,1)S(1)}, u32[]{:S(2)}, u32[]{:S(2)}) collective-permute-start(bf16[512,512]{1,0:T(8,128)(2,1)S(1)} %collective-permute-done.2.refs_5_), channel_id=1, source_target_pairs={{0,4},{1,5},{2,6},{3,7},{4,0},{5,1},{6,2},{7,3},{8,12},{9,13},{10,... | collective-permute-start | bytes 1572872 | tf_op jit(solution)/shard_map/features_xy/ppermute | solution.py:446
  20.1 13.3 %collective-permute-start.7 = (bf16[256,512]{1,0:T(8,128)(2,1)S(1)}, bf16[256,512]{1,0:T(8,128)(2,1)S(1)}, u32[]{:S(2)}, u32[]{:S(2)}) collective-permute-start(bf16[256,512]{1,0:T(8,128)(2,1)S(1)} %get-tuple-element.308), channel_id=1, source_target_pairs={{0,16},{1,17},{2,18},{3,19},{4,20},{5,21},{6,22},{7,23},{8,24},{9,... | collective-permute-start | bytes 786440 | tf_op jit(solution)/shard_map/features_z/ppermute | solution.py:446
  33.4 9.8 %copy-start.3 = (bf16[512,512]{1,0:T(8,128)(2,1)}, bf16[512,512]{1,0:T(8,128)(2,1)S(1)}, u32[]{:S(2)}) copy-start(bf16[512,512]{1,0:T(8,128)(2,1)S(1)} %collective-permute-done.6.refs_7_) | copy-start | bytes 1572868
  33.4 16.5 %collective-permute-start.10 = (bf16[512,512]{1,0:T(8,128)(2,1)S(1)}, bf16[512,512]{1,0:T(8,128)(2,1)S(1)}, u32[]{:S(2)}, u32[]{:S(2)}) collective-permute-start(bf16[512,512]{1,0:T(8,128)(2,1)S(1)} %collective-permute-done.6.refs_7_), channel_id=1, source_target_pairs={{0,2},{1,3},{2,0},{3,1},{4,6},{5,7},{6,4},{7,5},{8,10},{9,11},{10,... | collective-permute-start | bytes 1572872 | tf_op jit(solution)/shard_map/features_xy/ppermute | solution.py:446
  35.1 14.7 %collective-permute-start.9 = (bf16[512,512]{1,0:T(8,128)(2,1)S(1)}, bf16[512,512]{1,0:T(8,128)(2,1)S(1)}, u32[]{:S(2)}, u32[]{:S(2)}) collective-permute-start(bf16[512,512]{1,0:T(8,128)(2,1)S(1)} %collective-permute-done.3.refs_3_), channel_id=1, source_target_pairs={{0,4},{1,5},{2,6},{3,7},{4,0},{5,1},{6,2},{7,3},{8,12},{9,13},{10,... | collective-permute-start | bytes 1572872 | tf_op jit(solution)/shard_map/features_xy/ppermute | solution.py:446
  36.4 13.5 %collective-permute-start.8 = (bf16[256,512]{1,0:T(8,128)(2,1)S(1)}, bf16[256,512]{1,0:T(8,128)(2,1)S(1)}, u32[]{:S(2)}, u32[]{:S(2)}) collective-permute-start(bf16[256,512]{1,0:T(8,128)(2,1)S(1)} %get-tuple-element.307), channel_id=1, source_target_pairs={{0,16},{1,17},{2,18},{3,19},{4,20},{5,21},{6,22},{7,23},{8,24},{9,... | collective-permute-start | bytes 786440 | tf_op jit(solution)/shard_map/features_z/ppermute | solution.py:446
  36.5 15.3 %collective-permute-start.14 = (bf16[512,512]{1,0:T(8,128)(2,1)}, bf16[512,512]{1,0:T(8,128)(2,1)}, u32[]{:S(2)}, u32[]{:S(2)}) collective-permute-start(bf16[512,512]{1,0:T(8,128)(2,1)} %param.14), channel_id=1, source_target_pairs={{0,1},{1,0},{2,3},{3,2},{4,5},{5,4},{6,7},{7,6},{8,9},{9,8},{10,11... | collective-permute-start | bytes 1572872 | tf_op jit(solution)/shard_map/cotangents/ppermute | solution.py:446
  49.9 1.0 copy-start.5
  49.9 1.9 %copy-start.7 = (bf16[512,512]{1,0:T(8,128)(2,1)}, bf16[512,512]{1,0:T(8,128)(2,1)S(1)}, u32[]{:S(2)}) copy-start(bf16[512,512]{1,0:T(8,128)(2,1)S(1)} %collective-permute-done.9.refs_8_) | copy-start | bytes 1572868
  49.9 14.0 %collective-permute-start.11 = (bf16[512,512]{1,0:T(8,128)(2,1)S(1)}, bf16[512,512]{1,0:T(8,128)(2,1)}, u32[]{:S(2)}, u32[]{:S(2)}) collective-permute-start(bf16[512,512]{1,0:T(8,128)(2,1)S(1)} %constant_dynamic-update-slice_fusion.refs_10_), channel_id=1, source_target_pairs={{0,2},{1,3},{2,0},{3,1},{4,6},{5,7},{6,4},{7,5},{8,10},{9,11},{10,... | collective-permute-start | bytes 1572872 | tf_op jit(solution)/shard_map/features_xy/ppermute | solution.py:446
  50.9 13.7 %collective-permute-start.12 = (bf16[512,512]{1,0:T(8,128)(2,1)S(1)}, bf16[512,512]{1,0:T(8,128)(2,1)}, u32[]{:S(2)}, u32[]{:S(2)}) collective-permute-start(bf16[512,512]{1,0:T(8,128)(2,1)S(1)} %constant_dynamic-update-slice_fusion.refs_10_), channel_id=1, source_target_pairs={{0,4},{1,5},{2,6},{3,7},{4,0},{5,1},{6,2},{7,3},{8,12},{9,13},{10,... | collective-permute-start | bytes 1572872 | tf_op jit(solution)/shard_map/features_xy/ppermute | solution.py:446
  51.8 13.7 %collective-permute-start.13 = (bf16[512,512]{1,0:T(8,128)(2,1)S(1)}, bf16[512,512]{1,0:T(8,128)(2,1)}, u32[]{:S(2)}, u32[]{:S(2)}) collective-permute-start(bf16[512,512]{1,0:T(8,128)(2,1)S(1)} %constant_dynamic-update-slice_fusion.refs_10_), channel_id=1, source_target_pairs={{0,8},{1,9},{2,10},{3,11},{4,12},{5,13},{6,14},{7,15},{8,0},{9,1},... | collective-permute-start | bytes 1572872 | tf_op jit(solution)/shard_map/features_z/ppermute | solution.py:446
  53.2 14.6 %copy-start.4 = (bf16[512,512]{1,0:T(8,128)(2,1)S(1)}, bf16[512,512]{1,0:T(8,128)(2,1)}, u32[]{:S(2)}) copy-start(bf16[512,512]{1,0:T(8,128)(2,1)} %copy-done.3) | copy-start | bytes 1572868
  53.2 14.6 %copy-start.6 = (bf16[512,512]{1,0:T(8,128)(2,1)S(1)}, bf16[512,512]{1,0:T(8,128)(2,1)}, u32[]{:S(2)}) copy-start(bf16[512,512]{1,0:T(8,128)(2,1)} %copy-done.5) | copy-start | bytes 1572868
  53.2 14.6 %copy-start.8 = (bf16[512,512]{1,0:T(8,128)(2,1)S(1)}, bf16[512,512]{1,0:T(8,128)(2,1)}, u32[]{:S(2)}) copy-start(bf16[512,512]{1,0:T(8,128)(2,1)} %copy-done.7) | copy-start | bytes 1572868
  65.5 12.9 %collective-permute-start.15 = (bf16[512,512]{1,0:T(8,128)(2,1)}, bf16[512,512]{1,0:T(8,128)(2,1)S(1)}, u32[]{:S(2)}, u32[]{:S(2)}) collective-permute-start(bf16[512,512]{1,0:T(8,128)(2,1)} %collective-permute-done.12.refs_2_), channel_id=1, source_target_pairs={{0,2},{1,3},{2,0},{3,1},{4,6},{5,7},{6,4},{7,5},{8,10},{9,11},{10,... | collective-permute-start | bytes 1572872 | tf_op jit(solution)/shard_map/features_xy/ppermute | solution.py:446
  66.6 12.3 %collective-permute-start.16 = (bf16[512,512]{1,0:T(8,128)(2,1)}, bf16[512,512]{1,0:T(8,128)(2,1)S(1)}, u32[]{:S(2)}, u32[]{:S(2)}) collective-permute-start(bf16[512,512]{1,0:T(8,128)(2,1)} %collective-permute-done.13.refs_3_), channel_id=1, source_target_pairs={{0,4},{1,5},{2,6},{3,7},{4,0},{5,1},{6,2},{7,3},{8,12},{9,13},{10,... | collective-permute-start | bytes 1572872 | tf_op jit(solution)/shard_map/features_xy/ppermute | solution.py:446
  67.5 12.0 %collective-permute-start.17 = (bf16[512,512]{1,0:T(8,128)(2,1)}, bf16[512,512]{1,0:T(8,128)(2,1)S(1)}, u32[]{:S(2)}, u32[]{:S(2)}) collective-permute-start(bf16[512,512]{1,0:T(8,128)(2,1)} %collective-permute-done.11.refs_11_), channel_id=1, source_target_pairs={{0,8},{1,9},{2,10},{3,11},{4,12},{5,13},{6,14},{7,15},{8,0},{9,1},... | collective-permute-start | bytes 1572872 | tf_op jit(solution)/shard_map/features_z/ppermute | solution.py:446
  79.5 7.7 %collective-permute-start.18 = (bf16[256,512]{1,0:T(8,128)(2,1)S(1)}, bf16[256,512]{1,0:T(8,128)(2,1)S(1)}, u32[]{:S(2)}, u32[]{:S(2)}) collective-permute-start(bf16[256,512]{1,0:T(8,128)(2,1)S(1)} %slice.50), channel_id=1, source_target_pairs={{0,2},{1,3},{2,0},{3,1},{4,6},{5,7},{6,4},{7,5},{8,10},{9,11},{10,... | collective-permute-start | bytes 786440 | tf_op jit(solution)/shard_map/features_xy/ppermute | solution.py:446
  80.6 6.6 %collective-permute-start.19 = (bf16[256,512]{1,0:T(8,128)(2,1)S(1)}, bf16[256,512]{1,0:T(8,128)(2,1)S(1)}, u32[]{:S(2)}, u32[]{:S(2)}) collective-permute-start(bf16[256,512]{1,0:T(8,128)(2,1)S(1)} %slice.51), channel_id=1, source_target_pairs={{0,4},{1,5},{2,6},{3,7},{4,0},{5,1},{6,2},{7,3},{8,12},{9,13},{10,... | collective-permute-start | bytes 786440 | tf_op jit(solution)/shard_map/features_xy/ppermute | solution.py:446
  87.2 6.2 %copy-start.2 = (bf16[512,512]{1,0:T(8,128)(2,1)S(1)}, bf16[512,512]{1,0:T(8,128)(2,1)}, u32[]{:S(2)}) copy-start(bf16[512,512]{1,0:T(8,128)(2,1)} %weight_ref.3) | copy-start | bytes 1572868
  90.7 2.7 %collective-permute-start.20 = (bf16[1024,512]{1,0:T(8,128)(2,1)S(1)}, bf16[1024,512]{1,0:T(8,128)(2,1)S(1)}, u32[]{:S(2)}, u32[]{:S(2)}) collective-permute-start(bf16[1024,512]{1,0:T(8,128)(2,1)S(1)} %forward.5.mine_ref), channel_id=1, source_target_pairs={{0,1},{1,0},{2,3},{3,2},{4,5},{5,4},{6,7},{7,6},{8,9},{9,8},{10,11... | collective-permute-start | bytes 3145736 | tf_op jit(solution)/shard_map/partial_sums/ppermute | solution.py:446
  100.0 11.0 %collective-permute-start.21 = (bf16[64,512]{1,0:T(8,128)(2,1)S(1)}, bf16[64,512]{1,0:T(8,128)(2,1)S(1)}, u32[]{:S(2)}, u32[]{:S(2)}) collective-permute-start(bf16[64,512]{1,0:T(8,128)(2,1)S(1)} %get-tuple-element.309), channel_id=1, source_target_pairs={{0,8},{1,9},{2,10},{3,11},{4,12},{5,13},{6,14},{7,15},{8,0},{9,1},... | collective-permute-start | bytes 196616 | tf_op jit(solution)/shard_map/weight_grad/ppermute | solution.py:446
  100.6 11.7 %collective-permute-start.22 = (bf16[64,512]{1,0:T(8,128)(2,1)S(1)}, bf16[64,512]{1,0:T(8,128)(2,1)S(1)}, u32[]{:S(2)}, u32[]{:S(2)}) collective-permute-start(bf16[64,512]{1,0:T(8,128)(2,1)S(1)} %get-tuple-element.311), channel_id=1, source_target_pairs={{0,16},{1,17},{2,18},{3,19},{4,20},{5,21},{6,22},{7,23},{8,24},{9,... | collective-permute-start | bytes 196616 | tf_op jit(solution)/shard_map/weight_grad/ppermute | solution.py:446
  102.5 9.8 %collective-permute-start.23 = (bf16[64,512]{1,0:T(8,128)(2,1)S(1)}, bf16[64,512]{1,0:T(8,128)(2,1)S(1)}, u32[]{:S(2)}, u32[]{:S(2)}) collective-permute-start(bf16[64,512]{1,0:T(8,128)(2,1)S(1)} %get-tuple-element.310), channel_id=1, source_target_pairs={{0,24},{1,25},{2,26},{3,27},{4,28},{5,29},{6,30},{7,31},{8,16},{9,... | collective-permute-start | bytes 196616 | tf_op jit(solution)/shard_map/weight_grad/ppermute | solution.py:446
  104.4 8.0 %collective-permute-start.24 = (bf16[256,512]{1,0:T(8,128)(2,1)S(1)}, bf16[256,512]{1,0:T(8,128)(2,1)S(1)}, u32[]{:S(2)}, u32[]{:S(2)}) collective-permute-start(bf16[256,512]{1,0:T(8,128)(2,1)S(1)} %get-tuple-element.218), channel_id=1, source_target_pairs={{0,2},{1,3},{2,0},{3,1},{4,6},{5,7},{6,4},{7,5},{8,10},{9,11},{10,... | collective-permute-start | bytes 786440 | tf_op jit(solution)/shard_map/grads_xy/ppermute | solution.py:446
  105.2 7.2 %collective-permute-start.25 = (bf16[256,512]{1,0:T(8,128)(2,1)S(1)}, bf16[256,512]{1,0:T(8,128)(2,1)S(1)}, u32[]{:S(2)}, u32[]{:S(2)}) collective-permute-start(bf16[256,512]{1,0:T(8,128)(2,1)S(1)} %get-tuple-element.219), channel_id=1, source_target_pairs={{0,4},{1,5},{2,6},{3,7},{4,0},{5,1},{6,2},{7,3},{8,12},{9,13},{10,... | collective-permute-start | bytes 786440 | tf_op jit(solution)/shard_map/grads_xy/ppermute | solution.py:446
  111.0 14.1 %collective-permute-start.27 = (bf16[512,512]{1,0:T(8,128)(2,1)S(1)}, bf16[512,512]{1,0:T(8,128)(2,1)S(1)}, u32[]{:S(2)}, u32[]{:S(2)}) collective-permute-start(bf16[512,512]{1,0:T(8,128)(2,1)S(1)} %get-tuple-element.230), channel_id=1, source_target_pairs={{0,2},{1,3},{2,0},{3,1},{4,6},{5,7},{6,4},{7,5},{8,10},{9,11},{10,... | collective-permute-start | bytes 1572872 | tf_op jit(solution)/shard_map/grads_xy/ppermute | solution.py:446
  112.6 12.5 %collective-permute-start.28 = (bf16[512,512]{1,0:T(8,128)(2,1)S(1)}, bf16[512,512]{1,0:T(8,128)(2,1)S(1)}, u32[]{:S(2)}, u32[]{:S(2)}) collective-permute-start(bf16[512,512]{1,0:T(8,128)(2,1)S(1)} %get-tuple-element.235), channel_id=1, source_target_pairs={{0,4},{1,5},{2,6},{3,7},{4,0},{5,1},{6,2},{7,3},{8,12},{9,13},{10,... | collective-permute-start | bytes 1572872 | tf_op jit(solution)/shard_map/grads_xy/ppermute | solution.py:446
  113.8 11.6 %collective-permute-start.29 = (bf16[512,512]{1,0:T(8,128)(2,1)S(1)}, bf16[512,512]{1,0:T(8,128)(2,1)S(1)}, u32[]{:S(2)}, u32[]{:S(2)}) collective-permute-start(bf16[512,512]{1,0:T(8,128)(2,1)S(1)} %get-tuple-element.236), channel_id=1, source_target_pairs={{0,8},{1,9},{2,10},{3,11},{4,12},{5,13},{6,14},{7,15},{8,0},{9,1},... | collective-permute-start | bytes 1572872 | tf_op jit(solution)/shard_map/grads_z/ppermute | solution.py:446
  119.3 5.7 %collective-permute-start.26 = (bf16[64,512]{1,0:T(8,128)(2,1)S(1)}, bf16[64,512]{1,0:T(8,128)(2,1)S(1)}, u32[]{:S(2)}, u32[]{:S(2)}) collective-permute-start(bf16[64,512]{1,0:T(8,128)(2,1)S(1)} %fusion.2), channel_id=1, source_target_pairs={{0,2},{1,3},{2,0},{3,1},{4,6},{5,7},{6,4},{7,5},{8,10},{9,11},{10,... | collective-permute-start | bytes 196616 | tf_op jit(solution)/shard_map/weight_grad/ppermute | solution.py:446
  125.6 17.0 %collective-permute-start.33 = (bf16[512,512]{1,0:T(8,128)(2,1)S(1)}, bf16[512,512]{1,0:T(8,128)(2,1)S(1)}, u32[]{:S(2)}, u32[]{:S(2)}) collective-permute-start(bf16[512,512]{1,0:T(8,128)(2,1)S(1)} %add_convert_fusion.3), channel_id=1, source_target_pairs={{0,8},{1,9},{2,10},{3,11},{4,12},{5,13},{6,14},{7,15},{8,0},{9,1},... | collective-permute-start | bytes 1572872 | tf_op jit(solution)/shard_map/grads_z/ppermute | solution.py:446
  126.1 16.5 %collective-permute-start.32 = (bf16[512,512]{1,0:T(8,128)(2,1)S(1)}, bf16[512,512]{1,0:T(8,128)(2,1)S(1)}, u32[]{:S(2)}, u32[]{:S(2)}) collective-permute-start(bf16[512,512]{1,0:T(8,128)(2,1)S(1)} %add_convert_fusion.4), channel_id=1, source_target_pairs={{0,4},{1,5},{2,6},{3,7},{4,0},{5,1},{6,2},{7,3},{8,12},{9,13},{10,... | collective-permute-start | bytes 1572872 | tf_op jit(solution)/shard_map/grads_xy/ppermute | solution.py:446
  127.5 15.2 %collective-permute-start.31 = (bf16[512,512]{1,0:T(8,128)(2,1)S(1)}, bf16[512,512]{1,0:T(8,128)(2,1)S(1)}, u32[]{:S(2)}, u32[]{:S(2)}) collective-permute-start(bf16[512,512]{1,0:T(8,128)(2,1)S(1)} %add_convert_fusion.5), channel_id=1, source_target_pairs={{0,2},{1,3},{2,0},{3,1},{4,6},{5,7},{6,4},{7,5},{8,10},{9,11},{10,... | collective-permute-start | bytes 1572872 | tf_op jit(solution)/shard_map/grads_xy/ppermute | solution.py:446
  135.1 6.1 %collective-permute-start.30 = (bf16[64,512]{1,0:T(8,128)(2,1)S(1)}, bf16[64,512]{1,0:T(8,128)(2,1)S(1)}, u32[]{:S(2)}, u32[]{:S(2)}) collective-permute-start(bf16[64,512]{1,0:T(8,128)(2,1)S(1)} %add_convert_fusion.9), channel_id=1, source_target_pairs={{0,4},{1,5},{2,6},{3,7},{4,0},{5,1},{6,2},{7,3},{8,12},{9,13},{10,... | collective-permute-start | bytes 196616 | tf_op jit(solution)/shard_map/weight_grad/ppermute | solution.py:446
  136.4 18.9 %collective-permute-start.35 = (bf16[512,512]{1,0:T(8,128)(2,1)S(1)}, bf16[512,512]{1,0:T(8,128)(2,1)S(1)}, u32[]{:S(2)}, u32[]{:S(2)}) collective-permute-start(bf16[512,512]{1,0:T(8,128)(2,1)S(1)} %get-tuple-element.264), channel_id=1, source_target_pairs={{0,4},{1,5},{2,6},{3,7},{4,0},{5,1},{6,2},{7,3},{8,12},{9,13},{10,... | collective-permute-start | bytes 1572872 | tf_op jit(solution)/shard_map/grads_xy/ppermute | solution.py:446
  141.3 14.0 %collective-permute-start.36 = (bf16[512,512]{1,0:T(8,128)(2,1)S(1)}, bf16[512,512]{1,0:T(8,128)(2,1)S(1)}, u32[]{:S(2)}, u32[]{:S(2)}) collective-permute-start(bf16[512,512]{1,0:T(8,128)(2,1)S(1)} %get-tuple-element.265), channel_id=1, source_target_pairs={{0,2},{1,3},{2,0},{3,1},{4,6},{5,7},{6,4},{7,5},{8,10},{9,11},{10,... | collective-permute-start | bytes 1572872 | tf_op jit(solution)/shard_map/grads_xy/ppermute | solution.py:446
  142.9 12.4 %collective-permute-start.37 = (bf16[256,512]{1,0:T(8,128)(2,1)S(1)}, bf16[256,512]{1,0:T(8,128)(2,1)S(1)}, u32[]{:S(2)}, u32[]{:S(2)}) collective-permute-start(bf16[256,512]{1,0:T(8,128)(2,1)S(1)} %get-tuple-element.304), channel_id=1, source_target_pairs={{0,16},{1,17},{2,18},{3,19},{4,20},{5,21},{6,22},{7,23},{8,24},{9,... | collective-permute-start | bytes 786440 | tf_op jit(solution)/shard_map/grads_z/ppermute | solution.py:446
  149.7 5.6 %collective-permute-start.34 = (bf16[1,64,512]{2,1,0:T(8,128)(2,1)S(1)}, bf16[1,64,512]{2,1,0:T(8,128)(2,1)S(1)}, u32[]{:S(2)}, u32[]{:S(2)}) collective-permute-start(bf16[1,64,512]{2,1,0:T(8,128)(2,1)S(1)} %bitcast.19), channel_id=1, source_target_pairs={{0,16},{1,17},{2,18},{3,19},{4,20},{5,21},{6,22},{7,23},{8,24},{9,... | collective-permute-start | bytes 196616 | tf_op jit(solution)/shard_map/weight_grad/ppermute | solution.py:446
  150.6 17.2 %collective-permute-start.41 = (bf16[512,512]{1,0:T(8,128)(2,1)S(1)}, bf16[512,512]{1,0:T(8,128)(2,1)S(1)}, u32[]{:S(2)}, u32[]{:S(2)}) collective-permute-start(bf16[512,512]{1,0:T(8,128)(2,1)S(1)} %get-tuple-element.281), channel_id=1, source_target_pairs={{0,4},{1,5},{2,6},{3,7},{4,0},{5,1},{6,2},{7,3},{8,12},{9,13},{10,... | collective-permute-start | bytes 1572872 | tf_op jit(solution)/shard_map/grads_xy/ppermute | solution.py:446
  155.5 14.2 %collective-permute-start.40 = (bf16[512,512]{1,0:T(8,128)(2,1)S(1)}, bf16[512,512]{1,0:T(8,128)(2,1)S(1)}, u32[]{:S(2)}, u32[]{:S(2)}) collective-permute-start(bf16[512,512]{1,0:T(8,128)(2,1)S(1)} %add_convert_fusion.2), channel_id=1, source_target_pairs={{0,2},{1,3},{2,0},{3,1},{4,6},{5,7},{6,4},{7,5},{8,10},{9,11},{10,... | collective-permute-start | bytes 1572872 | tf_op jit(solution)/shard_map/grads_xy/ppermute | solution.py:446
  156.7 7.1 %collective-permute-start.38 = (bf16[2,64,512]{2,1,0:T(8,128)(2,1)S(1)}, bf16[2,64,512]{2,1,0:T(8,128)(2,1)S(1)}, u32[]{:S(2)}, u32[]{:S(2)}) collective-permute-start(bf16[2,64,512]{2,1,0:T(8,128)(2,1)S(1)} %pad_maximum_fusion.2), channel_id=1, source_target_pairs={{0,8},{1,9},{2,10},{3,11},{4,12},{5,13},{6,14},{7,15},{8,0},{9,1},... | collective-permute-start | bytes 393224 | tf_op jit(solution)/shard_map/weight_grad/ppermute | solution.py:446
  156.7 11.1 %collective-permute-start.39 = (bf16[256,512]{1,0:T(8,128)(2,1)S(1)}, bf16[256,512]{1,0:T(8,128)(2,1)S(1)}, u32[]{:S(2)}, u32[]{:S(2)}) collective-permute-start(bf16[256,512]{1,0:T(8,128)(2,1)S(1)} %get-tuple-element.277), channel_id=1, source_target_pairs={{0,16},{1,17},{2,18},{3,19},{4,20},{5,21},{6,22},{7,23},{8,24},{9,... | collective-permute-start | bytes 786440 | tf_op jit(solution)/shard_map/grads_z/ppermute | solution.py:446
  159.3 13.0 %collective-permute-start.43 = (bf16[512,512]{1,0:T(8,128)(2,1)S(1)}, bf16[512,512]{1,0:T(8,128)(2,1)S(1)}, u32[]{:S(2)}, u32[]{:S(2)}) collective-permute-start(bf16[512,512]{1,0:T(8,128)(2,1)S(1)} %add_convert_fusion.1), channel_id=1, source_target_pairs={{0,4},{1,5},{2,6},{3,7},{4,0},{5,1},{6,2},{7,3},{8,12},{9,13},{10,... | collective-permute-start | bytes 1572872 | tf_op jit(solution)/shard_map/grads_xy/ppermute | solution.py:446
  163.8 12.8 %collective-permute-start.42 = (bf16[512,512]{1,0:T(8,128)(2,1)S(1)}, bf16[512,512]{1,0:T(8,128)(2,1)S(1)}, u32[]{:S(2)}, u32[]{:S(2)}) collective-permute-start(bf16[512,512]{1,0:T(8,128)(2,1)S(1)} %get-tuple-element.285), channel_id=1, source_target_pairs={{0,2},{1,3},{2,0},{3,1},{4,6},{5,7},{6,4},{7,5},{8,10},{9,11},{10,... | collective-permute-start | bytes 1572872 | tf_op jit(solution)/shard_map/grads_xy/ppermute | solution.py:446
  169.7 12.5 %copy-start.1 = (bf16[1024,512]{1,0:T(8,128)(2,1)S(1)}, bf16[1024,512]{1,0:T(8,128)(2,1)}, u32[]{:S(2)}) copy-start(bf16[1024,512]{1,0:T(8,128)(2,1)} %param.8) | copy-start | bytes 3145732
  169.9 10.2 %collective-permute-start.44 = (bf16[512,512]{1,0:T(8,128)(2,1)S(1)}, bf16[512,512]{1,0:T(8,128)(2,1)S(1)}, u32[]{:S(2)}, u32[]{:S(2)}) collective-permute-start(bf16[512,512]{1,0:T(8,128)(2,1)S(1)} %add_convert_fusion), channel_id=1, source_target_pairs={{0,8},{1,9},{2,10},{3,11},{4,12},{5,13},{6,14},{7,15},{8,0},{9,1},... | collective-permute-start | bytes 1572872 | tf_op jit(solution)/shard_map/grads_z/ppermute | solution.py:446
  170.0 6.6 %collective-permute-start.45 = (bf16[4,64,512]{2,1,0:T(8,128)(2,1)S(1)}, bf16[4,64,512]{2,1,0:T(8,128)(2,1)S(1)}, u32[]{:S(2)}, u32[]{:S(2)}) collective-permute-start(bf16[4,64,512]{2,1,0:T(8,128)(2,1)S(1)} %pad_maximum_fusion.1.refs_6_), channel_id=1, source_target_pairs={{0,1},{1,0},{2,3},{3,2},{4,5},{5,4},{6,7},{7,6},{8,9},{9,8},{10,11... | collective-permute-start | bytes 786440 | tf_op jit(solution)/shard_map/weight_grad/ppermute | solution.py:446

commit v12 on v11

--- a/solution.py
+++ b/solution.py
@@ -535,7 +535,6 @@
         if pair == 0:
             with jax.named_scope(FEATURES_ACROSS):
                 live["odd_x"], live["odd_y"] = flip(live[odd], X), flip(live[odd], Y)
-            build_own(panels // 2)
         else:
             with jax.named_scope(FEATURES_ACROSS):
                 live["even_xy"], live["odd_y"] = flip(live["even_y"], X), flip(live[odd], Y)
@@ -548,9 +547,8 @@
                 live["total"] = forward_step(("early", pair), units, live["total"])
         if not last:
             with jax.named_scope(FEATURES_ALONG):
-                source, mask = live[later - low_bit(later)], low_bit(later)
-                live["coming"] = [flip(source[:half], mask)]
-        close()
+                live[later] = flip(live[later - low_bit(later)], low_bit(later))
+        close(*([] if last else [later]))
 
         if pair == 0:
             units = [live[even], live["even_x"], live["even_y"]]
@@ -558,6 +556,7 @@
             with jax.named_scope(FEATURES_ACROSS):
                 units += [flip(live["even_x"], Y), flip(live["odd_y"], X)]
             live["units"] = units
+            build_own(panels // 2)
             live["one"] = build_others(0)
         else:
             with jax.named_scope(FEATURES_ACROSS):
@@ -565,14 +564,9 @@
             live["units"] = [live["odd_x"], odd_xy]
             units = [live["even_y"], live[odd], live.pop("even_xy"), live["odd_y"]]
             live["total"] = forward_step(("more", pair), units, live["total"])
-        if not last:
-            with jax.named_scope(FEATURES_ALONG):
-                live["coming"].append(flip(source[half:], mask))
         for name in ("even_x", "even_y", "odd_x", "odd_y"):
             del live[name]
         close()
-        if not last:
-            live[later] = jnp.concatenate(live.pop("coming"))
     partial = forward_step(
         ("late", pair_count - 1), live.pop("units"), live.get("total"), BF16
     )

time: 184 us -> 184 us (level)
  starting transfers between devices: 48 us -> 45.1 us
    ppermute x46 -> x45, starting transfers between devices: 48 us -> 45.1 us  [flip(): return lax.ppermute(value, BOTH, pairs)]
    ppermute x46 -> x45, waiting for transfers between devices: 50.1 us -> 51.8 us  [flip(): return lax.ppermute(value, BOTH, pairs)]
  transfers between devices with their start and end apart: 46 -> 45, of which waited for: 20 -> 18; matrix products, arithmetic and copies ran while one was open for 3% -> 3% of each run, Pallas kernels for 36% -> 36%
where the time goes in v12:
time: 184 us
  Pallas kernels  78.6 us (43%)
  waiting for transfers between devices  51.8 us (28%)
  starting transfers between devices  45.1 us (25%)
  other arithmetic  4.16 us (2%)
  local copies, waits for them, and re-layouts  3.13 us (2%)
    ppermute x45, waiting for transfers between devices, flip(): return lax.ppermute(value, BOTH, pairs)  51.8 us
    ppermute x45, starting transfers between devices, flip(): return lax.ppermute(value, BOTH, pairs)  45.1 us
    pallas_call x4, Pallas kernels, backward_part(): pl.pallas_call(backward_kernel, out_shape=[jax.ShapeDtypeStruct((width, c...  21.4 us
    pallas_call x3, Pallas kernels, forward_part(): pl.pallas_call(functools.partial(forward_kernel, offset, n_pieces, n_othe...  18.2 us
    pallas_call x2, Pallas kernels, make_dense(): pl.pallas_call(functools.partial(dense_kernel, first), out_shape=pltpu.HB...  14.9 us
    pallas_call x2, Pallas kernels, make_other(): pl.pallas_call(functools.partial(other_kernel, first), out_shape=pltpu.HB...  13.5 us
    pallas_call x1, Pallas kernels, middle(): pl.pallas_call(functools.partial(middle_kernel, blocks), out_shape=[jax.S...  6.49 us
  transfers between devices with their start and end apart: 45, of which 18 were waited for; matrix products, arithmetic and copies ran while one was open for 3% of the time, Pallas kernels for 36%

profile of v12, /device:TPU:0, one launch (start us, length us, event | category | flops | bytes accessed | tf_op | source)
XLA Modules:
  0.0 183.8 jit_solution(12922142026869655491)
XLA Ops:
  1.2 0.7 copy-done
  1.9 3.1 %collective-permute-start.2 = (bf16[512,512]{1,0:T(8,128)(2,1)S(1)}, bf16[512,512]{1,0:T(8,128)(2,1)S(1)}, u32[]{:S(2)}, u32[]{:S(2)}) collective-permute-start(bf16[512,512]{1,0:T(8,128)(2,1)S(1)} %constant_dynamic-slice_fusion.refs_2_), channel_id=1, source_target_pairs={{0,8},{1,9},{2,10},{3,11},{4,12},{5,13},{6,14},{7,15},{8,0},{9,1},... | collective-permute-start | bytes 1572872 | tf_op jit(solution)/shard_map/features_z/ppermute | solution.py:446
  5.0 1.5 collective-permute-start.3
  6.5 1.5 collective-permute-start.4
  8.0 0.7 add_bitcast_fusion
  8.7 0.7 copy.12
  9.5 0.7 broadcast_xor_fusion
  10.3 7.4 %dense_blocks.2.refs_0_ = bf16[2,8,1024,512]{3,2,1,0:T(8,128)(2,1)} custom-call(s32[44]{0:T(128)S(1)} %pad_add_fusion.1.where_ref, s32[8,25]{1,0:T(8,128)S(1)} %pad_add_fusion.packed_ref, bf16[8,24,128,128]{3,2,1,0:T(8,128)(2,1)} %bitcast.17), custom_call_target="tpu_custom_call" | custom-call | bytes 393216 | tf_op jit(solution)/shard_map/dense_blocks/pallas_call | solution.py:44
  17.6 0.9 collective-permute-start.5
  18.6 1.5 collective-permute-start.6
  20.1 2.6 %collective-permute-start.7 = (bf16[512,512]{1,0:T(8,128)(2,1)S(1)}, bf16[512,512]{1,0:T(8,128)(2,1)}, u32[]{:S(2)}, u32[]{:S(2)}) collective-permute-start(bf16[512,512]{1,0:T(8,128)(2,1)S(1)} %constant_dynamic-slice_fusion.refs_2_), channel_id=1, source_target_pairs={{0,16},{1,17},{2,18},{3,19},{4,20},{5,21},{6,22},{7,23},{8,24},{9,... | collective-permute-start | bytes 1572872 | tf_op jit(solution)/shard_map/features_z/ppermute | solution.py:446
  22.7 9.5 %collective-permute-done.5.refs_6_ = bf16[512,512]{1,0:T(8,128)(2,1)S(1)} collective-permute-done((bf16[512,512]{1,0:T(8,128)(2,1)S(1)}, bf16[512,512]{1,0:T(8,128)(2,1)S(1)}, u32[]{:S(2)}, u32[]{:S(2)}) %collective-permute-start.5) | collective-permute-done | bytes 524320 | tf_op jit(solution)/shard_map/features_xy/ppermute | solution.py:446
  32.6 1.6 collective-permute-start.9
  34.2 7.5 %dense_blocks.3.dense_ref.a_ref = bf16[2,8,1024,512]{3,2,1,0:T(8,128)(2,1)} custom-call(s32[44]{0:T(128)S(1)} %pad_add_fusion.1.where_ref, s32[8,25]{1,0:T(8,128)S(1)} %pad_add_fusion.packed_ref, bf16[8,24,128,128]{3,2,1,0:T(8,128)(2,1)} %bitcast.18, bf16[2,8,1024,512]{3,2,1,0:T(8,128)(2,1)} %dense_blocks.2.refs_0_), custom_call_target="tpu_custom_call", output_to_operand_aliasing={{}: (3, {})} | custom-call | bytes 393216 | tf_op jit(solution)/shard_map/dense_blocks/pallas_call | solution.py:44
  41.7 6.7 %other_blocks.2.refs_0_ = bf16[4,1024,512]{2,1,0:T(8,128)(2,1)} custom-call(s32[44]{0:T(128)S(1)} %pad_add_fusion.1.where_ref, s32[8,25]{1,0:T(8,128)S(1)} %collective-permute-done.1.packed_ref, bf16[8,24,128,128]{3,2,1,0:T(8,128)(2,1)} %collective-permute-done.tiles_ref), custom_call_target="tpu_custom_call" | custom-call | bytes 393216 | tf_op jit(solution)/shard_map/other_blocks/pallas_call | solution.py:89
  48.5 0.8 copy-done.3
  49.3 0.8 copy-done.5
  50.7 1.3 broadcast_select_fusion.1
  52.1 6.8 %other_blocks.3.refs_1_ = bf16[4,1024,512]{2,1,0:T(8,128)(2,1)} custom-call(s32[44]{0:T(128)S(1)} %pad_add_fusion.1.where_ref, s32[8,25]{1,0:T(8,128)S(1)} %collective-permute-done.1.packed_ref, bf16[8,24,128,128]{3,2,1,0:T(8,128)(2,1)} %collective-permute-done.tiles_ref), custom_call_target="tpu_custom_call" | custom-call | bytes 393216 | tf_op jit(solution)/shard_map/other_blocks/pallas_call | solution.py:89
  58.9 5.7 %collective-permute-done.10.refs_11_ = bf16[512,512]{1,0:T(8,128)(2,1)} collective-permute-done((bf16[512,512]{1,0:T(8,128)(2,1)}, bf16[512,512]{1,0:T(8,128)(2,1)}, u32[]{:S(2)}, u32[]{:S(2)}) %collective-permute-start.10) | collective-permute-done | bytes 524320 | tf_op jit(solution)/shard_map/features_xy/ppermute | solution.py:446
  64.6 1.7 collective-permute-start.14
  66.4 1.7 collective-permute-start.15
  68.4 9.6 %forward.3.refs_6_ = f32[1024,512]{1,0:T(8,128)S(1)} custom-call(s32[44]{0:T(128)S(1)} %pad_add_fusion.1.where_ref, bf16[2,8,1024,512]{3,2,1,0:T(8,128)(2,1)} %dense_blocks.3.dense_ref.a_ref, bf16[4,1024,512]{2,1,0:T(8,128)(2,1)} %other_blocks.2.refs_0_, bf16[4,1024,512]{2,1,0:T(8,128)(2,1)} %other_blocks.3.refs_1_, ...), custom_call_target="tpu_custom_call" | custom-call | flops 5368709120 | bytes 14680064 | tf_op jit(solution)/shard_map/forward/pallas_call | solution.py:192
  78.3 1.1 collective-permute-done.15.refs_5_
  79.5 1.1 collective-permute-done.16.refs_2_
  80.6 0.7 collective-permute-start.17
  81.3 0.7 collective-permute-start.18
  82.0 5.2 %forward.4.refs_5_ = f32[1024,512]{1,0:T(8,128)S(1)} custom-call(s32[44]{0:T(128)S(1)} %pad_add_fusion.1.where_ref, bf16[2,8,1024,512]{3,2,1,0:T(8,128)(2,1)} %dense_blocks.3.dense_ref.a_ref, bf16[4,1024,512]{2,1,0:T(8,128)(2,1)} %other_blocks.2.refs_0_, bf16[4,1024,512]{2,1,0:T(8,128)(2,1)} %other_blocks.3.refs_1_, ...), custom_call_target="tpu_custom_call" | custom-call | flops 2147483648 | bytes 8388608 | tf_op jit(solution)/shard_map/forward/pallas_call | solution.py:192
  87.7 3.5 %forward.5.mine_ref = bf16[1024,512]{1,0:T(8,128)(2,1)S(1)} custom-call(s32[44]{0:T(128)S(1)} %pad_add_fusion.1.where_ref, bf16[2,8,1024,512]{3,2,1,0:T(8,128)(2,1)} %dense_blocks.3.dense_ref.a_ref, bf16[4,1024,512]{2,1,0:T(8,128)(2,1)} %other_blocks.2.refs_0_, bf16[4,1024,512]{2,1,0:T(8,128)(2,1)} %other_blocks.3.refs_1_, ...), custom_call_target="tpu_custom_call" | custom-call | flops 1073741824 | bytes 6291456 | tf_op jit(solution)/shard_map/forward/pallas_call | solution.py:192
  91.3 2.6 %collective-permute-done.19.other_ref = bf16[1024,512]{1,0:T(8,128)(2,1)S(1)} collective-permute-done((bf16[1024,512]{1,0:T(8,128)(2,1)S(1)}, bf16[1024,512]{1,0:T(8,128)(2,1)S(1)}, u32[]{:S(2)}, u32[]{:S(2)}) %collective-permute-start.19) | collective-permute-done | bytes 1048608 | tf_op jit(solution)/shard_map/partial_sums/ppermute | solution.py:446
  94.0 6.5 %middle.1 = (bf16[512,1024]{1,0:T(8,128)(2,1)S(1)}, bf16[256,512]{1,0:T(8,128)(2,1)S(1)}, bf16[256,512]{1,0:T(8,128)(2,1)S(1)}, bf16[4,64,512]{2,1,0:T(8,128)(2,1)S(1)}) custom-call(s32[44]{0:T(128)S(1)} %pad_add_fusion.1.where_ref, bf16[1024,512]{1,0:T(8,128)(2,1)S(1)} %forward.5.mine_ref, bf16[1024,512]{1,0:T(8,128)(2,1)S(1)} %collective-permute-done.19.other_ref, ...), custom_call_target="tpu_custom_call" | custom-call | flops 2684354560 | bytes 6291456 | tf_op jit(solution)/shard_map/middle/pallas_call | solution.py:277
  100.5 3.1 %collective-permute-start.22 = (bf16[64,512]{1,0:T(8,128)(2,1)S(1)}, bf16[64,512]{1,0:T(8,128)(2,1)S(1)}, u32[]{:S(2)}, u32[]{:S(2)}) collective-permute-start(bf16[64,512]{1,0:T(8,128)(2,1)S(1)} %get-tuple-element.304), channel_id=1, source_target_pairs={{0,24},{1,25},{2,26},{3,27},{4,28},{5,29},{6,30},{7,31},{8,16},{9,... | collective-permute-start | bytes 196616 | tf_op jit(solution)/shard_map/weight_grad/ppermute | solution.py:446
  103.6 1.3 collective-permute-start.20
  104.9 1.4 collective-permute-start.23
  106.4 0.9 collective-permute-start.24
  107.2 4.6 %backward.4 = (bf16[512,512]{1,0:T(8,128)(2,1)S(1)}, bf16[512,512]{1,0:T(8,128)(2,1)S(1)}, bf16[512,512]{1,0:T(8,128)(2,1)S(1)}) custom-call(s32[44]{0:T(128)S(1)} %pad_add_fusion.1.where_ref, bf16[512,1024]{1,0:T(8,128)(2,1)S(1)} %get-tuple-element.253.grad_ref, bf16[2,8,1024,512]{3,2,1,0:T(8,128)(2,1)} %dense_blocks.3.dense_ref.a_ref), custom_call_target="tpu_custom_call" | custom-call | flops 1610612736 | bytes 5767168 | tf_op jit(solution)/shard_map/backward/pallas_call | solution.py:350
  111.8 0.7 collective-permute-start.26
  112.6 1.0 collective-permute-done.24.end_ref
  113.7 0.9 collective-permute-start.27
  115.2 5.5 %backward.5 = (bf16[512,512]{1,0:T(8,128)(2,1)S(1)}, bf16[512,512]{1,0:T(8,128)(2,1)S(1)}, bf16[512,512]{1,0:T(8,128)(2,1)S(1)}, bf16[512,512]{1,0:T(8,128)(2,1)S(1)}) custom-call(s32[44]{0:T(128)S(1)} %pad_add_fusion.1.where_ref, bf16[512,1024]{1,0:T(8,128)(2,1)S(1)} %get-tuple-element.253.grad_ref, bf16[2,8,1024,512]{3,2,1,0:T(8,128)(2,1)} %dense_blocks.3.dense_ref.a_ref), custom_call_target="tpu_custom_call" | custom-call | flops 2147483648 | bytes 7340032 | tf_op jit(solution)/shard_map/backward/pallas_call | solution.py:350
  120.7 1.4 collective-permute-start.25
  122.1 3.8 %collective-permute-done.25 = bf16[64,512]{1,0:T(8,128)(2,1)S(1)} collective-permute-done((bf16[64,512]{1,0:T(8,128)(2,1)S(1)}, bf16[64,512]{1,0:T(8,128)(2,1)S(1)}, u32[]{:S(2)}, u32[]{:S(2)}) %collective-permute-start.25) | collective-permute-done | bytes 65568 | tf_op jit(solution)/shard_map/weight_grad/ppermute | solution.py:446
  126.4 1.2 collective-permute-start.30
  127.7 0.9 collective-permute-start.31
  128.8 1.1 collective-permute-start.32
  129.9 6.7 %backward.6 = (bf16[512,512]{1,0:T(8,128)(2,1)S(1)}, bf16[512,512]{1,0:T(8,128)(2,1)S(1)}, bf16[512,512]{1,0:T(8,128)(2,1)S(1)}, bf16[512,512]{1,0:T(8,128)(2,1)S(1)}, bf16[512,512]{1,0:T(8,128)(2,1)S(1)}) custom-call(s32[44]{0:T(128)S(1)} %pad_add_fusion.1.where_ref, bf16[512,1024]{1,0:T(8,128)(2,1)S(1)} %get-tuple-element.253.grad_ref, ...), custom_call_target="tpu_custom_call" | custom-call | flops 2684354560 | bytes 8912896 | tf_op jit(solution)/shard_map/backward/pallas_call | solution.py:350
  136.6 1.2 collective-permute-start.29
  137.9 0.8 collective-permute-start.34
  138.7 3.9 %collective-permute-done.29 = bf16[64,512]{1,0:T(8,128)(2,1)S(1)} collective-permute-done((bf16[64,512]{1,0:T(8,128)(2,1)S(1)}, bf16[64,512]{1,0:T(8,128)(2,1)S(1)}, u32[]{:S(2)}, u32[]{:S(2)}) %collective-permute-start.29) | collective-permute-done | bytes 65568 | tf_op jit(solution)/shard_map/weight_grad/ppermute | solution.py:446
  142.6 1.3 collective-permute-start.35
  144.2 1.4 collective-permute-start.36
  145.6 4.6 %backward.7 = (bf16[512,512]{1,0:T(8,128)(2,1)S(1)}, bf16[512,512]{1,0:T(8,128)(2,1)S(1)}, bf16[512,512]{1,0:T(8,128)(2,1)S(1)}) custom-call(s32[44]{0:T(128)S(1)} %pad_add_fusion.1.where_ref, bf16[512,1024]{1,0:T(8,128)(2,1)S(1)} %get-tuple-element.253.grad_ref, bf16[2,8,1024,512]{3,2,1,0:T(8,128)(2,1)} %dense_blocks.3.dense_ref.a_ref), custom_call_target="tpu_custom_call" | custom-call | flops 1610612736 | bytes 5767168 | tf_op jit(solution)/shard_map/backward/pallas_call | solution.py:350
  150.2 1.6 collective-permute-start.33
  151.9 1.5 collective-permute-start.40
  153.4 3.7 %collective-permute-done.33 = bf16[1,64,512]{2,1,0:T(8,128)(2,1)S(1)} collective-permute-done((bf16[1,64,512]{2,1,0:T(8,128)(2,1)S(1)}, bf16[1,64,512]{2,1,0:T(8,128)(2,1)S(1)}, u32[]{:S(2)}, u32[]{:S(2)}) %collective-permute-start.33) | collective-permute-done | bytes 65568 | tf_op jit(solution)/shard_map/weight_grad/ppermute | solution.py:446
  157.5 2.7 %collective-permute-start.37 = (bf16[2,64,512]{2,1,0:T(8,128)(2,1)S(1)}, bf16[2,64,512]{2,1,0:T(8,128)(2,1)S(1)}, u32[]{:S(2)}, u32[]{:S(2)}) collective-permute-start(bf16[2,64,512]{2,1,0:T(8,128)(2,1)S(1)} %pad_maximum_fusion.2), channel_id=1, source_target_pairs={{0,8},{1,9},{2,10},{3,11},{4,12},{5,13},{6,14},{7,15},{8,0},{9,1},... | collective-permute-start | bytes 393224 | tf_op jit(solution)/shard_map/weight_grad/ppermute | solution.py:446
  160.3 1.1 collective-permute-start.41
  161.6 3.0 %collective-permute-done.37 = bf16[2,64,512]{2,1,0:T(8,128)(2,1)S(1)} collective-permute-done((bf16[2,64,512]{2,1,0:T(8,128)(2,1)S(1)}, bf16[2,64,512]{2,1,0:T(8,128)(2,1)S(1)}, u32[]{:S(2)}, u32[]{:S(2)}) %collective-permute-start.37) | collective-permute-done | bytes 131104 | tf_op jit(solution)/shard_map/weight_grad/ppermute | solution.py:446
  164.6 5.2 %collective-permute-done.38.refs_5_ = bf16[256,512]{1,0:T(8,128)(2,1)S(1)} collective-permute-done((bf16[256,512]{1,0:T(8,128)(2,1)S(1)}, bf16[256,512]{1,0:T(8,128)(2,1)S(1)}, u32[]{:S(2)}, u32[]{:S(2)}) %collective-permute-start.38) | collective-permute-done | bytes 262176 | tf_op jit(solution)/shard_map/grads_z/ppermute | solution.py:446
  169.8 2.4 %collective-permute-done.39 = bf16[512,512]{1,0:T(8,128)(2,1)S(1)} collective-permute-done((bf16[512,512]{1,0:T(8,128)(2,1)S(1)}, bf16[512,512]{1,0:T(8,128)(2,1)S(1)}, u32[]{:S(2)}, u32[]{:S(2)}) %collective-permute-start.39) | collective-permute-done | bytes 524320 | tf_op jit(solution)/shard_map/grads_xy/ppermute | solution.py:446
  172.6 1.8 %activated.1 = bf16[512,512]{1,0:T(8,128)(2,1)} custom-call(s32[44]{0:T(128)S(1)} %pad_add_fusion.1.where_ref, bf16[1024,512]{1,0:T(8,128)(2,1)S(1)} %forward.5.mine_ref, bf16[1024,512]{1,0:T(8,128)(2,1)S(1)} %collective-permute-done.19.other_ref, bf16[512,512]{1,0:T(8,128)(2,1)S(1)} %copy-done.2, bf16[1024,512]{1,0:T(8,128)(2,1)S(1)} %pad_maximum_fusion.cot_ref), custom_call_target="tpu_custom_call" | custom-call | flops 268435456 | bytes 2097152 | tf_op jit(solution)/shard_map/activated/pallas_call | solution.py:314
  174.4 4.6 %collective-permute-done.41.refs_1_ = bf16[512,512]{1,0:T(8,128)(2,1)S(1)} collective-permute-done((bf16[512,512]{1,0:T(8,128)(2,1)S(1)}, bf16[512,512]{1,0:T(8,128)(2,1)S(1)}, u32[]{:S(2)}, u32[]{:S(2)}) %collective-permute-start.41) | collective-permute-done | bytes 524320 | tf_op jit(solution)/shard_map/grads_xy/ppermute | solution.py:446
  179.1 2.6 %collective-permute-done.43.refs_3_ = bf16[512,512]{1,0:T(8,128)(2,1)S(1)} collective-permute-done((bf16[512,512]{1,0:T(8,128)(2,1)S(1)}, bf16[512,512]{1,0:T(8,128)(2,1)S(1)}, u32[]{:S(2)}, u32[]{:S(2)}) %collective-permute-start.43) | collective-permute-done | bytes 524320 | tf_op jit(solution)/shard_map/grads_z/ppermute | solution.py:446
  181.7 2.1 %grads_out.1 = (bf16[1,512,512]{2,1,0:T(8,128)(2,1)}, f32[512,512]{1,0:T(8,128)}) custom-call(s32[44]{0:T(128)S(1)} %pad_add_fusion.1.where_ref, bf16[512,512]{1,0:T(8,128)(2,1)S(1)} %get-tuple-element.289.refs_0_, bf16[512,512]{1,0:T(8,128)(2,1)S(1)} %collective-permute-done.41.refs_1_, bf16[512,512]{1,0:T(8,128)(2,1)S(1)} %collective-permute-done.42.refs_2_, ...), custom_call_target="tpu_custom_call" | custom-call | flops 1048576 | bytes 2621440 | tf_op jit(solution)/shard_map/grads_out/pallas_call | solution.py:412
  (78 shorter events, 6.1 us)
Async XLA Ops:
  0.6 1.2 copy-start
  0.6 17.0 %collective-permute-start = (bf16[8,24,128,128]{3,2,1,0:T(8,128)(2,1)}, bf16[8,24,128,128]{3,2,1,0:T(8,128)(2,1)}, u32[]{:S(2)}, u32[]{:S(2)}) collective-permute-start(bf16[8,24,128,128]{3,2,1,0:T(8,128)(2,1)} %bitcast.16), channel_id=1, source_target_pairs={{0,1},{1,0},{2,3},{3,2},{4,5},{5,4},{6,7},{7,6},{8,9},{9,8},{10,11... | collective-permute-start | bytes 18874376 | tf_op jit(solution)/shard_map/tiles_exchange/ppermute | solution.py:446
  1.9 15.7 %collective-permute-start.2 = (bf16[512,512]{1,0:T(8,128)(2,1)S(1)}, bf16[512,512]{1,0:T(8,128)(2,1)S(1)}, u32[]{:S(2)}, u32[]{:S(2)}) collective-permute-start(bf16[512,512]{1,0:T(8,128)(2,1)S(1)} %constant_dynamic-slice_fusion.refs_2_), channel_id=1, source_target_pairs={{0,8},{1,9},{2,10},{3,11},{4,12},{5,13},{6,14},{7,15},{8,0},{9,1},... | collective-permute-start | bytes 1572872 | tf_op jit(solution)/shard_map/features_z/ppermute | solution.py:446
  5.0 17.7 %collective-permute-start.3 = (bf16[512,512]{1,0:T(8,128)(2,1)S(1)}, bf16[512,512]{1,0:T(8,128)(2,1)S(1)}, u32[]{:S(2)}, u32[]{:S(2)}) collective-permute-start(bf16[512,512]{1,0:T(8,128)(2,1)S(1)} %constant_dynamic-slice_fusion.refs_2_), channel_id=1, source_target_pairs={{0,2},{1,3},{2,0},{3,1},{4,6},{5,7},{6,4},{7,5},{8,10},{9,11},{10,... | collective-permute-start | bytes 1572872 | tf_op jit(solution)/shard_map/features_xy/ppermute | solution.py:446
  6.5 16.2 %collective-permute-start.4 = (bf16[512,512]{1,0:T(8,128)(2,1)S(1)}, bf16[512,512]{1,0:T(8,128)(2,1)S(1)}, u32[]{:S(2)}, u32[]{:S(2)}) collective-permute-start(bf16[512,512]{1,0:T(8,128)(2,1)S(1)} %constant_dynamic-slice_fusion.refs_2_), channel_id=1, source_target_pairs={{0,4},{1,5},{2,6},{3,7},{4,0},{5,1},{6,2},{7,3},{8,12},{9,13},{10,... | collective-permute-start | bytes 1572872 | tf_op jit(solution)/shard_map/features_xy/ppermute | solution.py:446
  9.5 8.1 %collective-permute-start.1 = (s32[8,25]{1,0:T(8,128)S(1)}, s32[8,25]{1,0:T(8,128)S(1)}, u32[]{:S(2)}, u32[]{:S(2)}) collective-permute-start(s32[8,25]{1,0:T(8,128)S(1)} %pad_add_fusion.packed_ref), channel_id=1, source_target_pairs={{0,1},{1,0},{2,3},{3,2},{4,5},{5,4},{6,7},{7,6},{8,9},{9,8},{10,11... | collective-permute-start | bytes 2408 | tf_op jit(solution)/shard_map/tiles_exchange/ppermute | solution.py:446
  17.6 14.5 %collective-permute-start.5 = (bf16[512,512]{1,0:T(8,128)(2,1)S(1)}, bf16[512,512]{1,0:T(8,128)(2,1)S(1)}, u32[]{:S(2)}, u32[]{:S(2)}) collective-permute-start(bf16[512,512]{1,0:T(8,128)(2,1)S(1)} %collective-permute-done.2.refs_5_), channel_id=1, source_target_pairs={{0,2},{1,3},{2,0},{3,1},{4,6},{5,7},{6,4},{7,5},{8,10},{9,11},{10,... | collective-permute-start | bytes 1572872 | tf_op jit(solution)/shard_map/features_xy/ppermute | solution.py:446
  18.6 13.7 %collective-permute-start.6 = (bf16[512,512]{1,0:T(8,128)(2,1)S(1)}, bf16[512,512]{1,0:T(8,128)(2,1)S(1)}, u32[]{:S(2)}, u32[]{:S(2)}) collective-permute-start(bf16[512,512]{1,0:T(8,128)(2,1)S(1)} %collective-permute-done.2.refs_5_), channel_id=1, source_target_pairs={{0,4},{1,5},{2,6},{3,7},{4,0},{5,1},{6,2},{7,3},{8,12},{9,13},{10,... | collective-permute-start | bytes 1572872 | tf_op jit(solution)/shard_map/features_xy/ppermute | solution.py:446
  20.1 28.4 %collective-permute-start.7 = (bf16[512,512]{1,0:T(8,128)(2,1)S(1)}, bf16[512,512]{1,0:T(8,128)(2,1)}, u32[]{:S(2)}, u32[]{:S(2)}) collective-permute-start(bf16[512,512]{1,0:T(8,128)(2,1)S(1)} %constant_dynamic-slice_fusion.refs_2_), channel_id=1, source_target_pairs={{0,16},{1,17},{2,18},{3,19},{4,20},{5,21},{6,22},{7,23},{8,24},{9,... | collective-permute-start | bytes 1572872 | tf_op jit(solution)/shard_map/features_z/ppermute | solution.py:446
  32.3 16.2 %collective-permute-start.8 = (bf16[512,512]{1,0:T(8,128)(2,1)S(1)}, bf16[512,512]{1,0:T(8,128)(2,1)S(1)}, u32[]{:S(2)}, u32[]{:S(2)}) collective-permute-start(bf16[512,512]{1,0:T(8,128)(2,1)S(1)} %collective-permute-done.3.refs_3_), channel_id=1, source_target_pairs={{0,4},{1,5},{2,6},{3,7},{4,0},{5,1},{6,2},{7,3},{8,12},{9,13},{10,... | collective-permute-start | bytes 1572872 | tf_op jit(solution)/shard_map/features_xy/ppermute | solution.py:446
  32.6 16.6 %collective-permute-start.9 = (bf16[512,512]{1,0:T(8,128)(2,1)S(1)}, bf16[512,512]{1,0:T(8,128)(2,1)S(1)}, u32[]{:S(2)}, u32[]{:S(2)}) collective-permute-start(bf16[512,512]{1,0:T(8,128)(2,1)S(1)} %collective-permute-done.6.refs_7_), channel_id=1, source_target_pairs={{0,2},{1,3},{2,0},{3,1},{4,6},{5,7},{6,4},{7,5},{8,10},{9,11},{10,... | collective-permute-start | bytes 1572872 | tf_op jit(solution)/shard_map/features_xy/ppermute | solution.py:446
  34.2 16.5 %collective-permute-start.13 = (bf16[512,512]{1,0:T(8,128)(2,1)}, bf16[512,512]{1,0:T(8,128)(2,1)}, u32[]{:S(2)}, u32[]{:S(2)}) collective-permute-start(bf16[512,512]{1,0:T(8,128)(2,1)} %param.14), channel_id=1, source_target_pairs={{0,1},{1,0},{2,3},{3,2},{4,5},{5,4},{6,7},{7,6},{8,9},{9,8},{10,11... | collective-permute-start | bytes 1572872 | tf_op jit(solution)/shard_map/cotangents/ppermute | solution.py:446
  48.5 0.8 copy-start.3
  49.3 0.8 copy-start.5
  50.0 14.6 %collective-permute-start.10 = (bf16[512,512]{1,0:T(8,128)(2,1)}, bf16[512,512]{1,0:T(8,128)(2,1)}, u32[]{:S(2)}, u32[]{:S(2)}) collective-permute-start(bf16[512,512]{1,0:T(8,128)(2,1)} %collective-permute-done.7.refs_10_), channel_id=1, source_target_pairs={{0,2},{1,3},{2,0},{3,1},{4,6},{5,7},{6,4},{7,5},{8,10},{9,11},{10,... | collective-permute-start | bytes 1572872 | tf_op jit(solution)/shard_map/features_xy/ppermute | solution.py:446
  50.0 14.6 %collective-permute-start.11 = (bf16[512,512]{1,0:T(8,128)(2,1)}, bf16[512,512]{1,0:T(8,128)(2,1)}, u32[]{:S(2)}, u32[]{:S(2)}) collective-permute-start(bf16[512,512]{1,0:T(8,128)(2,1)} %collective-permute-done.7.refs_10_), channel_id=1, source_target_pairs={{0,4},{1,5},{2,6},{3,7},{4,0},{5,1},{6,2},{7,3},{8,12},{9,13},{10,... | collective-permute-start | bytes 1572872 | tf_op jit(solution)/shard_map/features_xy/ppermute | solution.py:446
  50.1 14.5 %collective-permute-start.12 = (bf16[512,512]{1,0:T(8,128)(2,1)}, bf16[512,512]{1,0:T(8,128)(2,1)}, u32[]{:S(2)}, u32[]{:S(2)}) collective-permute-start(bf16[512,512]{1,0:T(8,128)(2,1)} %collective-permute-done.7.refs_10_), channel_id=1, source_target_pairs={{0,8},{1,9},{2,10},{3,11},{4,12},{5,13},{6,14},{7,15},{8,0},{9,1},... | collective-permute-start | bytes 1572872 | tf_op jit(solution)/shard_map/features_z/ppermute | solution.py:446
  52.1 16.4 %copy-start.4 = (bf16[512,512]{1,0:T(8,128)(2,1)S(1)}, bf16[512,512]{1,0:T(8,128)(2,1)}, u32[]{:S(2)}) copy-start(bf16[512,512]{1,0:T(8,128)(2,1)} %copy-done.3) | copy-start | bytes 1572868
  52.1 16.4 %copy-start.6 = (bf16[512,512]{1,0:T(8,128)(2,1)S(1)}, bf16[512,512]{1,0:T(8,128)(2,1)}, u32[]{:S(2)}) copy-start(bf16[512,512]{1,0:T(8,128)(2,1)} %copy-done.5) | copy-start | bytes 1572868
  64.6 13.7 %collective-permute-start.14 = (bf16[512,512]{1,0:T(8,128)(2,1)}, bf16[512,512]{1,0:T(8,128)(2,1)S(1)}, u32[]{:S(2)}, u32[]{:S(2)}) collective-permute-start(bf16[512,512]{1,0:T(8,128)(2,1)} %collective-permute-done.11.refs_2_), channel_id=1, source_target_pairs={{0,2},{1,3},{2,0},{3,1},{4,6},{5,7},{6,4},{7,5},{8,10},{9,11},{10,... | collective-permute-start | bytes 1572872 | tf_op jit(solution)/shard_map/features_xy/ppermute | solution.py:446
  66.4 13.1 %collective-permute-start.15 = (bf16[512,512]{1,0:T(8,128)(2,1)}, bf16[512,512]{1,0:T(8,128)(2,1)S(1)}, u32[]{:S(2)}, u32[]{:S(2)}) collective-permute-start(bf16[512,512]{1,0:T(8,128)(2,1)} %collective-permute-done.12.refs_3_), channel_id=1, source_target_pairs={{0,4},{1,5},{2,6},{3,7},{4,0},{5,1},{6,2},{7,3},{8,12},{9,13},{10,... | collective-permute-start | bytes 1572872 | tf_op jit(solution)/shard_map/features_xy/ppermute | solution.py:446
  68.1 12.5 %collective-permute-start.16 = (bf16[512,512]{1,0:T(8,128)(2,1)}, bf16[512,512]{1,0:T(8,128)(2,1)S(1)}, u32[]{:S(2)}, u32[]{:S(2)}) collective-permute-start(bf16[512,512]{1,0:T(8,128)(2,1)} %collective-permute-done.10.refs_11_), channel_id=1, source_target_pairs={{0,8},{1,9},{2,10},{3,11},{4,12},{5,13},{6,14},{7,15},{8,0},{9,1},... | collective-permute-start | bytes 1572872 | tf_op jit(solution)/shard_map/features_z/ppermute | solution.py:446
  80.6 6.5 %collective-permute-start.17 = (bf16[256,512]{1,0:T(8,128)(2,1)S(1)}, bf16[256,512]{1,0:T(8,128)(2,1)S(1)}, u32[]{:S(2)}, u32[]{:S(2)}) collective-permute-start(bf16[256,512]{1,0:T(8,128)(2,1)S(1)} %slice.42), channel_id=1, source_target_pairs={{0,2},{1,3},{2,0},{3,1},{4,6},{5,7},{6,4},{7,5},{8,10},{9,11},{10,... | collective-permute-start | bytes 786440 | tf_op jit(solution)/shard_map/features_xy/ppermute | solution.py:446
  81.3 6.4 %collective-permute-start.18 = (bf16[256,512]{1,0:T(8,128)(2,1)S(1)}, bf16[256,512]{1,0:T(8,128)(2,1)S(1)}, u32[]{:S(2)}, u32[]{:S(2)}) collective-permute-start(bf16[256,512]{1,0:T(8,128)(2,1)S(1)} %slice.43), channel_id=1, source_target_pairs={{0,4},{1,5},{2,6},{3,7},{4,0},{5,1},{6,2},{7,3},{8,12},{9,13},{10,... | collective-permute-start | bytes 786440 | tf_op jit(solution)/shard_map/features_xy/ppermute | solution.py:446
  87.1 6.8 %copy-start.2 = (bf16[512,512]{1,0:T(8,128)(2,1)S(1)}, bf16[512,512]{1,0:T(8,128)(2,1)}, u32[]{:S(2)}) copy-start(bf16[512,512]{1,0:T(8,128)(2,1)} %weight_ref.3) | copy-start | bytes 1572868
  91.2 2.7 %collective-permute-start.19 = (bf16[1024,512]{1,0:T(8,128)(2,1)S(1)}, bf16[1024,512]{1,0:T(8,128)(2,1)S(1)}, u32[]{:S(2)}, u32[]{:S(2)}) collective-permute-start(bf16[1024,512]{1,0:T(8,128)(2,1)S(1)} %forward.5.mine_ref), channel_id=1, source_target_pairs={{0,1},{1,0},{2,3},{3,2},{4,5},{5,4},{6,7},{7,6},{8,9},{9,8},{10,11... | collective-permute-start | bytes 3145736 | tf_op jit(solution)/shard_map/partial_sums/ppermute | solution.py:446
  100.5 11.4 %collective-permute-start.22 = (bf16[64,512]{1,0:T(8,128)(2,1)S(1)}, bf16[64,512]{1,0:T(8,128)(2,1)S(1)}, u32[]{:S(2)}, u32[]{:S(2)}) collective-permute-start(bf16[64,512]{1,0:T(8,128)(2,1)S(1)} %get-tuple-element.304), channel_id=1, source_target_pairs={{0,24},{1,25},{2,26},{3,27},{4,28},{5,29},{6,30},{7,31},{8,16},{9,... | collective-permute-start | bytes 196616 | tf_op jit(solution)/shard_map/weight_grad/ppermute | solution.py:446
  103.6 8.9 %collective-permute-start.21 = (bf16[64,512]{1,0:T(8,128)(2,1)S(1)}, bf16[64,512]{1,0:T(8,128)(2,1)S(1)}, u32[]{:S(2)}, u32[]{:S(2)}) collective-permute-start(bf16[64,512]{1,0:T(8,128)(2,1)S(1)} %get-tuple-element.305), channel_id=1, source_target_pairs={{0,16},{1,17},{2,18},{3,19},{4,20},{5,21},{6,22},{7,23},{8,24},{9,... | collective-permute-start | bytes 196616 | tf_op jit(solution)/shard_map/weight_grad/ppermute | solution.py:446
  103.6 8.9 %collective-permute-start.20 = (bf16[64,512]{1,0:T(8,128)(2,1)S(1)}, bf16[64,512]{1,0:T(8,128)(2,1)S(1)}, u32[]{:S(2)}, u32[]{:S(2)}) collective-permute-start(bf16[64,512]{1,0:T(8,128)(2,1)S(1)} %get-tuple-element.303), channel_id=1, source_target_pairs={{0,8},{1,9},{2,10},{3,11},{4,12},{5,13},{6,14},{7,15},{8,0},{9,1},... | collective-permute-start | bytes 196616 | tf_op jit(solution)/shard_map/weight_grad/ppermute | solution.py:446
  104.9 7.6 %collective-permute-start.23 = (bf16[256,512]{1,0:T(8,128)(2,1)S(1)}, bf16[256,512]{1,0:T(8,128)(2,1)S(1)}, u32[]{:S(2)}, u32[]{:S(2)}) collective-permute-start(bf16[256,512]{1,0:T(8,128)(2,1)S(1)} %get-tuple-element.214), channel_id=1, source_target_pairs={{0,2},{1,3},{2,0},{3,1},{4,6},{5,7},{6,4},{7,5},{8,10},{9,11},{10,... | collective-permute-start | bytes 786440 | tf_op jit(solution)/shard_map/grads_xy/ppermute | solution.py:446
  106.4 7.2 %collective-permute-start.24 = (bf16[256,512]{1,0:T(8,128)(2,1)S(1)}, bf16[256,512]{1,0:T(8,128)(2,1)S(1)}, u32[]{:S(2)}, u32[]{:S(2)}) collective-permute-start(bf16[256,512]{1,0:T(8,128)(2,1)S(1)} %get-tuple-element.215), channel_id=1, source_target_pairs={{0,4},{1,5},{2,6},{3,7},{4,0},{5,1},{6,2},{7,3},{8,12},{9,13},{10,... | collective-permute-start | bytes 786440 | tf_op jit(solution)/shard_map/grads_xy/ppermute | solution.py:446
  111.8 14.1 %collective-permute-start.26 = (bf16[512,512]{1,0:T(8,128)(2,1)S(1)}, bf16[512,512]{1,0:T(8,128)(2,1)S(1)}, u32[]{:S(2)}, u32[]{:S(2)}) collective-permute-start(bf16[512,512]{1,0:T(8,128)(2,1)S(1)} %get-tuple-element.226), channel_id=1, source_target_pairs={{0,2},{1,3},{2,0},{3,1},{4,6},{5,7},{6,4},{7,5},{8,10},{9,11},{10,... | collective-permute-start | bytes 1572872 | tf_op jit(solution)/shard_map/grads_xy/ppermute | solution.py:446
  113.7 12.2 %collective-permute-start.27 = (bf16[512,512]{1,0:T(8,128)(2,1)S(1)}, bf16[512,512]{1,0:T(8,128)(2,1)S(1)}, u32[]{:S(2)}, u32[]{:S(2)}) collective-permute-start(bf16[512,512]{1,0:T(8,128)(2,1)S(1)} %get-tuple-element.231), channel_id=1, source_target_pairs={{0,4},{1,5},{2,6},{3,7},{4,0},{5,1},{6,2},{7,3},{8,12},{9,13},{10,... | collective-permute-start | bytes 1572872 | tf_op jit(solution)/shard_map/grads_xy/ppermute | solution.py:446
  114.6 11.6 %collective-permute-start.28 = (bf16[512,512]{1,0:T(8,128)(2,1)S(1)}, bf16[512,512]{1,0:T(8,128)(2,1)S(1)}, u32[]{:S(2)}, u32[]{:S(2)}) collective-permute-start(bf16[512,512]{1,0:T(8,128)(2,1)S(1)} %get-tuple-element.232), channel_id=1, source_target_pairs={{0,8},{1,9},{2,10},{3,11},{4,12},{5,13},{6,14},{7,15},{8,0},{9,1},... | collective-permute-start | bytes 1572872 | tf_op jit(solution)/shard_map/grads_z/ppermute | solution.py:446
  120.7 5.2 %collective-permute-start.25 = (bf16[64,512]{1,0:T(8,128)(2,1)S(1)}, bf16[64,512]{1,0:T(8,128)(2,1)S(1)}, u32[]{:S(2)}, u32[]{:S(2)}) collective-permute-start(bf16[64,512]{1,0:T(8,128)(2,1)S(1)} %fusion.2), channel_id=1, source_target_pairs={{0,2},{1,3},{2,0},{3,1},{4,6},{5,7},{6,4},{7,5},{8,10},{9,11},{10,... | collective-permute-start | bytes 196616 | tf_op jit(solution)/shard_map/weight_grad/ppermute | solution.py:446
  126.4 17.5 %collective-permute-start.30 = (bf16[512,512]{1,0:T(8,128)(2,1)S(1)}, bf16[512,512]{1,0:T(8,128)(2,1)S(1)}, u32[]{:S(2)}, u32[]{:S(2)}) collective-permute-start(bf16[512,512]{1,0:T(8,128)(2,1)S(1)} %add_convert_fusion.5), channel_id=1, source_target_pairs={{0,2},{1,3},{2,0},{3,1},{4,6},{5,7},{6,4},{7,5},{8,10},{9,11},{10,... | collective-permute-start | bytes 1572872 | tf_op jit(solution)/shard_map/grads_xy/ppermute | solution.py:446
  127.7 16.2 %collective-permute-start.31 = (bf16[512,512]{1,0:T(8,128)(2,1)S(1)}, bf16[512,512]{1,0:T(8,128)(2,1)S(1)}, u32[]{:S(2)}, u32[]{:S(2)}) collective-permute-start(bf16[512,512]{1,0:T(8,128)(2,1)S(1)} %add_convert_fusion.4), channel_id=1, source_target_pairs={{0,4},{1,5},{2,6},{3,7},{4,0},{5,1},{6,2},{7,3},{8,12},{9,13},{10,... | collective-permute-start | bytes 1572872 | tf_op jit(solution)/shard_map/grads_xy/ppermute | solution.py:446
  128.8 15.1 %collective-permute-start.32 = (bf16[512,512]{1,0:T(8,128)(2,1)S(1)}, bf16[512,512]{1,0:T(8,128)(2,1)S(1)}, u32[]{:S(2)}, u32[]{:S(2)}) collective-permute-start(bf16[512,512]{1,0:T(8,128)(2,1)S(1)} %add_convert_fusion.3), channel_id=1, source_target_pairs={{0,8},{1,9},{2,10},{3,11},{4,12},{5,13},{6,14},{7,15},{8,0},{9,1},... | collective-permute-start | bytes 1572872 | tf_op jit(solution)/shard_map/grads_z/ppermute | solution.py:446
  136.6 6.0 %collective-permute-start.29 = (bf16[64,512]{1,0:T(8,128)(2,1)S(1)}, bf16[64,512]{1,0:T(8,128)(2,1)S(1)}, u32[]{:S(2)}, u32[]{:S(2)}) collective-permute-start(bf16[64,512]{1,0:T(8,128)(2,1)S(1)} %add_convert_fusion.9), channel_id=1, source_target_pairs={{0,4},{1,5},{2,6},{3,7},{4,0},{5,1},{6,2},{7,3},{8,12},{9,13},{10,... | collective-permute-start | bytes 196616 | tf_op jit(solution)/shard_map/weight_grad/ppermute | solution.py:446
  137.9 19.2 %collective-permute-start.34 = (bf16[512,512]{1,0:T(8,128)(2,1)S(1)}, bf16[512,512]{1,0:T(8,128)(2,1)S(1)}, u32[]{:S(2)}, u32[]{:S(2)}) collective-permute-start(bf16[512,512]{1,0:T(8,128)(2,1)S(1)} %get-tuple-element.260), channel_id=1, source_target_pairs={{0,4},{1,5},{2,6},{3,7},{4,0},{5,1},{6,2},{7,3},{8,12},{9,13},{10,... | collective-permute-start | bytes 1572872 | tf_op jit(solution)/shard_map/grads_xy/ppermute | solution.py:446
  142.6 14.5 %collective-permute-start.35 = (bf16[512,512]{1,0:T(8,128)(2,1)S(1)}, bf16[512,512]{1,0:T(8,128)(2,1)S(1)}, u32[]{:S(2)}, u32[]{:S(2)}) collective-permute-start(bf16[512,512]{1,0:T(8,128)(2,1)S(1)} %get-tuple-element.261), channel_id=1, source_target_pairs={{0,2},{1,3},{2,0},{3,1},{4,6},{5,7},{6,4},{7,5},{8,10},{9,11},{10,... | collective-permute-start | bytes 1572872 | tf_op jit(solution)/shard_map/grads_xy/ppermute | solution.py:446
  144.2 12.9 %collective-permute-start.36 = (bf16[256,512]{1,0:T(8,128)(2,1)S(1)}, bf16[256,512]{1,0:T(8,128)(2,1)S(1)}, u32[]{:S(2)}, u32[]{:S(2)}) collective-permute-start(bf16[256,512]{1,0:T(8,128)(2,1)S(1)} %get-tuple-element.300), channel_id=1, source_target_pairs={{0,16},{1,17},{2,18},{3,19},{4,20},{5,21},{6,22},{7,23},{8,24},{9,... | collective-permute-start | bytes 786440 | tf_op jit(solution)/shard_map/grads_z/ppermute | solution.py:446
  150.2 6.8 %collective-permute-start.33 = (bf16[1,64,512]{2,1,0:T(8,128)(2,1)S(1)}, bf16[1,64,512]{2,1,0:T(8,128)(2,1)S(1)}, u32[]{:S(2)}, u32[]{:S(2)}) collective-permute-start(bf16[1,64,512]{2,1,0:T(8,128)(2,1)S(1)} %bitcast.19), channel_id=1, source_target_pairs={{0,16},{1,17},{2,18},{3,19},{4,20},{5,21},{6,22},{7,23},{8,24},{9,... | collective-permute-start | bytes 196616 | tf_op jit(solution)/shard_map/weight_grad/ppermute | solution.py:446
  151.9 17.9 %collective-permute-start.40 = (bf16[512,512]{1,0:T(8,128)(2,1)S(1)}, bf16[512,512]{1,0:T(8,128)(2,1)S(1)}, u32[]{:S(2)}, u32[]{:S(2)}) collective-permute-start(bf16[512,512]{1,0:T(8,128)(2,1)S(1)} %get-tuple-element.277), channel_id=1, source_target_pairs={{0,4},{1,5},{2,6},{3,7},{4,0},{5,1},{6,2},{7,3},{8,12},{9,13},{10,... | collective-permute-start | bytes 1572872 | tf_op jit(solution)/shard_map/grads_xy/ppermute | solution.py:446
  157.3 14.9 %collective-permute-start.39 = (bf16[512,512]{1,0:T(8,128)(2,1)S(1)}, bf16[512,512]{1,0:T(8,128)(2,1)S(1)}, u32[]{:S(2)}, u32[]{:S(2)}) collective-permute-start(bf16[512,512]{1,0:T(8,128)(2,1)S(1)} %add_convert_fusion.2), channel_id=1, source_target_pairs={{0,2},{1,3},{2,0},{3,1},{4,6},{5,7},{6,4},{7,5},{8,10},{9,11},{10,... | collective-permute-start | bytes 1572872 | tf_op jit(solution)/shard_map/grads_xy/ppermute | solution.py:446
  157.5 7.1 %collective-permute-start.37 = (bf16[2,64,512]{2,1,0:T(8,128)(2,1)S(1)}, bf16[2,64,512]{2,1,0:T(8,128)(2,1)S(1)}, u32[]{:S(2)}, u32[]{:S(2)}) collective-permute-start(bf16[2,64,512]{2,1,0:T(8,128)(2,1)S(1)} %pad_maximum_fusion.2), channel_id=1, source_target_pairs={{0,8},{1,9},{2,10},{3,11},{4,12},{5,13},{6,14},{7,15},{8,0},{9,1},... | collective-permute-start | bytes 393224 | tf_op jit(solution)/shard_map/weight_grad/ppermute | solution.py:446
  160.2 9.6 %collective-permute-start.38 = (bf16[256,512]{1,0:T(8,128)(2,1)S(1)}, bf16[256,512]{1,0:T(8,128)(2,1)S(1)}, u32[]{:S(2)}, u32[]{:S(2)}) collective-permute-start(bf16[256,512]{1,0:T(8,128)(2,1)S(1)} %get-tuple-element.273), channel_id=1, source_target_pairs={{0,16},{1,17},{2,18},{3,19},{4,20},{5,21},{6,22},{7,23},{8,24},{9,... | collective-permute-start | bytes 786440 | tf_op jit(solution)/shard_map/grads_z/ppermute | solution.py:446
  160.3 18.8 %collective-permute-start.41 = (bf16[512,512]{1,0:T(8,128)(2,1)S(1)}, bf16[512,512]{1,0:T(8,128)(2,1)S(1)}, u32[]{:S(2)}, u32[]{:S(2)}) collective-permute-start(bf16[512,512]{1,0:T(8,128)(2,1)S(1)} %get-tuple-element.281), channel_id=1, source_target_pairs={{0,2},{1,3},{2,0},{3,1},{4,6},{5,7},{6,4},{7,5},{8,10},{9,11},{10,... | collective-permute-start | bytes 1572872 | tf_op jit(solution)/shard_map/grads_xy/ppermute | solution.py:446
  164.6 14.5 %collective-permute-start.42 = (bf16[512,512]{1,0:T(8,128)(2,1)S(1)}, bf16[512,512]{1,0:T(8,128)(2,1)S(1)}, u32[]{:S(2)}, u32[]{:S(2)}) collective-permute-start(bf16[512,512]{1,0:T(8,128)(2,1)S(1)} %add_convert_fusion.1), channel_id=1, source_target_pairs={{0,4},{1,5},{2,6},{3,7},{4,0},{5,1},{6,2},{7,3},{8,12},{9,13},{10,... | collective-permute-start | bytes 1572872 | tf_op jit(solution)/shard_map/grads_xy/ppermute | solution.py:446
  172.2 11.6 %copy-start.1 = (bf16[1024,512]{1,0:T(8,128)(2,1)S(1)}, bf16[1024,512]{1,0:T(8,128)(2,1)}, u32[]{:S(2)}) copy-start(bf16[1024,512]{1,0:T(8,128)(2,1)} %param.8) | copy-start | bytes 3145732
  172.4 9.2 %collective-permute-start.43 = (bf16[512,512]{1,0:T(8,128)(2,1)S(1)}, bf16[512,512]{1,0:T(8,128)(2,1)S(1)}, u32[]{:S(2)}, u32[]{:S(2)}) collective-permute-start(bf16[512,512]{1,0:T(8,128)(2,1)S(1)} %add_convert_fusion), channel_id=1, source_target_pairs={{0,8},{1,9},{2,10},{3,11},{4,12},{5,13},{6,14},{7,15},{8,0},{9,1},... | collective-permute-start | bytes 1572872 | tf_op jit(solution)/shard_map/grads_z/ppermute | solution.py:446
  172.5 6.6 %collective-permute-start.44 = (bf16[4,64,512]{2,1,0:T(8,128)(2,1)S(1)}, bf16[4,64,512]{2,1,0:T(8,128)(2,1)S(1)}, u32[]{:S(2)}, u32[]{:S(2)}) collective-permute-start(bf16[4,64,512]{2,1,0:T(8,128)(2,1)S(1)} %pad_maximum_fusion.1.refs_6_), channel_id=1, source_target_pairs={{0,1},{1,0},{2,3},{3,2},{4,5},{5,4},{6,7},{7,6},{8,9},{9,8},{10,11... | collective-permute-start | bytes 786440 | tf_op jit(solution)/shard_map/weight_grad/ppermute | solution.py:446

commit v13 on v12

--- a/solution.py
+++ b/solution.py
@@ -18,6 +18,12 @@
     return pltpu.with_memory_space_constraint(value, pltpu.HBM)
 
 
+def tile_place(place, row_tiles, per_part):
+    row_bits, part_bits = row_tiles.bit_length() - 1, per_part.bit_length() - 1
+    tile_col = place & (row_tiles - 1)
+    return place >> row_bits, tile_col >> part_bits, tile_col & (per_part - 1)
+
+
 def dense_kernel(first, where_ref, packed_ref, tiles_ref, *refs):
     out_ref = refs[-1]
     panel = first + pl.program_id(0)
@@ -26,11 +32,10 @@
     out_ref[...] = jnp.zeros_like(out_ref)
 
     def add_tile(slot, carry):
-        place = packed_ref[panel, slot]
-        row = pl.multiple_of(place // row_tiles * size, size)
-        tile_col = place % row_tiles
-        col = pl.multiple_of(tile_col % per_part * size, size)
-        out_ref[tile_col // per_part, 0, pl.ds(row, size), pl.ds(col, size)] += tiles_ref[0, slot]
+        row, part, col = tile_place(packed_ref[panel, slot], row_tiles, per_part)
+        rows = pl.ds(pl.multiple_of(row * size, size), size)
+        cols = pl.ds(pl.multiple_of(col * size, size), size)
+        out_ref[part, 0, rows, cols] += tiles_ref[0, slot]
         return carry
 
     lax.fori_loop(0, packed_ref[panel, slots], add_tile, 0)
@@ -52,7 +57,7 @@
             out_specs=pl.BlockSpec((n_rep, 1, block_rows, part), lambda p, *_: (0, at(p), 0, 0)),
         ),
         input_output_aliases={3: 0} if first else {},
-        compiler_params=pltpu.CompilerParams(vmem_limit_bytes=36 * 2**20),
+        compiler_params=pltpu.CompilerParams(vmem_limit_bytes=24 * 2**20),
         cost_estimate=pl.CostEstimate(
             flops=0,
             transcendentals=0,
@@ -68,14 +73,13 @@
     out_ref[...] = jnp.zeros_like(out_ref)
 
     def add_tile(slot, carry):
-        place = packed_ref[panel, slot]
-        row = pl.multiple_of(place // row_tiles * size, size)
-        tile_col = place % row_tiles
-        col = pl.multiple_of(tile_col % per_part * size, size)
-
-        @pl.when(tile_col // per_part == where_ref[0])
+        row, part, col = tile_place(packed_ref[panel, slot], row_tiles, per_part)
+        rows = pl.ds(pl.multiple_of(row * size, size), size)
+        cols = pl.ds(pl.multiple_of(col * size, size), size)
+
+        @pl.when(part == where_ref[0])
         def _():
-            out_ref[0, pl.ds(row, size), pl.ds(col, size)] += tiles_ref[0, slot]
+            out_ref[0, rows, cols] += tiles_ref[0, slot]
 
         return carry
 
@@ -95,7 +99,7 @@
             in_specs=[pl.BlockSpec((1, slots, size, size), lambda p, *_: (first + p, 0, 0, 0))],
             out_specs=pl.BlockSpec((1, block_rows, part), lambda p, *_: (p, 0, 0)),
         ),
-        compiler_params=pltpu.CompilerParams(vmem_limit_bytes=36 * 2**20),
+        compiler_params=pltpu.CompilerParams(vmem_limit_bytes=24 * 2**20),
         cost_estimate=pl.CostEstimate(
             flops=0, transcendentals=0, bytes_accessed=tiles.size // 8
         ),
@@ -205,7 +209,7 @@
                 pltpu.SemaphoreType.DMA,
             ],
         ),
-        compiler_params=pltpu.CompilerParams(vmem_limit_bytes=36 * 2**20),
+        compiler_params=pltpu.CompilerParams(vmem_limit_bytes=24 * 2**20),
         cost_estimate=pl.CostEstimate(
             flops=2 * n_units * rows * part * width,
             transcendentals=0,
@@ -293,7 +297,7 @@
             ],
             scratch_shapes=[pltpu.VMEM((width, width), F32), pltpu.VMEM((width, rows), BF16)],
         ),
-        compiler_params=pltpu.CompilerParams(vmem_limit_bytes=36 * 2**20),
+        compiler_params=pltpu.CompilerParams(vmem_limit_bytes=24 * 2**20),
         cost_estimate=pl.CostEstimate(
             flops=6 * rows * width * width + 4 * rows * width * cols,
             transcendentals=rows * width,
@@ -320,7 +324,7 @@
             in_specs=[block, block, fixed(width, width), block],
             out_specs=fixed(part, width),
         ),
-        compiler_params=pltpu.CompilerParams(vmem_limit_bytes=36 * 2**20),
+        compiler_params=pltpu.CompilerParams(vmem_limit_bytes=24 * 2**20),
         cost_estimate=pl.CostEstimate(
             flops=2 * part * width * width,
             transcendentals=part * width,
@@ -356,7 +360,7 @@
             in_specs=[fixed(width, rows), pl.BlockSpec((1, 1, rows, cols), a_block)],
             out_specs=[fixed(width, cols)] * count,
         ),
-        compiler_params=pltpu.CompilerParams(vmem_limit_bytes=36 * 2**20),
+        compiler_params=pltpu.CompilerParams(vmem_limit_bytes=24 * 2**20),
         cost_estimate=pl.CostEstimate(
             flops=2 * count * rows * width * cols,
             transcendentals=0,
@@ -377,7 +381,7 @@
     return pl.pallas_call(
         diagonals_kernel,
         out_shape=[jax.ShapeDtypeStruct(odd_y.shape, BF16)] * 2,
-        compiler_params=pltpu.CompilerParams(vmem_limit_bytes=36 * 2**20),
+        compiler_params=pltpu.CompilerParams(vmem_limit_bytes=24 * 2**20),
         cost_estimate=pl.CostEstimate(
             flops=odd_y.size, transcendentals=0, bytes_accessed=10 * odd_y.size
         ),
@@ -418,7 +422,7 @@
             in_specs=[whole(value) for value in [*parts, *halves, *terms]],
             out_specs=[whole(value) for value in outs],
         ),
-        compiler_params=pltpu.CompilerParams(vmem_limit_bytes=36 * 2**20),
+        compiler_params=pltpu.CompilerParams(vmem_limit_bytes=24 * 2**20),
         cost_estimate=pl.CostEstimate(
             flops=len(parts) * width * cols,
             transcendentals=0,

time: 184 us -> 183 us (level)
  starting transfers between devices: 45.1 us -> 51.8 us
  waiting for transfers between devices: 51.8 us -> 47.1 us
  Pallas kernels: 78.6 us -> 74.1 us
    ppermute x45, starting transfers between devices: 45.1 us -> 51.8 us  [flip(): return lax.ppermute(value, BOTH, pairs)]
    ppermute x45, waiting for transfers between devices: 51.8 us -> 47.1 us  [flip(): return lax.ppermute(value, BOTH, pairs)]
    pallas_call x2, Pallas kernels: 13.5 us -> 10.7 us  [make_other(): pl.pallas_call(functools.partial(other_kernel, first), out_shape=pltpu.HB...]
  transfers between devices with their start and end apart: 45 -> 45, of which waited for: 18 -> 20; matrix products, arithmetic and copies ran while one was open for 3% -> 3% of each run, Pallas kernels for 36% -> 34%
where the time goes in v13:
time: 183 us; the launch traced here: 181 us
  Pallas kernels  74.1 us (40%)
  starting transfers between devices  51.8 us (28%)
  waiting for transfers between devices  47.1 us (26%)
  other arithmetic  4.16 us (2%)
  local copies, waits for them, and re-layouts  3.13 us (2%)
    ppermute x45, starting transfers between devices, flip(): return lax.ppermute(value, BOTH, pairs)  51.8 us
    ppermute x45, waiting for transfers between devices, flip(): return lax.ppermute(value, BOTH, pairs)  47.1 us
    pallas_call x4, Pallas kernels, backward_part(): pl.pallas_call(backward_kernel, out_shape=[jax.ShapeDtypeStruct((width, c...  21.4 us
    pallas_call x3, Pallas kernels, forward_part(): pl.pallas_call(functools.partial(forward_kernel, offset, n_pieces, n_othe...  18.2 us
    pallas_call x2, Pallas kernels, make_dense(): pl.pallas_call(functools.partial(dense_kernel, first), out_shape=pltpu.HB...  13.2 us
    pallas_call x2, Pallas kernels, make_other(): pl.pallas_call(functools.partial(other_kernel, first), out_shape=pltpu.HB...  10.7 us
    pallas_call x1, Pallas kernels, middle(): pl.pallas_call(functools.partial(middle_kernel, blocks), out_shape=[jax.S...  6.49 us
  transfers between devices with their start and end apart: 45, of which 20 were waited for; matrix products, arithmetic and copies ran while one was open for 3% of the time, Pallas kernels for 34%

profile of v13, /device:TPU:0, one launch (start us, length us, event | category | flops | bytes accessed | tf_op | source)
XLA Modules:
  0.0 181.3 jit_solution(14364097156414689411)
XLA Ops:
  1.9 3.1 %collective-permute-start.2 = (bf16[512,512]{1,0:T(8,128)(2,1)S(1)}, bf16[512,512]{1,0:T(8,128)(2,1)S(1)}, u32[]{:S(2)}, u32[]{:S(2)}) collective-permute-start(bf16[512,512]{1,0:T(8,128)(2,1)S(1)} %constant_dynamic-slice_fusion.refs_2_), channel_id=1, source_target_pairs={{0,8},{1,9},{2,10},{3,11},{4,12},{5,13},{6,14},{7,15},{8,0},{9,1},... | collective-permute-start | bytes 1572872 | tf_op jit(solution)/shard_map/features_z/ppermute | solution.py:450
  5.0 1.5 collective-permute-start.3
  6.5 1.5 collective-permute-start.4
  10.3 6.6 %dense_blocks.2.refs_0_ = bf16[2,8,1024,512]{3,2,1,0:T(8,128)(2,1)} custom-call(s32[44]{0:T(128)S(1)} %pad_add_fusion.1.where_ref, s32[8,25]{1,0:T(8,128)S(1)} %pad_add_fusion.packed_ref, bf16[8,24,128,128]{3,2,1,0:T(8,128)(2,1)} %bitcast.17), custom_call_target="tpu_custom_call" | custom-call | bytes 393216 | tf_op jit(solution)/shard_map/dense_blocks/pallas_call | solution.py:49
  16.9 1.7 collective-permute-start.5
  18.6 1.5 collective-permute-start.6
  20.1 2.6 %collective-permute-start.7 = (bf16[512,512]{1,0:T(8,128)(2,1)S(1)}, bf16[512,512]{1,0:T(8,128)(2,1)}, u32[]{:S(2)}, u32[]{:S(2)}) collective-permute-start(bf16[512,512]{1,0:T(8,128)(2,1)S(1)} %constant_dynamic-slice_fusion.refs_2_), channel_id=1, source_target_pairs={{0,16},{1,17},{2,18},{3,19},{4,20},{5,21},{6,22},{7,23},{8,24},{9,... | collective-permute-start | bytes 1572872 | tf_op jit(solution)/shard_map/features_z/ppermute | solution.py:450
  22.7 8.5 %collective-permute-done.5.refs_6_ = bf16[512,512]{1,0:T(8,128)(2,1)S(1)} collective-permute-done((bf16[512,512]{1,0:T(8,128)(2,1)S(1)}, bf16[512,512]{1,0:T(8,128)(2,1)S(1)}, u32[]{:S(2)}, u32[]{:S(2)}) %collective-permute-start.5) | collective-permute-done | bytes 524320 | tf_op jit(solution)/shard_map/features_xy/ppermute | solution.py:450
  31.4 1.2 collective-permute-start.8
  32.6 0.9 collective-permute-start.9
  33.5 6.6 %dense_blocks.3.dense_ref.a_ref = bf16[2,8,1024,512]{3,2,1,0:T(8,128)(2,1)} custom-call(s32[44]{0:T(128)S(1)} %pad_add_fusion.1.where_ref, s32[8,25]{1,0:T(8,128)S(1)} %pad_add_fusion.packed_ref, bf16[8,24,128,128]{3,2,1,0:T(8,128)(2,1)} %bitcast.18, bf16[2,8,1024,512]{3,2,1,0:T(8,128)(2,1)} %dense_blocks.2.refs_0_), custom_call_target="tpu_custom_call", output_to_operand_aliasing={{}: (3, {})} | custom-call | bytes 393216 | tf_op jit(solution)/shard_map/dense_blocks/pallas_call | solution.py:49
  40.2 5.4 %other_blocks.2.refs_0_ = bf16[4,1024,512]{2,1,0:T(8,128)(2,1)} custom-call(s32[44]{0:T(128)S(1)} %pad_add_fusion.1.where_ref, s32[8,25]{1,0:T(8,128)S(1)} %collective-permute-done.1.packed_ref, bf16[8,24,128,128]{3,2,1,0:T(8,128)(2,1)} %collective-permute-done.tiles_ref), custom_call_target="tpu_custom_call" | custom-call | bytes 393216 | tf_op jit(solution)/shard_map/other_blocks/pallas_call | solution.py:93
  45.6 0.8 copy-done.3
  46.4 0.8 copy-done.5
  48.0 1.2 collective-permute-start.11
  49.2 1.2 collective-permute-start.12
  50.4 1.3 broadcast_select_fusion.1
  51.8 5.2 %other_blocks.3.refs_1_ = bf16[4,1024,512]{2,1,0:T(8,128)(2,1)} custom-call(s32[44]{0:T(128)S(1)} %pad_add_fusion.1.where_ref, s32[8,25]{1,0:T(8,128)S(1)} %collective-permute-done.1.packed_ref, bf16[8,24,128,128]{3,2,1,0:T(8,128)(2,1)} %collective-permute-done.tiles_ref), custom_call_target="tpu_custom_call" | custom-call | bytes 393216 | tf_op jit(solution)/shard_map/other_blocks/pallas_call | solution.py:93
  57.1 4.6 %collective-permute-done.10.refs_11_ = bf16[512,512]{1,0:T(8,128)(2,1)} collective-permute-done((bf16[512,512]{1,0:T(8,128)(2,1)}, bf16[512,512]{1,0:T(8,128)(2,1)}, u32[]{:S(2)}, u32[]{:S(2)}) %collective-permute-start.10) | collective-permute-done | bytes 524320 | tf_op jit(solution)/shard_map/features_xy/ppermute | solution.py:450
  61.7 0.9 collective-permute-done.11.refs_2_
  62.6 0.9 collective-permute-done.12.refs_3_
  63.4 1.2 collective-permute-start.14
  65.2 1.2 collective-permute-start.16
  66.4 9.6 %forward.3.refs_6_ = f32[1024,512]{1,0:T(8,128)S(1)} custom-call(s32[44]{0:T(128)S(1)} %pad_add_fusion.1.where_ref, bf16[2,8,1024,512]{3,2,1,0:T(8,128)(2,1)} %dense_blocks.3.dense_ref.a_ref, bf16[4,1024,512]{2,1,0:T(8,128)(2,1)} %other_blocks.2.refs_0_, bf16[4,1024,512]{2,1,0:T(8,128)(2,1)} %other_blocks.3.refs_1_, ...), custom_call_target="tpu_custom_call" | custom-call | flops 5368709120 | bytes 14680064 | tf_op jit(solution)/shard_map/forward/pallas_call | solution.py:196
  77.8 1.5 collective-permute-start.17
  79.3 1.1 collective-permute-start.18
  80.4 5.2 %forward.4.refs_5_ = f32[1024,512]{1,0:T(8,128)S(1)} custom-call(s32[44]{0:T(128)S(1)} %pad_add_fusion.1.where_ref, bf16[2,8,1024,512]{3,2,1,0:T(8,128)(2,1)} %dense_blocks.3.dense_ref.a_ref, bf16[4,1024,512]{2,1,0:T(8,128)(2,1)} %other_blocks.2.refs_0_, bf16[4,1024,512]{2,1,0:T(8,128)(2,1)} %other_blocks.3.refs_1_, ...), custom_call_target="tpu_custom_call" | custom-call | flops 2147483648 | bytes 8388608 | tf_op jit(solution)/shard_map/forward/pallas_call | solution.py:196
  85.7 3.5 %forward.5.mine_ref = bf16[1024,512]{1,0:T(8,128)(2,1)S(1)} custom-call(s32[44]{0:T(128)S(1)} %pad_add_fusion.1.where_ref, bf16[2,8,1024,512]{3,2,1,0:T(8,128)(2,1)} %dense_blocks.3.dense_ref.a_ref, bf16[4,1024,512]{2,1,0:T(8,128)(2,1)} %other_blocks.2.refs_0_, bf16[4,1024,512]{2,1,0:T(8,128)(2,1)} %other_blocks.3.refs_1_, ...), custom_call_target="tpu_custom_call" | custom-call | flops 1073741824 | bytes 6291456 | tf_op jit(solution)/shard_map/forward/pallas_call | solution.py:196
  89.3 2.6 %collective-permute-done.19.other_ref = bf16[1024,512]{1,0:T(8,128)(2,1)S(1)} collective-permute-done((bf16[1024,512]{1,0:T(8,128)(2,1)S(1)}, bf16[1024,512]{1,0:T(8,128)(2,1)S(1)}, u32[]{:S(2)}, u32[]{:S(2)}) %collective-permute-start.19) | collective-permute-done | bytes 1048608 | tf_op jit(solution)/shard_map/partial_sums/ppermute | solution.py:450
  91.9 6.5 %middle.1 = (bf16[512,1024]{1,0:T(8,128)(2,1)S(1)}, bf16[256,512]{1,0:T(8,128)(2,1)S(1)}, bf16[256,512]{1,0:T(8,128)(2,1)S(1)}, bf16[4,64,512]{2,1,0:T(8,128)(2,1)S(1)}) custom-call(s32[44]{0:T(128)S(1)} %pad_add_fusion.1.where_ref, bf16[1024,512]{1,0:T(8,128)(2,1)S(1)} %forward.5.mine_ref, bf16[1024,512]{1,0:T(8,128)(2,1)S(1)} %collective-permute-done.19.other_ref, ...), custom_call_target="tpu_custom_call" | custom-call | flops 2684354560 | bytes 6291456 | tf_op jit(solution)/shard_map/middle/pallas_call | solution.py:281
  98.4 3.2 %collective-permute-start.22 = (bf16[64,512]{1,0:T(8,128)(2,1)S(1)}, bf16[64,512]{1,0:T(8,128)(2,1)S(1)}, u32[]{:S(2)}, u32[]{:S(2)}) collective-permute-start(bf16[64,512]{1,0:T(8,128)(2,1)S(1)} %get-tuple-element.304), channel_id=1, source_target_pairs={{0,24},{1,25},{2,26},{3,27},{4,28},{5,29},{6,30},{7,31},{8,16},{9,... | collective-permute-start | bytes 196616 | tf_op jit(solution)/shard_map/weight_grad/ppermute | solution.py:450
  101.6 1.3 collective-permute-start.20
  102.9 0.9 collective-permute-start.23
  103.8 1.2 collective-permute-start.24
  104.9 4.6 %backward.4 = (bf16[512,512]{1,0:T(8,128)(2,1)S(1)}, bf16[512,512]{1,0:T(8,128)(2,1)S(1)}, bf16[512,512]{1,0:T(8,128)(2,1)S(1)}) custom-call(s32[44]{0:T(128)S(1)} %pad_add_fusion.1.where_ref, bf16[512,1024]{1,0:T(8,128)(2,1)S(1)} %get-tuple-element.253.grad_ref, bf16[2,8,1024,512]{3,2,1,0:T(8,128)(2,1)} %dense_blocks.3.dense_ref.a_ref), custom_call_target="tpu_custom_call" | custom-call | flops 1610612736 | bytes 5767168 | tf_op jit(solution)/shard_map/backward/pallas_call | solution.py:354
  109.6 1.1 collective-permute-start.26
  111.4 1.0 collective-permute-start.27
  112.4 1.5 collective-permute-start.28
  113.8 5.5 %backward.5 = (bf16[512,512]{1,0:T(8,128)(2,1)S(1)}, bf16[512,512]{1,0:T(8,128)(2,1)S(1)}, bf16[512,512]{1,0:T(8,128)(2,1)S(1)}, bf16[512,512]{1,0:T(8,128)(2,1)S(1)}) custom-call(s32[44]{0:T(128)S(1)} %pad_add_fusion.1.where_ref, bf16[512,1024]{1,0:T(8,128)(2,1)S(1)} %get-tuple-element.253.grad_ref, bf16[2,8,1024,512]{3,2,1,0:T(8,128)(2,1)} %dense_blocks.3.dense_ref.a_ref), custom_call_target="tpu_custom_call" | custom-call | flops 2147483648 | bytes 7340032 | tf_op jit(solution)/shard_map/backward/pallas_call | solution.py:354
  119.9 3.8 %collective-permute-done.25 = bf16[64,512]{1,0:T(8,128)(2,1)S(1)} collective-permute-done((bf16[64,512]{1,0:T(8,128)(2,1)S(1)}, bf16[64,512]{1,0:T(8,128)(2,1)S(1)}, u32[]{:S(2)}, u32[]{:S(2)}) %collective-permute-start.25) | collective-permute-done | bytes 65568 | tf_op jit(solution)/shard_map/weight_grad/ppermute | solution.py:450
  124.1 1.1 collective-permute-start.30
  125.4 1.0 collective-permute-start.31
  126.6 1.6 collective-permute-start.32
  128.1 6.7 %backward.6 = (bf16[512,512]{1,0:T(8,128)(2,1)S(1)}, bf16[512,512]{1,0:T(8,128)(2,1)S(1)}, bf16[512,512]{1,0:T(8,128)(2,1)S(1)}, bf16[512,512]{1,0:T(8,128)(2,1)S(1)}, bf16[512,512]{1,0:T(8,128)(2,1)S(1)}) custom-call(s32[44]{0:T(128)S(1)} %pad_add_fusion.1.where_ref, bf16[512,1024]{1,0:T(8,128)(2,1)S(1)} %get-tuple-element.253.grad_ref, ...), custom_call_target="tpu_custom_call" | custom-call | flops 2684354560 | bytes 8912896 | tf_op jit(solution)/shard_map/backward/pallas_call | solution.py:354
  134.8 1.2 collective-permute-start.29
  136.0 0.9 collective-permute-start.34
  136.9 3.3 %collective-permute-done.29 = bf16[64,512]{1,0:T(8,128)(2,1)S(1)} collective-permute-done((bf16[64,512]{1,0:T(8,128)(2,1)S(1)}, bf16[64,512]{1,0:T(8,128)(2,1)S(1)}, u32[]{:S(2)}, u32[]{:S(2)}) %collective-permute-start.29) | collective-permute-done | bytes 65568 | tf_op jit(solution)/shard_map/weight_grad/ppermute | solution.py:450
  140.2 1.2 collective-permute-start.35
  141.7 2.4 %collective-permute-start.36 = (bf16[256,512]{1,0:T(8,128)(2,1)S(1)}, bf16[256,512]{1,0:T(8,128)(2,1)S(1)}, u32[]{:S(2)}, u32[]{:S(2)}) collective-permute-start(bf16[256,512]{1,0:T(8,128)(2,1)S(1)} %get-tuple-element.300), channel_id=1, source_target_pairs={{0,16},{1,17},{2,18},{3,19},{4,20},{5,21},{6,22},{7,23},{8,24},{9,... | collective-permute-start | bytes 786440 | tf_op jit(solution)/shard_map/grads_z/ppermute | solution.py:450
  144.1 4.6 %backward.7 = (bf16[512,512]{1,0:T(8,128)(2,1)S(1)}, bf16[512,512]{1,0:T(8,128)(2,1)S(1)}, bf16[512,512]{1,0:T(8,128)(2,1)S(1)}) custom-call(s32[44]{0:T(128)S(1)} %pad_add_fusion.1.where_ref, bf16[512,1024]{1,0:T(8,128)(2,1)S(1)} %get-tuple-element.253.grad_ref, bf16[2,8,1024,512]{3,2,1,0:T(8,128)(2,1)} %dense_blocks.3.dense_ref.a_ref), custom_call_target="tpu_custom_call" | custom-call | flops 1610612736 | bytes 5767168 | tf_op jit(solution)/shard_map/backward/pallas_call | solution.py:354
  149.4 1.2 collective-permute-start.40
  150.6 3.4 %collective-permute-done.33 = bf16[1,64,512]{2,1,0:T(8,128)(2,1)S(1)} collective-permute-done((bf16[1,64,512]{2,1,0:T(8,128)(2,1)S(1)}, bf16[1,64,512]{2,1,0:T(8,128)(2,1)S(1)}, u32[]{:S(2)}, u32[]{:S(2)}) %collective-permute-start.33) | collective-permute-done | bytes 65568 | tf_op jit(solution)/shard_map/weight_grad/ppermute | solution.py:450
  154.2 1.4 collective-permute-start.39
  155.6 2.3 %collective-permute-start.37 = (bf16[2,64,512]{2,1,0:T(8,128)(2,1)S(1)}, bf16[2,64,512]{2,1,0:T(8,128)(2,1)S(1)}, u32[]{:S(2)}, u32[]{:S(2)}) collective-permute-start(bf16[2,64,512]{2,1,0:T(8,128)(2,1)S(1)} %pad_maximum_fusion.2), channel_id=1, source_target_pairs={{0,8},{1,9},{2,10},{3,11},{4,12},{5,13},{6,14},{7,15},{8,0},{9,1},... | collective-permute-start | bytes 393224 | tf_op jit(solution)/shard_map/weight_grad/ppermute | solution.py:450
  157.9 0.8 collective-permute-start.38
  158.7 1.4 collective-permute-start.41
  160.2 2.1 %collective-permute-done.37 = bf16[2,64,512]{2,1,0:T(8,128)(2,1)S(1)} collective-permute-done((bf16[2,64,512]{2,1,0:T(8,128)(2,1)S(1)}, bf16[2,64,512]{2,1,0:T(8,128)(2,1)S(1)}, u32[]{:S(2)}, u32[]{:S(2)}) %collective-permute-start.37) | collective-permute-done | bytes 131104 | tf_op jit(solution)/shard_map/weight_grad/ppermute | solution.py:450
  162.3 5.4 %collective-permute-done.38.refs_5_ = bf16[256,512]{1,0:T(8,128)(2,1)S(1)} collective-permute-done((bf16[256,512]{1,0:T(8,128)(2,1)S(1)}, bf16[256,512]{1,0:T(8,128)(2,1)S(1)}, u32[]{:S(2)}, u32[]{:S(2)}) %collective-permute-start.38) | collective-permute-done | bytes 262176 | tf_op jit(solution)/shard_map/grads_z/ppermute | solution.py:450
  167.7 1.4 collective-permute-done.39
  169.3 0.8 collective-permute-start.43
  170.2 1.8 %activated.1 = bf16[512,512]{1,0:T(8,128)(2,1)} custom-call(s32[44]{0:T(128)S(1)} %pad_add_fusion.1.where_ref, bf16[1024,512]{1,0:T(8,128)(2,1)S(1)} %forward.5.mine_ref, bf16[1024,512]{1,0:T(8,128)(2,1)S(1)} %collective-permute-done.19.other_ref, bf16[512,512]{1,0:T(8,128)(2,1)S(1)} %copy-done.2, bf16[1024,512]{1,0:T(8,128)(2,1)S(1)} %pad_maximum_fusion.cot_ref), custom_call_target="tpu_custom_call" | custom-call | flops 268435456 | bytes 2097152 | tf_op jit(solution)/shard_map/activated/pallas_call | solution.py:318
  172.0 5.6 %collective-permute-done.41.refs_1_ = bf16[512,512]{1,0:T(8,128)(2,1)S(1)} collective-permute-done((bf16[512,512]{1,0:T(8,128)(2,1)S(1)}, bf16[512,512]{1,0:T(8,128)(2,1)S(1)}, u32[]{:S(2)}, u32[]{:S(2)}) %collective-permute-start.41) | collective-permute-done | bytes 524320 | tf_op jit(solution)/shard_map/grads_xy/ppermute | solution.py:450
  177.6 1.6 collective-permute-done.43.refs_3_
  179.2 2.1 %grads_out.1 = (bf16[1,512,512]{2,1,0:T(8,128)(2,1)}, f32[512,512]{1,0:T(8,128)}) custom-call(s32[44]{0:T(128)S(1)} %pad_add_fusion.1.where_ref, bf16[512,512]{1,0:T(8,128)(2,1)S(1)} %get-tuple-element.289.refs_0_, bf16[512,512]{1,0:T(8,128)(2,1)S(1)} %collective-permute-done.41.refs_1_, bf16[512,512]{1,0:T(8,128)(2,1)S(1)} %collective-permute-done.42.refs_2_, ...), custom_call_target="tpu_custom_call" | custom-call | flops 1048576 | bytes 2621440 | tf_op jit(solution)/shard_map/grads_out/pallas_call | solution.py:416
  (78 shorter events, 10.6 us)
Async XLA Ops:
  0.6 1.2 copy-start
  0.6 16.3 %collective-permute-start = (bf16[8,24,128,128]{3,2,1,0:T(8,128)(2,1)}, bf16[8,24,128,128]{3,2,1,0:T(8,128)(2,1)}, u32[]{:S(2)}, u32[]{:S(2)}) collective-permute-start(bf16[8,24,128,128]{3,2,1,0:T(8,128)(2,1)} %bitcast.16), channel_id=1, source_target_pairs={{0,1},{1,0},{2,3},{3,2},{4,5},{5,4},{6,7},{7,6},{8,9},{9,8},{10,11... | collective-permute-start | bytes 18874376 | tf_op jit(solution)/shard_map/tiles_exchange/ppermute | solution.py:450
  1.9 15.0 %collective-permute-start.2 = (bf16[512,512]{1,0:T(8,128)(2,1)S(1)}, bf16[512,512]{1,0:T(8,128)(2,1)S(1)}, u32[]{:S(2)}, u32[]{:S(2)}) collective-permute-start(bf16[512,512]{1,0:T(8,128)(2,1)S(1)} %constant_dynamic-slice_fusion.refs_2_), channel_id=1, source_target_pairs={{0,8},{1,9},{2,10},{3,11},{4,12},{5,13},{6,14},{7,15},{8,0},{9,1},... | collective-permute-start | bytes 1572872 | tf_op jit(solution)/shard_map/features_z/ppermute | solution.py:450
  5.0 17.7 %collective-permute-start.3 = (bf16[512,512]{1,0:T(8,128)(2,1)S(1)}, bf16[512,512]{1,0:T(8,128)(2,1)S(1)}, u32[]{:S(2)}, u32[]{:S(2)}) collective-permute-start(bf16[512,512]{1,0:T(8,128)(2,1)S(1)} %constant_dynamic-slice_fusion.refs_2_), channel_id=1, source_target_pairs={{0,2},{1,3},{2,0},{3,1},{4,6},{5,7},{6,4},{7,5},{8,10},{9,11},{10,... | collective-permute-start | bytes 1572872 | tf_op jit(solution)/shard_map/features_xy/ppermute | solution.py:450
  6.5 16.2 %collective-permute-start.4 = (bf16[512,512]{1,0:T(8,128)(2,1)S(1)}, bf16[512,512]{1,0:T(8,128)(2,1)S(1)}, u32[]{:S(2)}, u32[]{:S(2)}) collective-permute-start(bf16[512,512]{1,0:T(8,128)(2,1)S(1)} %constant_dynamic-slice_fusion.refs_2_), channel_id=1, source_target_pairs={{0,4},{1,5},{2,6},{3,7},{4,0},{5,1},{6,2},{7,3},{8,12},{9,13},{10,... | collective-permute-start | bytes 1572872 | tf_op jit(solution)/shard_map/features_xy/ppermute | solution.py:450
  9.5 7.4 %collective-permute-start.1 = (s32[8,25]{1,0:T(8,128)S(1)}, s32[8,25]{1,0:T(8,128)S(1)}, u32[]{:S(2)}, u32[]{:S(2)}) collective-permute-start(s32[8,25]{1,0:T(8,128)S(1)} %pad_add_fusion.packed_ref), channel_id=1, source_target_pairs={{0,1},{1,0},{2,3},{3,2},{4,5},{5,4},{6,7},{7,6},{8,9},{9,8},{10,11... | collective-permute-start | bytes 2408 | tf_op jit(solution)/shard_map/tiles_exchange/ppermute | solution.py:450
  16.9 14.3 %collective-permute-start.5 = (bf16[512,512]{1,0:T(8,128)(2,1)S(1)}, bf16[512,512]{1,0:T(8,128)(2,1)S(1)}, u32[]{:S(2)}, u32[]{:S(2)}) collective-permute-start(bf16[512,512]{1,0:T(8,128)(2,1)S(1)} %collective-permute-done.2.refs_5_), channel_id=1, source_target_pairs={{0,2},{1,3},{2,0},{3,1},{4,6},{5,7},{6,4},{7,5},{8,10},{9,11},{10,... | collective-permute-start | bytes 1572872 | tf_op jit(solution)/shard_map/features_xy/ppermute | solution.py:450
  18.6 12.8 %collective-permute-start.6 = (bf16[512,512]{1,0:T(8,128)(2,1)S(1)}, bf16[512,512]{1,0:T(8,128)(2,1)S(1)}, u32[]{:S(2)}, u32[]{:S(2)}) collective-permute-start(bf16[512,512]{1,0:T(8,128)(2,1)S(1)} %collective-permute-done.2.refs_5_), channel_id=1, source_target_pairs={{0,4},{1,5},{2,6},{3,7},{4,0},{5,1},{6,2},{7,3},{8,12},{9,13},{10,... | collective-permute-start | bytes 1572872 | tf_op jit(solution)/shard_map/features_xy/ppermute | solution.py:450
  20.1 25.5 %collective-permute-start.7 = (bf16[512,512]{1,0:T(8,128)(2,1)S(1)}, bf16[512,512]{1,0:T(8,128)(2,1)}, u32[]{:S(2)}, u32[]{:S(2)}) collective-permute-start(bf16[512,512]{1,0:T(8,128)(2,1)S(1)} %constant_dynamic-slice_fusion.refs_2_), channel_id=1, source_target_pairs={{0,16},{1,17},{2,18},{3,19},{4,20},{5,21},{6,22},{7,23},{8,24},{9,... | collective-permute-start | bytes 1572872 | tf_op jit(solution)/shard_map/features_z/ppermute | solution.py:450
  31.4 14.3 %collective-permute-start.8 = (bf16[512,512]{1,0:T(8,128)(2,1)S(1)}, bf16[512,512]{1,0:T(8,128)(2,1)S(1)}, u32[]{:S(2)}, u32[]{:S(2)}) collective-permute-start(bf16[512,512]{1,0:T(8,128)(2,1)S(1)} %collective-permute-done.3.refs_3_), channel_id=1, source_target_pairs={{0,4},{1,5},{2,6},{3,7},{4,0},{5,1},{6,2},{7,3},{8,12},{9,13},{10,... | collective-permute-start | bytes 1572872 | tf_op jit(solution)/shard_map/features_xy/ppermute | solution.py:450
  32.6 13.8 %collective-permute-start.9 = (bf16[512,512]{1,0:T(8,128)(2,1)S(1)}, bf16[512,512]{1,0:T(8,128)(2,1)S(1)}, u32[]{:S(2)}, u32[]{:S(2)}) collective-permute-start(bf16[512,512]{1,0:T(8,128)(2,1)S(1)} %collective-permute-done.6.refs_7_), channel_id=1, source_target_pairs={{0,2},{1,3},{2,0},{3,1},{4,6},{5,7},{6,4},{7,5},{8,10},{9,11},{10,... | collective-permute-start | bytes 1572872 | tf_op jit(solution)/shard_map/features_xy/ppermute | solution.py:450
  33.5 16.9 %collective-permute-start.13 = (bf16[512,512]{1,0:T(8,128)(2,1)}, bf16[512,512]{1,0:T(8,128)(2,1)}, u32[]{:S(2)}, u32[]{:S(2)}) collective-permute-start(bf16[512,512]{1,0:T(8,128)(2,1)} %param.14), channel_id=1, source_target_pairs={{0,1},{1,0},{2,3},{3,2},{4,5},{5,4},{6,7},{7,6},{8,9},{9,8},{10,11... | collective-permute-start | bytes 1572872 | tf_op jit(solution)/shard_map/cotangents/ppermute | solution.py:450
  45.6 0.8 copy-start.3
  46.4 0.8 copy-start.5
  47.2 14.4 %collective-permute-start.10 = (bf16[512,512]{1,0:T(8,128)(2,1)}, bf16[512,512]{1,0:T(8,128)(2,1)}, u32[]{:S(2)}, u32[]{:S(2)}) collective-permute-start(bf16[512,512]{1,0:T(8,128)(2,1)} %collective-permute-done.7.refs_10_), channel_id=1, source_target_pairs={{0,2},{1,3},{2,0},{3,1},{4,6},{5,7},{6,4},{7,5},{8,10},{9,11},{10,... | collective-permute-start | bytes 1572872 | tf_op jit(solution)/shard_map/features_xy/ppermute | solution.py:450
  48.0 14.6 %collective-permute-start.11 = (bf16[512,512]{1,0:T(8,128)(2,1)}, bf16[512,512]{1,0:T(8,128)(2,1)}, u32[]{:S(2)}, u32[]{:S(2)}) collective-permute-start(bf16[512,512]{1,0:T(8,128)(2,1)} %collective-permute-done.7.refs_10_), channel_id=1, source_target_pairs={{0,4},{1,5},{2,6},{3,7},{4,0},{5,1},{6,2},{7,3},{8,12},{9,13},{10,... | collective-permute-start | bytes 1572872 | tf_op jit(solution)/shard_map/features_xy/ppermute | solution.py:450
  49.2 14.2 %collective-permute-start.12 = (bf16[512,512]{1,0:T(8,128)(2,1)}, bf16[512,512]{1,0:T(8,128)(2,1)}, u32[]{:S(2)}, u32[]{:S(2)}) collective-permute-start(bf16[512,512]{1,0:T(8,128)(2,1)} %collective-permute-done.7.refs_10_), channel_id=1, source_target_pairs={{0,8},{1,9},{2,10},{3,11},{4,12},{5,13},{6,14},{7,15},{8,0},{9,1},... | collective-permute-start | bytes 1572872 | tf_op jit(solution)/shard_map/features_z/ppermute | solution.py:450
  51.8 14.6 %copy-start.4 = (bf16[512,512]{1,0:T(8,128)(2,1)S(1)}, bf16[512,512]{1,0:T(8,128)(2,1)}, u32[]{:S(2)}) copy-start(bf16[512,512]{1,0:T(8,128)(2,1)} %copy-done.3) | copy-start | bytes 1572868
  51.8 14.6 %copy-start.6 = (bf16[512,512]{1,0:T(8,128)(2,1)S(1)}, bf16[512,512]{1,0:T(8,128)(2,1)}, u32[]{:S(2)}) copy-start(bf16[512,512]{1,0:T(8,128)(2,1)} %copy-done.5) | copy-start | bytes 1572868
  63.4 13.3 %collective-permute-start.14 = (bf16[512,512]{1,0:T(8,128)(2,1)}, bf16[512,512]{1,0:T(8,128)(2,1)S(1)}, u32[]{:S(2)}, u32[]{:S(2)}) collective-permute-start(bf16[512,512]{1,0:T(8,128)(2,1)} %collective-permute-done.11.refs_2_), channel_id=1, source_target_pairs={{0,2},{1,3},{2,0},{3,1},{4,6},{5,7},{6,4},{7,5},{8,10},{9,11},{10,... | collective-permute-start | bytes 1572872 | tf_op jit(solution)/shard_map/features_xy/ppermute | solution.py:450
  64.6 12.8 %collective-permute-start.15 = (bf16[512,512]{1,0:T(8,128)(2,1)}, bf16[512,512]{1,0:T(8,128)(2,1)S(1)}, u32[]{:S(2)}, u32[]{:S(2)}) collective-permute-start(bf16[512,512]{1,0:T(8,128)(2,1)} %collective-permute-done.12.refs_3_), channel_id=1, source_target_pairs={{0,4},{1,5},{2,6},{3,7},{4,0},{5,1},{6,2},{7,3},{8,12},{9,13},{10,... | collective-permute-start | bytes 1572872 | tf_op jit(solution)/shard_map/features_xy/ppermute | solution.py:450
  65.2 12.6 %collective-permute-start.16 = (bf16[512,512]{1,0:T(8,128)(2,1)}, bf16[512,512]{1,0:T(8,128)(2,1)S(1)}, u32[]{:S(2)}, u32[]{:S(2)}) collective-permute-start(bf16[512,512]{1,0:T(8,128)(2,1)} %collective-permute-done.10.refs_11_), channel_id=1, source_target_pairs={{0,8},{1,9},{2,10},{3,11},{4,12},{5,13},{6,14},{7,15},{8,0},{9,1},... | collective-permute-start | bytes 1572872 | tf_op jit(solution)/shard_map/features_z/ppermute | solution.py:450
  77.8 7.8 %collective-permute-start.17 = (bf16[256,512]{1,0:T(8,128)(2,1)S(1)}, bf16[256,512]{1,0:T(8,128)(2,1)S(1)}, u32[]{:S(2)}, u32[]{:S(2)}) collective-permute-start(bf16[256,512]{1,0:T(8,128)(2,1)S(1)} %slice.42), channel_id=1, source_target_pairs={{0,2},{1,3},{2,0},{3,1},{4,6},{5,7},{6,4},{7,5},{8,10},{9,11},{10,... | collective-permute-start | bytes 786440 | tf_op jit(solution)/shard_map/features_xy/ppermute | solution.py:450
  79.3 6.4 %collective-permute-start.18 = (bf16[256,512]{1,0:T(8,128)(2,1)S(1)}, bf16[256,512]{1,0:T(8,128)(2,1)S(1)}, u32[]{:S(2)}, u32[]{:S(2)}) collective-permute-start(bf16[256,512]{1,0:T(8,128)(2,1)S(1)} %slice.43), channel_id=1, source_target_pairs={{0,4},{1,5},{2,6},{3,7},{4,0},{5,1},{6,2},{7,3},{8,12},{9,13},{10,... | collective-permute-start | bytes 786440 | tf_op jit(solution)/shard_map/features_xy/ppermute | solution.py:450
  85.5 6.4 %copy-start.2 = (bf16[512,512]{1,0:T(8,128)(2,1)S(1)}, bf16[512,512]{1,0:T(8,128)(2,1)}, u32[]{:S(2)}) copy-start(bf16[512,512]{1,0:T(8,128)(2,1)} %weight_ref.3) | copy-start | bytes 1572868
  89.2 2.7 %collective-permute-start.19 = (bf16[1024,512]{1,0:T(8,128)(2,1)S(1)}, bf16[1024,512]{1,0:T(8,128)(2,1)S(1)}, u32[]{:S(2)}, u32[]{:S(2)}) collective-permute-start(bf16[1024,512]{1,0:T(8,128)(2,1)S(1)} %forward.5.mine_ref), channel_id=1, source_target_pairs={{0,1},{1,0},{2,3},{3,2},{4,5},{5,4},{6,7},{7,6},{8,9},{9,8},{10,11... | collective-permute-start | bytes 3145736 | tf_op jit(solution)/shard_map/partial_sums/ppermute | solution.py:450
  98.4 11.1 %collective-permute-start.22 = (bf16[64,512]{1,0:T(8,128)(2,1)S(1)}, bf16[64,512]{1,0:T(8,128)(2,1)S(1)}, u32[]{:S(2)}, u32[]{:S(2)}) collective-permute-start(bf16[64,512]{1,0:T(8,128)(2,1)S(1)} %get-tuple-element.304), channel_id=1, source_target_pairs={{0,24},{1,25},{2,26},{3,27},{4,28},{5,29},{6,30},{7,31},{8,16},{9,... | collective-permute-start | bytes 196616 | tf_op jit(solution)/shard_map/weight_grad/ppermute | solution.py:450
  101.6 9.0 %collective-permute-start.21 = (bf16[64,512]{1,0:T(8,128)(2,1)S(1)}, bf16[64,512]{1,0:T(8,128)(2,1)S(1)}, u32[]{:S(2)}, u32[]{:S(2)}) collective-permute-start(bf16[64,512]{1,0:T(8,128)(2,1)S(1)} %get-tuple-element.305), channel_id=1, source_target_pairs={{0,16},{1,17},{2,18},{3,19},{4,20},{5,21},{6,22},{7,23},{8,24},{9,... | collective-permute-start | bytes 196616 | tf_op jit(solution)/shard_map/weight_grad/ppermute | solution.py:450
  101.6 9.0 %collective-permute-start.20 = (bf16[64,512]{1,0:T(8,128)(2,1)S(1)}, bf16[64,512]{1,0:T(8,128)(2,1)S(1)}, u32[]{:S(2)}, u32[]{:S(2)}) collective-permute-start(bf16[64,512]{1,0:T(8,128)(2,1)S(1)} %get-tuple-element.303), channel_id=1, source_target_pairs={{0,8},{1,9},{2,10},{3,11},{4,12},{5,13},{6,14},{7,15},{8,0},{9,1},... | collective-permute-start | bytes 196616 | tf_op jit(solution)/shard_map/weight_grad/ppermute | solution.py:450
  102.9 7.8 %collective-permute-start.23 = (bf16[256,512]{1,0:T(8,128)(2,1)S(1)}, bf16[256,512]{1,0:T(8,128)(2,1)S(1)}, u32[]{:S(2)}, u32[]{:S(2)}) collective-permute-start(bf16[256,512]{1,0:T(8,128)(2,1)S(1)} %get-tuple-element.214), channel_id=1, source_target_pairs={{0,2},{1,3},{2,0},{3,1},{4,6},{5,7},{6,4},{7,5},{8,10},{9,11},{10,... | collective-permute-start | bytes 786440 | tf_op jit(solution)/shard_map/grads_xy/ppermute | solution.py:450
  103.8 7.5 %collective-permute-start.24 = (bf16[256,512]{1,0:T(8,128)(2,1)S(1)}, bf16[256,512]{1,0:T(8,128)(2,1)S(1)}, u32[]{:S(2)}, u32[]{:S(2)}) collective-permute-start(bf16[256,512]{1,0:T(8,128)(2,1)S(1)} %get-tuple-element.215), channel_id=1, source_target_pairs={{0,4},{1,5},{2,6},{3,7},{4,0},{5,1},{6,2},{7,3},{8,12},{9,13},{10,... | collective-permute-start | bytes 786440 | tf_op jit(solution)/shard_map/grads_xy/ppermute | solution.py:450
  109.6 14.1 %collective-permute-start.26 = (bf16[512,512]{1,0:T(8,128)(2,1)S(1)}, bf16[512,512]{1,0:T(8,128)(2,1)S(1)}, u32[]{:S(2)}, u32[]{:S(2)}) collective-permute-start(bf16[512,512]{1,0:T(8,128)(2,1)S(1)} %get-tuple-element.226), channel_id=1, source_target_pairs={{0,2},{1,3},{2,0},{3,1},{4,6},{5,7},{6,4},{7,5},{8,10},{9,11},{10,... | collective-permute-start | bytes 1572872 | tf_op jit(solution)/shard_map/grads_xy/ppermute | solution.py:450
  111.4 12.3 %collective-permute-start.27 = (bf16[512,512]{1,0:T(8,128)(2,1)S(1)}, bf16[512,512]{1,0:T(8,128)(2,1)S(1)}, u32[]{:S(2)}, u32[]{:S(2)}) collective-permute-start(bf16[512,512]{1,0:T(8,128)(2,1)S(1)} %get-tuple-element.231), channel_id=1, source_target_pairs={{0,4},{1,5},{2,6},{3,7},{4,0},{5,1},{6,2},{7,3},{8,12},{9,13},{10,... | collective-permute-start | bytes 1572872 | tf_op jit(solution)/shard_map/grads_xy/ppermute | solution.py:450
  112.4 11.6 %collective-permute-start.28 = (bf16[512,512]{1,0:T(8,128)(2,1)S(1)}, bf16[512,512]{1,0:T(8,128)(2,1)S(1)}, u32[]{:S(2)}, u32[]{:S(2)}) collective-permute-start(bf16[512,512]{1,0:T(8,128)(2,1)S(1)} %get-tuple-element.232), channel_id=1, source_target_pairs={{0,8},{1,9},{2,10},{3,11},{4,12},{5,13},{6,14},{7,15},{8,0},{9,1},... | collective-permute-start | bytes 1572872 | tf_op jit(solution)/shard_map/grads_z/ppermute | solution.py:450
  119.3 4.3 %collective-permute-start.25 = (bf16[64,512]{1,0:T(8,128)(2,1)S(1)}, bf16[64,512]{1,0:T(8,128)(2,1)S(1)}, u32[]{:S(2)}, u32[]{:S(2)}) collective-permute-start(bf16[64,512]{1,0:T(8,128)(2,1)S(1)} %fusion.2), channel_id=1, source_target_pairs={{0,2},{1,3},{2,0},{3,1},{4,6},{5,7},{6,4},{7,5},{8,10},{9,11},{10,... | collective-permute-start | bytes 196616 | tf_op jit(solution)/shard_map/weight_grad/ppermute | solution.py:450
  124.1 17.3 %collective-permute-start.30 = (bf16[512,512]{1,0:T(8,128)(2,1)S(1)}, bf16[512,512]{1,0:T(8,128)(2,1)S(1)}, u32[]{:S(2)}, u32[]{:S(2)}) collective-permute-start(bf16[512,512]{1,0:T(8,128)(2,1)S(1)} %add_convert_fusion.5), channel_id=1, source_target_pairs={{0,2},{1,3},{2,0},{3,1},{4,6},{5,7},{6,4},{7,5},{8,10},{9,11},{10,... | collective-permute-start | bytes 1572872 | tf_op jit(solution)/shard_map/grads_xy/ppermute | solution.py:450
  125.4 16.0 %collective-permute-start.31 = (bf16[512,512]{1,0:T(8,128)(2,1)S(1)}, bf16[512,512]{1,0:T(8,128)(2,1)S(1)}, u32[]{:S(2)}, u32[]{:S(2)}) collective-permute-start(bf16[512,512]{1,0:T(8,128)(2,1)S(1)} %add_convert_fusion.4), channel_id=1, source_target_pairs={{0,4},{1,5},{2,6},{3,7},{4,0},{5,1},{6,2},{7,3},{8,12},{9,13},{10,... | collective-permute-start | bytes 1572872 | tf_op jit(solution)/shard_map/grads_xy/ppermute | solution.py:450
  126.6 14.8 %collective-permute-start.32 = (bf16[512,512]{1,0:T(8,128)(2,1)S(1)}, bf16[512,512]{1,0:T(8,128)(2,1)S(1)}, u32[]{:S(2)}, u32[]{:S(2)}) collective-permute-start(bf16[512,512]{1,0:T(8,128)(2,1)S(1)} %add_convert_fusion.3), channel_id=1, source_target_pairs={{0,8},{1,9},{2,10},{3,11},{4,12},{5,13},{6,14},{7,15},{8,0},{9,1},... | collective-permute-start | bytes 1572872 | tf_op jit(solution)/shard_map/grads_z/ppermute | solution.py:450
  134.8 5.4 %collective-permute-start.29 = (bf16[64,512]{1,0:T(8,128)(2,1)S(1)}, bf16[64,512]{1,0:T(8,128)(2,1)S(1)}, u32[]{:S(2)}, u32[]{:S(2)}) collective-permute-start(bf16[64,512]{1,0:T(8,128)(2,1)S(1)} %add_convert_fusion.9), channel_id=1, source_target_pairs={{0,4},{1,5},{2,6},{3,7},{4,0},{5,1},{6,2},{7,3},{8,12},{9,13},{10,... | collective-permute-start | bytes 196616 | tf_op jit(solution)/shard_map/weight_grad/ppermute | solution.py:450
  136.0 18.0 %collective-permute-start.34 = (bf16[512,512]{1,0:T(8,128)(2,1)S(1)}, bf16[512,512]{1,0:T(8,128)(2,1)S(1)}, u32[]{:S(2)}, u32[]{:S(2)}) collective-permute-start(bf16[512,512]{1,0:T(8,128)(2,1)S(1)} %get-tuple-element.260), channel_id=1, source_target_pairs={{0,4},{1,5},{2,6},{3,7},{4,0},{5,1},{6,2},{7,3},{8,12},{9,13},{10,... | collective-permute-start | bytes 1572872 | tf_op jit(solution)/shard_map/grads_xy/ppermute | solution.py:450
  140.2 13.8 %collective-permute-start.35 = (bf16[512,512]{1,0:T(8,128)(2,1)S(1)}, bf16[512,512]{1,0:T(8,128)(2,1)S(1)}, u32[]{:S(2)}, u32[]{:S(2)}) collective-permute-start(bf16[512,512]{1,0:T(8,128)(2,1)S(1)} %get-tuple-element.261), channel_id=1, source_target_pairs={{0,2},{1,3},{2,0},{3,1},{4,6},{5,7},{6,4},{7,5},{8,10},{9,11},{10,... | collective-permute-start | bytes 1572872 | tf_op jit(solution)/shard_map/grads_xy/ppermute | solution.py:450
  141.7 12.3 %collective-permute-start.36 = (bf16[256,512]{1,0:T(8,128)(2,1)S(1)}, bf16[256,512]{1,0:T(8,128)(2,1)S(1)}, u32[]{:S(2)}, u32[]{:S(2)}) collective-permute-start(bf16[256,512]{1,0:T(8,128)(2,1)S(1)} %get-tuple-element.300), channel_id=1, source_target_pairs={{0,16},{1,17},{2,18},{3,19},{4,20},{5,21},{6,22},{7,23},{8,24},{9,... | collective-permute-start | bytes 786440 | tf_op jit(solution)/shard_map/grads_z/ppermute | solution.py:450
  148.8 5.3 %collective-permute-start.33 = (bf16[1,64,512]{2,1,0:T(8,128)(2,1)S(1)}, bf16[1,64,512]{2,1,0:T(8,128)(2,1)S(1)}, u32[]{:S(2)}, u32[]{:S(2)}) collective-permute-start(bf16[1,64,512]{2,1,0:T(8,128)(2,1)S(1)} %bitcast.19), channel_id=1, source_target_pairs={{0,16},{1,17},{2,18},{3,19},{4,20},{5,21},{6,22},{7,23},{8,24},{9,... | collective-permute-start | bytes 196616 | tf_op jit(solution)/shard_map/weight_grad/ppermute | solution.py:450
  149.4 18.3 %collective-permute-start.40 = (bf16[512,512]{1,0:T(8,128)(2,1)S(1)}, bf16[512,512]{1,0:T(8,128)(2,1)S(1)}, u32[]{:S(2)}, u32[]{:S(2)}) collective-permute-start(bf16[512,512]{1,0:T(8,128)(2,1)S(1)} %get-tuple-element.277), channel_id=1, source_target_pairs={{0,4},{1,5},{2,6},{3,7},{4,0},{5,1},{6,2},{7,3},{8,12},{9,13},{10,... | collective-permute-start | bytes 1572872 | tf_op jit(solution)/shard_map/grads_xy/ppermute | solution.py:450
  154.2 14.9 %collective-permute-start.39 = (bf16[512,512]{1,0:T(8,128)(2,1)S(1)}, bf16[512,512]{1,0:T(8,128)(2,1)S(1)}, u32[]{:S(2)}, u32[]{:S(2)}) collective-permute-start(bf16[512,512]{1,0:T(8,128)(2,1)S(1)} %add_convert_fusion.2), channel_id=1, source_target_pairs={{0,2},{1,3},{2,0},{3,1},{4,6},{5,7},{6,4},{7,5},{8,10},{9,11},{10,... | collective-permute-start | bytes 1572872 | tf_op jit(solution)/shard_map/grads_xy/ppermute | solution.py:450
  155.6 6.7 %collective-permute-start.37 = (bf16[2,64,512]{2,1,0:T(8,128)(2,1)S(1)}, bf16[2,64,512]{2,1,0:T(8,128)(2,1)S(1)}, u32[]{:S(2)}, u32[]{:S(2)}) collective-permute-start(bf16[2,64,512]{2,1,0:T(8,128)(2,1)S(1)} %pad_maximum_fusion.2), channel_id=1, source_target_pairs={{0,8},{1,9},{2,10},{3,11},{4,12},{5,13},{6,14},{7,15},{8,0},{9,1},... | collective-permute-start | bytes 393224 | tf_op jit(solution)/shard_map/weight_grad/ppermute | solution.py:450
  157.9 9.8 %collective-permute-start.38 = (bf16[256,512]{1,0:T(8,128)(2,1)S(1)}, bf16[256,512]{1,0:T(8,128)(2,1)S(1)}, u32[]{:S(2)}, u32[]{:S(2)}) collective-permute-start(bf16[256,512]{1,0:T(8,128)(2,1)S(1)} %get-tuple-element.273), channel_id=1, source_target_pairs={{0,16},{1,17},{2,18},{3,19},{4,20},{5,21},{6,22},{7,23},{8,24},{9,... | collective-permute-start | bytes 786440 | tf_op jit(solution)/shard_map/grads_z/ppermute | solution.py:450
  158.7 18.9 %collective-permute-start.41 = (bf16[512,512]{1,0:T(8,128)(2,1)S(1)}, bf16[512,512]{1,0:T(8,128)(2,1)S(1)}, u32[]{:S(2)}, u32[]{:S(2)}) collective-permute-start(bf16[512,512]{1,0:T(8,128)(2,1)S(1)} %get-tuple-element.281), channel_id=1, source_target_pairs={{0,2},{1,3},{2,0},{3,1},{4,6},{5,7},{6,4},{7,5},{8,10},{9,11},{10,... | collective-permute-start | bytes 1572872 | tf_op jit(solution)/shard_map/grads_xy/ppermute | solution.py:450
  162.3 15.3 %collective-permute-start.42 = (bf16[512,512]{1,0:T(8,128)(2,1)S(1)}, bf16[512,512]{1,0:T(8,128)(2,1)S(1)}, u32[]{:S(2)}, u32[]{:S(2)}) collective-permute-start(bf16[512,512]{1,0:T(8,128)(2,1)S(1)} %add_convert_fusion.1), channel_id=1, source_target_pairs={{0,4},{1,5},{2,6},{3,7},{4,0},{5,1},{6,2},{7,3},{8,12},{9,13},{10,... | collective-permute-start | bytes 1572872 | tf_op jit(solution)/shard_map/grads_xy/ppermute | solution.py:450
  169.1 12.2 %copy-start.1 = (bf16[1024,512]{1,0:T(8,128)(2,1)S(1)}, bf16[1024,512]{1,0:T(8,128)(2,1)}, u32[]{:S(2)}) copy-start(bf16[1024,512]{1,0:T(8,128)(2,1)} %param.8) | copy-start | bytes 3145732
  169.3 9.8 %collective-permute-start.43 = (bf16[512,512]{1,0:T(8,128)(2,1)S(1)}, bf16[512,512]{1,0:T(8,128)(2,1)S(1)}, u32[]{:S(2)}, u32[]{:S(2)}) collective-permute-start(bf16[512,512]{1,0:T(8,128)(2,1)S(1)} %add_convert_fusion), channel_id=1, source_target_pairs={{0,8},{1,9},{2,10},{3,11},{4,12},{5,13},{6,14},{7,15},{8,0},{9,1},... | collective-permute-start | bytes 1572872 | tf_op jit(solution)/shard_map/grads_z/ppermute | solution.py:450
  170.2 7.4 %collective-permute-start.44 = (bf16[4,64,512]{2,1,0:T(8,128)(2,1)S(1)}, bf16[4,64,512]{2,1,0:T(8,128)(2,1)S(1)}, u32[]{:S(2)}, u32[]{:S(2)}) collective-permute-start(bf16[4,64,512]{2,1,0:T(8,128)(2,1)S(1)} %pad_maximum_fusion.1.refs_6_), channel_id=1, source_target_pairs={{0,1},{1,0},{2,3},{3,2},{4,5},{5,4},{6,7},{7,6},{8,9},{9,8},{10,11... | collective-permute-start | bytes 786440 | tf_op jit(solution)/shard_map/weight_grad/ppermute | solution.py:450

commit v14 on v13

--- a/solution.py
+++ b/solution.py
@@ -477,11 +477,11 @@
         if pair == 0:
             plan(("first", pair), [odd + X + Y, even + X + Y])
             plan(("odd", pair), [odd + X, odd + Y, odd])
-            plan(("even", pair), [even + X, even + Y, even])
         else:
             plan(("first", pair), [odd + X + Y])
             plan(("mid", pair), [even + X + Y, odd + Y, odd + X])
-            plan(("last", pair), [even + X, even + Y, odd, even])
+            more = [X, Y, 0] if pair == 1 else []
+            plan(("last", pair), [even + X, even + Y, odd, even, *more])
     offsets["joined"] = 2 + len(masks)
     masks += [0, X, Y, Z, Z + X, Z + Y, X + Y, Z + X + Y, 2 * Z, 2 * Z + X]
     where = jnp.concatenate(
@@ -602,30 +602,31 @@
             for name, count in zip(names, counts):
                 live[name], chunks = chunks[:count], chunks[count:]
 
-    steps = ["z", X, Y, *(-(Z << bit) for bit in reversed(range(depth.bit_length() - 1)))]
-    steps.append("cores")
+    back = [-(Z << bit) for bit in reversed(range(depth.bit_length() - 1))]
+    steps = [["z"], [X], [], [Y, back[0]], *([step] for step in back[1:]), ["cores"]]
     z_order = [0]
 
     def weight_step(after=None):
-        if not steps:
-            return
-        step = steps.pop(0)
-        if after:
+        todo = steps.pop(0) if steps else []
+        if after and todo:
             live[after], live["term"] = lax.optimization_barrier((live[after], live["term"]))
-        term = live["term"]
-        with jax.named_scope("weight_grad"):
-            if step == "z":
-                parts = [term[0], *(flip(term[n], Z * n) for n in range(1, depth))]
-                live["term"] = add(*parts).astype(BF16)
-            elif step == "cores":
-                live["terms"] = [term, *(flip(term, 0, n) for n in range(1, n_rep))]
-                del live["term"]
-            elif step > 0:
-                live["term"] = add(term, flip(term, step)).astype(BF16)
-            else:
-                term = term[None] if term.ndim == 2 else term
-                live["term"] = jnp.concatenate([term, flip(term, -step)])
-                z_order.extend([-step // Z ^ other for other in z_order])
+        for step in todo:
+            with jax.named_scope("weight_grad"):
+                one_step(step, live["term"])
+
+    def one_step(step, term):
+        if step == "z":
+            parts = [term[0], *(flip(term[n], Z * n) for n in range(1, depth))]
+            live["term"] = add(*parts).astype(BF16)
+        elif step == "cores":
+            live["terms"] = [term, *(flip(term, 0, n) for n in range(1, n_rep))]
+            del live["term"]
+        elif step > 0:
+            live["term"] = add(term, flip(term, step)).astype(BF16)
+        else:
+            term = term[None] if term.ndim == 2 else term
+            live["term"] = jnp.concatenate([term, flip(term, -step)])
+            z_order.extend([-step // Z ^ other for other in z_order])
 
     half = width // 2
     tops = lambda values: [value[:half] for value in values]
@@ -645,8 +646,9 @@
         if not top:
             with jax.named_scope(GRADS_ALONG):
                 live[name] = [flip(live["passed"][0], mask)]
-        backward_step(pair, "even" if pair == 0 else "mid")
-        weight_step(None if top else "even" if pair == 0 else "mid")
+        if pair > 0:
+            backward_step(pair, "mid")
+        weight_step(None if top or pair == 0 else "mid")
         with jax.named_scope(GRADS_ACROSS):
             if pair == 0:
                 to_x, to_y, own = live.pop("odd")
@@ -674,7 +676,7 @@
                 live["to_odd"] = flip(odd_y, Y)
             with jax.named_scope(GRADS_ALONG):
                 live["to_x"] = flip(odd_x, Z)
-            backward_step(pair, "last")
+            backward_step(pair, "last", *(["even"] if pair == 1 else []))
         if not top:
             with jax.named_scope(GRADS_ALONG):
                 live[name].append(flip(live.pop("passed")[1], mask))

time: 183 us -> 186 us (1.016)
  waiting for transfers between devices: 47.1 us -> 51 us
    ppermute x45, waiting for transfers between devices: 47.1 us -> 51 us  [flip(): return lax.ppermute(value, BOTH, pairs)]
    pallas_call x4 -> x3, Pallas kernels: 21.4 us -> 20.3 us  [backward_part(): pl.pallas_call(backward_kernel, out_shape=[jax.ShapeDtypeStruct((width, c...]
  transfers between devices with their start and end apart: 45 -> 45, of which waited for: 20 -> 20; matrix products, arithmetic and copies ran while one was open for 3% -> 3% of each run, Pallas kernels for 34% -> 33%
where the time goes in v14:
time: 186 us; the launch traced here: 184 us
  Pallas kernels  72.9 us (39%)
  starting transfers between devices  51.8 us (28%)
  waiting for transfers between devices  51 us (27%)
  other arithmetic  4.15 us (2%)
  local copies, waits for them, and re-layouts  3.13 us (2%)
    ppermute x45, starting transfers between devices, flip(): return lax.ppermute(value, BOTH, pairs)  51.8 us
    ppermute x45, waiting for transfers between devices, flip(): return lax.ppermute(value, BOTH, pairs)  51 us
    pallas_call x3, Pallas kernels, backward_part(): pl.pallas_call(backward_kernel, out_shape=[jax.ShapeDtypeStruct((width, c...  20.3 us
    pallas_call x3, Pallas kernels, forward_part(): pl.pallas_call(functools.partial(forward_kernel, offset, n_pieces, n_othe...  18.2 us
    pallas_call x2, Pallas kernels, make_dense(): pl.pallas_call(functools.partial(dense_kernel, first), out_shape=pltpu.HB...  13.1 us
    pallas_call x2, Pallas kernels, make_other(): pl.pallas_call(functools.partial(other_kernel, first), out_shape=pltpu.HB...  10.7 us
    pallas_call x1, Pallas kernels, middle(): pl.pallas_call(functools.partial(middle_kernel, blocks), out_shape=[jax.S...  6.49 us
  transfers between devices with their start and end apart: 45, of which 20 were waited for; matrix products, arithmetic and copies ran while one was open for 3% of the time, Pallas kernels for 33%

profile of v14, /device:TPU:0, one launch (start us, length us, event | category | flops | bytes accessed | tf_op | source)
XLA Modules:
  0.0 183.9 jit_solution(410215713688085524)
XLA Ops:
  1.2 0.7 copy-done
  1.9 3.1 %collective-permute-start.2 = (bf16[512,512]{1,0:T(8,128)(2,1)S(1)}, bf16[512,512]{1,0:T(8,128)(2,1)S(1)}, u32[]{:S(2)}, u32[]{:S(2)}) collective-permute-start(bf16[512,512]{1,0:T(8,128)(2,1)S(1)} %constant_dynamic-slice_fusion.refs_2_), channel_id=1, source_target_pairs={{0,8},{1,9},{2,10},{3,11},{4,12},{5,13},{6,14},{7,15},{8,0},{9,1},... | collective-permute-start | bytes 1572872 | tf_op jit(solution)/shard_map/features_z/ppermute | solution.py:450
  5.0 1.5 collective-permute-start.3
  6.5 1.5 collective-permute-start.4
  8.0 0.7 add_bitcast_fusion
  8.7 0.7 copy.12
  10.3 6.7 %dense_blocks.2.refs_0_ = bf16[2,8,1024,512]{3,2,1,0:T(8,128)(2,1)} custom-call(s32[44]{0:T(128)S(1)} %pad_add_fusion.1.where_ref, s32[8,25]{1,0:T(8,128)S(1)} %pad_add_fusion.packed_ref, bf16[8,24,128,128]{3,2,1,0:T(8,128)(2,1)} %bitcast.18), custom_call_target="tpu_custom_call" | custom-call | bytes 393216 | tf_op jit(solution)/shard_map/dense_blocks/pallas_call | solution.py:49
  17.0 1.6 collective-permute-start.5
  18.6 1.5 collective-permute-start.6
  20.1 2.6 %collective-permute-start.7 = (bf16[512,512]{1,0:T(8,128)(2,1)S(1)}, bf16[512,512]{1,0:T(8,128)(2,1)}, u32[]{:S(2)}, u32[]{:S(2)}) collective-permute-start(bf16[512,512]{1,0:T(8,128)(2,1)S(1)} %constant_dynamic-slice_fusion.refs_2_), channel_id=1, source_target_pairs={{0,16},{1,17},{2,18},{3,19},{4,20},{5,21},{6,22},{7,23},{8,24},{9,... | collective-permute-start | bytes 1572872 | tf_op jit(solution)/shard_map/features_z/ppermute | solution.py:450
  22.7 8.5 %collective-permute-done.5.refs_6_ = bf16[512,512]{1,0:T(8,128)(2,1)S(1)} collective-permute-done((bf16[512,512]{1,0:T(8,128)(2,1)S(1)}, bf16[512,512]{1,0:T(8,128)(2,1)S(1)}, u32[]{:S(2)}, u32[]{:S(2)}) %collective-permute-start.5) | collective-permute-done | bytes 524320 | tf_op jit(solution)/shard_map/features_xy/ppermute | solution.py:450
  31.2 0.7 collective-permute-done.6.refs_7_
  31.9 0.7 collective-permute-start.8
  32.6 1.1 collective-permute-start.9
  33.7 6.5 %dense_blocks.3.dense_ref.a_ref = bf16[2,8,1024,512]{3,2,1,0:T(8,128)(2,1)} custom-call(s32[44]{0:T(128)S(1)} %pad_add_fusion.1.where_ref, s32[8,25]{1,0:T(8,128)S(1)} %pad_add_fusion.packed_ref, bf16[8,24,128,128]{3,2,1,0:T(8,128)(2,1)} %bitcast.19, bf16[2,8,1024,512]{3,2,1,0:T(8,128)(2,1)} %dense_blocks.2.refs_0_), custom_call_target="tpu_custom_call", output_to_operand_aliasing={{}: (3, {})} | custom-call | bytes 393216 | tf_op jit(solution)/shard_map/dense_blocks/pallas_call | solution.py:49
  40.2 5.3 %other_blocks.2.refs_0_ = bf16[4,1024,512]{2,1,0:T(8,128)(2,1)} custom-call(s32[44]{0:T(128)S(1)} %pad_add_fusion.1.where_ref, s32[8,25]{1,0:T(8,128)S(1)} %collective-permute-done.1.packed_ref, bf16[8,24,128,128]{3,2,1,0:T(8,128)(2,1)} %collective-permute-done.tiles_ref), custom_call_target="tpu_custom_call" | custom-call | bytes 393216 | tf_op jit(solution)/shard_map/other_blocks/pallas_call | solution.py:93
  45.5 0.8 copy-done.3
  46.3 0.8 copy-done.5
  47.1 2.1 %collective-permute-start.10 = (bf16[512,512]{1,0:T(8,128)(2,1)}, bf16[512,512]{1,0:T(8,128)(2,1)}, u32[]{:S(2)}, u32[]{:S(2)}) collective-permute-start(bf16[512,512]{1,0:T(8,128)(2,1)} %collective-permute-done.7.refs_10_), channel_id=1, source_target_pairs={{0,2},{1,3},{2,0},{3,1},{4,6},{5,7},{6,4},{7,5},{8,10},{9,11},{10,... | collective-permute-start | bytes 1572872 | tf_op jit(solution)/shard_map/features_xy/ppermute | solution.py:450
  49.3 0.9 collective-permute-start.12
  50.3 1.3 broadcast_select_fusion.1
  51.7 5.4 %other_blocks.3.refs_1_ = bf16[4,1024,512]{2,1,0:T(8,128)(2,1)} custom-call(s32[44]{0:T(128)S(1)} %pad_add_fusion.1.where_ref, s32[8,25]{1,0:T(8,128)S(1)} %collective-permute-done.1.packed_ref, bf16[8,24,128,128]{3,2,1,0:T(8,128)(2,1)} %collective-permute-done.tiles_ref), custom_call_target="tpu_custom_call" | custom-call | bytes 393216 | tf_op jit(solution)/shard_map/other_blocks/pallas_call | solution.py:93
  57.0 5.0 %collective-permute-done.10.refs_11_ = bf16[512,512]{1,0:T(8,128)(2,1)} collective-permute-done((bf16[512,512]{1,0:T(8,128)(2,1)}, bf16[512,512]{1,0:T(8,128)(2,1)}, u32[]{:S(2)}, u32[]{:S(2)}) %collective-permute-start.10) | collective-permute-done | bytes 524320 | tf_op jit(solution)/shard_map/features_xy/ppermute | solution.py:450
  62.0 1.5 collective-permute-done.11.refs_2_
  63.5 0.9 collective-permute-start.14
  64.4 1.1 collective-permute-start.15
  65.5 0.8 collective-permute-start.16
  66.4 9.6 %forward.3.refs_6_ = f32[1024,512]{1,0:T(8,128)S(1)} custom-call(s32[44]{0:T(128)S(1)} %pad_add_fusion.1.where_ref, bf16[2,8,1024,512]{3,2,1,0:T(8,128)(2,1)} %dense_blocks.3.dense_ref.a_ref, bf16[4,1024,512]{2,1,0:T(8,128)(2,1)} %other_blocks.2.refs_0_, bf16[4,1024,512]{2,1,0:T(8,128)(2,1)} %other_blocks.3.refs_1_, ...), custom_call_target="tpu_custom_call" | custom-call | flops 5368709120 | bytes 14680064 | tf_op jit(solution)/shard_map/forward/pallas_call | solution.py:196
  76.0 0.9 collective-permute-done.14.refs_4_
  77.2 1.1 collective-permute-done.16.refs_2_
  78.4 1.5 collective-permute-start.17
  80.6 5.2 %forward.4.refs_5_ = f32[1024,512]{1,0:T(8,128)S(1)} custom-call(s32[44]{0:T(128)S(1)} %pad_add_fusion.1.where_ref, bf16[2,8,1024,512]{3,2,1,0:T(8,128)(2,1)} %dense_blocks.3.dense_ref.a_ref, bf16[4,1024,512]{2,1,0:T(8,128)(2,1)} %other_blocks.2.refs_0_, bf16[4,1024,512]{2,1,0:T(8,128)(2,1)} %other_blocks.3.refs_1_, ...), custom_call_target="tpu_custom_call" | custom-call | flops 2147483648 | bytes 8388608 | tf_op jit(solution)/shard_map/forward/pallas_call | solution.py:196
  86.3 3.5 %forward.5.mine_ref = bf16[1024,512]{1,0:T(8,128)(2,1)S(1)} custom-call(s32[44]{0:T(128)S(1)} %pad_add_fusion.1.where_ref, bf16[2,8,1024,512]{3,2,1,0:T(8,128)(2,1)} %dense_blocks.3.dense_ref.a_ref, bf16[4,1024,512]{2,1,0:T(8,128)(2,1)} %other_blocks.2.refs_0_, bf16[4,1024,512]{2,1,0:T(8,128)(2,1)} %other_blocks.3.refs_1_, ...), custom_call_target="tpu_custom_call" | custom-call | flops 1073741824 | bytes 6291456 | tf_op jit(solution)/shard_map/forward/pallas_call | solution.py:196
  89.9 2.6 %collective-permute-done.19.other_ref = bf16[1024,512]{1,0:T(8,128)(2,1)S(1)} collective-permute-done((bf16[1024,512]{1,0:T(8,128)(2,1)S(1)}, bf16[1024,512]{1,0:T(8,128)(2,1)S(1)}, u32[]{:S(2)}, u32[]{:S(2)}) %collective-permute-start.19) | collective-permute-done | bytes 1048608 | tf_op jit(solution)/shard_map/partial_sums/ppermute | solution.py:450
  92.5 6.5 %middle.1 = (bf16[512,1024]{1,0:T(8,128)(2,1)S(1)}, bf16[256,512]{1,0:T(8,128)(2,1)S(1)}, bf16[256,512]{1,0:T(8,128)(2,1)S(1)}, bf16[4,64,512]{2,1,0:T(8,128)(2,1)S(1)}) custom-call(s32[44]{0:T(128)S(1)} %pad_add_fusion.1.where_ref, bf16[1024,512]{1,0:T(8,128)(2,1)S(1)} %forward.5.mine_ref, bf16[1024,512]{1,0:T(8,128)(2,1)S(1)} %collective-permute-done.19.other_ref, ...), custom_call_target="tpu_custom_call" | custom-call | flops 2684354560 | bytes 6291456 | tf_op jit(solution)/shard_map/middle/pallas_call | solution.py:281
  99.1 2.7 %collective-permute-start.22 = (bf16[64,512]{1,0:T(8,128)(2,1)S(1)}, bf16[64,512]{1,0:T(8,128)(2,1)S(1)}, u32[]{:S(2)}, u32[]{:S(2)}) collective-permute-start(bf16[64,512]{1,0:T(8,128)(2,1)S(1)} %get-tuple-element.298), channel_id=1, source_target_pairs={{0,24},{1,25},{2,26},{3,27},{4,28},{5,29},{6,30},{7,31},{8,16},{9,... | collective-permute-start | bytes 196616 | tf_op jit(solution)/shard_map/weight_grad/ppermute | solution.py:450
  101.8 1.8 collective-permute-start.20
  104.1 0.9 collective-permute-start.24
  105.0 4.6 %backward.3 = (bf16[512,512]{1,0:T(8,128)(2,1)S(1)}, bf16[512,512]{1,0:T(8,128)(2,1)S(1)}, bf16[512,512]{1,0:T(8,128)(2,1)S(1)}) custom-call(s32[44]{0:T(128)S(1)} %pad_add_fusion.1.where_ref, bf16[512,1024]{1,0:T(8,128)(2,1)S(1)} %get-tuple-element.237.grad_ref, bf16[2,8,1024,512]{3,2,1,0:T(8,128)(2,1)} %dense_blocks.3.dense_ref.a_ref), custom_call_target="tpu_custom_call" | custom-call | flops 1610612736 | bytes 5767168 | tf_op jit(solution)/shard_map/backward/pallas_call | solution.py:354
  109.6 1.5 collective-permute-start.26
  111.5 1.1 collective-permute-start.27
  112.6 1.4 collective-permute-start.28
  113.9 8.8 %backward.4 = (bf16[512,512]{1,0:T(8,128)(2,1)S(1)}, bf16[512,512]{1,0:T(8,128)(2,1)S(1)}, bf16[512,512]{1,0:T(8,128)(2,1)S(1)}, bf16[512,512]{1,0:T(8,128)(2,1)...) custom-call(s32[44]{0:T(128)S(1)} %pad_add_fusion.1.where_ref, ...), custom_call_target="tpu_custom_call" | custom-call | flops 3758096384 | bytes 12058624 | tf_op jit(solution)/shard_map/backward/pallas_call | solution.py:354
  123.4 3.9 %collective-permute-done.25 = bf16[64,512]{1,0:T(8,128)(2,1)S(1)} collective-permute-done((bf16[64,512]{1,0:T(8,128)(2,1)S(1)}, bf16[64,512]{1,0:T(8,128)(2,1)S(1)}, u32[]{:S(2)}, u32[]{:S(2)}) %collective-permute-start.25) | collective-permute-done | bytes 65568 | tf_op jit(solution)/shard_map/weight_grad/ppermute | solution.py:450
  128.3 1.0 collective-permute-start.30
  129.5 1.8 collective-permute-start.31
  131.3 6.9 %backward.5 = (bf16[512,512]{1,0:T(8,128)(2,1)S(1)}, bf16[512,512]{1,0:T(8,128)(2,1)S(1)}, bf16[512,512]{1,0:T(8,128)(2,1)S(1)}, bf16[512,512]{1,0:T(8,128)(2,1)S(1)}, bf16[512,512]{1,0:T(8,128)(2,1)S(1)}) custom-call(s32[44]{0:T(128)S(1)} %pad_add_fusion.1.where_ref, bf16[512,1024]{1,0:T(8,128)(2,1)S(1)} %get-tuple-element.237.grad_ref, ...), custom_call_target="tpu_custom_call" | custom-call | flops 2684354560 | bytes 8912896 | tf_op jit(solution)/shard_map/backward/pallas_call | solution.py:354
  138.2 0.9 collective-permute-start.34
  139.8 1.2 collective-permute-done.30
  141.0 1.3 collective-permute-start.32
  142.6 3.4 %collective-permute-start.36 = (bf16[256,512]{1,0:T(8,128)(2,1)S(1)}, bf16[256,512]{1,0:T(8,128)(2,1)S(1)}, u32[]{:S(2)}, u32[]{:S(2)}) collective-permute-start(bf16[256,512]{1,0:T(8,128)(2,1)S(1)} %get-tuple-element.294), channel_id=1, source_target_pairs={{0,16},{1,17},{2,18},{3,19},{4,20},{5,21},{6,22},{7,23},{8,24},{9,... | collective-permute-start | bytes 786440 | tf_op jit(solution)/shard_map/grads_z/ppermute | solution.py:450
  146.0 5.3 %collective-permute-done.32 = bf16[64,512]{1,0:T(8,128)(2,1)S(1)} collective-permute-done((bf16[64,512]{1,0:T(8,128)(2,1)S(1)}, bf16[64,512]{1,0:T(8,128)(2,1)S(1)}, u32[]{:S(2)}, u32[]{:S(2)}) %collective-permute-start.32) | collective-permute-done | bytes 65568 | tf_op jit(solution)/shard_map/weight_grad/ppermute | solution.py:450
  151.3 2.6 %collective-permute-start.33 = (bf16[1,64,512]{2,1,0:T(8,128)(2,1)S(1)}, bf16[1,64,512]{2,1,0:T(8,128)(2,1)S(1)}, u32[]{:S(2)}, u32[]{:S(2)}) collective-permute-start(bf16[1,64,512]{2,1,0:T(8,128)(2,1)S(1)} %fusion.3), channel_id=1, source_target_pairs={{0,16},{1,17},{2,18},{3,19},{4,20},{5,21},{6,22},{7,23},{8,24},{9,... | collective-permute-start | bytes 196616 | tf_op jit(solution)/shard_map/weight_grad/ppermute | solution.py:450
  153.9 1.4 collective-permute-start.40
  155.2 2.0 %collective-permute-done.33 = bf16[1,64,512]{2,1,0:T(8,128)(2,1)S(1)} collective-permute-done((bf16[1,64,512]{2,1,0:T(8,128)(2,1)S(1)}, bf16[1,64,512]{2,1,0:T(8,128)(2,1)S(1)}, u32[]{:S(2)}, u32[]{:S(2)}) %collective-permute-start.33) | collective-permute-done | bytes 65568 | tf_op jit(solution)/shard_map/weight_grad/ppermute | solution.py:450
  157.4 1.5 collective-permute-start.39
  159.0 2.4 %collective-permute-start.38 = (bf16[256,512]{1,0:T(8,128)(2,1)S(1)}, bf16[256,512]{1,0:T(8,128)(2,1)S(1)}, u32[]{:S(2)}, u32[]{:S(2)}) collective-permute-start(bf16[256,512]{1,0:T(8,128)(2,1)S(1)} %get-tuple-element.267), channel_id=1, source_target_pairs={{0,16},{1,17},{2,18},{3,19},{4,20},{5,21},{6,22},{7,23},{8,24},{9,... | collective-permute-start | bytes 786440 | tf_op jit(solution)/shard_map/grads_z/ppermute | solution.py:450
  162.0 4.5 %collective-permute-done.37 = bf16[2,64,512]{2,1,0:T(8,128)(2,1)S(1)} collective-permute-done((bf16[2,64,512]{2,1,0:T(8,128)(2,1)S(1)}, bf16[2,64,512]{2,1,0:T(8,128)(2,1)S(1)}, u32[]{:S(2)}, u32[]{:S(2)}) %collective-permute-start.37) | collective-permute-done | bytes 131104 | tf_op jit(solution)/shard_map/weight_grad/ppermute | solution.py:450
  167.0 2.9 %collective-permute-done.38.refs_5_ = bf16[256,512]{1,0:T(8,128)(2,1)S(1)} collective-permute-done((bf16[256,512]{1,0:T(8,128)(2,1)S(1)}, bf16[256,512]{1,0:T(8,128)(2,1)S(1)}, u32[]{:S(2)}, u32[]{:S(2)}) %collective-permute-start.38) | collective-permute-done | bytes 262176 | tf_op jit(solution)/shard_map/grads_z/ppermute | solution.py:450
  169.9 2.4 %collective-permute-done.39 = bf16[512,512]{1,0:T(8,128)(2,1)S(1)} collective-permute-done((bf16[512,512]{1,0:T(8,128)(2,1)S(1)}, bf16[512,512]{1,0:T(8,128)(2,1)S(1)}, u32[]{:S(2)}, u32[]{:S(2)}) %collective-permute-start.39) | collective-permute-done | bytes 524320 | tf_op jit(solution)/shard_map/grads_xy/ppermute | solution.py:450
  173.1 1.8 %activated.1 = bf16[512,512]{1,0:T(8,128)(2,1)} custom-call(s32[44]{0:T(128)S(1)} %pad_add_fusion.1.where_ref, bf16[1024,512]{1,0:T(8,128)(2,1)S(1)} %forward.5.mine_ref, bf16[1024,512]{1,0:T(8,128)(2,1)S(1)} %collective-permute-done.19.other_ref, bf16[512,512]{1,0:T(8,128)(2,1)S(1)} %copy-done.2, bf16[1024,512]{1,0:T(8,128)(2,1)S(1)} %pad_maximum_fusion.cot_ref), custom_call_target="tpu_custom_call" | custom-call | flops 268435456 | bytes 2097152 | tf_op jit(solution)/shard_map/activated/pallas_call | solution.py:318
  174.9 4.6 %collective-permute-done.41.refs_1_ = bf16[512,512]{1,0:T(8,128)(2,1)S(1)} collective-permute-done((bf16[512,512]{1,0:T(8,128)(2,1)S(1)}, bf16[512,512]{1,0:T(8,128)(2,1)S(1)}, u32[]{:S(2)}, u32[]{:S(2)}) %collective-permute-start.41) | collective-permute-done | bytes 524320 | tf_op jit(solution)/shard_map/grads_xy/ppermute | solution.py:450
  179.6 2.2 %collective-permute-done.43.refs_3_ = bf16[512,512]{1,0:T(8,128)(2,1)S(1)} collective-permute-done((bf16[512,512]{1,0:T(8,128)(2,1)S(1)}, bf16[512,512]{1,0:T(8,128)(2,1)S(1)}, u32[]{:S(2)}, u32[]{:S(2)}) %collective-permute-start.43) | collective-permute-done | bytes 524320 | tf_op jit(solution)/shard_map/grads_z/ppermute | solution.py:450
  181.8 2.1 %grads_out.1 = (bf16[1,512,512]{2,1,0:T(8,128)(2,1)}, f32[512,512]{1,0:T(8,128)}) custom-call(s32[44]{0:T(128)S(1)} %pad_add_fusion.1.where_ref, bf16[512,512]{1,0:T(8,128)(2,1)S(1)} %get-tuple-element.283.refs_0_, bf16[512,512]{1,0:T(8,128)(2,1)S(1)} %collective-permute-done.41.refs_1_, bf16[512,512]{1,0:T(8,128)(2,1)S(1)} %collective-permute-done.42.refs_2_, ...), custom_call_target="tpu_custom_call" | custom-call | flops 1048576 | bytes 2621440 | tf_op jit(solution)/shard_map/grads_out/pallas_call | solution.py:416
  (77 shorter events, 9.1 us)
Async XLA Ops:
  0.6 1.2 copy-start
  0.6 16.3 %collective-permute-start = (bf16[8,24,128,128]{3,2,1,0:T(8,128)(2,1)}, bf16[8,24,128,128]{3,2,1,0:T(8,128)(2,1)}, u32[]{:S(2)}, u32[]{:S(2)}) collective-permute-start(bf16[8,24,128,128]{3,2,1,0:T(8,128)(2,1)} %bitcast.17), channel_id=1, source_target_pairs={{0,1},{1,0},{2,3},{3,2},{4,5},{5,4},{6,7},{7,6},{8,9},{9,8},{10,11... | collective-permute-start | bytes 18874376 | tf_op jit(solution)/shard_map/tiles_exchange/ppermute | solution.py:450
  1.9 15.0 %collective-permute-start.2 = (bf16[512,512]{1,0:T(8,128)(2,1)S(1)}, bf16[512,512]{1,0:T(8,128)(2,1)S(1)}, u32[]{:S(2)}, u32[]{:S(2)}) collective-permute-start(bf16[512,512]{1,0:T(8,128)(2,1)S(1)} %constant_dynamic-slice_fusion.refs_2_), channel_id=1, source_target_pairs={{0,8},{1,9},{2,10},{3,11},{4,12},{5,13},{6,14},{7,15},{8,0},{9,1},... | collective-permute-start | bytes 1572872 | tf_op jit(solution)/shard_map/features_z/ppermute | solution.py:450
  5.0 17.7 %collective-permute-start.3 = (bf16[512,512]{1,0:T(8,128)(2,1)S(1)}, bf16[512,512]{1,0:T(8,128)(2,1)S(1)}, u32[]{:S(2)}, u32[]{:S(2)}) collective-permute-start(bf16[512,512]{1,0:T(8,128)(2,1)S(1)} %constant_dynamic-slice_fusion.refs_2_), channel_id=1, source_target_pairs={{0,2},{1,3},{2,0},{3,1},{4,6},{5,7},{6,4},{7,5},{8,10},{9,11},{10,... | collective-permute-start | bytes 1572872 | tf_op jit(solution)/shard_map/features_xy/ppermute | solution.py:450
  6.5 16.2 %collective-permute-start.4 = (bf16[512,512]{1,0:T(8,128)(2,1)S(1)}, bf16[512,512]{1,0:T(8,128)(2,1)S(1)}, u32[]{:S(2)}, u32[]{:S(2)}) collective-permute-start(bf16[512,512]{1,0:T(8,128)(2,1)S(1)} %constant_dynamic-slice_fusion.refs_2_), channel_id=1, source_target_pairs={{0,4},{1,5},{2,6},{3,7},{4,0},{5,1},{6,2},{7,3},{8,12},{9,13},{10,... | collective-permute-start | bytes 1572872 | tf_op jit(solution)/shard_map/features_xy/ppermute | solution.py:450
  9.5 7.4 %collective-permute-start.1 = (s32[8,25]{1,0:T(8,128)S(1)}, s32[8,25]{1,0:T(8,128)S(1)}, u32[]{:S(2)}, u32[]{:S(2)}) collective-permute-start(s32[8,25]{1,0:T(8,128)S(1)} %pad_add_fusion.packed_ref), channel_id=1, source_target_pairs={{0,1},{1,0},{2,3},{3,2},{4,5},{5,4},{6,7},{7,6},{8,9},{9,8},{10,11... | collective-permute-start | bytes 2408 | tf_op jit(solution)/shard_map/tiles_exchange/ppermute | solution.py:450
  17.0 14.2 %collective-permute-start.5 = (bf16[512,512]{1,0:T(8,128)(2,1)S(1)}, bf16[512,512]{1,0:T(8,128)(2,1)S(1)}, u32[]{:S(2)}, u32[]{:S(2)}) collective-permute-start(bf16[512,512]{1,0:T(8,128)(2,1)S(1)} %collective-permute-done.2.refs_5_), channel_id=1, source_target_pairs={{0,2},{1,3},{2,0},{3,1},{4,6},{5,7},{6,4},{7,5},{8,10},{9,11},{10,... | collective-permute-start | bytes 1572872 | tf_op jit(solution)/shard_map/features_xy/ppermute | solution.py:450
  18.6 13.4 %collective-permute-start.6 = (bf16[512,512]{1,0:T(8,128)(2,1)S(1)}, bf16[512,512]{1,0:T(8,128)(2,1)S(1)}, u32[]{:S(2)}, u32[]{:S(2)}) collective-permute-start(bf16[512,512]{1,0:T(8,128)(2,1)S(1)} %collective-permute-done.2.refs_5_), channel_id=1, source_target_pairs={{0,4},{1,5},{2,6},{3,7},{4,0},{5,1},{6,2},{7,3},{8,12},{9,13},{10,... | collective-permute-start | bytes 1572872 | tf_op jit(solution)/shard_map/features_xy/ppermute | solution.py:450
  20.1 25.4 %collective-permute-start.7 = (bf16[512,512]{1,0:T(8,128)(2,1)S(1)}, bf16[512,512]{1,0:T(8,128)(2,1)}, u32[]{:S(2)}, u32[]{:S(2)}) collective-permute-start(bf16[512,512]{1,0:T(8,128)(2,1)S(1)} %constant_dynamic-slice_fusion.refs_2_), channel_id=1, source_target_pairs={{0,16},{1,17},{2,18},{3,19},{4,20},{5,21},{6,22},{7,23},{8,24},{9,... | collective-permute-start | bytes 1572872 | tf_op jit(solution)/shard_map/features_z/ppermute | solution.py:450
  31.9 13.6 %collective-permute-start.8 = (bf16[512,512]{1,0:T(8,128)(2,1)S(1)}, bf16[512,512]{1,0:T(8,128)(2,1)S(1)}, u32[]{:S(2)}, u32[]{:S(2)}) collective-permute-start(bf16[512,512]{1,0:T(8,128)(2,1)S(1)} %collective-permute-done.3.refs_3_), channel_id=1, source_target_pairs={{0,4},{1,5},{2,6},{3,7},{4,0},{5,1},{6,2},{7,3},{8,12},{9,13},{10,... | collective-permute-start | bytes 1572872 | tf_op jit(solution)/shard_map/features_xy/ppermute | solution.py:450
  32.6 13.7 %collective-permute-start.9 = (bf16[512,512]{1,0:T(8,128)(2,1)S(1)}, bf16[512,512]{1,0:T(8,128)(2,1)S(1)}, u32[]{:S(2)}, u32[]{:S(2)}) collective-permute-start(bf16[512,512]{1,0:T(8,128)(2,1)S(1)} %collective-permute-done.6.refs_7_), channel_id=1, source_target_pairs={{0,2},{1,3},{2,0},{3,1},{4,6},{5,7},{6,4},{7,5},{8,10},{9,11},{10,... | collective-permute-start | bytes 1572872 | tf_op jit(solution)/shard_map/features_xy/ppermute | solution.py:450
  33.7 16.6 %collective-permute-start.13 = (bf16[512,512]{1,0:T(8,128)(2,1)}, bf16[512,512]{1,0:T(8,128)(2,1)}, u32[]{:S(2)}, u32[]{:S(2)}) collective-permute-start(bf16[512,512]{1,0:T(8,128)(2,1)} %param.14), channel_id=1, source_target_pairs={{0,1},{1,0},{2,3},{3,2},{4,5},{5,4},{6,7},{7,6},{8,9},{9,8},{10,11... | collective-permute-start | bytes 1572872 | tf_op jit(solution)/shard_map/cotangents/ppermute | solution.py:450
  45.5 0.8 copy-start.3
  46.3 0.8 copy-start.5
  47.1 14.9 %collective-permute-start.10 = (bf16[512,512]{1,0:T(8,128)(2,1)}, bf16[512,512]{1,0:T(8,128)(2,1)}, u32[]{:S(2)}, u32[]{:S(2)}) collective-permute-start(bf16[512,512]{1,0:T(8,128)(2,1)} %collective-permute-done.7.refs_10_), channel_id=1, source_target_pairs={{0,2},{1,3},{2,0},{3,1},{4,6},{5,7},{6,4},{7,5},{8,10},{9,11},{10,... | collective-permute-start | bytes 1572872 | tf_op jit(solution)/shard_map/features_xy/ppermute | solution.py:450
  49.2 14.3 %collective-permute-start.11 = (bf16[512,512]{1,0:T(8,128)(2,1)}, bf16[512,512]{1,0:T(8,128)(2,1)}, u32[]{:S(2)}, u32[]{:S(2)}) collective-permute-start(bf16[512,512]{1,0:T(8,128)(2,1)} %collective-permute-done.7.refs_10_), channel_id=1, source_target_pairs={{0,4},{1,5},{2,6},{3,7},{4,0},{5,1},{6,2},{7,3},{8,12},{9,13},{10,... | collective-permute-start | bytes 1572872 | tf_op jit(solution)/shard_map/features_xy/ppermute | solution.py:450
  49.3 14.2 %collective-permute-start.12 = (bf16[512,512]{1,0:T(8,128)(2,1)}, bf16[512,512]{1,0:T(8,128)(2,1)}, u32[]{:S(2)}, u32[]{:S(2)}) collective-permute-start(bf16[512,512]{1,0:T(8,128)(2,1)} %collective-permute-done.7.refs_10_), channel_id=1, source_target_pairs={{0,8},{1,9},{2,10},{3,11},{4,12},{5,13},{6,14},{7,15},{8,0},{9,1},... | collective-permute-start | bytes 1572872 | tf_op jit(solution)/shard_map/features_z/ppermute | solution.py:450
  51.6 14.7 %copy-start.4 = (bf16[512,512]{1,0:T(8,128)(2,1)S(1)}, bf16[512,512]{1,0:T(8,128)(2,1)}, u32[]{:S(2)}) copy-start(bf16[512,512]{1,0:T(8,128)(2,1)} %copy-done.3) | copy-start | bytes 1572868
  51.6 14.7 %copy-start.6 = (bf16[512,512]{1,0:T(8,128)(2,1)S(1)}, bf16[512,512]{1,0:T(8,128)(2,1)}, u32[]{:S(2)}) copy-start(bf16[512,512]{1,0:T(8,128)(2,1)} %copy-done.5) | copy-start | bytes 1572868
  63.5 13.4 %collective-permute-start.14 = (bf16[512,512]{1,0:T(8,128)(2,1)}, bf16[512,512]{1,0:T(8,128)(2,1)S(1)}, u32[]{:S(2)}, u32[]{:S(2)}) collective-permute-start(bf16[512,512]{1,0:T(8,128)(2,1)} %collective-permute-done.11.refs_2_), channel_id=1, source_target_pairs={{0,2},{1,3},{2,0},{3,1},{4,6},{5,7},{6,4},{7,5},{8,10},{9,11},{10,... | collective-permute-start | bytes 1572872 | tf_op jit(solution)/shard_map/features_xy/ppermute | solution.py:450
  64.4 12.8 %collective-permute-start.15 = (bf16[512,512]{1,0:T(8,128)(2,1)}, bf16[512,512]{1,0:T(8,128)(2,1)S(1)}, u32[]{:S(2)}, u32[]{:S(2)}) collective-permute-start(bf16[512,512]{1,0:T(8,128)(2,1)} %collective-permute-done.12.refs_3_), channel_id=1, source_target_pairs={{0,4},{1,5},{2,6},{3,7},{4,0},{5,1},{6,2},{7,3},{8,12},{9,13},{10,... | collective-permute-start | bytes 1572872 | tf_op jit(solution)/shard_map/features_xy/ppermute | solution.py:450
  65.5 12.8 %collective-permute-start.16 = (bf16[512,512]{1,0:T(8,128)(2,1)}, bf16[512,512]{1,0:T(8,128)(2,1)S(1)}, u32[]{:S(2)}, u32[]{:S(2)}) collective-permute-start(bf16[512,512]{1,0:T(8,128)(2,1)} %collective-permute-done.10.refs_11_), channel_id=1, source_target_pairs={{0,8},{1,9},{2,10},{3,11},{4,12},{5,13},{6,14},{7,15},{8,0},{9,1},... | collective-permute-start | bytes 1572872 | tf_op jit(solution)/shard_map/features_z/ppermute | solution.py:450
  78.4 7.4 %collective-permute-start.17 = (bf16[256,512]{1,0:T(8,128)(2,1)S(1)}, bf16[256,512]{1,0:T(8,128)(2,1)S(1)}, u32[]{:S(2)}, u32[]{:S(2)}) collective-permute-start(bf16[256,512]{1,0:T(8,128)(2,1)S(1)} %slice.42), channel_id=1, source_target_pairs={{0,2},{1,3},{2,0},{3,1},{4,6},{5,7},{6,4},{7,5},{8,10},{9,11},{10,... | collective-permute-start | bytes 786440 | tf_op jit(solution)/shard_map/features_xy/ppermute | solution.py:450
  79.9 6.4 %collective-permute-start.18 = (bf16[256,512]{1,0:T(8,128)(2,1)S(1)}, bf16[256,512]{1,0:T(8,128)(2,1)S(1)}, u32[]{:S(2)}, u32[]{:S(2)}) collective-permute-start(bf16[256,512]{1,0:T(8,128)(2,1)S(1)} %slice.43), channel_id=1, source_target_pairs={{0,4},{1,5},{2,6},{3,7},{4,0},{5,1},{6,2},{7,3},{8,12},{9,13},{10,... | collective-permute-start | bytes 786440 | tf_op jit(solution)/shard_map/features_xy/ppermute | solution.py:450
  85.7 6.8 %copy-start.2 = (bf16[512,512]{1,0:T(8,128)(2,1)S(1)}, bf16[512,512]{1,0:T(8,128)(2,1)}, u32[]{:S(2)}) copy-start(bf16[512,512]{1,0:T(8,128)(2,1)} %weight_ref.3) | copy-start | bytes 1572868
  89.8 2.7 %collective-permute-start.19 = (bf16[1024,512]{1,0:T(8,128)(2,1)S(1)}, bf16[1024,512]{1,0:T(8,128)(2,1)S(1)}, u32[]{:S(2)}, u32[]{:S(2)}) collective-permute-start(bf16[1024,512]{1,0:T(8,128)(2,1)S(1)} %forward.5.mine_ref), channel_id=1, source_target_pairs={{0,1},{1,0},{2,3},{3,2},{4,5},{5,4},{6,7},{7,6},{8,9},{9,8},{10,11... | collective-permute-start | bytes 3145736 | tf_op jit(solution)/shard_map/partial_sums/ppermute | solution.py:450
  99.1 10.5 %collective-permute-start.22 = (bf16[64,512]{1,0:T(8,128)(2,1)S(1)}, bf16[64,512]{1,0:T(8,128)(2,1)S(1)}, u32[]{:S(2)}, u32[]{:S(2)}) collective-permute-start(bf16[64,512]{1,0:T(8,128)(2,1)S(1)} %get-tuple-element.298), channel_id=1, source_target_pairs={{0,24},{1,25},{2,26},{3,27},{4,28},{5,29},{6,30},{7,31},{8,16},{9,... | collective-permute-start | bytes 196616 | tf_op jit(solution)/shard_map/weight_grad/ppermute | solution.py:450
  101.8 9.3 %collective-permute-start.21 = (bf16[64,512]{1,0:T(8,128)(2,1)S(1)}, bf16[64,512]{1,0:T(8,128)(2,1)S(1)}, u32[]{:S(2)}, u32[]{:S(2)}) collective-permute-start(bf16[64,512]{1,0:T(8,128)(2,1)S(1)} %get-tuple-element.299), channel_id=1, source_target_pairs={{0,16},{1,17},{2,18},{3,19},{4,20},{5,21},{6,22},{7,23},{8,24},{9,... | collective-permute-start | bytes 196616 | tf_op jit(solution)/shard_map/weight_grad/ppermute | solution.py:450
  101.8 9.3 %collective-permute-start.20 = (bf16[64,512]{1,0:T(8,128)(2,1)S(1)}, bf16[64,512]{1,0:T(8,128)(2,1)S(1)}, u32[]{:S(2)}, u32[]{:S(2)}) collective-permute-start(bf16[64,512]{1,0:T(8,128)(2,1)S(1)} %get-tuple-element.297), channel_id=1, source_target_pairs={{0,8},{1,9},{2,10},{3,11},{4,12},{5,13},{6,14},{7,15},{8,0},{9,1},... | collective-permute-start | bytes 196616 | tf_op jit(solution)/shard_map/weight_grad/ppermute | solution.py:450
  103.5 7.6 %collective-permute-start.23 = (bf16[256,512]{1,0:T(8,128)(2,1)S(1)}, bf16[256,512]{1,0:T(8,128)(2,1)S(1)}, u32[]{:S(2)}, u32[]{:S(2)}) collective-permute-start(bf16[256,512]{1,0:T(8,128)(2,1)S(1)} %get-tuple-element.211), channel_id=1, source_target_pairs={{0,2},{1,3},{2,0},{3,1},{4,6},{5,7},{6,4},{7,5},{8,10},{9,11},{10,... | collective-permute-start | bytes 786440 | tf_op jit(solution)/shard_map/grads_xy/ppermute | solution.py:450
  104.1 7.2 %collective-permute-start.24 = (bf16[256,512]{1,0:T(8,128)(2,1)S(1)}, bf16[256,512]{1,0:T(8,128)(2,1)S(1)}, u32[]{:S(2)}, u32[]{:S(2)}) collective-permute-start(bf16[256,512]{1,0:T(8,128)(2,1)S(1)} %get-tuple-element.212), channel_id=1, source_target_pairs={{0,4},{1,5},{2,6},{3,7},{4,0},{5,1},{6,2},{7,3},{8,12},{9,13},{10,... | collective-permute-start | bytes 786440 | tf_op jit(solution)/shard_map/grads_xy/ppermute | solution.py:450
  109.6 17.8 %collective-permute-start.26 = (bf16[512,512]{1,0:T(8,128)(2,1)S(1)}, bf16[512,512]{1,0:T(8,128)(2,1)S(1)}, u32[]{:S(2)}, u32[]{:S(2)}) collective-permute-start(bf16[512,512]{1,0:T(8,128)(2,1)S(1)} %get-tuple-element.223), channel_id=1, source_target_pairs={{0,2},{1,3},{2,0},{3,1},{4,6},{5,7},{6,4},{7,5},{8,10},{9,11},{10,... | collective-permute-start | bytes 1572872 | tf_op jit(solution)/shard_map/grads_xy/ppermute | solution.py:450
  111.5 15.9 %collective-permute-start.27 = (bf16[512,512]{1,0:T(8,128)(2,1)S(1)}, bf16[512,512]{1,0:T(8,128)(2,1)S(1)}, u32[]{:S(2)}, u32[]{:S(2)}) collective-permute-start(bf16[512,512]{1,0:T(8,128)(2,1)S(1)} %get-tuple-element.228), channel_id=1, source_target_pairs={{0,4},{1,5},{2,6},{3,7},{4,0},{5,1},{6,2},{7,3},{8,12},{9,13},{10,... | collective-permute-start | bytes 1572872 | tf_op jit(solution)/shard_map/grads_xy/ppermute | solution.py:450
  112.6 14.8 %collective-permute-start.28 = (bf16[512,512]{1,0:T(8,128)(2,1)S(1)}, bf16[512,512]{1,0:T(8,128)(2,1)S(1)}, u32[]{:S(2)}, u32[]{:S(2)}) collective-permute-start(bf16[512,512]{1,0:T(8,128)(2,1)S(1)} %get-tuple-element.229), channel_id=1, source_target_pairs={{0,8},{1,9},{2,10},{3,11},{4,12},{5,13},{6,14},{7,15},{8,0},{9,1},... | collective-permute-start | bytes 1572872 | tf_op jit(solution)/shard_map/grads_z/ppermute | solution.py:450
  122.7 4.6 %collective-permute-start.25 = (bf16[64,512]{1,0:T(8,128)(2,1)S(1)}, bf16[64,512]{1,0:T(8,128)(2,1)S(1)}, u32[]{:S(2)}, u32[]{:S(2)}) collective-permute-start(bf16[64,512]{1,0:T(8,128)(2,1)S(1)} %fusion.2), channel_id=1, source_target_pairs={{0,2},{1,3},{2,0},{3,1},{4,6},{5,7},{6,4},{7,5},{8,10},{9,11},{10,... | collective-permute-start | bytes 196616 | tf_op jit(solution)/shard_map/weight_grad/ppermute | solution.py:450
  127.5 12.2 %collective-permute-start.29 = (bf16[512,512]{1,0:T(8,128)(2,1)S(1)}, bf16[512,512]{1,0:T(8,128)(2,1)S(1)}, u32[]{:S(2)}, u32[]{:S(2)}) collective-permute-start(bf16[512,512]{1,0:T(8,128)(2,1)S(1)} %add_convert_fusion.5), channel_id=1, source_target_pairs={{0,2},{1,3},{2,0},{3,1},{4,6},{5,7},{6,4},{7,5},{8,10},{9,11},{10,... | collective-permute-start | bytes 1572872 | tf_op jit(solution)/shard_map/grads_xy/ppermute | solution.py:450
  128.3 12.7 %collective-permute-start.30 = (bf16[512,512]{1,0:T(8,128)(2,1)S(1)}, bf16[512,512]{1,0:T(8,128)(2,1)S(1)}, u32[]{:S(2)}, u32[]{:S(2)}) collective-permute-start(bf16[512,512]{1,0:T(8,128)(2,1)S(1)} %add_convert_fusion.4), channel_id=1, source_target_pairs={{0,4},{1,5},{2,6},{3,7},{4,0},{5,1},{6,2},{7,3},{8,12},{9,13},{10,... | collective-permute-start | bytes 1572872 | tf_op jit(solution)/shard_map/grads_xy/ppermute | solution.py:450
  129.5 11.5 %collective-permute-start.31 = (bf16[512,512]{1,0:T(8,128)(2,1)S(1)}, bf16[512,512]{1,0:T(8,128)(2,1)S(1)}, u32[]{:S(2)}, u32[]{:S(2)}) collective-permute-start(bf16[512,512]{1,0:T(8,128)(2,1)S(1)} %add_convert_fusion.3), channel_id=1, source_target_pairs={{0,8},{1,9},{2,10},{3,11},{4,12},{5,13},{6,14},{7,15},{8,0},{9,1},... | collective-permute-start | bytes 1572872 | tf_op jit(solution)/shard_map/grads_z/ppermute | solution.py:450
  138.2 19.1 %collective-permute-start.34 = (bf16[512,512]{1,0:T(8,128)(2,1)S(1)}, bf16[512,512]{1,0:T(8,128)(2,1)S(1)}, u32[]{:S(2)}, u32[]{:S(2)}) collective-permute-start(bf16[512,512]{1,0:T(8,128)(2,1)S(1)} %get-tuple-element.257), channel_id=1, source_target_pairs={{0,4},{1,5},{2,6},{3,7},{4,0},{5,1},{6,2},{7,3},{8,12},{9,13},{10,... | collective-permute-start | bytes 1572872 | tf_op jit(solution)/shard_map/grads_xy/ppermute | solution.py:450
  139.1 18.2 %collective-permute-start.35 = (bf16[512,512]{1,0:T(8,128)(2,1)S(1)}, bf16[512,512]{1,0:T(8,128)(2,1)S(1)}, u32[]{:S(2)}, u32[]{:S(2)}) collective-permute-start(bf16[512,512]{1,0:T(8,128)(2,1)S(1)} %get-tuple-element.258), channel_id=1, source_target_pairs={{0,2},{1,3},{2,0},{3,1},{4,6},{5,7},{6,4},{7,5},{8,10},{9,11},{10,... | collective-permute-start | bytes 1572872 | tf_op jit(solution)/shard_map/grads_xy/ppermute | solution.py:450
  141.0 10.3 %collective-permute-start.32 = (bf16[64,512]{1,0:T(8,128)(2,1)S(1)}, bf16[64,512]{1,0:T(8,128)(2,1)S(1)}, u32[]{:S(2)}, u32[]{:S(2)}) collective-permute-start(bf16[64,512]{1,0:T(8,128)(2,1)S(1)} %add_convert_fusion.9), channel_id=1, source_target_pairs={{0,4},{1,5},{2,6},{3,7},{4,0},{5,1},{6,2},{7,3},{8,12},{9,13},{10,... | collective-permute-start | bytes 196616 | tf_op jit(solution)/shard_map/weight_grad/ppermute | solution.py:450
  142.6 14.7 %collective-permute-start.36 = (bf16[256,512]{1,0:T(8,128)(2,1)S(1)}, bf16[256,512]{1,0:T(8,128)(2,1)S(1)}, u32[]{:S(2)}, u32[]{:S(2)}) collective-permute-start(bf16[256,512]{1,0:T(8,128)(2,1)S(1)} %get-tuple-element.294), channel_id=1, source_target_pairs={{0,16},{1,17},{2,18},{3,19},{4,20},{5,21},{6,22},{7,23},{8,24},{9,... | collective-permute-start | bytes 786440 | tf_op jit(solution)/shard_map/grads_z/ppermute | solution.py:450
  151.3 5.9 %collective-permute-start.33 = (bf16[1,64,512]{2,1,0:T(8,128)(2,1)S(1)}, bf16[1,64,512]{2,1,0:T(8,128)(2,1)S(1)}, u32[]{:S(2)}, u32[]{:S(2)}) collective-permute-start(bf16[1,64,512]{2,1,0:T(8,128)(2,1)S(1)} %fusion.3), channel_id=1, source_target_pairs={{0,16},{1,17},{2,18},{3,19},{4,20},{5,21},{6,22},{7,23},{8,24},{9,... | collective-permute-start | bytes 196616 | tf_op jit(solution)/shard_map/weight_grad/ppermute | solution.py:450
  153.9 16.0 %collective-permute-start.40 = (bf16[512,512]{1,0:T(8,128)(2,1)S(1)}, bf16[512,512]{1,0:T(8,128)(2,1)S(1)}, u32[]{:S(2)}, u32[]{:S(2)}) collective-permute-start(bf16[512,512]{1,0:T(8,128)(2,1)S(1)} %get-tuple-element.271), channel_id=1, source_target_pairs={{0,4},{1,5},{2,6},{3,7},{4,0},{5,1},{6,2},{7,3},{8,12},{9,13},{10,... | collective-permute-start | bytes 1572872 | tf_op jit(solution)/shard_map/grads_xy/ppermute | solution.py:450
  157.4 14.9 %collective-permute-start.39 = (bf16[512,512]{1,0:T(8,128)(2,1)S(1)}, bf16[512,512]{1,0:T(8,128)(2,1)S(1)}, u32[]{:S(2)}, u32[]{:S(2)}) collective-permute-start(bf16[512,512]{1,0:T(8,128)(2,1)S(1)} %add_convert_fusion.2), channel_id=1, source_target_pairs={{0,2},{1,3},{2,0},{3,1},{4,6},{5,7},{6,4},{7,5},{8,10},{9,11},{10,... | collective-permute-start | bytes 1572872 | tf_op jit(solution)/shard_map/grads_xy/ppermute | solution.py:450
  158.9 7.6 %collective-permute-start.37 = (bf16[2,64,512]{2,1,0:T(8,128)(2,1)S(1)}, bf16[2,64,512]{2,1,0:T(8,128)(2,1)S(1)}, u32[]{:S(2)}, u32[]{:S(2)}) collective-permute-start(bf16[2,64,512]{2,1,0:T(8,128)(2,1)S(1)} %pad_maximum_fusion.2), channel_id=1, source_target_pairs={{0,8},{1,9},{2,10},{3,11},{4,12},{5,13},{6,14},{7,15},{8,0},{9,1},... | collective-permute-start | bytes 393224 | tf_op jit(solution)/shard_map/weight_grad/ppermute | solution.py:450
  159.0 10.9 %collective-permute-start.38 = (bf16[256,512]{1,0:T(8,128)(2,1)S(1)}, bf16[256,512]{1,0:T(8,128)(2,1)S(1)}, u32[]{:S(2)}, u32[]{:S(2)}) collective-permute-start(bf16[256,512]{1,0:T(8,128)(2,1)S(1)} %get-tuple-element.267), channel_id=1, source_target_pairs={{0,16},{1,17},{2,18},{3,19},{4,20},{5,21},{6,22},{7,23},{8,24},{9,... | collective-permute-start | bytes 786440 | tf_op jit(solution)/shard_map/grads_z/ppermute | solution.py:450
  161.4 18.1 %collective-permute-start.41 = (bf16[512,512]{1,0:T(8,128)(2,1)S(1)}, bf16[512,512]{1,0:T(8,128)(2,1)S(1)}, u32[]{:S(2)}, u32[]{:S(2)}) collective-permute-start(bf16[512,512]{1,0:T(8,128)(2,1)S(1)} %get-tuple-element.275), channel_id=1, source_target_pairs={{0,2},{1,3},{2,0},{3,1},{4,6},{5,7},{6,4},{7,5},{8,10},{9,11},{10,... | collective-permute-start | bytes 1572872 | tf_op jit(solution)/shard_map/grads_xy/ppermute | solution.py:450
  166.5 13.1 %collective-permute-start.42 = (bf16[512,512]{1,0:T(8,128)(2,1)S(1)}, bf16[512,512]{1,0:T(8,128)(2,1)S(1)}, u32[]{:S(2)}, u32[]{:S(2)}) collective-permute-start(bf16[512,512]{1,0:T(8,128)(2,1)S(1)} %add_convert_fusion.1), channel_id=1, source_target_pairs={{0,4},{1,5},{2,6},{3,7},{4,0},{5,1},{6,2},{7,3},{8,12},{9,13},{10,... | collective-permute-start | bytes 1572872 | tf_op jit(solution)/shard_map/grads_xy/ppermute | solution.py:450
  172.3 11.6 %copy-start.1 = (bf16[1024,512]{1,0:T(8,128)(2,1)S(1)}, bf16[1024,512]{1,0:T(8,128)(2,1)}, u32[]{:S(2)}) copy-start(bf16[1024,512]{1,0:T(8,128)(2,1)} %param.8) | copy-start | bytes 3145732
  172.6 9.2 %collective-permute-start.43 = (bf16[512,512]{1,0:T(8,128)(2,1)S(1)}, bf16[512,512]{1,0:T(8,128)(2,1)S(1)}, u32[]{:S(2)}, u32[]{:S(2)}) collective-permute-start(bf16[512,512]{1,0:T(8,128)(2,1)S(1)} %add_convert_fusion), channel_id=1, source_target_pairs={{0,8},{1,9},{2,10},{3,11},{4,12},{5,13},{6,14},{7,15},{8,0},{9,1},... | collective-permute-start | bytes 1572872 | tf_op jit(solution)/shard_map/grads_z/ppermute | solution.py:450
  173.1 6.5 %collective-permute-start.44 = (bf16[4,64,512]{2,1,0:T(8,128)(2,1)S(1)}, bf16[4,64,512]{2,1,0:T(8,128)(2,1)S(1)}, u32[]{:S(2)}, u32[]{:S(2)}) collective-permute-start(bf16[4,64,512]{2,1,0:T(8,128)(2,1)S(1)} %pad_maximum_fusion.1.refs_6_), channel_id=1, source_target_pairs={{0,1},{1,0},{2,3},{3,2},{4,5},{5,4},{6,7},{7,6},{8,9},{9,8},{10,11... | collective-permute-start | bytes 786440 | tf_op jit(solution)/shard_map/weight_grad/ppermute | solution.py:450

commit v15 on v13

--- a/solution.py
+++ b/solution.py
@@ -509,6 +509,7 @@
         with jax.named_scope("other_blocks"):
             return [make_other(first, where, *sent, block_rows, n_rep) for sent in live["tiles"]]
 
+    live["cot"] = cotangent
     live[0] = lax.dynamic_slice_in_dim(features, rep * part, part, axis=0)
     with jax.named_scope("tiles_exchange"):
         live["tiles"] = [
@@ -527,11 +528,9 @@
         if pair == 0:
             build_own(0)
         if pair == 1:
-            two = build_others(panels // 2)
-            live["others"] = [side for sides in zip(live.pop("one"), two) for side in sides]
+            one, two = build_others(0), build_others(panels // 2)
+            live["others"] = [side for sides in zip(one, two) for side in sides]
             del live["tiles"]
-            with jax.named_scope("cotangents"):
-                live["cot"] = gather_rep(cotangent)
         if pair > 1:
             live["total"] = forward_step(("late", pair - 1), live.pop("units"), live["total"])
         close(*(["even_x", "even_y"] if pair == 0 else []))
@@ -561,7 +560,8 @@
                 units += [flip(live["even_x"], Y), flip(live["odd_y"], X)]
             live["units"] = units
             build_own(panels // 2)
-            live["one"] = build_others(0)
+            with jax.named_scope("cotangents"):
+                live["cot"] = gather_rep(live["cot"])
         else:
             with jax.named_scope(FEATURES_ACROSS):
                 odd_xy = [flip(live["odd_y"][:half], X), flip(live["odd_x"][half:], Y)]

time: 183 us -> 193 us (1.055)
  waiting for transfers between devices: 47.1 us -> 65.5 us
  starting transfers between devices: 51.8 us -> 45.6 us
    ppermute x45, waiting for transfers between devices: 47.1 us -> 65.5 us  [flip(): return lax.ppermute(value, BOTH, pairs)]
    ppermute x45, starting transfers between devices: 51.8 us -> 45.6 us  [flip(): return lax.ppermute(value, BOTH, pairs)]
  transfers between devices with their start and end apart: 45 -> 45, of which waited for: 20 -> 20; matrix products, arithmetic and copies ran while one was open for 3% -> 3% of each run, Pallas kernels for 34% -> 32%
where the time goes in v15:
time: 193 us; the launch traced here: 192 us
  Pallas kernels  73.9 us (38%)
  waiting for transfers between devices  65.5 us (34%)
  starting transfers between devices  45.6 us (24%)
  other arithmetic  4.16 us (2%)
    ppermute x45, waiting for transfers between devices, flip(): return lax.ppermute(value, BOTH, pairs)  65.5 us
    ppermute x45, starting transfers between devices, flip(): return lax.ppermute(value, BOTH, pairs)  45.6 us
    pallas_call x4, Pallas kernels, backward_part(): pl.pallas_call(backward_kernel, out_shape=[jax.ShapeDtypeStruct((width, c...  21.4 us
    pallas_call x3, Pallas kernels, forward_part(): pl.pallas_call(functools.partial(forward_kernel, offset, n_pieces, n_othe...  17.9 us
    pallas_call x2, Pallas kernels, make_dense(): pl.pallas_call(functools.partial(dense_kernel, first), out_shape=pltpu.HB...  13.1 us
    pallas_call x2, Pallas kernels, make_other(): pl.pallas_call(functools.partial(other_kernel, first), out_shape=pltpu.HB...  10.9 us
    pallas_call x1, Pallas kernels, middle(): pl.pallas_call(functools.partial(middle_kernel, blocks), out_shape=[jax.S...  6.49 us
  transfers between devices with their start and end apart: 45, of which 20 were waited for; matrix products, arithmetic and copies ran while one was open for 3% of the time, Pallas kernels for 32%

profile of v15, /device:TPU:0, one launch (start us, length us, event | category | flops | bytes accessed | tf_op | source)
XLA Modules:
  0.0 191.6 jit_solution(5428725080043687789)
XLA Ops:
  1.2 0.7 copy-done
  1.9 3.1 %collective-permute-start.2 = (bf16[512,512]{1,0:T(8,128)(2,1)S(1)}, bf16[512,512]{1,0:T(8,128)(2,1)S(1)}, u32[]{:S(2)}, u32[]{:S(2)}) collective-permute-start(bf16[512,512]{1,0:T(8,128)(2,1)S(1)} %constant_dynamic-slice_fusion.refs_2_), channel_id=1, source_target_pairs={{0,8},{1,9},{2,10},{3,11},{4,12},{5,13},{6,14},{7,15},{8,0},{9,1},... | collective-permute-start | bytes 1572872 | tf_op jit(solution)/shard_map/features_z/ppermute | solution.py:450
  5.0 1.5 collective-permute-start.3
  6.5 1.5 collective-permute-start.4
  8.0 0.7 add_bitcast_fusion
  8.7 0.7 copy.12
  9.5 0.7 broadcast_xor_fusion
  10.3 6.6 %dense_blocks.2.refs_0_ = bf16[2,8,1024,512]{3,2,1,0:T(8,128)(2,1)} custom-call(s32[44]{0:T(128)S(1)} %pad_add_fusion.1.where_ref, s32[8,25]{1,0:T(8,128)S(1)} %pad_add_fusion.packed_ref, bf16[8,24,128,128]{3,2,1,0:T(8,128)(2,1)} %bitcast.17), custom_call_target="tpu_custom_call" | custom-call | bytes 393216 | tf_op jit(solution)/shard_map/dense_blocks/pallas_call | solution.py:49
  16.9 1.7 collective-permute-start.5
  18.6 1.5 collective-permute-start.6
  20.1 11.2 %collective-permute-done.5.refs_6_ = bf16[512,512]{1,0:T(8,128)(2,1)S(1)} collective-permute-done((bf16[512,512]{1,0:T(8,128)(2,1)S(1)}, bf16[512,512]{1,0:T(8,128)(2,1)S(1)}, u32[]{:S(2)}, u32[]{:S(2)}) %collective-permute-start.5) | collective-permute-done | bytes 524320 | tf_op jit(solution)/shard_map/features_xy/ppermute | solution.py:450
  31.4 2.7 %collective-permute-start.8 = (bf16[512,512]{1,0:T(8,128)(2,1)S(1)}, bf16[512,512]{1,0:T(8,128)(2,1)}, u32[]{:S(2)}, u32[]{:S(2)}) collective-permute-start(bf16[512,512]{1,0:T(8,128)(2,1)S(1)} %constant_dynamic-slice_fusion.refs_2_), channel_id=1, source_target_pairs={{0,16},{1,17},{2,18},{3,19},{4,20},{5,21},{6,22},{7,23},{8,24},{9,... | collective-permute-start | bytes 1572872 | tf_op jit(solution)/shard_map/features_z/ppermute | solution.py:450
  34.1 1.7 collective-permute-start.10
  36.1 6.5 %dense_blocks.3.dense_ref.a_ref = bf16[2,8,1024,512]{3,2,1,0:T(8,128)(2,1)} custom-call(s32[44]{0:T(128)S(1)} %pad_add_fusion.1.where_ref, s32[8,25]{1,0:T(8,128)S(1)} %pad_add_fusion.packed_ref, bf16[8,24,128,128]{3,2,1,0:T(8,128)(2,1)} %bitcast.18, bf16[2,8,1024,512]{3,2,1,0:T(8,128)(2,1)} %dense_blocks.2.refs_0_), custom_call_target="tpu_custom_call", output_to_operand_aliasing={{}: (3, {})} | custom-call | bytes 393216 | tf_op jit(solution)/shard_map/dense_blocks/pallas_call | solution.py:49
  42.5 1.3 broadcast_select_fusion.1
  43.9 14.1 %collective-permute-done.8.refs_10_ = bf16[512,512]{1,0:T(8,128)(2,1)} collective-permute-done((bf16[512,512]{1,0:T(8,128)(2,1)S(1)}, bf16[512,512]{1,0:T(8,128)(2,1)}, u32[]{:S(2)}, u32[]{:S(2)}) %collective-permute-start.8) | collective-permute-done | bytes 524320 | tf_op jit(solution)/shard_map/features_z/ppermute | solution.py:450
  58.1 1.6 collective-permute-start.11
  60.4 5.5 %other_blocks.3.refs_1_ = bf16[4,1024,512]{2,1,0:T(8,128)(2,1)} custom-call(s32[44]{0:T(128)S(1)} %pad_add_fusion.1.where_ref, s32[8,25]{1,0:T(8,128)S(1)} %collective-permute-done.1.packed_ref, bf16[8,24,128,128]{3,2,1,0:T(8,128)(2,1)} %collective-permute-done.tiles_ref), custom_call_target="tpu_custom_call" | custom-call | bytes 393216 | tf_op jit(solution)/shard_map/other_blocks/pallas_call | solution.py:93
  65.9 5.4 %other_blocks.2.refs_0_ = bf16[4,1024,512]{2,1,0:T(8,128)(2,1)} custom-call(s32[44]{0:T(128)S(1)} %pad_add_fusion.1.where_ref, s32[8,25]{1,0:T(8,128)S(1)} %collective-permute-done.1.packed_ref, bf16[8,24,128,128]{3,2,1,0:T(8,128)(2,1)} %collective-permute-done.tiles_ref), custom_call_target="tpu_custom_call" | custom-call | bytes 393216 | tf_op jit(solution)/shard_map/other_blocks/pallas_call | solution.py:93
  71.3 0.7 collective-permute-done.11.refs_11_
  72.0 1.5 collective-permute-done.12.refs_2_
  73.5 0.9 collective-permute-start.14
  74.4 1.1 collective-permute-start.15
  75.9 9.5 %forward.3.refs_6_ = f32[1024,512]{1,0:T(8,128)S(1)} custom-call(s32[44]{0:T(128)S(1)} %pad_add_fusion.1.where_ref, bf16[2,8,1024,512]{3,2,1,0:T(8,128)(2,1)} %dense_blocks.3.dense_ref.a_ref, bf16[4,1024,512]{2,1,0:T(8,128)(2,1)} %other_blocks.2.refs_0_, bf16[4,1024,512]{2,1,0:T(8,128)(2,1)} %other_blocks.3.refs_1_, ...), custom_call_target="tpu_custom_call" | custom-call | flops 5368709120 | bytes 14680064 | tf_op jit(solution)/shard_map/forward/pallas_call | solution.py:196
  85.4 0.8 collective-permute-done.14.refs_4_
  86.6 0.8 collective-permute-done.16.refs_2_
  87.4 1.8 collective-permute-start.17
  89.2 0.7 collective-permute-start.18
  89.9 4.9 %forward.4.refs_5_ = f32[1024,512]{1,0:T(8,128)S(1)} custom-call(s32[44]{0:T(128)S(1)} %pad_add_fusion.1.where_ref, bf16[2,8,1024,512]{3,2,1,0:T(8,128)(2,1)} %dense_blocks.3.dense_ref.a_ref, bf16[4,1024,512]{2,1,0:T(8,128)(2,1)} %other_blocks.2.refs_0_, bf16[4,1024,512]{2,1,0:T(8,128)(2,1)} %other_blocks.3.refs_1_, ...), custom_call_target="tpu_custom_call" | custom-call | flops 2147483648 | bytes 8388608 | tf_op jit(solution)/shard_map/forward/pallas_call | solution.py:196
  94.8 0.8 collective-permute-done.18.refs_4_
  95.7 3.5 %forward.5.mine_ref = bf16[1024,512]{1,0:T(8,128)(2,1)S(1)} custom-call(s32[44]{0:T(128)S(1)} %pad_add_fusion.1.where_ref, bf16[2,8,1024,512]{3,2,1,0:T(8,128)(2,1)} %dense_blocks.3.dense_ref.a_ref, bf16[4,1024,512]{2,1,0:T(8,128)(2,1)} %other_blocks.2.refs_0_, bf16[4,1024,512]{2,1,0:T(8,128)(2,1)} %other_blocks.3.refs_1_, ...), custom_call_target="tpu_custom_call" | custom-call | flops 1073741824 | bytes 6291456 | tf_op jit(solution)/shard_map/forward/pallas_call | solution.py:196
  99.2 2.6 %collective-permute-done.19.other_ref = bf16[1024,512]{1,0:T(8,128)(2,1)S(1)} collective-permute-done((bf16[1024,512]{1,0:T(8,128)(2,1)S(1)}, bf16[1024,512]{1,0:T(8,128)(2,1)S(1)}, u32[]{:S(2)}, u32[]{:S(2)}) %collective-permute-start.19) | collective-permute-done | bytes 1048608 | tf_op jit(solution)/shard_map/partial_sums/ppermute | solution.py:450
  101.9 6.5 %middle.1 = (bf16[512,1024]{1,0:T(8,128)(2,1)S(1)}, bf16[256,512]{1,0:T(8,128)(2,1)S(1)}, bf16[256,512]{1,0:T(8,128)(2,1)S(1)}, bf16[4,64,512]{2,1,0:T(8,128)(2,1)S(1)}) custom-call(s32[44]{0:T(128)S(1)} %pad_add_fusion.1.where_ref, bf16[1024,512]{1,0:T(8,128)(2,1)S(1)} %forward.5.mine_ref, bf16[1024,512]{1,0:T(8,128)(2,1)S(1)} %collective-permute-done.19.other_ref, ...), custom_call_target="tpu_custom_call" | custom-call | flops 2684354560 | bytes 6291456 | tf_op jit(solution)/shard_map/middle/pallas_call | solution.py:281
  108.4 0.7 collective-permute-start.20
  109.1 2.1 %collective-permute-start.21 = (bf16[64,512]{1,0:T(8,128)(2,1)S(1)}, bf16[64,512]{1,0:T(8,128)(2,1)S(1)}, u32[]{:S(2)}, u32[]{:S(2)}) collective-permute-start(bf16[64,512]{1,0:T(8,128)(2,1)S(1)} %get-tuple-element.309), channel_id=1, source_target_pairs={{0,16},{1,17},{2,18},{3,19},{4,20},{5,21},{6,22},{7,23},{8,24},{9,... | collective-permute-start | bytes 196616 | tf_op jit(solution)/shard_map/weight_grad/ppermute | solution.py:450
  111.2 1.6 collective-permute-start.22
  113.1 1.0 collective-permute-start.24
  114.2 4.6 %backward.4 = (bf16[512,512]{1,0:T(8,128)(2,1)S(1)}, bf16[512,512]{1,0:T(8,128)(2,1)S(1)}, bf16[512,512]{1,0:T(8,128)(2,1)S(1)}) custom-call(s32[44]{0:T(128)S(1)} %pad_add_fusion.1.where_ref, bf16[512,1024]{1,0:T(8,128)(2,1)S(1)} %get-tuple-element.257.grad_ref, bf16[2,8,1024,512]{3,2,1,0:T(8,128)(2,1)} %dense_blocks.3.dense_ref.a_ref), custom_call_target="tpu_custom_call" | custom-call | flops 1610612736 | bytes 5767168 | tf_op jit(solution)/shard_map/backward/pallas_call | solution.py:354
  118.8 1.4 collective-permute-start.26
  120.5 1.4 collective-permute-start.27
  122.4 5.5 %backward.5 = (bf16[512,512]{1,0:T(8,128)(2,1)S(1)}, bf16[512,512]{1,0:T(8,128)(2,1)S(1)}, bf16[512,512]{1,0:T(8,128)(2,1)S(1)}, bf16[512,512]{1,0:T(8,128)(2,1)S(1)}) custom-call(s32[44]{0:T(128)S(1)} %pad_add_fusion.1.where_ref, bf16[512,1024]{1,0:T(8,128)(2,1)S(1)} %get-tuple-element.257.grad_ref, bf16[2,8,1024,512]{3,2,1,0:T(8,128)(2,1)} %dense_blocks.3.dense_ref.a_ref), custom_call_target="tpu_custom_call" | custom-call | flops 2147483648 | bytes 7340032 | tf_op jit(solution)/shard_map/backward/pallas_call | solution.py:354
  127.9 0.7 collective-permute-start.25
  128.6 4.5 %collective-permute-done.25 = bf16[64,512]{1,0:T(8,128)(2,1)S(1)} collective-permute-done((bf16[64,512]{1,0:T(8,128)(2,1)S(1)}, bf16[64,512]{1,0:T(8,128)(2,1)S(1)}, u32[]{:S(2)}, u32[]{:S(2)}) %collective-permute-start.25) | collective-permute-done | bytes 65568 | tf_op jit(solution)/shard_map/weight_grad/ppermute | solution.py:450
  133.1 0.8 collective-permute-done.28
  134.7 0.7 collective-permute-start.31
  135.5 1.4 collective-permute-start.30
  136.9 6.7 %backward.6 = (bf16[512,512]{1,0:T(8,128)(2,1)S(1)}, bf16[512,512]{1,0:T(8,128)(2,1)S(1)}, bf16[512,512]{1,0:T(8,128)(2,1)S(1)}, bf16[512,512]{1,0:T(8,128)(2,1)S(1)}, bf16[512,512]{1,0:T(8,128)(2,1)S(1)}) custom-call(s32[44]{0:T(128)S(1)} %pad_add_fusion.1.where_ref, bf16[512,1024]{1,0:T(8,128)(2,1)S(1)} %get-tuple-element.257.grad_ref, ...), custom_call_target="tpu_custom_call" | custom-call | flops 2684354560 | bytes 8912896 | tf_op jit(solution)/shard_map/backward/pallas_call | solution.py:354
  143.6 0.8 collective-permute-start.29
  144.4 1.3 collective-permute-start.34
  145.7 4.3 %collective-permute-done.29 = bf16[64,512]{1,0:T(8,128)(2,1)S(1)} collective-permute-done((bf16[64,512]{1,0:T(8,128)(2,1)S(1)}, bf16[64,512]{1,0:T(8,128)(2,1)S(1)}, u32[]{:S(2)}, u32[]{:S(2)}) %collective-permute-start.29) | collective-permute-done | bytes 65568 | tf_op jit(solution)/shard_map/weight_grad/ppermute | solution.py:450
  150.9 2.9 %collective-permute-start.36 = (bf16[256,512]{1,0:T(8,128)(2,1)S(1)}, bf16[256,512]{1,0:T(8,128)(2,1)S(1)}, u32[]{:S(2)}, u32[]{:S(2)}) collective-permute-start(bf16[256,512]{1,0:T(8,128)(2,1)S(1)} %get-tuple-element.304), channel_id=1, source_target_pairs={{0,16},{1,17},{2,18},{3,19},{4,20},{5,21},{6,22},{7,23},{8,24},{9,... | collective-permute-start | bytes 786440 | tf_op jit(solution)/shard_map/grads_z/ppermute | solution.py:450
  153.7 4.6 %backward.7 = (bf16[512,512]{1,0:T(8,128)(2,1)S(1)}, bf16[512,512]{1,0:T(8,128)(2,1)S(1)}, bf16[512,512]{1,0:T(8,128)(2,1)S(1)}) custom-call(s32[44]{0:T(128)S(1)} %pad_add_fusion.1.where_ref, bf16[512,1024]{1,0:T(8,128)(2,1)S(1)} %get-tuple-element.257.grad_ref, bf16[2,8,1024,512]{3,2,1,0:T(8,128)(2,1)} %dense_blocks.3.dense_ref.a_ref), custom_call_target="tpu_custom_call" | custom-call | flops 1610612736 | bytes 5767168 | tf_op jit(solution)/shard_map/backward/pallas_call | solution.py:354
  158.5 1.2 collective-permute-start.40
  159.8 4.4 %collective-permute-done.33 = bf16[1,64,512]{2,1,0:T(8,128)(2,1)S(1)} collective-permute-done((bf16[1,64,512]{2,1,0:T(8,128)(2,1)S(1)}, bf16[1,64,512]{2,1,0:T(8,128)(2,1)S(1)}, u32[]{:S(2)}, u32[]{:S(2)}) %collective-permute-start.33) | collective-permute-done | bytes 65568 | tf_op jit(solution)/shard_map/weight_grad/ppermute | solution.py:450
  164.4 1.7 collective-permute-start.39
  166.3 1.8 collective-permute-start.38
  168.2 0.6 collective-permute-start.42
  168.8 4.1 %collective-permute-done.37 = bf16[2,64,512]{2,1,0:T(8,128)(2,1)S(1)} collective-permute-done((bf16[2,64,512]{2,1,0:T(8,128)(2,1)S(1)}, bf16[2,64,512]{2,1,0:T(8,128)(2,1)S(1)}, u32[]{:S(2)}, u32[]{:S(2)}) %collective-permute-start.37) | collective-permute-done | bytes 131104 | tf_op jit(solution)/shard_map/weight_grad/ppermute | solution.py:450
  173.1 4.2 %collective-permute-done.38.refs_5_ = bf16[256,512]{1,0:T(8,128)(2,1)S(1)} collective-permute-done((bf16[256,512]{1,0:T(8,128)(2,1)S(1)}, bf16[256,512]{1,0:T(8,128)(2,1)S(1)}, u32[]{:S(2)}, u32[]{:S(2)}) %collective-permute-start.38) | collective-permute-done | bytes 262176 | tf_op jit(solution)/shard_map/grads_z/ppermute | solution.py:450
  177.3 2.0 %collective-permute-done.39 = bf16[512,512]{1,0:T(8,128)(2,1)S(1)} collective-permute-done((bf16[512,512]{1,0:T(8,128)(2,1)S(1)}, bf16[512,512]{1,0:T(8,128)(2,1)S(1)}, u32[]{:S(2)}, u32[]{:S(2)}) %collective-permute-start.39) | collective-permute-done | bytes 524320 | tf_op jit(solution)/shard_map/grads_xy/ppermute | solution.py:450
  179.7 1.9 activated.1
  181.5 5.0 %collective-permute-done.41.refs_1_ = bf16[512,512]{1,0:T(8,128)(2,1)S(1)} collective-permute-done((bf16[512,512]{1,0:T(8,128)(2,1)S(1)}, bf16[512,512]{1,0:T(8,128)(2,1)S(1)}, u32[]{:S(2)}, u32[]{:S(2)}) %collective-permute-start.41) | collective-permute-done | bytes 524320 | tf_op jit(solution)/shard_map/grads_xy/ppermute | solution.py:450
  186.6 2.9 %collective-permute-done.43.refs_3_ = bf16[512,512]{1,0:T(8,128)(2,1)S(1)} collective-permute-done((bf16[512,512]{1,0:T(8,128)(2,1)S(1)}, bf16[512,512]{1,0:T(8,128)(2,1)S(1)}, u32[]{:S(2)}, u32[]{:S(2)}) %collective-permute-start.43) | collective-permute-done | bytes 524320 | tf_op jit(solution)/shard_map/grads_z/ppermute | solution.py:450
  189.5 2.1 %grads_out.1 = (bf16[1,512,512]{2,1,0:T(8,128)(2,1)}, f32[512,512]{1,0:T(8,128)}) custom-call(s32[44]{0:T(128)S(1)} %pad_add_fusion.1.where_ref, bf16[512,512]{1,0:T(8,128)(2,1)S(1)} %get-tuple-element.293.refs_0_, bf16[512,512]{1,0:T(8,128)(2,1)S(1)} %collective-permute-done.41.refs_1_, bf16[512,512]{1,0:T(8,128)(2,1)S(1)} %collective-permute-done.42.refs_2_, ...), custom_call_target="tpu_custom_call" | custom-call | flops 1048576 | bytes 2621440 | tf_op jit(solution)/shard_map/grads_out/pallas_call | solution.py:416
  (70 shorter events, 7.0 us)
Async XLA Ops:
  0.6 1.2 copy-start
  0.6 16.3 %collective-permute-start = (bf16[8,24,128,128]{3,2,1,0:T(8,128)(2,1)}, bf16[8,24,128,128]{3,2,1,0:T(8,128)(2,1)}, u32[]{:S(2)}, u32[]{:S(2)}) collective-permute-start(bf16[8,24,128,128]{3,2,1,0:T(8,128)(2,1)} %bitcast.16), channel_id=1, source_target_pairs={{0,1},{1,0},{2,3},{3,2},{4,5},{5,4},{6,7},{7,6},{8,9},{9,8},{10,11... | collective-permute-start | bytes 18874376 | tf_op jit(solution)/shard_map/tiles_exchange/ppermute | solution.py:450
  1.9 15.0 %collective-permute-start.2 = (bf16[512,512]{1,0:T(8,128)(2,1)S(1)}, bf16[512,512]{1,0:T(8,128)(2,1)S(1)}, u32[]{:S(2)}, u32[]{:S(2)}) collective-permute-start(bf16[512,512]{1,0:T(8,128)(2,1)S(1)} %constant_dynamic-slice_fusion.refs_2_), channel_id=1, source_target_pairs={{0,8},{1,9},{2,10},{3,11},{4,12},{5,13},{6,14},{7,15},{8,0},{9,1},... | collective-permute-start | bytes 1572872 | tf_op jit(solution)/shard_map/features_z/ppermute | solution.py:450
  5.0 15.1 %collective-permute-start.3 = (bf16[512,512]{1,0:T(8,128)(2,1)S(1)}, bf16[512,512]{1,0:T(8,128)(2,1)S(1)}, u32[]{:S(2)}, u32[]{:S(2)}) collective-permute-start(bf16[512,512]{1,0:T(8,128)(2,1)S(1)} %constant_dynamic-slice_fusion.refs_2_), channel_id=1, source_target_pairs={{0,2},{1,3},{2,0},{3,1},{4,6},{5,7},{6,4},{7,5},{8,10},{9,11},{10,... | collective-permute-start | bytes 1572872 | tf_op jit(solution)/shard_map/features_xy/ppermute | solution.py:450
  6.5 13.6 %collective-permute-start.4 = (bf16[512,512]{1,0:T(8,128)(2,1)S(1)}, bf16[512,512]{1,0:T(8,128)(2,1)S(1)}, u32[]{:S(2)}, u32[]{:S(2)}) collective-permute-start(bf16[512,512]{1,0:T(8,128)(2,1)S(1)} %constant_dynamic-slice_fusion.refs_2_), channel_id=1, source_target_pairs={{0,4},{1,5},{2,6},{3,7},{4,0},{5,1},{6,2},{7,3},{8,12},{9,13},{10,... | collective-permute-start | bytes 1572872 | tf_op jit(solution)/shard_map/features_xy/ppermute | solution.py:450
  9.5 7.4 %collective-permute-start.1 = (s32[8,25]{1,0:T(8,128)S(1)}, s32[8,25]{1,0:T(8,128)S(1)}, u32[]{:S(2)}, u32[]{:S(2)}) collective-permute-start(s32[8,25]{1,0:T(8,128)S(1)} %pad_add_fusion.packed_ref), channel_id=1, source_target_pairs={{0,1},{1,0},{2,3},{3,2},{4,5},{5,4},{6,7},{7,6},{8,9},{9,8},{10,11... | collective-permute-start | bytes 2408 | tf_op jit(solution)/shard_map/tiles_exchange/ppermute | solution.py:450
  16.9 14.3 %collective-permute-start.5 = (bf16[512,512]{1,0:T(8,128)(2,1)S(1)}, bf16[512,512]{1,0:T(8,128)(2,1)S(1)}, u32[]{:S(2)}, u32[]{:S(2)}) collective-permute-start(bf16[512,512]{1,0:T(8,128)(2,1)S(1)} %collective-permute-done.2.refs_5_), channel_id=1, source_target_pairs={{0,2},{1,3},{2,0},{3,1},{4,6},{5,7},{6,4},{7,5},{8,10},{9,11},{10,... | collective-permute-start | bytes 1572872 | tf_op jit(solution)/shard_map/features_xy/ppermute | solution.py:450
  18.6 12.9 %collective-permute-start.6 = (bf16[512,512]{1,0:T(8,128)(2,1)S(1)}, bf16[512,512]{1,0:T(8,128)(2,1)S(1)}, u32[]{:S(2)}, u32[]{:S(2)}) collective-permute-start(bf16[512,512]{1,0:T(8,128)(2,1)S(1)} %collective-permute-done.2.refs_5_), channel_id=1, source_target_pairs={{0,4},{1,5},{2,6},{3,7},{4,0},{5,1},{6,2},{7,3},{8,12},{9,13},{10,... | collective-permute-start | bytes 1572872 | tf_op jit(solution)/shard_map/features_xy/ppermute | solution.py:450
  31.4 11.1 %collective-permute-start.7 = (bf16[512,512]{1,0:T(8,128)(2,1)}, bf16[512,512]{1,0:T(8,128)(2,1)}, u32[]{:S(2)}, u32[]{:S(2)}) collective-permute-start(bf16[512,512]{1,0:T(8,128)(2,1)} %param.14), channel_id=1, source_target_pairs={{0,1},{1,0},{2,3},{3,2},{4,5},{5,4},{6,7},{7,6},{8,9},{9,8},{10,11... | collective-permute-start | bytes 1572872 | tf_op jit(solution)/shard_map/cotangents/ppermute | solution.py:450
  31.4 26.6 %collective-permute-start.8 = (bf16[512,512]{1,0:T(8,128)(2,1)S(1)}, bf16[512,512]{1,0:T(8,128)(2,1)}, u32[]{:S(2)}, u32[]{:S(2)}) collective-permute-start(bf16[512,512]{1,0:T(8,128)(2,1)S(1)} %constant_dynamic-slice_fusion.refs_2_), channel_id=1, source_target_pairs={{0,16},{1,17},{2,18},{3,19},{4,20},{5,21},{6,22},{7,23},{8,24},{9,... | collective-permute-start | bytes 1572872 | tf_op jit(solution)/shard_map/features_z/ppermute | solution.py:450
  34.1 23.9 %collective-permute-start.10 = (bf16[512,512]{1,0:T(8,128)(2,1)S(1)}, bf16[512,512]{1,0:T(8,128)(2,1)}, u32[]{:S(2)}, u32[]{:S(2)}) collective-permute-start(bf16[512,512]{1,0:T(8,128)(2,1)S(1)} %collective-permute-done.6.refs_7_), channel_id=1, source_target_pairs={{0,2},{1,3},{2,0},{3,1},{4,6},{5,7},{6,4},{7,5},{8,10},{9,11},{10,... | collective-permute-start | bytes 1572872 | tf_op jit(solution)/shard_map/features_xy/ppermute | solution.py:450
  35.8 22.3 %collective-permute-start.9 = (bf16[512,512]{1,0:T(8,128)(2,1)S(1)}, bf16[512,512]{1,0:T(8,128)(2,1)}, u32[]{:S(2)}, u32[]{:S(2)}) collective-permute-start(bf16[512,512]{1,0:T(8,128)(2,1)S(1)} %collective-permute-done.3.refs_3_), channel_id=1, source_target_pairs={{0,4},{1,5},{2,6},{3,7},{4,0},{5,1},{6,2},{7,3},{8,12},{9,13},{10,... | collective-permute-start | bytes 1572872 | tf_op jit(solution)/shard_map/features_xy/ppermute | solution.py:450
  58.1 14.0 %collective-permute-start.11 = (bf16[512,512]{1,0:T(8,128)(2,1)}, bf16[512,512]{1,0:T(8,128)(2,1)S(1)}, u32[]{:S(2)}, u32[]{:S(2)}) collective-permute-start(bf16[512,512]{1,0:T(8,128)(2,1)} %collective-permute-done.8.refs_10_), channel_id=1, source_target_pairs={{0,2},{1,3},{2,0},{3,1},{4,6},{5,7},{6,4},{7,5},{8,10},{9,11},{10,... | collective-permute-start | bytes 1572872 | tf_op jit(solution)/shard_map/features_xy/ppermute | solution.py:450
  59.6 13.8 %collective-permute-start.12 = (bf16[512,512]{1,0:T(8,128)(2,1)}, bf16[512,512]{1,0:T(8,128)(2,1)S(1)}, u32[]{:S(2)}, u32[]{:S(2)}) collective-permute-start(bf16[512,512]{1,0:T(8,128)(2,1)} %collective-permute-done.8.refs_10_), channel_id=1, source_target_pairs={{0,4},{1,5},{2,6},{3,7},{4,0},{5,1},{6,2},{7,3},{8,12},{9,13},{10,... | collective-permute-start | bytes 1572872 | tf_op jit(solution)/shard_map/features_xy/ppermute | solution.py:450
  60.1 13.4 %collective-permute-start.13 = (bf16[512,512]{1,0:T(8,128)(2,1)}, bf16[512,512]{1,0:T(8,128)(2,1)S(1)}, u32[]{:S(2)}, u32[]{:S(2)}) collective-permute-start(bf16[512,512]{1,0:T(8,128)(2,1)} %collective-permute-done.8.refs_10_), channel_id=1, source_target_pairs={{0,8},{1,9},{2,10},{3,11},{4,12},{5,13},{6,14},{7,15},{8,0},{9,1},... | collective-permute-start | bytes 1572872 | tf_op jit(solution)/shard_map/features_z/ppermute | solution.py:450
  73.5 12.8 %collective-permute-start.14 = (bf16[512,512]{1,0:T(8,128)(2,1)S(1)}, bf16[512,512]{1,0:T(8,128)(2,1)S(1)}, u32[]{:S(2)}, u32[]{:S(2)}) collective-permute-start(bf16[512,512]{1,0:T(8,128)(2,1)S(1)} %collective-permute-done.12.refs_2_), channel_id=1, source_target_pairs={{0,2},{1,3},{2,0},{3,1},{4,6},{5,7},{6,4},{7,5},{8,10},{9,11},{10,... | collective-permute-start | bytes 1572872 | tf_op jit(solution)/shard_map/features_xy/ppermute | solution.py:450
  74.4 12.1 %collective-permute-start.15 = (bf16[512,512]{1,0:T(8,128)(2,1)S(1)}, bf16[512,512]{1,0:T(8,128)(2,1)S(1)}, u32[]{:S(2)}, u32[]{:S(2)}) collective-permute-start(bf16[512,512]{1,0:T(8,128)(2,1)S(1)} %collective-permute-done.13.refs_3_), channel_id=1, source_target_pairs={{0,4},{1,5},{2,6},{3,7},{4,0},{5,1},{6,2},{7,3},{8,12},{9,13},{10,... | collective-permute-start | bytes 1572872 | tf_op jit(solution)/shard_map/features_xy/ppermute | solution.py:450
  75.6 11.8 %collective-permute-start.16 = (bf16[512,512]{1,0:T(8,128)(2,1)S(1)}, bf16[512,512]{1,0:T(8,128)(2,1)S(1)}, u32[]{:S(2)}, u32[]{:S(2)}) collective-permute-start(bf16[512,512]{1,0:T(8,128)(2,1)S(1)} %collective-permute-done.11.refs_11_), channel_id=1, source_target_pairs={{0,8},{1,9},{2,10},{3,11},{4,12},{5,13},{6,14},{7,15},{8,0},{9,1},... | collective-permute-start | bytes 1572872 | tf_op jit(solution)/shard_map/features_z/ppermute | solution.py:450
  87.4 7.4 %collective-permute-start.17 = (bf16[256,512]{1,0:T(8,128)(2,1)S(1)}, bf16[256,512]{1,0:T(8,128)(2,1)S(1)}, u32[]{:S(2)}, u32[]{:S(2)}) collective-permute-start(bf16[256,512]{1,0:T(8,128)(2,1)S(1)} %slice.42), channel_id=1, source_target_pairs={{0,2},{1,3},{2,0},{3,1},{4,6},{5,7},{6,4},{7,5},{8,10},{9,11},{10,... | collective-permute-start | bytes 786440 | tf_op jit(solution)/shard_map/features_xy/ppermute | solution.py:450
  89.2 6.4 %collective-permute-start.18 = (bf16[256,512]{1,0:T(8,128)(2,1)S(1)}, bf16[256,512]{1,0:T(8,128)(2,1)S(1)}, u32[]{:S(2)}, u32[]{:S(2)}) collective-permute-start(bf16[256,512]{1,0:T(8,128)(2,1)S(1)} %slice.43), channel_id=1, source_target_pairs={{0,4},{1,5},{2,6},{3,7},{4,0},{5,1},{6,2},{7,3},{8,12},{9,13},{10,... | collective-permute-start | bytes 786440 | tf_op jit(solution)/shard_map/features_xy/ppermute | solution.py:450
  94.8 7.1 %copy-start.2 = (bf16[512,512]{1,0:T(8,128)(2,1)S(1)}, bf16[512,512]{1,0:T(8,128)(2,1)}, u32[]{:S(2)}) copy-start(bf16[512,512]{1,0:T(8,128)(2,1)} %weight_ref.3) | copy-start | bytes 1572868
  99.2 2.7 %collective-permute-start.19 = (bf16[1024,512]{1,0:T(8,128)(2,1)S(1)}, bf16[1024,512]{1,0:T(8,128)(2,1)S(1)}, u32[]{:S(2)}, u32[]{:S(2)}) collective-permute-start(bf16[1024,512]{1,0:T(8,128)(2,1)S(1)} %forward.5.mine_ref), channel_id=1, source_target_pairs={{0,1},{1,0},{2,3},{3,2},{4,5},{5,4},{6,7},{7,6},{8,9},{9,8},{10,11... | collective-permute-start | bytes 3145736 | tf_op jit(solution)/shard_map/partial_sums/ppermute | solution.py:450
  108.4 10.4 %collective-permute-start.20 = (bf16[64,512]{1,0:T(8,128)(2,1)S(1)}, bf16[64,512]{1,0:T(8,128)(2,1)S(1)}, u32[]{:S(2)}, u32[]{:S(2)}) collective-permute-start(bf16[64,512]{1,0:T(8,128)(2,1)S(1)} %get-tuple-element.307), channel_id=1, source_target_pairs={{0,8},{1,9},{2,10},{3,11},{4,12},{5,13},{6,14},{7,15},{8,0},{9,1},... | collective-permute-start | bytes 196616 | tf_op jit(solution)/shard_map/weight_grad/ppermute | solution.py:450
  109.1 11.1 %collective-permute-start.21 = (bf16[64,512]{1,0:T(8,128)(2,1)S(1)}, bf16[64,512]{1,0:T(8,128)(2,1)S(1)}, u32[]{:S(2)}, u32[]{:S(2)}) collective-permute-start(bf16[64,512]{1,0:T(8,128)(2,1)S(1)} %get-tuple-element.309), channel_id=1, source_target_pairs={{0,16},{1,17},{2,18},{3,19},{4,20},{5,21},{6,22},{7,23},{8,24},{9,... | collective-permute-start | bytes 196616 | tf_op jit(solution)/shard_map/weight_grad/ppermute | solution.py:450
  111.2 9.0 %collective-permute-start.22 = (bf16[64,512]{1,0:T(8,128)(2,1)S(1)}, bf16[64,512]{1,0:T(8,128)(2,1)S(1)}, u32[]{:S(2)}, u32[]{:S(2)}) collective-permute-start(bf16[64,512]{1,0:T(8,128)(2,1)S(1)} %get-tuple-element.308), channel_id=1, source_target_pairs={{0,24},{1,25},{2,26},{3,27},{4,28},{5,29},{6,30},{7,31},{8,16},{9,... | collective-permute-start | bytes 196616 | tf_op jit(solution)/shard_map/weight_grad/ppermute | solution.py:450
  112.9 7.5 %collective-permute-start.23 = (bf16[256,512]{1,0:T(8,128)(2,1)S(1)}, bf16[256,512]{1,0:T(8,128)(2,1)S(1)}, u32[]{:S(2)}, u32[]{:S(2)}) collective-permute-start(bf16[256,512]{1,0:T(8,128)(2,1)S(1)} %get-tuple-element.218), channel_id=1, source_target_pairs={{0,2},{1,3},{2,0},{3,1},{4,6},{5,7},{6,4},{7,5},{8,10},{9,11},{10,... | collective-permute-start | bytes 786440 | tf_op jit(solution)/shard_map/grads_xy/ppermute | solution.py:450
  113.1 7.2 %collective-permute-start.24 = (bf16[256,512]{1,0:T(8,128)(2,1)S(1)}, bf16[256,512]{1,0:T(8,128)(2,1)S(1)}, u32[]{:S(2)}, u32[]{:S(2)}) collective-permute-start(bf16[256,512]{1,0:T(8,128)(2,1)S(1)} %get-tuple-element.219), channel_id=1, source_target_pairs={{0,4},{1,5},{2,6},{3,7},{4,0},{5,1},{6,2},{7,3},{8,12},{9,13},{10,... | collective-permute-start | bytes 786440 | tf_op jit(solution)/shard_map/grads_xy/ppermute | solution.py:450
  118.8 14.3 %collective-permute-start.26 = (bf16[512,512]{1,0:T(8,128)(2,1)S(1)}, bf16[512,512]{1,0:T(8,128)(2,1)S(1)}, u32[]{:S(2)}, u32[]{:S(2)}) collective-permute-start(bf16[512,512]{1,0:T(8,128)(2,1)S(1)} %get-tuple-element.230), channel_id=1, source_target_pairs={{0,2},{1,3},{2,0},{3,1},{4,6},{5,7},{6,4},{7,5},{8,10},{9,11},{10,... | collective-permute-start | bytes 1572872 | tf_op jit(solution)/shard_map/grads_xy/ppermute | solution.py:450
  120.5 12.6 %collective-permute-start.27 = (bf16[512,512]{1,0:T(8,128)(2,1)S(1)}, bf16[512,512]{1,0:T(8,128)(2,1)S(1)}, u32[]{:S(2)}, u32[]{:S(2)}) collective-permute-start(bf16[512,512]{1,0:T(8,128)(2,1)S(1)} %get-tuple-element.235), channel_id=1, source_target_pairs={{0,4},{1,5},{2,6},{3,7},{4,0},{5,1},{6,2},{7,3},{8,12},{9,13},{10,... | collective-permute-start | bytes 1572872 | tf_op jit(solution)/shard_map/grads_xy/ppermute | solution.py:450
  121.9 12.0 %collective-permute-start.28 = (bf16[512,512]{1,0:T(8,128)(2,1)S(1)}, bf16[512,512]{1,0:T(8,128)(2,1)S(1)}, u32[]{:S(2)}, u32[]{:S(2)}) collective-permute-start(bf16[512,512]{1,0:T(8,128)(2,1)S(1)} %get-tuple-element.236), channel_id=1, source_target_pairs={{0,8},{1,9},{2,10},{3,11},{4,12},{5,13},{6,14},{7,15},{8,0},{9,1},... | collective-permute-start | bytes 1572872 | tf_op jit(solution)/shard_map/grads_z/ppermute | solution.py:450
  127.9 5.2 %collective-permute-start.25 = (bf16[64,512]{1,0:T(8,128)(2,1)S(1)}, bf16[64,512]{1,0:T(8,128)(2,1)S(1)}, u32[]{:S(2)}, u32[]{:S(2)}) collective-permute-start(bf16[64,512]{1,0:T(8,128)(2,1)S(1)} %fusion.2), channel_id=1, source_target_pairs={{0,2},{1,3},{2,0},{3,1},{4,6},{5,7},{6,4},{7,5},{8,10},{9,11},{10,... | collective-permute-start | bytes 196616 | tf_op jit(solution)/shard_map/weight_grad/ppermute | solution.py:450
  134.0 16.5 %collective-permute-start.32 = (bf16[512,512]{1,0:T(8,128)(2,1)S(1)}, bf16[512,512]{1,0:T(8,128)(2,1)S(1)}, u32[]{:S(2)}, u32[]{:S(2)}) collective-permute-start(bf16[512,512]{1,0:T(8,128)(2,1)S(1)} %add_convert_fusion.3), channel_id=1, source_target_pairs={{0,8},{1,9},{2,10},{3,11},{4,12},{5,13},{6,14},{7,15},{8,0},{9,1},... | collective-permute-start | bytes 1572872 | tf_op jit(solution)/shard_map/grads_z/ppermute | solution.py:450
  134.7 15.9 %collective-permute-start.31 = (bf16[512,512]{1,0:T(8,128)(2,1)S(1)}, bf16[512,512]{1,0:T(8,128)(2,1)S(1)}, u32[]{:S(2)}, u32[]{:S(2)}) collective-permute-start(bf16[512,512]{1,0:T(8,128)(2,1)S(1)} %add_convert_fusion.4), channel_id=1, source_target_pairs={{0,4},{1,5},{2,6},{3,7},{4,0},{5,1},{6,2},{7,3},{8,12},{9,13},{10,... | collective-permute-start | bytes 1572872 | tf_op jit(solution)/shard_map/grads_xy/ppermute | solution.py:450
  135.5 15.1 %collective-permute-start.30 = (bf16[512,512]{1,0:T(8,128)(2,1)S(1)}, bf16[512,512]{1,0:T(8,128)(2,1)S(1)}, u32[]{:S(2)}, u32[]{:S(2)}) collective-permute-start(bf16[512,512]{1,0:T(8,128)(2,1)S(1)} %add_convert_fusion.5), channel_id=1, source_target_pairs={{0,2},{1,3},{2,0},{3,1},{4,6},{5,7},{6,4},{7,5},{8,10},{9,11},{10,... | collective-permute-start | bytes 1572872 | tf_op jit(solution)/shard_map/grads_xy/ppermute | solution.py:450
  143.6 6.4 %collective-permute-start.29 = (bf16[64,512]{1,0:T(8,128)(2,1)S(1)}, bf16[64,512]{1,0:T(8,128)(2,1)S(1)}, u32[]{:S(2)}, u32[]{:S(2)}) collective-permute-start(bf16[64,512]{1,0:T(8,128)(2,1)S(1)} %add_convert_fusion.9), channel_id=1, source_target_pairs={{0,4},{1,5},{2,6},{3,7},{4,0},{5,1},{6,2},{7,3},{8,12},{9,13},{10,... | collective-permute-start | bytes 196616 | tf_op jit(solution)/shard_map/weight_grad/ppermute | solution.py:450
  144.4 19.9 %collective-permute-start.34 = (bf16[512,512]{1,0:T(8,128)(2,1)S(1)}, bf16[512,512]{1,0:T(8,128)(2,1)S(1)}, u32[]{:S(2)}, u32[]{:S(2)}) collective-permute-start(bf16[512,512]{1,0:T(8,128)(2,1)S(1)} %get-tuple-element.264), channel_id=1, source_target_pairs={{0,4},{1,5},{2,6},{3,7},{4,0},{5,1},{6,2},{7,3},{8,12},{9,13},{10,... | collective-permute-start | bytes 1572872 | tf_op jit(solution)/shard_map/grads_xy/ppermute | solution.py:450
  150.0 14.3 %collective-permute-start.35 = (bf16[512,512]{1,0:T(8,128)(2,1)S(1)}, bf16[512,512]{1,0:T(8,128)(2,1)S(1)}, u32[]{:S(2)}, u32[]{:S(2)}) collective-permute-start(bf16[512,512]{1,0:T(8,128)(2,1)S(1)} %get-tuple-element.265), channel_id=1, source_target_pairs={{0,2},{1,3},{2,0},{3,1},{4,6},{5,7},{6,4},{7,5},{8,10},{9,11},{10,... | collective-permute-start | bytes 1572872 | tf_op jit(solution)/shard_map/grads_xy/ppermute | solution.py:450
  150.9 13.4 %collective-permute-start.36 = (bf16[256,512]{1,0:T(8,128)(2,1)S(1)}, bf16[256,512]{1,0:T(8,128)(2,1)S(1)}, u32[]{:S(2)}, u32[]{:S(2)}) collective-permute-start(bf16[256,512]{1,0:T(8,128)(2,1)S(1)} %get-tuple-element.304), channel_id=1, source_target_pairs={{0,16},{1,17},{2,18},{3,19},{4,20},{5,21},{6,22},{7,23},{8,24},{9,... | collective-permute-start | bytes 786440 | tf_op jit(solution)/shard_map/grads_z/ppermute | solution.py:450
  158.4 5.8 %collective-permute-start.33 = (bf16[1,64,512]{2,1,0:T(8,128)(2,1)S(1)}, bf16[1,64,512]{2,1,0:T(8,128)(2,1)S(1)}, u32[]{:S(2)}, u32[]{:S(2)}) collective-permute-start(bf16[1,64,512]{2,1,0:T(8,128)(2,1)S(1)} %bitcast.19), channel_id=1, source_target_pairs={{0,16},{1,17},{2,18},{3,19},{4,20},{5,21},{6,22},{7,23},{8,24},{9,... | collective-permute-start | bytes 196616 | tf_op jit(solution)/shard_map/weight_grad/ppermute | solution.py:450
  158.5 18.8 %collective-permute-start.40 = (bf16[512,512]{1,0:T(8,128)(2,1)S(1)}, bf16[512,512]{1,0:T(8,128)(2,1)S(1)}, u32[]{:S(2)}, u32[]{:S(2)}) collective-permute-start(bf16[512,512]{1,0:T(8,128)(2,1)S(1)} %get-tuple-element.281), channel_id=1, source_target_pairs={{0,4},{1,5},{2,6},{3,7},{4,0},{5,1},{6,2},{7,3},{8,12},{9,13},{10,... | collective-permute-start | bytes 1572872 | tf_op jit(solution)/shard_map/grads_xy/ppermute | solution.py:450
  164.4 14.9 %collective-permute-start.39 = (bf16[512,512]{1,0:T(8,128)(2,1)S(1)}, bf16[512,512]{1,0:T(8,128)(2,1)S(1)}, u32[]{:S(2)}, u32[]{:S(2)}) collective-permute-start(bf16[512,512]{1,0:T(8,128)(2,1)S(1)} %add_convert_fusion.2), channel_id=1, source_target_pairs={{0,2},{1,3},{2,0},{3,1},{4,6},{5,7},{6,4},{7,5},{8,10},{9,11},{10,... | collective-permute-start | bytes 1572872 | tf_op jit(solution)/shard_map/grads_xy/ppermute | solution.py:450
  166.1 6.8 %collective-permute-start.37 = (bf16[2,64,512]{2,1,0:T(8,128)(2,1)S(1)}, bf16[2,64,512]{2,1,0:T(8,128)(2,1)S(1)}, u32[]{:S(2)}, u32[]{:S(2)}) collective-permute-start(bf16[2,64,512]{2,1,0:T(8,128)(2,1)S(1)} %pad_maximum_fusion.2), channel_id=1, source_target_pairs={{0,8},{1,9},{2,10},{3,11},{4,12},{5,13},{6,14},{7,15},{8,0},{9,1},... | collective-permute-start | bytes 393224 | tf_op jit(solution)/shard_map/weight_grad/ppermute | solution.py:450
  166.3 11.1 %collective-permute-start.38 = (bf16[256,512]{1,0:T(8,128)(2,1)S(1)}, bf16[256,512]{1,0:T(8,128)(2,1)S(1)}, u32[]{:S(2)}, u32[]{:S(2)}) collective-permute-start(bf16[256,512]{1,0:T(8,128)(2,1)S(1)} %get-tuple-element.277), channel_id=1, source_target_pairs={{0,16},{1,17},{2,18},{3,19},{4,20},{5,21},{6,22},{7,23},{8,24},{9,... | collective-permute-start | bytes 786440 | tf_op jit(solution)/shard_map/grads_z/ppermute | solution.py:450
  168.2 13.3 %collective-permute-start.42 = (bf16[512,512]{1,0:T(8,128)(2,1)S(1)}, bf16[512,512]{1,0:T(8,128)(2,1)S(1)}, u32[]{:S(2)}, u32[]{:S(2)}) collective-permute-start(bf16[512,512]{1,0:T(8,128)(2,1)S(1)} %add_convert_fusion.1), channel_id=1, source_target_pairs={{0,4},{1,5},{2,6},{3,7},{4,0},{5,1},{6,2},{7,3},{8,12},{9,13},{10,... | collective-permute-start | bytes 1572872 | tf_op jit(solution)/shard_map/grads_xy/ppermute | solution.py:450
  172.9 13.7 %collective-permute-start.41 = (bf16[512,512]{1,0:T(8,128)(2,1)S(1)}, bf16[512,512]{1,0:T(8,128)(2,1)S(1)}, u32[]{:S(2)}, u32[]{:S(2)}) collective-permute-start(bf16[512,512]{1,0:T(8,128)(2,1)S(1)} %get-tuple-element.285), channel_id=1, source_target_pairs={{0,2},{1,3},{2,0},{3,1},{4,6},{5,7},{6,4},{7,5},{8,10},{9,11},{10,... | collective-permute-start | bytes 1572872 | tf_op jit(solution)/shard_map/grads_xy/ppermute | solution.py:450
  179.3 12.3 %copy-start.1 = (bf16[1024,512]{1,0:T(8,128)(2,1)S(1)}, bf16[1024,512]{1,0:T(8,128)(2,1)}, u32[]{:S(2)}) copy-start(bf16[1024,512]{1,0:T(8,128)(2,1)} %param.8) | copy-start | bytes 3145732
  179.5 10.0 %collective-permute-start.43 = (bf16[512,512]{1,0:T(8,128)(2,1)S(1)}, bf16[512,512]{1,0:T(8,128)(2,1)S(1)}, u32[]{:S(2)}, u32[]{:S(2)}) collective-permute-start(bf16[512,512]{1,0:T(8,128)(2,1)S(1)} %add_convert_fusion), channel_id=1, source_target_pairs={{0,8},{1,9},{2,10},{3,11},{4,12},{5,13},{6,14},{7,15},{8,0},{9,1},... | collective-permute-start | bytes 1572872 | tf_op jit(solution)/shard_map/grads_z/ppermute | solution.py:450
  179.6 6.9 %collective-permute-start.44 = (bf16[4,64,512]{2,1,0:T(8,128)(2,1)S(1)}, bf16[4,64,512]{2,1,0:T(8,128)(2,1)S(1)}, u32[]{:S(2)}, u32[]{:S(2)}) collective-permute-start(bf16[4,64,512]{2,1,0:T(8,128)(2,1)S(1)} %pad_maximum_fusion.1.refs_6_), channel_id=1, source_target_pairs={{0,1},{1,0},{2,3},{3,2},{4,5},{5,4},{6,7},{7,6},{8,9},{9,8},{10,11... | collective-permute-start | bytes 786440 | tf_op jit(solution)/shard_map/weight_grad/ppermute | solution.py:450

commit v16 on v15

--- a/solution.py
+++ b/solution.py
@@ -509,7 +509,6 @@
         with jax.named_scope("other_blocks"):
             return [make_other(first, where, *sent, block_rows, n_rep) for sent in live["tiles"]]
 
-    live["cot"] = cotangent
     live[0] = lax.dynamic_slice_in_dim(features, rep * part, part, axis=0)
     with jax.named_scope("tiles_exchange"):
         live["tiles"] = [
@@ -561,7 +560,7 @@
             live["units"] = units
             build_own(panels // 2)
             with jax.named_scope("cotangents"):
-                live["cot"] = gather_rep(live["cot"])
+                live["cot"] = gather_rep(cotangent)
         else:
             with jax.named_scope(FEATURES_ACROSS):
                 odd_xy = [flip(live["odd_y"][:half], X), flip(live["odd_x"][half:], Y)]

time: 193 us -> 181 us (0.938)
  waiting for transfers between devices: 65.5 us -> 52.4 us
    ppermute x45, waiting for transfers between devices: 65.5 us -> 52.4 us  [flip(): return lax.ppermute(value, BOTH, pairs)]
  transfers between devices with their start and end apart: 45 -> 45, of which waited for: 20 -> 23; matrix products, arithmetic and copies ran while one was open for 3% -> 3% of each run, Pallas kernels for 32% -> 34%
where the time goes in v16:
time: 181 us; the launch traced here: 180 us
  Pallas kernels  73.7 us (41%)
  waiting for transfers between devices  52.4 us (29%)
  starting transfers between devices  47 us (26%)
  other arithmetic  4.16 us (2%)
    ppermute x45, waiting for transfers between devices, flip(): return lax.ppermute(value, BOTH, pairs)  52.4 us
    ppermute x45, starting transfers between devices, flip(): return lax.ppermute(value, BOTH, pairs)  47 us
    pallas_call x4, Pallas kernels, backward_part(): pl.pallas_call(backward_kernel, out_shape=[jax.ShapeDtypeStruct((width, c...  21.4 us
    pallas_call x3, Pallas kernels, forward_part(): pl.pallas_call(functools.partial(forward_kernel, offset, n_pieces, n_othe...  17.9 us
    pallas_call x2, Pallas kernels, make_dense(): pl.pallas_call(functools.partial(dense_kernel, first), out_shape=pltpu.HB...  13.1 us
    pallas_call x2, Pallas kernels, make_other(): pl.pallas_call(functools.partial(other_kernel, first), out_shape=pltpu.HB...  10.8 us
    pallas_call x1, Pallas kernels, middle(): pl.pallas_call(functools.partial(middle_kernel, blocks), out_shape=[jax.S...  6.49 us
  transfers between devices with their start and end apart: 45, of which 23 were waited for; matrix products, arithmetic and copies ran while one was open for 3% of the time, Pallas kernels for 34%

profile of v16, /device:TPU:0, one launch (start us, length us, event | category | flops | bytes accessed | tf_op | source)
XLA Modules:
  0.0 179.7 jit_solution(15747479647708712179)
XLA Ops:
  1.2 0.7 copy-done
  1.9 3.1 %collective-permute-start.2 = (bf16[512,512]{1,0:T(8,128)(2,1)S(1)}, bf16[512,512]{1,0:T(8,128)(2,1)S(1)}, u32[]{:S(2)}, u32[]{:S(2)}) collective-permute-start(bf16[512,512]{1,0:T(8,128)(2,1)S(1)} %constant_dynamic-slice_fusion.refs_2_), channel_id=1, source_target_pairs={{0,8},{1,9},{2,10},{3,11},{4,12},{5,13},{6,14},{7,15},{8,0},{9,1},... | collective-permute-start | bytes 1572872 | tf_op jit(solution)/shard_map/features_z/ppermute | solution.py:450
  5.0 1.5 collective-permute-start.3
  6.5 1.5 collective-permute-start.4
  8.0 0.7 add_bitcast_fusion
  8.7 0.7 copy.12
  9.5 0.7 broadcast_xor_fusion
  10.3 6.4 %dense_blocks.2.refs_0_ = bf16[2,8,1024,512]{3,2,1,0:T(8,128)(2,1)} custom-call(s32[44]{0:T(128)S(1)} %pad_add_fusion.1.where_ref, s32[8,25]{1,0:T(8,128)S(1)} %pad_add_fusion.packed_ref, bf16[8,24,128,128]{3,2,1,0:T(8,128)(2,1)} %bitcast.17), custom_call_target="tpu_custom_call" | custom-call | bytes 393216 | tf_op jit(solution)/shard_map/dense_blocks/pallas_call | solution.py:49
  16.9 1.7 collective-permute-start.5
  18.6 1.5 collective-permute-start.6
  20.1 2.6 %collective-permute-start.7 = (bf16[512,512]{1,0:T(8,128)(2,1)S(1)}, bf16[512,512]{1,0:T(8,128)(2,1)}, u32[]{:S(2)}, u32[]{:S(2)}) collective-permute-start(bf16[512,512]{1,0:T(8,128)(2,1)S(1)} %constant_dynamic-slice_fusion.refs_2_), channel_id=1, source_target_pairs={{0,16},{1,17},{2,18},{3,19},{4,20},{5,21},{6,22},{7,23},{8,24},{9,... | collective-permute-start | bytes 1572872 | tf_op jit(solution)/shard_map/features_z/ppermute | solution.py:450
  22.7 8.5 %collective-permute-done.5.refs_6_ = bf16[512,512]{1,0:T(8,128)(2,1)S(1)} collective-permute-done((bf16[512,512]{1,0:T(8,128)(2,1)S(1)}, bf16[512,512]{1,0:T(8,128)(2,1)S(1)}, u32[]{:S(2)}, u32[]{:S(2)}) %collective-permute-start.5) | collective-permute-done | bytes 524320 | tf_op jit(solution)/shard_map/features_xy/ppermute | solution.py:450
  31.4 1.2 collective-permute-start.8
  32.6 0.9 collective-permute-start.9
  33.5 1.3 broadcast_select_fusion.1
  34.9 6.6 %dense_blocks.3.dense_ref.a_ref = bf16[2,8,1024,512]{3,2,1,0:T(8,128)(2,1)} custom-call(s32[44]{0:T(128)S(1)} %pad_add_fusion.1.where_ref, s32[8,25]{1,0:T(8,128)S(1)} %pad_add_fusion.packed_ref, bf16[8,24,128,128]{3,2,1,0:T(8,128)(2,1)} %bitcast.18, bf16[2,8,1024,512]{3,2,1,0:T(8,128)(2,1)} %dense_blocks.2.refs_0_), custom_call_target="tpu_custom_call", output_to_operand_aliasing={{}: (3, {})} | custom-call | bytes 393216 | tf_op jit(solution)/shard_map/dense_blocks/pallas_call | solution.py:49
  41.5 5.1 %collective-permute-done.7.refs_10_ = bf16[512,512]{1,0:T(8,128)(2,1)} collective-permute-done((bf16[512,512]{1,0:T(8,128)(2,1)S(1)}, bf16[512,512]{1,0:T(8,128)(2,1)}, u32[]{:S(2)}, u32[]{:S(2)}) %collective-permute-start.7) | collective-permute-done | bytes 524320 | tf_op jit(solution)/shard_map/features_z/ppermute | solution.py:450
  47.2 0.9 collective-permute-start.12
  48.4 5.4 %other_blocks.3.refs_1_ = bf16[4,1024,512]{2,1,0:T(8,128)(2,1)} custom-call(s32[44]{0:T(128)S(1)} %pad_add_fusion.1.where_ref, s32[8,25]{1,0:T(8,128)S(1)} %collective-permute-done.1.packed_ref, bf16[8,24,128,128]{3,2,1,0:T(8,128)(2,1)} %collective-permute-done.tiles_ref), custom_call_target="tpu_custom_call" | custom-call | bytes 393216 | tf_op jit(solution)/shard_map/other_blocks/pallas_call | solution.py:93
  53.8 5.3 %other_blocks.2.refs_0_ = bf16[4,1024,512]{2,1,0:T(8,128)(2,1)} custom-call(s32[44]{0:T(128)S(1)} %pad_add_fusion.1.where_ref, s32[8,25]{1,0:T(8,128)S(1)} %collective-permute-done.1.packed_ref, bf16[8,24,128,128]{3,2,1,0:T(8,128)(2,1)} %collective-permute-done.tiles_ref), custom_call_target="tpu_custom_call" | custom-call | bytes 393216 | tf_op jit(solution)/shard_map/other_blocks/pallas_call | solution.py:93
  59.2 1.3 collective-permute-done.11.refs_11_
  60.8 1.6 collective-permute-start.14
  62.4 1.5 collective-permute-start.15
  63.9 0.9 collective-permute-start.16
  64.9 9.5 %forward.3.refs_6_ = f32[1024,512]{1,0:T(8,128)S(1)} custom-call(s32[44]{0:T(128)S(1)} %pad_add_fusion.1.where_ref, bf16[2,8,1024,512]{3,2,1,0:T(8,128)(2,1)} %dense_blocks.3.dense_ref.a_ref, bf16[4,1024,512]{2,1,0:T(8,128)(2,1)} %other_blocks.2.refs_0_, bf16[4,1024,512]{2,1,0:T(8,128)(2,1)} %other_blocks.3.refs_1_, ...), custom_call_target="tpu_custom_call" | custom-call | flops 5368709120 | bytes 14680064 | tf_op jit(solution)/shard_map/forward/pallas_call | solution.py:196
  74.4 1.0 collective-permute-done.16.refs_2_
  76.1 0.7 collective-permute-start.18
  76.8 4.9 %forward.4.refs_5_ = f32[1024,512]{1,0:T(8,128)S(1)} custom-call(s32[44]{0:T(128)S(1)} %pad_add_fusion.1.where_ref, bf16[2,8,1024,512]{3,2,1,0:T(8,128)(2,1)} %dense_blocks.3.dense_ref.a_ref, bf16[4,1024,512]{2,1,0:T(8,128)(2,1)} %other_blocks.2.refs_0_, bf16[4,1024,512]{2,1,0:T(8,128)(2,1)} %other_blocks.3.refs_1_, ...), custom_call_target="tpu_custom_call" | custom-call | flops 2147483648 | bytes 8388608 | tf_op jit(solution)/shard_map/forward/pallas_call | solution.py:196
  82.5 3.5 %forward.5.mine_ref = bf16[1024,512]{1,0:T(8,128)(2,1)S(1)} custom-call(s32[44]{0:T(128)S(1)} %pad_add_fusion.1.where_ref, bf16[2,8,1024,512]{3,2,1,0:T(8,128)(2,1)} %dense_blocks.3.dense_ref.a_ref, bf16[4,1024,512]{2,1,0:T(8,128)(2,1)} %other_blocks.2.refs_0_, bf16[4,1024,512]{2,1,0:T(8,128)(2,1)} %other_blocks.3.refs_1_, ...), custom_call_target="tpu_custom_call" | custom-call | flops 1073741824 | bytes 6291456 | tf_op jit(solution)/shard_map/forward/pallas_call | solution.py:196
  86.1 2.6 %collective-permute-done.19.other_ref = bf16[1024,512]{1,0:T(8,128)(2,1)S(1)} collective-permute-done((bf16[1024,512]{1,0:T(8,128)(2,1)S(1)}, bf16[1024,512]{1,0:T(8,128)(2,1)S(1)}, u32[]{:S(2)}, u32[]{:S(2)}) %collective-permute-start.19) | collective-permute-done | bytes 1048608 | tf_op jit(solution)/shard_map/partial_sums/ppermute | solution.py:450
  88.8 6.5 %middle.1 = (bf16[512,1024]{1,0:T(8,128)(2,1)S(1)}, bf16[256,512]{1,0:T(8,128)(2,1)S(1)}, bf16[256,512]{1,0:T(8,128)(2,1)S(1)}, bf16[4,64,512]{2,1,0:T(8,128)(2,1)S(1)}) custom-call(s32[44]{0:T(128)S(1)} %pad_add_fusion.1.where_ref, bf16[1024,512]{1,0:T(8,128)(2,1)S(1)} %forward.5.mine_ref, bf16[1024,512]{1,0:T(8,128)(2,1)S(1)} %collective-permute-done.19.other_ref, ...), custom_call_target="tpu_custom_call" | custom-call | flops 2684354560 | bytes 6291456 | tf_op jit(solution)/shard_map/middle/pallas_call | solution.py:281
  95.3 1.5 collective-permute-start.20
  96.8 3.3 %collective-permute-start.21 = (bf16[64,512]{1,0:T(8,128)(2,1)S(1)}, bf16[64,512]{1,0:T(8,128)(2,1)S(1)}, u32[]{:S(2)}, u32[]{:S(2)}) collective-permute-start(bf16[64,512]{1,0:T(8,128)(2,1)S(1)} %get-tuple-element.305), channel_id=1, source_target_pairs={{0,16},{1,17},{2,18},{3,19},{4,20},{5,21},{6,22},{7,23},{8,24},{9,... | collective-permute-start | bytes 196616 | tf_op jit(solution)/shard_map/weight_grad/ppermute | solution.py:450
  100.2 1.5 collective-permute-start.23
  102.2 4.6 %backward.4 = (bf16[512,512]{1,0:T(8,128)(2,1)S(1)}, bf16[512,512]{1,0:T(8,128)(2,1)S(1)}, bf16[512,512]{1,0:T(8,128)(2,1)S(1)}) custom-call(s32[44]{0:T(128)S(1)} %pad_add_fusion.1.where_ref, bf16[512,1024]{1,0:T(8,128)(2,1)S(1)} %get-tuple-element.253.grad_ref, bf16[2,8,1024,512]{3,2,1,0:T(8,128)(2,1)} %dense_blocks.3.dense_ref.a_ref), custom_call_target="tpu_custom_call" | custom-call | flops 1610612736 | bytes 5767168 | tf_op jit(solution)/shard_map/backward/pallas_call | solution.py:354
  106.9 0.6 collective-permute-start.26
  107.9 1.2 collective-permute-done.24.end_ref
  109.3 0.6 collective-permute-start.27
  110.5 5.5 %backward.5 = (bf16[512,512]{1,0:T(8,128)(2,1)S(1)}, bf16[512,512]{1,0:T(8,128)(2,1)S(1)}, bf16[512,512]{1,0:T(8,128)(2,1)S(1)}, bf16[512,512]{1,0:T(8,128)(2,1)S(1)}) custom-call(s32[44]{0:T(128)S(1)} %pad_add_fusion.1.where_ref, bf16[512,1024]{1,0:T(8,128)(2,1)S(1)} %get-tuple-element.253.grad_ref, bf16[2,8,1024,512]{3,2,1,0:T(8,128)(2,1)} %dense_blocks.3.dense_ref.a_ref), custom_call_target="tpu_custom_call" | custom-call | flops 2147483648 | bytes 7340032 | tf_op jit(solution)/shard_map/backward/pallas_call | solution.py:354
  116.0 0.8 collective-permute-start.25
  116.8 4.4 %collective-permute-done.25 = bf16[64,512]{1,0:T(8,128)(2,1)S(1)} collective-permute-done((bf16[64,512]{1,0:T(8,128)(2,1)S(1)}, bf16[64,512]{1,0:T(8,128)(2,1)S(1)}, u32[]{:S(2)}, u32[]{:S(2)}) %collective-permute-start.25) | collective-permute-done | bytes 65568 | tf_op jit(solution)/shard_map/weight_grad/ppermute | solution.py:450
  122.0 0.6 collective-permute-start.32
  122.8 1.5 collective-permute-start.31
  124.4 0.6 collective-permute-start.30
  125.1 6.7 %backward.6 = (bf16[512,512]{1,0:T(8,128)(2,1)S(1)}, bf16[512,512]{1,0:T(8,128)(2,1)S(1)}, bf16[512,512]{1,0:T(8,128)(2,1)S(1)}, bf16[512,512]{1,0:T(8,128)(2,1)S(1)}, bf16[512,512]{1,0:T(8,128)(2,1)S(1)}) custom-call(s32[44]{0:T(128)S(1)} %pad_add_fusion.1.where_ref, bf16[512,1024]{1,0:T(8,128)(2,1)S(1)} %get-tuple-element.253.grad_ref, ...), custom_call_target="tpu_custom_call" | custom-call | flops 2684354560 | bytes 8912896 | tf_op jit(solution)/shard_map/backward/pallas_call | solution.py:354
  131.8 1.2 collective-permute-start.29
  132.9 0.9 collective-permute-start.34
  133.9 4.2 %collective-permute-done.29 = bf16[64,512]{1,0:T(8,128)(2,1)S(1)} collective-permute-done((bf16[64,512]{1,0:T(8,128)(2,1)S(1)}, bf16[64,512]{1,0:T(8,128)(2,1)S(1)}, u32[]{:S(2)}, u32[]{:S(2)}) %collective-permute-start.29) | collective-permute-done | bytes 65568 | tf_op jit(solution)/shard_map/weight_grad/ppermute | solution.py:450
  138.0 1.0 collective-permute-start.35
  139.4 3.1 %collective-permute-start.36 = (bf16[256,512]{1,0:T(8,128)(2,1)S(1)}, bf16[256,512]{1,0:T(8,128)(2,1)S(1)}, u32[]{:S(2)}, u32[]{:S(2)}) collective-permute-start(bf16[256,512]{1,0:T(8,128)(2,1)S(1)} %get-tuple-element.300), channel_id=1, source_target_pairs={{0,16},{1,17},{2,18},{3,19},{4,20},{5,21},{6,22},{7,23},{8,24},{9,... | collective-permute-start | bytes 786440 | tf_op jit(solution)/shard_map/grads_z/ppermute | solution.py:450
  142.5 4.6 %backward.7 = (bf16[512,512]{1,0:T(8,128)(2,1)S(1)}, bf16[512,512]{1,0:T(8,128)(2,1)S(1)}, bf16[512,512]{1,0:T(8,128)(2,1)S(1)}) custom-call(s32[44]{0:T(128)S(1)} %pad_add_fusion.1.where_ref, bf16[512,1024]{1,0:T(8,128)(2,1)S(1)} %get-tuple-element.253.grad_ref, bf16[2,8,1024,512]{3,2,1,0:T(8,128)(2,1)} %dense_blocks.3.dense_ref.a_ref), custom_call_target="tpu_custom_call" | custom-call | flops 1610612736 | bytes 5767168 | tf_op jit(solution)/shard_map/backward/pallas_call | solution.py:354
  147.2 1.0 collective-permute-start.40
  148.2 4.8 %collective-permute-done.33 = bf16[1,64,512]{2,1,0:T(8,128)(2,1)S(1)} collective-permute-done((bf16[1,64,512]{2,1,0:T(8,128)(2,1)S(1)}, bf16[1,64,512]{2,1,0:T(8,128)(2,1)S(1)}, u32[]{:S(2)}, u32[]{:S(2)}) %collective-permute-start.33) | collective-permute-done | bytes 65568 | tf_op jit(solution)/shard_map/weight_grad/ppermute | solution.py:450
  153.2 1.0 collective-permute-start.39
  154.2 1.9 %collective-permute-start.38 = (bf16[256,512]{1,0:T(8,128)(2,1)S(1)}, bf16[256,512]{1,0:T(8,128)(2,1)S(1)}, u32[]{:S(2)}, u32[]{:S(2)}) collective-permute-start(bf16[256,512]{1,0:T(8,128)(2,1)S(1)} %get-tuple-element.273), channel_id=1, source_target_pairs={{0,16},{1,17},{2,18},{3,19},{4,20},{5,21},{6,22},{7,23},{8,24},{9,... | collective-permute-start | bytes 786440 | tf_op jit(solution)/shard_map/grads_z/ppermute | solution.py:450
  156.3 1.6 collective-permute-start.42
  157.8 3.1 %collective-permute-done.37 = bf16[2,64,512]{2,1,0:T(8,128)(2,1)S(1)} collective-permute-done((bf16[2,64,512]{2,1,0:T(8,128)(2,1)S(1)}, bf16[2,64,512]{2,1,0:T(8,128)(2,1)S(1)}, u32[]{:S(2)}, u32[]{:S(2)}) %collective-permute-start.37) | collective-permute-done | bytes 131104 | tf_op jit(solution)/shard_map/weight_grad/ppermute | solution.py:450
  161.0 1.1 collective-permute-start.41
  162.1 3.3 %collective-permute-done.38.refs_5_ = bf16[256,512]{1,0:T(8,128)(2,1)S(1)} collective-permute-done((bf16[256,512]{1,0:T(8,128)(2,1)S(1)}, bf16[256,512]{1,0:T(8,128)(2,1)S(1)}, u32[]{:S(2)}, u32[]{:S(2)}) %collective-permute-start.38) | collective-permute-done | bytes 262176 | tf_op jit(solution)/shard_map/grads_z/ppermute | solution.py:450
  165.4 2.7 %collective-permute-done.39 = bf16[512,512]{1,0:T(8,128)(2,1)S(1)} collective-permute-done((bf16[512,512]{1,0:T(8,128)(2,1)S(1)}, bf16[512,512]{1,0:T(8,128)(2,1)S(1)}, u32[]{:S(2)}, u32[]{:S(2)}) %collective-permute-start.39) | collective-permute-done | bytes 524320 | tf_op jit(solution)/shard_map/grads_xy/ppermute | solution.py:450
  168.5 1.9 %activated.1 = bf16[512,512]{1,0:T(8,128)(2,1)} custom-call(s32[44]{0:T(128)S(1)} %pad_add_fusion.1.where_ref, bf16[1024,512]{1,0:T(8,128)(2,1)S(1)} %forward.5.mine_ref, bf16[1024,512]{1,0:T(8,128)(2,1)S(1)} %collective-permute-done.19.other_ref, bf16[512,512]{1,0:T(8,128)(2,1)S(1)} %copy-done.2, bf16[1024,512]{1,0:T(8,128)(2,1)S(1)} %pad_maximum_fusion.cot_ref), custom_call_target="tpu_custom_call" | custom-call | flops 268435456 | bytes 2097152 | tf_op jit(solution)/shard_map/activated/pallas_call | solution.py:318
  170.4 4.9 %collective-permute-done.41.refs_1_ = bf16[512,512]{1,0:T(8,128)(2,1)S(1)} collective-permute-done((bf16[512,512]{1,0:T(8,128)(2,1)S(1)}, bf16[512,512]{1,0:T(8,128)(2,1)S(1)}, u32[]{:S(2)}, u32[]{:S(2)}) %collective-permute-start.41) | collective-permute-done | bytes 524320 | tf_op jit(solution)/shard_map/grads_xy/ppermute | solution.py:450
  175.3 2.4 %collective-permute-done.43.refs_3_ = bf16[512,512]{1,0:T(8,128)(2,1)S(1)} collective-permute-done((bf16[512,512]{1,0:T(8,128)(2,1)S(1)}, bf16[512,512]{1,0:T(8,128)(2,1)S(1)}, u32[]{:S(2)}, u32[]{:S(2)}) %collective-permute-start.43) | collective-permute-done | bytes 524320 | tf_op jit(solution)/shard_map/grads_z/ppermute | solution.py:450
  177.6 2.1 %grads_out.1 = (bf16[1,512,512]{2,1,0:T(8,128)(2,1)}, f32[512,512]{1,0:T(8,128)}) custom-call(s32[44]{0:T(128)S(1)} %pad_add_fusion.1.where_ref, bf16[512,512]{1,0:T(8,128)(2,1)S(1)} %get-tuple-element.289.refs_0_, bf16[512,512]{1,0:T(8,128)(2,1)S(1)} %collective-permute-done.41.refs_1_, bf16[512,512]{1,0:T(8,128)(2,1)S(1)} %collective-permute-done.42.refs_2_, ...), custom_call_target="tpu_custom_call" | custom-call | flops 1048576 | bytes 2621440 | tf_op jit(solution)/shard_map/grads_out/pallas_call | solution.py:416
  (70 shorter events, 8.1 us)
Async XLA Ops:
  0.6 1.2 copy-start
  0.6 16.3 %collective-permute-start = (bf16[8,24,128,128]{3,2,1,0:T(8,128)(2,1)}, bf16[8,24,128,128]{3,2,1,0:T(8,128)(2,1)}, u32[]{:S(2)}, u32[]{:S(2)}) collective-permute-start(bf16[8,24,128,128]{3,2,1,0:T(8,128)(2,1)} %bitcast.16), channel_id=1, source_target_pairs={{0,1},{1,0},{2,3},{3,2},{4,5},{5,4},{6,7},{7,6},{8,9},{9,8},{10,11... | collective-permute-start | bytes 18874376 | tf_op jit(solution)/shard_map/tiles_exchange/ppermute | solution.py:450
  1.9 15.0 %collective-permute-start.2 = (bf16[512,512]{1,0:T(8,128)(2,1)S(1)}, bf16[512,512]{1,0:T(8,128)(2,1)S(1)}, u32[]{:S(2)}, u32[]{:S(2)}) collective-permute-start(bf16[512,512]{1,0:T(8,128)(2,1)S(1)} %constant_dynamic-slice_fusion.refs_2_), channel_id=1, source_target_pairs={{0,8},{1,9},{2,10},{3,11},{4,12},{5,13},{6,14},{7,15},{8,0},{9,1},... | collective-permute-start | bytes 1572872 | tf_op jit(solution)/shard_map/features_z/ppermute | solution.py:450
  5.0 15.1 %collective-permute-start.3 = (bf16[512,512]{1,0:T(8,128)(2,1)S(1)}, bf16[512,512]{1,0:T(8,128)(2,1)S(1)}, u32[]{:S(2)}, u32[]{:S(2)}) collective-permute-start(bf16[512,512]{1,0:T(8,128)(2,1)S(1)} %constant_dynamic-slice_fusion.refs_2_), channel_id=1, source_target_pairs={{0,2},{1,3},{2,0},{3,1},{4,6},{5,7},{6,4},{7,5},{8,10},{9,11},{10,... | collective-permute-start | bytes 1572872 | tf_op jit(solution)/shard_map/features_xy/ppermute | solution.py:450
  6.5 16.2 %collective-permute-start.4 = (bf16[512,512]{1,0:T(8,128)(2,1)S(1)}, bf16[512,512]{1,0:T(8,128)(2,1)S(1)}, u32[]{:S(2)}, u32[]{:S(2)}) collective-permute-start(bf16[512,512]{1,0:T(8,128)(2,1)S(1)} %constant_dynamic-slice_fusion.refs_2_), channel_id=1, source_target_pairs={{0,4},{1,5},{2,6},{3,7},{4,0},{5,1},{6,2},{7,3},{8,12},{9,13},{10,... | collective-permute-start | bytes 1572872 | tf_op jit(solution)/shard_map/features_xy/ppermute | solution.py:450
  9.5 7.2 %collective-permute-start.1 = (s32[8,25]{1,0:T(8,128)S(1)}, s32[8,25]{1,0:T(8,128)S(1)}, u32[]{:S(2)}, u32[]{:S(2)}) collective-permute-start(s32[8,25]{1,0:T(8,128)S(1)} %pad_add_fusion.packed_ref), channel_id=1, source_target_pairs={{0,1},{1,0},{2,3},{3,2},{4,5},{5,4},{6,7},{7,6},{8,9},{9,8},{10,11... | collective-permute-start | bytes 2408 | tf_op jit(solution)/shard_map/tiles_exchange/ppermute | solution.py:450
  16.9 14.3 %collective-permute-start.5 = (bf16[512,512]{1,0:T(8,128)(2,1)S(1)}, bf16[512,512]{1,0:T(8,128)(2,1)S(1)}, u32[]{:S(2)}, u32[]{:S(2)}) collective-permute-start(bf16[512,512]{1,0:T(8,128)(2,1)S(1)} %collective-permute-done.2.refs_5_), channel_id=1, source_target_pairs={{0,2},{1,3},{2,0},{3,1},{4,6},{5,7},{6,4},{7,5},{8,10},{9,11},{10,... | collective-permute-start | bytes 1572872 | tf_op jit(solution)/shard_map/features_xy/ppermute | solution.py:450
  18.6 12.9 %collective-permute-start.6 = (bf16[512,512]{1,0:T(8,128)(2,1)S(1)}, bf16[512,512]{1,0:T(8,128)(2,1)S(1)}, u32[]{:S(2)}, u32[]{:S(2)}) collective-permute-start(bf16[512,512]{1,0:T(8,128)(2,1)S(1)} %collective-permute-done.2.refs_5_), channel_id=1, source_target_pairs={{0,4},{1,5},{2,6},{3,7},{4,0},{5,1},{6,2},{7,3},{8,12},{9,13},{10,... | collective-permute-start | bytes 1572872 | tf_op jit(solution)/shard_map/features_xy/ppermute | solution.py:450
  20.1 13.4 %collective-permute-start.10 = (bf16[512,512]{1,0:T(8,128)(2,1)}, bf16[512,512]{1,0:T(8,128)(2,1)}, u32[]{:S(2)}, u32[]{:S(2)}) collective-permute-start(bf16[512,512]{1,0:T(8,128)(2,1)} %param.14), channel_id=1, source_target_pairs={{0,1},{1,0},{2,3},{3,2},{4,5},{5,4},{6,7},{7,6},{8,9},{9,8},{10,11... | collective-permute-start | bytes 1572872 | tf_op jit(solution)/shard_map/cotangents/ppermute | solution.py:450
  20.1 26.6 %collective-permute-start.7 = (bf16[512,512]{1,0:T(8,128)(2,1)S(1)}, bf16[512,512]{1,0:T(8,128)(2,1)}, u32[]{:S(2)}, u32[]{:S(2)}) collective-permute-start(bf16[512,512]{1,0:T(8,128)(2,1)S(1)} %constant_dynamic-slice_fusion.refs_2_), channel_id=1, source_target_pairs={{0,16},{1,17},{2,18},{3,19},{4,20},{5,21},{6,22},{7,23},{8,24},{9,... | collective-permute-start | bytes 1572872 | tf_op jit(solution)/shard_map/features_z/ppermute | solution.py:450
  31.4 15.2 %collective-permute-start.8 = (bf16[512,512]{1,0:T(8,128)(2,1)S(1)}, bf16[512,512]{1,0:T(8,128)(2,1)}, u32[]{:S(2)}, u32[]{:S(2)}) collective-permute-start(bf16[512,512]{1,0:T(8,128)(2,1)S(1)} %collective-permute-done.3.refs_3_), channel_id=1, source_target_pairs={{0,4},{1,5},{2,6},{3,7},{4,0},{5,1},{6,2},{7,3},{8,12},{9,13},{10,... | collective-permute-start | bytes 1572872 | tf_op jit(solution)/shard_map/features_xy/ppermute | solution.py:450
  32.6 14.1 %collective-permute-start.9 = (bf16[512,512]{1,0:T(8,128)(2,1)S(1)}, bf16[512,512]{1,0:T(8,128)(2,1)}, u32[]{:S(2)}, u32[]{:S(2)}) collective-permute-start(bf16[512,512]{1,0:T(8,128)(2,1)S(1)} %collective-permute-done.6.refs_7_), channel_id=1, source_target_pairs={{0,2},{1,3},{2,0},{3,1},{4,6},{5,7},{6,4},{7,5},{8,10},{9,11},{10,... | collective-permute-start | bytes 1572872 | tf_op jit(solution)/shard_map/features_xy/ppermute | solution.py:450
  46.7 13.8 %collective-permute-start.11 = (bf16[512,512]{1,0:T(8,128)(2,1)}, bf16[512,512]{1,0:T(8,128)(2,1)S(1)}, u32[]{:S(2)}, u32[]{:S(2)}) collective-permute-start(bf16[512,512]{1,0:T(8,128)(2,1)} %collective-permute-done.7.refs_10_), channel_id=1, source_target_pairs={{0,2},{1,3},{2,0},{3,1},{4,6},{5,7},{6,4},{7,5},{8,10},{9,11},{10,... | collective-permute-start | bytes 1572872 | tf_op jit(solution)/shard_map/features_xy/ppermute | solution.py:450
  47.2 13.5 %collective-permute-start.12 = (bf16[512,512]{1,0:T(8,128)(2,1)}, bf16[512,512]{1,0:T(8,128)(2,1)S(1)}, u32[]{:S(2)}, u32[]{:S(2)}) collective-permute-start(bf16[512,512]{1,0:T(8,128)(2,1)} %collective-permute-done.7.refs_10_), channel_id=1, source_target_pairs={{0,4},{1,5},{2,6},{3,7},{4,0},{5,1},{6,2},{7,3},{8,12},{9,13},{10,... | collective-permute-start | bytes 1572872 | tf_op jit(solution)/shard_map/features_xy/ppermute | solution.py:450
  48.1 12.8 %collective-permute-start.13 = (bf16[512,512]{1,0:T(8,128)(2,1)}, bf16[512,512]{1,0:T(8,128)(2,1)S(1)}, u32[]{:S(2)}, u32[]{:S(2)}) collective-permute-start(bf16[512,512]{1,0:T(8,128)(2,1)} %collective-permute-done.7.refs_10_), channel_id=1, source_target_pairs={{0,8},{1,9},{2,10},{3,11},{4,12},{5,13},{6,14},{7,15},{8,0},{9,1},... | collective-permute-start | bytes 1572872 | tf_op jit(solution)/shard_map/features_z/ppermute | solution.py:450
  60.8 13.6 %collective-permute-start.14 = (bf16[512,512]{1,0:T(8,128)(2,1)S(1)}, bf16[512,512]{1,0:T(8,128)(2,1)S(1)}, u32[]{:S(2)}, u32[]{:S(2)}) collective-permute-start(bf16[512,512]{1,0:T(8,128)(2,1)S(1)} %collective-permute-done.12.refs_2_), channel_id=1, source_target_pairs={{0,2},{1,3},{2,0},{3,1},{4,6},{5,7},{6,4},{7,5},{8,10},{9,11},{10,... | collective-permute-start | bytes 1572872 | tf_op jit(solution)/shard_map/features_xy/ppermute | solution.py:450
  62.4 12.0 %collective-permute-start.15 = (bf16[512,512]{1,0:T(8,128)(2,1)S(1)}, bf16[512,512]{1,0:T(8,128)(2,1)S(1)}, u32[]{:S(2)}, u32[]{:S(2)}) collective-permute-start(bf16[512,512]{1,0:T(8,128)(2,1)S(1)} %collective-permute-done.13.refs_3_), channel_id=1, source_target_pairs={{0,4},{1,5},{2,6},{3,7},{4,0},{5,1},{6,2},{7,3},{8,12},{9,13},{10,... | collective-permute-start | bytes 1572872 | tf_op jit(solution)/shard_map/features_xy/ppermute | solution.py:450
  63.9 11.5 %collective-permute-start.16 = (bf16[512,512]{1,0:T(8,128)(2,1)S(1)}, bf16[512,512]{1,0:T(8,128)(2,1)S(1)}, u32[]{:S(2)}, u32[]{:S(2)}) collective-permute-start(bf16[512,512]{1,0:T(8,128)(2,1)S(1)} %collective-permute-done.11.refs_11_), channel_id=1, source_target_pairs={{0,8},{1,9},{2,10},{3,11},{4,12},{5,13},{6,14},{7,15},{8,0},{9,1},... | collective-permute-start | bytes 1572872 | tf_op jit(solution)/shard_map/features_z/ppermute | solution.py:450
  75.5 6.4 %collective-permute-start.17 = (bf16[256,512]{1,0:T(8,128)(2,1)S(1)}, bf16[256,512]{1,0:T(8,128)(2,1)S(1)}, u32[]{:S(2)}, u32[]{:S(2)}) collective-permute-start(bf16[256,512]{1,0:T(8,128)(2,1)S(1)} %slice.42), channel_id=1, source_target_pairs={{0,2},{1,3},{2,0},{3,1},{4,6},{5,7},{6,4},{7,5},{8,10},{9,11},{10,... | collective-permute-start | bytes 786440 | tf_op jit(solution)/shard_map/features_xy/ppermute | solution.py:450
  76.1 6.4 %collective-permute-start.18 = (bf16[256,512]{1,0:T(8,128)(2,1)S(1)}, bf16[256,512]{1,0:T(8,128)(2,1)S(1)}, u32[]{:S(2)}, u32[]{:S(2)}) collective-permute-start(bf16[256,512]{1,0:T(8,128)(2,1)S(1)} %slice.43), channel_id=1, source_target_pairs={{0,4},{1,5},{2,6},{3,7},{4,0},{5,1},{6,2},{7,3},{8,12},{9,13},{10,... | collective-permute-start | bytes 786440 | tf_op jit(solution)/shard_map/features_xy/ppermute | solution.py:450
  81.7 7.1 %copy-start.2 = (bf16[512,512]{1,0:T(8,128)(2,1)S(1)}, bf16[512,512]{1,0:T(8,128)(2,1)}, u32[]{:S(2)}) copy-start(bf16[512,512]{1,0:T(8,128)(2,1)} %weight_ref.3) | copy-start | bytes 1572868
  86.0 2.7 %collective-permute-start.19 = (bf16[1024,512]{1,0:T(8,128)(2,1)S(1)}, bf16[1024,512]{1,0:T(8,128)(2,1)S(1)}, u32[]{:S(2)}, u32[]{:S(2)}) collective-permute-start(bf16[1024,512]{1,0:T(8,128)(2,1)S(1)} %forward.5.mine_ref), channel_id=1, source_target_pairs={{0,1},{1,0},{2,3},{3,2},{4,5},{5,4},{6,7},{7,6},{8,9},{9,8},{10,11... | collective-permute-start | bytes 3145736 | tf_op jit(solution)/shard_map/partial_sums/ppermute | solution.py:450
  95.3 11.6 %collective-permute-start.20 = (bf16[64,512]{1,0:T(8,128)(2,1)S(1)}, bf16[64,512]{1,0:T(8,128)(2,1)S(1)}, u32[]{:S(2)}, u32[]{:S(2)}) collective-permute-start(bf16[64,512]{1,0:T(8,128)(2,1)S(1)} %get-tuple-element.303), channel_id=1, source_target_pairs={{0,8},{1,9},{2,10},{3,11},{4,12},{5,13},{6,14},{7,15},{8,0},{9,1},... | collective-permute-start | bytes 196616 | tf_op jit(solution)/shard_map/weight_grad/ppermute | solution.py:450
  96.8 10.7 %collective-permute-start.21 = (bf16[64,512]{1,0:T(8,128)(2,1)S(1)}, bf16[64,512]{1,0:T(8,128)(2,1)S(1)}, u32[]{:S(2)}, u32[]{:S(2)}) collective-permute-start(bf16[64,512]{1,0:T(8,128)(2,1)S(1)} %get-tuple-element.305), channel_id=1, source_target_pairs={{0,16},{1,17},{2,18},{3,19},{4,20},{5,21},{6,22},{7,23},{8,24},{9,... | collective-permute-start | bytes 196616 | tf_op jit(solution)/shard_map/weight_grad/ppermute | solution.py:450
  100.1 7.4 %collective-permute-start.22 = (bf16[64,512]{1,0:T(8,128)(2,1)S(1)}, bf16[64,512]{1,0:T(8,128)(2,1)S(1)}, u32[]{:S(2)}, u32[]{:S(2)}) collective-permute-start(bf16[64,512]{1,0:T(8,128)(2,1)S(1)} %get-tuple-element.304), channel_id=1, source_target_pairs={{0,24},{1,25},{2,26},{3,27},{4,28},{5,29},{6,30},{7,31},{8,16},{9,... | collective-permute-start | bytes 196616 | tf_op jit(solution)/shard_map/weight_grad/ppermute | solution.py:450
  100.2 7.8 %collective-permute-start.23 = (bf16[256,512]{1,0:T(8,128)(2,1)S(1)}, bf16[256,512]{1,0:T(8,128)(2,1)S(1)}, u32[]{:S(2)}, u32[]{:S(2)}) collective-permute-start(bf16[256,512]{1,0:T(8,128)(2,1)S(1)} %get-tuple-element.214), channel_id=1, source_target_pairs={{0,2},{1,3},{2,0},{3,1},{4,6},{5,7},{6,4},{7,5},{8,10},{9,11},{10,... | collective-permute-start | bytes 786440 | tf_op jit(solution)/shard_map/grads_xy/ppermute | solution.py:450
  101.6 7.5 %collective-permute-start.24 = (bf16[256,512]{1,0:T(8,128)(2,1)S(1)}, bf16[256,512]{1,0:T(8,128)(2,1)S(1)}, u32[]{:S(2)}, u32[]{:S(2)}) collective-permute-start(bf16[256,512]{1,0:T(8,128)(2,1)S(1)} %get-tuple-element.215), channel_id=1, source_target_pairs={{0,4},{1,5},{2,6},{3,7},{4,0},{5,1},{6,2},{7,3},{8,12},{9,13},{10,... | collective-permute-start | bytes 786440 | tf_op jit(solution)/shard_map/grads_xy/ppermute | solution.py:450
  106.9 14.3 %collective-permute-start.26 = (bf16[512,512]{1,0:T(8,128)(2,1)S(1)}, bf16[512,512]{1,0:T(8,128)(2,1)S(1)}, u32[]{:S(2)}, u32[]{:S(2)}) collective-permute-start(bf16[512,512]{1,0:T(8,128)(2,1)S(1)} %get-tuple-element.226), channel_id=1, source_target_pairs={{0,2},{1,3},{2,0},{3,1},{4,6},{5,7},{6,4},{7,5},{8,10},{9,11},{10,... | collective-permute-start | bytes 1572872 | tf_op jit(solution)/shard_map/grads_xy/ppermute | solution.py:450
  109.3 12.3 %collective-permute-start.27 = (bf16[512,512]{1,0:T(8,128)(2,1)S(1)}, bf16[512,512]{1,0:T(8,128)(2,1)S(1)}, u32[]{:S(2)}, u32[]{:S(2)}) collective-permute-start(bf16[512,512]{1,0:T(8,128)(2,1)S(1)} %get-tuple-element.231), channel_id=1, source_target_pairs={{0,4},{1,5},{2,6},{3,7},{4,0},{5,1},{6,2},{7,3},{8,12},{9,13},{10,... | collective-permute-start | bytes 1572872 | tf_op jit(solution)/shard_map/grads_xy/ppermute | solution.py:450
  109.9 11.9 %collective-permute-start.28 = (bf16[512,512]{1,0:T(8,128)(2,1)S(1)}, bf16[512,512]{1,0:T(8,128)(2,1)S(1)}, u32[]{:S(2)}, u32[]{:S(2)}) collective-permute-start(bf16[512,512]{1,0:T(8,128)(2,1)S(1)} %get-tuple-element.232), channel_id=1, source_target_pairs={{0,8},{1,9},{2,10},{3,11},{4,12},{5,13},{6,14},{7,15},{8,0},{9,1},... | collective-permute-start | bytes 1572872 | tf_op jit(solution)/shard_map/grads_z/ppermute | solution.py:450
  116.0 5.2 %collective-permute-start.25 = (bf16[64,512]{1,0:T(8,128)(2,1)S(1)}, bf16[64,512]{1,0:T(8,128)(2,1)S(1)}, u32[]{:S(2)}, u32[]{:S(2)}) collective-permute-start(bf16[64,512]{1,0:T(8,128)(2,1)S(1)} %fusion.2), channel_id=1, source_target_pairs={{0,2},{1,3},{2,0},{3,1},{4,6},{5,7},{6,4},{7,5},{8,10},{9,11},{10,... | collective-permute-start | bytes 196616 | tf_op jit(solution)/shard_map/weight_grad/ppermute | solution.py:450
  122.0 17.1 %collective-permute-start.32 = (bf16[512,512]{1,0:T(8,128)(2,1)S(1)}, bf16[512,512]{1,0:T(8,128)(2,1)S(1)}, u32[]{:S(2)}, u32[]{:S(2)}) collective-permute-start(bf16[512,512]{1,0:T(8,128)(2,1)S(1)} %add_convert_fusion.3), channel_id=1, source_target_pairs={{0,8},{1,9},{2,10},{3,11},{4,12},{5,13},{6,14},{7,15},{8,0},{9,1},... | collective-permute-start | bytes 1572872 | tf_op jit(solution)/shard_map/grads_z/ppermute | solution.py:450
  122.8 16.3 %collective-permute-start.31 = (bf16[512,512]{1,0:T(8,128)(2,1)S(1)}, bf16[512,512]{1,0:T(8,128)(2,1)S(1)}, u32[]{:S(2)}, u32[]{:S(2)}) collective-permute-start(bf16[512,512]{1,0:T(8,128)(2,1)S(1)} %add_convert_fusion.4), channel_id=1, source_target_pairs={{0,4},{1,5},{2,6},{3,7},{4,0},{5,1},{6,2},{7,3},{8,12},{9,13},{10,... | collective-permute-start | bytes 1572872 | tf_op jit(solution)/shard_map/grads_xy/ppermute | solution.py:450
  124.4 14.6 %collective-permute-start.30 = (bf16[512,512]{1,0:T(8,128)(2,1)S(1)}, bf16[512,512]{1,0:T(8,128)(2,1)S(1)}, u32[]{:S(2)}, u32[]{:S(2)}) collective-permute-start(bf16[512,512]{1,0:T(8,128)(2,1)S(1)} %add_convert_fusion.5), channel_id=1, source_target_pairs={{0,2},{1,3},{2,0},{3,1},{4,6},{5,7},{6,4},{7,5},{8,10},{9,11},{10,... | collective-permute-start | bytes 1572872 | tf_op jit(solution)/shard_map/grads_xy/ppermute | solution.py:450
  131.8 6.3 %collective-permute-start.29 = (bf16[64,512]{1,0:T(8,128)(2,1)S(1)}, bf16[64,512]{1,0:T(8,128)(2,1)S(1)}, u32[]{:S(2)}, u32[]{:S(2)}) collective-permute-start(bf16[64,512]{1,0:T(8,128)(2,1)S(1)} %add_convert_fusion.9), channel_id=1, source_target_pairs={{0,4},{1,5},{2,6},{3,7},{4,0},{5,1},{6,2},{7,3},{8,12},{9,13},{10,... | collective-permute-start | bytes 196616 | tf_op jit(solution)/shard_map/weight_grad/ppermute | solution.py:450
  132.9 20.1 %collective-permute-start.34 = (bf16[512,512]{1,0:T(8,128)(2,1)S(1)}, bf16[512,512]{1,0:T(8,128)(2,1)S(1)}, u32[]{:S(2)}, u32[]{:S(2)}) collective-permute-start(bf16[512,512]{1,0:T(8,128)(2,1)S(1)} %get-tuple-element.260), channel_id=1, source_target_pairs={{0,4},{1,5},{2,6},{3,7},{4,0},{5,1},{6,2},{7,3},{8,12},{9,13},{10,... | collective-permute-start | bytes 1572872 | tf_op jit(solution)/shard_map/grads_xy/ppermute | solution.py:450
  138.0 15.1 %collective-permute-start.35 = (bf16[512,512]{1,0:T(8,128)(2,1)S(1)}, bf16[512,512]{1,0:T(8,128)(2,1)S(1)}, u32[]{:S(2)}, u32[]{:S(2)}) collective-permute-start(bf16[512,512]{1,0:T(8,128)(2,1)S(1)} %get-tuple-element.261), channel_id=1, source_target_pairs={{0,2},{1,3},{2,0},{3,1},{4,6},{5,7},{6,4},{7,5},{8,10},{9,11},{10,... | collective-permute-start | bytes 1572872 | tf_op jit(solution)/shard_map/grads_xy/ppermute | solution.py:450
  139.4 13.7 %collective-permute-start.36 = (bf16[256,512]{1,0:T(8,128)(2,1)S(1)}, bf16[256,512]{1,0:T(8,128)(2,1)S(1)}, u32[]{:S(2)}, u32[]{:S(2)}) collective-permute-start(bf16[256,512]{1,0:T(8,128)(2,1)S(1)} %get-tuple-element.300), channel_id=1, source_target_pairs={{0,16},{1,17},{2,18},{3,19},{4,20},{5,21},{6,22},{7,23},{8,24},{9,... | collective-permute-start | bytes 786440 | tf_op jit(solution)/shard_map/grads_z/ppermute | solution.py:450
  147.1 5.9 %collective-permute-start.33 = (bf16[1,64,512]{2,1,0:T(8,128)(2,1)S(1)}, bf16[1,64,512]{2,1,0:T(8,128)(2,1)S(1)}, u32[]{:S(2)}, u32[]{:S(2)}) collective-permute-start(bf16[1,64,512]{2,1,0:T(8,128)(2,1)S(1)} %bitcast.19), channel_id=1, source_target_pairs={{0,16},{1,17},{2,18},{3,19},{4,20},{5,21},{6,22},{7,23},{8,24},{9,... | collective-permute-start | bytes 196616 | tf_op jit(solution)/shard_map/weight_grad/ppermute | solution.py:450
  147.2 18.2 %collective-permute-start.40 = (bf16[512,512]{1,0:T(8,128)(2,1)S(1)}, bf16[512,512]{1,0:T(8,128)(2,1)S(1)}, u32[]{:S(2)}, u32[]{:S(2)}) collective-permute-start(bf16[512,512]{1,0:T(8,128)(2,1)S(1)} %get-tuple-element.277), channel_id=1, source_target_pairs={{0,4},{1,5},{2,6},{3,7},{4,0},{5,1},{6,2},{7,3},{8,12},{9,13},{10,... | collective-permute-start | bytes 1572872 | tf_op jit(solution)/shard_map/grads_xy/ppermute | solution.py:450
  153.2 14.9 %collective-permute-start.39 = (bf16[512,512]{1,0:T(8,128)(2,1)S(1)}, bf16[512,512]{1,0:T(8,128)(2,1)S(1)}, u32[]{:S(2)}, u32[]{:S(2)}) collective-permute-start(bf16[512,512]{1,0:T(8,128)(2,1)S(1)} %add_convert_fusion.2), channel_id=1, source_target_pairs={{0,2},{1,3},{2,0},{3,1},{4,6},{5,7},{6,4},{7,5},{8,10},{9,11},{10,... | collective-permute-start | bytes 1572872 | tf_op jit(solution)/shard_map/grads_xy/ppermute | solution.py:450
  154.2 6.7 %collective-permute-start.37 = (bf16[2,64,512]{2,1,0:T(8,128)(2,1)S(1)}, bf16[2,64,512]{2,1,0:T(8,128)(2,1)S(1)}, u32[]{:S(2)}, u32[]{:S(2)}) collective-permute-start(bf16[2,64,512]{2,1,0:T(8,128)(2,1)S(1)} %pad_maximum_fusion.2), channel_id=1, source_target_pairs={{0,8},{1,9},{2,10},{3,11},{4,12},{5,13},{6,14},{7,15},{8,0},{9,1},... | collective-permute-start | bytes 393224 | tf_op jit(solution)/shard_map/weight_grad/ppermute | solution.py:450
  154.2 11.2 %collective-permute-start.38 = (bf16[256,512]{1,0:T(8,128)(2,1)S(1)}, bf16[256,512]{1,0:T(8,128)(2,1)S(1)}, u32[]{:S(2)}, u32[]{:S(2)}) collective-permute-start(bf16[256,512]{1,0:T(8,128)(2,1)S(1)} %get-tuple-element.273), channel_id=1, source_target_pairs={{0,16},{1,17},{2,18},{3,19},{4,20},{5,21},{6,22},{7,23},{8,24},{9,... | collective-permute-start | bytes 786440 | tf_op jit(solution)/shard_map/grads_z/ppermute | solution.py:450
  156.3 14.1 %collective-permute-start.42 = (bf16[512,512]{1,0:T(8,128)(2,1)S(1)}, bf16[512,512]{1,0:T(8,128)(2,1)S(1)}, u32[]{:S(2)}, u32[]{:S(2)}) collective-permute-start(bf16[512,512]{1,0:T(8,128)(2,1)S(1)} %add_convert_fusion.1), channel_id=1, source_target_pairs={{0,4},{1,5},{2,6},{3,7},{4,0},{5,1},{6,2},{7,3},{8,12},{9,13},{10,... | collective-permute-start | bytes 1572872 | tf_op jit(solution)/shard_map/grads_xy/ppermute | solution.py:450
  161.0 14.3 %collective-permute-start.41 = (bf16[512,512]{1,0:T(8,128)(2,1)S(1)}, bf16[512,512]{1,0:T(8,128)(2,1)S(1)}, u32[]{:S(2)}, u32[]{:S(2)}) collective-permute-start(bf16[512,512]{1,0:T(8,128)(2,1)S(1)} %get-tuple-element.281), channel_id=1, source_target_pairs={{0,2},{1,3},{2,0},{3,1},{4,6},{5,7},{6,4},{7,5},{8,10},{9,11},{10,... | collective-permute-start | bytes 1572872 | tf_op jit(solution)/shard_map/grads_xy/ppermute | solution.py:450
  168.2 11.6 %copy-start.1 = (bf16[1024,512]{1,0:T(8,128)(2,1)S(1)}, bf16[1024,512]{1,0:T(8,128)(2,1)}, u32[]{:S(2)}) copy-start(bf16[1024,512]{1,0:T(8,128)(2,1)} %param.8) | copy-start | bytes 3145732
  168.4 9.3 %collective-permute-start.43 = (bf16[512,512]{1,0:T(8,128)(2,1)S(1)}, bf16[512,512]{1,0:T(8,128)(2,1)S(1)}, u32[]{:S(2)}, u32[]{:S(2)}) collective-permute-start(bf16[512,512]{1,0:T(8,128)(2,1)S(1)} %add_convert_fusion), channel_id=1, source_target_pairs={{0,8},{1,9},{2,10},{3,11},{4,12},{5,13},{6,14},{7,15},{8,0},{9,1},... | collective-permute-start | bytes 1572872 | tf_op jit(solution)/shard_map/grads_z/ppermute | solution.py:450
  168.4 6.8 %collective-permute-start.44 = (bf16[4,64,512]{2,1,0:T(8,128)(2,1)S(1)}, bf16[4,64,512]{2,1,0:T(8,128)(2,1)S(1)}, u32[]{:S(2)}, u32[]{:S(2)}) collective-permute-start(bf16[4,64,512]{2,1,0:T(8,128)(2,1)S(1)} %pad_maximum_fusion.1.refs_6_), channel_id=1, source_target_pairs={{0,1},{1,0},{2,3},{3,2},{4,5},{5,4},{6,7},{7,6},{8,9},{9,8},{10,11... | collective-permute-start | bytes 786440 | tf_op jit(solution)/shard_map/weight_grad/ppermute | solution.py:450
